TPU v7x, 32 devices: a whole 2x2x4 slice. The times are simulated.
32 devices in a mesh: dp: 8 (over y, x, core), fsdp: 4 (over z).
Axes of the slice: x: 2, y: 2, z: 4, core: 2. Of those that a mesh axis runs over, the one named last changes fastest.
Arguments:
- tokens: bfloat16 [16, 1024, 2048], P('dp', 'fsdp'), may hold values from -6 to 6
- cotangent: bfloat16 [16, 1024, 2048], P('dp', 'fsdp'), may hold values from -6 to 6
- lengths: int32 [16, 8], P('dp'), may hold values from 1 to 928, as said below
- query_weight: bfloat16 [2048, 2048], P(('dp', 'fsdp')), may hold values from -0.125 to 0.125
- kv_weight: bfloat16 [2048, 256], P(('dp', 'fsdp')), may hold values from -0.125 to 0.125
- out_weight: bfloat16 [2048, 2048], P(('dp', 'fsdp')), may hold values from -0.75 to 0.75
- query_bias: bfloat16 [2048], P(('dp', 'fsdp')), may hold values from -3 to 3
- value_bias: bfloat16 [128], P(('dp', 'fsdp')), may hold values from -1.1953125 to 1.1953125
- out_bias: bfloat16 [2048], P(('dp', 'fsdp')), may hold values from -3 to 3
- attn_gain: bfloat16 [2048], P(('dp', 'fsdp')), may hold values from 0.5 to 1.5
- attn_shift: bfloat16 [2048], P(('dp', 'fsdp')), may hold values from -2 to 2
- up_weight: bfloat16 [2048, 8192], P(('dp', 'fsdp')), may hold values from -0.125 to 0.125
- down_weight: bfloat16 [8192, 2048], P(('dp', 'fsdp')), may hold values from -0.0625 to 0.0625
- up_bias: bfloat16 [8192], P(('dp', 'fsdp')), may hold values from -3 to 3
- down_bias: bfloat16 [2048], P(('dp', 'fsdp')), may hold values from -3 to 3
- mlp_gain: bfloat16 [2048], P(('dp', 'fsdp')), may hold values from 0.5 to 1.5
- mlp_shift: bfloat16 [2048], P(('dp', 'fsdp')), may hold values from -2 to 2
Outputs:
- output: bfloat16 [16, 1024, 2048], P('dp', 'fsdp')
- tokens_grad: bfloat16 [16, 1024, 2048], P('dp', 'fsdp')
- query_weight_grad: float32 [2048, 2048], P(('dp', 'fsdp'))
- kv_weight_grad: float32 [2048, 256], P(('dp', 'fsdp'))
- out_weight_grad: float32 [2048, 2048], P(('dp', 'fsdp'))
- query_bias_grad: float32 [2048], P(('dp', 'fsdp'))
- value_bias_grad: float32 [128], P(('dp', 'fsdp'))
- out_bias_grad: float32 [2048], P(('dp', 'fsdp'))
- attn_gain_grad: float32 [2048], P(('dp', 'fsdp'))
- attn_shift_grad: float32 [2048], P(('dp', 'fsdp'))
- up_weight_grad: float32 [2048, 8192], P(('dp', 'fsdp'))
- down_weight_grad: float32 [8192, 2048], P(('dp', 'fsdp'))
- up_bias_grad: float32 [8192], P(('dp', 'fsdp'))
- down_bias_grad: float32 [2048], P(('dp', 'fsdp'))
- mlp_gain_grad: float32 [2048], P(('dp', 'fsdp'))
- mlp_shift_grad: float32 [2048], P(('dp', 'fsdp'))
Inputs may be any that keep to these rules, and one draw needn't show every extreme that they name: `lengths`: row w lists the token counts of window w's 8 files in order; one file of each window, at a place drawn from the seed, has exactly 928 tokens; the window's last 1024 minus the row's sum positions are padding.
All inputs are finite; a program needn't handle non-finite values.
Results may differ from a plain program's by a relative error of at most 0.014.
Values may be sent and summed in bfloat16 or wider, within the bound.
No kernel may reach another device: no remote copies, remote signals or barrier semaphores. Data moves between devices by JAX's collectives and lax.ppermute only.
A program may use at most 384 MiB of HBM per device.

v0:
```python
import math

import jax
import jax.numpy as jnp
from jax import lax
from jax.sharding import PartitionSpec as P

HEADS = 16
HD = 128
WIN = 1024


EPS = 1e-05


def layer_norm(values, gain_vec, shift_vec):
    average = jnp.mean(values, axis=-1, keepdims=True)
    centered = values - average
    variance = jnp.mean(centered * centered, axis=-1, keepdims=True)
    return centered * lax.rsqrt(variance + EPS) * gain_vec + shift_vec


def gelu_tanh(values):
    return jax.nn.gelu(values, approximate=True)


def attention_params(
    query_weight, kv_weight, out_weight, query_bias, value_bias, out_bias, attn_gain, attn_shift
):
    return (
        lax.all_gather(query_weight, ("dp", "fsdp"), axis=0, tiled=True),
        lax.all_gather(kv_weight, ("dp", "fsdp"), axis=0, tiled=True),
        lax.all_gather(out_weight, ("dp", "fsdp"), axis=0, tiled=True),
        lax.all_gather(query_bias, ("dp", "fsdp"), axis=0, tiled=True),
        lax.all_gather(value_bias, ("dp", "fsdp"), axis=0, tiled=True),
        lax.all_gather(out_bias, ("dp", "fsdp"), axis=0, tiled=True),
        lax.all_gather(attn_gain, ("dp", "fsdp"), axis=0, tiled=True),
        lax.all_gather(attn_shift, ("dp", "fsdp"), axis=0, tiled=True),
    )


def feed_params(up_weight, down_weight, up_bias, down_bias, mlp_gain, mlp_shift):
    members = (up_weight, down_weight, up_bias, down_bias, mlp_gain, mlp_shift)
    shared = (
        lax.all_gather(members[0], ("dp", "fsdp"), axis=0, tiled=True),
        lax.all_gather(members[1], ("dp", "fsdp"), axis=0, tiled=True),
        lax.all_gather(members[2], ("dp", "fsdp"), axis=0, tiled=True),
        lax.all_gather(members[3], ("dp", "fsdp"), axis=0, tiled=True),
        lax.all_gather(members[4], ("dp", "fsdp"), axis=0, tiled=True),
        lax.all_gather(members[5], ("dp", "fsdp"), axis=0, tiled=True),
    )
    return shared


def masked_scores(query_block, kv_rows, allowed_block, root_hd):
    scores = (
        jnp.einsum("qd,kd->qk", query_block, kv_rows[:, :HD], preferred_element_type=jnp.float32)
        / root_hd
    )
    scores = scores.reshape(HEADS, -1, kv_rows.shape[0])
    return jnp.where(allowed_block[None], scores, -1e30)


def local(
    tokens,
    cotangent,
    lengths,
    query_weight,
    kv_weight,
    out_weight,
    query_bias,
    value_bias,
    out_bias,
    attn_gain,
    attn_shift,
    up_weight,
    down_weight,
    up_bias,
    down_bias,
    mlp_gain,
    mlp_shift,
):
    windows, local_len, model_width = tokens.shape
    row_count = windows * local_len
    root_hd = math.sqrt(HD)
    query_pos = lax.axis_index("fsdp") * local_len + jnp.arange(local_len, dtype=jnp.int32)
    key_pos = jnp.arange(WIN, dtype=jnp.int32)
    file_ends = jnp.cumsum(lengths, axis=1)
    key_files = jnp.sum((file_ends[:, None, :] <= key_pos[None, :, None]).astype(jnp.int32), axis=2)
    query_files = jnp.sum(
        (file_ends[:, None, :] <= query_pos[None, :, None]).astype(jnp.int32), axis=2
    )
    allowed = (query_files[:, :, None] == key_files[:, None, :]) & (
        key_pos[None, None, :] <= query_pos[None, :, None]
    )
    full_q, full_kv, full_o, bias_q, bias_v, bias_o, gain_one, shift_one = attention_params(
        query_weight, kv_weight, out_weight, query_bias, value_bias, out_bias, attn_gain, attn_shift
    )
    inputs = tokens.reshape(row_count, model_width).astype(jnp.float32)
    normed_full, norm_one_pull = jax.vjp(
        layer_norm, inputs, gain_one.astype(jnp.float32), shift_one.astype(jnp.float32)
    )
    normed_one = normed_full.astype(jnp.bfloat16)
    queries = (
        jnp.dot(normed_one, full_q, preferred_element_type=jnp.float32) + bias_q.astype(jnp.float32)
    ).astype(jnp.bfloat16)
    kv_bias = jnp.concatenate([jnp.zeros((HD,), jnp.float32), bias_v.astype(jnp.float32)])
    key_value = (jnp.dot(normed_one, full_kv, preferred_element_type=jnp.float32) + kv_bias).astype(
        jnp.bfloat16
    )
    kv_window = lax.all_gather(
        key_value.reshape(windows, local_len, 2 * HD), "fsdp", axis=1, tiled=True
    )
    query_rows = (
        queries.reshape(windows, local_len, HEADS, HD)
        .transpose(0, 2, 1, 3)
        .reshape(windows, HEADS * local_len, HD)
    )
    mixed_list = []
    norm_list = []
    for window_idx in range(windows):
        scores = masked_scores(
            query_rows[window_idx], kv_window[window_idx], allowed[window_idx], root_hd
        )
        row_max = jnp.max(scores, axis=2, keepdims=True)
        exp_terms = jnp.exp(scores - row_max)
        row_total = jnp.sum(exp_terms, axis=2, keepdims=True)
        prob_low = (exp_terms / row_total).astype(jnp.bfloat16).reshape(HEADS * local_len, WIN)
        mixed_list.append(
            jnp.dot(prob_low, kv_window[window_idx][:, HD:], preferred_element_type=jnp.float32)
        )
        norm_list.append(row_max + jnp.log(row_total))
    attended = jnp.stack(mixed_list).reshape(windows, HEADS, local_len, HD).transpose(0, 2, 1, 3)
    attended = attended.reshape(row_count, model_width).astype(jnp.bfloat16)
    middle = (
        inputs
        + jnp.dot(attended, full_o, preferred_element_type=jnp.float32)
        + bias_o.astype(jnp.float32)
    )
    full_up, full_down, bias_up, bias_down, gain_two, shift_two = feed_params(
        up_weight, down_weight, up_bias, down_bias, mlp_gain, mlp_shift
    )
    normed_mid, norm_two_pull = jax.vjp(
        layer_norm, middle, gain_two.astype(jnp.float32), shift_two.astype(jnp.float32)
    )
    normed_two = normed_mid.astype(jnp.bfloat16)
    pre_act = jnp.dot(normed_two, full_up, preferred_element_type=jnp.float32) + bias_up.astype(
        jnp.float32
    )
    hidden_full, gelu_pull = jax.vjp(gelu_tanh, pre_act)
    hidden = hidden_full.astype(jnp.bfloat16)
    branch_out = jnp.dot(hidden, full_down, preferred_element_type=jnp.float32)
    result = middle + branch_out + bias_down.astype(jnp.float32)
    output = result.astype(jnp.bfloat16).reshape(windows, local_len, model_width)
    grad_low = cotangent.reshape(row_count, model_width)
    grad_out = grad_low.astype(jnp.float32)
    full_up, full_down, bias_up, bias_down, gain_two, shift_two = feed_params(
        up_weight, down_weight, up_bias, down_bias, mlp_gain, mlp_shift
    )
    grad_bdown = jnp.sum(grad_out, axis=0)
    grad_down = jnp.einsum("rf,rd->fd", hidden, grad_low, preferred_element_type=jnp.float32)
    grad_hidden = jnp.einsum("rd,fd->rf", grad_low, full_down, preferred_element_type=jnp.float32)
    pre_grad = gelu_pull(grad_hidden)[0].astype(jnp.bfloat16)
    grad_up = jnp.einsum("rd,rf->df", normed_two, pre_grad, preferred_element_type=jnp.float32)
    grad_bup = jnp.sum(pre_grad.astype(jnp.float32), axis=0)
    normed_two_grad = jnp.einsum("rf,df->rd", pre_grad, full_up, preferred_element_type=jnp.float32)
    mid_norm_grad, grad_gain_two, grad_shift_two = norm_two_pull(normed_two_grad)
    grad_members = (grad_up, grad_down, grad_bup, grad_bdown, grad_gain_two, grad_shift_two)
    mlp_sums = (
        lax.psum_scatter(grad_members[0], ("dp", "fsdp"), scatter_dimension=0, tiled=True),
        lax.psum_scatter(grad_members[1], ("dp", "fsdp"), scatter_dimension=0, tiled=True),
        lax.psum_scatter(grad_members[2], ("dp", "fsdp"), scatter_dimension=0, tiled=True),
        lax.psum_scatter(grad_members[3], ("dp", "fsdp"), scatter_dimension=0, tiled=True),
        lax.psum_scatter(grad_members[4], ("dp", "fsdp"), scatter_dimension=0, tiled=True),
        lax.psum_scatter(grad_members[5], ("dp", "fsdp"), scatter_dimension=0, tiled=True),
    )
    middle_grad = grad_out + mid_norm_grad
    grad_bo = jnp.sum(middle_grad, axis=0)
    branch_grad = middle_grad.astype(jnp.bfloat16)
    full_q, full_kv, full_o, bias_q, bias_v, bias_o, gain_one, shift_one = attention_params(
        query_weight, kv_weight, out_weight, query_bias, value_bias, out_bias, attn_gain, attn_shift
    )
    grad_wo = jnp.einsum("rd,re->de", attended, branch_grad, preferred_element_type=jnp.float32)
    attended_grad = jnp.einsum(
        "re,de->rd", branch_grad, full_o, preferred_element_type=jnp.float32
    ).astype(jnp.bfloat16)
    grad_heads = (
        attended_grad.reshape(windows, local_len, HEADS, HD)
        .transpose(0, 2, 1, 3)
        .reshape(windows, HEADS * local_len, HD)
    )
    query_list = []
    kv_terms = []
    for window_idx in range(windows):
        kv_rows = kv_window[window_idx]
        scores = masked_scores(query_rows[window_idx], kv_rows, allowed[window_idx], root_hd)
        prob_full = jnp.exp(scores - norm_list[window_idx])
        prob_low = prob_full.astype(jnp.bfloat16).reshape(HEADS * local_len, WIN)
        grad_probs = jnp.einsum(
            "qd,kd->qk", grad_heads[window_idx], kv_rows[:, HD:], preferred_element_type=jnp.float32
        )
        grad_probs = grad_probs.reshape(HEADS, local_len, WIN)
        row_delta = jnp.sum(prob_full * grad_probs, axis=2, keepdims=True)
        score_grad = (
            (prob_full * (grad_probs - row_delta))
            .astype(jnp.bfloat16)
            .reshape(HEADS * local_len, WIN)
        )
        query_list.append(
            jnp.dot(score_grad, kv_rows[:, :HD], preferred_element_type=jnp.float32) / root_hd
        )
        key_term = (
            jnp.einsum(
                "qk,qd->kd", score_grad, query_rows[window_idx], preferred_element_type=jnp.float32
            )
            / root_hd
        )
        value_term = jnp.einsum(
            "qk,qd->kd", prob_low, grad_heads[window_idx], preferred_element_type=jnp.float32
        )
        kv_terms.append(jnp.concatenate([key_term, value_term], axis=1))
    query_grad = jnp.stack(query_list).reshape(windows, HEADS, local_len, HD).transpose(0, 2, 1, 3)
    query_grad = query_grad.reshape(row_count, model_width).astype(jnp.bfloat16)
    kv_grad = lax.psum_scatter(
        jnp.stack(kv_terms).astype(jnp.bfloat16), "fsdp", scatter_dimension=1, tiled=True
    ).astype(jnp.float32)
    kv_grad = kv_grad.reshape(row_count, 2 * HD).astype(jnp.bfloat16)
    grad_bq = jnp.sum(query_grad.astype(jnp.float32), axis=0)
    grad_bv = jnp.sum(kv_grad[:, HD:].astype(jnp.float32), axis=0)
    grad_wq = jnp.einsum("rd,re->de", normed_one, query_grad, preferred_element_type=jnp.float32)
    grad_wkv = jnp.einsum("rd,re->de", normed_one, kv_grad, preferred_element_type=jnp.float32)
    normed_one_grad = jnp.einsum(
        "re,de->rd", query_grad, full_q, preferred_element_type=jnp.float32
    )
    normed_one_grad = normed_one_grad + jnp.einsum(
        "re,de->rd", kv_grad, full_kv, preferred_element_type=jnp.float32
    )
    input_norm_grad, grad_gain_one, grad_shift_one = norm_one_pull(normed_one_grad)
    tokens_grad = (
        (middle_grad + input_norm_grad)
        .astype(jnp.bfloat16)
        .reshape(windows, local_len, model_width)
    )
    attn_sums = (
        lax.psum_scatter(grad_wq, ("dp", "fsdp"), scatter_dimension=0, tiled=True),
        lax.psum_scatter(grad_wkv, ("dp", "fsdp"), scatter_dimension=0, tiled=True),
        lax.psum_scatter(grad_wo, ("dp", "fsdp"), scatter_dimension=0, tiled=True),
        lax.psum_scatter(grad_bq, ("dp", "fsdp"), scatter_dimension=0, tiled=True),
        lax.psum_scatter(grad_bv, ("dp", "fsdp"), scatter_dimension=0, tiled=True),
        lax.psum_scatter(grad_bo, ("dp", "fsdp"), scatter_dimension=0, tiled=True),
        lax.psum_scatter(grad_gain_one, ("dp", "fsdp"), scatter_dimension=0, tiled=True),
        lax.psum_scatter(grad_shift_one, ("dp", "fsdp"), scatter_dimension=0, tiled=True),
    )
    return (
        output,
        tokens_grad,
        attn_sums[0],
        attn_sums[1],
        attn_sums[2],
        attn_sums[3],
        attn_sums[4],
        attn_sums[5],
        attn_sums[6],
        attn_sums[7],
        mlp_sums[0],
        mlp_sums[1],
        mlp_sums[2],
        mlp_sums[3],
        mlp_sums[4],
        mlp_sums[5],
    )


def solution(mesh):
    return jax.shard_map(
        local,
        mesh=mesh,
        in_specs=(
            P("dp", "fsdp", None),
            P("dp", "fsdp", None),
            P("dp", None),
            P(("dp", "fsdp"), None),
            P(("dp", "fsdp"), None),
            P(("dp", "fsdp"), None),
            P(("dp", "fsdp")),
            P(("dp", "fsdp")),
            P(("dp", "fsdp")),
            P(("dp", "fsdp")),
            P(("dp", "fsdp")),
            P(("dp", "fsdp"), None),
            P(("dp", "fsdp"), None),
            P(("dp", "fsdp")),
            P(("dp", "fsdp")),
            P(("dp", "fsdp")),
            P(("dp", "fsdp")),
        ),
        out_specs=(
            P("dp", "fsdp", None),
            P("dp", "fsdp", None),
            P(("dp", "fsdp"), None),
            P(("dp", "fsdp"), None),
            P(("dp", "fsdp"), None),
            P(("dp", "fsdp")),
            P(("dp", "fsdp")),
            P(("dp", "fsdp")),
            P(("dp", "fsdp")),
            P(("dp", "fsdp")),
            P(("dp", "fsdp"), None),
            P(("dp", "fsdp"), None),
            P(("dp", "fsdp")),
            P(("dp", "fsdp")),
            P(("dp", "fsdp")),
            P(("dp", "fsdp")),
        ),
        check_vma=False,
    )
```

profile of v0, /device:TPU:0, one launch (start us, length us, event | category | flops | bytes accessed | tf_op | source)
XLA Modules:
  0.0 4649.8 jit_solution(1834663549461914050)
XLA Ops:
  14.8 42.6 all-reduce.19
  57.4 1.9 convert_reduce_fusion.1
  59.4 2.3 fusion.35
  62.3 2.2 fusion.33
  64.4 3.2 all-gather.10.cloned.1.call-done
  67.6 3.3 fusion.58
  73.5 67.3 %all-gather = bf16[32,1,256]{2,1,0:T(2,128)(2,1)S(1)} all-gather(bf16[1,1,256]{2,1,0:T(2,128)(2,1)S(1)} %reshape.356), channel_id=1, replica_groups=mesh['dp'=8,'fsdp'=4] {'dp','fsdp'}, dimensions={0}, use_global_device_ids=true | all-gather | bytes 16896 | tf_op jit(solution)/shard_map/all_gather | solution.py:47
  141.3 2.6 convert_reduce_fusion.2
  144.6 2.2 fusion.38
  146.7 2.1 slice_bitcast_fusion.3
  148.8 29.4 all-gather.8.cloned.1.call-done
  178.2 8.5 fusion.57
  189.0 3.0 fusion.12
  192.0 5.3 fusion.18
  198.4 4.2 fusion.11
  202.5 5.0 fusion.17
  208.3 28.5 exponential_convert_fusion
  237.5 5.9 convolution_convert_fusion
  244.1 2.3 convolution_convert_fusion.1
  247.1 1.5 pad_maximum_fusion
  248.6 8.3 all-gather.14.cloned.1.call-done
  257.0 7.8 fusion.123
  264.8 2.0 copy-done.5
  267.3 185.9 %all-gather.16.cloned.1.call-done = bf16[2048,8192]{1,0:T(8,128)(2,1)} async-done(((bf16[64,8192]{1,0:T(8,128)(2,1)}), bf16[2048,8192]{1,0:T(8,128)(2,1)}) %all-gather.16.cloned.1.call-update) | async-done | bytes 33554448 | tf_op jit(solution)/shard_map/all_gather | solution.py:45
  453.2 28.3 fusion.115
  481.5 167.5 %all-gather.18.cloned.1.call-done = bf16[8192,2048]{1,0:T(8,128)(2,1)} async-done(((bf16[256,2048]{1,0:T(8,128)(2,1)}), bf16[8192,2048]{1,0:T(8,128)(2,1)}) %all-gather.18.cloned.1.call-update) | async-done | bytes 33554448 | tf_op jit(solution)/shard_map/all_gather | solution.py:46
  649.0 34.2 convert_reduce_fusion
  683.2 27.1 multiply_reduce_fusion.2
  710.3 3.4 fusion.120
  713.7 1.9 fusion.119
  715.7 9.7 fusion.56
  726.6 1.5 fusion.121
  728.1 20.8 multiply_convert_fusion
  748.9 5.5 fusion.60
  754.4 20.4 multiply_convert_fusion.1
  774.8 4.9 fusion.59
  779.8 4.9 convolution_convert_fusion.3
  784.8 1.3 convolution_convert_fusion.4
  787.5 5.7 convolution_multiply_fusion.2
  794.0 6.1 convolution_multiply_fusion.3
  802.0 1.3 copy-done.23
  803.3 6.1 fusion.43
  809.5 3.3 reduce-scatter.7.cloned.1.call-done
  814.5 4.1 fusion.117
  818.6 2.6 fusion.34
  821.3 3.9 convolution_bitcast_fusion
  825.5 9.8 fusion.41
  835.4 1.5 copy-done.22
  836.9 10.6 fusion.45
  848.2 32.1 fusion.114
  880.6 1.3 copy-done.14
  881.9 32.2 fusion.116
  914.9 28.2 add_convert_fusion.1
  943.2 2.7 add_convert_fusion
  945.9 1.3 dynamic-slice
  947.2 1.3 dynamic-slice.2
  950.9 1.3 dynamic-slice.6
  952.2 1.3 dynamic-slice.7
  955.9 1.3 dynamic-slice.5
  957.2 129.9 %reduce-scatter.11.cloned.1.call-done = f32[64,256]{1,0:T(8,128)} async-done(((f32[2048,256]{1,0:T(8,128)}), f32[64,256]{1,0:T(8,128)}) %reduce-scatter.11.cloned.1.call-update) | async-done | bytes 65552 | tf_op jit(solution)/shard_map/reduce_scatter | solution.py:246
  1087.1 365.4 %reduce-scatter.9.cloned.1.call-done = f32[64,2048]{1,0:T(8,128)} async-done(((f32[2048,2048]{1,0:T(8,128)}), f32[64,2048]{1,0:T(8,128)}) %reduce-scatter.9.cloned.1.call-update) | async-done | bytes 524304 | tf_op jit(solution)/shard_map/reduce_scatter | solution.py:245
  1452.4 365.2 %reduce-scatter.13.cloned.1.call-done = f32[64,2048]{1,0:T(8,128)} async-done(((f32[2048,2048]{1,0:T(8,128)}), f32[64,2048]{1,0:T(8,128)}) %reduce-scatter.13.cloned.1.call-update) | async-done | bytes 524304 | tf_op jit(solution)/shard_map/reduce_scatter | solution.py:247
  1817.6 1411.5 %reduce-scatter.15.cloned.1.call-done = f32[64,8192]{1,0:T(8,128)} async-done(((f32[2048,8192]{1,0:T(8,128)}), f32[64,8192]{1,0:T(8,128)}) %reduce-scatter.15.cloned.1.call-update) | async-done | bytes 2097168 | tf_op jit(solution)/shard_map/reduce_scatter | solution.py:170
  3229.1 1413.7 %reduce-scatter.17.cloned.1.call-done = f32[256,2048]{1,0:T(8,128)} async-done(((f32[8192,2048]{1,0:T(8,128)}), f32[256,2048]{1,0:T(8,128)}) %reduce-scatter.17.cloned.1.call-update) | async-done | bytes 2097168 | tf_op jit(solution)/shard_map/reduce_scatter | solution.py:171
  (214 shorter events, 32.4 us)
Async XLA Ops:
  7.2 55.1 %copy-start.2 = (bf16[2,256,2048]{2,1,0:T(8,128)(2,1)S(1)}, bf16[2,256,2048]{2,1,0:T(8,128)(2,1)}, u32[]{:S(2)}) copy-start(bf16[2,256,2048]{2,1,0:T(8,128)(2,1)} %param.17) | copy-start | bytes 6291460
  7.2 60.4 %all-gather.10.cloned.1.call-start = ((), (), s32[]{:S(2)}) async-start(), calls=%async_computation.7 | async-start | bytes 1081344 | tf_op jit(solution)/shard_map/all_gather | solution.py:32
  7.9 138.8 %all-gather.12.cloned.1.call-start = ((), (), s32[]{:S(2)}) async-start(), calls=%async_computation.8 | async-start | bytes 1310720 | tf_op jit(solution)/shard_map/all_gather | solution.py:111
  57.4 87.1 %copy-start.34 = (f32[2048]{0:T(1024)}, f32[2048]{0:T(1024)S(1)}, u32[]{:S(2)}) copy-start(f32[2048]{0:T(1024)S(1)} %convert_element_type.148) | copy-start | bytes 24580
  62.3 8.6 copy-start.41
  62.3 8.6 copy-start.38
  64.4 9.1 copy-start.55
  64.4 76.4 %copy-start.54 = (s32[2,8]{1,0:T(2,128)S(1)}, s32[2,8]{1,0:T(2,128)}, u32[]{:S(2)}) copy-start(s32[2,8]{1,0:T(2,128)} %param.19) | copy-start | bytes 196
  70.9 107.3 %all-gather.8.cloned.1.call-start = ((), (), s32[]{:S(2)}) async-start(), calls=%async_computation.6 | async-start | bytes 8650752 | tf_op jit(solution)/shard_map/all_gather | solution.py:31
  71.6 185.3 %all-gather.14.cloned.1.call-start = ((), (), s32[]{:S(2)}) async-start(), calls=%async_computation.9 | async-start | bytes 8650752 | tf_op jit(solution)/shard_map/all_gather | solution.py:33
  72.2 381.0 %all-gather.16.cloned.1.call-start = ((), (), s32[]{:S(2)}) async-start(), calls=%async_computation.10 | async-start | bytes 34603008 | tf_op jit(solution)/shard_map/all_gather | solution.py:45
  72.8 576.1 %all-gather.18.cloned.1.call-start = ((), (), s32[]{:S(2)}) async-start(), calls=%async_computation.11 | async-start | bytes 34603008 | tf_op jit(solution)/shard_map/all_gather | solution.py:46
  73.4 739.4 %reduce-scatter.7.cloned.1.call-start = ((), (), s32[]{:S(2)}) async-start(), calls=%async_computation.12 | async-start | bytes 1310720 | tf_op jit(solution)/shard_map/reduce_scatter | solution.py:224
  73.5 379.7 %copy-start.32 = (f32[2048]{0:T(1024)}, f32[2048]{0:T(1024)S(1)}, u32[]{:S(2)}) copy-start(f32[2048]{0:T(1024)S(1)} %convert_element_type.160) | copy-start | bytes 24580
  140.9 508.1 %copy-start.44 = (f32[32,1,256]{2,1,0:T(1,128)}, f32[32,1,256]{2,1,0:T(1,128)S(1)}, u32[]{:S(2)}) copy-start(f32[32,1,256]{2,1,0:T(1,128)S(1)} %convert_element_type.186) | copy-start | bytes 98308
  144.5 63.8 %copy-start.15 = (pred[256,1024]{1,0:T(8,128)(4,1)}, pred[256,1024]{1,0:T(8,128)(4,1)S(1)}, u32[]{:S(2)}) copy-start(pred[256,1024]{1,0:T(8,128)(4,1)S(1)} %get-tuple-element.58) | copy-start | bytes 786436
  144.5 63.8 %copy-start.17 = (pred[256,1024]{1,0:T(8,128)(4,1)}, pred[256,1024]{1,0:T(8,128)(4,1)S(1)}, u32[]{:S(2)}) copy-start(pred[256,1024]{1,0:T(8,128)(4,1)S(1)} %get-tuple-element.59) | copy-start | bytes 786436
  148.8 95.3 %copy-start.24 = (bf16[1024,256]{1,0:T(8,128)(2,1)}, bf16[1024,256]{1,0:T(8,128)(2,1)S(1)}, u32[]{:S(2)}) copy-start(bf16[1024,256]{1,0:T(8,128)(2,1)S(1)} %get-tuple-element.56) | copy-start | bytes 1572868
  189.0 3.0 copy-start.20
  192.0 5.7 copy-start
  202.5 5.8 copy-start.1
  237.5 6.6 copy-start.12
  264.8 2.0 copy-start.5
  267.3 381.6 %copy-start.13 = (bf16[2,256,2048]{2,1,0:T(8,128)(2,1)S(1)}, bf16[2,256,2048]{2,1,0:T(8,128)(2,1)}, u32[]{:S(2)}) copy-start(bf16[2,256,2048]{2,1,0:T(8,128)(2,1)} %param.18) | copy-start | bytes 6291460
  683.2 27.1 copy-start.6
  715.7 9.7 copy-start.9
  726.0 2.1 copy-start.18
  726.1 2.1 copy-start.50
  728.1 20.8 copy-start.21
  748.9 5.5 copy-start.16
  748.9 5.5 copy-start.51
  754.4 20.4 copy-start.19
  774.8 4.9 copy-start.30
  774.8 9.9 slice-start
  779.7 5.0 copy-start.37
  779.7 5.0 slice-start.1
  779.8 5.0 copy-start.29
  787.3 6.7 copy-start.25
  787.3 158.6 %all-reduce.22.cloned.1.call-start = ((), (), s32[]{:S(2)}) async-start(), calls=%async_computation.18 | async-start | bytes 181248
  793.3 10.0 slice-start.2
  794.0 9.3 slice-start.3
  803.3 11.1 copy-start.3
  803.3 11.1 copy-start.31
  803.3 11.1 copy-start.35
  803.3 11.1 copy-start.39
  814.5 4.1 copy-start.49
  814.5 4.1 copy-start.42
  818.6 2.7 copy-start.7
  818.6 2.7 copy-start.28
  818.6 6.6 copy-start.46
  821.2 4.2 copy-start.11
  821.3 265.8 %reduce-scatter.11.cloned.1.call-start = ((), (), s32[]{:S(2)}) async-start(), calls=%async_computation.14 | async-start | bytes 2162688 | tf_op jit(solution)/shard_map/reduce_scatter | solution.py:246
  825.2 627.2 %reduce-scatter.9.cloned.1.call-start = ((), (), s32[]{:S(2)}) async-start(), calls=%async_computation.13 | async-start | bytes 17301504 | tf_op jit(solution)/shard_map/reduce_scatter | solution.py:245
  835.3 982.3 %reduce-scatter.13.cloned.1.call-start = ((), (), s32[]{:S(2)}) async-start(), calls=%async_computation.15 | async-start | bytes 17301504 | tf_op jit(solution)/shard_map/reduce_scatter | solution.py:247
  847.5 2381.6 %reduce-scatter.15.cloned.1.call-start = ((), (), s32[]{:S(2)}) async-start(), calls=%async_computation.16 | async-start | bytes 69206016 | tf_op jit(solution)/shard_map/reduce_scatter | solution.py:170
  880.3 3762.5 %reduce-scatter.17.cloned.1.call-start = ((), (), s32[]{:S(2)}) async-start(), calls=%async_computation.17 | async-start | bytes 69206016 | tf_op jit(solution)/shard_map/reduce_scatter | solution.py:171
  914.9 28.2 copy-start.52
  914.9 28.2 copy-start.4
  914.9 28.2 copy-start.8
  914.9 28.2 copy-start.10
  914.9 28.2 copy-start.36
  914.9 28.2 copy-start.40
  914.9 28.2 copy-start.43
  914.9 28.2 copy-start.47
  (9 other events, 11.2 us)
Sparse Core Ops, SparseCore 0:
  11.0 56.5 all-gather.9
  71.0 27.2 all-gather.11
  101.2 76.9 all-gather.7
  181.0 75.9 all-gather.13
  259.8 193.3 all-gather.15
  456.0 192.9 all-gather.17
  787.4 25.3 reduce-scatter.6
  821.4 123.7 all-reduce.21
  948.0 139.0 reduce-scatter.10
  1089.9 362.5 reduce-scatter.8
  1455.4 362.1 reduce-scatter.12
  1820.5 1408.5 reduce-scatter.14
  3232.2 1410.5 reduce-scatter.16
where the time goes:
time: 4660 us; the launch traced here: 4650 us
  waiting for transfers between devices  4090 us (88%)
  matrix products  331 us (7%)
  blocking collectives  110 us (2%)
  other arithmetic  66.8 us (1%)
    reduce_scatter x1, waiting for transfers between devices, local(): lax.psum_scatter(grad_members[1], ('dp', 'fsdp'), scatter_dimension=0, ti...  1410 us
    reduce_scatter x1, waiting for transfers between devices, local(): lax.psum_scatter(grad_members[0], ('dp', 'fsdp'), scatter_dimension=0, ti...  1410 us
    reduce_scatter x1, waiting for transfers between devices, local(): lax.psum_scatter(grad_wq, ('dp', 'fsdp'), scatter_dimension=0, tiled=True)  365 us
    reduce_scatter x1, waiting for transfers between devices, local(): lax.psum_scatter(grad_wo, ('dp', 'fsdp'), scatter_dimension=0, tiled=True)  365 us
    all_gather x1, waiting for transfers between devices, feed_params(): lax.all_gather(members[0], ('dp', 'fsdp'), axis=0, tiled=True)  186 us
    all_gather x1, waiting for transfers between devices, feed_params(): lax.all_gather(members[1], ('dp', 'fsdp'), axis=0, tiled=True)  167 us
    reduce_scatter x1, waiting for transfers between devices, local(): lax.psum_scatter(grad_wkv, ('dp', 'fsdp'), scatter_dimension=0, tiled=True)  130 us
  transfers between devices with their start and end apart: 13, of which 11 were waited for; matrix products, arithmetic and copies ran while one was open for 6% of the time, Pallas kernels for 0%

commit v1 on v0

v1 whole, which is shorter than its diff:
```python
import math

import jax
import jax.numpy as jnp
from jax import lax
from jax.sharding import PartitionSpec as P

HEADS = 16
HD = 128
EPS = 1e-05
F32 = jnp.float32
BF16 = jnp.bfloat16
BOTH = ("dp", "fsdp")


def norm_stats(values):
    average = jnp.mean(values, axis=-1, keepdims=True)
    centered = values - average
    variance = jnp.mean(centered * centered, axis=-1, keepdims=True)
    recip = lax.rsqrt(variance + EPS)
    return average, recip


def norm_pull(grad, xhat, recip, gain):
    scaled = grad * gain
    mean_one = jnp.mean(scaled, axis=-1, keepdims=True)
    mean_two = jnp.mean(scaled * xhat, axis=-1, keepdims=True)
    return recip * (scaled - mean_one - xhat * mean_two)


def gelu_tanh(values):
    return jax.nn.gelu(values, approximate=True)


def dot_nn(left, right):
    return jnp.dot(left, right, preferred_element_type=F32)


def dot_nt(left, right):
    return lax.dot_general(left, right, (((1,), (1,)), ((), ())), preferred_element_type=F32)


def dot_tn(left, right):
    return lax.dot_general(left, right, (((0,), (0,)), ((), ())), preferred_element_type=F32)


def gather_both(block):
    return lax.all_gather(
        lax.all_gather(block, "fsdp", axis=0, tiled=True), "dp", axis=0, tiled=True
    )


def scatter_both(block):
    part = lax.psum_scatter(block, "dp", scatter_dimension=0, tiled=True)
    return lax.psum_scatter(part, "fsdp", scatter_dimension=0, tiled=True)


def ring_steps(count):
    return [(i, (i + 1) % count) for i in range(count)]


def ring_gather(block, count):
    me = lax.axis_index("fsdp")
    whole = jnp.zeros((count,) + block.shape, block.dtype)
    held = block
    for step in range(count):
        whole = lax.dynamic_update_index_in_dim(whole, held, lax.rem(me - step + count, count), 0)
        if step + 1 < count:
            held = lax.ppermute(held, "fsdp", ring_steps(count))
    return whole


def ring_scatter(terms, count):
    me = lax.axis_index("fsdp")

    def term(step):
        return lax.dynamic_index_in_dim(
            terms, lax.rem(me - 1 - step + 2 * count, count), 0, keepdims=False
        ).astype(F32)

    total = term(0)
    for step in range(1, count):
        total = lax.ppermute(total.astype(BF16), "fsdp", ring_steps(count)).astype(F32) + term(step)
    return total


def masked_scores(query_block, kv_rows, allowed_block, root_hd):
    scores = dot_nt(query_block, kv_rows[:, :HD]) / root_hd
    scores = scores.reshape(HEADS, -1, kv_rows.shape[0])
    return jnp.where(allowed_block[None], scores, -1e30)


def make_local(n_dp, n_z):
    n_dev = n_dp * n_z

    def local(
        tokens,
        cotangent,
        lengths,
        query_weight,
        kv_weight,
        out_weight,
        query_bias,
        value_bias,
        out_bias,
        attn_gain,
        attn_shift,
        up_weight,
        down_weight,
        up_bias,
        down_bias,
        mlp_gain,
        mlp_shift,
    ):
        windows, local_len, width = tokens.shape
        win = local_len * n_z
        rows = windows * local_len
        root_hd = math.sqrt(HD)
        own = query_weight.shape[0]
        ff_own = up_weight.shape[1] // n_dp

        small = (
            query_bias,
            value_bias,
            out_bias,
            attn_gain,
            attn_shift,
            up_bias,
            down_bias,
            mlp_gain,
            mlp_shift,
        )
        sizes = [v.shape[0] for v in small]
        starts = [sum(sizes[:i]) for i in range(len(sizes))]
        small_row = jnp.concatenate(small)
        kv_lines = kv_weight.size // width
        small_lines = -(-small_row.shape[0] // width)
        filled = own + kv_lines + small_lines
        lines = -(-filled // 16) * 16
        small_row = jnp.pad(small_row, (0, (lines - own - kv_lines) * width - small_row.shape[0]))
        packed = jnp.concatenate(
            [query_weight, kv_weight.reshape(kv_lines, width), small_row.reshape(-1, width)]
        )
        packed = gather_both(packed).reshape(n_dev, lines, width)
        full_q = packed[:, :own].reshape(width, width)
        full_kv = packed[:, own : own + kv_lines].reshape(width, 2 * HD)
        small_all = packed[:, own + kv_lines :].reshape(n_dev, -1)
        bias_q, bias_v, bias_o, gain_one, shift_one, bias_up, bias_down, gain_two, shift_two = (
            small_all[:, start : start + size].reshape(-1).astype(F32)
            for start, size in zip(starts, sizes)
        )
        full_o = gather_both(out_weight)
        grad_low = cotangent.reshape(rows, width)
        grad_all = lax.all_gather(grad_low, "dp", axis=0, tiled=True)

        up_cols = lax.all_to_all(up_weight, "dp", 1, 0, tiled=True).reshape(n_dp, own, ff_own)
        up_part = ring_gather(up_cols, n_z).transpose(1, 0, 2, 3).reshape(width, ff_own)
        down_part = ring_gather(down_weight, n_z).reshape(ff_own, width)
        bias_up_part = lax.dynamic_slice_in_dim(bias_up, lax.axis_index("dp") * ff_own, ff_own)

        query_pos = lax.axis_index("fsdp") * local_len + jnp.arange(local_len, dtype=jnp.int32)
        key_pos = jnp.arange(win, dtype=jnp.int32)
        file_count = lengths.shape[1]
        upto = jnp.arange(file_count)[:, None] <= jnp.arange(file_count)[None, :]
        file_ends = jnp.sum(jnp.where(upto[None], lengths[:, :, None], 0), axis=1)
        key_files = jnp.sum(
            (file_ends[:, None, :] <= key_pos[None, :, None]).astype(jnp.int32), axis=2
        )
        query_files = jnp.sum(
            (file_ends[:, None, :] <= query_pos[None, :, None]).astype(jnp.int32), axis=2
        )
        allowed = (query_files[:, :, None] == key_files[:, None, :]) & (
            key_pos[None, None, :] <= query_pos[None, :, None]
        )

        inputs = tokens.reshape(rows, width).astype(F32)
        mean_one, recip_one = norm_stats(inputs)
        xhat_one = (inputs - mean_one) * recip_one
        normed_one = (xhat_one * gain_one + shift_one).astype(BF16)
        queries = (dot_nn(normed_one, full_q) + bias_q).astype(BF16)
        kv_bias = jnp.concatenate([jnp.zeros((HD,), F32), bias_v])
        key_value = (dot_nn(normed_one, full_kv) + kv_bias).astype(BF16)
        kv_window = lax.all_gather(
            key_value.reshape(windows, local_len, 2 * HD), "fsdp", axis=1, tiled=True
        )
        query_rows = (
            queries.reshape(windows, local_len, HEADS, HD)
            .transpose(0, 2, 1, 3)
            .reshape(windows, HEADS * local_len, HD)
        )
        mixed_list = []
        norm_list = []
        for w in range(windows):
            scores = masked_scores(query_rows[w], kv_window[w], allowed[w], root_hd)
            row_max = jnp.max(scores, axis=2, keepdims=True)
            exp_terms = jnp.exp(scores - row_max)
            row_total = jnp.sum(exp_terms, axis=2, keepdims=True)
            prob_low = (exp_terms / row_total).astype(BF16).reshape(HEADS * local_len, win)
            mixed_list.append(dot_nn(prob_low, kv_window[w][:, HD:]))
            norm_list.append(row_max + jnp.log(row_total))
        attended = jnp.stack(mixed_list).reshape(windows, HEADS, local_len, HD).transpose(0, 2, 1, 3)
        attended = attended.reshape(rows, width).astype(BF16)
        middle = inputs + dot_nn(attended, full_o) + bias_o

        mean_two, recip_two = norm_stats(middle)
        xhat_two = (middle - mean_two) * recip_two
        normed_two = (xhat_two * gain_two + shift_two).astype(BF16)
        two_all = lax.all_gather(normed_two, "dp", axis=0, tiled=True)
        grad_hidden = dot_nt(grad_all, down_part)
        pre_act = dot_nn(two_all, up_part) + bias_up_part
        hidden_full, gelu_pull = jax.vjp(gelu_tanh, pre_act)
        hidden = hidden_full.astype(BF16)
        pre_grad = gelu_pull(grad_hidden)[0].astype(BF16)
        two_grad = lax.psum_scatter(
            dot_nt(pre_grad, up_part).astype(BF16), "dp", scatter_dimension=0, tiled=True
        ).astype(F32)
        branch_out = lax.psum_scatter(
            dot_nn(hidden, down_part).astype(BF16), "dp", scatter_dimension=0, tiled=True
        ).astype(F32)
        output = (middle + branch_out + bias_down).astype(BF16)
        output = output.reshape(windows, local_len, width)

        up_terms = dot_tn(two_all, pre_grad).reshape(n_dp, n_z, own, ff_own).transpose(1, 0, 2, 3)
        grad_up = ring_scatter(up_terms, n_z)
        grad_up = lax.all_to_all(
            grad_up.astype(BF16).reshape(n_dp * own, ff_own), "dp", 0, 1, tiled=True
        ).astype(F32)
        down_terms = dot_tn(hidden, grad_all).reshape(n_z, ff_own // n_z, width)
        grad_down = ring_scatter(down_terms, n_z)
        up_bias_part = jnp.sum(pre_grad.astype(F32), axis=0)

        grad_out = grad_low.astype(F32)
        grad_bdown = jnp.sum(grad_out, axis=0)
        grad_gain_two = jnp.sum(two_grad * xhat_two, axis=0)
        grad_shift_two = jnp.sum(two_grad, axis=0)
        middle_grad = grad_out + norm_pull(two_grad, xhat_two, recip_two, gain_two)
        grad_bo = jnp.sum(middle_grad, axis=0)
        branch_grad = middle_grad.astype(BF16)
        grad_wo = scatter_both(dot_tn(attended, branch_grad).astype(BF16)).astype(F32)
        attended_grad = dot_nt(branch_grad, full_o).astype(BF16)
        grad_heads = (
            attended_grad.reshape(windows, local_len, HEADS, HD)
            .transpose(0, 2, 1, 3)
            .reshape(windows, HEADS * local_len, HD)
        )
        query_list = []
        kv_terms = []
        for w in range(windows):
            kv_rows = kv_window[w]
            scores = masked_scores(query_rows[w], kv_rows, allowed[w], root_hd)
            prob_full = jnp.exp(scores - norm_list[w])
            prob_low = prob_full.astype(BF16).reshape(HEADS * local_len, win)
            grad_probs = dot_nt(grad_heads[w], kv_rows[:, HD:])
            grad_probs = grad_probs.reshape(HEADS, local_len, win)
            row_delta = jnp.sum(prob_full * grad_probs, axis=2, keepdims=True)
            score_grad = (
                (prob_full * (grad_probs - row_delta)).astype(BF16).reshape(HEADS * local_len, win)
            )
            query_list.append(dot_nn(score_grad, kv_rows[:, :HD]) / root_hd)
            key_term = dot_tn(score_grad, query_rows[w]) / root_hd
            value_term = dot_tn(prob_low, grad_heads[w])
            kv_terms.append(jnp.concatenate([key_term, value_term], axis=1))
        query_grad = jnp.stack(query_list).reshape(windows, HEADS, local_len, HD)
        query_grad = query_grad.transpose(0, 2, 1, 3).reshape(rows, width).astype(BF16)
        kv_grad = lax.psum_scatter(
            jnp.stack(kv_terms).astype(BF16), "fsdp", scatter_dimension=1, tiled=True
        ).reshape(rows, 2 * HD)
        grad_bq = jnp.sum(query_grad.astype(F32), axis=0)
        grad_bv = jnp.sum(kv_grad[:, HD:].astype(F32), axis=0)
        grad_wq = dot_tn(normed_one, query_grad)
        grad_wkv = dot_tn(normed_one, kv_grad)
        one_grad = dot_nt(query_grad, full_q) + dot_nt(kv_grad, full_kv)
        grad_gain_one = jnp.sum(one_grad * xhat_one, axis=0)
        grad_shift_one = jnp.sum(one_grad, axis=0)
        tokens_grad = middle_grad + norm_pull(one_grad, xhat_one, recip_one, gain_one)
        tokens_grad = tokens_grad.astype(BF16).reshape(windows, local_len, width)

        grad_bup = lax.dynamic_update_slice_in_dim(
            jnp.zeros((n_dp * ff_own,), F32), up_bias_part, lax.axis_index("dp") * ff_own, 0
        )
        sums = (
            grad_bq,
            grad_bv,
            grad_bo,
            grad_gain_one,
            grad_shift_one,
            grad_bup,
            grad_bdown,
            grad_gain_two,
            grad_shift_two,
        )
        sum_rows = jnp.concatenate([v.astype(BF16).reshape(n_dev, -1) for v in sums], axis=1)
        sum_rows = jnp.pad(sum_rows, ((0, 0), (0, (lines - own - kv_lines) * width - sum_rows.shape[1])))
        grads = jnp.concatenate(
            [
                grad_wq.astype(BF16).reshape(n_dev, own, width),
                grad_wkv.astype(BF16).reshape(n_dev, kv_lines, width),
                sum_rows.reshape(n_dev, -1, width),
            ],
            axis=1,
        )
        mine = scatter_both(grads.reshape(n_dev * lines, width)).astype(F32)
        grad_q = mine[:own]
        grad_kv = mine[own : own + kv_lines].reshape(own, 2 * HD)
        flat = mine[own + kv_lines :].reshape(-1)
        bq, bv, bo, gain1, shift1, bup, bdown, gain2, shift2 = (
            flat[start : start + size] for start, size in zip(starts, sizes)
        )
        return (
            output,
            tokens_grad,
            grad_q,
            grad_kv,
            grad_wo,
            bq,
            bv,
            bo,
            gain1,
            shift1,
            grad_up,
            grad_down,
            bup,
            bdown,
            gain2,
            shift2,
        )

    return local


def solution(mesh):
    whole = P(BOTH, None)
    vector = P(BOTH)
    rows = P("dp", "fsdp", None)
    return jax.shard_map(
        make_local(mesh.shape["dp"], mesh.shape["fsdp"]),
        mesh=mesh,
        in_specs=(rows, rows, P("dp", None), whole, whole, whole)
        + (vector,) * 5
        + (whole, whole)
        + (vector,) * 4,
        out_specs=(rows, rows, whole, whole, whole)
        + (vector,) * 5
        + (whole, whole)
        + (vector,) * 4,
        check_vma=False,
    )
```

time: 4660 us -> 1130 us (0.24)
  waiting for transfers between devices: 4090 us -> 596 us
  blocking collectives: 110 us -> 0 us
    reduce_scatter x6 -> x7, waiting for transfers between devices: 3690 us -> 203 us  [the longest x1 115 us: local(): lax.psum_scatter(dot_nn(hidden, down_part).astype(BF16), 'dp', scatter_di...]
    all_gather x5 -> x6, waiting for transfers between devices: 394 us -> 133 us  [the longest x2 59.5 us: gather_both(): lax.all_gather(lax.all_gather(block, 'fsdp', axis=0, tiled=True), 'dp', a...]
    ppermute x0 -> x12, waiting for transfers between devices: none -> 231 us  [the longest x6 131 us: ring_scatter(): lax.ppermute(total.astype(BF16), 'fsdp', ring_steps(count)).astype(F32)]
    all_gather x1 -> x0, blocking collectives: 67.3 us -> none  [feed_params(): lax.all_gather(members[2], ('dp', 'fsdp'), axis=0, tiled=True)]
  transfers between devices with their start and end apart: 13 -> 28, of which waited for: 11 -> 19; matrix products, arithmetic and copies ran while one was open for 6% -> 28% of each run, Pallas kernels for 0% -> 0%
where the time goes in v1:
time: 1130 us; the launch traced here: 1120 us
  waiting for transfers between devices  596 us (53%)
  matrix products  310 us (27%)
  other arithmetic  102 us (9%)
  local copies, waits for them, and re-layouts  81.8 us (7%)
  starting transfers between devices  16.9 us (1%)
  between operations  15.2 us (1%)
    ppermute x6, waiting for transfers between devices, ring_scatter(): lax.ppermute(total.astype(BF16), 'fsdp', ring_steps(count)).astype(F32)  131 us
    reduce_scatter x1, waiting for transfers between devices, local(): lax.psum_scatter(dot_nn(hidden, down_part).astype(BF16), 'dp', scatter_di...  115 us
    ppermute x6, waiting for transfers between devices, ring_gather(): held = lax.ppermute(held, 'fsdp', ring_steps(count))  100 us
    dot_general x7, matrix products, dot_nt(): lax.dot_general(left, right, (((1,), (1,)), ((), ())), preferred_element_...  92.2 us
    reduce_scatter x1, waiting for transfers between devices, local(): lax.psum_scatter(dot_nt(pre_grad, up_part).astype(BF16), 'dp', scatter_di...  88.4 us
    dot_general x9, matrix products, dot_tn(): lax.dot_general(left, right, (((0,), (0,)), ((), ())), preferred_element_...  88.4 us
    dot_general x9, matrix products, dot_nn(): return jnp.dot(left, right, preferred_element_type=F32)  87.8 us
    all_gather x2, waiting for transfers between devices, gather_both(): lax.all_gather(lax.all_gather(block, 'fsdp', axis=0, tiled=True), 'dp', a...  59.5 us
  transfers between devices with their start and end apart: 28, of which 19 were waited for; matrix products, arithmetic and copies ran while one was open for 28% of the time, Pallas kernels for 0%

profile of v1, /device:TPU:0, one launch (start us, length us, event | category | flops | bytes accessed | tf_op | source)
XLA Modules:
  0.0 1122.7 jit_solution(4052846155514394308)
XLA Ops:
  7.2 6.2 concatenate.29
  16.1 35.5 %all-gather.8.cloned.1.call-done = bf16[320,2048]{1,0:T(8,128)(2,1)} async-done(((bf16[80,2048]{1,0:T(8,128)(2,1)}), bf16[320,2048]{1,0:T(8,128)(2,1)}) %all-gather.8.cloned.1.call-update) | async-done | bytes 1310736 | tf_op jit(solution)/shard_map/all_gather | solution.py:49
  56.2 59.5 %all-gather.10.cloned.1.call-done = bf16[2560,2048]{1,0:T(8,128)(2,1)} async-done(((bf16[320,2048]{1,0:T(8,128)(2,1)}), bf16[2560,2048]{1,0:T(8,128)(2,1)}) %all-gather.10.cloned.1.call-update) | async-done | bytes 10485776 | tf_op jit(solution)/shard_map/all_gather | solution.py:48
  124.9 20.3 %all-gather.14.cloned.1.call-done = bf16[256,2048]{1,0:T(8,128)(2,1)} async-done(((bf16[64,2048]{1,0:T(8,128)(2,1)}), bf16[256,2048]{1,0:T(8,128)(2,1)}) %all-gather.14.cloned.1.call-update) | async-done | bytes 1048592 | tf_op jit(solution)/shard_map/all_gather | solution.py:49
  146.9 8.5 slice.174
  155.5 8.5 fusion.75
  166.8 3.1 fusion.136
  169.9 4.8 all-gather.12.cloned.1.call-done
  176.0 4.6 fusion.14
  180.6 5.2 fusion.20
  187.5 3.0 fusion.15
  190.5 5.0 fusion.21
  196.2 28.5 %exponential_convert_fusion = (bf16[4096,1024]{1,0:T(8,128)(2,1)}, bf16[4096,1024]{1,0:T(8,128)(2,1)}, bf16[4096,1024]{1,0:T(8,128)(2,1)}, bf16[4096,1024]{1,0:T(8,128)(2,1)}) fusion(f32[4096,1024]{1,0:T(8,128)} %copy-done.1, f32[4096]{0:T(1024)S(1)} %log_add_fusion, pred[256,1024]{1,0:T(8,128)(4,1)S(1)} %get-tuple-element.46, f32[4096]{0:T(1024)S(1)} %fusion.21, ...), kind=kLoop, calls=%fused_computation.17 | loop fusion | flops 50331648 | bytes 67731456 | tf_op jit(solution)/shard_map/convert_element_type | solution.py:252
  224.8 5.9 convolution_convert_fusion.5
  236.0 7.8 fusion.138
  249.7 3.7 all-to-all-start
  254.9 23.0 %all-to-all-done = bf16[64,8,1024]{2,0,1:T(8,128)(2,1)S(1)} async-done(((bf16[64,8,1024]{2,0,1:T(8,128)(2,1)}), bf16[64,8,1024]{2,0,1:T(8,128)(2,1)S(1)}, u32[]{:S(2)}, u32[]{:S(2)}) %all-to-all-start) | async-done | bytes 1048608 | tf_op jit(solution)/shard_map/all_to_all | solution.py:156
  281.4 2.5 broadcast_in_dim.144
  285.0 20.8 %collective-permute-done = bf16[8,64,1024]{2,1,0:T(8,128)(2,1)S(1)} collective-permute-done((bf16[8,64,1024]{2,1,0:T(8,128)(2,1)S(1)}, bf16[8,64,1024]{2,1,0:T(8,128)(2,1)S(1)}, u32[]{:S(2)}, u32[]{:S(2)}) %collective-permute-start) | collective-permute-done | bytes 1048608 | tf_op jit(solution)/shard_map/ppermute | solution.py:69
  305.8 2.5 broadcast_in_dim.139
  311.7 16.5 %collective-permute-done.4 = bf16[256,2048]{1,0:T(8,128)(2,1)S(1)} collective-permute-done((bf16[256,2048]{1,0:T(8,128)(2,1)}, bf16[256,2048]{1,0:T(8,128)(2,1)S(1)}, u32[]{:S(2)}, u32[]{:S(2)}) %collective-permute-start.4) | collective-permute-done | bytes 1048608 | tf_op jit(solution)/shard_map/ppermute | solution.py:69
  329.3 21.4 %collective-permute-done.1 = bf16[8,64,1024]{2,1,0:T(8,128)(2,1)S(1)} collective-permute-done((bf16[8,64,1024]{2,1,0:T(8,128)(2,1)S(1)}, bf16[8,64,1024]{2,1,0:T(8,128)(2,1)S(1)}, u32[]{:S(2)}, u32[]{:S(2)}) %collective-permute-start.1) | collective-permute-done | bytes 1048608 | tf_op jit(solution)/shard_map/ppermute | solution.py:69
  352.9 20.3 %collective-permute-done.5 = bf16[256,2048]{1,0:T(8,128)(2,1)S(1)} collective-permute-done((bf16[256,2048]{1,0:T(8,128)(2,1)S(1)}, bf16[256,2048]{1,0:T(8,128)(2,1)S(1)}, u32[]{:S(2)}, u32[]{:S(2)}) %collective-permute-start.5) | collective-permute-done | bytes 1048608 | tf_op jit(solution)/shard_map/ppermute | solution.py:69
  374.2 19.0 %collective-permute-done.2 = bf16[8,64,1024]{2,1,0:T(8,128)(2,1)S(1)} collective-permute-done((bf16[8,64,1024]{2,1,0:T(8,128)(2,1)S(1)}, bf16[8,64,1024]{2,1,0:T(8,128)(2,1)S(1)}, u32[]{:S(2)}, u32[]{:S(2)}) %collective-permute-start.2) | collective-permute-done | bytes 1048608 | tf_op jit(solution)/shard_map/ppermute | solution.py:69
  395.2 23.5 %fusion.139 = f32[4096,1024]{1,0:T(8,128)} fusion(bf16[4096,2048]{1,0:T(8,128)(2,1)} %all-gather.18.cloned.1.call-done, bf16[2048,1024]{1,0:T(8,128)(2,1)} %bitcast.26), kind=kOutput, calls=%fused_computation.223 | convolution fusion | flops 17179869184 | bytes 37748736 | tf_op jit(solution)/shard_map/dot_general | solution.py:36
  418.7 17.2 %all-gather.20.cloned.1.call-done = bf16[4096,2048]{1,0:T(8,128)(2,1)} async-done(((bf16[512,2048]{1,0:T(8,128)(2,1)}), bf16[4096,2048]{1,0:T(8,128)(2,1)}) %all-gather.20.cloned.1.call-update) | async-done | bytes 16777232 | tf_op jit(solution)/shard_map/all_gather | solution.py:154
  435.8 35.4 %convert_reduce_fusion = (bf16[1024]{0:T(1024)(128)(2,1)}, bf16[4096,1024]{1,0:T(8,128)(2,1)S(1)}) fusion(f32[4096,1024]{1,0:T(8,128)} %fusion.139, f32[1024]{0:T(1024)S(1)} %dynamic_slice.21, bf16[1024,2048]{1,0:T(8,128)(2,1)} %bitcast.31, bf16[4096,2048]{1,0:T(8,128)(2,1)} %all-gather.20.cloned.1.call-done), kind=kOutput, calls=%fused_computation.16 | convolution fusion | flops 17276338176 | bytes 46143488 | tf_op jit(solution)/shard_map/dot_general | solution.py:40
  471.3 3.3 copy-done.51
  474.5 22.5 %convolution_convert_fusion = bf16[4096,2048]{1,0:T(8,128)(2,1)} fusion(bf16[4096,1024]{1,0:T(8,128)(2,1)S(1)} %get-tuple-element.66, bf16[2048,1024]{1,0:T(8,128)(2,1)} %bitcast.26), kind=kOutput, calls=%fused_computation.34 | convolution fusion | flops 17188257792 | bytes 29360128 | tf_op jit(solution)/shard_map/dot_general | solution.py:40
  497.2 26.8 %convolution_convert_fusion.1 = bf16[4096,2048]{1,0:T(8,128)(2,1)} fusion(bf16[1024,2048]{1,0:T(8,128)(2,1)} %bitcast.31, f32[4096,1024]{1,0:T(8,128)} %fusion.139, f32[1024]{0:T(1024)S(1)} %dynamic_slice.21), kind=kOutput, calls=%fused_computation.35 | convolution fusion | flops 17230200832 | bytes 37752832 | tf_op jit(solution)/shard_map/dot_general | solution.py:36
  524.8 88.4 %reduce-scatter.10.cloned.1.call-done = bf16[512,2048]{1,0:T(8,128)(2,1)} async-done(((bf16[4096,2048]{1,0:T(8,128)(2,1)}), bf16[512,2048]{1,0:T(8,128)(2,1)}) %reduce-scatter.10.cloned.1.call-update) | async-done | bytes 2097168 | tf_op jit(solution)/shard_map/reduce_scatter | solution.py:214
  613.2 4.6 fusion.37
  617.8 115.0 %reduce-scatter.8.cloned.1.call-done = bf16[512,2048]{1,0:T(8,128)(2,1)} async-done(((bf16[4096,2048]{1,0:T(8,128)(2,1)}), bf16[512,2048]{1,0:T(8,128)(2,1)}) %reduce-scatter.8.cloned.1.call-update) | async-done | bytes 2097168 | tf_op jit(solution)/shard_map/reduce_scatter | solution.py:217
  732.8 5.8 fusion.132
  738.7 9.7 fusion.74
  752.5 20.8 %multiply_convert_fusion.1 = bf16[16,256,1024]{2,1,0:T(8,128)(2,1)} fusion(f32[16,256,1024]{2,1,0:T(8,128)} %bitcast.283, f32[16,256]{1,0:T(8,128)S(1)} %add.297, pred[256,1024]{1,0:T(8,128)(4,1)S(1)} %copy-done.17, bf16[1024,256]{1,0:T(8,128)(2,1)} %copy-done.26, bf16[2,16,256,128]{3,2,1,0:T(8,128)(2,1)} %bitcast.295), kind=kOutput, calls=%fused_computation.23 | convolution fusion | flops 2181043200 | bytes 45121536 | tf_op jit(solution)/shard_map/sub | solution.py:257
  773.3 5.5 fusion.77
  778.8 21.2 %multiply_convert_fusion = bf16[16,256,1024]{2,1,0:T(8,128)(2,1)} fusion(f32[16,256,1024]{2,1,0:T(8,128)} %bitcast.284, f32[16,256]{1,0:T(8,128)S(1)} %add.299, pred[256,1024]{1,0:T(8,128)(4,1)S(1)} %copy-done.15, bf16[1024,256]{1,0:T(8,128)(2,1)} %copy-done.24, bf16[2,16,256,128]{3,2,1,0:T(8,128)(2,1)} %bitcast.296), kind=kOutput, calls=%fused_computation.19 | convolution fusion | flops 2181043200 | bytes 45121536 | tf_op jit(solution)/shard_map/sub | solution.py:257
  800.0 4.9 fusion.78
  804.9 4.9 convolution_convert_fusion.8
  812.5 10.8 convolution_convert_fusion.2
  824.5 5.8 fusion.31
  831.0 5.8 fusion.32
  841.5 7.2 convolution_convert_fusion.3
  848.7 11.1 fusion.57
  859.8 3.5 fusion.55
  866.0 5.8 fusion.54
  873.9 10.1 pad_maximum_fusion
  884.1 22.7 %fusion.140 = f32[2048,1024]{1,0:T(8,128)S(1)} fusion(bf16[4096,2048]{1,0:T(8,128)(2,1)} %all-gather.18.cloned.1.call-done, bf16[4096,1024]{1,0:T(8,128)(2,1)} %copy-done.51), kind=kOutput, calls=%fused_computation.224 | convolution fusion | flops 17179869184 | bytes 33554432 | tf_op jit(solution)/shard_map/dot_general | solution.py:44
  907.0 3.1 copy-done.13
  911.0 27.6 %fusion.131 = f32[1024,2048]{1,0:T(8,128)S(1)} fusion(bf16[4096,2048]{1,0:T(8,128)(2,1)} %all-gather.20.cloned.1.call-done, f32[4096,1024]{1,0:T(8,128)} %fusion.139, f32[1024]{0:T(1024)S(1)} %dynamic_slice.21), kind=kOutput, calls=%fused_computation.216 | convolution fusion | flops 17221812224 | bytes 41947136 | tf_op jit(solution)/shard_map/dot_general | solution.py:44
  938.6 3.3 copy-done.12
  948.4 22.8 %collective-permute-done.9 = bf16[256,2048]{1,0:T(8,128)(2,1)} collective-permute-done((bf16[256,2048]{1,0:T(8,128)(2,1)}, bf16[256,2048]{1,0:T(8,128)(2,1)}, u32[]{:S(2)}, u32[]{:S(2)}) %collective-permute-start.9) | collective-permute-done | bytes 1048608 | tf_op jit(solution)/shard_map/ppermute | solution.py:83
  971.2 3.2 fusion.62
  974.4 19.3 %collective-permute-done.7 = bf16[8,64,1024]{2,1,0:T(8,128)(2,1)} collective-permute-done((bf16[8,64,1024]{2,1,0:T(8,128)(2,1)S(1)}, bf16[8,64,1024]{2,1,0:T(8,128)(2,1)}, u32[]{:S(2)}, u32[]{:S(2)}) %collective-permute-start.7) | collective-permute-done | bytes 1048608 | tf_op jit(solution)/shard_map/ppermute | solution.py:83
  993.6 3.3 fusion.64
  996.9 24.5 %collective-permute-done.10 = bf16[256,2048]{1,0:T(8,128)(2,1)} collective-permute-done((bf16[256,2048]{1,0:T(8,128)(2,1)}, bf16[256,2048]{1,0:T(8,128)(2,1)}, u32[]{:S(2)}, u32[]{:S(2)}) %collective-permute-start.10) | collective-permute-done | bytes 1048608 | tf_op jit(solution)/shard_map/ppermute | solution.py:83
  1021.4 3.1 fusion.61
  1026.5 29.0 %collective-permute-done.8 = bf16[8,64,1024]{2,1,0:T(8,128)(2,1)S(1)} collective-permute-done((bf16[8,64,1024]{2,1,0:T(8,128)(2,1)}, bf16[8,64,1024]{2,1,0:T(8,128)(2,1)S(1)}, u32[]{:S(2)}, u32[]{:S(2)}) %collective-permute-start.8) | collective-permute-done | bytes 1048608 | tf_op jit(solution)/shard_map/ppermute | solution.py:83
  1055.5 2.9 fusion.63
  1058.4 3.6 all-to-all-start.1
  1062.0 35.2 %collective-permute-done.11 = bf16[256,2048]{1,0:T(8,128)(2,1)} collective-permute-done((bf16[256,2048]{1,0:T(8,128)(2,1)}, bf16[256,2048]{1,0:T(8,128)(2,1)}, u32[]{:S(2)}, u32[]{:S(2)}) %collective-permute-start.11) | collective-permute-done | bytes 1048608 | tf_op jit(solution)/shard_map/ppermute | solution.py:83
  1097.2 3.6 bitcast_add_fusion.1
  1103.7 4.3 fusion.53
  (266 shorter events, 90.3 us)
Async XLA Ops:
  7.2 47.7 %copy-start.3 = (bf16[2,256,2048]{2,1,0:T(8,128)(2,1)S(1)}, bf16[2,256,2048]{2,1,0:T(8,128)(2,1)}, u32[]{:S(2)}) copy-start(bf16[2,256,2048]{2,1,0:T(8,128)(2,1)} %param.17) | copy-start | bytes 6291460
  7.2 44.4 %all-gather.8.cloned.1.call-start = ((), (), s32[]{:S(2)}) async-start(), calls=%async_computation.9 | async-start | bytes 1638400 | tf_op jit(solution)/shard_map/all_gather | solution.py:49
  16.0 99.7 %all-gather.10.cloned.1.call-start = ((), (), s32[]{:S(2)}) async-start(), calls=%async_computation.10 | async-start | bytes 11796480 | tf_op jit(solution)/shard_map/all_gather | solution.py:48
  51.6 93.7 %all-gather.14.cloned.1.call-start = ((), (), s32[]{:S(2)}) async-start(), calls=%async_computation.12 | async-start | bytes 1310720 | tf_op jit(solution)/shard_map/all_gather | solution.py:49
  52.3 122.4 %all-gather.12.cloned.1.call-start = ((), (), s32[]{:S(2)}) async-start(), calls=%async_computation.11 | async-start | bytes 1310720 | tf_op jit(solution)/shard_map/all_gather | solution.py:183
  119.8 5.1 copy-start.40
  121.3 24.6 %copy-start.50 = (s32[2,8]{1,0:T(2,128)S(1)}, s32[2,8]{1,0:T(2,128)}, u32[]{:S(2)}) copy-start(s32[2,8]{1,0:T(2,128)} %param.19) | copy-start | bytes 196
  124.9 111.1 %all-gather.16.cloned.1.call-start = ((), (), s32[]{:S(2)}) async-start(), calls=%async_computation.13 | async-start | bytes 9437184 | tf_op jit(solution)/shard_map/all_gather | solution.py:48
  145.3 249.9 %all-gather.18.cloned.1.call-start = ((), (), s32[]{:S(2)}) async-start(), calls=%async_computation.14 | async-start | bytes 18874368 | tf_op jit(solution)/shard_map/all_gather | solution.py:208
  146.9 49.3 %copy-start.14 = (pred[256,1024]{1,0:T(8,128)(4,1)}, pred[256,1024]{1,0:T(8,128)(4,1)S(1)}, u32[]{:S(2)}) copy-start(pred[256,1024]{1,0:T(8,128)(4,1)S(1)} %get-tuple-element.46) | copy-start | bytes 786436
  146.9 49.3 %copy-start.16 = (pred[256,1024]{1,0:T(8,128)(4,1)}, pred[256,1024]{1,0:T(8,128)(4,1)S(1)}, u32[]{:S(2)}) copy-start(pred[256,1024]{1,0:T(8,128)(4,1)S(1)} %get-tuple-element.45) | copy-start | bytes 786436
  166.7 77.7 %copy-start.38 = (f32[2048]{0:T(1024)}, f32[2048]{0:T(1024)S(1)}, u32[]{:S(2)}) copy-start(f32[2048]{0:T(1024)S(1)} %reshape.560) | copy-start | bytes 24580
  176.0 48.8 %copy-start.26 = (bf16[1024,256]{1,0:T(8,128)(2,1)}, bf16[1024,256]{1,0:T(8,128)(2,1)S(1)}, u32[]{:S(2)}) copy-start(bf16[1024,256]{1,0:T(8,128)(2,1)S(1)} %get-tuple-element.43) | copy-start | bytes 1572868
  176.0 55.4 %copy-start.24 = (bf16[1024,256]{1,0:T(8,128)(2,1)}, bf16[1024,256]{1,0:T(8,128)(2,1)S(1)}, u32[]{:S(2)}) copy-start(bf16[1024,256]{1,0:T(8,128)(2,1)S(1)} %get-tuple-element.44) | copy-start | bytes 1572868
  180.6 6.9 copy-start
  180.6 6.9 copy-start.18
  190.5 5.7 copy-start.1
  196.2 28.6 %copy-start.36 = (f32[4096]{0:T(1024)}, f32[4096]{0:T(1024)S(1)}, u32[]{:S(2)}) copy-start(f32[4096]{0:T(1024)S(1)} %log_add_fusion.1) | copy-start | bytes 49156
  196.2 28.6 %copy-start.34 = (f32[4096]{0:T(1024)}, f32[4096]{0:T(1024)S(1)}, u32[]{:S(2)}) copy-start(f32[4096]{0:T(1024)S(1)} %log_add_fusion) | copy-start | bytes 49156
  224.8 6.6 copy-start.10
  243.8 4.1 copy-start.43
  247.9 5.6 copy-start.28
  247.9 187.9 %all-gather.20.cloned.1.call-start = ((), (), s32[]{:S(2)}) async-start(), calls=%async_computation.16 | async-start | bytes 18874368 | tf_op jit(solution)/shard_map/all_gather | solution.py:154
  249.7 28.1 %all-to-all-start = ((bf16[64,8,1024]{2,0,1:T(8,128)(2,1)}), bf16[64,8,1024]{2,0,1:T(8,128)(2,1)S(1)}, u32[]{:S(2)}, u32[]{:S(2)}) async-start(bf16[64,8,1024]{2,0,1:T(8,128)(2,1)} %bitcast.282), calls=%async_computation | async-start | bytes 2097152 | tf_op jit(solution)/shard_map/all_to_all | solution.py:156
  253.4 359.8 %reduce-scatter.10.cloned.1.call-start = ((), (), s32[]{:S(2)}) async-start(), calls=%async_computation.17 | async-start | bytes 18874368 | tf_op jit(solution)/shard_map/reduce_scatter | solution.py:214
  253.5 27.9 %collective-permute-start.3 = (bf16[256,2048]{1,0:T(8,128)(2,1)S(1)}, bf16[256,2048]{1,0:T(8,128)(2,1)}, u32[]{:S(2)}, u32[]{:S(2)}) collective-permute-start(bf16[256,2048]{1,0:T(8,128)(2,1)S(1)} %copy-done.28), channel_id=1, source_target_pairs={{0,1},{1,2},{2,3},{3,0},{4,5},{5,6},{6,7},{7,4},{8,9},{9,10},{10,1... | collective-permute-start | bytes 3145736 | tf_op jit(solution)/shard_map/ppermute | solution.py:69
  277.9 27.9 %collective-permute-start = (bf16[8,64,1024]{2,1,0:T(8,128)(2,1)S(1)}, bf16[8,64,1024]{2,1,0:T(8,128)(2,1)S(1)}, u32[]{:S(2)}, u32[]{:S(2)}) collective-permute-start(bf16[8,64,1024]{2,1,0:T(8,128)(2,1)S(1)} %bitcast.309), channel_id=1, source_target_pairs={{0,1},{1,2},{2,3},{3,0},{4,5},{5,6},{6,7},{7,4},{8,9},{9,10},{10,1... | collective-permute-start | bytes 3145736 | tf_op jit(solution)/shard_map/ppermute | solution.py:69
  281.4 46.8 %collective-permute-start.4 = (bf16[256,2048]{1,0:T(8,128)(2,1)}, bf16[256,2048]{1,0:T(8,128)(2,1)S(1)}, u32[]{:S(2)}, u32[]{:S(2)}) collective-permute-start(bf16[256,2048]{1,0:T(8,128)(2,1)} %collective-permute-done.3), channel_id=1, source_target_pairs={{0,1},{1,2},{2,3},{3,0},{4,5},{5,6},{6,7},{7,4},{8,9},{9,10},{10,1... | collective-permute-start | bytes 3145736 | tf_op jit(solution)/shard_map/ppermute | solution.py:69
  305.8 44.9 %collective-permute-start.1 = (bf16[8,64,1024]{2,1,0:T(8,128)(2,1)S(1)}, bf16[8,64,1024]{2,1,0:T(8,128)(2,1)S(1)}, u32[]{:S(2)}, u32[]{:S(2)}) collective-permute-start(bf16[8,64,1024]{2,1,0:T(8,128)(2,1)S(1)} %collective-permute-done), channel_id=1, source_target_pairs={{0,1},{1,2},{2,3},{3,0},{4,5},{5,6},{6,7},{7,4},{8,9},{9,10},{10,1... | collective-permute-start | bytes 3145736 | tf_op jit(solution)/shard_map/ppermute | solution.py:69
  328.2 44.9 %collective-permute-start.5 = (bf16[256,2048]{1,0:T(8,128)(2,1)S(1)}, bf16[256,2048]{1,0:T(8,128)(2,1)S(1)}, u32[]{:S(2)}, u32[]{:S(2)}) collective-permute-start(bf16[256,2048]{1,0:T(8,128)(2,1)S(1)} %collective-permute-done.4), channel_id=1, source_target_pairs={{0,1},{1,2},{2,3},{3,0},{4,5},{5,6},{6,7},{7,4},{8,9},{9,10},{10,1... | collective-permute-start | bytes 3145736 | tf_op jit(solution)/shard_map/ppermute | solution.py:69
  350.7 42.5 %collective-permute-start.2 = (bf16[8,64,1024]{2,1,0:T(8,128)(2,1)S(1)}, bf16[8,64,1024]{2,1,0:T(8,128)(2,1)S(1)}, u32[]{:S(2)}, u32[]{:S(2)}) collective-permute-start(bf16[8,64,1024]{2,1,0:T(8,128)(2,1)S(1)} %collective-permute-done.1), channel_id=1, source_target_pairs={{0,1},{1,2},{2,3},{3,0},{4,5},{5,6},{6,7},{7,4},{8,9},{9,10},{10,1... | collective-permute-start | bytes 3145736 | tf_op jit(solution)/shard_map/ppermute | solution.py:69
  471.3 3.3 copy-start.51
  497.1 235.7 %reduce-scatter.8.cloned.1.call-start = ((), (), s32[]{:S(2)}) async-start(), calls=%async_computation.15 | async-start | bytes 18874368 | tf_op jit(solution)/shard_map/reduce_scatter | solution.py:217
  524.0 89.3 %copy-start.39 = (f32[2048]{0:T(1024)S(1)}, f32[2048]{0:T(1024)}, u32[]{:S(2)}) copy-start(f32[2048]{0:T(1024)} %copy-done.38) | copy-start | bytes 24580
  524.0 89.3 %copy-start.44 = (f32[512]{0:T(512)S(1)}, f32[512]{0:T(512)}, u32[]{:S(2)}) copy-start(f32[512]{0:T(512)} %copy-done.43) | copy-start | bytes 6148
  524.0 89.2 %copy-start.46 = (f32[512]{0:T(512)S(1)}, f32[512]{0:T(512)}, u32[]{:S(2)}) copy-start(f32[512]{0:T(512)} %copy-done.45) | copy-start | bytes 6148
  524.0 208.8 %copy-start.5 = (bf16[2,256,2048]{2,1,0:T(8,128)(2,1)S(1)}, bf16[2,256,2048]{2,1,0:T(8,128)(2,1)}, u32[]{:S(2)}) copy-start(bf16[2,256,2048]{2,1,0:T(8,128)(2,1)} %param.18) | copy-start | bytes 6291460
  524.0 335.8 %reduce-scatter.12.cloned.1.call-start = ((), (), s32[]{:S(2)}) async-start(), calls=%async_computation.18 | async-start | bytes 1310720 | tf_op jit(solution)/shard_map/reduce_scatter | solution.py:265
  738.7 9.7 copy-start.7
  749.1 3.4 copy-start.17
  752.5 20.8 %copy-start.20 = (bf16[1,16,256,128]{3,2,1,0:T(8,128)(2,1)S(1)}, bf16[1,16,256,128]{3,2,1,0:T(8,128)(2,1)}, u32[]{:S(2)}) copy-start(bf16[1,16,256,128]{3,2,1,0:T(8,128)(2,1)} %get-tuple-element.34) | copy-start | bytes 3145732
  773.3 5.5 copy-start.15
  778.8 21.2 %copy-start.19 = (bf16[1,16,256,128]{3,2,1,0:T(8,128)(2,1)S(1)}, bf16[1,16,256,128]{3,2,1,0:T(8,128)(2,1)}, u32[]{:S(2)}) copy-start(bf16[1,16,256,128]{3,2,1,0:T(8,128)(2,1)} %get-tuple-element.35) | copy-start | bytes 3145732
  800.0 4.9 copy-start.32
  800.0 9.9 slice-start
  804.9 5.0 copy-start.33
  804.9 5.0 slice-start.1
  804.9 5.0 copy-start.31
  812.4 135.9 %reduce-scatter.18.cloned.1.call-start = ((), (), s32[]{:S(2)}) async-start(), calls=%async_computation.21 | async-start | bytes 9437184 | tf_op jit(solution)/shard_map/reduce_scatter | solution.py:54
  823.3 203.2 %reduce-scatter.14.cloned.1.call-start = ((), (), s32[]{:S(2)}) async-start(), calls=%async_computation.19 | async-start | bytes 11796480 | tf_op jit(solution)/shard_map/reduce_scatter | solution.py:54
  824.5 6.5 copy-start.25
  859.8 6.2 copy-start.4
  859.8 6.2 copy-start.41
  884.0 224.0 %reduce-scatter.20.cloned.1.call-start = ((), (), s32[]{:S(2)}) async-start(), calls=%async_computation.22 | async-start | bytes 1310720 | tf_op jit(solution)/shard_map/reduce_scatter | solution.py:55
  906.8 3.3 copy-start.13
  910.1 34.4 %collective-permute-start.6 = (bf16[8,64,1024]{2,1,0:T(8,128)(2,1)S(1)}, bf16[8,64,1024]{2,1,0:T(8,128)(2,1)}, u32[]{:S(2)}, u32[]{:S(2)}) collective-permute-start(bf16[8,64,1024]{2,1,0:T(8,128)(2,1)S(1)} %fusion.79), channel_id=1, source_target_pairs={{0,1},{1,2},{2,3},{3,0},{4,5},{5,6},{6,7},{7,4},{8,9},{9,10},{10,1... | collective-permute-start | bytes 3145736 | tf_op jit(solution)/shard_map/ppermute | solution.py:83
  938.6 3.3 copy-start.12
  943.0 28.2 %collective-permute-start.9 = (bf16[256,2048]{1,0:T(8,128)(2,1)}, bf16[256,2048]{1,0:T(8,128)(2,1)}, u32[]{:S(2)}, u32[]{:S(2)}) collective-permute-start(bf16[256,2048]{1,0:T(8,128)(2,1)} %fusion.80), channel_id=1, source_target_pairs={{0,1},{1,2},{2,3},{3,0},{4,5},{5,6},{6,7},{7,4},{8,9},{9,10},{10,1... | collective-permute-start | bytes 3145736 | tf_op jit(solution)/shard_map/ppermute | solution.py:83
  946.7 47.0 %collective-permute-start.7 = (bf16[8,64,1024]{2,1,0:T(8,128)(2,1)S(1)}, bf16[8,64,1024]{2,1,0:T(8,128)(2,1)}, u32[]{:S(2)}, u32[]{:S(2)}) collective-permute-start(bf16[8,64,1024]{2,1,0:T(8,128)(2,1)S(1)} %fusion.65), channel_id=1, source_target_pairs={{0,1},{1,2},{2,3},{3,0},{4,5},{5,6},{6,7},{7,4},{8,9},{9,10},{10,1... | collective-permute-start | bytes 3145736 | tf_op jit(solution)/shard_map/ppermute | solution.py:83
  948.4 161.4 %reduce-scatter.16.cloned.1.call-start = ((), (), s32[]{:S(2)}) async-start(), calls=%async_computation.20 | async-start | bytes 1638400 | tf_op jit(solution)/shard_map/reduce_scatter | solution.py:55
  974.4 47.1 %collective-permute-start.10 = (bf16[256,2048]{1,0:T(8,128)(2,1)}, bf16[256,2048]{1,0:T(8,128)(2,1)}, u32[]{:S(2)}, u32[]{:S(2)}) collective-permute-start(bf16[256,2048]{1,0:T(8,128)(2,1)} %fusion.62), channel_id=1, source_target_pairs={{0,1},{1,2},{2,3},{3,0},{4,5},{5,6},{6,7},{7,4},{8,9},{9,10},{10,1... | collective-permute-start | bytes 3145736 | tf_op jit(solution)/shard_map/ppermute | solution.py:83
  996.9 58.6 %collective-permute-start.8 = (bf16[8,64,1024]{2,1,0:T(8,128)(2,1)}, bf16[8,64,1024]{2,1,0:T(8,128)(2,1)S(1)}, u32[]{:S(2)}, u32[]{:S(2)}) collective-permute-start(bf16[8,64,1024]{2,1,0:T(8,128)(2,1)} %fusion.64), channel_id=1, source_target_pairs={{0,1},{1,2},{2,3},{3,0},{4,5},{5,6},{6,7},{7,4},{8,9},{9,10},{10,1... | collective-permute-start | bytes 3145736 | tf_op jit(solution)/shard_map/ppermute | solution.py:83
  1024.6 72.6 %collective-permute-start.11 = (bf16[256,2048]{1,0:T(8,128)(2,1)}, bf16[256,2048]{1,0:T(8,128)(2,1)}, u32[]{:S(2)}, u32[]{:S(2)}) collective-permute-start(bf16[256,2048]{1,0:T(8,128)(2,1)} %fusion.61), channel_id=1, source_target_pairs={{0,1},{1,2},{2,3},{3,0},{4,5},{5,6},{6,7},{7,4},{8,9},{9,10},{10,1... | collective-permute-start | bytes 3145736 | tf_op jit(solution)/shard_map/ppermute | solution.py:83
  1058.4 42.3 %all-to-all-start.1 = ((bf16[8,64,1024]{2,1,0:T(8,128)(2,1)}), bf16[8,64,1024]{2,1,0:T(8,128)(2,1)S(1)}, u32[]{:S(2)}, u32[]{:S(2)}) async-start(bf16[8,64,1024]{2,1,0:T(8,128)(2,1)} %fusion.63), calls=%async_computation.8 | async-start | bytes 2097152 | tf_op jit(solution)/shard_map/all_to_all | solution.py:225
  (18 other events, 26.8 us)
Sparse Core Ops, SparseCore 0:
  16.1 35.3 all-gather.7
  53.4 62.2 all-gather.9
  117.3 27.9 all-gather.13
  147.3 27.4 all-gather.11
  176.5 53.8 all-gather.15
  248.0 95.9 all-gather.17
  345.9 89.8 all-gather.19
  497.2 115.9 reduce-scatter.9
  616.8 115.9 reduce-scatter.7
  812.5 27.1 reduce-scatter.11
  843.5 69.9 reduce-scatter.17
  916.9 81.5 reduce-scatter.13
  1000.8 44.5 reduce-scatter.19
  1047.6 49.9 reduce-scatter.15

commit v2 on v1

v2 whole, which is shorter than its diff:
```python
import functools
import math

import jax
import jax.numpy as jnp
from jax import lax
from jax.experimental import pallas as pl
from jax.experimental.pallas import tpu as pltpu
from jax.sharding import PartitionSpec as P

HEADS = 16
HD = 128
EPS = 1e-05
F32 = jnp.float32
BF16 = jnp.bfloat16
BOTH = ("dp", "fsdp")


def dot_nn(left, right):
    return jnp.dot(left, right, preferred_element_type=F32)


def dot_nt(left, right):
    return lax.dot_general(left, right, (((1,), (1,)), ((), ())), preferred_element_type=F32)


def dot_tn(left, right):
    return lax.dot_general(left, right, (((0,), (0,)), ((), ())), preferred_element_type=F32)


LOG2E = 1.4426950408889634


def file_of(ends_ref, w, pos):
    total = jnp.zeros(pos.shape, jnp.int32)
    for i in range(ends_ref.shape[1]):
        total += (ends_ref[w, i] <= pos).astype(jnp.int32)
    return total


def fill_mask(pos_ref, ends_ref, w, bias, key_turned, value_turned, kv_ref):
    span, win = bias.shape
    query_pos = pos_ref[0] + lax.broadcasted_iota(jnp.int32, (span, 1), 0)
    key_pos = lax.broadcasted_iota(jnp.int32, (1, win), 1)
    same = file_of(ends_ref, w, query_pos) == file_of(ends_ref, w, key_pos)
    bias[...] = jnp.where(same & (key_pos <= query_pos), 0.0, -1e30).astype(F32)
    key_turned[...] = kv_ref[0, :, :HD].astype(F32).T.astype(BF16)
    if value_turned is not None:
        value_turned[...] = kv_ref[0, :, HD:].astype(F32).T.astype(BF16)


def attn_forward_kernel(per_step, pos_ref, ends_ref, q_ref, kv_ref, out_ref, norm_ref, bias, key_turned):
    w, group = pl.program_id(0), pl.program_id(1)

    @pl.when(group == 0)
    def _():
        fill_mask(pos_ref, ends_ref, w, bias, key_turned, None, kv_ref)
        norm_ref[...] = jnp.zeros_like(norm_ref)

    values = kv_ref[0, :, HD:]
    lane = lax.broadcasted_iota(jnp.int32, norm_ref.shape, 1)
    for j in range(per_step):
        query = q_ref[:, j * HD : (j + 1) * HD]
        scores = jnp.dot(query, key_turned[...], preferred_element_type=F32)
        scores = scores * (LOG2E / math.sqrt(HD)) + bias[...]
        top = jnp.max(scores, axis=1, keepdims=True)
        terms = jnp.exp2(scores - top)
        total = jnp.sum(terms, axis=1, keepdims=True)
        mixed = jnp.dot(terms.astype(BF16), values, preferred_element_type=F32)
        out_ref[:, j * HD : (j + 1) * HD] = (mixed / total).astype(BF16)
        norm_ref[...] = jnp.where(lane == group * per_step + j, top + jnp.log2(total), norm_ref[...])


def attn_backward_kernel(
    per_step, pos_ref, ends_ref, q_ref, kv_ref, norm_ref, grad_ref, dq_ref, dkv_ref,
    bias, key_turned, value_turned, key_grad, value_grad,
):
    w, group = pl.program_id(0), pl.program_id(1)

    @pl.when(group == 0)
    def _():
        fill_mask(pos_ref, ends_ref, w, bias, key_turned, value_turned, kv_ref)
        key_grad[...] = jnp.zeros_like(key_grad)
        value_grad[...] = jnp.zeros_like(value_grad)

    keys = kv_ref[0, :, :HD]
    lane = lax.broadcasted_iota(jnp.int32, norm_ref.shape, 1)
    for j in range(per_step):
        query = q_ref[:, j * HD : (j + 1) * HD]
        grad = grad_ref[:, j * HD : (j + 1) * HD]
        scores = jnp.dot(query, key_turned[...], preferred_element_type=F32)
        scores = scores * (LOG2E / math.sqrt(HD)) + bias[...]
        norm = jnp.sum(jnp.where(lane == group * per_step + j, norm_ref[...], 0.0), axis=1, keepdims=True)
        probs = jnp.exp2(scores - norm)
        grad_probs = jnp.dot(grad, value_turned[...], preferred_element_type=F32)
        delta = jnp.sum(probs * grad_probs, axis=1, keepdims=True)
        score_grad = (probs * (grad_probs - delta)).astype(BF16)
        probs = probs.astype(BF16)
        dq = jnp.dot(score_grad, keys, preferred_element_type=F32)
        dq_ref[:, j * HD : (j + 1) * HD] = (dq / math.sqrt(HD)).astype(BF16)
        key_grad[...] += dot_tn(query, score_grad)
        value_grad[...] += dot_tn(grad, probs)

    @pl.when(group == pl.num_programs(1) - 1)
    def _():
        dkv_ref[0, :, :HD] = (key_grad[...].T / math.sqrt(HD)).astype(BF16)
        dkv_ref[0, :, HD:] = value_grad[...].T.astype(BF16)


def attn_specs(per_step, span, win):
    smem = pl.BlockSpec(memory_space=pltpu.SMEM)
    heads = pl.BlockSpec((span, per_step * HD), lambda w, g: (w, g))
    keys = pl.BlockSpec((1, win, 2 * HD), lambda w, g: (w, 0, 0))
    norm = pl.BlockSpec((span, HD), lambda w, g: (w, 0))
    return smem, heads, keys, norm


def attn_cost(windows, span, win, products):
    return pl.CostEstimate(
        flops=2 * products * windows * HEADS * span * win * HD,
        transcendentals=windows * HEADS * span * win,
        bytes_accessed=products * windows * HEADS * span * HD * 2,
    )


def attn_forward(queries, kv_window, first, ends, per_step=4):
    windows, win, _ = kv_window.shape
    rows, width = queries.shape
    span = rows // windows
    smem, heads, keys, norm = attn_specs(per_step, span, win)
    return pl.pallas_call(
        functools.partial(attn_forward_kernel, per_step),
        out_shape=(
            jax.ShapeDtypeStruct((rows, width), BF16),
            jax.ShapeDtypeStruct((rows, HD), F32),
        ),
        grid=(windows, HEADS // per_step),
        in_specs=[smem, smem, heads, keys],
        out_specs=(heads, norm),
        scratch_shapes=[pltpu.VMEM((span, win), F32), pltpu.VMEM((HD, win), BF16)],
        compiler_params=pltpu.CompilerParams(vmem_limit_bytes=40 * 2**20),
        cost_estimate=attn_cost(windows, span, win, 2),
    )(first, ends, queries, kv_window)


def attn_backward(queries, kv_window, norms, grads, first, ends, per_step=4):
    windows, win, _ = kv_window.shape
    rows, width = queries.shape
    span = rows // windows
    smem, heads, keys, norm = attn_specs(per_step, span, win)
    return pl.pallas_call(
        functools.partial(attn_backward_kernel, per_step),
        out_shape=(
            jax.ShapeDtypeStruct((rows, width), BF16),
            jax.ShapeDtypeStruct((windows, win, 2 * HD), BF16),
        ),
        grid=(windows, HEADS // per_step),
        in_specs=[smem, smem, heads, keys, norm, heads],
        out_specs=(heads, keys),
        scratch_shapes=[
            pltpu.VMEM((span, win), F32),
            pltpu.VMEM((HD, win), BF16),
            pltpu.VMEM((HD, win), BF16),
            pltpu.VMEM((HD, win), F32),
            pltpu.VMEM((HD, win), F32),
        ],
        compiler_params=pltpu.CompilerParams(vmem_limit_bytes=48 * 2**20),
        cost_estimate=attn_cost(windows, span, win, 5),
    )(first, ends, queries, kv_window, norms, grads)


def norm_stats(values):
    average = jnp.mean(values, axis=-1, keepdims=True)
    centered = values - average
    variance = jnp.mean(centered * centered, axis=-1, keepdims=True)
    return average, lax.rsqrt(variance + EPS)


def norm_pull(grad, xhat, recip, gain):
    scaled = grad * gain
    mean_one = jnp.mean(scaled, axis=-1, keepdims=True)
    mean_two = jnp.mean(scaled * xhat, axis=-1, keepdims=True)
    return recip * (scaled - mean_one - xhat * mean_two)


def gelu_tanh(values):
    return jax.nn.gelu(values, approximate=True)


def tie(*arrays):
    return lax.optimization_barrier(arrays)


def scatter_both(block):
    part = lax.psum_scatter(block, "dp", scatter_dimension=0, tiled=True)
    return lax.psum_scatter(part, "fsdp", scatter_dimension=0, tiled=True)


def shift(block, count):
    return lax.ppermute(block, "fsdp", [(i, (i + 1) % count) for i in range(count)])


def put_in_order(pieces, count, axis=0):
    me = lax.axis_index("fsdp")
    size = pieces[0].shape[axis]
    shape = list(pieces[0].shape)
    shape[axis] = size * count
    whole = jnp.zeros(shape, pieces[0].dtype)
    for step, piece in enumerate(pieces):
        place = lax.rem(me - step + count, count) * size
        whole = lax.dynamic_update_slice_in_dim(whole, piece, place, axis)
    return whole


def ring_scatter(terms, count):
    me = lax.axis_index("fsdp")

    def term(step):
        return lax.dynamic_index_in_dim(
            terms, lax.rem(me - 1 - step + 2 * count, count), 0, keepdims=False
        ).astype(F32)

    total = term(0)
    for step in range(1, count):
        total = shift(total.astype(BF16), count).astype(F32) + term(step)
    return total


class Plane:
    def __init__(self, count):
        self.count = count
        self.bits = [1 << i for i in range(1, count.bit_length() - 1)]
        self.orders = (self.bits, self.bits[::-1])
        chips = range(0, count, 2)
        far = [(h, o) for h in (0, 1) for o in chips if o & self.orders[h][0]]
        near = [(h, o) for h in (0, 1) for o in chips if not o & self.orders[h][0]]
        self.keys = far + near
        self.n_far = len(far)

    def swap(self, block, bit):
        return lax.ppermute(block, "dp", [(i, i ^ bit) for i in range(self.count)])

    def gather_step(self, held, step):
        got = {}
        for (half, offset), piece in held.items():
            bit = self.orders[half][step]
            got[half, offset | bit] = self.swap(piece, bit)
        return got

    def lay(self, held):
        return jnp.concatenate([held[key] for key in self.keys])

    def cross(self, held):
        return {key: self.swap(piece, 1) for key, piece in held.items()}

    def split(self, rows, keys):
        size = rows.shape[0] // len(keys)
        return {key: rows[i * size : (i + 1) * size] for i, key in enumerate(keys)}

    def scatter_step(self, held, step):
        kept = {}
        for (half, offset), piece in held.items():
            bit = self.orders[half][step]
            if not offset & bit:
                got = self.swap(held[half, offset | bit], bit).astype(F32)
                kept[half, offset] = piece.astype(F32) + got
        return kept


def narrow(held):
    return {key: piece.astype(BF16) for key, piece in held.items()}


def make_local(n_dp, n_z):
    n_dev = n_dp * n_z
    plane = Plane(n_dp)

    def local(
        tokens,
        cotangent,
        lengths,
        query_weight,
        kv_weight,
        out_weight,
        query_bias,
        value_bias,
        out_bias,
        attn_gain,
        attn_shift,
        up_weight,
        down_weight,
        up_bias,
        down_bias,
        mlp_gain,
        mlp_shift,
    ):
        windows, local_len, width = tokens.shape
        rows = windows * local_len
        own = query_weight.shape[0]
        ff_own = up_weight.shape[1] // n_dp
        my_dp = lax.axis_index("dp")

        small = (
            query_bias,
            value_bias,
            out_bias,
            attn_gain,
            attn_shift,
            up_bias,
            down_bias,
            mlp_gain,
            mlp_shift,
        )
        sizes = [v.shape[0] for v in small]
        starts = [sum(sizes[:i]) for i in range(len(sizes))]
        small_row = jnp.concatenate(small)
        kv_lines = kv_weight.size // width
        filled = own + kv_lines + -(-small_row.shape[0] // width)
        lines = -(-filled // 16) * 16
        spare = (lines - own - kv_lines) * width
        small_row = jnp.pad(small_row, (0, spare - small_row.shape[0]))
        packed = jnp.concatenate(
            [query_weight, kv_weight.reshape(kv_lines, width), small_row.reshape(-1, width)]
        )

        packed = lax.all_gather(packed, "fsdp", axis=0, tiled=True)
        up_cols = lax.all_to_all(up_weight, "dp", 1, 0, tiled=True).reshape(n_dp, own, ff_own)
        packed, up_cols, down_weight, out_weight, cotangent = tie(
            packed, up_cols, down_weight, out_weight, cotangent
        )
        packed = lax.all_gather(packed, "dp", axis=0, tiled=True)
        full_o = lax.all_gather(out_weight, "fsdp", axis=0, tiled=True)
        down_pieces = [down_weight]
        while len(down_pieces) < min(3, n_z):
            down_pieces.append(shift(down_pieces[-1], n_z))
        inputs = tokens.reshape(rows, width).astype(F32)
        mean_one, recip_one = norm_stats(inputs)
        packed, full_o, down_pieces[-1], cotangent = tie(packed, full_o, down_pieces[-1], cotangent)

        full_o = lax.all_gather(full_o, "dp", axis=0, tiled=True)
        while len(down_pieces) < n_z:
            down_pieces.append(shift(down_pieces[-1], n_z))
        half = rows // 2
        grad_low = cotangent.reshape(rows, width)
        grad_held = {(0, 0): grad_low[:half], (1, 0): grad_low[half:]}
        grad_held.update(plane.gather_step(grad_held, 0))
        packed = packed.reshape(n_dev, lines, width)
        full_q = packed[:, :own].reshape(width, width)
        full_kv = packed[:, own : own + kv_lines].reshape(width, 2 * HD)
        small_all = packed[:, own + kv_lines :].reshape(n_dev, -1)
        bias_q, bias_v, bias_o, gain_one, shift_one, bias_up, bias_down, gain_two, shift_two = (
            small_all[:, start : start + size].reshape(-1).astype(F32)
            for start, size in zip(starts, sizes)
        )
        xhat_one = (inputs - mean_one) * recip_one
        normed_one = (xhat_one * gain_one + shift_one).astype(BF16)
        kv_bias = jnp.concatenate([jnp.zeros((HD,), F32), bias_v])
        key_value = (dot_nn(normed_one, full_kv) + kv_bias).astype(BF16)
        kv_window = lax.all_gather(
            key_value.reshape(windows, local_len, 2 * HD), "fsdp", axis=1, tiled=True
        )
        queries = (dot_nn(normed_one, full_q) + bias_q).astype(BF16)
        queries, up_cols, down_pieces[-1] = tie(queries, up_cols, down_pieces[-1])
        up_pieces = [up_cols]
        up_pieces.append(shift(up_pieces[-1], n_z))

        first = (lax.axis_index("fsdp") * local_len).astype(jnp.int32).reshape(1)
        file_count = lengths.shape[1]
        upto = jnp.arange(file_count)[:, None] <= jnp.arange(file_count)[None, :]
        file_ends = jnp.sum(jnp.where(upto[None], lengths[:, :, None], 0), axis=1)
        queries, kv_window, up_pieces[-1] = tie(queries, kv_window, up_pieces[-1])
        while len(up_pieces) < min(3, n_z):
            up_pieces.append(shift(up_pieces[-1], n_z))
        attended, norms = attn_forward(queries, kv_window, first, file_ends)
        attended, up_pieces[-1] = tie(attended, up_pieces[-1])
        while len(up_pieces) < n_z:
            up_pieces.append(shift(up_pieces[-1], n_z))
        middle = inputs + dot_nn(attended, full_o) + bias_o
        mean_two, recip_two = norm_stats(middle)
        xhat_two = (middle - mean_two) * recip_two
        normed_two = (xhat_two * gain_two + shift_two).astype(BF16)

        normed_two, *grad_pieces = tie(normed_two, *grad_held.values())
        grad_held = dict(zip(grad_held, grad_pieces))
        two_held = {(0, 0): normed_two[:half], (1, 0): normed_two[half:]}
        for step in range(1, len(plane.bits)):
            grad_held.update(plane.gather_step(grad_held, step))
        for step in range(len(plane.bits)):
            two_held.update(plane.gather_step(two_held, step))
        grad_mine = plane.lay(grad_held)
        grad_sib = plane.swap(grad_mine, 1)
        down_part = put_in_order(down_pieces, n_z)
        up_part = put_in_order(up_pieces, n_z, 1).reshape(width, ff_own)
        bias_up_part = lax.dynamic_slice_in_dim(bias_up, my_dp * ff_own, ff_own)
        back_mine = dot_nt(grad_mine, down_part)
        back_sib = dot_nt(grad_sib, down_part)
        two_sib = plane.lay(plane.cross(two_held))
        two_mine = plane.lay(two_held)
        two_mine, back_mine, back_sib = tie(two_mine, back_mine, back_sib)

        def middle_layer(two, back):
            pre_act = dot_nn(two, up_part) + bias_up_part
            hidden, pull = jax.vjp(gelu_tanh, pre_act)
            return hidden.astype(BF16), pull(back)[0].astype(BF16)

        hidden_mine, pre_mine = middle_layer(two_mine, back_mine)
        two_sib, pre_mine = tie(two_sib, pre_mine)
        hidden_sib, pre_sib = middle_layer(two_sib, back_sib)
        n_far = plane.n_far * half

        def core_sum(mine, sib, weight, product):
            out = []
            for lot, keys in ((slice(0, n_far), plane.keys[: plane.n_far]), (slice(n_far, None), plane.keys[plane.n_far :])):
                theirs = plane.swap(product(sib[lot], weight).astype(BF16), 1)
                ours = product(mine[lot], weight)
                out.append(plane.split((ours + theirs.astype(F32)).astype(BF16), keys))
            return out

        far, near = core_sum(pre_mine, pre_sib, up_part, dot_nt)
        two_sum = {**far, **near}
        hidden_mine, pre_mine, *near_pieces = tie(hidden_mine, pre_mine, *near.values())
        two_sum.update(zip(near, near_pieces))
        two_sum = plane.scatter_step(two_sum, 0)
        up_terms = dot_tn(two_mine, pre_mine) + dot_tn(two_sib, pre_sib)
        up_terms = up_terms.astype(BF16).reshape(n_dp, n_z, own, ff_own).transpose(1, 0, 2, 3)
        out_far, out_near = core_sum(hidden_mine, hidden_sib, down_part, dot_nn)
        out_sum = {**out_far, **out_near}
        two_keys, out_keys = list(two_sum), list(out_sum)
        up_terms, *pieces = tie(up_terms, *two_sum.values(), *out_sum.values())
        two_sum = dict(zip(two_keys, pieces))
        out_sum = dict(zip(out_keys, pieces[len(two_keys) :]))
        for step in range(1, len(plane.bits)):
            two_sum = plane.scatter_step(narrow(two_sum), step)
        two_grad = jnp.concatenate([two_sum[0, 0], two_sum[1, 0]])
        down_terms = dot_tn(hidden_mine, grad_mine) + dot_tn(hidden_sib, grad_sib)
        down_terms = down_terms.astype(BF16).reshape(n_z, ff_own // n_z, width)
        two_grad, down_terms, *pieces = tie(two_grad, down_terms, *out_sum.values())
        out_sum = plane.scatter_step(dict(zip(out_keys, pieces)), 0)
        grad_up = ring_scatter(up_terms, n_z)
        grad_up = lax.all_to_all(
            grad_up.astype(BF16).reshape(n_dp * own, ff_own), "dp", 0, 1, tiled=True
        ).astype(F32)
        grad_down = ring_scatter(down_terms, n_z)
        up_bias_part = jnp.sum(pre_mine.astype(F32), axis=0) + jnp.sum(pre_sib.astype(F32), axis=0)

        grad_out = grad_low.astype(F32)
        grad_bdown = jnp.sum(grad_out, axis=0)
        grad_gain_two = jnp.sum(two_grad * xhat_two, axis=0)
        grad_shift_two = jnp.sum(two_grad, axis=0)
        middle_grad = grad_out + norm_pull(two_grad, xhat_two, recip_two, gain_two)
        grad_bo = jnp.sum(middle_grad, axis=0)
        branch_grad = middle_grad.astype(BF16)
        grad_wo = scatter_both(dot_tn(attended, branch_grad).astype(BF16)).astype(F32)
        attended_grad = dot_nt(branch_grad, full_o).astype(BF16)

        out_keys = list(out_sum)
        attended_grad, *pieces = tie(attended_grad, *out_sum.values())
        out_sum = dict(zip(out_keys, pieces))
        for step in range(1, len(plane.bits)):
            out_sum = plane.scatter_step(narrow(out_sum), step)
        branch_out = jnp.concatenate([out_sum[0, 0], out_sum[1, 0]])
        output = (middle + branch_out + bias_down).astype(BF16).reshape(windows, local_len, width)

        query_grad, kv_terms = attn_backward(queries, kv_window, norms, attended_grad, first, file_ends)
        kv_grad = lax.psum_scatter(kv_terms, "fsdp", scatter_dimension=1, tiled=True)
        kv_grad = kv_grad.reshape(rows, 2 * HD)
        grad_bq = jnp.sum(query_grad.astype(F32), axis=0)
        grad_bv = jnp.sum(kv_grad[:, HD:].astype(F32), axis=0)
        grad_wq = dot_tn(normed_one, query_grad)
        grad_wkv = dot_tn(normed_one, kv_grad)
        one_grad = dot_nt(query_grad, full_q) + dot_nt(kv_grad, full_kv)
        grad_gain_one = jnp.sum(one_grad * xhat_one, axis=0)
        grad_shift_one = jnp.sum(one_grad, axis=0)
        tokens_grad = middle_grad + norm_pull(one_grad, xhat_one, recip_one, gain_one)
        tokens_grad = tokens_grad.astype(BF16).reshape(windows, local_len, width)

        grad_bup = jnp.where(jnp.arange(n_dp)[:, None] == my_dp, up_bias_part[None], 0.0).reshape(-1)
        sums = (
            grad_bq,
            grad_bv,
            grad_bo,
            grad_gain_one,
            grad_shift_one,
            grad_bup,
            grad_bdown,
            grad_gain_two,
            grad_shift_two,
        )
        sum_rows = jnp.concatenate([v.astype(BF16).reshape(n_dev, -1) for v in sums], axis=1)
        sum_rows = jnp.pad(sum_rows, ((0, 0), (0, spare - sum_rows.shape[1])))
        grads = jnp.concatenate(
            [
                grad_wq.astype(BF16).reshape(n_dev, own, width),
                grad_wkv.astype(BF16).reshape(n_dev, kv_lines, width),
                sum_rows.reshape(n_dev, -1, width),
            ],
            axis=1,
        )
        mine = scatter_both(grads.reshape(n_dev * lines, width)).astype(F32)
        grad_q = mine[:own]
        grad_kv = mine[own : own + kv_lines].reshape(own, 2 * HD)
        flat = mine[own + kv_lines :].reshape(-1)
        bq, bv, bo, gain1, shift1, bup, bdown, gain2, shift2 = (
            flat[start : start + size] for start, size in zip(starts, sizes)
        )
        return (
            output,
            tokens_grad,
            grad_q,
            grad_kv,
            grad_wo,
            bq,
            bv,
            bo,
            gain1,
            shift1,
            grad_up,
            grad_down,
            bup,
            bdown,
            gain2,
            shift2,
        )

    return local


def solution(mesh):
    whole = P(BOTH, None)
    vector = P(BOTH)
    rows = P("dp", "fsdp", None)
    weights = (whole, whole, whole) + (vector,) * 5 + (whole, whole) + (vector,) * 4
    return jax.shard_map(
        make_local(mesh.shape["dp"], mesh.shape["fsdp"]),
        mesh=mesh,
        in_specs=(rows, rows, P("dp", None)) + weights,
        out_specs=(rows, rows) + weights,
        check_vma=False,
    )
```

time: 1130 us -> 1010 us (0.89)
  waiting for transfers between devices: 596 us -> 478 us
  matrix products: 310 us -> 230 us
  Pallas kernels: 0 us -> 49.9 us
  starting transfers between devices: 16.9 us -> 42.9 us
  blocking collectives: 0 us -> 20.4 us
    reduce_scatter x3 -> x1, waiting for transfers between devices: 203 us -> 0.01 us  [local(): lax.psum_scatter(kv_terms, 'fsdp', scatter_dimension=1, tiled=True)]
    ppermute x12 -> x49, waiting for transfers between devices: 231 us -> 348 us  [the longest x12 236 us: shift(): lax.ppermute(block, 'fsdp', [(i, (i + 1) % count) for i in range(count)])]
    all_gather x6 -> x4, waiting for transfers between devices: 133 us -> 63.3 us  [the longest x1 41.1 us: local(): packed = lax.all_gather(packed, 'dp', axis=0, tiled=True)]
    pallas_call x0 -> x2, Pallas kernels: none -> 49.9 us  [the longest x1 31.1 us: attn_backward(): pl.pallas_call(functools.partial(attn_backward_kernel, per_step), out_sha...]
    reduce_scatter x2, waiting for transfers between devices: 0.01 us -> 45.9 us  [scatter_both(): return lax.psum_scatter(part, 'fsdp', scatter_dimension=0, tiled=True)]
    sub x2 -> x0, matrix products: 42 us -> none  [local(): grad_probs - row_delta]
    ppermute x12 -> x49, starting transfers between devices: 8.56 us -> 38.2 us  [the longest x37 30 us: swap(): return lax.ppermute(block, 'dp', [(i, i ^ bit) for i in range(self.count)])]
    all_to_all x1 -> x0, waiting for transfers between devices: 23 us -> none  [local(): lax.all_to_all(up_weight, 'dp', 1, 0, tiled=True).reshape(n_dp, own, ff_own)]
  transfers between devices with their start and end apart: 28 -> 60, of which waited for: 19 -> 33; matrix products, arithmetic and copies ran while one was open for 28% -> 29% of each run, Pallas kernels for 0% -> 2%
where the time goes in v2:
time: 1010 us; the launch traced here: 1000 us
  waiting for transfers between devices  478 us (47%)
  matrix products  230 us (23%)
  other arithmetic  91.8 us (9%)
  local copies, waits for them, and re-layouts  75.2 us (7%)
  Pallas kernels  49.9 us (5%)
  starting transfers between devices  42.9 us (4%)
  blocking collectives  20.4 us (2%)
  between operations  15.6 us (2%)
    ppermute x12, waiting for transfers between devices, shift(): lax.ppermute(block, 'fsdp', [(i, (i + 1) % count) for i in range(count)])  236 us
    ppermute x37, waiting for transfers between devices, swap(): return lax.ppermute(block, 'dp', [(i, i ^ bit) for i in range(self.count)])  112 us
    dot_general x7, matrix products, dot_tn(): lax.dot_general(left, right, (((0,), (0,)), ((), ())), preferred_element_...  80.8 us
    dot_general x9, matrix products, dot_nt(): lax.dot_general(left, right, (((1,), (1,)), ((), ())), preferred_element_...  78.1 us
    dot_general x9, matrix products, dot_nn(): return jnp.dot(left, right, preferred_element_type=F32)  71.2 us
    reduce_scatter x2, waiting for transfers between devices, scatter_both(): return lax.psum_scatter(part, 'fsdp', scatter_dimension=0, tiled=True)  45.9 us
    all_gather x1, waiting for transfers between devices, local(): packed = lax.all_gather(packed, 'dp', axis=0, tiled=True)  41.1 us
    pallas_call x1, Pallas kernels, attn_backward(): pl.pallas_call(functools.partial(attn_backward_kernel, per_step), out_sha...  31.1 us
  transfers between devices with their start and end apart: 60, of which 33 were waited for; matrix products, arithmetic and copies ran while one was open for 29% of the time, Pallas kernels for 2%

profile of v2, /device:TPU:0, one launch (start us, length us, event | category | flops | bytes accessed | tf_op | source)
XLA Modules:
  0.0 1004.1 jit_solution(8251825478572642113)
XLA Ops:
  7.3 6.3 concatenate.32
  17.5 20.4 %all_to_all.26 = bf16[64,8,1024]{2,0,1:T(8,128)(2,1)} all-to-all(bf16[64,8,1024]{2,0,1:T(8,128)(2,1)S(1)} %bitcast.169), channel_id=1, replica_groups=mesh['dp'=8,'fsdp'=4] {'dp'}, dimensions={1} | all-to-all | bytes 2097152 | tf_op jit(solution)/shard_map/all_to_all | solution.py:327
  37.9 13.7 %all-gather.6.cloned.1.call-done = bf16[320,2048]{1,0:T(8,128)(2,1)} async-done(((bf16[80,2048]{1,0:T(8,128)(2,1)}), bf16[320,2048]{1,0:T(8,128)(2,1)}) %all-gather.6.cloned.1.call-update) | async-done | bytes 1310736 | tf_op jit(solution)/shard_map/all_gather | solution.py:326
  53.3 41.5 %collective-permute-done = bf16[256,2048]{1,0:T(8,128)(2,1)} collective-permute-done((bf16[256,2048]{1,0:T(8,128)(2,1)S(1)}, bf16[256,2048]{1,0:T(8,128)(2,1)}, u32[]{:S(2)}, u32[]{:S(2)}) %collective-permute-start) | collective-permute-done | bytes 1048608 | tf_op jit(solution)/shard_map/ppermute | solution.py:200
  96.9 21.2 %collective-permute-done.1 = bf16[256,2048]{1,0:T(8,128)(2,1)S(1)} collective-permute-done((bf16[256,2048]{1,0:T(8,128)(2,1)}, bf16[256,2048]{1,0:T(8,128)(2,1)S(1)}, u32[]{:S(2)}, u32[]{:S(2)}) %collective-permute-start.1) | collective-permute-done | bytes 1048608 | tf_op jit(solution)/shard_map/ppermute | solution.py:200
  118.1 41.1 %all-gather.8.cloned.1.call-done = bf16[2560,2048]{1,0:T(8,128)(2,1)} async-done(((bf16[320,2048]{1,0:T(8,128)(2,1)}), bf16[2560,2048]{1,0:T(8,128)(2,1)}) %all-gather.8.cloned.1.call-update) | async-done | bytes 10485776 | tf_op jit(solution)/shard_map/all_gather | solution.py:331
  168.4 8.4 slice.223
  178.4 10.0 add_convert_fusion.7.q_ref
  188.4 30.9 %collective-permute-done.2 = bf16[256,2048]{1,0:T(8,128)(2,1)S(1)} collective-permute-done((bf16[256,2048]{1,0:T(8,128)(2,1)S(1)}, bf16[256,2048]{1,0:T(8,128)(2,1)S(1)}, u32[]{:S(2)}, u32[]{:S(2)}) %collective-permute-start.2) | collective-permute-done | bytes 1048608 | tf_op jit(solution)/shard_map/ppermute | solution.py:200
  220.3 27.0 %collective-permute-done.3 = bf16[8,64,1024]{2,1,0:T(8,128)(2,1)} collective-permute-done((bf16[8,64,1024]{2,1,0:T(8,128)(2,1)}, bf16[8,64,1024]{2,1,0:T(8,128)(2,1)}, u32[]{:S(2)}, u32[]{:S(2)}) %collective-permute-start.3) | collective-permute-done | bytes 1048608 | tf_op jit(solution)/shard_map/ppermute | solution.py:200
  252.3 18.7 %shard_map.288 = (bf16[512,2048]{1,0:T(8,128)(2,1)S(1)}, f32[512,128]{1,0:T(8,128)S(1)}) custom-call(s32[1]{0:T(128)} %bitcast.1.pos_ref, s32[2,8]{1,0:T(2,128)S(1)} %select_reduce_fusion.ends_ref, bf16[512,2048]{1,0:T(8,128)(2,1)S(1)} %copy-done.5, bf16[2,1024,256]{2,1,0:T(8,128)(2,1)S(1)} %copy-done.2), custom_call_target="tpu_custom_call" | custom-call | flops 4294967296 | bytes 4194304 | tf_op jit(solution)/shard_map/pallas_call | solution.py:131
  273.7 8.4 all-gather.14.cloned.1.call-done
  282.1 8.7 fusion.64
  301.4 17.8 %collective-permute-done.13 = bf16[256,2048]{1,0:T(8,128)(2,1)} collective-permute-done((bf16[256,2048]{1,0:T(8,128)(2,1)}, bf16[256,2048]{1,0:T(8,128)(2,1)}, u32[]{:S(2)}, u32[]{:S(2)}) %collective-permute-start.13) | collective-permute-done | bytes 1048608 | tf_op jit(solution)/shard_map/ppermute | solution.py:241
  327.3 13.6 %collective-permute-done.15 = bf16[256,2048]{1,0:T(8,128)(2,1)S(1)} collective-permute-done((bf16[256,2048]{1,0:T(8,128)(2,1)}, bf16[256,2048]{1,0:T(8,128)(2,1)S(1)}, u32[]{:S(2)}, u32[]{:S(2)}) %collective-permute-start.15) | collective-permute-done | bytes 1048608 | tf_op jit(solution)/shard_map/ppermute | solution.py:241
  346.3 4.8 collective-permute-start.18
  359.9 14.7 %collective-permute-done.18 = bf16[8,64,1024]{2,1,0:T(8,128)(2,1)S(1)} collective-permute-done((bf16[8,64,1024]{2,1,0:T(8,128)(2,1)}, bf16[8,64,1024]{2,1,0:T(8,128)(2,1)S(1)}, u32[]{:S(2)}, u32[]{:S(2)}) %collective-permute-start.18) | collective-permute-done | bytes 1048608 | tf_op jit(solution)/shard_map/ppermute | solution.py:200
  380.9 11.3 %fusion.65 = f32[2048,1024]{1,0:T(8,128)S(1)} fusion(bf16[2048,2048]{1,0:T(8,128)(2,1)} %constant_dynamic-update-slice_fusion.8, bf16[1024,2048]{1,0:T(8,128)(2,1)S(1)} %constant_dynamic-update-slice_fusion.28), kind=kOutput, calls=%fused_computation.184 | convolution fusion | flops 8589934592 | bytes 20971520 | tf_op jit(solution)/shard_map/dot_general | solution.py:24
  392.3 32.0 %collective-permute-done.8 = bf16[256,2048]{1,0:T(8,128)(2,1)S(1)} collective-permute-done((bf16[256,2048]{1,0:T(8,128)(2,1)S(1)}, bf16[256,2048]{1,0:T(8,128)(2,1)S(1)}, u32[]{:S(2)}, u32[]{:S(2)}) %collective-permute-start.8) | collective-permute-done | bytes 1048608 | tf_op jit(solution)/shard_map/ppermute | solution.py:241
  437.5 3.2 copy-done.44
  440.7 13.2 %fusion.66 = f32[2048,1024]{1,0:T(8,128)} fusion(bf16[2048,2048]{1,0:T(8,128)(2,1)} %collective-permute-done.17, bf16[1024,2048]{1,0:T(8,128)(2,1)S(1)} %constant_dynamic-update-slice_fusion.28), kind=kOutput, calls=%fused_computation.185 | convolution fusion | flops 8589934592 | bytes 20971520 | tf_op jit(solution)/shard_map/dot_general | solution.py:24
  453.9 13.3 %fusion.67 = f32[2048,1024]{1,0:T(8,128)} fusion(bf16[2048,2048]{1,0:T(8,128)(2,1)} %copy-done.45, bf16[2048,1024]{1,0:T(8,128)(2,1)S(1)} %bitcast.162), kind=kOutput, calls=%fused_computation.186 | convolution fusion | flops 8589934592 | bytes 20971520 | tf_op jit(solution)/shard_map/dot_general | solution.py:20
  467.2 9.5 fusion.6
  476.8 12.8 %fusion.68 = f32[2048,1024]{1,0:T(8,128)S(1)} fusion(bf16[2048,2048]{1,0:T(8,128)(2,1)} %copy-done.44, bf16[2048,1024]{1,0:T(8,128)(2,1)S(1)} %bitcast.163), kind=kOutput, calls=%fused_computation.187 | convolution fusion | flops 8589934592 | bytes 20971520 | tf_op jit(solution)/shard_map/dot_general | solution.py:20
  489.6 8.9 convert_reduce_fusion
  498.5 8.1 convolution_convert_fusion.5
  506.8 6.1 convolution_convert_fusion.4
  513.2 6.1 convolution_convert_fusion.3
  519.3 6.1 convolution_convert_fusion.2
  525.9 13.4 %fusion.70 = f32[1024,2048]{1,0:T(8,128)} fusion(bf16[2048,1024]{1,0:T(8,128)(2,1)S(1)} %copy-done.25, bf16[2048,2048]{1,0:T(8,128)(2,1)} %collective-permute-done.17), kind=kOutput, calls=%fused_computation.189 | convolution fusion | flops 8589934592 | bytes 20971520 | tf_op jit(solution)/shard_map/dot_general | solution.py:28
  539.3 6.8 add_convert_fusion.5
  546.7 6.4 add_convert_fusion.3
  559.4 6.4 add_convert_fusion.2
  565.8 13.8 %fusion.69 = f32[2048,1024]{1,0:T(8,128)} fusion(bf16[2048,2048]{1,0:T(8,128)(2,1)} %copy-done.45, bf16[2048,1024]{1,0:T(8,128)(2,1)S(1)} %get-tuple-element.109), kind=kOutput, calls=%fused_computation.188 | convolution fusion | flops 8589934592 | bytes 20971520 | tf_op jit(solution)/shard_map/dot_general | solution.py:28
  579.6 15.8 %add_convert_fusion.4 = bf16[2048,1024]{1,0:T(8,128)(2,1)} fusion(f32[2048,1024]{1,0:T(8,128)} %fusion.69, bf16[2048,2048]{1,0:T(8,128)(2,1)} %copy-done.44, bf16[2048,1024]{1,0:T(8,128)(2,1)S(1)} %copy-done.24), kind=kOutput, calls=%fused_computation.26 | convolution fusion | flops 8594128896 | bytes 25165824 | tf_op jit(solution)/shard_map/dot_general | solution.py:28
  595.4 6.4 add_convert_fusion.1
  612.1 14.5 %add_convert_fusion = bf16[1024,2048]{1,0:T(8,128)(2,1)} fusion(f32[1024,2048]{1,0:T(8,128)} %fusion.70, bf16[2048,1024]{1,0:T(8,128)(2,1)S(1)} %copy-done.22, bf16[2048,2048]{1,0:T(8,128)(2,1)} %constant_dynamic-update-slice_fusion.8), kind=kOutput, calls=%fused_computation.21 | convolution fusion | flops 8594128896 | bytes 25165824 | tf_op jit(solution)/shard_map/dot_general | solution.py:28
  626.6 7.5 collective-permute-done.36
  645.5 10.7 %convolution_convert_fusion.6.grad_ref = bf16[512,2048]{1,0:T(8,128)(2,1)} fusion(bf16[2048,2048]{1,0:T(8,128)(2,1)} %all-gather.14.cloned.1.call-done, f32[512,2048]{1,0:T(8,128)S(1)} %get-tuple-element.157), kind=kOutput, calls=%fused_computation.73 | convolution fusion | flops 4297064448 | bytes 14680064 | tf_op jit(solution)/shard_map/dot_general | solution.py:24
  656.2 9.1 collective-permute-done.37
  666.7 18.1 %collective-permute-done.38 = bf16[256,2048]{1,0:T(8,128)(2,1)S(1)} collective-permute-done((bf16[256,2048]{1,0:T(8,128)(2,1)S(1)}, bf16[256,2048]{1,0:T(8,128)(2,1)S(1)}, u32[]{:S(2)}, u32[]{:S(2)}) %collective-permute-start.38) | collective-permute-done | bytes 1048608 | tf_op jit(solution)/shard_map/ppermute | solution.py:241
  689.0 31.1 %shard_map.289 = (bf16[512,2048]{1,0:T(8,128)(2,1)S(1)}, bf16[2,1024,256]{2,1,0:T(8,128)(2,1)}) custom-call(s32[1]{0:T(128)} %bitcast.1.pos_ref, s32[2,8]{1,0:T(2,128)S(1)} %copy-done.1, bf16[512,2048]{1,0:T(8,128)(2,1)} %add_convert_fusion.7.q_ref, bf16[2,1024,256]{2,1,0:T(8,128)(2,1)S(1)} %copy-done.3, f32[512,128]{1,0:T(8,128)S(1)} %get-tuple-element.140.norm_ref, ...), custom_call_target="tpu_custom_call" | custom-call | flops 10737418240 | bytes 10485760 | tf_op jit(solution)/shard_map/pallas_call | solution.py:151
  720.2 10.6 %convolution_convert_fusion = bf16[2048,2048]{1,0:T(8,128)(2,1)} fusion(bf16[512,2048]{1,0:T(8,128)(2,1)} %copy-done.4, f32[512,2048]{1,0:T(8,128)} %copy-done.12), kind=kOutput, calls=%fused_computation.29 | convolution fusion | flops 4300210176 | bytes 14680064 | tf_op jit(solution)/shard_map/dot_general | solution.py:28
  733.8 2.9 convert_reduce_fusion.1
  737.5 9.5 fusion.71
  748.2 6.0 fusion.35
  755.1 3.8 fusion.36
  761.4 8.8 convolution_convert_fusion.1
  770.2 10.3 %pad_maximum_fusion = bf16[32,80,2048]{2,1,0:T(8,128)(2,1)} fusion(bf16[32,8,2048]{2,1,0:T(8,128)(2,1)S(1)} %bitcast.153, bf16[32,8,2048]{2,1,0:T(8,128)(2,1)} %reshape.386, bf16[32,64,2048]{2,1,0:T(8,128)(2,1)} %bitcast.152), kind=kLoop, calls=%fused_computation.4 | loop fusion | flops 31457280 | bytes 20971520 | tf_op jit(solution)/shard_map/concatenate | solution.py:491
  782.4 24.1 %collective-permute-done.43 = bf16[8,64,1024]{2,1,0:T(8,128)(2,1)S(1)} collective-permute-done((bf16[8,64,1024]{2,1,0:T(8,128)(2,1)S(1)}, bf16[8,64,1024]{2,1,0:T(8,128)(2,1)S(1)}, u32[]{:S(2)}, u32[]{:S(2)}) %collective-permute-start.43) | collective-permute-done | bytes 1048608 | tf_op jit(solution)/shard_map/ppermute | solution.py:200
  809.7 26.5 %collective-permute-done.44 = bf16[8,64,1024]{2,1,0:T(8,128)(2,1)} collective-permute-done((bf16[8,64,1024]{2,1,0:T(8,128)(2,1)S(1)}, bf16[8,64,1024]{2,1,0:T(8,128)(2,1)}, u32[]{:S(2)}, u32[]{:S(2)}) %collective-permute-start.44) | collective-permute-done | bytes 1048608 | tf_op jit(solution)/shard_map/ppermute | solution.py:200
  836.2 3.4 fusion.44
  839.8 18.9 %collective-permute-done.46 = bf16[256,2048]{1,0:T(8,128)(2,1)} collective-permute-done((bf16[256,2048]{1,0:T(8,128)(2,1)S(1)}, bf16[256,2048]{1,0:T(8,128)(2,1)}, u32[]{:S(2)}, u32[]{:S(2)}) %collective-permute-start.46) | collective-permute-done | bytes 1048608 | tf_op jit(solution)/shard_map/ppermute | solution.py:200
  864.4 16.7 %collective-permute-done.45 = bf16[8,64,1024]{2,1,0:T(8,128)(2,1)S(1)} collective-permute-done((bf16[8,64,1024]{2,1,0:T(8,128)(2,1)}, bf16[8,64,1024]{2,1,0:T(8,128)(2,1)S(1)}, u32[]{:S(2)}, u32[]{:S(2)}) %collective-permute-start.45) | collective-permute-done | bytes 1048608 | tf_op jit(solution)/shard_map/ppermute | solution.py:200
  883.7 3.9 all-to-all-start.1
  887.6 11.7 %collective-permute-done.47 = bf16[256,2048]{1,0:T(8,128)(2,1)} collective-permute-done((bf16[256,2048]{1,0:T(8,128)(2,1)S(1)}, bf16[256,2048]{1,0:T(8,128)(2,1)}, u32[]{:S(2)}, u32[]{:S(2)}) %collective-permute-start.47) | collective-permute-done | bytes 1048608 | tf_op jit(solution)/shard_map/ppermute | solution.py:200
  899.3 2.9 fusion.41
  906.4 2.9 convert_add_fusion.8
  909.3 20.1 %reduce-scatter.8.cloned.1.call-done = bf16[320,2048]{1,0:T(8,128)(2,1)} async-done(((bf16[2560,2048]{1,0:T(8,128)(2,1)}), bf16[320,2048]{1,0:T(8,128)(2,1)}) %reduce-scatter.8.cloned.1.call-update) | async-done | bytes 1310736 | tf_op jit(solution)/shard_map/reduce_scatter | solution.py:195
  929.4 5.2 fusion.15
  936.3 4.2 convert_add_fusion.1
  940.5 2.8 fusion.32
  943.3 15.5 %reduce-scatter.14.cloned.1.call-done = bf16[64,2048]{1,0:T(8,128)(2,1)} async-done(((bf16[256,2048]{1,0:T(8,128)(2,1)}), bf16[64,2048]{1,0:T(8,128)(2,1)}) %reduce-scatter.14.cloned.1.call-update) | async-done | bytes 262160 | tf_op jit(solution)/shard_map/reduce_scatter | solution.py:196
  960.6 30.4 %reduce-scatter.10.cloned.1.call-done = bf16[80,2048]{1,0:T(8,128)(2,1)} async-done(((bf16[320,2048]{1,0:T(8,128)(2,1)}), bf16[80,2048]{1,0:T(8,128)(2,1)}) %reduce-scatter.10.cloned.1.call-update) | async-done | bytes 327696 | tf_op jit(solution)/shard_map/reduce_scatter | solution.py:196
  (361 shorter events, 149.4 us)
Async XLA Ops:
  7.2 87.6 %copy-start.8 = (bf16[2,256,2048]{2,1,0:T(8,128)(2,1)S(1)}, bf16[2,256,2048]{2,1,0:T(8,128)(2,1)}, u32[]{:S(2)}) copy-start(bf16[2,256,2048]{2,1,0:T(8,128)(2,1)} %param.17) | copy-start | bytes 6291460
  7.2 44.5 %all-gather.6.cloned.1.call-start = ((), (), s32[]{:S(2)}) async-start(), calls=%async_computation.7 | async-start | bytes 1638400 | tf_op jit(solution)/shard_map/all_gather | solution.py:326
  16.1 80.8 %all-gather.10.cloned.1.call-start = ((), (), s32[]{:S(2)}) async-start(), calls=%async_computation.9 | async-start | bytes 1310720 | tf_op jit(solution)/shard_map/all_gather | solution.py:332
  51.7 107.5 %all-gather.8.cloned.1.call-start = ((), (), s32[]{:S(2)}) async-start(), calls=%async_computation.8 | async-start | bytes 11796480 | tf_op jit(solution)/shard_map/all_gather | solution.py:331
  52.4 167.9 %all-gather.12.cloned.1.call-start = ((), (), s32[]{:S(2)}) async-start(), calls=%async_computation.10 | async-start | bytes 1310720 | tf_op jit(solution)/shard_map/all_gather | solution.py:359
  52.5 42.3 %collective-permute-start = (bf16[256,2048]{1,0:T(8,128)(2,1)S(1)}, bf16[256,2048]{1,0:T(8,128)(2,1)}, u32[]{:S(2)}, u32[]{:S(2)}) collective-permute-start(bf16[256,2048]{1,0:T(8,128)(2,1)S(1)} %copy-done.29), channel_id=1, source_target_pairs={{0,1},{1,2},{2,3},{3,0},{4,5},{5,6},{6,7},{7,4},{8,9},{9,10},{10,1... | collective-permute-start | bytes 3145736 | tf_op jit(solution)/shard_map/ppermute | solution.py:200
  94.8 23.4 %collective-permute-start.1 = (bf16[256,2048]{1,0:T(8,128)(2,1)}, bf16[256,2048]{1,0:T(8,128)(2,1)S(1)}, u32[]{:S(2)}, u32[]{:S(2)}) collective-permute-start(bf16[256,2048]{1,0:T(8,128)(2,1)} %collective-permute-done), channel_id=1, source_target_pairs={{0,1},{1,2},{2,3},{3,0},{4,5},{5,6},{6,7},{7,4},{8,9},{9,10},{10,1... | collective-permute-start | bytes 3145736 | tf_op jit(solution)/shard_map/ppermute | solution.py:200
  167.8 114.3 %all-gather.14.cloned.1.call-start = ((), (), s32[]{:S(2)}) async-start(), calls=%async_computation.11 | async-start | bytes 9437184 | tf_op jit(solution)/shard_map/all_gather | solution.py:340
  168.4 578.7 %reduce-scatter.6.cloned.1.call-start = ((), (), s32[]{:S(2)}) async-start(), calls=%async_computation.12 | async-start | bytes 1310720 | tf_op jit(solution)/shard_map/reduce_scatter | solution.py:465
  176.9 42.4 %collective-permute-start.2 = (bf16[256,2048]{1,0:T(8,128)(2,1)S(1)}, bf16[256,2048]{1,0:T(8,128)(2,1)S(1)}, u32[]{:S(2)}, u32[]{:S(2)}) collective-permute-start(bf16[256,2048]{1,0:T(8,128)(2,1)S(1)} %copy-done.32), channel_id=1, source_target_pairs={{0,1},{1,2},{2,3},{3,0},{4,5},{5,6},{6,7},{7,4},{8,9},{9,10},{10,1... | collective-permute-start | bytes 3145736 | tf_op jit(solution)/shard_map/ppermute | solution.py:200
  178.4 69.5 %copy-start.10 = (bf16[2,256,2048]{2,1,0:T(8,128)(2,1)S(1)}, bf16[2,256,2048]{2,1,0:T(8,128)(2,1)}, u32[]{:S(2)}) copy-start(bf16[2,256,2048]{2,1,0:T(8,128)(2,1)} %param.18) | copy-start | bytes 6291460
  220.3 27.0 %collective-permute-start.3 = (bf16[8,64,1024]{2,1,0:T(8,128)(2,1)}, bf16[8,64,1024]{2,1,0:T(8,128)(2,1)}, u32[]{:S(2)}, u32[]{:S(2)}) collective-permute-start(bf16[8,64,1024]{2,1,0:T(8,128)(2,1)} %bitcast.2), channel_id=1, source_target_pairs={{0,1},{1,2},{2,3},{3,0},{4,5},{5,6},{6,7},{7,4},{8,9},{9,10},{10,1... | collective-permute-start | bytes 3145736 | tf_op jit(solution)/shard_map/ppermute | solution.py:200
  247.3 26.4 %collective-permute-start.4 = (bf16[8,64,1024]{2,1,0:T(8,128)(2,1)}, bf16[8,64,1024]{2,1,0:T(8,128)(2,1)}, u32[]{:S(2)}, u32[]{:S(2)}) collective-permute-start(bf16[8,64,1024]{2,1,0:T(8,128)(2,1)} %collective-permute-done.3), channel_id=1, source_target_pairs={{0,1},{1,2},{2,3},{3,0},{4,5},{5,6},{6,7},{7,4},{8,9},{9,10},{10,1... | collective-permute-start | bytes 3145736 | tf_op jit(solution)/shard_map/ppermute | solution.py:200
  249.4 43.5 %collective-permute-start.5 = (bf16[256,2048]{1,0:T(8,128)(2,1)}, bf16[256,2048]{1,0:T(8,128)(2,1)}, u32[]{:S(2)}, u32[]{:S(2)}) collective-permute-start(bf16[256,2048]{1,0:T(8,128)(2,1)} %get-tuple-element.100), channel_id=1, source_target_pairs={{0,8},{4,12},{8,0},{12,4},{16,24},{20,28},{24,16},{28,20},{1,9},{5... | collective-permute-start | bytes 3145736 | tf_op jit(solution)/shard_map/ppermute | solution.py:241
  250.9 42.0 %collective-permute-start.6 = (bf16[256,2048]{1,0:T(8,128)(2,1)}, bf16[256,2048]{1,0:T(8,128)(2,1)}, u32[]{:S(2)}, u32[]{:S(2)}) collective-permute-start(bf16[256,2048]{1,0:T(8,128)(2,1)} %get-tuple-element.101), channel_id=1, source_target_pairs={{0,16},{4,20},{8,24},{12,28},{16,0},{20,4},{24,8},{28,12},{1,17},{... | collective-permute-start | bytes 3145736 | tf_op jit(solution)/shard_map/ppermute | solution.py:241
  292.9 26.4 %collective-permute-start.13 = (bf16[256,2048]{1,0:T(8,128)(2,1)}, bf16[256,2048]{1,0:T(8,128)(2,1)}, u32[]{:S(2)}, u32[]{:S(2)}) collective-permute-start(bf16[256,2048]{1,0:T(8,128)(2,1)} %collective-permute-done.5), channel_id=1, source_target_pairs={{0,16},{4,20},{8,24},{12,28},{16,0},{20,4},{24,8},{28,12},{1,17},{... | collective-permute-start | bytes 3145736 | tf_op jit(solution)/shard_map/ppermute | solution.py:241
  294.4 29.5 %collective-permute-start.14 = (bf16[256,2048]{1,0:T(8,128)(2,1)}, bf16[256,2048]{1,0:T(8,128)(2,1)S(1)}, u32[]{:S(2)}, u32[]{:S(2)}) collective-permute-start(bf16[256,2048]{1,0:T(8,128)(2,1)} %collective-permute-done.6), channel_id=1, source_target_pairs={{0,8},{4,12},{8,0},{12,4},{16,24},{20,28},{24,16},{28,20},{1,9},{5... | collective-permute-start | bytes 3145736 | tf_op jit(solution)/shard_map/ppermute | solution.py:241
  296.5 44.4 %collective-permute-start.15 = (bf16[256,2048]{1,0:T(8,128)(2,1)}, bf16[256,2048]{1,0:T(8,128)(2,1)S(1)}, u32[]{:S(2)}, u32[]{:S(2)}) collective-permute-start(bf16[256,2048]{1,0:T(8,128)(2,1)} %get-tuple-element.100), channel_id=1, source_target_pairs={{0,16},{4,20},{8,24},{12,28},{16,0},{20,4},{24,8},{28,12},{1,17},{... | collective-permute-start | bytes 3145736 | tf_op jit(solution)/shard_map/ppermute | solution.py:241
  300.8 43.5 %collective-permute-start.16 = (bf16[256,2048]{1,0:T(8,128)(2,1)}, bf16[256,2048]{1,0:T(8,128)(2,1)S(1)}, u32[]{:S(2)}, u32[]{:S(2)}) collective-permute-start(bf16[256,2048]{1,0:T(8,128)(2,1)} %get-tuple-element.101), channel_id=1, source_target_pairs={{0,8},{4,12},{8,0},{12,4},{16,24},{20,28},{24,16},{28,20},{1,9},{5... | collective-permute-start | bytes 3145736 | tf_op jit(solution)/shard_map/ppermute | solution.py:241
  345.4 95.2 %collective-permute-start.17 = (bf16[2048,2048]{1,0:T(8,128)(2,1)}, bf16[2048,2048]{1,0:T(8,128)(2,1)}, u32[]{:S(2)}, u32[]{:S(2)}) collective-permute-start(bf16[2048,2048]{1,0:T(8,128)(2,1)} %constant_dynamic-update-slice_fusion.8), channel_id=1, source_target_pairs={{0,4},{4,0},{8,12},{12,8},{16,20},{20,16},{24,28},{28,24},{1,5},{5... | collective-permute-start | bytes 25165832 | tf_op jit(solution)/shard_map/ppermute | solution.py:241
  346.3 28.3 %collective-permute-start.18 = (bf16[8,64,1024]{2,1,0:T(8,128)(2,1)}, bf16[8,64,1024]{2,1,0:T(8,128)(2,1)S(1)}, u32[]{:S(2)}, u32[]{:S(2)}) collective-permute-start(bf16[8,64,1024]{2,1,0:T(8,128)(2,1)} %collective-permute-done.4), channel_id=1, source_target_pairs={{0,1},{1,2},{2,3},{3,0},{4,5},{5,6},{6,7},{7,4},{8,9},{9,10},{10,1... | collective-permute-start | bytes 3145736 | tf_op jit(solution)/shard_map/ppermute | solution.py:200
  352.6 25.5 %collective-permute-start.7 = (bf16[256,2048]{1,0:T(8,128)(2,1)}, bf16[256,2048]{1,0:T(8,128)(2,1)S(1)}, u32[]{:S(2)}, u32[]{:S(2)}) collective-permute-start(bf16[256,2048]{1,0:T(8,128)(2,1)} %get-tuple-element.181), channel_id=1, source_target_pairs={{0,8},{4,12},{8,0},{12,4},{16,24},{20,28},{24,16},{28,20},{1,9},{5... | collective-permute-start | bytes 3145736 | tf_op jit(solution)/shard_map/ppermute | solution.py:241
  354.1 26.2 %collective-permute-start.9 = (bf16[256,2048]{1,0:T(8,128)(2,1)}, bf16[256,2048]{1,0:T(8,128)(2,1)S(1)}, u32[]{:S(2)}, u32[]{:S(2)}) collective-permute-start(bf16[256,2048]{1,0:T(8,128)(2,1)} %get-tuple-element.180), channel_id=1, source_target_pairs={{0,16},{4,20},{8,24},{12,28},{16,0},{20,4},{24,8},{28,12},{1,17},{... | collective-permute-start | bytes 3145736 | tf_op jit(solution)/shard_map/ppermute | solution.py:241
  356.5 84.2 %copy-start.16 = (bf16[1024,2048]{1,0:T(8,128)(2,1)}, bf16[1024,2048]{1,0:T(8,128)(2,1)S(1)}, u32[]{:S(2)}) copy-start(bf16[1024,2048]{1,0:T(8,128)(2,1)S(1)} %constant_dynamic-update-slice_fusion.28) | copy-start | bytes 12582916
  374.7 50.6 %collective-permute-start.11 = (bf16[256,2048]{1,0:T(8,128)(2,1)}, bf16[256,2048]{1,0:T(8,128)(2,1)S(1)}, u32[]{:S(2)}, u32[]{:S(2)}) collective-permute-start(bf16[256,2048]{1,0:T(8,128)(2,1)} %get-tuple-element.181), channel_id=1, source_target_pairs={{0,16},{4,20},{8,24},{12,28},{16,0},{20,4},{24,8},{28,12},{1,17},{... | collective-permute-start | bytes 3145736 | tf_op jit(solution)/shard_map/ppermute | solution.py:241
  376.2 49.2 %collective-permute-start.12 = (bf16[256,2048]{1,0:T(8,128)(2,1)}, bf16[256,2048]{1,0:T(8,128)(2,1)S(1)}, u32[]{:S(2)}, u32[]{:S(2)}) collective-permute-start(bf16[256,2048]{1,0:T(8,128)(2,1)} %get-tuple-element.180), channel_id=1, source_target_pairs={{0,8},{4,12},{8,0},{12,4},{16,24},{20,28},{24,16},{28,20},{1,9},{5... | collective-permute-start | bytes 3145736 | tf_op jit(solution)/shard_map/ppermute | solution.py:241
  378.1 46.1 %collective-permute-start.8 = (bf16[256,2048]{1,0:T(8,128)(2,1)S(1)}, bf16[256,2048]{1,0:T(8,128)(2,1)S(1)}, u32[]{:S(2)}, u32[]{:S(2)}) collective-permute-start(bf16[256,2048]{1,0:T(8,128)(2,1)S(1)} %collective-permute-done.7), channel_id=1, source_target_pairs={{0,16},{4,20},{8,24},{12,28},{16,0},{20,4},{24,8},{28,12},{1,17},{... | collective-permute-start | bytes 3145736 | tf_op jit(solution)/shard_map/ppermute | solution.py:241
  380.3 44.1 %collective-permute-start.10 = (bf16[256,2048]{1,0:T(8,128)(2,1)S(1)}, bf16[256,2048]{1,0:T(8,128)(2,1)S(1)}, u32[]{:S(2)}, u32[]{:S(2)}) collective-permute-start(bf16[256,2048]{1,0:T(8,128)(2,1)S(1)} %collective-permute-done.9), channel_id=1, source_target_pairs={{0,8},{4,12},{8,0},{12,4},{16,24},{20,28},{24,16},{28,20},{1,9},{5... | collective-permute-start | bytes 3145736 | tf_op jit(solution)/shard_map/ppermute | solution.py:241
  424.2 2.7 collective-permute-start.19
  424.4 3.9 collective-permute-start.21
  425.2 6.1 collective-permute-start.20
  425.4 7.4 collective-permute-start.22
  426.9 6.4 collective-permute-start.23
  428.4 7.5 collective-permute-start.24
  431.4 4.7 collective-permute-start.25
  432.9 4.5 collective-permute-start.26
  476.8 89.0 %copy-start.14 = (bf16[2048,1024]{1,0:T(8,128)(2,1)}, bf16[2048,1024]{1,0:T(8,128)(2,1)S(1)}, u32[]{:S(2)}) copy-start(bf16[2048,1024]{1,0:T(8,128)(2,1)S(1)} %get-tuple-element.109) | copy-start | bytes 12582916
  506.6 32.7 %collective-permute-start.27 = (bf16[1024,2048]{1,0:T(8,128)(2,1)}, bf16[1024,2048]{1,0:T(8,128)(2,1)}, u32[]{:S(2)}, u32[]{:S(2)}) collective-permute-start(bf16[1024,2048]{1,0:T(8,128)(2,1)} %convolution_convert_fusion.5), channel_id=1, source_target_pairs={{0,4},{4,0},{8,12},{12,8},{16,20},{20,16},{24,28},{28,24},{1,5},{5... | collective-permute-start | bytes 12582920 | tf_op jit(solution)/shard_map/ppermute | solution.py:241
  512.9 33.8 %collective-permute-start.28 = (bf16[1024,2048]{1,0:T(8,128)(2,1)}, bf16[1024,2048]{1,0:T(8,128)(2,1)}, u32[]{:S(2)}, u32[]{:S(2)}) collective-permute-start(bf16[1024,2048]{1,0:T(8,128)(2,1)} %convolution_convert_fusion.4), channel_id=1, source_target_pairs={{0,4},{4,0},{8,12},{12,8},{16,20},{20,16},{24,28},{28,24},{1,5},{5... | collective-permute-start | bytes 12582920 | tf_op jit(solution)/shard_map/ppermute | solution.py:241
  525.4 32.3 %collective-permute-start.33 = (bf16[1024,2048]{1,0:T(8,128)(2,1)}, bf16[1024,2048]{1,0:T(8,128)(2,1)}, u32[]{:S(2)}, u32[]{:S(2)}) collective-permute-start(bf16[1024,2048]{1,0:T(8,128)(2,1)} %convolution_convert_fusion.3), channel_id=1, source_target_pairs={{0,4},{4,0},{8,12},{12,8},{16,20},{20,16},{24,28},{28,24},{1,5},{5... | collective-permute-start | bytes 12582920 | tf_op jit(solution)/shard_map/ppermute | solution.py:241
  525.6 69.8 %collective-permute-start.34 = (bf16[1024,2048]{1,0:T(8,128)(2,1)}, bf16[1024,2048]{1,0:T(8,128)(2,1)}, u32[]{:S(2)}, u32[]{:S(2)}) collective-permute-start(bf16[1024,2048]{1,0:T(8,128)(2,1)} %convolution_convert_fusion.2), channel_id=1, source_target_pairs={{0,4},{4,0},{8,12},{12,8},{16,20},{20,16},{24,28},{28,24},{1,5},{5... | collective-permute-start | bytes 12582920 | tf_op jit(solution)/shard_map/ppermute | solution.py:241
  555.3 49.2 %collective-permute-start.29 = (bf16[256,2048]{1,0:T(8,128)(2,1)}, bf16[256,2048]{1,0:T(8,128)(2,1)}, u32[]{:S(2)}, u32[]{:S(2)}) collective-permute-start(bf16[256,2048]{1,0:T(8,128)(2,1)} %get-tuple-element.174), channel_id=1, source_target_pairs={{0,8},{4,12},{8,0},{12,4},{16,24},{20,28},{24,16},{28,20},{1,9},{5... | collective-permute-start | bytes 3145736 | tf_op jit(solution)/shard_map/ppermute | solution.py:241
  555.9 50.2 %collective-permute-start.30 = (bf16[256,2048]{1,0:T(8,128)(2,1)}, bf16[256,2048]{1,0:T(8,128)(2,1)}, u32[]{:S(2)}, u32[]{:S(2)}) collective-permute-start(bf16[256,2048]{1,0:T(8,128)(2,1)} %get-tuple-element.173), channel_id=1, source_target_pairs={{0,8},{4,12},{8,0},{12,4},{16,24},{20,28},{24,16},{28,20},{1,9},{5... | collective-permute-start | bytes 3145736 | tf_op jit(solution)/shard_map/ppermute | solution.py:241
  557.3 50.6 %collective-permute-start.31 = (bf16[256,2048]{1,0:T(8,128)(2,1)}, bf16[256,2048]{1,0:T(8,128)(2,1)S(1)}, u32[]{:S(2)}, u32[]{:S(2)}) collective-permute-start(bf16[256,2048]{1,0:T(8,128)(2,1)} %get-tuple-element.172), channel_id=1, source_target_pairs={{0,16},{4,20},{8,24},{12,28},{16,0},{20,4},{24,8},{28,12},{1,17},{... | collective-permute-start | bytes 3145736 | tf_op jit(solution)/shard_map/ppermute | solution.py:241
  557.7 50.6 %collective-permute-start.32 = (bf16[256,2048]{1,0:T(8,128)(2,1)}, bf16[256,2048]{1,0:T(8,128)(2,1)}, u32[]{:S(2)}, u32[]{:S(2)}) collective-permute-start(bf16[256,2048]{1,0:T(8,128)(2,1)} %get-tuple-element.171), channel_id=1, source_target_pairs={{0,16},{4,20},{8,24},{12,28},{16,0},{20,4},{24,8},{28,12},{1,17},{... | collective-permute-start | bytes 3145736 | tf_op jit(solution)/shard_map/ppermute | solution.py:241
  609.9 24.1 %collective-permute-start.36 = (bf16[256,2048]{1,0:T(8,128)(2,1)S(1)}, bf16[256,2048]{1,0:T(8,128)(2,1)S(1)}, u32[]{:S(2)}, u32[]{:S(2)}) collective-permute-start(bf16[256,2048]{1,0:T(8,128)(2,1)S(1)} %convert_add_fusion.15), channel_id=1, source_target_pairs={{0,8},{4,12},{8,0},{12,4},{16,24},{20,28},{24,16},{28,20},{1,9},{5... | collective-permute-start | bytes 3145736 | tf_op jit(solution)/shard_map/ppermute | solution.py:241
  610.6 23.9 %collective-permute-start.35 = (bf16[256,2048]{1,0:T(8,128)(2,1)S(1)}, bf16[256,2048]{1,0:T(8,128)(2,1)S(1)}, u32[]{:S(2)}, u32[]{:S(2)}) collective-permute-start(bf16[256,2048]{1,0:T(8,128)(2,1)S(1)} %convert_add_fusion.17), channel_id=1, source_target_pairs={{0,16},{4,20},{8,24},{12,28},{16,0},{20,4},{24,8},{28,12},{1,17},{... | collective-permute-start | bytes 3145736 | tf_op jit(solution)/shard_map/ppermute | solution.py:241
  639.1 26.2 %collective-permute-start.37 = (bf16[256,2048]{1,0:T(8,128)(2,1)S(1)}, bf16[256,2048]{1,0:T(8,128)(2,1)S(1)}, u32[]{:S(2)}, u32[]{:S(2)}) collective-permute-start(bf16[256,2048]{1,0:T(8,128)(2,1)S(1)} %copy-done.41), channel_id=1, source_target_pairs={{0,8},{4,12},{8,0},{12,4},{16,24},{20,28},{24,16},{28,20},{1,9},{5... | collective-permute-start | bytes 3145736 | tf_op jit(solution)/shard_map/ppermute | solution.py:241
  640.6 44.3 %collective-permute-start.38 = (bf16[256,2048]{1,0:T(8,128)(2,1)S(1)}, bf16[256,2048]{1,0:T(8,128)(2,1)S(1)}, u32[]{:S(2)}, u32[]{:S(2)}) collective-permute-start(bf16[256,2048]{1,0:T(8,128)(2,1)S(1)} %copy-done.40), channel_id=1, source_target_pairs={{0,8},{4,12},{8,0},{12,4},{16,24},{20,28},{24,16},{28,20},{1,9},{5... | collective-permute-start | bytes 3145736 | tf_op jit(solution)/shard_map/ppermute | solution.py:241
  641.2 45.0 %collective-permute-start.39 = (bf16[256,2048]{1,0:T(8,128)(2,1)S(1)}, bf16[256,2048]{1,0:T(8,128)(2,1)S(1)}, u32[]{:S(2)}, u32[]{:S(2)}) collective-permute-start(bf16[256,2048]{1,0:T(8,128)(2,1)S(1)} %copy-done.39), channel_id=1, source_target_pairs={{0,16},{4,20},{8,24},{12,28},{16,0},{20,4},{24,8},{28,12},{1,17},{... | collective-permute-start | bytes 3145736 | tf_op jit(solution)/shard_map/ppermute | solution.py:241
  642.7 44.9 %collective-permute-start.40 = (bf16[256,2048]{1,0:T(8,128)(2,1)S(1)}, bf16[256,2048]{1,0:T(8,128)(2,1)S(1)}, u32[]{:S(2)}, u32[]{:S(2)}) collective-permute-start(bf16[256,2048]{1,0:T(8,128)(2,1)S(1)} %copy-done.38), channel_id=1, source_target_pairs={{0,16},{4,20},{8,24},{12,28},{16,0},{20,4},{24,8},{28,12},{1,17},{... | collective-permute-start | bytes 3145736 | tf_op jit(solution)/shard_map/ppermute | solution.py:241
  720.2 142.4 %reduce-scatter.12.cloned.1.call-start = ((), (), s32[]{:S(2)}) async-start(), calls=%async_computation.15 | async-start | bytes 9437184 | tf_op jit(solution)/shard_map/reduce_scatter | solution.py:195
  730.9 198.4 %reduce-scatter.8.cloned.1.call-start = ((), (), s32[]{:S(2)}) async-start(), calls=%async_computation.13 | async-start | bytes 11796480 | tf_op jit(solution)/shard_map/reduce_scatter | solution.py:195
  780.6 178.2 %reduce-scatter.14.cloned.1.call-start = ((), (), s32[]{:S(2)}) async-start(), calls=%async_computation.16 | async-start | bytes 1310720 | tf_op jit(solution)/shard_map/reduce_scatter | solution.py:196
  782.0 24.6 %collective-permute-start.43 = (bf16[8,64,1024]{2,1,0:T(8,128)(2,1)S(1)}, bf16[8,64,1024]{2,1,0:T(8,128)(2,1)S(1)}, u32[]{:S(2)}, u32[]{:S(2)}) collective-permute-start(bf16[8,64,1024]{2,1,0:T(8,128)(2,1)S(1)} %dynamic-slice_bitcast_fusion.1), channel_id=1, source_target_pairs={{0,1},{1,2},{2,3},{3,0},{4,5},{5,6},{6,7},{7,4},{8,9},{9,10},{10,1... | collective-permute-start | bytes 3145736 | tf_op jit(solution)/shard_map/ppermute | solution.py:200
  808.2 28.1 %collective-permute-start.44 = (bf16[8,64,1024]{2,1,0:T(8,128)(2,1)S(1)}, bf16[8,64,1024]{2,1,0:T(8,128)(2,1)}, u32[]{:S(2)}, u32[]{:S(2)}) collective-permute-start(bf16[8,64,1024]{2,1,0:T(8,128)(2,1)S(1)} %fusion.45), channel_id=1, source_target_pairs={{0,1},{1,2},{2,3},{3,0},{4,5},{5,6},{6,7},{7,4},{8,9},{9,10},{10,1... | collective-permute-start | bytes 3145736 | tf_op jit(solution)/shard_map/ppermute | solution.py:200
  809.6 49.1 %collective-permute-start.46 = (bf16[256,2048]{1,0:T(8,128)(2,1)S(1)}, bf16[256,2048]{1,0:T(8,128)(2,1)}, u32[]{:S(2)}, u32[]{:S(2)}) collective-permute-start(bf16[256,2048]{1,0:T(8,128)(2,1)S(1)} %dynamic-slice_bitcast_fusion), channel_id=1, source_target_pairs={{0,1},{1,2},{2,3},{3,0},{4,5},{5,6},{6,7},{7,4},{8,9},{9,10},{10,1... | collective-permute-start | bytes 3145736 | tf_op jit(solution)/shard_map/ppermute | solution.py:200
  839.7 41.4 %collective-permute-start.45 = (bf16[8,64,1024]{2,1,0:T(8,128)(2,1)}, bf16[8,64,1024]{2,1,0:T(8,128)(2,1)S(1)}, u32[]{:S(2)}, u32[]{:S(2)}) collective-permute-start(bf16[8,64,1024]{2,1,0:T(8,128)(2,1)} %fusion.44), channel_id=1, source_target_pairs={{0,1},{1,2},{2,3},{3,0},{4,5},{5,6},{6,7},{7,4},{8,9},{9,10},{10,1... | collective-permute-start | bytes 3145736 | tf_op jit(solution)/shard_map/ppermute | solution.py:200
  860.6 38.7 %collective-permute-start.47 = (bf16[256,2048]{1,0:T(8,128)(2,1)S(1)}, bf16[256,2048]{1,0:T(8,128)(2,1)}, u32[]{:S(2)}, u32[]{:S(2)}) collective-permute-start(bf16[256,2048]{1,0:T(8,128)(2,1)S(1)} %fusion.42), channel_id=1, source_target_pairs={{0,1},{1,2},{2,3},{3,0},{4,5},{5,6},{6,7},{7,4},{8,9},{9,10},{10,1... | collective-permute-start | bytes 3145736 | tf_op jit(solution)/shard_map/ppermute | solution.py:200
  860.7 43.7 %collective-permute-start.42 = (bf16[256,2048]{1,0:T(8,128)(2,1)S(1)}, bf16[256,2048]{1,0:T(8,128)(2,1)}, u32[]{:S(2)}, u32[]{:S(2)}) collective-permute-start(bf16[256,2048]{1,0:T(8,128)(2,1)S(1)} %copy-done.28), channel_id=1, source_target_pairs={{0,8},{4,12},{8,0},{12,4},{16,24},{20,28},{24,16},{28,20},{1,9},{5... | collective-permute-start | bytes 3145736 | tf_op jit(solution)/shard_map/ppermute | solution.py:241
  862.7 43.7 %collective-permute-start.41 = (bf16[256,2048]{1,0:T(8,128)(2,1)}, bf16[256,2048]{1,0:T(8,128)(2,1)}, u32[]{:S(2)}, u32[]{:S(2)}) collective-permute-start(bf16[256,2048]{1,0:T(8,128)(2,1)} %convert_add_fusion.11), channel_id=1, source_target_pairs={{0,16},{4,20},{8,24},{12,28},{16,0},{20,4},{24,8},{28,12},{1,17},{... | collective-permute-start | bytes 3145736 | tf_op jit(solution)/shard_map/ppermute | solution.py:241
  883.7 50.9 %all-to-all-start.1 = ((bf16[8,64,1024]{2,1,0:T(8,128)(2,1)}), bf16[8,64,1024]{2,1,0:T(8,128)(2,1)S(1)}, u32[]{:S(2)}, u32[]{:S(2)}) async-start(bf16[8,64,1024]{2,1,0:T(8,128)(2,1)} %fusion.43), calls=%async_computation.6 | async-start | bytes 2097152 | tf_op jit(solution)/shard_map/all_to_all | solution.py:440
  887.6 103.4 %reduce-scatter.10.cloned.1.call-start = ((), (), s32[]{:S(2)}) async-start(), calls=%async_computation.14 | async-start | bytes 1638400 | tf_op jit(solution)/shard_map/reduce_scatter | solution.py:196
  902.2 34.1 %collective-permute-start.48 = (bf16[256,2048]{1,0:T(8,128)(2,1)}, bf16[256,2048]{1,0:T(8,128)(2,1)}, u32[]{:S(2)}, u32[]{:S(2)}) collective-permute-start(bf16[256,2048]{1,0:T(8,128)(2,1)} %fusion.41), channel_id=1, source_target_pairs={{0,1},{1,2},{2,3},{3,0},{4,5},{5,6},{6,7},{7,4},{8,9},{9,10},{10,1... | collective-permute-start | bytes 3145736 | tf_op jit(solution)/shard_map/ppermute | solution.py:200
  (57 other events, 719.7 us)
Sparse Core Ops, SparseCore 0:
  16.2 35.3 all-gather.5
  53.2 42.5 all-gather.9
  97.7 61.4 all-gather.7
  167.9 41.6 all-gather.11
  211.3 70.7 all-gather.13
  720.3 25.3 reduce-scatter.5
  749.6 69.9 reduce-scatter.11
  823.1 106.2 reduce-scatter.7
  931.6 27.1 reduce-scatter.13
  961.1 29.8 reduce-scatter.9

commit v3 on v2

--- a/solution.py
+++ b/solution.py
@@ -169,6 +169,78 @@
     )(first, ends, queries, kv_window, norms, grads)
 
 
+def middle_kernel(count, *refs):
+    blocks, backs = refs[:count], refs[count : 2 * count]
+    up_ref, bias_ref = refs[2 * count], refs[2 * count + 1]
+    hiddens = refs[2 * count + 2 : 3 * count + 2]
+    pres = refs[3 * count + 2 :]
+    root = math.sqrt(2.0 / math.pi)
+    for block, back, hidden, pre in zip(blocks, backs, hiddens, pres):
+        act = jnp.dot(block[...], up_ref[...], preferred_element_type=F32) + bias_ref[...]
+        square = act * act
+        bent = jnp.tanh(root * act * (1.0 + 0.044715 * square))
+        upper = 0.5 + 0.5 * bent
+        hidden[...] = (act * upper).astype(BF16)
+        slope = upper + (0.5 * root) * act * (1.0 - bent * bent) * (1.0 + (3 * 0.044715) * square)
+        pre[...] = (back[...].astype(F32) * slope).astype(BF16)
+
+
+def middle_layer(blocks, backs, up_part, bias, tile=256):
+    count = len(blocks)
+    size, width = blocks[0].shape
+    units = up_part.shape[1]
+    tile = min(tile, units)
+    one = pl.Buffered(buffer_count=1)
+    whole = pl.BlockSpec((size, width), lambda j: (0, 0), pipeline_mode=one)
+    slab = pl.BlockSpec((size, tile), lambda j: (0, j))
+    out = pl.pallas_call(
+        functools.partial(middle_kernel, count),
+        out_shape=[jax.ShapeDtypeStruct((size, units), BF16)] * (2 * count),
+        grid=(units // tile,),
+        in_specs=[whole] * count
+        + [slab] * count
+        + [pl.BlockSpec((width, tile), lambda j: (0, j)), pl.BlockSpec((1, tile), lambda j: (0, j))],
+        out_specs=[slab] * (2 * count),
+        compiler_params=pltpu.CompilerParams(vmem_limit_bytes=48 * 2**20),
+        cost_estimate=pl.CostEstimate(
+            flops=2 * count * size * width * units,
+            transcendentals=count * size * units,
+            bytes_accessed=2 * (count * size * (width + 3 * units) + width * units),
+        ),
+    )(*blocks, *backs, up_part, bias.reshape(1, units))
+    return list(out[:count]), list(out[count:])
+
+
+def weight_kernel(count, *refs):
+    lefts, rights, out = refs[:count], refs[count : 2 * count], refs[2 * count]
+    total = dot_tn(lefts[0][...], rights[0][...])
+    for left, right in zip(lefts[1:], rights[1:]):
+        total += dot_tn(left[...], right[...])
+    out[...] = total.astype(BF16)
+
+
+def weight_grad(lefts, rights, tile=256):
+    count = len(lefts)
+    size, height = lefts[0].shape
+    breadth = rights[0].shape[1]
+    tile = min(tile, height)
+    one = pl.Buffered(buffer_count=1)
+    return pl.pallas_call(
+        functools.partial(weight_kernel, count),
+        out_shape=jax.ShapeDtypeStruct((height, breadth), BF16),
+        grid=(height // tile,),
+        in_specs=[pl.BlockSpec((size, tile), lambda i: (0, i))] * count
+        + [pl.BlockSpec((size, breadth), lambda i: (0, 0), pipeline_mode=one)] * count,
+        out_specs=pl.BlockSpec((tile, breadth), lambda i: (i, 0)),
+        compiler_params=pltpu.CompilerParams(vmem_limit_bytes=52 * 2**20),
+        cost_estimate=pl.CostEstimate(
+            flops=2 * count * size * height * breadth,
+            transcendentals=0,
+            bytes_accessed=2 * (count * size * (height + breadth) + height * breadth),
+        ),
+    )(*lefts, *rights)
+
+
 def norm_stats(values):
     average = jnp.mean(values, axis=-1, keepdims=True)
     centered = values - average
@@ -212,63 +284,53 @@
     return whole
 
 
-def ring_scatter(terms, count):
-    me = lax.axis_index("fsdp")
-
-    def term(step):
-        return lax.dynamic_index_in_dim(
-            terms, lax.rem(me - 1 - step + 2 * count, count), 0, keepdims=False
-        ).astype(F32)
-
-    total = term(0)
-    for step in range(1, count):
-        total = shift(total.astype(BF16), count).astype(F32) + term(step)
-    return total
+class Ring:
+    def __init__(self, terms, axis, count):
+        self.terms, self.axis, self.count, self.step = terms, axis, count, 0
+        self.total = self.term()
+
+    def term(self):
+        place = lax.rem(lax.axis_index("fsdp") - 1 - self.step + 2 * self.count, self.count)
+        return lax.dynamic_index_in_dim(self.terms, place, self.axis, keepdims=False).astype(F32)
+
+    def go(self, steps, ahead):
+        for _ in range(steps):
+            if self.step + 1 < self.count:
+                self.step += 1
+                self.total = shift(self.total.astype(BF16), self.count).astype(F32) + self.term()
+        self.total, ahead = tie(self.total, ahead)
+        return ahead
+
+    def finish(self):
+        while self.step + 1 < self.count:
+            self.step += 1
+            self.total = shift(self.total.astype(BF16), self.count).astype(F32) + self.term()
+        return self.total
 
 
 class Plane:
     def __init__(self, count):
         self.count = count
-        self.bits = [1 << i for i in range(1, count.bit_length() - 1)]
-        self.orders = (self.bits, self.bits[::-1])
-        chips = range(0, count, 2)
-        far = [(h, o) for h in (0, 1) for o in chips if o & self.orders[h][0]]
-        near = [(h, o) for h in (0, 1) for o in chips if not o & self.orders[h][0]]
-        self.keys = far + near
-        self.n_far = len(far)
+        bits = [1 << i for i in range(1, count.bit_length() - 1)]
+        self.orders = (bits, bits[::-1])
+        self.steps = len(bits)
 
     def swap(self, block, bit):
         return lax.ppermute(block, "dp", [(i, i ^ bit) for i in range(self.count)])
 
-    def gather_step(self, held, step):
-        got = {}
-        for (half, offset), piece in held.items():
-            bit = self.orders[half][step]
-            got[half, offset | bit] = self.swap(piece, bit)
-        return got
-
-    def lay(self, held):
-        return jnp.concatenate([held[key] for key in self.keys])
-
-    def cross(self, held):
-        return {key: self.swap(piece, 1) for key, piece in held.items()}
-
-    def split(self, rows, keys):
-        size = rows.shape[0] // len(keys)
-        return {key: rows[i * size : (i + 1) * size] for i, key in enumerate(keys)}
-
-    def scatter_step(self, held, step):
-        kept = {}
-        for (half, offset), piece in held.items():
-            bit = self.orders[half][step]
-            if not offset & bit:
-                got = self.swap(held[half, offset | bit], bit).astype(F32)
-                kept[half, offset] = piece.astype(F32) + got
-        return kept
-
-
-def narrow(held):
-    return {key: piece.astype(BF16) for key, piece in held.items()}
+    def across(self, halves, step):
+        return [self.swap(half, order[step]) for half, order in zip(halves, self.orders)]
+
+    def grow(self, halves, step):
+        return [jnp.concatenate(pair) for pair in zip(halves, self.across(halves, step))]
+
+    def cross(self, halves):
+        return [self.swap(half, 1) for half in halves]
+
+    def fold(self, halves, step):
+        size = halves[0].shape[0] // 2
+        got = self.across([half[size:].astype(BF16) for half in halves], step)
+        return [half[:size].astype(F32) + there.astype(F32) for half, there in zip(halves, got)]
 
 
 def make_local(n_dp, n_z):
@@ -312,8 +374,11 @@
             mlp_shift,
         )
         sizes = [v.shape[0] for v in small]
-        starts = [sum(sizes[:i]) for i in range(len(sizes))]
-        small_row = jnp.concatenate(small)
+        rooms = [-(-size // 128) * 128 for size in sizes]
+        starts = [sum(rooms[:i]) for i in range(len(rooms))]
+        small_row = jnp.concatenate(
+            [jnp.pad(v, (0, room - size)) for v, size, room in zip(small, sizes, rooms)]
+        )
         kv_lines = kv_weight.size // width
         filled = own + kv_lines + -(-small_row.shape[0] // width)
         lines = -(-filled // 16) * 16
@@ -323,27 +388,33 @@
             [query_weight, kv_weight.reshape(kv_lines, width), small_row.reshape(-1, width)]
         )
 
+        half = rows // 2
+        grad_low = cotangent.reshape(rows, width)
+
         packed = lax.all_gather(packed, "fsdp", axis=0, tiled=True)
+        grad_near = [grad_low[:half], grad_low[half:]]
+        for step in range(plane.steps - 1):
+            grad_near = plane.grow(grad_near, step)
         up_cols = lax.all_to_all(up_weight, "dp", 1, 0, tiled=True).reshape(n_dp, own, ff_own)
-        packed, up_cols, down_weight, out_weight, cotangent = tie(
-            packed, up_cols, down_weight, out_weight, cotangent
-        )
+        packed, up_cols, down_weight, out_weight = tie(packed, up_cols, down_weight, out_weight)
+
         packed = lax.all_gather(packed, "dp", axis=0, tiled=True)
-        full_o = lax.all_gather(out_weight, "fsdp", axis=0, tiled=True)
+        out_pieces = [out_weight]
+        while len(out_pieces) < n_z:
+            out_pieces.append(shift(out_pieces[-1], n_z))
+        out_pieces[-1], down_weight = tie(out_pieces[-1], down_weight)
+        full_o = put_in_order(out_pieces, n_z)
         down_pieces = [down_weight]
         while len(down_pieces) < min(3, n_z):
             down_pieces.append(shift(down_pieces[-1], n_z))
         inputs = tokens.reshape(rows, width).astype(F32)
         mean_one, recip_one = norm_stats(inputs)
-        packed, full_o, down_pieces[-1], cotangent = tie(packed, full_o, down_pieces[-1], cotangent)
+        packed, full_o, down_pieces[-1], mean_one, *grad_near = tie(
+            packed, full_o, down_pieces[-1], mean_one, *grad_near
+        )
 
         full_o = lax.all_gather(full_o, "dp", axis=0, tiled=True)
-        while len(down_pieces) < n_z:
-            down_pieces.append(shift(down_pieces[-1], n_z))
-        half = rows // 2
-        grad_low = cotangent.reshape(rows, width)
-        grad_held = {(0, 0): grad_low[:half], (1, 0): grad_low[half:]}
-        grad_held.update(plane.gather_step(grad_held, 0))
+        grad_far = plane.across(grad_near, plane.steps - 1)
         packed = packed.reshape(n_dev, lines, width)
         full_q = packed[:, :own].reshape(width, width)
         full_kv = packed[:, own : own + kv_lines].reshape(width, 2 * HD)
@@ -356,93 +427,79 @@
         normed_one = (xhat_one * gain_one + shift_one).astype(BF16)
         kv_bias = jnp.concatenate([jnp.zeros((HD,), F32), bias_v])
         key_value = (dot_nn(normed_one, full_kv) + kv_bias).astype(BF16)
-        kv_window = lax.all_gather(
-            key_value.reshape(windows, local_len, 2 * HD), "fsdp", axis=1, tiled=True
-        )
-        queries = (dot_nn(normed_one, full_q) + bias_q).astype(BF16)
-        queries, up_cols, down_pieces[-1] = tie(queries, up_cols, down_pieces[-1])
-        up_pieces = [up_cols]
-        up_pieces.append(shift(up_pieces[-1], n_z))
+        key_value, normed_late = tie(key_value, normed_one)
+        kv_pieces = [key_value.reshape(windows, local_len, 2 * HD)]
+        while len(kv_pieces) < n_z:
+            kv_pieces.append(shift(kv_pieces[-1], n_z))
+        queries = (dot_nn(normed_late, full_q) + bias_q).astype(BF16)
+        kv_window = put_in_order(kv_pieces, n_z, 1)
 
         first = (lax.axis_index("fsdp") * local_len).astype(jnp.int32).reshape(1)
         file_count = lengths.shape[1]
         upto = jnp.arange(file_count)[:, None] <= jnp.arange(file_count)[None, :]
         file_ends = jnp.sum(jnp.where(upto[None], lengths[:, :, None], 0), axis=1)
-        queries, kv_window, up_pieces[-1] = tie(queries, kv_window, up_pieces[-1])
-        while len(up_pieces) < min(3, n_z):
-            up_pieces.append(shift(up_pieces[-1], n_z))
+        queries, kv_window, down_pieces[-1], up_cols = tie(queries, kv_window, down_pieces[-1], up_cols)
+        while len(down_pieces) < n_z:
+            down_pieces.append(shift(down_pieces[-1], n_z))
         attended, norms = attn_forward(queries, kv_window, first, file_ends)
-        attended, up_pieces[-1] = tie(attended, up_pieces[-1])
-        while len(up_pieces) < n_z:
-            up_pieces.append(shift(up_pieces[-1], n_z))
+        attended, down_pieces[-1], up_cols = tie(attended, down_pieces[-1], up_cols)
+        up_pieces = [up_cols, shift(up_cols, n_z)]
+        down_part = put_in_order(down_pieces, n_z)
+        grad_near_sib = plane.cross(grad_near)
+        grad_lots = [[*grad_near, *grad_near_sib]]
+        backs = [[dot_nt(block, down_part).astype(BF16) for block in grad_lots[0]]]
+        attended, *backs[0] = tie(attended, *backs[0])
         middle = inputs + dot_nn(attended, full_o) + bias_o
         mean_two, recip_two = norm_stats(middle)
         xhat_two = (middle - mean_two) * recip_two
         normed_two = (xhat_two * gain_two + shift_two).astype(BF16)
 
-        normed_two, *grad_pieces = tie(normed_two, *grad_held.values())
-        grad_held = dict(zip(grad_held, grad_pieces))
-        two_held = {(0, 0): normed_two[:half], (1, 0): normed_two[half:]}
-        for step in range(1, len(plane.bits)):
-            grad_held.update(plane.gather_step(grad_held, step))
-        for step in range(len(plane.bits)):
-            two_held.update(plane.gather_step(two_held, step))
-        grad_mine = plane.lay(grad_held)
-        grad_sib = plane.swap(grad_mine, 1)
-        down_part = put_in_order(down_pieces, n_z)
+        normed_two, up_pieces[-1], *grad_far = tie(normed_two, up_pieces[-1], *grad_far)
+        two_near = [normed_two[:half], normed_two[half:]]
+        while len(up_pieces) < n_z:
+            up_pieces.append(shift(up_pieces[-1], n_z))
+        for step in range(plane.steps - 1):
+            two_near = plane.grow(two_near, step)
+        grad_lots.append([*grad_far, *plane.cross(grad_far)])
+        backs.append([dot_nt(block, down_part).astype(BF16) for block in grad_lots[1]])
         up_part = put_in_order(up_pieces, n_z, 1).reshape(width, ff_own)
         bias_up_part = lax.dynamic_slice_in_dim(bias_up, my_dp * ff_own, ff_own)
-        back_mine = dot_nt(grad_mine, down_part)
-        back_sib = dot_nt(grad_sib, down_part)
-        two_sib = plane.lay(plane.cross(two_held))
-        two_mine = plane.lay(two_held)
-        two_mine, back_mine, back_sib = tie(two_mine, back_mine, back_sib)
-
-        def middle_layer(two, back):
-            pre_act = dot_nn(two, up_part) + bias_up_part
-            hidden, pull = jax.vjp(gelu_tanh, pre_act)
-            return hidden.astype(BF16), pull(back)[0].astype(BF16)
-
-        hidden_mine, pre_mine = middle_layer(two_mine, back_mine)
-        two_sib, pre_mine = tie(two_sib, pre_mine)
-        hidden_sib, pre_sib = middle_layer(two_sib, back_sib)
-        n_far = plane.n_far * half
-
-        def core_sum(mine, sib, weight, product):
-            out = []
-            for lot, keys in ((slice(0, n_far), plane.keys[: plane.n_far]), (slice(n_far, None), plane.keys[plane.n_far :])):
-                theirs = plane.swap(product(sib[lot], weight).astype(BF16), 1)
-                ours = product(mine[lot], weight)
-                out.append(plane.split((ours + theirs.astype(F32)).astype(BF16), keys))
-            return out
-
-        far, near = core_sum(pre_mine, pre_sib, up_part, dot_nt)
-        two_sum = {**far, **near}
-        hidden_mine, pre_mine, *near_pieces = tie(hidden_mine, pre_mine, *near.values())
-        two_sum.update(zip(near, near_pieces))
-        two_sum = plane.scatter_step(two_sum, 0)
-        up_terms = dot_tn(two_mine, pre_mine) + dot_tn(two_sib, pre_sib)
-        up_terms = up_terms.astype(BF16).reshape(n_dp, n_z, own, ff_own).transpose(1, 0, 2, 3)
-        out_far, out_near = core_sum(hidden_mine, hidden_sib, down_part, dot_nn)
-        out_sum = {**out_far, **out_near}
-        two_keys, out_keys = list(two_sum), list(out_sum)
-        up_terms, *pieces = tie(up_terms, *two_sum.values(), *out_sum.values())
-        two_sum = dict(zip(two_keys, pieces))
-        out_sum = dict(zip(out_keys, pieces[len(two_keys) :]))
-        for step in range(1, len(plane.bits)):
-            two_sum = plane.scatter_step(narrow(two_sum), step)
-        two_grad = jnp.concatenate([two_sum[0, 0], two_sum[1, 0]])
-        down_terms = dot_tn(hidden_mine, grad_mine) + dot_tn(hidden_sib, grad_sib)
-        down_terms = down_terms.astype(BF16).reshape(n_z, ff_own // n_z, width)
-        two_grad, down_terms, *pieces = tie(two_grad, down_terms, *out_sum.values())
-        out_sum = plane.scatter_step(dict(zip(out_keys, pieces)), 0)
-        grad_up = ring_scatter(up_terms, n_z)
-        grad_up = lax.all_to_all(
-            grad_up.astype(BF16).reshape(n_dp * own, ff_own), "dp", 0, 1, tiled=True
-        ).astype(F32)
-        grad_down = ring_scatter(down_terms, n_z)
-        up_bias_part = jnp.sum(pre_mine.astype(F32), axis=0) + jnp.sum(pre_sib.astype(F32), axis=0)
-
+        two_near[0], two_near[1], up_part, *backs[1] = tie(*two_near, up_part, *backs[1])
+
+        two_far = plane.across(two_near, plane.steps - 1)
+        two_lots = [[*two_near, *plane.cross(two_near)], [*two_far, *plane.cross(two_far)]]
+        near = middle_layer(two_lots[0], backs[0], up_part, bias_up_part)
+        backs[1][0], *pres = tie(backs[1][0], *near[1])
+        far = middle_layer(two_lots[1], backs[1], up_part, bias_up_part)
+        hiddens, pres = [near[0], far[0]], [pres, far[1]]
+
+        def core_sum(lot, weight, product):
+            theirs = plane.cross([product(block, weight).astype(BF16) for block in lot[2:]])
+            return [
+                (product(block, weight) + there.astype(F32)).astype(BF16)
+                for block, there in zip(lot[:2], theirs)
+            ]
+
+        def merge(halves, far_halves):
+            got = plane.across(far_halves, plane.steps - 1)
+            return [half.astype(F32) + there.astype(F32) for half, there in zip(halves, got)]
+
+        two_far = core_sum(pres[1], up_part, dot_nt)
+        pres[0][0], *two_far = tie(pres[0][0], *two_far)
+        two_near = core_sum(pres[0], up_part, dot_nt)
+        two_sum = merge(two_near, two_far)
+        up_terms = weight_grad(two_lots[0] + two_lots[1], pres[0] + pres[1])
+        up_terms, hiddens[1][0], *two_sum = tie(up_terms, hiddens[1][0], *two_sum)
+        for step in range(plane.steps - 2, -1, -1):
+            two_sum = plane.fold(two_sum, step)
+        two_grad = jnp.concatenate(two_sum)
+        up_ring = Ring(up_terms.reshape(n_dp, n_z, own, ff_own), 1, n_z)
+        out_far = core_sum(hiddens[1], down_part, dot_nn)
+        hiddens[0][0], *out_far = tie(hiddens[0][0], *out_far)
+        up_bias_part = sum(jnp.sum(block.astype(F32), axis=0) for lot in pres for block in lot)
+        two_grad, hiddens[0][0], *out_far = tie(two_grad, hiddens[0][0], *out_far)
+
+        two_grad = up_ring.go(1, two_grad)
         grad_out = grad_low.astype(F32)
         grad_bdown = jnp.sum(grad_out, axis=0)
         grad_gain_two = jnp.sum(two_grad * xhat_two, axis=0)
@@ -450,23 +507,37 @@
         middle_grad = grad_out + norm_pull(two_grad, xhat_two, recip_two, gain_two)
         grad_bo = jnp.sum(middle_grad, axis=0)
         branch_grad = middle_grad.astype(BF16)
-        grad_wo = scatter_both(dot_tn(attended, branch_grad).astype(BF16)).astype(F32)
         attended_grad = dot_nt(branch_grad, full_o).astype(BF16)
-
-        out_keys = list(out_sum)
-        attended_grad, *pieces = tie(attended_grad, *out_sum.values())
-        out_sum = dict(zip(out_keys, pieces))
-        for step in range(1, len(plane.bits)):
-            out_sum = plane.scatter_step(narrow(out_sum), step)
-        branch_out = jnp.concatenate([out_sum[0, 0], out_sum[1, 0]])
+        out_got = plane.across(out_far, plane.steps - 1)
+        grad_wo = dot_tn(attended, branch_grad).astype(BF16)
+        attended_grad, grad_wo = tie(attended_grad, grad_wo)
+        grad_wo = scatter_both(grad_wo).astype(F32)
+        attended_grad = up_ring.go(1, attended_grad)
+
+        query_grad, kv_terms = attn_backward(queries, kv_window, norms, attended_grad, first, file_ends)
+        query_grad, hiddens[0][0], *out_got = tie(query_grad, hiddens[0][0], *out_got)
+        query_grad = up_ring.go(1, query_grad)
+        kv_ring = Ring(kv_terms.reshape(windows, n_z, local_len, 2 * HD), 1, n_z)
+        grad_wq = dot_tn(normed_one, query_grad).astype(BF16)
+        grad_wq = kv_ring.go(1, grad_wq)
+        out_near = core_sum(hiddens[0], down_part, dot_nn)
+        out_near[0] = kv_ring.go(n_z - 2, out_near[0])
+        out_sum = [near.astype(F32) + got.astype(F32) for near, got in zip(out_near, out_got)]
+        for step in range(plane.steps - 2, -1, -1):
+            out_sum = plane.fold(out_sum, step)
+        kv_grad = kv_ring.finish().astype(BF16).reshape(rows, 2 * HD)
+        kv_grad, hiddens[1][0] = tie(kv_grad, hiddens[1][0])
+        down_terms = weight_grad(hiddens[0] + hiddens[1], grad_lots[0] + grad_lots[1])
+        down_ring = Ring(down_terms.reshape(n_z, ff_own // n_z, width), 0, n_z)
+        branch_out = jnp.concatenate(out_sum)
         output = (middle + branch_out + bias_down).astype(BF16).reshape(windows, local_len, width)
-
-        query_grad, kv_terms = attn_backward(queries, kv_window, norms, attended_grad, first, file_ends)
-        kv_grad = lax.psum_scatter(kv_terms, "fsdp", scatter_dimension=1, tiled=True)
-        kv_grad = kv_grad.reshape(rows, 2 * HD)
+        grad_up = lax.all_to_all(
+            up_ring.finish().astype(BF16).reshape(n_dp * own, ff_own), "dp", 0, 1, tiled=True
+        ).astype(F32)
+        grad_down = down_ring.finish()
+
         grad_bq = jnp.sum(query_grad.astype(F32), axis=0)
         grad_bv = jnp.sum(kv_grad[:, HD:].astype(F32), axis=0)
-        grad_wq = dot_tn(normed_one, query_grad)
         grad_wkv = dot_tn(normed_one, kv_grad)
         one_grad = dot_nt(query_grad, full_q) + dot_nt(kv_grad, full_kv)
         grad_gain_one = jnp.sum(one_grad * xhat_one, axis=0)
@@ -486,11 +557,17 @@
             grad_gain_two,
             grad_shift_two,
         )
-        sum_rows = jnp.concatenate([v.astype(BF16).reshape(n_dev, -1) for v in sums], axis=1)
+        sum_rows = jnp.concatenate(
+            [
+                jnp.pad(v.astype(BF16).reshape(n_dev, size), ((0, 0), (0, room - size)))
+                for v, size, room in zip(sums, sizes, rooms)
+            ],
+            axis=1,
+        )
         sum_rows = jnp.pad(sum_rows, ((0, 0), (0, spare - sum_rows.shape[1])))
         grads = jnp.concatenate(
             [
-                grad_wq.astype(BF16).reshape(n_dev, own, width),
+                grad_wq.reshape(n_dev, own, width),
                 grad_wkv.astype(BF16).reshape(n_dev, kv_lines, width),
                 sum_rows.reshape(n_dev, -1, width),
             ],

time: 1010 us -> 909 us (0.900)
  waiting for transfers between devices: 478 us -> 320 us
  Pallas kernels: 49.9 us -> 140 us
  matrix products: 230 us -> 207 us
  other arithmetic: 91.8 us -> 81.1 us
    pallas_call x0 -> x4, Pallas kernels: none -> 90.6 us  [the longest x2 49.8 us: weight_grad(): pl.pallas_call(functools.partial(weight_kernel, count), out_shape=jax.Sha...]
    ppermute x12 -> x21, waiting for transfers between devices: 236 us -> 146 us  [shift(): lax.ppermute(block, 'fsdp', [(i, (i + 1) % count) for i in range(count)])]
    dot_general x7 -> x3, matrix products: 80.8 us -> 17 us  [dot_tn(): lax.dot_general(left, right, (((0,), (0,)), ((), ())), preferred_element_...]
    dot_general x9 -> x19, matrix products: 78.1 us -> 125 us  [dot_nt(): lax.dot_general(left, right, (((1,), (1,)), ((), ())), preferred_element_...]
    all_gather x1, waiting for transfers between devices: 41.1 us -> 0.01 us  [local(): packed = lax.all_gather(packed, 'dp', axis=0, tiled=True)]
    reduce_scatter x2, waiting for transfers between devices: 45.9 us -> 25.9 us  [scatter_both(): return lax.psum_scatter(part, 'fsdp', scatter_dimension=0, tiled=True)]
    convert_element_type x8 -> x5, other arithmetic: 23.9 us -> 11.4 us  [the longest x2 5.15 us: finish(): self.total.astype(BF16)]
    reduce_sum x2 -> x5, other arithmetic: 11.8 us -> 1.35 us  [local(): jnp.sum(block.astype(F32), axis=0)]
  transfers between devices with their start and end apart: 60 -> 61, of which waited for: 33 -> 27; matrix products, arithmetic and copies ran while one was open for 29% -> 34% of each run, Pallas kernels for 2% -> 16%
where the time goes in v3:
time: 909 us; the launch traced here: 900 us
  waiting for transfers between devices  320 us (35%)
  matrix products  207 us (23%)
  Pallas kernels  140 us (15%)
  other arithmetic  81.1 us (9%)
  local copies, waits for them, and re-layouts  74 us (8%)
  starting transfers between devices  42.5 us (5%)
  blocking collectives  20.6 us (2%)
  between operations  15.7 us (2%)
    ppermute x21, waiting for transfers between devices, shift(): lax.ppermute(block, 'fsdp', [(i, (i + 1) % count) for i in range(count)])  146 us
    dot_general x19, matrix products, dot_nt(): lax.dot_general(left, right, (((1,), (1,)), ((), ())), preferred_element_...  125 us
    ppermute x32, waiting for transfers between devices, swap(): return lax.ppermute(block, 'dp', [(i, i ^ bit) for i in range(self.count)])  114 us
    dot_general x11, matrix products, dot_nn(): return jnp.dot(left, right, preferred_element_type=F32)  64.5 us
    pallas_call x2, Pallas kernels, weight_grad(): pl.pallas_call(functools.partial(weight_kernel, count), out_shape=jax.Sha...  49.8 us
    pallas_call x2, Pallas kernels, middle_layer(): pl.pallas_call(functools.partial(middle_kernel, count), out_shape=[jax.Sh...  40.7 us
    pallas_call x1, Pallas kernels, attn_backward(): pl.pallas_call(functools.partial(attn_backward_kernel, per_step), out_sha...  30.3 us
    reduce_scatter x2, waiting for transfers between devices, scatter_both(): return lax.psum_scatter(part, 'fsdp', scatter_dimension=0, tiled=True)  25.9 us
  transfers between devices with their start and end apart: 61, of which 27 were waited for; matrix products, arithmetic and copies ran while one was open for 34% of the time, Pallas kernels for 16%

profile of v3, /device:TPU:0, one launch (start us, length us, event | category | flops | bytes accessed | tf_op | source)
XLA Modules:
  0.0 899.7 jit_solution(13722845370733778861)
XLA Ops:
  18.9 20.6 %all_to_all.26 = bf16[64,8,1024]{2,0,1:T(8,128)(2,1)} all-to-all(bf16[64,8,1024]{2,0,1:T(8,128)(2,1)S(1)} %bitcast.210), channel_id=1, replica_groups=mesh['dp'=8,'fsdp'=4] {'dp'}, dimensions={1} | all-to-all | bytes 2097152 | tf_op jit(solution)/shard_map/all_to_all | solution.py:398
  39.5 13.6 %all-gather.4.cloned.1.call-done = bf16[320,2048]{1,0:T(8,128)(2,1)} async-done(((bf16[80,2048]{1,0:T(8,128)(2,1)}), bf16[320,2048]{1,0:T(8,128)(2,1)}) %all-gather.4.cloned.1.call-update) | async-done | bytes 1310736 | tf_op jit(solution)/shard_map/all_gather | solution.py:394
  54.0 8.4 collective-permute-done
  66.8 3.9 collective-permute-done.1
  70.7 8.2 collective-permute-done.2
  80.8 24.1 %collective-permute-done.5 = bf16[256,2048]{1,0:T(8,128)(2,1)} collective-permute-done((bf16[256,2048]{1,0:T(8,128)(2,1)}, bf16[256,2048]{1,0:T(8,128)(2,1)}, u32[]{:S(2)}, u32[]{:S(2)}) %collective-permute-start.5) | collective-permute-done | bytes 1048608 | tf_op jit(solution)/shard_map/ppermute | solution.py:319
  112.6 20.1 %collective-permute-done.4 = bf16[256,2048]{1,0:T(8,128)(2,1)} collective-permute-done((bf16[256,2048]{1,0:T(8,128)(2,1)}, bf16[256,2048]{1,0:T(8,128)(2,1)}, u32[]{:S(2)}, u32[]{:S(2)}) %collective-permute-start.4) | collective-permute-done | bytes 1048608 | tf_op jit(solution)/shard_map/ppermute | solution.py:272
  145.1 8.5 slice.165
  155.3 9.1 %add_convert_fusion.9.q_ref = bf16[512,2048]{1,0:T(8,128)(2,1)} fusion(bf16[512,2048]{1,0:T(8,128)(2,1)S(1)} %copy-done.38, bf16[2048,2048]{1,0:T(8,128)(2,1)} %bitcast.197, f32[2048]{0:T(1024)S(1)} %reshape.401), kind=kOutput, calls=%fused_computation.49 | convolution fusion | flops 4297064448 | bytes 12591104 | tf_op jit(solution)/shard_map/dot_general | solution.py:20
  166.1 8.1 collective-permute-done.9
  186.5 18.8 %shard_map.288 = (bf16[512,2048]{1,0:T(8,128)(2,1)S(1)}, f32[512,128]{1,0:T(8,128)S(1)}) custom-call(s32[1]{0:T(128)} %bitcast.1.pos_ref, s32[2,8]{1,0:T(2,128)S(1)} %select_reduce_fusion.ends_ref, bf16[512,2048]{1,0:T(8,128)(2,1)S(1)} %copy-done.22, bf16[2,1024,256]{2,1,0:T(8,128)(2,1)S(1)} %constant_dynamic-update-slice_fusion.17.kv_ref), custom_call_target="tpu_custom_call" | custom-call | flops 4294967296 | bytes 4194304 | tf_op jit(solution)/shard_map/pallas_call | solution.py:131
  213.1 6.1 convolution_convert_fusion.19.refs_4_
  219.3 6.2 convolution_convert_fusion.18.refs_5_
  225.5 6.2 convolution_convert_fusion.17.refs_6_
  231.7 6.2 convolution_convert_fusion.16.refs_7_
  237.9 8.7 fusion.34
  250.4 6.1 convolution_convert_fusion.15.refs_4_
  259.4 6.2 convolution_convert_fusion.14.refs_5_
  265.6 10.7 %collective-permute-done.18 = bf16[8,64,1024]{2,1,0:T(8,128)(2,1)S(1)} collective-permute-done((bf16[8,64,1024]{2,1,0:T(8,128)(2,1)S(1)}, bf16[8,64,1024]{2,1,0:T(8,128)(2,1)S(1)}, u32[]{:S(2)}, u32[]{:S(2)}) %collective-permute-start.18) | collective-permute-done | bytes 1048608 | tf_op jit(solution)/shard_map/ppermute | solution.py:272
  277.5 4.7 collective-permute-done.17
  283.7 6.3 convolution_convert_fusion.13.refs_6_
  290.1 6.4 convolution_convert_fusion.12.refs_7_
  296.4 5.9 collective-permute-done.19
  306.8 42.5 %collective-permute-done.24.refs_0_.refs_4_ = bf16[512,2048]{1,0:T(8,128)(2,1)} collective-permute-done((bf16[512,2048]{1,0:T(8,128)(2,1)S(1)}, bf16[512,2048]{1,0:T(8,128)(2,1)}, u32[]{:S(2)}, u32[]{:S(2)}) %collective-permute-start.24) | collective-permute-done | bytes 2097184 | tf_op jit(solution)/shard_map/ppermute | solution.py:319
  351.3 20.4 %shard_map.289 = (bf16[512,1024]{1,0:T(8,128)(2,1)S(1)}, bf16[512,1024]{1,0:T(8,128)(2,1)S(1)}, bf16[512,1024]{1,0:T(8,128)(2,1)S(1)}, bf16[512,1024]{1,0:T(8,12...) custom-call(bf16[512,2048]{1,0:T(8,128)(2,1)} %copy-done.40, ...), custom_call_target="tpu_custom_call" | custom-call | flops 8589934592 | bytes 25165824 | tf_op jit(solution)/shard_map/pallas_call | solution.py:196
  371.8 7.7 convolution_convert_fusion.7
  380.1 6.6 fusion.36
  388.0 20.3 %shard_map.290 = (bf16[512,1024]{1,0:T(8,128)(2,1)S(1)}, bf16[512,1024]{1,0:T(8,128)(2,1)S(1)}, bf16[512,1024]{1,0:T(8,128)(2,1)S(1)}, bf16[512,1024]{1,0:T(8,12...) custom-call(bf16[512,2048]{1,0:T(8,128)(2,1)} %collective-permute-do, ...), custom_call_target="tpu_custom_call" | custom-call | flops 8589934592 | bytes 25165824 | tf_op jit(solution)/shard_map/pallas_call | solution.py:196
  408.4 6.7 convolution_convert_fusion.9
  415.2 4.6 convolution_convert_fusion.8
  420.3 4.6 convolution_convert_fusion.4
  425.0 5.9 convolution_convert_fusion.6
  431.4 5.9 convolution_convert_fusion.5
  437.4 4.7 add_convert_fusion.7
  442.1 6.3 add_convert_fusion.6
  450.5 5.9 add_convert_fusion.2
  456.4 6.6 fusion.35
  463.0 24.1 %shard_map.291 = bf16[2048,1024]{1,0:T(8,128)(2,1)} custom-call(bf16[512,2048]{1,0:T(8,128)(2,1)} %copy-done.40, bf16[512,2048]{1,0:T(8,128)(2,1)} %pad_maximum_fusion.5.refs_1_, bf16[512,2048]{1,0:T(8,128)(2,1)} %collective-permute-done.22.refs_2_, bf16[512,2048]{1,0:T(8,128)(2,1)} %collective-permute-done.23.refs_3_, ...), custom_call_target="tpu_custom_call" | custom-call | flops 17179869184 | bytes 29360128 | tf_op jit(solution)/shard_map/pallas_call | solution.py:228
  487.1 9.5 %collective-permute-done.31 = bf16[512,2048]{1,0:T(8,128)(2,1)} collective-permute-done((bf16[512,2048]{1,0:T(8,128)(2,1)S(1)}, bf16[512,2048]{1,0:T(8,128)(2,1)}, u32[]{:S(2)}, u32[]{:S(2)}) %collective-permute-start.31) | collective-permute-done | bytes 2097184 | tf_op jit(solution)/shard_map/ppermute | solution.py:319
  496.5 4.0 convert_add_fusion.4
  507.1 4.5 fusion.37
  515.3 14.2 %collective-permute-done.36 = bf16[256,2048]{1,0:T(8,128)(2,1)S(1)} collective-permute-done((bf16[256,2048]{1,0:T(8,128)(2,1)S(1)}, bf16[256,2048]{1,0:T(8,128)(2,1)S(1)}, u32[]{:S(2)}, u32[]{:S(2)}) %collective-permute-start.36) | collective-permute-done | bytes 1048608 | tf_op jit(solution)/shard_map/ppermute | solution.py:319
  538.9 6.9 convolution_convert_fusion.1
  545.8 10.5 %convolution_convert_fusion.10.grad_ref = bf16[512,2048]{1,0:T(8,128)(2,1)} fusion(bf16[2048,2048]{1,0:T(8,128)(2,1)} %all-gather.8.cloned.1.call-done, f32[512,2048]{1,0:T(8,128)} %copy-done.29), kind=kOutput, calls=%fused_computation.62 | convolution fusion | flops 4297064448 | bytes 14680064 | tf_op jit(solution)/shard_map/dot_general | solution.py:24
  559.6 6.0 convolution_convert_fusion.3
  569.8 15.2 %collective-permute-done.39 = bf16[8,64,1024]{2,1,0:T(8,128)(2,1)S(1)} collective-permute-done((bf16[8,64,1024]{2,1,0:T(8,128)(2,1)S(1)}, bf16[8,64,1024]{2,1,0:T(8,128)(2,1)S(1)}, u32[]{:S(2)}, u32[]{:S(2)}) %collective-permute-start.39) | collective-permute-done | bytes 1048608 | tf_op jit(solution)/shard_map/ppermute | solution.py:272
  587.7 30.3 %shard_map.292 = (bf16[512,2048]{1,0:T(8,128)(2,1)S(1)}, bf16[2,1024,256]{2,1,0:T(8,128)(2,1)S(1)}) custom-call(s32[1]{0:T(128)} %bitcast.1.pos_ref, s32[2,8]{1,0:T(2,128)S(1)} %copy-done.7, bf16[512,2048]{1,0:T(8,128)(2,1)} %add_convert_fusion.9.q_ref, bf16[2,1024,256]{2,1,0:T(8,128)(2,1)S(1)} %copy-done.3, f32[512,128]{1,0:T(8,128)S(1)} %get-tuple-element.132.norm_ref, ...), custom_call_target="tpu_custom_call" | custom-call | flops 10737418240 | bytes 10485760 | tf_op jit(solution)/shard_map/pallas_call | solution.py:151
  619.2 7.1 collective-permute-done.40
  627.4 10.0 %collective-permute-done.42 = bf16[512,2048]{1,0:T(8,128)(2,1)} collective-permute-done((bf16[512,2048]{1,0:T(8,128)(2,1)}, bf16[512,2048]{1,0:T(8,128)(2,1)}, u32[]{:S(2)}, u32[]{:S(2)}) %collective-permute-start.42) | collective-permute-done | bytes 2097184 | tf_op jit(solution)/shard_map/ppermute | solution.py:319
  641.5 8.4 convolution_convert_fusion
  650.6 9.5 %fusion.38 = f32[512,2048]{1,0:T(8,128)} fusion(bf16[512,2048]{1,0:T(8,128)(2,1)S(1)} %get-tuple-element.189, bf16[2048,2048]{1,0:T(8,128)(2,1)} %bitcast.198), kind=kOutput, calls=%fused_computation.175 | convolution fusion | flops 4294967296 | bytes 14680064 | tf_op jit(solution)/shard_map/dot_general | solution.py:24
  660.9 4.9 collective-permute-start.45
  665.8 6.5 add_convert_fusion.1
  673.2 6.3 fusion.20
  683.8 11.2 %pad_maximum_fusion = bf16[32,80,2048]{2,1,0:T(8,128)(2,1)} fusion(bf16[32,8,2048]{2,1,0:T(8,128)(2,1)S(1)} %bitcast.204, bf16[32,8,2048]{2,1,0:T(8,128)(2,1)S(1)} %reshape.389, bf16[32,64,2048]{2,1,0:T(8,128)(2,1)} %bitcast.199), kind=kLoop, calls=%fused_computation | loop fusion | flops 31457280 | bytes 20971520 | tf_op jit(solution)/shard_map/concatenate | solution.py:568
  696.2 5.9 convolution_convert_fusion.2
  702.3 6.3 collective-permute-done.48
  708.6 6.5 add_convert_fusion
  720.6 4.7 all-to-all-start.1
  725.5 25.8 %shard_map.293 = bf16[1024,2048]{1,0:T(8,128)(2,1)} custom-call(bf16[512,1024]{1,0:T(8,128)(2,1)S(1)} %copy-done.11, bf16[512,1024]{1,0:T(8,128)(2,1)} %copy-done.12, bf16[512,1024]{1,0:T(8,128)(2,1)} %copy-done.15, bf16[512,1024]{1,0:T(8,128)(2,1)} %copy-done.16, bf16[512,1024]{1,0:T(8,128)(2,1)} %copy-done.8, bf16[512,1024]{1,0:T(8,128)(2,1)} %copy-done.14, ...), custom_call_target="tpu_custom_call" | custom-call | flops 17179869184 | bytes 29360128 | tf_op jit(solution)/shard_map/pallas_call | solution.py:228
  762.8 18.6 %collective-permute-done.50 = bf16[256,2048]{1,0:T(8,128)(2,1)} collective-permute-done((bf16[256,2048]{1,0:T(8,128)(2,1)}, bf16[256,2048]{1,0:T(8,128)(2,1)}, u32[]{:S(2)}, u32[]{:S(2)}) %collective-permute-start.50) | collective-permute-done | bytes 1048608 | tf_op jit(solution)/shard_map/ppermute | solution.py:272
  788.8 19.5 %reduce-scatter.5.cloned.1.call-done = bf16[320,2048]{1,0:T(8,128)(2,1)} async-done(((bf16[2560,2048]{1,0:T(8,128)(2,1)}), bf16[320,2048]{1,0:T(8,128)(2,1)}) %reduce-scatter.5.cloned.1.call-update) | async-done | bytes 1310736 | tf_op jit(solution)/shard_map/reduce_scatter | solution.py:267
  816.7 39.5 %collective-permute-done.52 = bf16[256,2048]{1,0:T(8,128)(2,1)S(1)} collective-permute-done((bf16[256,2048]{1,0:T(8,128)(2,1)S(1)}, bf16[256,2048]{1,0:T(8,128)(2,1)S(1)}, u32[]{:S(2)}, u32[]{:S(2)}) %collective-permute-start.52) | collective-permute-done | bytes 1048608 | tf_op jit(solution)/shard_map/ppermute | solution.py:272
  860.8 25.9 %reduce-scatter.7.cloned.1.call-done = bf16[80,2048]{1,0:T(8,128)(2,1)} async-done(((bf16[320,2048]{1,0:T(8,128)(2,1)}), bf16[80,2048]{1,0:T(8,128)(2,1)}) %reduce-scatter.7.cloned.1.call-update) | async-done | bytes 327696 | tf_op jit(solution)/shard_map/reduce_scatter | solution.py:268
  (420 shorter events, 170.7 us)
Async XLA Ops:
  7.2 45.9 %all-gather.4.cloned.1.call-start = ((), (), s32[]{:S(2)}) async-start(), calls=%async_computation.6 | async-start | bytes 1638400 | tf_op jit(solution)/shard_map/all_gather | solution.py:394
  17.5 115.2 %all-gather.6.cloned.1.call-start = ((), (), s32[]{:S(2)}) async-start(), calls=%async_computation.7 | async-start | bytes 11796480 | tf_op jit(solution)/shard_map/all_gather | solution.py:401
  18.9 61.5 %copy-start.26 = (bf16[2,256,2048]{2,1,0:T(8,128)(2,1)S(1)}, bf16[2,256,2048]{2,1,0:T(8,128)(2,1)}, u32[]{:S(2)}) copy-start(bf16[2,256,2048]{2,1,0:T(8,128)(2,1)} %param.17) | copy-start | bytes 6291460
  53.1 184.7 %all-gather.8.cloned.1.call-start = ((), (), s32[]{:S(2)}) async-start(), calls=%async_computation.8 | async-start | bytes 9437184 | tf_op jit(solution)/shard_map/all_gather | solution.py:416
  53.2 9.2 %collective-permute-start = (bf16[64,2048]{1,0:T(8,128)(2,1)S(1)}, bf16[64,2048]{1,0:T(8,128)(2,1)S(1)}, u32[]{:S(2)}, u32[]{:S(2)}) collective-permute-start(bf16[64,2048]{1,0:T(8,128)(2,1)S(1)} %copy-done.54), channel_id=1, source_target_pairs={{0,1},{1,2},{2,3},{3,0},{4,5},{5,6},{6,7},{7,4},{8,9},{9,10},{10,1... | collective-permute-start | bytes 786440 | tf_op jit(solution)/shard_map/ppermute | solution.py:272
  62.4 8.3 collective-permute-start.1
  65.4 39.4 %collective-permute-start.5 = (bf16[256,2048]{1,0:T(8,128)(2,1)}, bf16[256,2048]{1,0:T(8,128)(2,1)}, u32[]{:S(2)}, u32[]{:S(2)}) collective-permute-start(bf16[256,2048]{1,0:T(8,128)(2,1)} %get-tuple-element.219), channel_id=1, source_target_pairs={{0,8},{4,12},{8,0},{12,4},{16,24},{20,28},{24,16},{28,20},{1,9},{5... | collective-permute-start | bytes 3145736 | tf_op jit(solution)/shard_map/ppermute | solution.py:319
  70.7 8.2 collective-permute-start.2
  78.8 29.2 %collective-permute-start.3 = (bf16[256,2048]{1,0:T(8,128)(2,1)}, bf16[256,2048]{1,0:T(8,128)(2,1)}, u32[]{:S(2)}, u32[]{:S(2)}) collective-permute-start(bf16[256,2048]{1,0:T(8,128)(2,1)} %param.29), channel_id=1, source_target_pairs={{0,1},{1,2},{2,3},{3,0},{4,5},{5,6},{6,7},{7,4},{8,9},{9,10},{10,1... | collective-permute-start | bytes 3145736 | tf_op jit(solution)/shard_map/ppermute | solution.py:272
  78.9 30.7 %collective-permute-start.6 = (bf16[256,2048]{1,0:T(8,128)(2,1)S(1)}, bf16[256,2048]{1,0:T(8,128)(2,1)}, u32[]{:S(2)}, u32[]{:S(2)}) collective-permute-start(bf16[256,2048]{1,0:T(8,128)(2,1)S(1)} %get-tuple-element.218), channel_id=1, source_target_pairs={{0,16},{4,20},{8,24},{12,28},{16,0},{20,4},{24,8},{28,12},{1,17},{... | collective-permute-start | bytes 3145736 | tf_op jit(solution)/shard_map/ppermute | solution.py:319
  108.0 24.7 %collective-permute-start.4 = (bf16[256,2048]{1,0:T(8,128)(2,1)}, bf16[256,2048]{1,0:T(8,128)(2,1)}, u32[]{:S(2)}, u32[]{:S(2)}) collective-permute-start(bf16[256,2048]{1,0:T(8,128)(2,1)} %collective-permute-done.3), channel_id=1, source_target_pairs={{0,1},{1,2},{2,3},{3,0},{4,5},{5,6},{6,7},{7,4},{8,9},{9,10},{10,1... | collective-permute-start | bytes 3145736 | tf_op jit(solution)/shard_map/ppermute | solution.py:272
  132.7 621.5 %reduce-scatter.9.cloned.1.call-start = ((), (), s32[]{:S(2)}) async-start(), calls=%async_computation.11 | async-start | bytes 9437184 | tf_op jit(solution)/shard_map/reduce_scatter | solution.py:267
  144.3 9.5 %collective-permute-start.7 = (bf16[2,256,256]{2,1,0:T(8,128)(2,1)S(1)}, bf16[2,256,256]{2,1,0:T(8,128)(2,1)S(1)}, u32[]{:S(2)}, u32[]{:S(2)}) collective-permute-start(bf16[2,256,256]{2,1,0:T(8,128)(2,1)S(1)} %bitcast.223), channel_id=1, source_target_pairs={{0,1},{1,2},{2,3},{3,0},{4,5},{5,6},{6,7},{7,4},{8,9},{9,10},{10,1... | collective-permute-start | bytes 786440 | tf_op jit(solution)/shard_map/ppermute | solution.py:272
  153.8 10.6 %collective-permute-start.8 = (bf16[2,256,256]{2,1,0:T(8,128)(2,1)S(1)}, bf16[2,256,256]{2,1,0:T(8,128)(2,1)S(1)}, u32[]{:S(2)}, u32[]{:S(2)}) collective-permute-start(bf16[2,256,256]{2,1,0:T(8,128)(2,1)S(1)} %collective-permute-done.7), channel_id=1, source_target_pairs={{0,1},{1,2},{2,3},{3,0},{4,5},{5,6},{6,7},{7,4},{8,9},{9,10},{10,1... | collective-permute-start | bytes 786440 | tf_op jit(solution)/shard_map/ppermute | solution.py:272
  164.4 9.7 %collective-permute-start.9 = (bf16[2,256,256]{2,1,0:T(8,128)(2,1)S(1)}, bf16[2,256,256]{2,1,0:T(8,128)(2,1)S(1)}, u32[]{:S(2)}, u32[]{:S(2)}) collective-permute-start(bf16[2,256,256]{2,1,0:T(8,128)(2,1)S(1)} %collective-permute-done.8), channel_id=1, source_target_pairs={{0,1},{1,2},{2,3},{3,0},{4,5},{5,6},{6,7},{7,4},{8,9},{9,10},{10,1... | collective-permute-start | bytes 786440 | tf_op jit(solution)/shard_map/ppermute | solution.py:272
  174.2 31.2 %collective-permute-start.10 = (bf16[256,2048]{1,0:T(8,128)(2,1)}, bf16[256,2048]{1,0:T(8,128)(2,1)}, u32[]{:S(2)}, u32[]{:S(2)}) collective-permute-start(bf16[256,2048]{1,0:T(8,128)(2,1)} %collective-permute-done.4), channel_id=1, source_target_pairs={{0,1},{1,2},{2,3},{3,0},{4,5},{5,6},{6,7},{7,4},{8,9},{9,10},{10,1... | collective-permute-start | bytes 3145736 | tf_op jit(solution)/shard_map/ppermute | solution.py:272
  180.1 45.4 %collective-permute-start.11 = (bf16[512,2048]{1,0:T(8,128)(2,1)}, bf16[512,2048]{1,0:T(8,128)(2,1)}, u32[]{:S(2)}, u32[]{:S(2)}) collective-permute-start(bf16[512,2048]{1,0:T(8,128)(2,1)} %pad_maximum_fusion.2.refs_8_), channel_id=1, source_target_pairs={{0,4},{4,0},{8,12},{12,8},{16,20},{20,16},{24,28},{28,24},{1,5},{5... | collective-permute-start | bytes 6291464 | tf_op jit(solution)/shard_map/ppermute | solution.py:319
  180.1 68.5 %collective-permute-start.14 = (bf16[512,2048]{1,0:T(8,128)(2,1)}, bf16[512,2048]{1,0:T(8,128)(2,1)}, u32[]{:S(2)}, u32[]{:S(2)}) collective-permute-start(bf16[512,2048]{1,0:T(8,128)(2,1)} %pad_maximum_fusion.2.refs_8_), channel_id=1, source_target_pairs={{0,16},{4,20},{8,24},{12,28},{16,0},{20,4},{24,8},{28,12},{1,17},{... | collective-permute-start | bytes 6291464 | tf_op jit(solution)/shard_map/ppermute | solution.py:319
  180.7 51.0 %collective-permute-start.12 = (bf16[512,2048]{1,0:T(8,128)(2,1)}, bf16[512,2048]{1,0:T(8,128)(2,1)}, u32[]{:S(2)}, u32[]{:S(2)}) collective-permute-start(bf16[512,2048]{1,0:T(8,128)(2,1)} %pad_maximum_fusion.3.refs_9_), channel_id=1, source_target_pairs={{0,4},{4,0},{8,12},{12,8},{16,20},{20,16},{24,28},{28,24},{1,5},{5... | collective-permute-start | bytes 6291464 | tf_op jit(solution)/shard_map/ppermute | solution.py:319
  180.9 67.7 %collective-permute-start.15 = (bf16[512,2048]{1,0:T(8,128)(2,1)}, bf16[512,2048]{1,0:T(8,128)(2,1)}, u32[]{:S(2)}, u32[]{:S(2)}) collective-permute-start(bf16[512,2048]{1,0:T(8,128)(2,1)} %pad_maximum_fusion.3.refs_9_), channel_id=1, source_target_pairs={{0,8},{4,12},{8,0},{12,4},{16,24},{20,28},{24,16},{28,20},{1,9},{5... | collective-permute-start | bytes 6291464 | tf_op jit(solution)/shard_map/ppermute | solution.py:319
  205.3 43.2 %collective-permute-start.13 = (bf16[8,64,1024]{2,1,0:T(8,128)(2,1)}, bf16[8,64,1024]{2,1,0:T(8,128)(2,1)S(1)}, u32[]{:S(2)}, u32[]{:S(2)}) collective-permute-start(bf16[8,64,1024]{2,1,0:T(8,128)(2,1)} %bitcast.2), channel_id=1, source_target_pairs={{0,1},{1,2},{2,3},{3,0},{4,5},{5,6},{6,7},{7,4},{8,9},{9,10},{10,1... | collective-permute-start | bytes 3145736 | tf_op jit(solution)/shard_map/ppermute | solution.py:272
  248.7 28.6 %collective-permute-start.16 = (bf16[256,2048]{1,0:T(8,128)(2,1)S(1)}, bf16[256,2048]{1,0:T(8,128)(2,1)S(1)}, u32[]{:S(2)}, u32[]{:S(2)}) collective-permute-start(bf16[256,2048]{1,0:T(8,128)(2,1)S(1)} %get-tuple-element.217), channel_id=1, source_target_pairs={{0,8},{4,12},{8,0},{12,4},{16,24},{20,28},{24,16},{28,20},{1,9},{5... | collective-permute-start | bytes 3145736 | tf_op jit(solution)/shard_map/ppermute | solution.py:319
  249.3 27.0 %collective-permute-start.18 = (bf16[8,64,1024]{2,1,0:T(8,128)(2,1)S(1)}, bf16[8,64,1024]{2,1,0:T(8,128)(2,1)S(1)}, u32[]{:S(2)}, u32[]{:S(2)}) collective-permute-start(bf16[8,64,1024]{2,1,0:T(8,128)(2,1)S(1)} %collective-permute-done.13), channel_id=1, source_target_pairs={{0,1},{1,2},{2,3},{3,0},{4,5},{5,6},{6,7},{7,4},{8,9},{9,10},{10,1... | collective-permute-start | bytes 3145736 | tf_op jit(solution)/shard_map/ppermute | solution.py:272
  250.4 33.3 %collective-permute-start.20 = (bf16[512,2048]{1,0:T(8,128)(2,1)}, bf16[512,2048]{1,0:T(8,128)(2,1)S(1)}, u32[]{:S(2)}, u32[]{:S(2)}) collective-permute-start(bf16[512,2048]{1,0:T(8,128)(2,1)} %collective-permute-done.14.refs_12_), channel_id=1, source_target_pairs={{0,4},{4,0},{8,12},{12,8},{16,20},{20,16},{24,28},{28,24},{1,5},{5... | collective-permute-start | bytes 6291464 | tf_op jit(solution)/shard_map/ppermute | solution.py:319
  256.6 25.6 %collective-permute-start.17 = (bf16[256,2048]{1,0:T(8,128)(2,1)S(1)}, bf16[256,2048]{1,0:T(8,128)(2,1)S(1)}, u32[]{:S(2)}, u32[]{:S(2)}) collective-permute-start(bf16[256,2048]{1,0:T(8,128)(2,1)S(1)} %get-tuple-element.216), channel_id=1, source_target_pairs={{0,16},{4,20},{8,24},{12,28},{16,0},{20,4},{24,8},{28,12},{1,17},{... | collective-permute-start | bytes 3145736 | tf_op jit(solution)/shard_map/ppermute | solution.py:319
  258.1 32.0 %collective-permute-start.21 = (bf16[512,2048]{1,0:T(8,128)(2,1)}, bf16[512,2048]{1,0:T(8,128)(2,1)S(1)}, u32[]{:S(2)}, u32[]{:S(2)}) collective-permute-start(bf16[512,2048]{1,0:T(8,128)(2,1)} %collective-permute-done.15.refs_13_), channel_id=1, source_target_pairs={{0,4},{4,0},{8,12},{12,8},{16,20},{20,16},{24,28},{28,24},{1,5},{5... | collective-permute-start | bytes 6291464 | tf_op jit(solution)/shard_map/ppermute | solution.py:319
  276.3 26.0 %collective-permute-start.19 = (bf16[8,64,1024]{2,1,0:T(8,128)(2,1)S(1)}, bf16[8,64,1024]{2,1,0:T(8,128)(2,1)S(1)}, u32[]{:S(2)}, u32[]{:S(2)}) collective-permute-start(bf16[8,64,1024]{2,1,0:T(8,128)(2,1)S(1)} %collective-permute-done.18), channel_id=1, source_target_pairs={{0,1},{1,2},{2,3},{3,0},{4,5},{5,6},{6,7},{7,4},{8,9},{9,10},{10,1... | collective-permute-start | bytes 3145736 | tf_op jit(solution)/shard_map/ppermute | solution.py:272
  303.4 45.9 %collective-permute-start.24 = (bf16[512,2048]{1,0:T(8,128)(2,1)S(1)}, bf16[512,2048]{1,0:T(8,128)(2,1)}, u32[]{:S(2)}, u32[]{:S(2)}) collective-permute-start(bf16[512,2048]{1,0:T(8,128)(2,1)S(1)} %pad_maximum_fusion.4.refs_0_), channel_id=1, source_target_pairs={{0,16},{4,20},{8,24},{12,28},{16,0},{20,4},{24,8},{28,12},{1,17},{... | collective-permute-start | bytes 6291464 | tf_op jit(solution)/shard_map/ppermute | solution.py:319
  304.8 45.8 %collective-permute-start.25 = (bf16[512,2048]{1,0:T(8,128)(2,1)}, bf16[512,2048]{1,0:T(8,128)(2,1)}, u32[]{:S(2)}, u32[]{:S(2)}) collective-permute-start(bf16[512,2048]{1,0:T(8,128)(2,1)} %pad_maximum_fusion.5.refs_1_), channel_id=1, source_target_pairs={{0,8},{4,12},{8,0},{12,4},{16,24},{20,28},{24,16},{28,20},{1,9},{5... | collective-permute-start | bytes 6291464 | tf_op jit(solution)/shard_map/ppermute | solution.py:319
  306.3 45.1 %collective-permute-start.22 = (bf16[512,2048]{1,0:T(8,128)(2,1)S(1)}, bf16[512,2048]{1,0:T(8,128)(2,1)}, u32[]{:S(2)}, u32[]{:S(2)}) collective-permute-start(bf16[512,2048]{1,0:T(8,128)(2,1)S(1)} %pad_maximum_fusion.4.refs_0_), channel_id=1, source_target_pairs={{0,4},{4,0},{8,12},{12,8},{16,20},{20,16},{24,28},{28,24},{1,5},{5... | collective-permute-start | bytes 6291464 | tf_op jit(solution)/shard_map/ppermute | solution.py:319
  306.3 45.1 %collective-permute-start.23 = (bf16[512,2048]{1,0:T(8,128)(2,1)}, bf16[512,2048]{1,0:T(8,128)(2,1)}, u32[]{:S(2)}, u32[]{:S(2)}) collective-permute-start(bf16[512,2048]{1,0:T(8,128)(2,1)} %pad_maximum_fusion.5.refs_1_), channel_id=1, source_target_pairs={{0,4},{4,0},{8,12},{12,8},{16,20},{20,16},{24,28},{28,24},{1,5},{5... | collective-permute-start | bytes 6291464 | tf_op jit(solution)/shard_map/ppermute | solution.py:319
  349.2 37.4 %collective-permute-start.26 = (bf16[512,2048]{1,0:T(8,128)(2,1)}, bf16[512,2048]{1,0:T(8,128)(2,1)S(1)}, u32[]{:S(2)}, u32[]{:S(2)}) collective-permute-start(bf16[512,2048]{1,0:T(8,128)(2,1)} %collective-permute-done.24.refs_0_.refs_4_), channel_id=1, source_target_pairs={{0,4},{4,0},{8,12},{12,8},{16,20},{20,16},{24,28},{28,24},{1,5},{5... | collective-permute-start | bytes 6291464 | tf_op jit(solution)/shard_map/ppermute | solution.py:319
  350.6 36.1 %collective-permute-start.27 = (bf16[512,2048]{1,0:T(8,128)(2,1)}, bf16[512,2048]{1,0:T(8,128)(2,1)}, u32[]{:S(2)}, u32[]{:S(2)}) collective-permute-start(bf16[512,2048]{1,0:T(8,128)(2,1)} %collective-permute-done.25.refs_1_.refs_5_), channel_id=1, source_target_pairs={{0,4},{4,0},{8,12},{12,8},{16,20},{20,16},{24,28},{28,24},{1,5},{5... | collective-permute-start | bytes 6291464 | tf_op jit(solution)/shard_map/ppermute | solution.py:319
  371.8 187.8 %copy-start.15 = (bf16[512,1024]{1,0:T(8,128)(2,1)}, bf16[512,1024]{1,0:T(8,128)(2,1)S(1)}, u32[]{:S(2)}) copy-start(bf16[512,1024]{1,0:T(8,128)(2,1)S(1)} %get-tuple-element.192.refs_2_) | copy-start | bytes 3145732
  379.5 107.5 %collective-permute-start.30 = (bf16[512,2048]{1,0:T(8,128)(2,1)}, bf16[512,2048]{1,0:T(8,128)(2,1)S(1)}, u32[]{:S(2)}, u32[]{:S(2)}) collective-permute-start(bf16[512,2048]{1,0:T(8,128)(2,1)} %convolution_convert_fusion.7), channel_id=1, source_target_pairs={{0,4},{4,0},{8,12},{12,8},{16,20},{20,16},{24,28},{28,24},{1,5},{5... | collective-permute-start | bytes 6291464 | tf_op jit(solution)/shard_map/ppermute | solution.py:319
  408.4 98.7 %copy-start.8 = (bf16[512,1024]{1,0:T(8,128)(2,1)}, bf16[512,1024]{1,0:T(8,128)(2,1)S(1)}, u32[]{:S(2)}) copy-start(bf16[512,1024]{1,0:T(8,128)(2,1)S(1)} %get-tuple-element.203.refs_4_) | copy-start | bytes 3145732
  415.1 22.2 %collective-permute-start.28 = (bf16[512,2048]{1,0:T(8,128)(2,1)S(1)}, bf16[512,2048]{1,0:T(8,128)(2,1)S(1)}, u32[]{:S(2)}, u32[]{:S(2)}) collective-permute-start(bf16[512,2048]{1,0:T(8,128)(2,1)S(1)} %convolution_convert_fusion.9), channel_id=1, source_target_pairs={{0,4},{4,0},{8,12},{12,8},{16,20},{20,16},{24,28},{28,24},{1,5},{5... | collective-permute-start | bytes 6291464 | tf_op jit(solution)/shard_map/ppermute | solution.py:319
  419.8 22.3 %collective-permute-start.29 = (bf16[512,2048]{1,0:T(8,128)(2,1)S(1)}, bf16[512,2048]{1,0:T(8,128)(2,1)S(1)}, u32[]{:S(2)}, u32[]{:S(2)}) collective-permute-start(bf16[512,2048]{1,0:T(8,128)(2,1)S(1)} %convolution_convert_fusion.8), channel_id=1, source_target_pairs={{0,4},{4,0},{8,12},{12,8},{16,20},{20,16},{24,28},{28,24},{1,5},{5... | collective-permute-start | bytes 6291464 | tf_op jit(solution)/shard_map/ppermute | solution.py:319
  424.9 24.1 %collective-permute-start.38 = (bf16[512,2048]{1,0:T(8,128)(2,1)S(1)}, bf16[512,2048]{1,0:T(8,128)(2,1)S(1)}, u32[]{:S(2)}, u32[]{:S(2)}) collective-permute-start(bf16[512,2048]{1,0:T(8,128)(2,1)S(1)} %convolution_convert_fusion.4), channel_id=1, source_target_pairs={{0,4},{4,0},{8,12},{12,8},{16,20},{20,16},{24,28},{28,24},{1,5},{5... | collective-permute-start | bytes 6291464 | tf_op jit(solution)/shard_map/ppermute | solution.py:319
  430.9 69.7 %collective-permute-start.32 = (bf16[512,2048]{1,0:T(8,128)(2,1)}, bf16[512,2048]{1,0:T(8,128)(2,1)}, u32[]{:S(2)}, u32[]{:S(2)}) collective-permute-start(bf16[512,2048]{1,0:T(8,128)(2,1)} %convolution_convert_fusion.6), channel_id=1, source_target_pairs={{0,4},{4,0},{8,12},{12,8},{16,20},{20,16},{24,28},{28,24},{1,5},{5... | collective-permute-start | bytes 6291464 | tf_op jit(solution)/shard_map/ppermute | solution.py:319
  437.3 74.3 %collective-permute-start.37 = (bf16[512,2048]{1,0:T(8,128)(2,1)}, bf16[512,2048]{1,0:T(8,128)(2,1)}, u32[]{:S(2)}, u32[]{:S(2)}) collective-permute-start(bf16[512,2048]{1,0:T(8,128)(2,1)} %convolution_convert_fusion.5), channel_id=1, source_target_pairs={{0,4},{4,0},{8,12},{12,8},{16,20},{20,16},{24,28},{28,24},{1,5},{5... | collective-permute-start | bytes 6291464 | tf_op jit(solution)/shard_map/ppermute | solution.py:319
  448.4 48.1 %collective-permute-start.31 = (bf16[512,2048]{1,0:T(8,128)(2,1)S(1)}, bf16[512,2048]{1,0:T(8,128)(2,1)}, u32[]{:S(2)}, u32[]{:S(2)}) collective-permute-start(bf16[512,2048]{1,0:T(8,128)(2,1)S(1)} %add_convert_fusion.7), channel_id=1, source_target_pairs={{0,16},{4,20},{8,24},{12,28},{16,0},{20,4},{24,8},{28,12},{1,17},{... | collective-permute-start | bytes 6291464 | tf_op jit(solution)/shard_map/ppermute | solution.py:319
  449.0 51.6 %collective-permute-start.33 = (bf16[512,2048]{1,0:T(8,128)(2,1)}, bf16[512,2048]{1,0:T(8,128)(2,1)}, u32[]{:S(2)}, u32[]{:S(2)}) collective-permute-start(bf16[512,2048]{1,0:T(8,128)(2,1)} %add_convert_fusion.6), channel_id=1, source_target_pairs={{0,8},{4,12},{8,0},{12,4},{16,24},{20,28},{24,16},{28,20},{1,9},{5... | collective-permute-start | bytes 6291464 | tf_op jit(solution)/shard_map/ppermute | solution.py:319
  504.3 26.8 %collective-permute-start.34 = (bf16[8,64,1024]{2,1,0:T(8,128)(2,1)S(1)}, bf16[8,64,1024]{2,1,0:T(8,128)(2,1)S(1)}, u32[]{:S(2)}, u32[]{:S(2)}) collective-permute-start(bf16[8,64,1024]{2,1,0:T(8,128)(2,1)S(1)} %dynamic-slice_bitcast_fusion.1), channel_id=1, source_target_pairs={{0,1},{1,2},{2,3},{3,0},{4,5},{5,6},{6,7},{7,4},{8,9},{9,10},{10,1... | collective-permute-start | bytes 3145736 | tf_op jit(solution)/shard_map/ppermute | solution.py:272
  504.7 24.8 %collective-permute-start.36 = (bf16[256,2048]{1,0:T(8,128)(2,1)S(1)}, bf16[256,2048]{1,0:T(8,128)(2,1)S(1)}, u32[]{:S(2)}, u32[]{:S(2)}) collective-permute-start(bf16[256,2048]{1,0:T(8,128)(2,1)S(1)} %slice.212), channel_id=1, source_target_pairs={{0,16},{4,20},{8,24},{12,28},{16,0},{20,4},{24,8},{28,12},{1,17},{... | collective-permute-start | bytes 3145736 | tf_op jit(solution)/shard_map/ppermute | solution.py:319
  505.5 24.6 %collective-permute-start.35 = (bf16[256,2048]{1,0:T(8,128)(2,1)S(1)}, bf16[256,2048]{1,0:T(8,128)(2,1)S(1)}, u32[]{:S(2)}, u32[]{:S(2)}) collective-permute-start(bf16[256,2048]{1,0:T(8,128)(2,1)S(1)} %slice.213), channel_id=1, source_target_pairs={{0,8},{4,12},{8,0},{12,4},{16,24},{20,28},{24,16},{28,20},{1,9},{5... | collective-permute-start | bytes 3145736 | tf_op jit(solution)/shard_map/ppermute | solution.py:319
  556.3 251.9 %reduce-scatter.5.cloned.1.call-start = ((), (), s32[]{:S(2)}) async-start(), calls=%async_computation.9 | async-start | bytes 11796480 | tf_op jit(solution)/shard_map/reduce_scatter | solution.py:267
  559.1 25.8 %collective-permute-start.39 = (bf16[8,64,1024]{2,1,0:T(8,128)(2,1)S(1)}, bf16[8,64,1024]{2,1,0:T(8,128)(2,1)S(1)}, u32[]{:S(2)}, u32[]{:S(2)}) collective-permute-start(bf16[8,64,1024]{2,1,0:T(8,128)(2,1)S(1)} %convert_add_fusion.10), channel_id=1, source_target_pairs={{0,1},{1,2},{2,3},{3,0},{4,5},{5,6},{6,7},{7,4},{8,9},{9,10},{10,1... | collective-permute-start | bytes 3145736 | tf_op jit(solution)/shard_map/ppermute | solution.py:272
  565.6 100.2 %collective-permute-start.46 = (bf16[512,2048]{1,0:T(8,128)(2,1)}, bf16[512,2048]{1,0:T(8,128)(2,1)}, u32[]{:S(2)}, u32[]{:S(2)}) collective-permute-start(bf16[512,2048]{1,0:T(8,128)(2,1)} %convolution_convert_fusion.3), channel_id=1, source_target_pairs={{0,4},{4,0},{8,12},{12,8},{16,20},{20,16},{24,28},{28,24},{1,5},{5... | collective-permute-start | bytes 6291464 | tf_op jit(solution)/shard_map/ppermute | solution.py:319
  566.5 70.9 %collective-permute-start.42 = (bf16[512,2048]{1,0:T(8,128)(2,1)}, bf16[512,2048]{1,0:T(8,128)(2,1)}, u32[]{:S(2)}, u32[]{:S(2)}) collective-permute-start(bf16[512,2048]{1,0:T(8,128)(2,1)} %add_convert_fusion.3), channel_id=1, source_target_pairs={{0,16},{4,20},{8,24},{12,28},{16,0},{20,4},{24,8},{28,12},{1,17},{... | collective-permute-start | bytes 6291464 | tf_op jit(solution)/shard_map/ppermute | solution.py:319
  568.0 70.5 %collective-permute-start.43 = (bf16[512,2048]{1,0:T(8,128)(2,1)}, bf16[512,2048]{1,0:T(8,128)(2,1)}, u32[]{:S(2)}, u32[]{:S(2)}) collective-permute-start(bf16[512,2048]{1,0:T(8,128)(2,1)} %add_convert_fusion.2), channel_id=1, source_target_pairs={{0,8},{4,12},{8,0},{12,4},{16,24},{20,28},{24,16},{28,20},{1,9},{5... | collective-permute-start | bytes 6291464 | tf_op jit(solution)/shard_map/ppermute | solution.py:319
  587.7 50.9 %collective-permute-start.41 = (bf16[8,64,1024]{2,1,0:T(8,128)(2,1)}, bf16[8,64,1024]{2,1,0:T(8,128)(2,1)}, u32[]{:S(2)}, u32[]{:S(2)}) collective-permute-start(bf16[8,64,1024]{2,1,0:T(8,128)(2,1)} %convert_add_fusion.9), channel_id=1, source_target_pairs={{0,1},{1,2},{2,3},{3,0},{4,5},{5,6},{6,7},{7,4},{8,9},{9,10},{10,1... | collective-permute-start | bytes 3145736 | tf_op jit(solution)/shard_map/ppermute | solution.py:272
  618.0 8.3 collective-permute-start.40
  649.9 10.2 %collective-permute-start.44 = (bf16[2,256,256]{2,1,0:T(8,128)(2,1)S(1)}, bf16[2,256,256]{2,1,0:T(8,128)(2,1)S(1)}, u32[]{:S(2)}, u32[]{:S(2)}) collective-permute-start(bf16[2,256,256]{2,1,0:T(8,128)(2,1)S(1)} %convert_add_fusion.15), channel_id=1, source_target_pairs={{0,1},{1,2},{2,3},{3,0},{4,5},{5,6},{6,7},{7,4},{8,9},{9,10},{10,1... | collective-permute-start | bytes 786440 | tf_op jit(solution)/shard_map/ppermute | solution.py:272
  660.9 11.9 %collective-permute-start.45 = (bf16[2,256,256]{2,1,0:T(8,128)(2,1)}, bf16[2,256,256]{2,1,0:T(8,128)(2,1)S(1)}, u32[]{:S(2)}, u32[]{:S(2)}) collective-permute-start(bf16[2,256,256]{2,1,0:T(8,128)(2,1)} %fusion.27), channel_id=1, source_target_pairs={{0,1},{1,2},{2,3},{3,0},{4,5},{5,6},{6,7},{7,4},{8,9},{9,10},{10,1... | collective-permute-start | bytes 786440 | tf_op jit(solution)/shard_map/ppermute | solution.py:272
  702.2 6.4 collective-permute-start.48
  720.6 87.7 %collective-permute-start.49 = (bf16[256,2048]{1,0:T(8,128)(2,1)}, bf16[256,2048]{1,0:T(8,128)(2,1)S(1)}, u32[]{:S(2)}, u32[]{:S(2)}) collective-permute-start(bf16[256,2048]{1,0:T(8,128)(2,1)} %slice.210), channel_id=1, source_target_pairs={{0,16},{4,20},{8,24},{12,28},{16,0},{20,4},{24,8},{28,12},{1,17},{... | collective-permute-start | bytes 3145736 | tf_op jit(solution)/shard_map/ppermute | solution.py:319
  720.6 66.5 %all-to-all-start.1 = ((bf16[8,64,1024]{2,1,0:T(8,128)(2,1)}), bf16[8,64,1024]{2,1,0:T(8,128)(2,1)S(1)}, u32[]{:S(2)}, u32[]{:S(2)}) async-start(bf16[8,64,1024]{2,1,0:T(8,128)(2,1)} %convert_add_fusion.8), calls=%async_computation.5 | async-start | bytes 2097152 | tf_op jit(solution)/shard_map/all_to_all | solution.py:534
  725.3 133.8 %reduce-scatter.11.cloned.1.call-start = ((), (), s32[]{:S(2)}) async-start(), calls=%async_computation.12 | async-start | bytes 1310720 | tf_op jit(solution)/shard_map/reduce_scatter | solution.py:268
  753.8 27.5 %collective-permute-start.50 = (bf16[256,2048]{1,0:T(8,128)(2,1)}, bf16[256,2048]{1,0:T(8,128)(2,1)}, u32[]{:S(2)}, u32[]{:S(2)}) collective-permute-start(bf16[256,2048]{1,0:T(8,128)(2,1)} %dynamic-slice_bitcast_fusion), channel_id=1, source_target_pairs={{0,1},{1,2},{2,3},{3,0},{4,5},{5,6},{6,7},{7,4},{8,9},{9,10},{10,1... | collective-permute-start | bytes 3145736 | tf_op jit(solution)/shard_map/ppermute | solution.py:272
  754.3 132.5 %reduce-scatter.7.cloned.1.call-start = ((), (), s32[]{:S(2)}) async-start(), calls=%async_computation.10 | async-start | bytes 1638400 | tf_op jit(solution)/shard_map/reduce_scatter | solution.py:268
  760.8 53.2 %collective-permute-start.47 = (bf16[256,2048]{1,0:T(8,128)(2,1)}, bf16[256,2048]{1,0:T(8,128)(2,1)S(1)}, u32[]{:S(2)}, u32[]{:S(2)}) collective-permute-start(bf16[256,2048]{1,0:T(8,128)(2,1)} %slice.211), channel_id=1, source_target_pairs={{0,8},{4,12},{8,0},{12,4},{16,24},{20,28},{24,16},{28,20},{1,9},{5... | collective-permute-start | bytes 3145736 | tf_op jit(solution)/shard_map/ppermute | solution.py:319
  784.3 26.7 %collective-permute-start.51 = (bf16[256,2048]{1,0:T(8,128)(2,1)}, bf16[256,2048]{1,0:T(8,128)(2,1)}, u32[]{:S(2)}, u32[]{:S(2)}) collective-permute-start(bf16[256,2048]{1,0:T(8,128)(2,1)} %fusion.23), channel_id=1, source_target_pairs={{0,1},{1,2},{2,3},{3,0},{4,5},{5,6},{6,7},{7,4},{8,9},{9,10},{10,1... | collective-permute-start | bytes 3145736 | tf_op jit(solution)/shard_map/ppermute | solution.py:272
  813.2 42.9 %collective-permute-start.52 = (bf16[256,2048]{1,0:T(8,128)(2,1)S(1)}, bf16[256,2048]{1,0:T(8,128)(2,1)S(1)}, u32[]{:S(2)}, u32[]{:S(2)}) collective-permute-start(bf16[256,2048]{1,0:T(8,128)(2,1)S(1)} %fusion.22), channel_id=1, source_target_pairs={{0,1},{1,2},{2,3},{3,0},{4,5},{5,6},{6,7},{7,4},{8,9},{9,10},{10,1... | collective-permute-start | bytes 3145736 | tf_op jit(solution)/shard_map/ppermute | solution.py:272
  (72 other events, 848.5 us)
Sparse Core Ops, SparseCore 0:
  17.6 35.3 all-gather.3
  55.0 77.0 all-gather.5
  134.5 58.0 all-gather.7
  556.5 96.4 reduce-scatter.8
  695.2 113.0 reduce-scatter.4
  810.5 44.5 reduce-scatter.10
  857.4 29.3 reduce-scatter.6

commit v4 on v3

--- a/solution.py
+++ b/solution.py
@@ -14,6 +14,7 @@
 F32 = jnp.float32
 BF16 = jnp.bfloat16
 BOTH = ("dp", "fsdp")
+HASTE = 8
 
 
 def dot_nn(left, right):
@@ -117,9 +118,9 @@
 
 def attn_cost(windows, span, win, products):
     return pl.CostEstimate(
-        flops=2 * products * windows * HEADS * span * win * HD,
-        transcendentals=windows * HEADS * span * win,
-        bytes_accessed=products * windows * HEADS * span * HD * 2,
+        flops=2 * products * windows * HEADS * span * win * HD // HASTE,
+        transcendentals=windows * HEADS * span * win // HASTE,
+        bytes_accessed=products * windows * HEADS * span * HD * 2 // HASTE,
     )
 
 
@@ -170,45 +171,82 @@
 
 
 def middle_kernel(count, *refs):
-    blocks, backs = refs[:count], refs[count : 2 * count]
-    up_ref, bias_ref = refs[2 * count], refs[2 * count + 1]
-    hiddens = refs[2 * count + 2 : 3 * count + 2]
-    pres = refs[3 * count + 2 :]
+    blocks, back_ref = refs[:count], refs[count]
+    up_ref, bias_ref = refs[count + 1], refs[count + 2]
+    outs = refs[count + 3 :]
+    groups = len(outs) // 2
+    size = blocks[0].shape[0]
     root = math.sqrt(2.0 / math.pi)
-    for block, back, hidden, pre in zip(blocks, backs, hiddens, pres):
+    for i, block in enumerate(blocks):
         act = jnp.dot(block[...], up_ref[...], preferred_element_type=F32) + bias_ref[...]
         square = act * act
-        bent = jnp.tanh(root * act * (1.0 + 0.044715 * square))
+        bent = jnp.tanh(act * (root + (root * 0.044715) * square))
         upper = 0.5 + 0.5 * bent
-        hidden[...] = (act * upper).astype(BF16)
-        slope = upper + (0.5 * root) * act * (1.0 - bent * bent) * (1.0 + (3 * 0.044715) * square)
-        pre[...] = (back[...].astype(F32) * slope).astype(BF16)
-
-
-def middle_layer(blocks, backs, up_part, bias, tile=256):
+        slope = upper + act * (1.0 - bent * bent) * (0.5 * root + (1.5 * 0.044715 * root) * square)
+        back = back_ref[i * size : (i + 1) * size, :].astype(F32)
+        group, place = divmod(i, count // groups)
+        at = slice(place * size, (place + 1) * size)
+        outs[group][at, :] = (act * upper).astype(BF16)
+        outs[groups + group][at, :] = (back * slope).astype(BF16)
+
+
+def middle_layer(blocks, back, up_part, bias, tile=512):
     count = len(blocks)
     size, width = blocks[0].shape
     units = up_part.shape[1]
     tile = min(tile, units)
     one = pl.Buffered(buffer_count=1)
+    group = size * count // 2
     whole = pl.BlockSpec((size, width), lambda j: (0, 0), pipeline_mode=one)
-    slab = pl.BlockSpec((size, tile), lambda j: (0, j))
+    slab = pl.BlockSpec((group, tile), lambda j: (0, j))
     out = pl.pallas_call(
         functools.partial(middle_kernel, count),
-        out_shape=[jax.ShapeDtypeStruct((size, units), BF16)] * (2 * count),
+        out_shape=[jax.ShapeDtypeStruct((group, units), BF16)] * 4,
         grid=(units // tile,),
         in_specs=[whole] * count
-        + [slab] * count
-        + [pl.BlockSpec((width, tile), lambda j: (0, j)), pl.BlockSpec((1, tile), lambda j: (0, j))],
-        out_specs=[slab] * (2 * count),
+        + [
+            pl.BlockSpec((size * count, tile), lambda j: (0, j)),
+            pl.BlockSpec((width, tile), lambda j: (0, j)),
+            pl.BlockSpec((1, tile), lambda j: (0, j)),
+        ],
+        out_specs=[slab] * 4,
         compiler_params=pltpu.CompilerParams(vmem_limit_bytes=48 * 2**20),
         cost_estimate=pl.CostEstimate(
-            flops=2 * count * size * width * units,
-            transcendentals=count * size * units,
-            bytes_accessed=2 * (count * size * (width + 3 * units) + width * units),
+            flops=2 * count * size * width * units // HASTE,
+            transcendentals=count * size * units // HASTE,
+            bytes_accessed=2 * (count * size * (width + 3 * units) + width * units) // HASTE,
         ),
-    )(*blocks, *backs, up_part, bias.reshape(1, units))
-    return list(out[:count]), list(out[count:])
+    )(*blocks, back, up_part, bias.reshape(1, units))
+    return list(out[:2]), list(out[2:])
+
+
+def back_kernel(count, *refs):
+    blocks, weight_ref, out = refs[:count], refs[count], refs[count + 1]
+    size = blocks[0].shape[0]
+    for i, block in enumerate(blocks):
+        out[i * size : (i + 1) * size, :] = dot_nt(block[...], weight_ref[...]).astype(BF16)
+
+
+def back_product(blocks, weight, tile=512):
+    count = len(blocks)
+    size, width = blocks[0].shape
+    units = weight.shape[0]
+    tile = min(tile, units)
+    one = pl.Buffered(buffer_count=1)
+    return pl.pallas_call(
+        functools.partial(back_kernel, count),
+        out_shape=jax.ShapeDtypeStruct((size * count, units), BF16),
+        grid=(units // tile,),
+        in_specs=[pl.BlockSpec((size, width), lambda j: (0, 0), pipeline_mode=one)] * count
+        + [pl.BlockSpec((tile, width), lambda j: (j, 0))],
+        out_specs=pl.BlockSpec((size * count, tile), lambda j: (0, j)),
+        compiler_params=pltpu.CompilerParams(vmem_limit_bytes=48 * 2**20),
+        cost_estimate=pl.CostEstimate(
+            flops=2 * count * size * width * units // HASTE,
+            transcendentals=0,
+            bytes_accessed=2 * (count * size * (width + units) + width * units) // HASTE,
+        ),
+    )(*blocks, weight)
 
 
 def weight_kernel(count, *refs):
@@ -219,26 +257,69 @@
     out[...] = total.astype(BF16)
 
 
-def weight_grad(lefts, rights, tile=256):
+def in_blocks(arrays, size):
+    return [(array, i) for array in arrays for i in range(array.shape[0] // size)]
+
+
+def weight_grad(lefts, rights, size, tile=256):
+    lefts, rights = in_blocks(lefts, size), in_blocks(rights, size)
     count = len(lefts)
-    size, height = lefts[0].shape
-    breadth = rights[0].shape[1]
+    height, breadth = lefts[0][0].shape[1], rights[0][0].shape[1]
     tile = min(tile, height)
-    one = pl.Buffered(buffer_count=1)
+
+    def left_spec(row):
+        return pl.BlockSpec((size, tile), lambda i: (row, i))
+
+    def right_spec(row):
+        return pl.BlockSpec((size, breadth), lambda i: (row, 0), pipeline_mode=pl.Buffered(buffer_count=1))
+
     return pl.pallas_call(
         functools.partial(weight_kernel, count),
         out_shape=jax.ShapeDtypeStruct((height, breadth), BF16),
         grid=(height // tile,),
-        in_specs=[pl.BlockSpec((size, tile), lambda i: (0, i))] * count
-        + [pl.BlockSpec((size, breadth), lambda i: (0, 0), pipeline_mode=one)] * count,
+        in_specs=[left_spec(row) for _, row in lefts] + [right_spec(row) for _, row in rights],
         out_specs=pl.BlockSpec((tile, breadth), lambda i: (i, 0)),
         compiler_params=pltpu.CompilerParams(vmem_limit_bytes=52 * 2**20),
         cost_estimate=pl.CostEstimate(
-            flops=2 * count * size * height * breadth,
+            flops=2 * count * size * height * breadth // HASTE,
             transcendentals=0,
-            bytes_accessed=2 * (count * size * (height + breadth) + height * breadth),
+            bytes_accessed=2 * (count * size * (height + breadth) + height * breadth) // HASTE,
         ),
-    )(*lefts, *rights)
+    )(*[array for array, _ in lefts], *[array for array, _ in rights])
+
+
+def reorder_kernel(place_ref, first_ref, second_ref, first_out, second_out):
+    first_out[...] = first_ref[...]
+    second_out[...] = second_ref[...]
+
+
+def reorder(values, places):
+    rows, width = values.shape
+    count = places.shape[1]
+    block = width // (2 * count)
+    if block % 128:
+        return [
+            jnp.concatenate(
+                [lax.dynamic_slice_in_dim(values, places[i, j] * block, block, 1) for j in range(count)],
+                axis=1,
+            )
+            for i in (0, 1)
+        ]
+    out = pl.BlockSpec((rows, block), lambda i, place: (0, i))
+    return pl.pallas_call(
+        reorder_kernel,
+        out_shape=[jax.ShapeDtypeStruct((rows, width // 2), values.dtype)] * 2,
+        grid_spec=pltpu.PrefetchScalarGridSpec(
+            num_scalar_prefetch=1,
+            grid=(count,),
+            in_specs=[
+                pl.BlockSpec((rows, block), lambda i, place: (0, place[0, i])),
+                pl.BlockSpec((rows, block), lambda i, place: (0, place[1, i])),
+            ],
+            out_specs=[out, out],
+        ),
+        cost_estimate=pl.CostEstimate(flops=0, transcendentals=0, bytes_accessed=4 * rows * width // HASTE),
+    )(places, values, values)
 
 
 def norm_stats(values):
@@ -314,6 +395,20 @@
         bits = [1 << i for i in range(1, count.bit_length() - 1)]
         self.orders = (bits, bits[::-1])
         self.steps = len(bits)
+        self.near, self.far = [], []
+        for order in self.orders:
+            near = [0]
+            for bit in order[:-1]:
+                near = near + [offset ^ bit for offset in near]
+            self.near.append(near)
+            self.far.append([offset ^ order[-1] for offset in near])
+
+    def places(self):
+        me = lax.axis_index("dp")
+        order = [(o, h) for h in (0, 1) for o in self.far[h] + self.near[h]]
+        return jnp.stack(
+            [jnp.stack([2 * (me ^ o ^ core) + h for o, h in order]) for core in (0, 1)]
+        ).astype(jnp.int32)
 
     def swap(self, block, bit):
         return lax.ppermute(block, "dp", [(i, i ^ bit) for i in range(self.count)])
@@ -445,10 +540,9 @@
         attended, down_pieces[-1], up_cols = tie(attended, down_pieces[-1], up_cols)
         up_pieces = [up_cols, shift(up_cols, n_z)]
         down_part = put_in_order(down_pieces, n_z)
-        grad_near_sib = plane.cross(grad_near)
-        grad_lots = [[*grad_near, *grad_near_sib]]
-        backs = [[dot_nt(block, down_part).astype(BF16) for block in grad_lots[0]]]
-        attended, *backs[0] = tie(attended, *backs[0])
+        grad_lots = [[*grad_near, *plane.cross(grad_near)]]
+        back_near = back_product(grad_lots[0], down_part)
+        attended, back_near = tie(attended, back_near)
         middle = inputs + dot_nn(attended, full_o) + bias_o
         mean_two, recip_two = norm_stats(middle)
         xhat_two = (middle - mean_two) * recip_two
@@ -456,50 +550,66 @@
 
         normed_two, up_pieces[-1], *grad_far = tie(normed_two, up_pieces[-1], *grad_far)
         two_near = [normed_two[:half], normed_two[half:]]
-        while len(up_pieces) < n_z:
+        while len(up_pieces) < min(3, n_z):
             up_pieces.append(shift(up_pieces[-1], n_z))
         for step in range(plane.steps - 1):
             two_near = plane.grow(two_near, step)
         grad_lots.append([*grad_far, *plane.cross(grad_far)])
-        backs.append([dot_nt(block, down_part).astype(BF16) for block in grad_lots[1]])
+        back_far = back_product(grad_lots[1], down_part)
+        two_near[0], two_near[1], up_pieces[-1], back_far = tie(*two_near, up_pieces[-1], back_far)
+
+        while len(up_pieces) < n_z:
+            up_pieces.append(shift(up_pieces[-1], n_z))
         up_part = put_in_order(up_pieces, n_z, 1).reshape(width, ff_own)
         bias_up_part = lax.dynamic_slice_in_dim(bias_up, my_dp * ff_own, ff_own)
-        two_near[0], two_near[1], up_part, *backs[1] = tie(*two_near, up_part, *backs[1])
-
         two_far = plane.across(two_near, plane.steps - 1)
         two_lots = [[*two_near, *plane.cross(two_near)], [*two_far, *plane.cross(two_far)]]
-        near = middle_layer(two_lots[0], backs[0], up_part, bias_up_part)
-        backs[1][0], *pres = tie(backs[1][0], *near[1])
-        far = middle_layer(two_lots[1], backs[1], up_part, bias_up_part)
-        hiddens, pres = [near[0], far[0]], [pres, far[1]]
-
-        def core_sum(lot, weight, product):
-            theirs = plane.cross([product(block, weight).astype(BF16) for block in lot[2:]])
+        hid_near, pre_near = middle_layer(two_lots[0], back_near, up_part, bias_up_part)
+        places = plane.places()
+        back_far, attended, pre_near[0], pre_near[1], places = tie(back_far, attended, *pre_near, places)
+        one_mine, one_sib = reorder(normed_one, places)
+        att_mine, att_sib = reorder(attended, places)
+        hid_far, pre_far = middle_layer(two_lots[1], back_far, up_part, bias_up_part)
+        block = two_near[0].shape[0]
+
+        def lot_sum(lot, weight, product):
+            theirs = plane.swap(product(lot[1], weight).astype(BF16), 1)
+            return (product(lot[0], weight) + theirs.astype(F32)).astype(BF16)
+
+        def lot_halves(lot, weight, product):
+            theirs = plane.swap(product(lot[1], weight).astype(BF16), 1).astype(F32)
+            ours = lot[0]
             return [
-                (product(block, weight) + there.astype(F32)).astype(BF16)
-                for block, there in zip(lot[:2], theirs)
+                (product(ours[at], weight) + theirs[at]).astype(BF16)
+                for at in (slice(None, block), slice(block, None))
             ]
 
-        def merge(halves, far_halves):
-            got = plane.across(far_halves, plane.steps - 1)
-            return [half.astype(F32) + there.astype(F32) for half, there in zip(halves, got)]
-
-        two_far = core_sum(pres[1], up_part, dot_nt)
-        pres[0][0], *two_far = tie(pres[0][0], *two_far)
-        two_near = core_sum(pres[0], up_part, dot_nt)
-        two_sum = merge(two_near, two_far)
-        up_terms = weight_grad(two_lots[0] + two_lots[1], pres[0] + pres[1])
-        up_terms, hiddens[1][0], *two_sum = tie(up_terms, hiddens[1][0], *two_sum)
+        def merge(whole, got):
+            size = got[0].shape[0]
+            return [whole[i * size : (i + 1) * size].astype(F32) + got[i].astype(F32) for i in (0, 1)]
+
+        two_far = lot_halves(pre_far, up_part, dot_nt)
+        pre_near[0], pre_near[1], *two_far = tie(*pre_near, *two_far)
+        got = plane.across(two_far, plane.steps - 1)
+        two_near_sum = lot_sum(pre_near, up_part, dot_nt)
+        two_near_sum, hid_far[0], hid_far[1] = tie(two_near_sum, *hid_far)
+        out_far = lot_halves(hid_far, down_part, dot_nn)
+        out_far[0], out_far[1], pre_far[0] = tie(*out_far, pre_far[0])
+        up_terms = weight_grad(two_lots[0] + two_lots[1], pre_near + pre_far, block)
+        up_ring = Ring(up_terms.reshape(n_dp, n_z, own, ff_own), 1, n_z)
+        two_near_sum, up_terms, hid_far[0], *got = tie(two_near_sum, up_terms, hid_far[0], *got)
+        up_ring.terms = up_terms.reshape(n_dp, n_z, own, ff_own)
+        two_sum = merge(two_near_sum, got)
         for step in range(plane.steps - 2, -1, -1):
             two_sum = plane.fold(two_sum, step)
         two_grad = jnp.concatenate(two_sum)
-        up_ring = Ring(up_terms.reshape(n_dp, n_z, own, ff_own), 1, n_z)
-        out_far = core_sum(hiddens[1], down_part, dot_nn)
-        hiddens[0][0], *out_far = tie(hiddens[0][0], *out_far)
-        up_bias_part = sum(jnp.sum(block.astype(F32), axis=0) for lot in pres for block in lot)
-        two_grad, hiddens[0][0], *out_far = tie(two_grad, hiddens[0][0], *out_far)
-
-        two_grad = up_ring.go(1, two_grad)
+        down_terms = weight_grad(hid_near + hid_far, grad_lots[0] + grad_lots[1], block)
+        two_grad, down_terms = tie(two_grad, down_terms)
+        down_ring = Ring(down_terms.reshape(n_z, ff_own // n_z, width), 0, n_z)
+        up_bias_part = sum(jnp.sum(lot.astype(F32), axis=0) for lot in pre_near + pre_far)
+
+        two_grad, out_far[0], out_far[1] = tie(up_ring.go(1, two_grad), *out_far)
+        out_got = plane.across(out_far, plane.steps - 1)
         grad_out = grad_low.astype(F32)
         grad_bdown = jnp.sum(grad_out, axis=0)
         grad_gain_two = jnp.sum(two_grad * xhat_two, axis=0)
@@ -508,38 +618,57 @@
         grad_bo = jnp.sum(middle_grad, axis=0)
         branch_grad = middle_grad.astype(BF16)
         attended_grad = dot_nt(branch_grad, full_o).astype(BF16)
-        out_got = plane.across(out_far, plane.steps - 1)
-        grad_wo = dot_tn(attended, branch_grad).astype(BF16)
-        attended_grad, grad_wo = tie(attended_grad, grad_wo)
-        grad_wo = scatter_both(grad_wo).astype(F32)
-        attended_grad = up_ring.go(1, attended_grad)
+        attended_grad, branch_late = tie(attended_grad, branch_grad)
+
+        def row_sum(mine, sib, right):
+            theirs = plane.swap(dot_tn(sib, right).astype(BF16), 1)
+            total = (dot_tn(mine, right) + theirs.astype(F32)).astype(BF16)
+            size = total.shape[0] // 4
+            return [total[i * size : (i + 1) * size] for i in range(4)]
+
+        def send_rows(lots):
+            return plane.across([lots[0], lots[2]], plane.steps - 1)
+
+        def own_rows(lots, got):
+            total = [near.astype(F32) + there.astype(F32) for near, there in zip((lots[1], lots[3]), got)]
+            for step in range(plane.steps - 2, -1, -1):
+                total = plane.fold(total, step)
+            return jnp.concatenate(total)
+
+        out_lots = row_sum(att_mine, att_sib, branch_late)
+        attended_grad, *out_lots = tie(up_ring.go(1, attended_grad), *out_lots)
+        out_lots_got = send_rows(out_lots)
 
         query_grad, kv_terms = attn_backward(queries, kv_window, norms, attended_grad, first, file_ends)
-        query_grad, hiddens[0][0], *out_got = tie(query_grad, hiddens[0][0], *out_got)
+        query_grad, kv_terms, hid_near[0], *got = tie(query_grad, kv_terms, hid_near[0], *out_got, *out_lots_got)
+        out_got, out_lots_got = got[:2], got[2:]
         query_grad = up_ring.go(1, query_grad)
         kv_ring = Ring(kv_terms.reshape(windows, n_z, local_len, 2 * HD), 1, n_z)
-        grad_wq = dot_tn(normed_one, query_grad).astype(BF16)
-        grad_wq = kv_ring.go(1, grad_wq)
-        out_near = core_sum(hiddens[0], down_part, dot_nn)
-        out_near[0] = kv_ring.go(n_z - 2, out_near[0])
-        out_sum = [near.astype(F32) + got.astype(F32) for near, got in zip(out_near, out_got)]
+        q_lots = row_sum(one_mine, one_sib, query_grad)
+        q_lots[0] = kv_ring.go(1, q_lots[0])
+        hid_near[0], hid_near[1], query_late, *pieces = tie(*hid_near, query_grad, *q_lots, *out_lots_got)
+        q_lots, out_lots_got = pieces[:4], pieces[4:]
+        q_got = send_rows(q_lots)
+        wo_rows = own_rows(out_lots, out_lots_got)
+        hid_near[0] = kv_ring.go(n_z - 2, hid_near[0])
+        out_sum = merge(lot_sum(hid_near, down_part, dot_nn), out_got)
         for step in range(plane.steps - 2, -1, -1):
             out_sum = plane.fold(out_sum, step)
         kv_grad = kv_ring.finish().astype(BF16).reshape(rows, 2 * HD)
-        kv_grad, hiddens[1][0] = tie(kv_grad, hiddens[1][0])
-        down_terms = weight_grad(hiddens[0] + hiddens[1], grad_lots[0] + grad_lots[1])
-        down_ring = Ring(down_terms.reshape(n_z, ff_own // n_z, width), 0, n_z)
         branch_out = jnp.concatenate(out_sum)
         output = (middle + branch_out + bias_down).astype(BF16).reshape(windows, local_len, width)
+        wo_ring = Ring(wo_rows.reshape(n_z, own, width), 0, n_z)
+        wq_ring = Ring(own_rows(q_lots, q_got).reshape(n_z, own, width), 0, n_z)
+        grad_wo, grad_q = wo_ring.finish(), wq_ring.finish()
         grad_up = lax.all_to_all(
             up_ring.finish().astype(BF16).reshape(n_dp * own, ff_own), "dp", 0, 1, tiled=True
         ).astype(F32)
         grad_down = down_ring.finish()
 
-        grad_bq = jnp.sum(query_grad.astype(F32), axis=0)
+        grad_bq = jnp.sum(query_late.astype(F32), axis=0)
         grad_bv = jnp.sum(kv_grad[:, HD:].astype(F32), axis=0)
         grad_wkv = dot_tn(normed_one, kv_grad)
-        one_grad = dot_nt(query_grad, full_q) + dot_nt(kv_grad, full_kv)
+        one_grad = dot_nt(query_late, full_q) + dot_nt(kv_grad, full_kv)
         grad_gain_one = jnp.sum(one_grad * xhat_one, axis=0)
         grad_shift_one = jnp.sum(one_grad, axis=0)
         tokens_grad = middle_grad + norm_pull(one_grad, xhat_one, recip_one, gain_one)
@@ -564,19 +693,20 @@
             ],
             axis=1,
         )
-        sum_rows = jnp.pad(sum_rows, ((0, 0), (0, spare - sum_rows.shape[1])))
+        sum_lines = -(-(kv_lines + -(-sum(rooms) // width)) // 16) * 16
+        sum_rows = jnp.pad(
+            sum_rows, ((0, 0), (0, (sum_lines - kv_lines) * width - sum_rows.shape[1]))
+        )
         grads = jnp.concatenate(
             [
-                grad_wq.reshape(n_dev, own, width),
                 grad_wkv.astype(BF16).reshape(n_dev, kv_lines, width),
                 sum_rows.reshape(n_dev, -1, width),
             ],
             axis=1,
         )
-        mine = scatter_both(grads.reshape(n_dev * lines, width)).astype(F32)
-        grad_q = mine[:own]
-        grad_kv = mine[own : own + kv_lines].reshape(own, 2 * HD)
-        flat = mine[own + kv_lines :].reshape(-1)
+        mine = scatter_both(grads.reshape(n_dev * sum_lines, width)).astype(F32)
+        grad_kv = mine[:kv_lines].reshape(own, 2 * HD)
+        flat = mine[kv_lines:].reshape(-1)
         bq, bv, bo, gain1, shift1, bup, bdown, gain2, shift2 = (
             flat[start : start + size] for start, size in zip(starts, sizes)
         )

time: 909 us -> 901 us (level)
  matrix products: 207 us -> 117 us
  Pallas kernels: 140 us -> 181 us
  waiting for transfers between devices: 320 us -> 333 us
  local copies, waits for them, and re-layouts: 74 us -> 86.6 us
  other arithmetic: 81.1 us -> 90.4 us
    dot_general x19 -> x8, matrix products: 125 us -> 42.2 us  [dot_nt(): lax.dot_general(left, right, (((1,), (1,)), ((), ())), preferred_element_...]
    pallas_call x0 -> x4, Pallas kernels: none -> 41.6 us  [the longest x2 28.6 us: back_product(): pl.pallas_call(functools.partial(back_kernel, count), out_shape=jax.Shape...]
    ppermute x21 -> x27, waiting for transfers between devices: 146 us -> 178 us  [shift(): lax.ppermute(block, 'fsdp', [(i, (i + 1) % count) for i in range(count)])]
    reduce_scatter x2 -> x1, waiting for transfers between devices: 25.9 us -> 1.03 us  [scatter_both(): return lax.psum_scatter(part, 'fsdp', scatter_dimension=0, tiled=True)]
    ppermute x32 -> x38, waiting for transfers between devices: 114 us -> 138 us  [swap(): return lax.ppermute(block, 'dp', [(i, i ^ bit) for i in range(self.count)])]
    reduce_scatter x2 -> x1, waiting for transfers between devices: 19.5 us -> 0.02 us  [scatter_both(): part = lax.psum_scatter(block, 'dp', scatter_dimension=0, tiled=True)]
    dot_general x11 -> x8, matrix products: 64.5 us -> 54.9 us  [dot_nn(): return jnp.dot(left, right, preferred_element_type=F32)]
    ppermute x32 -> x38, starting transfers between devices: 21.9 us -> 27.8 us  [swap(): return lax.ppermute(block, 'dp', [(i, i ^ bit) for i in range(self.count)])]
  transfers between devices with their start and end apart: 61 -> 71, of which waited for: 27 -> 33; matrix products, arithmetic and copies ran while one was open for 34% -> 22% of each run, Pallas kernels for 16% -> 18%
where the time goes in v4:
time: 901 us; the launch traced here: 891 us
  waiting for transfers between devices  333 us (37%)
  Pallas kernels  181 us (20%)
  matrix products  117 us (13%)
  other arithmetic  90.4 us (10%)
  local copies, waits for them, and re-layouts  86.6 us (10%)
  starting transfers between devices  46.4 us (5%)
  blocking collectives  20.6 us (2%)
  between operations  16 us (2%)
    ppermute x27, waiting for transfers between devices, shift(): lax.ppermute(block, 'fsdp', [(i, (i + 1) % count) for i in range(count)])  178 us
    ppermute x38, waiting for transfers between devices, swap(): return lax.ppermute(block, 'dp', [(i, i ^ bit) for i in range(self.count)])  138 us
    dot_general x8, matrix products, dot_nn(): return jnp.dot(left, right, preferred_element_type=F32)  54.9 us
    pallas_call x2, Pallas kernels, weight_grad(): pl.pallas_call(functools.partial(weight_kernel, count), out_shape=jax.Sha...  51.1 us
    dot_general x8, matrix products, dot_nt(): lax.dot_general(left, right, (((1,), (1,)), ((), ())), preferred_element_...  42.2 us
    pallas_call x2, Pallas kernels, middle_layer(): pl.pallas_call(functools.partial(middle_kernel, count), out_shape=[jax.Sh...  39.4 us
    pallas_call x1, Pallas kernels, attn_backward(): pl.pallas_call(functools.partial(attn_backward_kernel, per_step), out_sha...  30.4 us
    pallas_call x2, Pallas kernels, back_product(): pl.pallas_call(functools.partial(back_kernel, count), out_shape=jax.Shape...  28.6 us
  transfers between devices with their start and end apart: 71, of which 33 were waited for; matrix products, arithmetic and copies ran while one was open for 22% of the time, Pallas kernels for 18%

profile of v4, /device:TPU:0, one launch (start us, length us, event | category | flops | bytes accessed | tf_op | source)
XLA Modules:
  0.0 890.9 jit_solution(12073325264960894165)
XLA Ops:
  18.9 20.6 %all_to_all.26 = bf16[64,8,1024]{2,0,1:T(8,128)(2,1)} all-to-all(bf16[64,8,1024]{2,0,1:T(8,128)(2,1)S(1)} %bitcast.249), channel_id=1, replica_groups=mesh['dp'=8,'fsdp'=4] {'dp'}, dimensions={1} | all-to-all | bytes 2097152 | tf_op jit(solution)/shard_map/all_to_all | solution.py:493
  39.5 13.6 %all-gather.4.cloned.1.call-done = bf16[320,2048]{1,0:T(8,128)(2,1)} async-done(((bf16[80,2048]{1,0:T(8,128)(2,1)}), bf16[320,2048]{1,0:T(8,128)(2,1)}) %all-gather.4.cloned.1.call-update) | async-done | bytes 1310736 | tf_op jit(solution)/shard_map/all_gather | solution.py:489
  54.0 8.4 collective-permute-done
  66.8 3.9 collective-permute-done.1
  71.4 8.2 collective-permute-done.2
  82.2 22.5 %collective-permute-done.5 = bf16[256,2048]{1,0:T(8,128)(2,1)} collective-permute-done((bf16[256,2048]{1,0:T(8,128)(2,1)S(1)}, bf16[256,2048]{1,0:T(8,128)(2,1)}, u32[]{:S(2)}, u32[]{:S(2)}) %collective-permute-start.5) | collective-permute-done | bytes 1048608 | tf_op jit(solution)/shard_map/ppermute | solution.py:414
  108.9 3.3 pad_maximum_fusion.2.refs_1_.refs_9_
  112.5 18.6 %collective-permute-done.4 = bf16[256,2048]{1,0:T(8,128)(2,1)} collective-permute-done((bf16[256,2048]{1,0:T(8,128)(2,1)}, bf16[256,2048]{1,0:T(8,128)(2,1)}, u32[]{:S(2)}, u32[]{:S(2)}) %collective-permute-start.4) | collective-permute-done | bytes 1048608 | tf_op jit(solution)/shard_map/ppermute | solution.py:353
  148.3 8.2 slice.277
  158.8 9.8 %add_convert_fusion.5.q_ref = bf16[512,2048]{1,0:T(8,128)(2,1)} fusion(bf16[512,2048]{1,0:T(8,128)(2,1)} %fusion.18.first_ref.second_ref, bf16[2048,2048]{1,0:T(8,128)(2,1)} %bitcast.235, f32[2048]{0:T(1024)S(1)} %reshape.415), kind=kOutput, calls=%fused_computation.54 | convolution fusion | flops 4297064448 | bytes 12591104 | tf_op jit(solution)/shard_map/dot_general | solution.py:21
  171.3 7.1 collective-permute-done.9
  189.1 18.8 %shard_map.288 = (bf16[512,2048]{1,0:T(8,128)(2,1)S(1)}, f32[512,128]{1,0:T(8,128)S(1)}) custom-call(s32[1]{0:T(128)} %bitcast.1.pos_ref, s32[2,8]{1,0:T(2,128)S(1)} %select_reduce_fusion.ends_ref, bf16[512,2048]{1,0:T(8,128)(2,1)S(1)} %copy-done.7, bf16[2,1024,256]{2,1,0:T(8,128)(2,1)S(1)} %constant_dynamic-update-slice_fusion.17.kv_ref), custom_call_target="tpu_custom_call" | custom-call | flops 536870912 | bytes 524288 | tf_op jit(solution)/shard_map/pallas_call | solution.py:132
  208.0 3.1 constant_dynamic-update-slice_fusion.14
  213.8 14.0 %shard_map.289.refs_4_ = bf16[2048,1024]{1,0:T(8,128)(2,1)} custom-call(bf16[512,2048]{1,0:T(8,128)(2,1)S(1)} %pad_maximum_fusion.1.refs_0_.refs_8_, bf16[512,2048]{1,0:T(8,128)(2,1)} %pad_maximum_fusion.2.refs_1_.refs_9_, bf16[512,2048]{1,0:T(8,128)(2,1)} %collective-permute-done.11.refs_2_.refs_10_, ...), custom_call_target="tpu_custom_call" | custom-call | flops 1073741824 | bytes 2097152 | tf_op jit(solution)/shard_map/pallas_call | solution.py:236
  227.9 9.3 %fusion.49 = (f32[512]{0:T(512)S(1)}, f32[512,2048]{1,0:T(8,128)S(1)}) fusion(f32[2048]{0:T(1024)S(1)} %reshape.416, bf16[512,2048]{1,0:T(8,128)(2,1)} %copy-done.8, bf16[2048,2048]{1,0:T(8,128)(2,1)} %all-gather.8.cloned.1.call-done, bf16[2,256,2048]{2,1,0:T(8,128)(2,1)} %param.17), kind=kOutput, calls=%fused_computation.193 | convolution fusion | flops 4299161088 | bytes 16787456 | tf_op jit(solution)/shard_map/dot_general | solution.py:21
  243.0 22.2 %collective-permute-done.16 = bf16[256,2048]{1,0:T(8,128)(2,1)S(1)} collective-permute-done((bf16[256,2048]{1,0:T(8,128)(2,1)S(1)}, bf16[256,2048]{1,0:T(8,128)(2,1)S(1)}, u32[]{:S(2)}, u32[]{:S(2)}) %collective-permute-start.16) | collective-permute-done | bytes 1048608 | tf_op jit(solution)/shard_map/ppermute | solution.py:414
  269.9 14.5 %shard_map.290.refs_4_ = bf16[2048,1024]{1,0:T(8,128)(2,1)} custom-call(bf16[512,2048]{1,0:T(8,128)(2,1)} %collective-permute-done.14.refs_0_.refs_12_, bf16[512,2048]{1,0:T(8,128)(2,1)} %collective-permute-done.15.refs_1_.refs_13_, bf16[512,2048]{1,0:T(8,128)(2,1)} %copy-done.35, bf16[512,2048]{1,0:T(8,128)(2,1)} %copy-done.36, ...), custom_call_target="tpu_custom_call" | custom-call | flops 1073741824 | bytes 2097152 | tf_op jit(solution)/shard_map/pallas_call | solution.py:236
  286.8 44.5 %collective-permute-done.23.refs_0_.refs_4_ = bf16[512,2048]{1,0:T(8,128)(2,1)} collective-permute-done((bf16[512,2048]{1,0:T(8,128)(2,1)S(1)}, bf16[512,2048]{1,0:T(8,128)(2,1)}, u32[]{:S(2)}, u32[]{:S(2)}) %collective-permute-start.23) | collective-permute-done | bytes 2097184 | tf_op jit(solution)/shard_map/ppermute | solution.py:414
  339.3 20.3 %collective-permute-done.27 = bf16[8,64,1024]{2,1,0:T(8,128)(2,1)} collective-permute-done((bf16[8,64,1024]{2,1,0:T(8,128)(2,1)}, bf16[8,64,1024]{2,1,0:T(8,128)(2,1)}, u32[]{:S(2)}, u32[]{:S(2)}) %collective-permute-start.27) | collective-permute-done | bytes 1048608 | tf_op jit(solution)/shard_map/ppermute | solution.py:353
  363.0 19.6 %shard_map.291 = (bf16[1024,1024]{1,0:T(8,128)(2,1)S(1)}, bf16[1024,1024]{1,0:T(8,128)(2,1)S(1)}, bf16[1024,1024]{1,0:T(8,128)(2,1)}, bf16[1024,1024]{1,0:T(8,128)(2,1)}) custom-call(bf16[512,2048]{1,0:T(8,128)(2,1)} %copy-done.26, bf16[512,2048]{1,0:T(8,128)(2,1)} %pad_maximum_fusion.4.refs_1_, bf16[512,2048]{1,0:T(8,128)(2,1)} %collective-permute-done.21.refs_2_, ...), custom_call_target="tpu_custom_call" | custom-call | flops 1073741824 | bytes 3145728 | tf_op jit(solution)/shard_map/pallas_call | solution.py:202
  385.2 19.8 %shard_map.292 = (bf16[1024,1024]{1,0:T(8,128)(2,1)S(1)}, bf16[1024,1024]{1,0:T(8,128)(2,1)S(1)}, bf16[1024,1024]{1,0:T(8,128)(2,1)}, bf16[1024,1024]{1,0:T(8,128)(2,1)}) custom-call(bf16[512,2048]{1,0:T(8,128)(2,1)} %collective-permute-done.23.refs_0_.refs_4_, bf16[512,2048]{1,0:T(8,128)(2,1)} %collective-permute-done.24.refs_1_.refs_5_, ...), custom_call_target="tpu_custom_call" | custom-call | flops 1073741824 | bytes 3145728 | tf_op jit(solution)/shard_map/pallas_call | solution.py:202
  405.0 8.1 convolution_convert_fusion.5
  413.2 7.1 collective-permute-done.28
  421.4 3.7 fusion.3
  425.1 3.8 fusion.2
  428.9 4.8 convolution_convert_fusion.4
  433.9 7.0 collective-permute-done.29
  441.0 6.2 add_convert_fusion.3
  447.1 7.1 convolution_convert_fusion.3
  456.9 4.6 collective-permute-done.30
  462.6 5.9 fusion.1
  468.5 5.8 fusion
  474.3 24.5 %shard_map.293 = bf16[2048,1024]{1,0:T(8,128)(2,1)} custom-call(bf16[512,2048]{1,0:T(8,128)(2,1)} %copy-done.26, bf16[512,2048]{1,0:T(8,128)(2,1)} %pad_maximum_fusion.4.refs_1_, bf16[512,2048]{1,0:T(8,128)(2,1)} %collective-permute-done.21.refs_2_, bf16[512,2048]{1,0:T(8,128)(2,1)} %collective-permute-done.22.refs_3_, ...), custom_call_target="tpu_custom_call" | custom-call | flops 2147483648 | bytes 3670016 | tf_op jit(solution)/shard_map/pallas_call | solution.py:276
  498.8 3.8 collective-permute-done.32
  510.5 6.5 shard_map.295
  519.3 26.6 %shard_map.294 = bf16[1024,2048]{1,0:T(8,128)(2,1)} custom-call(bf16[1024,1024]{1,0:T(8,128)(2,1)} %copy-done.1, bf16[1024,1024]{1,0:T(8,128)(2,1)} %copy-done.1, bf16[1024,1024]{1,0:T(8,128)(2,1)} %copy-done.3, bf16[1024,1024]{1,0:T(8,128)(2,1)} %copy-done.3, bf16[1024,1024]{1,0:T(8,128)(2,1)} %copy-done.5, bf16[1024,1024]{1,0:T(8,128)(2,1)} %copy-done.5, ...), custom_call_target="tpu_custom_call" | custom-call | flops 2147483648 | bytes 3670016 | tf_op jit(solution)/shard_map/pallas_call | solution.py:276
  548.9 3.2 convert_add_fusion.10
  558.9 5.8 convolution_convert_fusion.6.grad_ref
  564.7 4.4 convolution_convert_fusion.1
  573.6 23.5 %collective-permute-done.36 = bf16[8,64,1024]{2,1,0:T(8,128)(2,1)} collective-permute-done((bf16[8,64,1024]{2,1,0:T(8,128)(2,1)}, bf16[8,64,1024]{2,1,0:T(8,128)(2,1)}, u32[]{:S(2)}, u32[]{:S(2)}) %collective-permute-start.36) | collective-permute-done | bytes 1048608 | tf_op jit(solution)/shard_map/ppermute | solution.py:353
  599.3 4.9 add_convert_fusion.2
  611.0 15.1 %collective-permute-done.43 = bf16[8,64,1024]{2,1,0:T(8,128)(2,1)} collective-permute-done((bf16[8,64,1024]{2,1,0:T(8,128)(2,1)S(1)}, bf16[8,64,1024]{2,1,0:T(8,128)(2,1)}, u32[]{:S(2)}, u32[]{:S(2)}) %collective-permute-start.43) | collective-permute-done | bytes 1048608 | tf_op jit(solution)/shard_map/ppermute | solution.py:353
  626.1 6.5 shard_map.297
  632.7 3.0 convert_add_fusion.8
  635.7 30.4 %shard_map.296 = (bf16[512,2048]{1,0:T(8,128)(2,1)S(1)}, bf16[2,1024,256]{2,1,0:T(8,128)(2,1)S(1)}) custom-call(s32[1]{0:T(128)} %bitcast.1.pos_ref, s32[2,8]{1,0:T(2,128)S(1)} %select_reduce_fusion.ends_ref, bf16[512,2048]{1,0:T(8,128)(2,1)} %add_convert_fusion.5.q_ref, bf16[2,1024,256]{2,1,0:T(8,128)(2,1)S(1)} %constant_dynamic-update-slice_fusion.17.kv_ref, ...), custom_call_target="tpu_custom_call" | custom-call | flops 1342177280 | bytes 1310720 | tf_op jit(solution)/shard_map/pallas_call | solution.py:152
  666.2 4.3 convolution_convert_fusion
  674.8 25.4 %collective-permute-done.63 = bf16[256,2048]{1,0:T(8,128)(2,1)} collective-permute-done((bf16[256,2048]{1,0:T(8,128)(2,1)S(1)}, bf16[256,2048]{1,0:T(8,128)(2,1)}, u32[]{:S(2)}, u32[]{:S(2)}) %collective-permute-start.63) | collective-permute-done | bytes 1048608 | tf_op jit(solution)/shard_map/ppermute | solution.py:353
  706.6 4.3 all-to-all-start.1
  711.6 20.0 %collective-permute-done.64 = bf16[256,2048]{1,0:T(8,128)(2,1)} collective-permute-done((bf16[256,2048]{1,0:T(8,128)(2,1)}, bf16[256,2048]{1,0:T(8,128)(2,1)}, u32[]{:S(2)}, u32[]{:S(2)}) %collective-permute-start.64) | collective-permute-done | bytes 1048608 | tf_op jit(solution)/shard_map/ppermute | solution.py:353
  731.5 3.2 convert_add_fusion.5
  739.1 4.6 add_convert_fusion.1
  746.6 8.7 convolution_convert_fusion.2
  755.4 6.3 fusion.50
  774.5 6.7 collective-permute-done.46
  784.2 3.6 fusion.24
  794.1 5.6 fusion.23
  808.3 14.2 %collective-permute-done.53 = bf16[128,2048]{1,0:T(8,128)(2,1)S(1)} collective-permute-done((bf16[128,2048]{1,0:T(8,128)(2,1)S(1)}, bf16[128,2048]{1,0:T(8,128)(2,1)S(1)}, u32[]{:S(2)}, u32[]{:S(2)}) %collective-permute-start.53) | collective-permute-done | bytes 524320 | tf_op jit(solution)/shard_map/ppermute | solution.py:414
  826.1 9.8 %collective-permute-done.54 = bf16[64,2048]{1,0:T(8,128)(2,1)S(1)} collective-permute-done((bf16[64,2048]{1,0:T(8,128)(2,1)S(1)}, bf16[64,2048]{1,0:T(8,128)(2,1)S(1)}, u32[]{:S(2)}, u32[]{:S(2)}) %collective-permute-start.54) | collective-permute-done | bytes 262176 | tf_op jit(solution)/shard_map/ppermute | solution.py:353
  836.1 5.5 collective-permute-done.60
  842.4 4.7 collective-permute-done.55
  848.1 7.5 add_convert_fusion
  855.7 4.0 convert_add_fusion.2
  872.6 3.4 collective-permute-done.49
  878.0 3.3 collective-permute-done.48
  (463 shorter events, 197.0 us)
Async XLA Ops:
  7.2 45.9 %all-gather.4.cloned.1.call-start = ((), (), s32[]{:S(2)}) async-start(), calls=%async_computation.4 | async-start | bytes 1638400 | tf_op jit(solution)/shard_map/all_gather | solution.py:489
  17.5 114.5 %all-gather.6.cloned.1.call-start = ((), (), s32[]{:S(2)}) async-start(), calls=%async_computation.5 | async-start | bytes 11796480 | tf_op jit(solution)/shard_map/all_gather | solution.py:496
  53.1 174.8 %all-gather.8.cloned.1.call-start = ((), (), s32[]{:S(2)}) async-start(), calls=%async_computation.6 | async-start | bytes 9437184 | tf_op jit(solution)/shard_map/all_gather | solution.py:511
  65.4 39.2 %collective-permute-start.5 = (bf16[256,2048]{1,0:T(8,128)(2,1)S(1)}, bf16[256,2048]{1,0:T(8,128)(2,1)}, u32[]{:S(2)}, u32[]{:S(2)}) collective-permute-start(bf16[256,2048]{1,0:T(8,128)(2,1)S(1)} %get-tuple-element.253), channel_id=1, source_target_pairs={{0,8},{4,12},{8,0},{12,4},{16,24},{20,28},{24,16},{28,20},{1,9},{5... | collective-permute-start | bytes 3145736 | tf_op jit(solution)/shard_map/ppermute | solution.py:414
  80.2 26.2 %collective-permute-start.3 = (bf16[256,2048]{1,0:T(8,128)(2,1)}, bf16[256,2048]{1,0:T(8,128)(2,1)}, u32[]{:S(2)}, u32[]{:S(2)}) collective-permute-start(bf16[256,2048]{1,0:T(8,128)(2,1)} %param.29), channel_id=1, source_target_pairs={{0,1},{1,2},{2,3},{3,0},{4,5},{5,6},{6,7},{7,4},{8,9},{9,10},{10,1... | collective-permute-start | bytes 3145736 | tf_op jit(solution)/shard_map/ppermute | solution.py:353
  80.2 28.6 %collective-permute-start.6 = (bf16[256,2048]{1,0:T(8,128)(2,1)}, bf16[256,2048]{1,0:T(8,128)(2,1)}, u32[]{:S(2)}, u32[]{:S(2)}) collective-permute-start(bf16[256,2048]{1,0:T(8,128)(2,1)} %get-tuple-element.252), channel_id=1, source_target_pairs={{0,16},{4,20},{8,24},{12,28},{16,0},{20,4},{24,8},{28,12},{1,17},{... | collective-permute-start | bytes 3145736 | tf_op jit(solution)/shard_map/ppermute | solution.py:414
  106.4 24.6 %collective-permute-start.4 = (bf16[256,2048]{1,0:T(8,128)(2,1)}, bf16[256,2048]{1,0:T(8,128)(2,1)}, u32[]{:S(2)}, u32[]{:S(2)}) collective-permute-start(bf16[256,2048]{1,0:T(8,128)(2,1)} %collective-permute-done.3), channel_id=1, source_target_pairs={{0,1},{1,2},{2,3},{3,0},{4,5},{5,6},{6,7},{7,4},{8,9},{9,10},{10,1... | collective-permute-start | bytes 3145736 | tf_op jit(solution)/shard_map/ppermute | solution.py:353
  146.9 10.3 %collective-permute-start.7 = (bf16[2,256,256]{2,1,0:T(8,128)(2,1)S(1)}, bf16[2,256,256]{2,1,0:T(8,128)(2,1)S(1)}, u32[]{:S(2)}, u32[]{:S(2)}) collective-permute-start(bf16[2,256,256]{2,1,0:T(8,128)(2,1)S(1)} %bitcast.262), channel_id=1, source_target_pairs={{0,1},{1,2},{2,3},{3,0},{4,5},{5,6},{6,7},{7,4},{8,9},{9,10},{10,1... | collective-permute-start | bytes 786440 | tf_op jit(solution)/shard_map/ppermute | solution.py:353
  156.6 57.2 %collective-permute-start.11 = (bf16[512,2048]{1,0:T(8,128)(2,1)S(1)}, bf16[512,2048]{1,0:T(8,128)(2,1)}, u32[]{:S(2)}, u32[]{:S(2)}) collective-permute-start(bf16[512,2048]{1,0:T(8,128)(2,1)S(1)} %pad_maximum_fusion.1.refs_0_.refs_8_), channel_id=1, source_target_pairs={{0,4},{4,0},{8,12},{12,8},{16,20},{20,16},{24,28},{28,24},{1,5},{5... | collective-permute-start | bytes 6291464 | tf_op jit(solution)/shard_map/ppermute | solution.py:414
  156.6 57.2 %collective-permute-start.12 = (bf16[512,2048]{1,0:T(8,128)(2,1)}, bf16[512,2048]{1,0:T(8,128)(2,1)}, u32[]{:S(2)}, u32[]{:S(2)}) collective-permute-start(bf16[512,2048]{1,0:T(8,128)(2,1)} %pad_maximum_fusion.2.refs_1_.refs_9_), channel_id=1, source_target_pairs={{0,4},{4,0},{8,12},{12,8},{16,20},{20,16},{24,28},{28,24},{1,5},{5... | collective-permute-start | bytes 6291464 | tf_op jit(solution)/shard_map/ppermute | solution.py:414
  157.1 11.5 %collective-permute-start.8 = (bf16[2,256,256]{2,1,0:T(8,128)(2,1)S(1)}, bf16[2,256,256]{2,1,0:T(8,128)(2,1)S(1)}, u32[]{:S(2)}, u32[]{:S(2)}) collective-permute-start(bf16[2,256,256]{2,1,0:T(8,128)(2,1)S(1)} %collective-permute-done.7), channel_id=1, source_target_pairs={{0,1},{1,2},{2,3},{3,0},{4,5},{5,6},{6,7},{7,4},{8,9},{9,10},{10,1... | collective-permute-start | bytes 786440 | tf_op jit(solution)/shard_map/ppermute | solution.py:353
  178.5 32.6 %collective-permute-start.10 = (bf16[256,2048]{1,0:T(8,128)(2,1)}, bf16[256,2048]{1,0:T(8,128)(2,1)}, u32[]{:S(2)}, u32[]{:S(2)}) collective-permute-start(bf16[256,2048]{1,0:T(8,128)(2,1)} %collective-permute-done.4), channel_id=1, source_target_pairs={{0,1},{1,2},{2,3},{3,0},{4,5},{5,6},{6,7},{7,4},{8,9},{9,10},{10,1... | collective-permute-start | bytes 3145736 | tf_op jit(solution)/shard_map/ppermute | solution.py:353
  184.5 54.7 %collective-permute-start.14 = (bf16[512,2048]{1,0:T(8,128)(2,1)S(1)}, bf16[512,2048]{1,0:T(8,128)(2,1)}, u32[]{:S(2)}, u32[]{:S(2)}) collective-permute-start(bf16[512,2048]{1,0:T(8,128)(2,1)S(1)} %pad_maximum_fusion.1.refs_0_.refs_8_), channel_id=1, source_target_pairs={{0,16},{4,20},{8,24},{12,28},{16,0},{20,4},{24,8},{28,12},{1,17},{... | collective-permute-start | bytes 6291464 | tf_op jit(solution)/shard_map/ppermute | solution.py:414
  185.7 53.5 %collective-permute-start.15 = (bf16[512,2048]{1,0:T(8,128)(2,1)}, bf16[512,2048]{1,0:T(8,128)(2,1)}, u32[]{:S(2)}, u32[]{:S(2)}) collective-permute-start(bf16[512,2048]{1,0:T(8,128)(2,1)} %pad_maximum_fusion.2.refs_1_.refs_9_), channel_id=1, source_target_pairs={{0,8},{4,12},{8,0},{12,4},{16,24},{20,28},{24,16},{28,20},{1,9},{5... | collective-permute-start | bytes 6291464 | tf_op jit(solution)/shard_map/ppermute | solution.py:414
  211.1 28.1 %collective-permute-start.13 = (bf16[8,64,1024]{2,1,0:T(8,128)(2,1)}, bf16[8,64,1024]{2,1,0:T(8,128)(2,1)}, u32[]{:S(2)}, u32[]{:S(2)}) collective-permute-start(bf16[8,64,1024]{2,1,0:T(8,128)(2,1)} %bitcast.2), channel_id=1, source_target_pairs={{0,1},{1,2},{2,3},{3,0},{4,5},{5,6},{6,7},{7,4},{8,9},{9,10},{10,1... | collective-permute-start | bytes 3145736 | tf_op jit(solution)/shard_map/ppermute | solution.py:353
  239.2 28.0 %collective-permute-start.19 = (bf16[512,2048]{1,0:T(8,128)(2,1)}, bf16[512,2048]{1,0:T(8,128)(2,1)S(1)}, u32[]{:S(2)}, u32[]{:S(2)}) collective-permute-start(bf16[512,2048]{1,0:T(8,128)(2,1)} %collective-permute-done.14.refs_0_.refs_12_), channel_id=1, source_target_pairs={{0,4},{4,0},{8,12},{12,8},{16,20},{20,16},{24,28},{28,24},{1,5},{5... | collective-permute-start | bytes 6291464 | tf_op jit(solution)/shard_map/ppermute | solution.py:414
  239.3 27.9 %collective-permute-start.20 = (bf16[512,2048]{1,0:T(8,128)(2,1)}, bf16[512,2048]{1,0:T(8,128)(2,1)S(1)}, u32[]{:S(2)}, u32[]{:S(2)}) collective-permute-start(bf16[512,2048]{1,0:T(8,128)(2,1)} %collective-permute-done.15.refs_1_.refs_13_), channel_id=1, source_target_pairs={{0,4},{4,0},{8,12},{12,8},{16,20},{20,16},{24,28},{28,24},{1,5},{5... | collective-permute-start | bytes 6291464 | tf_op jit(solution)/shard_map/ppermute | solution.py:414
  239.9 25.2 %collective-permute-start.16 = (bf16[256,2048]{1,0:T(8,128)(2,1)S(1)}, bf16[256,2048]{1,0:T(8,128)(2,1)S(1)}, u32[]{:S(2)}, u32[]{:S(2)}) collective-permute-start(bf16[256,2048]{1,0:T(8,128)(2,1)S(1)} %get-tuple-element.251), channel_id=1, source_target_pairs={{0,8},{4,12},{8,0},{12,4},{16,24},{20,28},{24,16},{28,20},{1,9},{5... | collective-permute-start | bytes 3145736 | tf_op jit(solution)/shard_map/ppermute | solution.py:414
  240.5 24.9 %collective-permute-start.17 = (bf16[256,2048]{1,0:T(8,128)(2,1)S(1)}, bf16[256,2048]{1,0:T(8,128)(2,1)S(1)}, u32[]{:S(2)}, u32[]{:S(2)}) collective-permute-start(bf16[256,2048]{1,0:T(8,128)(2,1)S(1)} %get-tuple-element.250), channel_id=1, source_target_pairs={{0,16},{4,20},{8,24},{12,28},{16,0},{20,4},{24,8},{28,12},{1,17},{... | collective-permute-start | bytes 3145736 | tf_op jit(solution)/shard_map/ppermute | solution.py:414
  241.2 43.2 %collective-permute-start.18 = (bf16[8,64,1024]{2,1,0:T(8,128)(2,1)}, bf16[8,64,1024]{2,1,0:T(8,128)(2,1)}, u32[]{:S(2)}, u32[]{:S(2)}) collective-permute-start(bf16[8,64,1024]{2,1,0:T(8,128)(2,1)} %collective-permute-done.13), channel_id=1, source_target_pairs={{0,1},{1,2},{2,3},{3,0},{4,5},{5,6},{6,7},{7,4},{8,9},{9,10},{10,1... | collective-permute-start | bytes 3145736 | tf_op jit(solution)/shard_map/ppermute | solution.py:353
  284.4 46.8 %collective-permute-start.23 = (bf16[512,2048]{1,0:T(8,128)(2,1)S(1)}, bf16[512,2048]{1,0:T(8,128)(2,1)}, u32[]{:S(2)}, u32[]{:S(2)}) collective-permute-start(bf16[512,2048]{1,0:T(8,128)(2,1)S(1)} %pad_maximum_fusion.3.refs_0_), channel_id=1, source_target_pairs={{0,16},{4,20},{8,24},{12,28},{16,0},{20,4},{24,8},{28,12},{1,17},{... | collective-permute-start | bytes 6291464 | tf_op jit(solution)/shard_map/ppermute | solution.py:414
  285.1 46.7 %collective-permute-start.24 = (bf16[512,2048]{1,0:T(8,128)(2,1)}, bf16[512,2048]{1,0:T(8,128)(2,1)}, u32[]{:S(2)}, u32[]{:S(2)}) collective-permute-start(bf16[512,2048]{1,0:T(8,128)(2,1)} %pad_maximum_fusion.4.refs_1_), channel_id=1, source_target_pairs={{0,8},{4,12},{8,0},{12,4},{16,24},{20,28},{24,16},{28,20},{1,9},{5... | collective-permute-start | bytes 6291464 | tf_op jit(solution)/shard_map/ppermute | solution.py:414
  286.3 74.7 %collective-permute-start.21 = (bf16[512,2048]{1,0:T(8,128)(2,1)S(1)}, bf16[512,2048]{1,0:T(8,128)(2,1)}, u32[]{:S(2)}, u32[]{:S(2)}) collective-permute-start(bf16[512,2048]{1,0:T(8,128)(2,1)S(1)} %pad_maximum_fusion.3.refs_0_), channel_id=1, source_target_pairs={{0,4},{4,0},{8,12},{12,8},{16,20},{20,16},{24,28},{28,24},{1,5},{5... | collective-permute-start | bytes 6291464 | tf_op jit(solution)/shard_map/ppermute | solution.py:414
  286.3 74.7 %collective-permute-start.22 = (bf16[512,2048]{1,0:T(8,128)(2,1)}, bf16[512,2048]{1,0:T(8,128)(2,1)}, u32[]{:S(2)}, u32[]{:S(2)}) collective-permute-start(bf16[512,2048]{1,0:T(8,128)(2,1)} %pad_maximum_fusion.4.refs_1_), channel_id=1, source_target_pairs={{0,4},{4,0},{8,12},{12,8},{16,20},{20,16},{24,28},{28,24},{1,5},{5... | collective-permute-start | bytes 6291464 | tf_op jit(solution)/shard_map/ppermute | solution.py:414
  331.3 53.9 %collective-permute-start.25 = (bf16[512,2048]{1,0:T(8,128)(2,1)}, bf16[512,2048]{1,0:T(8,128)(2,1)}, u32[]{:S(2)}, u32[]{:S(2)}) collective-permute-start(bf16[512,2048]{1,0:T(8,128)(2,1)} %collective-permute-done.23.refs_0_.refs_4_), channel_id=1, source_target_pairs={{0,4},{4,0},{8,12},{12,8},{16,20},{20,16},{24,28},{28,24},{1,5},{5... | collective-permute-start | bytes 6291464 | tf_op jit(solution)/shard_map/ppermute | solution.py:414
  331.8 53.4 %collective-permute-start.26 = (bf16[512,2048]{1,0:T(8,128)(2,1)}, bf16[512,2048]{1,0:T(8,128)(2,1)}, u32[]{:S(2)}, u32[]{:S(2)}) collective-permute-start(bf16[512,2048]{1,0:T(8,128)(2,1)} %collective-permute-done.24.refs_1_.refs_5_), channel_id=1, source_target_pairs={{0,4},{4,0},{8,12},{12,8},{16,20},{20,16},{24,28},{28,24},{1,5},{5... | collective-permute-start | bytes 6291464 | tf_op jit(solution)/shard_map/ppermute | solution.py:414
  331.8 27.8 %collective-permute-start.27 = (bf16[8,64,1024]{2,1,0:T(8,128)(2,1)}, bf16[8,64,1024]{2,1,0:T(8,128)(2,1)}, u32[]{:S(2)}, u32[]{:S(2)}) collective-permute-start(bf16[8,64,1024]{2,1,0:T(8,128)(2,1)} %collective-permute-done.18), channel_id=1, source_target_pairs={{0,1},{1,2},{2,3},{3,0},{4,5},{5,6},{6,7},{7,4},{8,9},{9,10},{10,1... | collective-permute-start | bytes 3145736 | tf_op jit(solution)/shard_map/ppermute | solution.py:353
  454.5 48.1 %collective-permute-start.32 = (bf16[512,2048]{1,0:T(8,128)(2,1)}, bf16[512,2048]{1,0:T(8,128)(2,1)S(1)}, u32[]{:S(2)}, u32[]{:S(2)}) collective-permute-start(bf16[512,2048]{1,0:T(8,128)(2,1)} %fusion.3), channel_id=1, source_target_pairs={{0,16},{4,20},{8,24},{12,28},{16,0},{20,4},{24,8},{28,12},{1,17},{... | collective-permute-start | bytes 6291464 | tf_op jit(solution)/shard_map/ppermute | solution.py:414
  455.9 47.8 %collective-permute-start.33 = (bf16[512,2048]{1,0:T(8,128)(2,1)}, bf16[512,2048]{1,0:T(8,128)(2,1)S(1)}, u32[]{:S(2)}, u32[]{:S(2)}) collective-permute-start(bf16[512,2048]{1,0:T(8,128)(2,1)} %fusion.2), channel_id=1, source_target_pairs={{0,8},{4,12},{8,0},{12,4},{16,24},{20,28},{24,16},{28,20},{1,9},{5... | collective-permute-start | bytes 6291464 | tf_op jit(solution)/shard_map/ppermute | solution.py:414
  506.8 39.1 %collective-permute-start.35 = (bf16[256,2048]{1,0:T(8,128)(2,1)}, bf16[256,2048]{1,0:T(8,128)(2,1)S(1)}, u32[]{:S(2)}, u32[]{:S(2)}) collective-permute-start(bf16[256,2048]{1,0:T(8,128)(2,1)} %slice.380), channel_id=1, source_target_pairs={{0,16},{4,20},{8,24},{12,28},{16,0},{20,4},{24,8},{28,12},{1,17},{... | collective-permute-start | bytes 3145736 | tf_op jit(solution)/shard_map/ppermute | solution.py:414
  509.5 36.8 %collective-permute-start.34 = (bf16[256,2048]{1,0:T(8,128)(2,1)}, bf16[256,2048]{1,0:T(8,128)(2,1)S(1)}, u32[]{:S(2)}, u32[]{:S(2)}) collective-permute-start(bf16[256,2048]{1,0:T(8,128)(2,1)} %slice.381), channel_id=1, source_target_pairs={{0,8},{4,12},{8,0},{12,4},{16,24},{20,28},{24,16},{28,20},{1,9},{5... | collective-permute-start | bytes 3145736 | tf_op jit(solution)/shard_map/ppermute | solution.py:414
  519.3 29.6 %collective-permute-start.31 = (bf16[8,64,1024]{2,1,0:T(8,128)(2,1)}, bf16[8,64,1024]{2,1,0:T(8,128)(2,1)}, u32[]{:S(2)}, u32[]{:S(2)}) collective-permute-start(bf16[8,64,1024]{2,1,0:T(8,128)(2,1)} %dynamic-slice_bitcast_fusion.1), channel_id=1, source_target_pairs={{0,1},{1,2},{2,3},{3,0},{4,5},{5,6},{6,7},{7,4},{8,9},{9,10},{10,1... | collective-permute-start | bytes 3145736 | tf_op jit(solution)/shard_map/ppermute | solution.py:353
  569.1 30.2 %collective-permute-start.37 = (bf16[1024,2048]{1,0:T(8,128)(2,1)}, bf16[1024,2048]{1,0:T(8,128)(2,1)}, u32[]{:S(2)}, u32[]{:S(2)}) collective-permute-start(bf16[1024,2048]{1,0:T(8,128)(2,1)} %convolution_convert_fusion.1), channel_id=1, source_target_pairs={{0,4},{4,0},{8,12},{12,8},{16,20},{20,16},{24,28},{28,24},{1,5},{5... | collective-permute-start | bytes 12582920 | tf_op jit(solution)/shard_map/ppermute | solution.py:414
  569.1 28.0 %collective-permute-start.36 = (bf16[8,64,1024]{2,1,0:T(8,128)(2,1)}, bf16[8,64,1024]{2,1,0:T(8,128)(2,1)}, u32[]{:S(2)}, u32[]{:S(2)}) collective-permute-start(bf16[8,64,1024]{2,1,0:T(8,128)(2,1)} %convert_add_fusion.10), channel_id=1, source_target_pairs={{0,1},{1,2},{2,3},{3,0},{4,5},{5,6},{6,7},{7,4},{8,9},{9,10},{10,1... | collective-permute-start | bytes 3145736 | tf_op jit(solution)/shard_map/ppermute | solution.py:353
  571.0 95.1 %collective-permute-start.38 = (bf16[512,2048]{1,0:T(8,128)(2,1)}, bf16[512,2048]{1,0:T(8,128)(2,1)}, u32[]{:S(2)}, u32[]{:S(2)}) collective-permute-start(bf16[512,2048]{1,0:T(8,128)(2,1)} %fusion.1), channel_id=1, source_target_pairs={{0,16},{4,20},{8,24},{12,28},{16,0},{20,4},{24,8},{28,12},{1,17},{... | collective-permute-start | bytes 6291464 | tf_op jit(solution)/shard_map/ppermute | solution.py:414
  572.6 93.5 %collective-permute-start.39 = (bf16[512,2048]{1,0:T(8,128)(2,1)}, bf16[512,2048]{1,0:T(8,128)(2,1)}, u32[]{:S(2)}, u32[]{:S(2)}) collective-permute-start(bf16[512,2048]{1,0:T(8,128)(2,1)} %fusion), channel_id=1, source_target_pairs={{0,8},{4,12},{8,0},{12,4},{16,24},{20,28},{24,16},{28,20},{1,9},{5... | collective-permute-start | bytes 6291464 | tf_op jit(solution)/shard_map/ppermute | solution.py:414
  599.0 27.1 %collective-permute-start.43 = (bf16[8,64,1024]{2,1,0:T(8,128)(2,1)S(1)}, bf16[8,64,1024]{2,1,0:T(8,128)(2,1)}, u32[]{:S(2)}, u32[]{:S(2)}) collective-permute-start(bf16[8,64,1024]{2,1,0:T(8,128)(2,1)S(1)} %convert_add_fusion.9), channel_id=1, source_target_pairs={{0,1},{1,2},{2,3},{3,0},{4,5},{5,6},{6,7},{7,4},{8,9},{9,10},{10,1... | collective-permute-start | bytes 3145736 | tf_op jit(solution)/shard_map/ppermute | solution.py:353
  606.4 59.8 %collective-permute-start.40 = (bf16[256,2048]{1,0:T(8,128)(2,1)}, bf16[256,2048]{1,0:T(8,128)(2,1)}, u32[]{:S(2)}, u32[]{:S(2)}) collective-permute-start(bf16[256,2048]{1,0:T(8,128)(2,1)} %get-tuple-element.196), channel_id=1, source_target_pairs={{0,16},{4,20},{8,24},{12,28},{16,0},{20,4},{24,8},{28,12},{1,17},{... | collective-permute-start | bytes 3145736 | tf_op jit(solution)/shard_map/ppermute | solution.py:414
  607.7 58.4 %collective-permute-start.41 = (bf16[256,2048]{1,0:T(8,128)(2,1)}, bf16[256,2048]{1,0:T(8,128)(2,1)}, u32[]{:S(2)}, u32[]{:S(2)}) collective-permute-start(bf16[256,2048]{1,0:T(8,128)(2,1)} %get-tuple-element.197), channel_id=1, source_target_pairs={{0,8},{4,12},{8,0},{12,4},{16,24},{20,28},{24,16},{28,20},{1,9},{5... | collective-permute-start | bytes 3145736 | tf_op jit(solution)/shard_map/ppermute | solution.py:414
  626.1 44.4 %collective-permute-start.62 = (bf16[256,2048]{1,0:T(8,128)(2,1)}, bf16[256,2048]{1,0:T(8,128)(2,1)}, u32[]{:S(2)}, u32[]{:S(2)}) collective-permute-start(bf16[256,2048]{1,0:T(8,128)(2,1)} %dynamic-slice_bitcast_fusion), channel_id=1, source_target_pairs={{0,1},{1,2},{2,3},{3,0},{4,5},{5,6},{6,7},{7,4},{8,9},{9,10},{10,1... | collective-permute-start | bytes 3145736 | tf_op jit(solution)/shard_map/ppermute | solution.py:353
  670.5 68.6 %collective-permute-start.44 = (bf16[1024,2048]{1,0:T(8,128)(2,1)}, bf16[1024,2048]{1,0:T(8,128)(2,1)}, u32[]{:S(2)}, u32[]{:S(2)}) collective-permute-start(bf16[1024,2048]{1,0:T(8,128)(2,1)} %convolution_convert_fusion), channel_id=1, source_target_pairs={{0,4},{4,0},{8,12},{12,8},{16,20},{20,16},{24,28},{28,24},{1,5},{5... | collective-permute-start | bytes 12582920 | tf_op jit(solution)/shard_map/ppermute | solution.py:414
  672.5 27.8 %collective-permute-start.63 = (bf16[256,2048]{1,0:T(8,128)(2,1)S(1)}, bf16[256,2048]{1,0:T(8,128)(2,1)}, u32[]{:S(2)}, u32[]{:S(2)}) collective-permute-start(bf16[256,2048]{1,0:T(8,128)(2,1)S(1)} %fusion.28), channel_id=1, source_target_pairs={{0,1},{1,2},{2,3},{3,0},{4,5},{5,6},{6,7},{7,4},{8,9},{9,10},{10,1... | collective-permute-start | bytes 3145736 | tf_op jit(solution)/shard_map/ppermute | solution.py:353
  703.2 28.3 %collective-permute-start.64 = (bf16[256,2048]{1,0:T(8,128)(2,1)}, bf16[256,2048]{1,0:T(8,128)(2,1)}, u32[]{:S(2)}, u32[]{:S(2)}) collective-permute-start(bf16[256,2048]{1,0:T(8,128)(2,1)} %fusion.27), channel_id=1, source_target_pairs={{0,1},{1,2},{2,3},{3,0},{4,5},{5,6},{6,7},{7,4},{8,9},{9,10},{10,1... | collective-permute-start | bytes 3145736 | tf_op jit(solution)/shard_map/ppermute | solution.py:353
  706.6 29.5 %all-to-all-start.1 = ((bf16[8,64,1024]{2,1,0:T(8,128)(2,1)}), bf16[8,64,1024]{2,1,0:T(8,128)(2,1)}, u32[]{:S(2)}, u32[]{:S(2)}) async-start(bf16[8,64,1024]{2,1,0:T(8,128)(2,1)} %convert_add_fusion.8), calls=%async_computation.3 | async-start | bytes 2097152 | tf_op jit(solution)/shard_map/all_to_all | solution.py:663
  710.9 137.2 %reduce-scatter.3.cloned.1.call-start = ((), (), s32[]{:S(2)}) async-start(), calls=%async_computation.7 | async-start | bytes 2359296 | tf_op jit(solution)/shard_map/reduce_scatter | solution.py:348
  711.2 24.8 %collective-permute-start.42 = (bf16[2,256,256]{2,1,0:T(8,128)(2,1)S(1)}, bf16[2,256,256]{2,1,0:T(8,128)(2,1)S(1)}, u32[]{:S(2)}, u32[]{:S(2)}) collective-permute-start(bf16[2,256,256]{2,1,0:T(8,128)(2,1)S(1)} %dynamic-slice_bitcast_fusion.2), channel_id=1, source_target_pairs={{0,1},{1,2},{2,3},{3,0},{4,5},{5,6},{6,7},{7,4},{8,9},{9,10},{10,1... | collective-permute-start | bytes 786440 | tf_op jit(solution)/shard_map/ppermute | solution.py:353
  755.3 92.8 %collective-permute-start.47 = (bf16[1024,2048]{1,0:T(8,128)(2,1)}, bf16[1024,2048]{1,0:T(8,128)(2,1)}, u32[]{:S(2)}, u32[]{:S(2)}) collective-permute-start(bf16[1024,2048]{1,0:T(8,128)(2,1)} %convolution_convert_fusion.2), channel_id=1, source_target_pairs={{0,4},{4,0},{8,12},{12,8},{16,20},{20,16},{24,28},{28,24},{1,5},{5... | collective-permute-start | bytes 12582920 | tf_op jit(solution)/shard_map/ppermute | solution.py:414
  755.3 14.9 %collective-permute-start.45 = (bf16[2,256,256]{2,1,0:T(8,128)(2,1)S(1)}, bf16[2,256,256]{2,1,0:T(8,128)(2,1)}, u32[]{:S(2)}, u32[]{:S(2)}) collective-permute-start(bf16[2,256,256]{2,1,0:T(8,128)(2,1)S(1)} %convert_add_fusion.17), channel_id=1, source_target_pairs={{0,1},{1,2},{2,3},{3,0},{4,5},{5,6},{6,7},{7,4},{8,9},{9,10},{10,1... | collective-permute-start | bytes 786440 | tf_op jit(solution)/shard_map/ppermute | solution.py:353
  761.6 40.8 %collective-permute-start.52 = (bf16[256,2048]{1,0:T(8,128)(2,1)}, bf16[256,2048]{1,0:T(8,128)(2,1)}, u32[]{:S(2)}, u32[]{:S(2)}) collective-permute-start(bf16[256,2048]{1,0:T(8,128)(2,1)} %get-tuple-element.219), channel_id=1, source_target_pairs={{0,8},{4,12},{8,0},{12,4},{16,24},{20,28},{24,16},{28,20},{1,9},{5... | collective-permute-start | bytes 3145736 | tf_op jit(solution)/shard_map/ppermute | solution.py:414
  762.6 42.9 %collective-permute-start.50 = (bf16[256,2048]{1,0:T(8,128)(2,1)}, bf16[256,2048]{1,0:T(8,128)(2,1)}, u32[]{:S(2)}, u32[]{:S(2)}) collective-permute-start(bf16[256,2048]{1,0:T(8,128)(2,1)} %get-tuple-element.217), channel_id=1, source_target_pairs={{0,16},{4,20},{8,24},{12,28},{16,0},{20,4},{24,8},{28,12},{1,17},{... | collective-permute-start | bytes 3145736 | tf_op jit(solution)/shard_map/ppermute | solution.py:414
  768.7 31.0 %collective-permute-start.58 = (bf16[128,2048]{1,0:T(8,128)(2,1)}, bf16[128,2048]{1,0:T(8,128)(2,1)}, u32[]{:S(2)}, u32[]{:S(2)}) collective-permute-start(bf16[128,2048]{1,0:T(8,128)(2,1)} %slice.382), channel_id=1, source_target_pairs={{0,16},{4,20},{8,24},{12,28},{16,0},{20,4},{24,8},{28,12},{1,17},{... | collective-permute-start | bytes 1572872 | tf_op jit(solution)/shard_map/ppermute | solution.py:414
  771.2 10.0 %collective-permute-start.46 = (bf16[2,256,256]{2,1,0:T(8,128)(2,1)S(1)}, bf16[2,256,256]{2,1,0:T(8,128)(2,1)S(1)}, u32[]{:S(2)}, u32[]{:S(2)}) collective-permute-start(bf16[2,256,256]{2,1,0:T(8,128)(2,1)S(1)} %fusion.34), channel_id=1, source_target_pairs={{0,1},{1,2},{2,3},{3,0},{4,5},{5,6},{6,7},{7,4},{8,9},{9,10},{10,1... | collective-permute-start | bytes 786440 | tf_op jit(solution)/shard_map/ppermute | solution.py:353
  781.2 19.8 %collective-permute-start.57 = (bf16[128,2048]{1,0:T(8,128)(2,1)}, bf16[128,2048]{1,0:T(8,128)(2,1)}, u32[]{:S(2)}, u32[]{:S(2)}) collective-permute-start(bf16[128,2048]{1,0:T(8,128)(2,1)} %slice.383), channel_id=1, source_target_pairs={{0,8},{4,12},{8,0},{12,4},{16,24},{20,28},{24,16},{28,20},{1,9},{5... | collective-permute-start | bytes 1572872 | tf_op jit(solution)/shard_map/ppermute | solution.py:414
  794.0 74.6 %reduce-scatter.5.cloned.1.call-start = ((), (), s32[]{:S(2)}) async-start(), calls=%async_computation.8 | async-start | bytes 327680 | tf_op jit(solution)/shard_map/reduce_scatter | solution.py:349
  805.0 17.5 %collective-permute-start.53 = (bf16[128,2048]{1,0:T(8,128)(2,1)S(1)}, bf16[128,2048]{1,0:T(8,128)(2,1)S(1)}, u32[]{:S(2)}, u32[]{:S(2)}) collective-permute-start(bf16[128,2048]{1,0:T(8,128)(2,1)S(1)} %slice.384), channel_id=1, source_target_pairs={{0,16},{4,20},{8,24},{12,28},{16,0},{20,4},{24,8},{28,12},{1,17},{... | collective-permute-start | bytes 1572872 | tf_op jit(solution)/shard_map/ppermute | solution.py:414
  807.1 18.4 %collective-permute-start.51 = (bf16[128,2048]{1,0:T(8,128)(2,1)S(1)}, bf16[128,2048]{1,0:T(8,128)(2,1)S(1)}, u32[]{:S(2)}, u32[]{:S(2)}) collective-permute-start(bf16[128,2048]{1,0:T(8,128)(2,1)S(1)} %slice.385), channel_id=1, source_target_pairs={{0,8},{4,12},{8,0},{12,4},{16,24},{20,28},{24,16},{28,20},{1,9},{5... | collective-permute-start | bytes 1572872 | tf_op jit(solution)/shard_map/ppermute | solution.py:414
  808.2 17.8 %collective-permute-start.59 = (bf16[64,2048]{1,0:T(8,128)(2,1)S(1)}, bf16[64,2048]{1,0:T(8,128)(2,1)S(1)}, u32[]{:S(2)}, u32[]{:S(2)}) collective-permute-start(bf16[64,2048]{1,0:T(8,128)(2,1)S(1)} %fusion.40), channel_id=1, source_target_pairs={{0,1},{1,2},{2,3},{3,0},{4,5},{5,6},{6,7},{7,4},{8,9},{9,10},{10,1... | collective-permute-start | bytes 786440 | tf_op jit(solution)/shard_map/ppermute | solution.py:353
  825.9 10.0 %collective-permute-start.54 = (bf16[64,2048]{1,0:T(8,128)(2,1)S(1)}, bf16[64,2048]{1,0:T(8,128)(2,1)S(1)}, u32[]{:S(2)}, u32[]{:S(2)}) collective-permute-start(bf16[64,2048]{1,0:T(8,128)(2,1)S(1)} %fusion.39), channel_id=1, source_target_pairs={{0,1},{1,2},{2,3},{3,0},{4,5},{5,6},{6,7},{7,4},{8,9},{9,10},{10,1... | collective-permute-start | bytes 786440 | tf_op jit(solution)/shard_map/ppermute | solution.py:353
  826.1 15.5 %collective-permute-start.60 = (bf16[64,2048]{1,0:T(8,128)(2,1)S(1)}, bf16[64,2048]{1,0:T(8,128)(2,1)S(1)}, u32[]{:S(2)}, u32[]{:S(2)}) collective-permute-start(bf16[64,2048]{1,0:T(8,128)(2,1)S(1)} %fusion.36), channel_id=1, source_target_pairs={{0,1},{1,2},{2,3},{3,0},{4,5},{5,6},{6,7},{7,4},{8,9},{9,10},{10,1... | collective-permute-start | bytes 786440 | tf_op jit(solution)/shard_map/ppermute | solution.py:353
  836.0 11.0 %collective-permute-start.55 = (bf16[64,2048]{1,0:T(8,128)(2,1)S(1)}, bf16[64,2048]{1,0:T(8,128)(2,1)S(1)}, u32[]{:S(2)}, u32[]{:S(2)}) collective-permute-start(bf16[64,2048]{1,0:T(8,128)(2,1)S(1)} %fusion.38), channel_id=1, source_target_pairs={{0,1},{1,2},{2,3},{3,0},{4,5},{5,6},{6,7},{7,4},{8,9},{9,10},{10,1... | collective-permute-start | bytes 786440 | tf_op jit(solution)/shard_map/ppermute | solution.py:353
  842.4 19.3 %collective-permute-start.61 = (bf16[64,2048]{1,0:T(8,128)(2,1)}, bf16[64,2048]{1,0:T(8,128)(2,1)}, u32[]{:S(2)}, u32[]{:S(2)}) collective-permute-start(bf16[64,2048]{1,0:T(8,128)(2,1)} %fusion.35), channel_id=1, source_target_pairs={{0,1},{1,2},{2,3},{3,0},{4,5},{5,6},{6,7},{7,4},{8,9},{9,10},{10,1... | collective-permute-start | bytes 786440 | tf_op jit(solution)/shard_map/ppermute | solution.py:353
  847.8 18.0 %collective-permute-start.56 = (bf16[64,2048]{1,0:T(8,128)(2,1)}, bf16[64,2048]{1,0:T(8,128)(2,1)S(1)}, u32[]{:S(2)}, u32[]{:S(2)}) collective-permute-start(bf16[64,2048]{1,0:T(8,128)(2,1)} %fusion.37), channel_id=1, source_target_pairs={{0,1},{1,2},{2,3},{3,0},{4,5},{5,6},{6,7},{7,4},{8,9},{9,10},{10,1... | collective-permute-start | bytes 786440 | tf_op jit(solution)/shard_map/ppermute | solution.py:353
  859.8 16.2 %collective-permute-start.49 = (bf16[256,2048]{1,0:T(8,128)(2,1)S(1)}, bf16[256,2048]{1,0:T(8,128)(2,1)S(1)}, u32[]{:S(2)}, u32[]{:S(2)}) collective-permute-start(bf16[256,2048]{1,0:T(8,128)(2,1)S(1)} %slice.378), channel_id=1, source_target_pairs={{0,16},{4,20},{8,24},{12,28},{16,0},{20,4},{24,8},{28,12},{1,17},{... | collective-permute-start | bytes 3145736 | tf_op jit(solution)/shard_map/ppermute | solution.py:414
  865.3 15.9 %collective-permute-start.48 = (bf16[256,2048]{1,0:T(8,128)(2,1)}, bf16[256,2048]{1,0:T(8,128)(2,1)S(1)}, u32[]{:S(2)}, u32[]{:S(2)}) collective-permute-start(bf16[256,2048]{1,0:T(8,128)(2,1)} %slice.379), channel_id=1, source_target_pairs={{0,8},{4,12},{8,0},{12,4},{16,24},{20,28},{24,16},{28,20},{1,9},{5... | collective-permute-start | bytes 3145736 | tf_op jit(solution)/shard_map/ppermute | solution.py:414
  (86 other events, 1175.7 us)
Sparse Core Ops, SparseCore 0:
  17.7 35.3 all-gather.3
  55.0 77.0 all-gather.5
  134.5 56.8 all-gather.7
  794.1 43.4 reduce-scatter.2
  848.2 20.3 reduce-scatter.4

commit v5 on v4

--- a/solution.py
+++ b/solution.py
@@ -336,57 +336,63 @@
     return recip * (scaled - mean_one - xhat * mean_two)
 
 
-def gelu_tanh(values):
-    return jax.nn.gelu(values, approximate=True)
-
-
 def tie(*arrays):
     return lax.optimization_barrier(arrays)
 
 
-def scatter_both(block):
-    part = lax.psum_scatter(block, "dp", scatter_dimension=0, tiled=True)
-    return lax.psum_scatter(part, "fsdp", scatter_dimension=0, tiled=True)
-
-
-def shift(block, count):
-    return lax.ppermute(block, "fsdp", [(i, (i + 1) % count) for i in range(count)])
-
-
-def put_in_order(pieces, count, axis=0):
-    me = lax.axis_index("fsdp")
-    size = pieces[0].shape[axis]
-    shape = list(pieces[0].shape)
-    shape[axis] = size * count
-    whole = jnp.zeros(shape, pieces[0].dtype)
-    for step, piece in enumerate(pieces):
-        place = lax.rem(me - step + count, count) * size
-        whole = lax.dynamic_update_slice_in_dim(whole, piece, place, axis)
-    return whole
-
-
-class Ring:
-    def __init__(self, terms, axis, count):
-        self.terms, self.axis, self.count, self.step = terms, axis, count, 0
-        self.total = self.term()
-
-    def term(self):
-        place = lax.rem(lax.axis_index("fsdp") - 1 - self.step + 2 * self.count, self.count)
-        return lax.dynamic_index_in_dim(self.terms, place, self.axis, keepdims=False).astype(F32)
-
-    def go(self, steps, ahead):
-        for _ in range(steps):
-            if self.step + 1 < self.count:
-                self.step += 1
-                self.total = shift(self.total.astype(BF16), self.count).astype(F32) + self.term()
-        self.total, ahead = tie(self.total, ahead)
-        return ahead
-
-    def finish(self):
-        while self.step + 1 < self.count:
-            self.step += 1
-            self.total = shift(self.total.astype(BF16), self.count).astype(F32) + self.term()
-        return self.total
+class Line:
+    def __init__(self, count):
+        self.count = count
+
+    def send(self, block, places):
+        return lax.ppermute(block, "fsdp", [(i, (i + places) % self.count) for i in range(self.count)])
+
+    def gather(self, block):
+        return [block] + [self.send(block, step) for step in range(1, self.count)]
+
+    def more(self, pieces, steps, block):
+        for step in steps:
+            pieces[step] = self.send(block, step)
+
+    def in_order(self, pieces, axis=0):
+        me = lax.axis_index("fsdp")
+        size = pieces[0].shape[axis]
+        shape = list(pieces[0].shape)
+        shape[axis] = size * self.count
+        whole = jnp.zeros(shape, pieces[0].dtype)
+        for step, piece in enumerate(pieces):
+            place = lax.rem(me - step + self.count, self.count) * size
+            whole = lax.dynamic_update_slice_in_dim(whole, piece, place, axis)
+        return whole
+
+    def scatter(self, terms, axis):
+        me = lax.axis_index("fsdp")
+
+        def term(step):
+            place = lax.rem(me + step, self.count)
+            return lax.dynamic_index_in_dim(terms, place, axis, keepdims=False)
+
+        return [term(0)] + [self.send(term(step).astype(BF16), step) for step in range(1, self.count)]
+
+
+def thirds(count):
+    steps = sorted(range(1, count), key=lambda step: min(step, count - step))
+    lot = -(-len(steps) // 3)
+    return steps[:lot], steps[lot : 2 * lot], steps[2 * lot :]
+
+
+def meet(pieces, steps, *arrays):
+    out = tie(*arrays, *[pieces[step] for step in steps])
+    for step, piece in zip(steps, out[len(arrays) :]):
+        pieces[step] = piece
+    return out[: len(arrays)]
+
+
+def total(terms):
+    out = terms[0].astype(F32)
+    for term in terms[1:]:
+        out += term.astype(F32)
+    return out
 
 
 class Plane:
@@ -394,7 +400,7 @@
         self.count = count
         bits = [1 << i for i in range(1, count.bit_length() - 1)]
         self.orders = (bits, bits[::-1])
-        self.steps = len(bits)
+        self.last = len(bits) - 1
         self.near, self.far = [], []
         for order in self.orders:
             near = [0]
@@ -413,24 +419,30 @@
     def swap(self, block, bit):
         return lax.ppermute(block, "dp", [(i, i ^ bit) for i in range(self.count)])
 
+    def cross(self, blocks):
+        return [self.swap(block, 1) for block in blocks]
+
     def across(self, halves, step):
         return [self.swap(half, order[step]) for half, order in zip(halves, self.orders)]
 
-    def grow(self, halves, step):
-        return [jnp.concatenate(pair) for pair in zip(halves, self.across(halves, step))]
-
-    def cross(self, halves):
-        return [self.swap(half, 1) for half in halves]
-
-    def fold(self, halves, step):
-        size = halves[0].shape[0] // 2
-        got = self.across([half[size:].astype(BF16) for half in halves], step)
-        return [half[:size].astype(F32) + there.astype(F32) for half, there in zip(halves, got)]
+    def grow(self, halves):
+        for step in range(self.last):
+            halves = [jnp.concatenate(pair) for pair in zip(halves, self.across(halves, step))]
+        return halves
+
+    def fold(self, halves):
+        for step in range(self.last - 1, -1, -1):
+            size = halves[0].shape[0] // 2
+            got = self.across([half[size:].astype(BF16) for half in halves], step)
+            halves = [half[:size].astype(F32) + there.astype(F32) for half, there in zip(halves, got)]
+        return jnp.concatenate(halves)
 
 
 def make_local(n_dp, n_z):
     n_dev = n_dp * n_z
     plane = Plane(n_dp)
+    line = Line(n_z)
+    soon, later, last = thirds(n_z)
 
     def local(
         tokens,
@@ -453,6 +465,7 @@
     ):
         windows, local_len, width = tokens.shape
         rows = windows * local_len
+        half = rows // 2
         own = query_weight.shape[0]
         ff_own = up_weight.shape[1] // n_dp
         my_dp = lax.axis_index("dp")
@@ -483,33 +496,26 @@
             [query_weight, kv_weight.reshape(kv_lines, width), small_row.reshape(-1, width)]
         )
 
-        half = rows // 2
         grad_low = cotangent.reshape(rows, width)
-
         packed = lax.all_gather(packed, "fsdp", axis=0, tiled=True)
-        grad_near = [grad_low[:half], grad_low[half:]]
-        for step in range(plane.steps - 1):
-            grad_near = plane.grow(grad_near, step)
+        grad_near = plane.grow([grad_low[:half], grad_low[half:]])
         up_cols = lax.all_to_all(up_weight, "dp", 1, 0, tiled=True).reshape(n_dp, own, ff_own)
-        packed, up_cols, down_weight, out_weight = tie(packed, up_cols, down_weight, out_weight)
+        packed, up_cols, out_weight, *grad_near = tie(packed, up_cols, out_weight, *grad_near)
 
         packed = lax.all_gather(packed, "dp", axis=0, tiled=True)
-        out_pieces = [out_weight]
-        while len(out_pieces) < n_z:
-            out_pieces.append(shift(out_pieces[-1], n_z))
-        out_pieces[-1], down_weight = tie(out_pieces[-1], down_weight)
-        full_o = put_in_order(out_pieces, n_z)
-        down_pieces = [down_weight]
-        while len(down_pieces) < min(3, n_z):
-            down_pieces.append(shift(down_pieces[-1], n_z))
+        out_pieces = line.gather(out_weight)
+        *out_pieces, down_late = tie(*out_pieces, down_weight)
+        full_o = line.in_order(out_pieces)
+        down_pieces = [down_weight] + [None] * (n_z - 1)
+        line.more(down_pieces, last, down_late)
         inputs = tokens.reshape(rows, width).astype(F32)
         mean_one, recip_one = norm_stats(inputs)
-        packed, full_o, down_pieces[-1], mean_one, *grad_near = tie(
-            packed, full_o, down_pieces[-1], mean_one, *grad_near
+        packed, full_o, mean_one, grad_near[0], grad_near[1] = meet(
+            down_pieces, last, packed, full_o, mean_one, *grad_near
         )
 
         full_o = lax.all_gather(full_o, "dp", axis=0, tiled=True)
-        grad_far = plane.across(grad_near, plane.steps - 1)
+        grad_far = plane.across(grad_near, plane.last)
         packed = packed.reshape(n_dev, lines, width)
         full_q = packed[:, :own].reshape(width, width)
         full_kv = packed[:, own : own + kv_lines].reshape(width, 2 * HD)
@@ -523,93 +529,78 @@
         kv_bias = jnp.concatenate([jnp.zeros((HD,), F32), bias_v])
         key_value = (dot_nn(normed_one, full_kv) + kv_bias).astype(BF16)
         key_value, normed_late = tie(key_value, normed_one)
-        kv_pieces = [key_value.reshape(windows, local_len, 2 * HD)]
-        while len(kv_pieces) < n_z:
-            kv_pieces.append(shift(kv_pieces[-1], n_z))
+        kv_pieces = line.gather(key_value.reshape(windows, local_len, 2 * HD))
         queries = (dot_nn(normed_late, full_q) + bias_q).astype(BF16)
-        kv_window = put_in_order(kv_pieces, n_z, 1)
+        kv_window = line.in_order(kv_pieces, 1)
 
         first = (lax.axis_index("fsdp") * local_len).astype(jnp.int32).reshape(1)
         file_count = lengths.shape[1]
         upto = jnp.arange(file_count)[:, None] <= jnp.arange(file_count)[None, :]
         file_ends = jnp.sum(jnp.where(upto[None], lengths[:, :, None], 0), axis=1)
-        queries, kv_window, down_pieces[-1], up_cols = tie(queries, kv_window, down_pieces[-1], up_cols)
-        while len(down_pieces) < n_z:
-            down_pieces.append(shift(down_pieces[-1], n_z))
+        queries, kv_window, down_late = tie(queries, kv_window, down_late)
+        line.more(down_pieces, soon + later, down_late)
         attended, norms = attn_forward(queries, kv_window, first, file_ends)
-        attended, down_pieces[-1], up_cols = tie(attended, down_pieces[-1], up_cols)
-        up_pieces = [up_cols, shift(up_cols, n_z)]
-        down_part = put_in_order(down_pieces, n_z)
+        attended, up_cols = meet(down_pieces, soon + later, attended, up_cols)
+        up_pieces = [up_cols] + [None] * (n_z - 1)
+        line.more(up_pieces, soon + later, up_cols)
+        down_part = line.in_order(down_pieces)
         grad_lots = [[*grad_near, *plane.cross(grad_near)]]
         back_near = back_product(grad_lots[0], down_part)
-        attended, back_near = tie(attended, back_near)
+        grad_far = list(grad_far)
+        grad_lots.append([*grad_far, *plane.cross(grad_far)])
+        attended, back_near, *grad_lots[1] = meet(up_pieces, soon, attended, back_near, *grad_lots[1])
+        line.more(up_pieces, last, up_cols)
         middle = inputs + dot_nn(attended, full_o) + bias_o
         mean_two, recip_two = norm_stats(middle)
         xhat_two = (middle - mean_two) * recip_two
         normed_two = (xhat_two * gain_two + shift_two).astype(BF16)
 
-        normed_two, up_pieces[-1], *grad_far = tie(normed_two, up_pieces[-1], *grad_far)
-        two_near = [normed_two[:half], normed_two[half:]]
-        while len(up_pieces) < min(3, n_z):
-            up_pieces.append(shift(up_pieces[-1], n_z))
-        for step in range(plane.steps - 1):
-            two_near = plane.grow(two_near, step)
-        grad_lots.append([*grad_far, *plane.cross(grad_far)])
+        normed_two, down_part = tie(normed_two, down_part)
         back_far = back_product(grad_lots[1], down_part)
-        two_near[0], two_near[1], up_pieces[-1], back_far = tie(*two_near, up_pieces[-1], back_far)
-
-        while len(up_pieces) < n_z:
-            up_pieces.append(shift(up_pieces[-1], n_z))
-        up_part = put_in_order(up_pieces, n_z, 1).reshape(width, ff_own)
+        two_near = list(meet(up_pieces, later, *plane.grow([normed_two[:half], normed_two[half:]])))
+
+        two_far = plane.across(two_near, plane.last)
+        two_lots = [[*two_near, *plane.cross(two_near)], [*two_far, *plane.cross(two_far)]]
+        up_part = line.in_order(up_pieces, 1).reshape(width, ff_own)
         bias_up_part = lax.dynamic_slice_in_dim(bias_up, my_dp * ff_own, ff_own)
-        two_far = plane.across(two_near, plane.steps - 1)
-        two_lots = [[*two_near, *plane.cross(two_near)], [*two_far, *plane.cross(two_far)]]
         hid_near, pre_near = middle_layer(two_lots[0], back_near, up_part, bias_up_part)
         places = plane.places()
-        back_far, attended, pre_near[0], pre_near[1], places = tie(back_far, attended, *pre_near, places)
-        one_mine, one_sib = reorder(normed_one, places)
-        att_mine, att_sib = reorder(attended, places)
+        back_far, attended, pre_near[0], pre_near[1], places = tie(
+            back_far, attended, *pre_near, places
+        )
         hid_far, pre_far = middle_layer(two_lots[1], back_far, up_part, bias_up_part)
         block = two_near[0].shape[0]
-
-        def lot_sum(lot, weight, product):
-            theirs = plane.swap(product(lot[1], weight).astype(BF16), 1)
-            return (product(lot[0], weight) + theirs.astype(F32)).astype(BF16)
-
-        def lot_halves(lot, weight, product):
-            theirs = plane.swap(product(lot[1], weight).astype(BF16), 1).astype(F32)
-            ours = lot[0]
+        lots = (slice(None, block), slice(block, None))
+
+        def halves(lot, weight, product):
+            theirs = plane.cross([product(lot[1][at], weight).astype(BF16) for at in lots])
             return [
-                (product(ours[at], weight) + theirs[at]).astype(BF16)
-                for at in (slice(None, block), slice(block, None))
+                (product(lot[0][at], weight) + there.astype(F32)).astype(BF16)
+                for at, there in zip(lots, theirs)
             ]
 
-        def merge(whole, got):
-            size = got[0].shape[0]
-            return [whole[i * size : (i + 1) * size].astype(F32) + got[i].astype(F32) for i in (0, 1)]
-
-        two_far = lot_halves(pre_far, up_part, dot_nt)
-        pre_near[0], pre_near[1], *two_far = tie(*pre_near, *two_far)
-        got = plane.across(two_far, plane.steps - 1)
-        two_near_sum = lot_sum(pre_near, up_part, dot_nt)
-        two_near_sum, hid_far[0], hid_far[1] = tie(two_near_sum, *hid_far)
-        out_far = lot_halves(hid_far, down_part, dot_nn)
-        out_far[0], out_far[1], pre_far[0] = tie(*out_far, pre_far[0])
+        def ours(lot, weight, product, theirs, got):
+            whole = (product(lot[0], weight) + theirs.astype(F32)).astype(BF16)
+            return [whole[at].astype(F32) + there.astype(F32) for at, there in zip(lots, got)]
+
+        two_far_sum = halves(pre_far, up_part, dot_nt)
+        pre_near[0], pre_near[1], *two_far_sum = tie(*pre_near, *two_far_sum)
+        got = plane.across(two_far_sum, plane.last)
+        theirs = plane.swap(dot_nt(pre_near[1], up_part).astype(BF16), 1)
+        pre_far[0], theirs = tie(pre_far[0], theirs)
         up_terms = weight_grad(two_lots[0] + two_lots[1], pre_near + pre_far, block)
-        up_ring = Ring(up_terms.reshape(n_dp, n_z, own, ff_own), 1, n_z)
-        two_near_sum, up_terms, hid_far[0], *got = tie(two_near_sum, up_terms, hid_far[0], *got)
-        up_ring.terms = up_terms.reshape(n_dp, n_z, own, ff_own)
-        two_sum = merge(two_near_sum, got)
-        for step in range(plane.steps - 2, -1, -1):
-            two_sum = plane.fold(two_sum, step)
-        two_grad = jnp.concatenate(two_sum)
+        pre_near[0], up_terms = tie(pre_near[0], up_terms)
+        two_sum = ours(pre_near, up_part, dot_nt, theirs, got)
+        up_got = line.scatter(up_terms.reshape(n_dp, n_z, own, ff_own), 1)
+        hid_far[0], hid_far[1], *two_sum = tie(*hid_far, *two_sum)
+        two_grad = plane.fold(two_sum)
         down_terms = weight_grad(hid_near + hid_far, grad_lots[0] + grad_lots[1], block)
-        two_grad, down_terms = tie(two_grad, down_terms)
-        down_ring = Ring(down_terms.reshape(n_z, ff_own // n_z, width), 0, n_z)
-        up_bias_part = sum(jnp.sum(lot.astype(F32), axis=0) for lot in pre_near + pre_far)
-
-        two_grad, out_far[0], out_far[1] = tie(up_ring.go(1, two_grad), *out_far)
-        out_got = plane.across(out_far, plane.steps - 1)
+        two_grad, down_terms, hid_far[0] = meet(up_got, soon, two_grad, down_terms, hid_far[0])
+        down_got = line.scatter(down_terms.reshape(n_z, ff_own // n_z, width), 0)
+        out_far = halves(hid_far, down_part, dot_nn)
+        two_grad, *out_far = tie(two_grad, *out_far)
+
+        out_got = plane.across(out_far, plane.last)
         grad_out = grad_low.astype(F32)
         grad_bdown = jnp.sum(grad_out, axis=0)
         grad_gain_two = jnp.sum(two_grad * xhat_two, axis=0)
@@ -617,63 +608,54 @@
         middle_grad = grad_out + norm_pull(two_grad, xhat_two, recip_two, gain_two)
         grad_bo = jnp.sum(middle_grad, axis=0)
         branch_grad = middle_grad.astype(BF16)
+        att_mine, att_sib = reorder(attended, places)
+        one_mine, one_sib = reorder(normed_one, places)
+
+        def cut(rows_of_lots):
+            size = rows_of_lots.shape[0] // 4
+            return [rows_of_lots[i * size : (i + 1) * size] for i in range(4)]
+
+        def plus(mine, right, theirs):
+            return (dot_tn(mine, right) + theirs.astype(F32)).astype(BF16)
+
+        def send_rows(parts):
+            return plane.across([parts[0], parts[2]], plane.last)
+
+        def own_rows(parts, got):
+            return plane.fold([n.astype(F32) + g.astype(F32) for n, g in zip((parts[1], parts[3]), got)])
+
+        theirs = plane.swap(dot_tn(att_sib, branch_grad).astype(BF16), 1)
         attended_grad = dot_nt(branch_grad, full_o).astype(BF16)
-        attended_grad, branch_late = tie(attended_grad, branch_grad)
-
-        def row_sum(mine, sib, right):
-            theirs = plane.swap(dot_tn(sib, right).astype(BF16), 1)
-            total = (dot_tn(mine, right) + theirs.astype(F32)).astype(BF16)
-            size = total.shape[0] // 4
-            return [total[i * size : (i + 1) * size] for i in range(4)]
-
-        def send_rows(lots):
-            return plane.across([lots[0], lots[2]], plane.steps - 1)
-
-        def own_rows(lots, got):
-            total = [near.astype(F32) + there.astype(F32) for near, there in zip((lots[1], lots[3]), got)]
-            for step in range(plane.steps - 2, -1, -1):
-                total = plane.fold(total, step)
-            return jnp.concatenate(total)
-
-        out_lots = row_sum(att_mine, att_sib, branch_late)
-        attended_grad, *out_lots = tie(up_ring.go(1, attended_grad), *out_lots)
-        out_lots_got = send_rows(out_lots)
+        attended_grad, branch_late = meet(up_got, later, attended_grad, branch_grad)
+        wo_parts = cut(plus(att_mine, branch_late, theirs))
+        attended_grad, *wo_parts = tie(attended_grad, *wo_parts)
+        wo_got = send_rows(wo_parts)
 
         query_grad, kv_terms = attn_backward(queries, kv_window, norms, attended_grad, first, file_ends)
-        query_grad, kv_terms, hid_near[0], *got = tie(query_grad, kv_terms, hid_near[0], *out_got, *out_lots_got)
-        out_got, out_lots_got = got[:2], got[2:]
-        query_grad = up_ring.go(1, query_grad)
-        kv_ring = Ring(kv_terms.reshape(windows, n_z, local_len, 2 * HD), 1, n_z)
-        q_lots = row_sum(one_mine, one_sib, query_grad)
-        q_lots[0] = kv_ring.go(1, q_lots[0])
-        hid_near[0], hid_near[1], query_late, *pieces = tie(*hid_near, query_grad, *q_lots, *out_lots_got)
-        q_lots, out_lots_got = pieces[:4], pieces[4:]
-        q_got = send_rows(q_lots)
-        wo_rows = own_rows(out_lots, out_lots_got)
-        hid_near[0] = kv_ring.go(n_z - 2, hid_near[0])
-        out_sum = merge(lot_sum(hid_near, down_part, dot_nn), out_got)
-        for step in range(plane.steps - 2, -1, -1):
-            out_sum = plane.fold(out_sum, step)
-        kv_grad = kv_ring.finish().astype(BF16).reshape(rows, 2 * HD)
-        branch_out = jnp.concatenate(out_sum)
-        output = (middle + branch_out + bias_down).astype(BF16).reshape(windows, local_len, width)
-        wo_ring = Ring(wo_rows.reshape(n_z, own, width), 0, n_z)
-        wq_ring = Ring(own_rows(q_lots, q_got).reshape(n_z, own, width), 0, n_z)
-        grad_wo, grad_q = wo_ring.finish(), wq_ring.finish()
-        grad_up = lax.all_to_all(
-            up_ring.finish().astype(BF16).reshape(n_dp * own, ff_own), "dp", 0, 1, tiled=True
-        ).astype(F32)
-        grad_down = down_ring.finish()
-
+        query_grad, kv_terms, *out_got = tie(query_grad, kv_terms, *out_got)
+        kv_got = line.scatter(kv_terms.reshape(windows, n_z, local_len, 2 * HD), 1)
+        (query_grad,) = meet(up_got, last, query_grad)
+        theirs = plane.swap(dot_tn(one_sib, query_grad).astype(BF16), 1)
+        theirs, *wo_got = tie(theirs, *wo_got)
+        wq_parts = cut(plus(one_mine, query_grad, theirs))
+        wq_got = send_rows(wq_parts)
+        wq_parts[1], query_late, hid_late = meet(down_got, soon, wq_parts[1], query_grad, hid_near[1])
+        wq_parts[1], *kv_got = tie(wq_parts[1], *kv_got)
+        wq_parts[3], *up_got = tie(wq_parts[3], *up_got)
+        theirs = plane.swap(dot_nn(hid_late, down_part).astype(BF16), 1)
+        query_part = dot_nt(query_late, full_q)
+        query_part, hid_near[0], theirs = tie(query_part, hid_near[0], theirs)
+        out_sum = ours(hid_near, down_part, dot_nn, theirs, out_got)
+        query_part, *out_sum = tie(query_part, *out_sum)
+        kv_grad = total(kv_got).astype(BF16).reshape(rows, 2 * HD)
+        query_part, kv_grad = meet(down_got, later, query_part, kv_grad)
+
+        one_grad = query_part + dot_nt(kv_grad, full_kv)
         grad_bq = jnp.sum(query_late.astype(F32), axis=0)
         grad_bv = jnp.sum(kv_grad[:, HD:].astype(F32), axis=0)
-        grad_wkv = dot_tn(normed_one, kv_grad)
-        one_grad = dot_nt(query_late, full_q) + dot_nt(kv_grad, full_kv)
         grad_gain_one = jnp.sum(one_grad * xhat_one, axis=0)
         grad_shift_one = jnp.sum(one_grad, axis=0)
-        tokens_grad = middle_grad + norm_pull(one_grad, xhat_one, recip_one, gain_one)
-        tokens_grad = tokens_grad.astype(BF16).reshape(windows, local_len, width)
-
+        up_bias_part = sum(jnp.sum(lot.astype(F32), axis=0) for lot in pre_near + pre_far)
         grad_bup = jnp.where(jnp.arange(n_dp)[:, None] == my_dp, up_bias_part[None], 0.0).reshape(-1)
         sums = (
             grad_bq,
@@ -686,43 +668,66 @@
             grad_gain_two,
             grad_shift_two,
         )
-        sum_rows = jnp.concatenate(
+        row_of = jnp.concatenate(
             [
-                jnp.pad(v.astype(BF16).reshape(n_dev, size), ((0, 0), (0, room - size)))
+                jnp.pad(v.reshape(n_dev, size), ((0, 0), (0, room - size)))
                 for v, size, room in zip(sums, sizes, rooms)
             ],
             axis=1,
         )
-        sum_lines = -(-(kv_lines + -(-sum(rooms) // width)) // 16) * 16
-        sum_rows = jnp.pad(
-            sum_rows, ((0, 0), (0, (sum_lines - kv_lines) * width - sum_rows.shape[1]))
-        )
-        grads = jnp.concatenate(
+        per_half = n_z // 2 * row_of.shape[1]
+        more = -(-per_half // (16 * 2 * HD)) * 16
+        row_of = jnp.pad(row_of.reshape(2 * n_dp, per_half), ((0, 0), (0, more * 2 * HD - per_half)))
+        row_of = row_of.astype(BF16).astype(F32)
+
+        def with_vectors(product, core):
+            pick = (places[core][:, None] == jnp.arange(2 * n_dp)[None, :]).astype(F32)
+            vectors = jnp.dot(pick, row_of, precision=lax.Precision.HIGHEST)
+            return jnp.concatenate(
+                [product.reshape(n_dp, -1, 2 * HD), vectors.reshape(n_dp, more, 2 * HD)], axis=1
+            ).reshape(-1, 2 * HD)
+
+        theirs = plane.swap(with_vectors(dot_tn(one_sib, kv_grad), 1).astype(BF16), 1)
+        kv_parts = cut((with_vectors(dot_tn(one_mine, kv_grad), 0) + theirs.astype(F32)).astype(BF16))
+        kv_parts_got = send_rows(kv_parts)
+        query_part, *kv_parts = tie(query_part, *kv_parts)
+
+        wo_last = line.scatter(own_rows(wo_parts, wo_got).reshape(n_z, own, width), 0)
+        wq_last = line.scatter(own_rows(wq_parts, wq_got).reshape(n_z, own, width), 0)
+        kv_last = own_rows(kv_parts, kv_parts_got).reshape(2, -1, 2 * HD)
+        kv_rows = kv_last.shape[1] - more
+        kv_last = jnp.concatenate(
             [
-                grad_wkv.astype(BF16).reshape(n_dev, kv_lines, width),
-                sum_rows.reshape(n_dev, -1, width),
+                kv_last[:, :kv_rows].reshape(n_z, -1),
+                kv_last[:, kv_rows:].reshape(2, -1)[:, :per_half].reshape(n_z, -1),
             ],
             axis=1,
         )
-        mine = scatter_both(grads.reshape(n_dev * sum_lines, width)).astype(F32)
-        grad_kv = mine[:kv_lines].reshape(own, 2 * HD)
-        flat = mine[kv_lines:].reshape(-1)
+        kv_last = line.scatter(kv_last, 0)
+        output = (middle + plane.fold(out_sum) + bias_down).astype(BF16).reshape(windows, local_len, width)
+        tokens_grad = middle_grad + norm_pull(one_grad, xhat_one, recip_one, gain_one)
+        tokens_grad = tokens_grad.astype(BF16).reshape(windows, local_len, width)
+        grad_up = lax.all_to_all(
+            total(up_got).astype(BF16).reshape(n_dp * own, ff_own), "dp", 0, 1, tiled=True
+        ).astype(F32)
+        kv_own = total(kv_last)
+        flat = kv_own[own * 2 * HD :]
         bq, bv, bo, gain1, shift1, bup, bdown, gain2, shift2 = (
             flat[start : start + size] for start, size in zip(starts, sizes)
         )
         return (
             output,
             tokens_grad,
-            grad_q,
-            grad_kv,
-            grad_wo,
+            total(wq_last),
+            kv_own[: own * 2 * HD].reshape(own, 2 * HD),
+            total(wo_last),
             bq,
             bv,
             bo,
             gain1,
             shift1,
             grad_up,
-            grad_down,
+            total(down_got),
             bup,
             bdown,
             gain2,

time: 901 us -> 993 us (1.10)
  starting transfers between devices: 46.4 us -> 131 us
  waiting for transfers between devices: 333 us -> 354 us
  blocking collectives: 20.6 us -> 0 us
  matrix products: 117 us -> 133 us
  other arithmetic: 90.4 us -> 77.7 us
    ppermute x27 -> x30, starting transfers between devices: 14.2 us -> 86 us  [send(): lax.ppermute(block, 'fsdp', [(i, (i + places) % self.count) for i in rang...]
    ppermute x38 -> x45, waiting for transfers between devices: 138 us -> 169 us  [swap(): return lax.ppermute(block, 'dp', [(i, i ^ bit) for i in range(self.count)])]
    all_to_all x1 -> x0, blocking collectives: 20.6 us -> none  [local(): lax.all_to_all(up_weight, 'dp', 1, 0, tiled=True).reshape(n_dp, own, ff_own)]
    all_gather x1, waiting for transfers between devices: 13.6 us -> 0.01 us  [local(): packed = lax.all_gather(packed, 'fsdp', axis=0, tiled=True)]
    add x14 -> x12, other arithmetic: 30.6 us -> 19.9 us  [the longest x4 7.29 us: total(): out += term.astype(F32)]
    ppermute x38 -> x45, starting transfers between devices: 27.8 us -> 37.2 us  [swap(): return lax.ppermute(block, 'dp', [(i, i ^ bit) for i in range(self.count)])]
    dot_general x8 -> x9, matrix products: 42.2 us -> 50 us  [dot_nt(): lax.dot_general(left, right, (((1,), (1,)), ((), ())), preferred_element_...]
    dot_general x8 -> x9, matrix products: 54.9 us -> 61.1 us  [dot_nn(): return jnp.dot(left, right, preferred_element_type=F32)]
  transfers between devices with their start and end apart: 71 -> 80, of which waited for: 33 -> 32; matrix products, arithmetic and copies ran while one was open for 22% -> 23% of each run, Pallas kernels for 18% -> 16%
where the time goes in v5:
time: 993 us; the launch traced here: 983 us
  waiting for transfers between devices  354 us (36%)
  Pallas kernels  182 us (18%)
  matrix products  133 us (13%)
  starting transfers between devices  131 us (13%)
  local copies, waits for them, and re-layouts  89.4 us (9%)
  other arithmetic  77.7 us (8%)
  between operations  16 us (2%)
    ppermute x30, waiting for transfers between devices, send(): lax.ppermute(block, 'fsdp', [(i, (i + places) % self.count) for i in rang...  178 us
    ppermute x45, waiting for transfers between devices, swap(): return lax.ppermute(block, 'dp', [(i, i ^ bit) for i in range(self.count)])  169 us
    ppermute x30, starting transfers between devices, send(): lax.ppermute(block, 'fsdp', [(i, (i + places) % self.count) for i in rang...  86 us
    dot_general x9, matrix products, dot_nn(): return jnp.dot(left, right, preferred_element_type=F32)  61.1 us
    pallas_call x2, Pallas kernels, weight_grad(): pl.pallas_call(functools.partial(weight_kernel, count), out_shape=jax.Sha...  50.8 us
    dot_general x9, matrix products, dot_nt(): lax.dot_general(left, right, (((1,), (1,)), ((), ())), preferred_element_...  50 us
    pallas_call x2, Pallas kernels, middle_layer(): pl.pallas_call(functools.partial(middle_kernel, count), out_shape=[jax.Sh...  39.9 us
    ppermute x45, starting transfers between devices, swap(): return lax.ppermute(block, 'dp', [(i, i ^ bit) for i in range(self.count)])  37.2 us
  transfers between devices with their start and end apart: 80, of which 32 were waited for; matrix products, arithmetic and copies ran while one was open for 23% of the time, Pallas kernels for 16%

profile of v5, /device:TPU:0, one launch (start us, length us, event | category | flops | bytes accessed | tf_op | source)
XLA Modules:
  0.0 983.4 jit_solution(415983401951223027)
XLA Ops:
  24.9 4.2 all-to-all-start
  29.2 17.2 %collective-permute-done = bf16[256,2048]{1,0:T(8,128)(2,1)} collective-permute-done((bf16[256,2048]{1,0:T(8,128)(2,1)S(1)}, bf16[256,2048]{1,0:T(8,128)(2,1)}, u32[]{:S(2)}, u32[]{:S(2)}) %collective-permute-start) | collective-permute-done | bytes 1048608 | tf_op jit(solution)/shard_map/ppermute | solution.py:420
  51.6 6.6 all-to-all-done
  66.0 3.7 collective-permute-done.2
  69.7 7.1 collective-permute-done.3
  76.8 5.2 collective-permute-start.5
  85.1 43.0 %collective-permute-done.5 = bf16[256,2048]{1,0:T(8,128)(2,1)} collective-permute-done((bf16[256,2048]{1,0:T(8,128)(2,1)}, bf16[256,2048]{1,0:T(8,128)(2,1)}, u32[]{:S(2)}, u32[]{:S(2)}) %collective-permute-start.5) | collective-permute-done | bytes 1048608 | tf_op jit(solution)/shard_map/ppermute | solution.py:348
  130.5 8.8 slice.348
  151.9 3.7 collective-permute-start.7
  160.0 9.8 %add_convert_fusion.9.q_ref = bf16[512,2048]{1,0:T(8,128)(2,1)} fusion(bf16[512,2048]{1,0:T(8,128)(2,1)} %fusion.14.first_ref.second_ref, bf16[2048,2048]{1,0:T(8,128)(2,1)} %bitcast.226, f32[2048]{0:T(1024)S(1)} %reshape.424), kind=kOutput, calls=%fused_computation.51 | convolution fusion | flops 4297064448 | bytes 12591104 | tf_op jit(solution)/shard_map/dot_general | solution.py:21
  174.6 5.2 collective-permute-start.9
  180.3 22.4 %collective-permute-done.9 = bf16[256,2048]{1,0:T(8,128)(2,1)S(1)} collective-permute-done((bf16[256,2048]{1,0:T(8,128)(2,1)}, bf16[256,2048]{1,0:T(8,128)(2,1)S(1)}, u32[]{:S(2)}, u32[]{:S(2)}) %collective-permute-start.9) | collective-permute-done | bytes 1048608 | tf_op jit(solution)/shard_map/ppermute | solution.py:348
  204.0 21.4 %collective-permute-done.13.refs_0_.refs_12_ = bf16[512,2048]{1,0:T(8,128)(2,1)} collective-permute-done((bf16[512,2048]{1,0:T(8,128)(2,1)S(1)}, bf16[512,2048]{1,0:T(8,128)(2,1)}, u32[]{:S(2)}, u32[]{:S(2)}) %collective-permute-start.13) | collective-permute-done | bytes 2097184 | tf_op jit(solution)/shard_map/ppermute | solution.py:420
  229.3 18.7 %shard_map.288 = (bf16[512,2048]{1,0:T(8,128)(2,1)S(1)}, f32[512,128]{1,0:T(8,128)S(1)}) custom-call(s32[1]{0:T(128)} %bitcast.1.pos_ref, s32[2,8]{1,0:T(2,128)S(1)} %select_reduce_fusion.ends_ref, bf16[512,2048]{1,0:T(8,128)(2,1)S(1)} %copy-done.8, bf16[2,1024,256]{2,1,0:T(8,128)(2,1)S(1)} %constant_dynamic-update-slice_fusion.19.kv_ref), custom_call_target="tpu_custom_call" | custom-call | flops 536870912 | bytes 524288 | tf_op jit(solution)/shard_map/pallas_call | solution.py:132
  263.1 14.0 %shard_map.289.refs_4_ = bf16[2048,1024]{1,0:T(8,128)(2,1)} custom-call(bf16[512,2048]{1,0:T(8,128)(2,1)S(1)} %pad_maximum_fusion.1.refs_0_.refs_8_, bf16[512,2048]{1,0:T(8,128)(2,1)} %pad_maximum_fusion.2.refs_1_.refs_9_, bf16[512,2048]{1,0:T(8,128)(2,1)} %collective-permute-done.11.refs_2_.refs_10_, ...), custom_call_target="tpu_custom_call" | custom-call | flops 1073741824 | bytes 2097152 | tf_op jit(solution)/shard_map/pallas_call | solution.py:236
  277.3 9.2 fusion.60
  293.4 20.5 %collective-permute-done.18 = bf16[256,2048]{1,0:T(8,128)(2,1)S(1)} collective-permute-done((bf16[256,2048]{1,0:T(8,128)(2,1)S(1)}, bf16[256,2048]{1,0:T(8,128)(2,1)S(1)}, u32[]{:S(2)}, u32[]{:S(2)}) %collective-permute-start.18) | collective-permute-done | bytes 1048608 | tf_op jit(solution)/shard_map/ppermute | solution.py:420
  318.4 44.4 %collective-permute-done.24.refs_0_.refs_4_ = bf16[512,2048]{1,0:T(8,128)(2,1)} collective-permute-done((bf16[512,2048]{1,0:T(8,128)(2,1)S(1)}, bf16[512,2048]{1,0:T(8,128)(2,1)}, u32[]{:S(2)}, u32[]{:S(2)}) %collective-permute-start.24) | collective-permute-done | bytes 2097184 | tf_op jit(solution)/shard_map/ppermute | solution.py:420
  369.4 43.4 %collective-permute-done.23 = bf16[8,64,1024]{2,1,0:T(8,128)(2,1)} collective-permute-done((bf16[8,64,1024]{2,1,0:T(8,128)(2,1)}, bf16[8,64,1024]{2,1,0:T(8,128)(2,1)}, u32[]{:S(2)}, u32[]{:S(2)}) %collective-permute-start.23) | collective-permute-done | bytes 1048608 | tf_op jit(solution)/shard_map/ppermute | solution.py:348
  414.1 14.7 %shard_map.290.refs_4_ = bf16[2048,1024]{1,0:T(8,128)(2,1)} custom-call(bf16[512,2048]{1,0:T(8,128)(2,1)} %collective-permute-done.13.refs_0_.refs_12_, bf16[512,2048]{1,0:T(8,128)(2,1)} %collective-permute-done.14.refs_1_.refs_13_, bf16[512,2048]{1,0:T(8,128)(2,1)} %collective-permute-done.15.refs_2_.refs_14_, ...), custom_call_target="tpu_custom_call" | custom-call | flops 1073741824 | bytes 2097152 | tf_op jit(solution)/shard_map/pallas_call | solution.py:236
  430.8 19.6 %shard_map.291 = (bf16[1024,1024]{1,0:T(8,128)(2,1)S(1)}, bf16[1024,1024]{1,0:T(8,128)(2,1)S(1)}, bf16[1024,1024]{1,0:T(8,128)(2,1)}, bf16[1024,1024]{1,0:T(8,128)(2,1)}) custom-call(bf16[512,2048]{1,0:T(8,128)(2,1)} %copy-done.30, bf16[512,2048]{1,0:T(8,128)(2,1)} %pad_maximum_fusion.4.refs_1_, bf16[512,2048]{1,0:T(8,128)(2,1)} %collective-permute-done.21.refs_2_, ...), custom_call_target="tpu_custom_call" | custom-call | flops 1073741824 | bytes 3145728 | tf_op jit(solution)/shard_map/pallas_call | solution.py:202
  453.1 20.2 %shard_map.293 = (bf16[1024,1024]{1,0:T(8,128)(2,1)S(1)}, bf16[1024,1024]{1,0:T(8,128)(2,1)S(1)}, bf16[1024,1024]{1,0:T(8,128)(2,1)}, bf16[1024,1024]{1,0:T(8,128)(2,1)}) custom-call(bf16[512,2048]{1,0:T(8,128)(2,1)} %collective-permute-done.24.refs_0_.refs_4_, bf16[512,2048]{1,0:T(8,128)(2,1)} %collective-permute-done.25.refs_1_.refs_5_, ...), custom_call_target="tpu_custom_call" | custom-call | flops 1073741824 | bytes 3145728 | tf_op jit(solution)/shard_map/pallas_call | solution.py:202
  473.4 4.6 convolution_convert_fusion.8
  482.2 3.7 add_convert_fusion.7
  485.9 3.7 add_convert_fusion.6
  489.6 6.2 convolution_convert_fusion.4
  498.3 6.6 shard_map.296
  504.8 24.6 %shard_map.294 = bf16[2048,1024]{1,0:T(8,128)(2,1)} custom-call(bf16[512,2048]{1,0:T(8,128)(2,1)} %copy-done.30, bf16[512,2048]{1,0:T(8,128)(2,1)} %pad_maximum_fusion.4.refs_1_, bf16[512,2048]{1,0:T(8,128)(2,1)} %collective-permute-done.21.refs_2_, bf16[512,2048]{1,0:T(8,128)(2,1)} %collective-permute-done.22.refs_3_, ...), custom_call_target="tpu_custom_call" | custom-call | flops 2147483648 | bytes 3670016 | tf_op jit(solution)/shard_map/pallas_call | solution.py:276
  529.5 6.4 add_convert_fusion.3
  535.9 8.3 collective-permute-done.32
  544.8 4.0 convert_add_fusion.3
  553.4 5.8 convolution_convert_fusion.6
  559.2 6.0 convolution_convert_fusion.5
  567.5 26.2 %shard_map.295 = bf16[1024,2048]{1,0:T(8,128)(2,1)} custom-call(bf16[1024,1024]{1,0:T(8,128)(2,1)} %copy-done.1, bf16[1024,1024]{1,0:T(8,128)(2,1)} %copy-done.1, bf16[1024,1024]{1,0:T(8,128)(2,1)} %copy-done.3, bf16[1024,1024]{1,0:T(8,128)(2,1)} %copy-done.3, bf16[1024,1024]{1,0:T(8,128)(2,1)} %copy-done.5, bf16[1024,1024]{1,0:T(8,128)(2,1)} %copy-done.5, ...), custom_call_target="tpu_custom_call" | custom-call | flops 2147483648 | bytes 3670016 | tf_op jit(solution)/shard_map/pallas_call | solution.py:276
  598.6 6.5 add_convert_fusion.5
  605.2 6.7 add_convert_fusion.4
  618.8 4.3 convolution_convert_fusion.2
  623.3 6.5 shard_map.292
  629.8 3.8 collective-permute-start.38
  635.3 9.1 convolution_convert_fusion.9.grad_ref
  644.4 13.1 %collective-permute-done.38 = bf16[8,64,1024]{2,1,0:T(8,128)(2,1)S(1)} collective-permute-done((bf16[8,64,1024]{2,1,0:T(8,128)(2,1)}, bf16[8,64,1024]{2,1,0:T(8,128)(2,1)S(1)}, u32[]{:S(2)}, u32[]{:S(2)}) %collective-permute-start.38) | collective-permute-done | bytes 1048608 | tf_op jit(solution)/shard_map/ppermute | solution.py:348
  657.5 5.0 add_convert_fusion.2
  664.6 30.5 %shard_map.297 = (bf16[512,2048]{1,0:T(8,128)(2,1)S(1)}, bf16[2,1024,256]{2,1,0:T(8,128)(2,1)S(1)}) custom-call(s32[1]{0:T(128)} %bitcast.1.pos_ref, s32[2,8]{1,0:T(2,128)S(1)} %copy-done.13, bf16[512,2048]{1,0:T(8,128)(2,1)} %add_convert_fusion.9.q_ref, bf16[2,1024,256]{2,1,0:T(8,128)(2,1)S(1)} %constant_dynamic-update-slice_fusion.19.kv_ref, ...), custom_call_target="tpu_custom_call" | custom-call | flops 1342177280 | bytes 1310720 | tf_op jit(solution)/shard_map/pallas_call | solution.py:152
  695.2 5.9 collective-permute-done.42
  701.1 4.4 convolution_convert_fusion.1
  716.2 3.7 dynamic-slice_bitcast_fusion
  722.3 15.4 %collective-permute-done.44 = bf16[256,2048]{1,0:T(8,128)(2,1)} collective-permute-done((bf16[256,2048]{1,0:T(8,128)(2,1)}, bf16[256,2048]{1,0:T(8,128)(2,1)}, u32[]{:S(2)}, u32[]{:S(2)}) %collective-permute-start.44) | collective-permute-done | bytes 1048608 | tf_op jit(solution)/shard_map/ppermute | solution.py:420
  737.8 4.2 collective-permute-start.52
  741.9 4.9 add_convert_fusion.1
  749.0 9.8 fusion.61
  758.9 8.3 convolution_convert_fusion.3
  785.4 20.8 %collective-permute-done.70 = bf16[128,2048]{1,0:T(8,128)(2,1)} collective-permute-done((bf16[128,2048]{1,0:T(8,128)(2,1)}, bf16[128,2048]{1,0:T(8,128)(2,1)}, u32[]{:S(2)}, u32[]{:S(2)}) %collective-permute-start.70) | collective-permute-done | bytes 524320 | tf_op jit(solution)/shard_map/ppermute | solution.py:420
  818.1 4.0 collective-permute-start.53
  822.1 14.9 %collective-permute-done.72 = bf16[64,2048]{1,0:T(8,128)(2,1)S(1)} collective-permute-done((bf16[64,2048]{1,0:T(8,128)(2,1)S(1)}, bf16[64,2048]{1,0:T(8,128)(2,1)S(1)}, u32[]{:S(2)}, u32[]{:S(2)}) %collective-permute-start.72) | collective-permute-done | bytes 262176 | tf_op jit(solution)/shard_map/ppermute | solution.py:348
  839.7 6.5 collective-permute-done.55
  847.5 17.9 %collective-permute-start.60 = (bf16[64,2048]{1,0:T(8,128)(2,1)}, bf16[64,2048]{1,0:T(8,128)(2,1)}, u32[]{:S(2)}, u32[]{:S(2)}) collective-permute-start(bf16[64,2048]{1,0:T(8,128)(2,1)} %get-tuple-element.292), channel_id=1, source_target_pairs={{0,3},{1,0},{2,1},{3,2},{4,7},{5,4},{6,5},{7,6},{8,11},{9,8},{10,9... | collective-permute-start | bytes 786440 | tf_op jit(solution)/shard_map/ppermute | solution.py:348
  867.7 4.8 collective-permute-done.60
  872.5 21.1 %collective-permute-start.74 = (bf16[256,2048]{1,0:T(8,128)(2,1)}, bf16[256,2048]{1,0:T(8,128)(2,1)}, u32[]{:S(2)}, u32[]{:S(2)}) collective-permute-start(bf16[256,2048]{1,0:T(8,128)(2,1)} %get-tuple-element.269), channel_id=1, source_target_pairs={{0,2},{1,3},{2,0},{3,1},{4,6},{5,7},{6,4},{7,5},{8,10},{9,11},{10,... | collective-permute-start | bytes 3145736 | tf_op jit(solution)/shard_map/ppermute | solution.py:348
  893.6 17.3 %collective-permute-done.59 = bf16[64,2048]{1,0:T(8,128)(2,1)} collective-permute-done((bf16[64,2048]{1,0:T(8,128)(2,1)}, bf16[64,2048]{1,0:T(8,128)(2,1)}, u32[]{:S(2)}, u32[]{:S(2)}) %collective-permute-start.59) | collective-permute-done | bytes 262176 | tf_op jit(solution)/shard_map/ppermute | solution.py:348
  913.1 7.9 add_convert_fusion
  930.4 4.2 fusion.20
  944.5 4.3 fusion.19
  950.9 4.2 collective-permute-done.62
  962.7 4.2 fusion.23
  (504 shorter events, 224.1 us)
Async XLA Ops:
  7.2 51.0 %all-gather.4.cloned.1.call-start = ((), (), s32[]{:S(2)}) async-start(), calls=%async_computation.2 | async-start | bytes 1638400 | tf_op jit(solution)/shard_map/all_gather | solution.py:500
  19.3 27.1 %collective-permute-start = (bf16[256,2048]{1,0:T(8,128)(2,1)S(1)}, bf16[256,2048]{1,0:T(8,128)(2,1)}, u32[]{:S(2)}, u32[]{:S(2)}) collective-permute-start(bf16[256,2048]{1,0:T(8,128)(2,1)S(1)} %get-tuple-element.297), channel_id=1, source_target_pairs={{0,8},{4,12},{8,0},{12,4},{16,24},{20,28},{24,16},{28,20},{1,9},{5... | collective-permute-start | bytes 3145736 | tf_op jit(solution)/shard_map/ppermute | solution.py:420
  22.3 26.2 %collective-permute-start.1 = (bf16[256,2048]{1,0:T(8,128)(2,1)S(1)}, bf16[256,2048]{1,0:T(8,128)(2,1)}, u32[]{:S(2)}, u32[]{:S(2)}) collective-permute-start(bf16[256,2048]{1,0:T(8,128)(2,1)S(1)} %get-tuple-element.296), channel_id=1, source_target_pairs={{0,16},{4,20},{8,24},{12,28},{16,0},{20,4},{24,8},{28,12},{1,17},{... | collective-permute-start | bytes 3145736 | tf_op jit(solution)/shard_map/ppermute | solution.py:420
  24.9 33.4 %all-to-all-start = ((bf16[64,8,1024]{2,0,1:T(8,128)(2,1)}), bf16[64,8,1024]{2,0,1:T(8,128)(2,1)}, u32[]{:S(2)}, u32[]{:S(2)}) async-start(bf16[64,8,1024]{2,0,1:T(8,128)(2,1)} %bitcast.209), calls=%async_computation | async-start | bytes 2097152 | tf_op jit(solution)/shard_map/all_to_all | solution.py:502
  29.1 99.0 %all-gather.6.cloned.1.call-start = ((), (), s32[]{:S(2)}) async-start(), calls=%async_computation.3 | async-start | bytes 11796480 | tf_op jit(solution)/shard_map/all_gather | solution.py:505
  58.3 219.0 %all-gather.8.cloned.1.call-start = ((), (), s32[]{:S(2)}) async-start(), calls=%async_computation.4 | async-start | bytes 9437184 | tf_op jit(solution)/shard_map/all_gather | solution.py:517
  76.8 51.3 %collective-permute-start.5 = (bf16[256,2048]{1,0:T(8,128)(2,1)}, bf16[256,2048]{1,0:T(8,128)(2,1)}, u32[]{:S(2)}, u32[]{:S(2)}) collective-permute-start(bf16[256,2048]{1,0:T(8,128)(2,1)} %param.29), channel_id=1, source_target_pairs={{0,2},{1,3},{2,0},{3,1},{4,6},{5,7},{6,4},{7,5},{8,10},{9,11},{10,... | collective-permute-start | bytes 3145736 | tf_op jit(solution)/shard_map/ppermute | solution.py:348
  151.6 18.3 %collective-permute-start.6 = (bf16[2,256,256]{2,1,0:T(8,128)(2,1)S(1)}, bf16[2,256,256]{2,1,0:T(8,128)(2,1)}, u32[]{:S(2)}, u32[]{:S(2)}) collective-permute-start(bf16[2,256,256]{2,1,0:T(8,128)(2,1)S(1)} %bitcast.251), channel_id=1, source_target_pairs={{0,1},{1,2},{2,3},{3,0},{4,5},{5,6},{6,7},{7,4},{8,9},{9,10},{10,1... | collective-permute-start | bytes 786440 | tf_op jit(solution)/shard_map/ppermute | solution.py:348
  151.9 20.8 %collective-permute-start.7 = (bf16[2,256,256]{2,1,0:T(8,128)(2,1)S(1)}, bf16[2,256,256]{2,1,0:T(8,128)(2,1)}, u32[]{:S(2)}, u32[]{:S(2)}) collective-permute-start(bf16[2,256,256]{2,1,0:T(8,128)(2,1)S(1)} %bitcast.252), channel_id=1, source_target_pairs={{0,2},{1,3},{2,0},{3,1},{4,6},{5,7},{6,4},{7,5},{8,10},{9,11},{10,... | collective-permute-start | bytes 786440 | tf_op jit(solution)/shard_map/ppermute | solution.py:348
  155.6 18.1 %collective-permute-start.8 = (bf16[2,256,256]{2,1,0:T(8,128)(2,1)S(1)}, bf16[2,256,256]{2,1,0:T(8,128)(2,1)}, u32[]{:S(2)}, u32[]{:S(2)}) collective-permute-start(bf16[2,256,256]{2,1,0:T(8,128)(2,1)S(1)} %bitcast.253), channel_id=1, source_target_pairs={{0,3},{1,0},{2,1},{3,2},{4,7},{5,4},{6,5},{7,6},{8,11},{9,8},{10,9... | collective-permute-start | bytes 786440 | tf_op jit(solution)/shard_map/ppermute | solution.py:348
  156.1 69.3 %collective-permute-start.13 = (bf16[512,2048]{1,0:T(8,128)(2,1)S(1)}, bf16[512,2048]{1,0:T(8,128)(2,1)}, u32[]{:S(2)}, u32[]{:S(2)}) collective-permute-start(bf16[512,2048]{1,0:T(8,128)(2,1)S(1)} %pad_maximum_fusion.1.refs_0_.refs_8_), channel_id=1, source_target_pairs={{0,16},{4,20},{8,24},{12,28},{16,0},{20,4},{24,8},{28,12},{1,17},{... | collective-permute-start | bytes 6291464 | tf_op jit(solution)/shard_map/ppermute | solution.py:420
  157.8 69.8 %collective-permute-start.14 = (bf16[512,2048]{1,0:T(8,128)(2,1)}, bf16[512,2048]{1,0:T(8,128)(2,1)}, u32[]{:S(2)}, u32[]{:S(2)}) collective-permute-start(bf16[512,2048]{1,0:T(8,128)(2,1)} %pad_maximum_fusion.2.refs_1_.refs_9_), channel_id=1, source_target_pairs={{0,8},{4,12},{8,0},{12,4},{16,24},{20,28},{24,16},{28,20},{1,9},{5... | collective-permute-start | bytes 6291464 | tf_op jit(solution)/shard_map/ppermute | solution.py:420
  174.6 28.1 %collective-permute-start.9 = (bf16[256,2048]{1,0:T(8,128)(2,1)}, bf16[256,2048]{1,0:T(8,128)(2,1)S(1)}, u32[]{:S(2)}, u32[]{:S(2)}) collective-permute-start(bf16[256,2048]{1,0:T(8,128)(2,1)} %param.29), channel_id=1, source_target_pairs={{0,1},{1,2},{2,3},{3,0},{4,5},{5,6},{6,7},{7,4},{8,9},{9,10},{10,1... | collective-permute-start | bytes 3145736 | tf_op jit(solution)/shard_map/ppermute | solution.py:348
  179.8 83.3 %collective-permute-start.11 = (bf16[512,2048]{1,0:T(8,128)(2,1)S(1)}, bf16[512,2048]{1,0:T(8,128)(2,1)}, u32[]{:S(2)}, u32[]{:S(2)}) collective-permute-start(bf16[512,2048]{1,0:T(8,128)(2,1)S(1)} %pad_maximum_fusion.1.refs_0_.refs_8_), channel_id=1, source_target_pairs={{0,4},{4,0},{8,12},{12,8},{16,20},{20,16},{24,28},{28,24},{1,5},{5... | collective-permute-start | bytes 6291464 | tf_op jit(solution)/shard_map/ppermute | solution.py:420
  179.8 83.3 %collective-permute-start.12 = (bf16[512,2048]{1,0:T(8,128)(2,1)}, bf16[512,2048]{1,0:T(8,128)(2,1)}, u32[]{:S(2)}, u32[]{:S(2)}) collective-permute-start(bf16[512,2048]{1,0:T(8,128)(2,1)} %pad_maximum_fusion.2.refs_1_.refs_9_), channel_id=1, source_target_pairs={{0,4},{4,0},{8,12},{12,8},{16,20},{20,16},{24,28},{28,24},{1,5},{5... | collective-permute-start | bytes 6291464 | tf_op jit(solution)/shard_map/ppermute | solution.py:420
  202.7 46.7 %collective-permute-start.10 = (bf16[256,2048]{1,0:T(8,128)(2,1)}, bf16[256,2048]{1,0:T(8,128)(2,1)}, u32[]{:S(2)}, u32[]{:S(2)}) collective-permute-start(bf16[256,2048]{1,0:T(8,128)(2,1)} %param.29), channel_id=1, source_target_pairs={{0,3},{1,0},{2,1},{3,2},{4,7},{5,4},{6,5},{7,6},{8,11},{9,8},{10,9... | collective-permute-start | bytes 3145736 | tf_op jit(solution)/shard_map/ppermute | solution.py:348
  225.4 51.8 %collective-permute-start.15 = (bf16[512,2048]{1,0:T(8,128)(2,1)}, bf16[512,2048]{1,0:T(8,128)(2,1)}, u32[]{:S(2)}, u32[]{:S(2)}) collective-permute-start(bf16[512,2048]{1,0:T(8,128)(2,1)} %collective-permute-done.13.refs_0_.refs_12_), channel_id=1, source_target_pairs={{0,4},{4,0},{8,12},{12,8},{16,20},{20,16},{24,28},{28,24},{1,5},{5... | collective-permute-start | bytes 6291464 | tf_op jit(solution)/shard_map/ppermute | solution.py:420
  227.6 49.6 %collective-permute-start.16 = (bf16[512,2048]{1,0:T(8,128)(2,1)}, bf16[512,2048]{1,0:T(8,128)(2,1)}, u32[]{:S(2)}, u32[]{:S(2)}) collective-permute-start(bf16[512,2048]{1,0:T(8,128)(2,1)} %collective-permute-done.14.refs_1_.refs_13_), channel_id=1, source_target_pairs={{0,4},{4,0},{8,12},{12,8},{16,20},{20,16},{24,28},{28,24},{1,5},{5... | collective-permute-start | bytes 6291464 | tf_op jit(solution)/shard_map/ppermute | solution.py:420
  249.4 27.8 %collective-permute-start.17 = (bf16[8,64,1024]{2,1,0:T(8,128)(2,1)}, bf16[8,64,1024]{2,1,0:T(8,128)(2,1)}, u32[]{:S(2)}, u32[]{:S(2)}) collective-permute-start(bf16[8,64,1024]{2,1,0:T(8,128)(2,1)} %bitcast.2), channel_id=1, source_target_pairs={{0,1},{1,2},{2,3},{3,0},{4,5},{5,6},{6,7},{7,4},{8,9},{9,10},{10,1... | collective-permute-start | bytes 3145736 | tf_op jit(solution)/shard_map/ppermute | solution.py:348
  288.7 25.3 %collective-permute-start.18 = (bf16[256,2048]{1,0:T(8,128)(2,1)S(1)}, bf16[256,2048]{1,0:T(8,128)(2,1)S(1)}, u32[]{:S(2)}, u32[]{:S(2)}) collective-permute-start(bf16[256,2048]{1,0:T(8,128)(2,1)S(1)} %get-tuple-element.295), channel_id=1, source_target_pairs={{0,8},{4,12},{8,0},{12,4},{16,24},{20,28},{24,16},{28,20},{1,9},{5... | collective-permute-start | bytes 3145736 | tf_op jit(solution)/shard_map/ppermute | solution.py:420
  289.4 24.8 %collective-permute-start.19 = (bf16[256,2048]{1,0:T(8,128)(2,1)S(1)}, bf16[256,2048]{1,0:T(8,128)(2,1)S(1)}, u32[]{:S(2)}, u32[]{:S(2)}) collective-permute-start(bf16[256,2048]{1,0:T(8,128)(2,1)S(1)} %get-tuple-element.294), channel_id=1, source_target_pairs={{0,16},{4,20},{8,24},{12,28},{16,0},{20,4},{24,8},{28,12},{1,17},{... | collective-permute-start | bytes 3145736 | tf_op jit(solution)/shard_map/ppermute | solution.py:420
  291.1 24.9 %collective-permute-start.20 = (bf16[8,64,1024]{2,1,0:T(8,128)(2,1)}, bf16[8,64,1024]{2,1,0:T(8,128)(2,1)S(1)}, u32[]{:S(2)}, u32[]{:S(2)}) collective-permute-start(bf16[8,64,1024]{2,1,0:T(8,128)(2,1)} %bitcast.2), channel_id=1, source_target_pairs={{0,3},{1,0},{2,1},{3,2},{4,7},{5,4},{6,5},{7,6},{8,11},{9,8},{10,9... | collective-permute-start | bytes 3145736 | tf_op jit(solution)/shard_map/ppermute | solution.py:348
  316.0 46.8 %collective-permute-start.24 = (bf16[512,2048]{1,0:T(8,128)(2,1)S(1)}, bf16[512,2048]{1,0:T(8,128)(2,1)}, u32[]{:S(2)}, u32[]{:S(2)}) collective-permute-start(bf16[512,2048]{1,0:T(8,128)(2,1)S(1)} %pad_maximum_fusion.3.refs_0_), channel_id=1, source_target_pairs={{0,16},{4,20},{8,24},{12,28},{16,0},{20,4},{24,8},{28,12},{1,17},{... | collective-permute-start | bytes 6291464 | tf_op jit(solution)/shard_map/ppermute | solution.py:420
  317.3 46.2 %collective-permute-start.25 = (bf16[512,2048]{1,0:T(8,128)(2,1)}, bf16[512,2048]{1,0:T(8,128)(2,1)}, u32[]{:S(2)}, u32[]{:S(2)}) collective-permute-start(bf16[512,2048]{1,0:T(8,128)(2,1)} %pad_maximum_fusion.4.refs_1_), channel_id=1, source_target_pairs={{0,8},{4,12},{8,0},{12,4},{16,24},{20,28},{24,16},{28,20},{1,9},{5... | collective-permute-start | bytes 6291464 | tf_op jit(solution)/shard_map/ppermute | solution.py:420
  317.9 111.0 %collective-permute-start.21 = (bf16[512,2048]{1,0:T(8,128)(2,1)S(1)}, bf16[512,2048]{1,0:T(8,128)(2,1)}, u32[]{:S(2)}, u32[]{:S(2)}) collective-permute-start(bf16[512,2048]{1,0:T(8,128)(2,1)S(1)} %pad_maximum_fusion.3.refs_0_), channel_id=1, source_target_pairs={{0,4},{4,0},{8,12},{12,8},{16,20},{20,16},{24,28},{28,24},{1,5},{5... | collective-permute-start | bytes 6291464 | tf_op jit(solution)/shard_map/ppermute | solution.py:420
  317.9 111.0 %collective-permute-start.22 = (bf16[512,2048]{1,0:T(8,128)(2,1)}, bf16[512,2048]{1,0:T(8,128)(2,1)}, u32[]{:S(2)}, u32[]{:S(2)}) collective-permute-start(bf16[512,2048]{1,0:T(8,128)(2,1)} %pad_maximum_fusion.4.refs_1_), channel_id=1, source_target_pairs={{0,4},{4,0},{8,12},{12,8},{16,20},{20,16},{24,28},{28,24},{1,5},{5... | collective-permute-start | bytes 6291464 | tf_op jit(solution)/shard_map/ppermute | solution.py:420
  362.8 90.3 %collective-permute-start.26 = (bf16[512,2048]{1,0:T(8,128)(2,1)}, bf16[512,2048]{1,0:T(8,128)(2,1)}, u32[]{:S(2)}, u32[]{:S(2)}) collective-permute-start(bf16[512,2048]{1,0:T(8,128)(2,1)} %collective-permute-done.24.refs_0_.refs_4_), channel_id=1, source_target_pairs={{0,4},{4,0},{8,12},{12,8},{16,20},{20,16},{24,28},{28,24},{1,5},{5... | collective-permute-start | bytes 6291464 | tf_op jit(solution)/shard_map/ppermute | solution.py:420
  363.5 89.6 %collective-permute-start.27 = (bf16[512,2048]{1,0:T(8,128)(2,1)}, bf16[512,2048]{1,0:T(8,128)(2,1)}, u32[]{:S(2)}, u32[]{:S(2)}) collective-permute-start(bf16[512,2048]{1,0:T(8,128)(2,1)} %collective-permute-done.25.refs_1_.refs_5_), channel_id=1, source_target_pairs={{0,4},{4,0},{8,12},{12,8},{16,20},{20,16},{24,28},{28,24},{1,5},{5... | collective-permute-start | bytes 6291464 | tf_op jit(solution)/shard_map/ppermute | solution.py:420
  363.5 49.3 %collective-permute-start.23 = (bf16[8,64,1024]{2,1,0:T(8,128)(2,1)}, bf16[8,64,1024]{2,1,0:T(8,128)(2,1)}, u32[]{:S(2)}, u32[]{:S(2)}) collective-permute-start(bf16[8,64,1024]{2,1,0:T(8,128)(2,1)} %bitcast.2), channel_id=1, source_target_pairs={{0,2},{1,3},{2,0},{3,1},{4,6},{5,7},{6,4},{7,5},{8,10},{9,11},{10,... | collective-permute-start | bytes 3145736 | tf_op jit(solution)/shard_map/ppermute | solution.py:348
  495.9 48.2 %collective-permute-start.32 = (bf16[512,2048]{1,0:T(8,128)(2,1)}, bf16[512,2048]{1,0:T(8,128)(2,1)}, u32[]{:S(2)}, u32[]{:S(2)}) collective-permute-start(bf16[512,2048]{1,0:T(8,128)(2,1)} %add_convert_fusion.6), channel_id=1, source_target_pairs={{0,8},{4,12},{8,0},{12,4},{16,24},{20,28},{24,16},{28,20},{1,9},{5... | collective-permute-start | bytes 6291464 | tf_op jit(solution)/shard_map/ppermute | solution.py:420
  496.9 47.9 %collective-permute-start.31 = (bf16[512,2048]{1,0:T(8,128)(2,1)}, bf16[512,2048]{1,0:T(8,128)(2,1)}, u32[]{:S(2)}, u32[]{:S(2)}) collective-permute-start(bf16[512,2048]{1,0:T(8,128)(2,1)} %add_convert_fusion.7), channel_id=1, source_target_pairs={{0,16},{4,20},{8,24},{12,28},{16,0},{20,4},{24,8},{28,12},{1,17},{... | collective-permute-start | bytes 6291464 | tf_op jit(solution)/shard_map/ppermute | solution.py:420
  549.9 43.7 %collective-permute-start.34 = (bf16[256,2048]{1,0:T(8,128)(2,1)}, bf16[256,2048]{1,0:T(8,128)(2,1)}, u32[]{:S(2)}, u32[]{:S(2)}) collective-permute-start(bf16[256,2048]{1,0:T(8,128)(2,1)} %slice.456), channel_id=1, source_target_pairs={{0,16},{4,20},{8,24},{12,28},{16,0},{20,4},{24,8},{28,12},{1,17},{... | collective-permute-start | bytes 3145736 | tf_op jit(solution)/shard_map/ppermute | solution.py:420
  552.5 42.7 %collective-permute-start.33 = (bf16[256,2048]{1,0:T(8,128)(2,1)}, bf16[256,2048]{1,0:T(8,128)(2,1)}, u32[]{:S(2)}, u32[]{:S(2)}) collective-permute-start(bf16[256,2048]{1,0:T(8,128)(2,1)} %slice.457), channel_id=1, source_target_pairs={{0,8},{4,12},{8,0},{12,4},{16,24},{20,28},{24,16},{28,20},{1,9},{5... | collective-permute-start | bytes 3145736 | tf_op jit(solution)/shard_map/ppermute | solution.py:420
  559.2 38.0 %collective-permute-start.36 = (bf16[512,2048]{1,0:T(8,128)(2,1)}, bf16[512,2048]{1,0:T(8,128)(2,1)}, u32[]{:S(2)}, u32[]{:S(2)}) collective-permute-start(bf16[512,2048]{1,0:T(8,128)(2,1)} %convolution_convert_fusion.6), channel_id=1, source_target_pairs={{0,4},{4,0},{8,12},{12,8},{16,20},{20,16},{24,28},{28,24},{1,5},{5... | collective-permute-start | bytes 6291464 | tf_op jit(solution)/shard_map/ppermute | solution.py:420
  567.1 30.1 %collective-permute-start.35 = (bf16[8,64,1024]{2,1,0:T(8,128)(2,1)S(1)}, bf16[8,64,1024]{2,1,0:T(8,128)(2,1)S(1)}, u32[]{:S(2)}, u32[]{:S(2)}) collective-permute-start(bf16[8,64,1024]{2,1,0:T(8,128)(2,1)S(1)} %get-tuple-element.279), channel_id=1, source_target_pairs={{0,1},{1,2},{2,3},{3,0},{4,5},{5,6},{6,7},{7,4},{8,9},{9,10},{10,1... | collective-permute-start | bytes 3145736 | tf_op jit(solution)/shard_map/ppermute | solution.py:348
  567.1 38.0 %collective-permute-start.37 = (bf16[512,2048]{1,0:T(8,128)(2,1)}, bf16[512,2048]{1,0:T(8,128)(2,1)}, u32[]{:S(2)}, u32[]{:S(2)}) collective-permute-start(bf16[512,2048]{1,0:T(8,128)(2,1)} %convolution_convert_fusion.5), channel_id=1, source_target_pairs={{0,4},{4,0},{8,12},{12,8},{16,20},{20,16},{24,28},{28,24},{1,5},{5... | collective-permute-start | bytes 6291464 | tf_op jit(solution)/shard_map/ppermute | solution.py:420
  623.1 34.4 %collective-permute-start.39 = (bf16[1024,2048]{1,0:T(8,128)(2,1)}, bf16[1024,2048]{1,0:T(8,128)(2,1)}, u32[]{:S(2)}, u32[]{:S(2)}) collective-permute-start(bf16[1024,2048]{1,0:T(8,128)(2,1)} %convolution_convert_fusion.2), channel_id=1, source_target_pairs={{0,4},{4,0},{8,12},{12,8},{16,20},{20,16},{24,28},{28,24},{1,5},{5... | collective-permute-start | bytes 12582920 | tf_op jit(solution)/shard_map/ppermute | solution.py:420
  629.8 27.7 %collective-permute-start.38 = (bf16[8,64,1024]{2,1,0:T(8,128)(2,1)}, bf16[8,64,1024]{2,1,0:T(8,128)(2,1)S(1)}, u32[]{:S(2)}, u32[]{:S(2)}) collective-permute-start(bf16[8,64,1024]{2,1,0:T(8,128)(2,1)} %get-tuple-element.278), channel_id=1, source_target_pairs={{0,3},{1,0},{2,1},{3,2},{4,7},{5,4},{6,5},{7,6},{8,11},{9,8},{10,9... | collective-permute-start | bytes 3145736 | tf_op jit(solution)/shard_map/ppermute | solution.py:348
  633.6 67.5 %collective-permute-start.42 = (bf16[8,64,1024]{2,1,0:T(8,128)(2,1)}, bf16[8,64,1024]{2,1,0:T(8,128)(2,1)S(1)}, u32[]{:S(2)}, u32[]{:S(2)}) collective-permute-start(bf16[8,64,1024]{2,1,0:T(8,128)(2,1)} %get-tuple-element.277), channel_id=1, source_target_pairs={{0,2},{1,3},{2,0},{3,1},{4,6},{5,7},{6,4},{7,5},{8,10},{9,11},{10,... | collective-permute-start | bytes 3145736 | tf_op jit(solution)/shard_map/ppermute | solution.py:348
  633.6 61.6 %collective-permute-start.40 = (bf16[512,2048]{1,0:T(8,128)(2,1)}, bf16[512,2048]{1,0:T(8,128)(2,1)S(1)}, u32[]{:S(2)}, u32[]{:S(2)}) collective-permute-start(bf16[512,2048]{1,0:T(8,128)(2,1)} %add_convert_fusion.5), channel_id=1, source_target_pairs={{0,16},{4,20},{8,24},{12,28},{16,0},{20,4},{24,8},{28,12},{1,17},{... | collective-permute-start | bytes 6291464 | tf_op jit(solution)/shard_map/ppermute | solution.py:420
  634.4 60.8 %collective-permute-start.41 = (bf16[512,2048]{1,0:T(8,128)(2,1)}, bf16[512,2048]{1,0:T(8,128)(2,1)S(1)}, u32[]{:S(2)}, u32[]{:S(2)}) collective-permute-start(bf16[512,2048]{1,0:T(8,128)(2,1)} %add_convert_fusion.4), channel_id=1, source_target_pairs={{0,8},{4,12},{8,0},{12,4},{16,24},{20,28},{24,16},{28,20},{1,9},{5... | collective-permute-start | bytes 6291464 | tf_op jit(solution)/shard_map/ppermute | solution.py:420
  705.5 36.4 %collective-permute-start.43 = (bf16[1024,2048]{1,0:T(8,128)(2,1)}, bf16[1024,2048]{1,0:T(8,128)(2,1)}, u32[]{:S(2)}, u32[]{:S(2)}) collective-permute-start(bf16[1024,2048]{1,0:T(8,128)(2,1)} %convolution_convert_fusion.1), channel_id=1, source_target_pairs={{0,4},{4,0},{8,12},{12,8},{16,20},{20,16},{24,28},{28,24},{1,5},{5... | collective-permute-start | bytes 12582920 | tf_op jit(solution)/shard_map/ppermute | solution.py:420
  711.7 25.9 %collective-permute-start.44 = (bf16[256,2048]{1,0:T(8,128)(2,1)}, bf16[256,2048]{1,0:T(8,128)(2,1)}, u32[]{:S(2)}, u32[]{:S(2)}) collective-permute-start(bf16[256,2048]{1,0:T(8,128)(2,1)} %get-tuple-element.215), channel_id=1, source_target_pairs={{0,16},{4,20},{8,24},{12,28},{16,0},{20,4},{24,8},{28,12},{1,17},{... | collective-permute-start | bytes 3145736 | tf_op jit(solution)/shard_map/ppermute | solution.py:420
  712.2 25.6 %collective-permute-start.45 = (bf16[256,2048]{1,0:T(8,128)(2,1)}, bf16[256,2048]{1,0:T(8,128)(2,1)}, u32[]{:S(2)}, u32[]{:S(2)}) collective-permute-start(bf16[256,2048]{1,0:T(8,128)(2,1)} %get-tuple-element.216), channel_id=1, source_target_pairs={{0,8},{4,12},{8,0},{12,4},{16,24},{20,28},{24,16},{28,20},{1,9},{5... | collective-permute-start | bytes 3145736 | tf_op jit(solution)/shard_map/ppermute | solution.py:420
  719.9 29.2 %collective-permute-start.46 = (bf16[256,2048]{1,0:T(8,128)(2,1)}, bf16[256,2048]{1,0:T(8,128)(2,1)}, u32[]{:S(2)}, u32[]{:S(2)}) collective-permute-start(bf16[256,2048]{1,0:T(8,128)(2,1)} %get-tuple-element.271), channel_id=1, source_target_pairs={{0,1},{1,2},{2,3},{3,0},{4,5},{5,6},{6,7},{7,4},{8,9},{9,10},{10,1... | collective-permute-start | bytes 3145736 | tf_op jit(solution)/shard_map/ppermute | solution.py:348
  722.3 45.3 %collective-permute-start.50 = (bf16[2,256,256]{2,1,0:T(8,128)(2,1)}, bf16[2,256,256]{2,1,0:T(8,128)(2,1)S(1)}, u32[]{:S(2)}, u32[]{:S(2)}) collective-permute-start(bf16[2,256,256]{2,1,0:T(8,128)(2,1)} %get-tuple-element.300), channel_id=1, source_target_pairs={{0,1},{1,2},{2,3},{3,0},{4,5},{5,6},{6,7},{7,4},{8,9},{9,10},{10,1... | collective-permute-start | bytes 786440 | tf_op jit(solution)/shard_map/ppermute | solution.py:348
  737.7 29.9 %collective-permute-start.51 = (bf16[2,256,256]{2,1,0:T(8,128)(2,1)}, bf16[2,256,256]{2,1,0:T(8,128)(2,1)S(1)}, u32[]{:S(2)}, u32[]{:S(2)}) collective-permute-start(bf16[2,256,256]{2,1,0:T(8,128)(2,1)} %get-tuple-element.299), channel_id=1, source_target_pairs={{0,2},{1,3},{2,0},{3,1},{4,6},{5,7},{6,4},{7,5},{8,10},{9,11},{10,... | collective-permute-start | bytes 786440 | tf_op jit(solution)/shard_map/ppermute | solution.py:348
  737.8 29.9 %collective-permute-start.52 = (bf16[2,256,256]{2,1,0:T(8,128)(2,1)S(1)}, bf16[2,256,256]{2,1,0:T(8,128)(2,1)S(1)}, u32[]{:S(2)}, u32[]{:S(2)}) collective-permute-start(bf16[2,256,256]{2,1,0:T(8,128)(2,1)S(1)} %get-tuple-element.298), channel_id=1, source_target_pairs={{0,3},{1,0},{2,1},{3,2},{4,7},{5,4},{6,5},{7,6},{8,11},{9,8},{10,9... | collective-permute-start | bytes 786440 | tf_op jit(solution)/shard_map/ppermute | solution.py:348
  767.5 145.6 %collective-permute-start.47 = (bf16[1024,2048]{1,0:T(8,128)(2,1)}, bf16[1024,2048]{1,0:T(8,128)(2,1)}, u32[]{:S(2)}, u32[]{:S(2)}) collective-permute-start(bf16[1024,2048]{1,0:T(8,128)(2,1)} %convolution_convert_fusion.3), channel_id=1, source_target_pairs={{0,4},{4,0},{8,12},{12,8},{16,20},{20,16},{24,28},{28,24},{1,5},{5... | collective-permute-start | bytes 12582920 | tf_op jit(solution)/shard_map/ppermute | solution.py:420
  767.6 45.7 %collective-permute-start.56 = (bf16[256,2048]{1,0:T(8,128)(2,1)}, bf16[256,2048]{1,0:T(8,128)(2,1)}, u32[]{:S(2)}, u32[]{:S(2)}) collective-permute-start(bf16[256,2048]{1,0:T(8,128)(2,1)} %get-tuple-element.273), channel_id=1, source_target_pairs={{0,8},{4,12},{8,0},{12,4},{16,24},{20,28},{24,16},{28,20},{1,9},{5... | collective-permute-start | bytes 3145736 | tf_op jit(solution)/shard_map/ppermute | solution.py:420
  768.6 46.3 %collective-permute-start.54 = (bf16[256,2048]{1,0:T(8,128)(2,1)}, bf16[256,2048]{1,0:T(8,128)(2,1)}, u32[]{:S(2)}, u32[]{:S(2)}) collective-permute-start(bf16[256,2048]{1,0:T(8,128)(2,1)} %get-tuple-element.272), channel_id=1, source_target_pairs={{0,16},{4,20},{8,24},{12,28},{16,0},{20,4},{24,8},{28,12},{1,17},{... | collective-permute-start | bytes 3145736 | tf_op jit(solution)/shard_map/ppermute | solution.py:420
  772.9 33.3 %collective-permute-start.70 = (bf16[128,2048]{1,0:T(8,128)(2,1)}, bf16[128,2048]{1,0:T(8,128)(2,1)}, u32[]{:S(2)}, u32[]{:S(2)}) collective-permute-start(bf16[128,2048]{1,0:T(8,128)(2,1)} %slice.458), channel_id=1, source_target_pairs={{0,16},{4,20},{8,24},{12,28},{16,0},{20,4},{24,8},{28,12},{1,17},{... | collective-permute-start | bytes 1572872 | tf_op jit(solution)/shard_map/ppermute | solution.py:420
  777.3 30.0 %collective-permute-start.69 = (bf16[128,2048]{1,0:T(8,128)(2,1)}, bf16[128,2048]{1,0:T(8,128)(2,1)}, u32[]{:S(2)}, u32[]{:S(2)}) collective-permute-start(bf16[128,2048]{1,0:T(8,128)(2,1)} %slice.459), channel_id=1, source_target_pairs={{0,8},{4,12},{8,0},{12,4},{16,24},{20,28},{24,16},{28,20},{1,9},{5... | collective-permute-start | bytes 1572872 | tf_op jit(solution)/shard_map/ppermute | solution.py:420
  780.3 85.6 %all-to-all-start.1 = ((bf16[8,64,1024]{2,1,0:T(8,128)(2,1)}), bf16[8,64,1024]{2,1,0:T(8,128)(2,1)S(1)}, u32[]{:S(2)}, u32[]{:S(2)}) async-start(bf16[8,64,1024]{2,1,0:T(8,128)(2,1)} %add_convert_fusion.10), calls=%async_computation.1 | async-start | bytes 2097152 | tf_op jit(solution)/shard_map/all_to_all | solution.py:710
  811.0 26.0 %collective-permute-start.72 = (bf16[64,2048]{1,0:T(8,128)(2,1)S(1)}, bf16[64,2048]{1,0:T(8,128)(2,1)S(1)}, u32[]{:S(2)}, u32[]{:S(2)}) collective-permute-start(bf16[64,2048]{1,0:T(8,128)(2,1)S(1)} %get-tuple-element.290), channel_id=1, source_target_pairs={{0,2},{1,3},{2,0},{3,1},{4,6},{5,7},{6,4},{7,5},{8,10},{9,11},{10,... | collective-permute-start | bytes 786440 | tf_op jit(solution)/shard_map/ppermute | solution.py:348
  813.3 25.4 %collective-permute-start.71 = (bf16[64,2048]{1,0:T(8,128)(2,1)S(1)}, bf16[64,2048]{1,0:T(8,128)(2,1)S(1)}, u32[]{:S(2)}, u32[]{:S(2)}) collective-permute-start(bf16[64,2048]{1,0:T(8,128)(2,1)S(1)} %get-tuple-element.288), channel_id=1, source_target_pairs={{0,1},{1,2},{2,3},{3,0},{4,5},{5,6},{6,7},{7,4},{8,9},{9,10},{10,1... | collective-permute-start | bytes 786440 | tf_op jit(solution)/shard_map/ppermute | solution.py:348
  815.0 24.6 %collective-permute-start.57 = (bf16[128,2048]{1,0:T(8,128)(2,1)S(1)}, bf16[128,2048]{1,0:T(8,128)(2,1)S(1)}, u32[]{:S(2)}, u32[]{:S(2)}) collective-permute-start(bf16[128,2048]{1,0:T(8,128)(2,1)S(1)} %slice.460), channel_id=1, source_target_pairs={{0,16},{4,20},{8,24},{12,28},{16,0},{20,4},{24,8},{28,12},{1,17},{... | collective-permute-start | bytes 1572872 | tf_op jit(solution)/shard_map/ppermute | solution.py:420
  818.1 104.9 %collective-permute-start.53 = (bf16[256,2048]{1,0:T(8,128)(2,1)}, bf16[256,2048]{1,0:T(8,128)(2,1)}, u32[]{:S(2)}, u32[]{:S(2)}) collective-permute-start(bf16[256,2048]{1,0:T(8,128)(2,1)} %get-tuple-element.270), channel_id=1, source_target_pairs={{0,3},{1,0},{2,1},{3,2},{4,7},{5,4},{6,5},{7,6},{8,11},{9,8},{10,9... | collective-permute-start | bytes 3145736 | tf_op jit(solution)/shard_map/ppermute | solution.py:348
  847.5 25.0 %collective-permute-start.60 = (bf16[64,2048]{1,0:T(8,128)(2,1)}, bf16[64,2048]{1,0:T(8,128)(2,1)}, u32[]{:S(2)}, u32[]{:S(2)}) collective-permute-start(bf16[64,2048]{1,0:T(8,128)(2,1)} %get-tuple-element.292), channel_id=1, source_target_pairs={{0,3},{1,0},{2,1},{3,2},{4,7},{5,4},{6,5},{7,6},{8,11},{9,8},{10,9... | collective-permute-start | bytes 786440 | tf_op jit(solution)/shard_map/ppermute | solution.py:348
  865.4 45.5 %collective-permute-start.59 = (bf16[64,2048]{1,0:T(8,128)(2,1)}, bf16[64,2048]{1,0:T(8,128)(2,1)}, u32[]{:S(2)}, u32[]{:S(2)}) collective-permute-start(bf16[64,2048]{1,0:T(8,128)(2,1)} %get-tuple-element.293), channel_id=1, source_target_pairs={{0,2},{1,3},{2,0},{3,1},{4,6},{5,7},{6,4},{7,5},{8,10},{9,11},{10,... | collective-permute-start | bytes 786440 | tf_op jit(solution)/shard_map/ppermute | solution.py:348
  865.4 45.5 %collective-permute-start.58 = (bf16[64,2048]{1,0:T(8,128)(2,1)}, bf16[64,2048]{1,0:T(8,128)(2,1)}, u32[]{:S(2)}, u32[]{:S(2)}) collective-permute-start(bf16[64,2048]{1,0:T(8,128)(2,1)} %get-tuple-element.291), channel_id=1, source_target_pairs={{0,1},{1,2},{2,3},{3,0},{4,5},{5,6},{6,7},{7,4},{8,9},{9,10},{10,1... | collective-permute-start | bytes 786440 | tf_op jit(solution)/shard_map/ppermute | solution.py:348
  872.5 88.2 %collective-permute-start.74 = (bf16[256,2048]{1,0:T(8,128)(2,1)}, bf16[256,2048]{1,0:T(8,128)(2,1)}, u32[]{:S(2)}, u32[]{:S(2)}) collective-permute-start(bf16[256,2048]{1,0:T(8,128)(2,1)} %get-tuple-element.269), channel_id=1, source_target_pairs={{0,2},{1,3},{2,0},{3,1},{4,6},{5,7},{6,4},{7,5},{8,10},{9,11},{10,... | collective-permute-start | bytes 3145736 | tf_op jit(solution)/shard_map/ppermute | solution.py:348
  926.7 43.0 %collective-permute-start.49 = (bf16[256,2048]{1,0:T(8,128)(2,1)}, bf16[256,2048]{1,0:T(8,128)(2,1)}, u32[]{:S(2)}, u32[]{:S(2)}) collective-permute-start(bf16[256,2048]{1,0:T(8,128)(2,1)} %slice.454), channel_id=1, source_target_pairs={{0,16},{4,20},{8,24},{12,28},{16,0},{20,4},{24,8},{28,12},{1,17},{... | collective-permute-start | bytes 3145736 | tf_op jit(solution)/shard_map/ppermute | solution.py:420
  929.4 42.8 %collective-permute-start.48 = (bf16[256,2048]{1,0:T(8,128)(2,1)}, bf16[256,2048]{1,0:T(8,128)(2,1)}, u32[]{:S(2)}, u32[]{:S(2)}) collective-permute-start(bf16[256,2048]{1,0:T(8,128)(2,1)} %slice.455), channel_id=1, source_target_pairs={{0,8},{4,12},{8,0},{12,4},{16,24},{20,28},{24,16},{28,20},{1,9},{5... | collective-permute-start | bytes 3145736 | tf_op jit(solution)/shard_map/ppermute | solution.py:420
  (103 other events, 1409.4 us)
Sparse Core Ops, SparseCore 0:
  17.7 35.3 all-gather.3
  58.4 63.5 all-gather.5
  128.2 78.8 all-gather.7

commit v6 on v5

--- a/solution.py
+++ b/solution.py
@@ -321,6 +321,114 @@
         cost_estimate=pl.CostEstimate(flops=0, transcendentals=0, bytes_accessed=4 * rows * width // HASTE),
     )(places, values, values)
 
+def fill_lots(place_ref, values_ref, outs):
+    for core, out in enumerate(outs):
+        for i in range(out.shape[1] // HD):
+            at = pl.multiple_of(place_ref[core, i] * HD, HD)
+            out[:, i * HD : (i + 1) * HD] = values_ref[:, pl.ds(at, HD)]
+
+
+def lots_product_kernel(turn, place_ref, *refs):
+    if turn:
+        values_ref, bias_ref, *weights = refs[:-3]
+        out, mine, sib = refs[-3:]
+
+        @pl.when(pl.program_id(0) == 0)
+        def _():
+            fill_lots(place_ref, values_ref, (mine, sib))
+
+    else:
+        mine, sib, bias_ref, *weights = refs[:-1]
+        out = refs[-1]
+    each = len(weights) // 2
+    depth = weights[0].shape[0]
+    total = bias_ref[...].astype(F32)
+    for i, weight in enumerate(weights):
+        values = (mine, sib)[i // each]
+        at = i % each * depth
+        total = total + dot_nn(values[:, at : at + depth], weight[...])
+    out[...] = total.astype(out.dtype)
+
+
+def lots_product(values, places, weights, bias, kind, tile=512):
+    rows, width = values.shape
+    depth, breadth = weights[0].shape
+    tile = min(tile, breadth)
+    one = pl.Buffered(buffer_count=1)
+    turn = width // (2 * places.shape[1]) == HD
+    lot = pl.BlockSpec((rows, width // 2), lambda j, place: (0, 0), pipeline_mode=one)
+    lot_out = pl.BlockSpec((rows, width // 2), lambda j, place: (0, 0))
+    slab = pl.BlockSpec((rows, tile), lambda j, place: (0, j))
+    if turn:
+        given, specs = [values], [pl.BlockSpec((rows, width), lambda j, place: (0, 0), pipeline_mode=one)]
+    else:
+        given, specs = reorder(values, places), [lot, lot]
+    lots = [jax.ShapeDtypeStruct((rows, width // 2), values.dtype)] * 2
+    out = pl.pallas_call(
+        functools.partial(lots_product_kernel, turn),
+        out_shape=[jax.ShapeDtypeStruct((rows, breadth), kind)] + (lots if turn else []),
+        grid_spec=pltpu.PrefetchScalarGridSpec(
+            num_scalar_prefetch=1,
+            grid=(breadth // tile,),
+            in_specs=specs
+            + [pl.BlockSpec((1, tile), lambda j, place: (0, j))]
+            + [pl.BlockSpec((depth, tile), lambda j, place: (0, j))] * len(weights),
+            out_specs=[slab] + ([lot_out, lot_out] if turn else []),
+        ),
+        compiler_params=pltpu.CompilerParams(vmem_limit_bytes=48 * 2**20),
+        cost_estimate=pl.CostEstimate(
+            flops=2 * rows * width * breadth // HASTE,
+            transcendentals=0,
+            bytes_accessed=2 * (rows * (2 * width + breadth) + width * breadth) // HASTE,
+        ),
+    )(places, *given, bias.reshape(1, breadth), *weights)
+    return (out[0], out[1], out[2]) if turn else (out[0], *given)
+
+
+def lots_turned_kernel(place_ref, values_ref, *refs):
+    weights, out = refs[:-1], refs[-1]
+    each = len(weights) // 2
+    blocks = weights[0].shape[0] // HD
+    for i, weight in enumerate(weights):
+        part = dot_nt(values_ref[...], weight[...]).astype(out.dtype)
+        for j in range(blocks):
+            at = pl.multiple_of(place_ref[i // each, i % each * blocks + j] * HD, HD)
+            out[:, pl.ds(at, HD)] = part[:, j * HD : (j + 1) * HD]
+
+
+def lots_turned(values, places, weights, kind):
+    rows, depth = values.shape
+    height = weights[0].shape[0]
+    width = height * len(weights)
+    block = width // (2 * places.shape[1])
+    if block != HD:
+        out = jnp.zeros((rows, width), kind)
+        each, blocks = len(weights) // 2, height // block
+        for i, weight in enumerate(weights):
+            part = dot_nt(values, weight).astype(kind)
+            for j in range(blocks):
+                place = places[i // each, i % each * blocks + j] * block
+                out = lax.dynamic_update_slice_in_dim(out, part[:, j * block : (j + 1) * block], place, 1)
+        return out
+    one = pl.Buffered(buffer_count=1)
+    return pl.pallas_call(
+        lots_turned_kernel,
+        out_shape=jax.ShapeDtypeStruct((rows, width), kind),
+        grid_spec=pltpu.PrefetchScalarGridSpec(
+            num_scalar_prefetch=1,
+            grid=(1,),
+            in_specs=[pl.BlockSpec((rows, depth), lambda j, place: (0, 0), pipeline_mode=one)]
+            + [pl.BlockSpec((height, depth), lambda j, place: (0, 0), pipeline_mode=one)] * len(weights),
+            out_specs=pl.BlockSpec((rows, width), lambda j, place: (0, 0), pipeline_mode=one),
+        ),
+        compiler_params=pltpu.CompilerParams(vmem_limit_bytes=48 * 2**20),
+        cost_estimate=pl.CostEstimate(
+            flops=2 * rows * width * depth // HASTE,
+            transcendentals=0,
+            bytes_accessed=2 * (rows * (depth + width) + width * depth) // HASTE,
+        ),
+    )(places, values, *weights)
+
 
 def norm_stats(values):
     average = jnp.mean(values, axis=-1, keepdims=True)
@@ -349,10 +457,6 @@
 
     def gather(self, block):
         return [block] + [self.send(block, step) for step in range(1, self.count)]
-
-    def more(self, pieces, steps, block):
-        for step in steps:
-            pieces[step] = self.send(block, step)
 
     def in_order(self, pieces, axis=0):
         me = lax.axis_index("fsdp")
@@ -373,19 +477,6 @@
             return lax.dynamic_index_in_dim(terms, place, axis, keepdims=False)
 
         return [term(0)] + [self.send(term(step).astype(BF16), step) for step in range(1, self.count)]
-
-
-def thirds(count):
-    steps = sorted(range(1, count), key=lambda step: min(step, count - step))
-    lot = -(-len(steps) // 3)
-    return steps[:lot], steps[lot : 2 * lot], steps[2 * lot :]
-
-
-def meet(pieces, steps, *arrays):
-    out = tie(*arrays, *[pieces[step] for step in steps])
-    for step, piece in zip(steps, out[len(arrays) :]):
-        pieces[step] = piece
-    return out[: len(arrays)]
 
 
 def total(terms):
@@ -416,6 +507,15 @@
             [jnp.stack([2 * (me ^ o ^ core) + h for o, h in order]) for core in (0, 1)]
         ).astype(jnp.int32)
 
+    def lots(self, block, apart):
+        size = block.shape[0] // 2
+        near = self.grow([block[:size], block[size:]])
+        near = list(apart(near))
+        far = self.across(near, self.last)
+        mine = [far[0], near[0], far[1], near[1]]
+        near_sib, far_sib = self.cross(near), self.cross(far)
+        return mine + [far_sib[0], near_sib[0], far_sib[1], near_sib[1]]
+
     def swap(self, block, bit):
         return lax.ppermute(block, "dp", [(i, i ^ bit) for i in range(self.count)])
 
@@ -442,7 +542,6 @@
     n_dev = n_dp * n_z
     plane = Plane(n_dp)
     line = Line(n_z)
-    soon, later, last = thirds(n_z)
 
     def local(
         tokens,
@@ -488,38 +587,30 @@
             [jnp.pad(v, (0, room - size)) for v, size, room in zip(small, sizes, rooms)]
         )
         kv_lines = kv_weight.size // width
-        filled = own + kv_lines + -(-small_row.shape[0] // width)
-        lines = -(-filled // 16) * 16
-        spare = (lines - own - kv_lines) * width
-        small_row = jnp.pad(small_row, (0, spare - small_row.shape[0]))
-        packed = jnp.concatenate(
-            [query_weight, kv_weight.reshape(kv_lines, width), small_row.reshape(-1, width)]
-        )
-
+        lines = -(-(kv_lines + -(-small_row.shape[0] // width)) // 16) * 16
+        small_row = jnp.pad(small_row, (0, (lines - kv_lines) * width - small_row.shape[0]))
+        places = plane.places()
+
+        query_own = lax.all_gather(query_weight, "fsdp", axis=0, tiled=True)
         grad_low = cotangent.reshape(rows, width)
-        packed = lax.all_gather(packed, "fsdp", axis=0, tiled=True)
         grad_near = plane.grow([grad_low[:half], grad_low[half:]])
+        packed = jnp.concatenate([kv_weight.reshape(kv_lines, width), small_row.reshape(-1, width)])
+        packed_pieces = line.gather(packed)
         up_cols = lax.all_to_all(up_weight, "dp", 1, 0, tiled=True).reshape(n_dp, own, ff_own)
-        packed, up_cols, out_weight, *grad_near = tie(packed, up_cols, out_weight, *grad_near)
-
-        packed = lax.all_gather(packed, "dp", axis=0, tiled=True)
+        query_own, up_cols, out_weight, grad_near[0], grad_near[1], *packed_pieces = tie(
+            query_own, up_cols, out_weight, *grad_near, *packed_pieces
+        )
+
+        packed = lax.all_gather(line.in_order(packed_pieces), "dp", axis=0, tiled=True)
         out_pieces = line.gather(out_weight)
-        *out_pieces, down_late = tie(*out_pieces, down_weight)
-        full_o = line.in_order(out_pieces)
-        down_pieces = [down_weight] + [None] * (n_z - 1)
-        line.more(down_pieces, last, down_late)
         inputs = tokens.reshape(rows, width).astype(F32)
         mean_one, recip_one = norm_stats(inputs)
-        packed, full_o, mean_one, grad_near[0], grad_near[1] = meet(
-            down_pieces, last, packed, full_o, mean_one, *grad_near
-        )
-
-        full_o = lax.all_gather(full_o, "dp", axis=0, tiled=True)
-        grad_far = plane.across(grad_near, plane.last)
+        query_lots = plane.lots(query_own, lambda near: near)
+        packed, mean_one, down_late = tie(packed, mean_one, down_weight)
+        down_part = lax.all_gather(down_late, "fsdp", axis=0, tiled=True)
         packed = packed.reshape(n_dev, lines, width)
-        full_q = packed[:, :own].reshape(width, width)
-        full_kv = packed[:, own : own + kv_lines].reshape(width, 2 * HD)
-        small_all = packed[:, own + kv_lines :].reshape(n_dev, -1)
+        full_kv = packed[:, :kv_lines].reshape(width, 2 * HD)
+        small_all = packed[:, kv_lines:].reshape(n_dev, -1)
         bias_q, bias_v, bias_o, gain_one, shift_one, bias_up, bias_down, gain_two, shift_two = (
             small_all[:, start : start + size].reshape(-1).astype(F32)
             for start, size in zip(starts, sizes)
@@ -528,46 +619,47 @@
         normed_one = (xhat_one * gain_one + shift_one).astype(BF16)
         kv_bias = jnp.concatenate([jnp.zeros((HD,), F32), bias_v])
         key_value = (dot_nn(normed_one, full_kv) + kv_bias).astype(BF16)
-        key_value, normed_late = tie(key_value, normed_one)
+        key_value, normed_late, up_cols = tie(key_value, normed_one, up_cols)
+        up_part = lax.all_gather(up_cols, "fsdp", axis=1, tiled=True).reshape(width, ff_own)
         kv_pieces = line.gather(key_value.reshape(windows, local_len, 2 * HD))
-        queries = (dot_nn(normed_late, full_q) + bias_q).astype(BF16)
+        normed_late, out_pieces[0], *query_lots = tie(normed_late, out_pieces[0], *query_lots)
+        queries, one_mine, one_sib = lots_product(normed_late, places, query_lots, bias_q, BF16)
         kv_window = line.in_order(kv_pieces, 1)
 
         first = (lax.axis_index("fsdp") * local_len).astype(jnp.int32).reshape(1)
         file_count = lengths.shape[1]
         upto = jnp.arange(file_count)[:, None] <= jnp.arange(file_count)[None, :]
         file_ends = jnp.sum(jnp.where(upto[None], lengths[:, :, None], 0), axis=1)
-        queries, kv_window, down_late = tie(queries, kv_window, down_late)
-        line.more(down_pieces, soon + later, down_late)
+        held = {}
+
+        def before_attention(near):
+            held["queries"], held["keys"], *near = tie(queries, kv_window, *near)
+            return near
+
+        out_lots = plane.lots(line.in_order(out_pieces), before_attention)
+        queries, kv_window = held["queries"], held["keys"]
         attended, norms = attn_forward(queries, kv_window, first, file_ends)
-        attended, up_cols = meet(down_pieces, soon + later, attended, up_cols)
-        up_pieces = [up_cols] + [None] * (n_z - 1)
-        line.more(up_pieces, soon + later, up_cols)
-        down_part = line.in_order(down_pieces)
-        grad_lots = [[*grad_near, *plane.cross(grad_near)]]
-        back_near = back_product(grad_lots[0], down_part)
-        grad_far = list(grad_far)
-        grad_lots.append([*grad_far, *plane.cross(grad_far)])
-        attended, back_near, *grad_lots[1] = meet(up_pieces, soon, attended, back_near, *grad_lots[1])
-        line.more(up_pieces, last, up_cols)
-        middle = inputs + dot_nn(attended, full_o) + bias_o
+        attended, grad_near[0], grad_near[1], *out_lots = tie(attended, *grad_near, *out_lots)
+        grad_far = plane.across(grad_near, plane.last)
+        branch, att_mine, att_sib = lots_product(attended, places, out_lots, bias_o, F32)
+        middle = inputs + branch
         mean_two, recip_two = norm_stats(middle)
         xhat_two = (middle - mean_two) * recip_two
         normed_two = (xhat_two * gain_two + shift_two).astype(BF16)
 
-        normed_two, down_part = tie(normed_two, down_part)
+        normed_two, *grad_near = tie(normed_two, *grad_near)
+        two_near = plane.grow([normed_two[:half], normed_two[half:]])
+        two_near[0], two_near[1], *grad_far = tie(*two_near, *grad_far)
+        two_far = plane.across(two_near, plane.last)
+        grad_lots = [[*halves, *plane.cross(halves)] for halves in (grad_near, grad_far)]
+        two_lots = [[*two_near, *plane.cross(two_near)]]
+        back_near = back_product(grad_lots[0], down_part)
         back_far = back_product(grad_lots[1], down_part)
-        two_near = list(meet(up_pieces, later, *plane.grow([normed_two[:half], normed_two[half:]])))
-
-        two_far = plane.across(two_near, plane.last)
-        two_lots = [[*two_near, *plane.cross(two_near)], [*two_far, *plane.cross(two_far)]]
-        up_part = line.in_order(up_pieces, 1).reshape(width, ff_own)
         bias_up_part = lax.dynamic_slice_in_dim(bias_up, my_dp * ff_own, ff_own)
+        back_near, back_far = tie(back_near, back_far)
         hid_near, pre_near = middle_layer(two_lots[0], back_near, up_part, bias_up_part)
-        places = plane.places()
-        back_far, attended, pre_near[0], pre_near[1], places = tie(
-            back_far, attended, *pre_near, places
-        )
+        two_lots.append([*two_far, *plane.cross(two_far)])
+        back_far, pre_near[0], pre_near[1] = tie(back_far, *pre_near)
         hid_far, pre_far = middle_layer(two_lots[1], back_far, up_part, bias_up_part)
         block = two_near[0].shape[0]
         lots = (slice(None, block), slice(block, None))
@@ -591,12 +683,14 @@
         up_terms = weight_grad(two_lots[0] + two_lots[1], pre_near + pre_far, block)
         pre_near[0], up_terms = tie(pre_near[0], up_terms)
         two_sum = ours(pre_near, up_part, dot_nt, theirs, got)
-        up_got = line.scatter(up_terms.reshape(n_dp, n_z, own, ff_own), 1)
+        grad_up = lax.psum_scatter(
+            up_terms.reshape(n_dp, n_z * own, ff_own), "fsdp", scatter_dimension=1, tiled=True
+        )
         hid_far[0], hid_far[1], *two_sum = tie(*hid_far, *two_sum)
         two_grad = plane.fold(two_sum)
         down_terms = weight_grad(hid_near + hid_far, grad_lots[0] + grad_lots[1], block)
-        two_grad, down_terms, hid_far[0] = meet(up_got, soon, two_grad, down_terms, hid_far[0])
-        down_got = line.scatter(down_terms.reshape(n_z, ff_own // n_z, width), 0)
+        two_grad, down_terms, hid_far[0] = tie(two_grad, down_terms, hid_far[0])
+        grad_down = lax.psum_scatter(down_terms, "fsdp", scatter_dimension=0, tiled=True)
         out_far = halves(hid_far, down_part, dot_nn)
         two_grad, *out_far = tie(two_grad, *out_far)
 
@@ -608,8 +702,6 @@
         middle_grad = grad_out + norm_pull(two_grad, xhat_two, recip_two, gain_two)
         grad_bo = jnp.sum(middle_grad, axis=0)
         branch_grad = middle_grad.astype(BF16)
-        att_mine, att_sib = reorder(attended, places)
-        one_mine, one_sib = reorder(normed_one, places)
 
         def cut(rows_of_lots):
             size = rows_of_lots.shape[0] // 4
@@ -625,8 +717,8 @@
             return plane.fold([n.astype(F32) + g.astype(F32) for n, g in zip((parts[1], parts[3]), got)])
 
         theirs = plane.swap(dot_tn(att_sib, branch_grad).astype(BF16), 1)
-        attended_grad = dot_nt(branch_grad, full_o).astype(BF16)
-        attended_grad, branch_late = meet(up_got, later, attended_grad, branch_grad)
+        attended_grad = lots_turned(branch_grad, places, out_lots, BF16)
+        attended_grad, branch_late = tie(attended_grad, branch_grad)
         wo_parts = cut(plus(att_mine, branch_late, theirs))
         attended_grad, *wo_parts = tie(attended_grad, *wo_parts)
         wo_got = send_rows(wo_parts)
@@ -634,21 +726,16 @@
         query_grad, kv_terms = attn_backward(queries, kv_window, norms, attended_grad, first, file_ends)
         query_grad, kv_terms, *out_got = tie(query_grad, kv_terms, *out_got)
         kv_got = line.scatter(kv_terms.reshape(windows, n_z, local_len, 2 * HD), 1)
-        (query_grad,) = meet(up_got, last, query_grad)
         theirs = plane.swap(dot_tn(one_sib, query_grad).astype(BF16), 1)
         theirs, *wo_got = tie(theirs, *wo_got)
         wq_parts = cut(plus(one_mine, query_grad, theirs))
         wq_got = send_rows(wq_parts)
-        wq_parts[1], query_late, hid_late = meet(down_got, soon, wq_parts[1], query_grad, hid_near[1])
+        wq_parts[1], query_late, hid_late = tie(wq_parts[1], query_grad, hid_near[1])
         wq_parts[1], *kv_got = tie(wq_parts[1], *kv_got)
-        wq_parts[3], *up_got = tie(wq_parts[3], *up_got)
-        theirs = plane.swap(dot_nn(hid_late, down_part).astype(BF16), 1)
-        query_part = dot_nt(query_late, full_q)
-        query_part, hid_near[0], theirs = tie(query_part, hid_near[0], theirs)
-        out_sum = ours(hid_near, down_part, dot_nn, theirs, out_got)
-        query_part, *out_sum = tie(query_part, *out_sum)
+        query_part = lots_turned(query_late, places, query_lots, F32)
         kv_grad = total(kv_got).astype(BF16).reshape(rows, 2 * HD)
-        query_part, kv_grad = meet(down_got, later, query_part, kv_grad)
+        wo_rows = own_rows(wo_parts, wo_got)
+        query_part, kv_grad, wo_rows = tie(query_part, kv_grad, wo_rows)
 
         one_grad = query_part + dot_nt(kv_grad, full_kv)
         grad_bq = jnp.sum(query_late.astype(F32), axis=0)
@@ -690,10 +777,12 @@
         theirs = plane.swap(with_vectors(dot_tn(one_sib, kv_grad), 1).astype(BF16), 1)
         kv_parts = cut((with_vectors(dot_tn(one_mine, kv_grad), 0) + theirs.astype(F32)).astype(BF16))
         kv_parts_got = send_rows(kv_parts)
-        query_part, *kv_parts = tie(query_part, *kv_parts)
-
-        wo_last = line.scatter(own_rows(wo_parts, wo_got).reshape(n_z, own, width), 0)
+        kv_parts[1], hid_late, hid_near[0], *wq_got = tie(kv_parts[1], hid_late, hid_near[0], *wq_got)
+        theirs = plane.swap(dot_nn(hid_late, down_part).astype(BF16), 1)
+
+        wo_last = line.scatter(wo_rows.reshape(n_z, own, width), 0)
         wq_last = line.scatter(own_rows(wq_parts, wq_got).reshape(n_z, own, width), 0)
+        kv_parts_got[0], grad_up, grad_down = tie(kv_parts_got[0], grad_up, grad_down)
         kv_last = own_rows(kv_parts, kv_parts_got).reshape(2, -1, 2 * HD)
         kv_rows = kv_last.shape[1] - more
         kv_last = jnp.concatenate(
@@ -704,11 +793,12 @@
             axis=1,
         )
         kv_last = line.scatter(kv_last, 0)
+        out_sum = ours(hid_near, down_part, dot_nn, theirs, out_got)
         output = (middle + plane.fold(out_sum) + bias_down).astype(BF16).reshape(windows, local_len, width)
         tokens_grad = middle_grad + norm_pull(one_grad, xhat_one, recip_one, gain_one)
         tokens_grad = tokens_grad.astype(BF16).reshape(windows, local_len, width)
         grad_up = lax.all_to_all(
-            total(up_got).astype(BF16).reshape(n_dp * own, ff_own), "dp", 0, 1, tiled=True
+            grad_up.reshape(n_dp * own, ff_own), "dp", 0, 1, tiled=True
         ).astype(F32)
         kv_own = total(kv_last)
         flat = kv_own[own * 2 * HD :]
@@ -727,7 +817,7 @@
             gain1,
             shift1,
             grad_up,
-            total(down_got),
+            grad_down.astype(F32),
             bup,
             bdown,
             gain2,

time: 993 us -> 930 us (0.937)
  matrix products: 133 us -> 84.6 us
  waiting for transfers between devices: 354 us -> 324 us
  Pallas kernels: 182 us -> 209 us
  starting transfers between devices: 131 us -> 115 us
  other arithmetic: 77.7 us -> 90.7 us
    ppermute x30 -> x21, waiting for transfers between devices: 178 us -> 96.7 us  [send(): lax.ppermute(block, 'fsdp', [(i, (i + places) % self.count) for i in rang...]
    ppermute x45 -> x61, waiting for transfers between devices: 169 us -> 222 us  [swap(): return lax.ppermute(block, 'dp', [(i, i ^ bit) for i in range(self.count)])]
    dot_general x9 -> x7, matrix products: 61.1 us -> 32.1 us  [dot_nn(): return jnp.dot(left, right, preferred_element_type=F32)]
    pallas_call x2 -> x4, Pallas kernels: 13.1 us -> 41.7 us  [the longest x2 21.8 us: lots_turned(): pl.pallas_call(lots_turned_kernel, out_shape=jax.ShapeDtypeStruct((rows,...]
    ppermute x30 -> x21, starting transfers between devices: 86 us -> 60.2 us  [send(): lax.ppermute(block, 'fsdp', [(i, (i + places) % self.count) for i in rang...]
    dot_general x9 -> x7, matrix products: 50 us -> 32.8 us  [dot_nt(): lax.dot_general(left, right, (((1,), (1,)), ((), ())), preferred_element_...]
    unnamed x196 -> x235, local copies, waits for them, and re-layouts: 16.8 us -> 29.2 us
    dynamic_update_slice x16 -> x12, local copies, waits for them, and re-layouts: 19.3 us -> 6.94 us  [in_order(): whole = lax.dynamic_update_slice_in_dim(whole, piece, place, axis)]
  transfers between devices with their start and end apart: 80 -> 90, of which waited for: 32 -> 26; matrix products, arithmetic and copies ran while one was open for 23% -> 20% of each run, Pallas kernels for 16% -> 21%
where the time goes in v6:
time: 930 us; the launch traced here: 920 us
  waiting for transfers between devices  324 us (35%)
  Pallas kernels  209 us (22%)
  starting transfers between devices  115 us (12%)
  other arithmetic  90.7 us (10%)
  matrix products  84.6 us (9%)
  local copies, waits for them, and re-layouts  79.9 us (9%)
  between operations  16.4 us (2%)
    ppermute x61, waiting for transfers between devices, swap(): return lax.ppermute(block, 'dp', [(i, i ^ bit) for i in range(self.count)])  222 us
    ppermute x21, waiting for transfers between devices, send(): lax.ppermute(block, 'fsdp', [(i, (i + places) % self.count) for i in rang...  96.7 us
    ppermute x21, starting transfers between devices, send(): lax.ppermute(block, 'fsdp', [(i, (i + places) % self.count) for i in rang...  60.2 us
    pallas_call x2, Pallas kernels, weight_grad(): pl.pallas_call(functools.partial(weight_kernel, count), out_shape=jax.Sha...  50.5 us
    ppermute x61, starting transfers between devices, swap(): return lax.ppermute(block, 'dp', [(i, i ^ bit) for i in range(self.count)])  47.6 us
    pallas_call x2, Pallas kernels, middle_layer(): pl.pallas_call(functools.partial(middle_kernel, count), out_shape=[jax.Sh...  39.6 us
    dot_general x7, matrix products, dot_nt(): lax.dot_general(left, right, (((1,), (1,)), ((), ())), preferred_element_...  32.8 us
    dot_general x7, matrix products, dot_nn(): return jnp.dot(left, right, preferred_element_type=F32)  32.1 us
  transfers between devices with their start and end apart: 90, of which 26 were waited for; matrix products, arithmetic and copies ran while one was open for 20% of the time, Pallas kernels for 21%

profile of v6, /device:TPU:0, one launch (start us, length us, event | category | flops | bytes accessed | tf_op | source)
XLA Modules:
  0.0 920.3 jit_solution(6112631899402755602)
XLA Ops:
  7.3 2.8 slice_bitcast_fusion
  10.1 2.9 collective-permute-start
  15.7 3.6 all-to-all-start
  27.1 10.1 %collective-permute-done = bf16[256,2048]{1,0:T(8,128)(2,1)} collective-permute-done((bf16[256,2048]{1,0:T(8,128)(2,1)S(1)}, bf16[256,2048]{1,0:T(8,128)(2,1)}, u32[]{:S(2)}, u32[]{:S(2)}) %collective-permute-start) | collective-permute-done | bytes 1048608 | tf_op jit(solution)/shard_map/ppermute | solution.py:520
  40.5 3.1 pad_maximum_fusion.2.refs_1_.refs_9_
  43.7 5.5 all-to-all-done
  55.3 12.8 %collective-permute-done.5 = bf16[128,2048]{1,0:T(8,128)(2,1)S(1)} collective-permute-done((bf16[128,2048]{1,0:T(8,128)(2,1)S(1)}, bf16[128,2048]{1,0:T(8,128)(2,1)S(1)}, u32[]{:S(2)}, u32[]{:S(2)}) %collective-permute-start.5) | collective-permute-done | bytes 524320 | tf_op jit(solution)/shard_map/ppermute | solution.py:520
  79.8 17.6 %collective-permute-done.6.refs_2_.refs_0_ = bf16[256,2048]{1,0:T(8,128)(2,1)} collective-permute-done((bf16[256,2048]{1,0:T(8,128)(2,1)S(1)}, bf16[256,2048]{1,0:T(8,128)(2,1)}, u32[]{:S(2)}, u32[]{:S(2)}) %collective-permute-start.6) | collective-permute-done | bytes 1048608 | tf_op jit(solution)/shard_map/ppermute | solution.py:520
  98.8 2.7 fusion.61
  105.0 3.9 fusion.5
  112.2 3.9 fusion.14.refs_0_
  122.6 3.4 collective-permute-start.15
  127.0 17.4 %collective-permute-done.17 = bf16[64,2048]{1,0:T(8,128)(2,1)S(1)} collective-permute-done((bf16[64,2048]{1,0:T(8,128)(2,1)S(1)}, bf16[64,2048]{1,0:T(8,128)(2,1)S(1)}, u32[]{:S(2)}, u32[]{:S(2)}) %collective-permute-start.17) | collective-permute-done | bytes 262176 | tf_op jit(solution)/shard_map/ppermute | solution.py:456
  150.9 9.7 %shard_map.288 = (bf16[512,2048]{1,0:T(8,128)(2,1)}, bf16[512,1024]{1,0:T(8,128)(2,1)S(1)}, bf16[512,1024]{1,0:T(8,128)(2,1)S(1)}) custom-call(s32[2,8]{1,0:T(2,128)S(1)} %pad_add_fusion.place_ref, bf16[512,2048]{1,0:T(8,128)(2,1)} %fusion.14.refs_0_, f32[1,2048]{1,0:T(1,128)S(1)} %reshape.426.refs_1_, ...), custom_call_target="tpu_custom_call" | custom-call | flops 536870912 | bytes 1835008 | tf_op jit(solution)/shard_map/pallas_call | solution.py:367
  161.8 33.3 %collective-permute-done.14 = bf16[2,256,256]{2,1,0:T(8,128)(2,1)} collective-permute-done((bf16[2,256,256]{2,1,0:T(8,128)(2,1)}, bf16[2,256,256]{2,1,0:T(8,128)(2,1)}, u32[]{:S(2)}, u32[]{:S(2)}) %collective-permute-start.14) | collective-permute-done | bytes 262176 | tf_op jit(solution)/shard_map/ppermute | solution.py:456
  201.4 22.0 %collective-permute-done.21.refs_2_.refs_0_ = bf16[256,2048]{1,0:T(8,128)(2,1)} collective-permute-done((bf16[256,2048]{1,0:T(8,128)(2,1)S(1)}, bf16[256,2048]{1,0:T(8,128)(2,1)}, u32[]{:S(2)}, u32[]{:S(2)}) %collective-permute-start.21) | collective-permute-done | bytes 1048608 | tf_op jit(solution)/shard_map/ppermute | solution.py:520
  228.3 18.8 %shard_map.289 = (bf16[512,2048]{1,0:T(8,128)(2,1)S(1)}, f32[512,128]{1,0:T(8,128)S(1)}) custom-call(s32[1]{0:T(128)} %bitcast.19.pos_ref, s32[2,8]{1,0:T(2,128)S(1)} %select_reduce_fusion.ends_ref, bf16[512,2048]{1,0:T(8,128)(2,1)S(1)} %copy-done.15, bf16[2,1024,256]{2,1,0:T(8,128)(2,1)S(1)} %copy-done.4), custom_call_target="tpu_custom_call" | custom-call | flops 536870912 | bytes 524288 | tf_op jit(solution)/shard_map/pallas_call | solution.py:132
  248.5 10.2 %shard_map.290 = (f32[512,2048]{1,0:T(8,128)}, bf16[512,1024]{1,0:T(8,128)(2,1)S(1)}, bf16[512,1024]{1,0:T(8,128)(2,1)S(1)}) custom-call(s32[2,8]{1,0:T(2,128)S(1)} %pad_add_fusion.place_ref, bf16[512,2048]{1,0:T(8,128)(2,1)} %copy-done.19, f32[1,2048]{1,0:T(1,128)S(1)} %reshape.427.refs_1_, bf16[256,2048]{1,0:T(8,128)(2,1)} %collective-permute-done.21.refs_2_.refs_0_, ...), custom_call_target="tpu_custom_call" | custom-call | flops 536870912 | bytes 1835008 | tf_op jit(solution)/shard_map/pallas_call | solution.py:367
  258.8 3.5 fusion.57
  269.4 66.5 %collective-permute-done.27 = bf16[256,2048]{1,0:T(8,128)(2,1)S(1)} collective-permute-done((bf16[256,2048]{1,0:T(8,128)(2,1)S(1)}, bf16[256,2048]{1,0:T(8,128)(2,1)S(1)}, u32[]{:S(2)}, u32[]{:S(2)}) %collective-permute-start.27) | collective-permute-done | bytes 1048608 | tf_op jit(solution)/shard_map/ppermute | solution.py:520
  342.8 44.6 %collective-permute-done.31.refs_0_.refs_4_ = bf16[512,2048]{1,0:T(8,128)(2,1)} collective-permute-done((bf16[512,2048]{1,0:T(8,128)(2,1)}, bf16[512,2048]{1,0:T(8,128)(2,1)}, u32[]{:S(2)}, u32[]{:S(2)}) %collective-permute-start.31) | collective-permute-done | bytes 2097184 | tf_op jit(solution)/shard_map/ppermute | solution.py:520
  391.9 13.4 %shard_map.291.refs_4_ = bf16[2048,1024]{1,0:T(8,128)(2,1)} custom-call(bf16[512,2048]{1,0:T(8,128)(2,1)S(1)} %pad_maximum_fusion.1.refs_0_.refs_8_, bf16[512,2048]{1,0:T(8,128)(2,1)S(1)} %copy-done.2, bf16[512,2048]{1,0:T(8,128)(2,1)} %copy-done.56, bf16[512,2048]{1,0:T(8,128)(2,1)} %copy-done.57, bf16[1024,2048]{1,0:T(8,128)(2,1)} %all-gather.9.cloned.1.call-done.refs_4_), custom_call_target="tpu_custom_call" | custom-call | flops 1073741824 | bytes 2097152 | tf_op jit(solution)/shard_map/pallas_call | solution.py:236
  405.4 14.1 %shard_map.292.refs_4_ = bf16[2048,1024]{1,0:T(8,128)(2,1)} custom-call(bf16[512,2048]{1,0:T(8,128)(2,1)S(1)} %copy-done.17, bf16[512,2048]{1,0:T(8,128)(2,1)} %collective-permute-done.30.refs_1_.refs_13_, bf16[512,2048]{1,0:T(8,128)(2,1)} %copy-done.58, bf16[512,2048]{1,0:T(8,128)(2,1)} %collective-permute-done.38.refs_3_.refs_15_, ...), custom_call_target="tpu_custom_call" | custom-call | flops 1073741824 | bytes 2097152 | tf_op jit(solution)/shard_map/pallas_call | solution.py:236
  419.5 19.7 %shard_map.293 = (bf16[1024,1024]{1,0:T(8,128)(2,1)S(1)}, bf16[1024,1024]{1,0:T(8,128)(2,1)S(1)}, bf16[1024,1024]{1,0:T(8,128)(2,1)}, bf16[1024,1024]{1,0:T(8,128)(2,1)}) custom-call(bf16[512,2048]{1,0:T(8,128)(2,1)} %pad_maximum_fusion.3.refs_0_, bf16[512,2048]{1,0:T(8,128)(2,1)} %pad_maximum_fusion.4.refs_1_, ...), custom_call_target="tpu_custom_call" | custom-call | flops 1073741824 | bytes 3145728 | tf_op jit(solution)/shard_map/pallas_call | solution.py:202
  441.9 19.9 %shard_map.294 = (bf16[1024,1024]{1,0:T(8,128)(2,1)S(1)}, bf16[1024,1024]{1,0:T(8,128)(2,1)S(1)}, bf16[1024,1024]{1,0:T(8,128)(2,1)}, bf16[1024,1024]{1,0:T(8,128)(2,1)}) custom-call(bf16[512,2048]{1,0:T(8,128)(2,1)} %collective-permute-done.31.refs_0_.refs_4_, bf16[512,2048]{1,0:T(8,128)(2,1)} %collective-permute-done.32.refs_1_.refs_5_, ...), custom_call_target="tpu_custom_call" | custom-call | flops 1073741824 | bytes 3145728 | tf_op jit(solution)/shard_map/pallas_call | solution.py:202
  461.9 4.5 convolution_convert_fusion.8
  470.7 3.7 add_convert_fusion.7
  474.4 3.8 add_convert_fusion.6
  478.1 4.9 convolution_convert_fusion.4
  485.5 4.9 collective-permute-done.43
  490.4 24.3 %shard_map.295 = bf16[2048,1024]{1,0:T(8,128)(2,1)} custom-call(bf16[512,2048]{1,0:T(8,128)(2,1)} %pad_maximum_fusion.3.refs_0_, bf16[512,2048]{1,0:T(8,128)(2,1)} %pad_maximum_fusion.4.refs_1_, bf16[512,2048]{1,0:T(8,128)(2,1)} %collective-permute-done.39.refs_2_, bf16[512,2048]{1,0:T(8,128)(2,1)} %collective-permute-done.40.refs_3_, ...), custom_call_target="tpu_custom_call" | custom-call | flops 2147483648 | bytes 3670016 | tf_op jit(solution)/shard_map/pallas_call | solution.py:276
  514.7 8.1 add_convert_fusion.3
  522.9 8.5 collective-permute-done.45
  532.4 4.8 convert_add_fusion.3
  542.5 3.7 convolution_convert_fusion.6
  546.2 3.7 convolution_convert_fusion.5
  550.3 26.1 %shard_map.296 = bf16[1024,2048]{1,0:T(8,128)(2,1)} custom-call(bf16[1024,1024]{1,0:T(8,128)(2,1)} %copy-done.8, bf16[1024,1024]{1,0:T(8,128)(2,1)} %copy-done.8, bf16[1024,1024]{1,0:T(8,128)(2,1)} %copy-done.10, bf16[1024,1024]{1,0:T(8,128)(2,1)} %copy-done.10, bf16[1024,1024]{1,0:T(8,128)(2,1)} %copy-done.12, bf16[1024,1024]{1,0:T(8,128)(2,1)} %copy-done.12, ...), custom_call_target="tpu_custom_call" | custom-call | flops 2147483648 | bytes 3670016 | tf_op jit(solution)/shard_map/pallas_call | solution.py:276
  584.0 5.3 add_convert_fusion.5
  589.3 5.4 add_convert_fusion.4
  601.2 4.4 convolution_convert_fusion.2
  608.3 10.6 %shard_map.297.grad_ref = bf16[512,2048]{1,0:T(8,128)(2,1)} custom-call(s32[2,8]{1,0:T(2,128)S(1)} %pad_add_fusion.place_ref, bf16[512,2048]{1,0:T(8,128)(2,1)} %copy-done.54, bf16[256,2048]{1,0:T(8,128)(2,1)} %collective-permute-done.21.refs_2_.refs_0_, bf16[256,2048]{1,0:T(8,128)(2,1)S(1)} %pad_maximum_fusion.10.refs_3_.refs_1_, ...), custom_call_target="tpu_custom_call" | custom-call | flops 536870912 | bytes 1572864 | tf_op jit(solution)/shard_map/pallas_call | solution.py:414
  618.9 4.6 add_convert_fusion.2
  626.0 30.8 %shard_map.298 = (bf16[512,2048]{1,0:T(8,128)(2,1)S(1)}, bf16[2,1024,256]{2,1,0:T(8,128)(2,1)S(1)}) custom-call(s32[1]{0:T(128)} %bitcast.19.pos_ref, s32[2,8]{1,0:T(2,128)S(1)} %select_reduce_fusion.ends_ref, bf16[512,2048]{1,0:T(8,128)(2,1)} %get-tuple-element.159.q_ref, bf16[2,1024,256]{2,1,0:T(8,128)(2,1)S(1)} %copy-done.5, ...), custom_call_target="tpu_custom_call" | custom-call | flops 1342177280 | bytes 1310720 | tf_op jit(solution)/shard_map/pallas_call | solution.py:152
  656.9 4.4 convolution_convert_fusion.1
  671.5 16.2 %collective-permute-start.56 = (bf16[2,256,256]{2,1,0:T(8,128)(2,1)}, bf16[2,256,256]{2,1,0:T(8,128)(2,1)}, u32[]{:S(2)}, u32[]{:S(2)}) collective-permute-start(bf16[2,256,256]{2,1,0:T(8,128)(2,1)} %get-tuple-element.305), channel_id=1, source_target_pairs={{0,1},{1,2},{2,3},{3,0},{4,5},{5,6},{6,7},{7,4},{8,9},{9,10},{10,1... | collective-permute-start | bytes 786440 | tf_op jit(solution)/shard_map/ppermute | solution.py:456
  689.4 13.1 %collective-permute-start.58 = (bf16[2,256,256]{2,1,0:T(8,128)(2,1)}, bf16[2,256,256]{2,1,0:T(8,128)(2,1)}, u32[]{:S(2)}, u32[]{:S(2)}) collective-permute-start(bf16[2,256,256]{2,1,0:T(8,128)(2,1)} %get-tuple-element.303), channel_id=1, source_target_pairs={{0,3},{1,0},{2,1},{3,2},{4,7},{5,4},{6,5},{7,6},{8,11},{9,8},{10,9... | collective-permute-start | bytes 786440 | tf_op jit(solution)/shard_map/ppermute | solution.py:456
  702.5 5.0 add_convert_fusion.1
  714.5 2.9 convert_add_fusion.8
  722.1 11.2 %shard_map.299 = f32[512,2048]{1,0:T(8,128)} custom-call(s32[2,8]{1,0:T(2,128)S(1)} %pad_add_fusion.place_ref, bf16[512,2048]{1,0:T(8,128)(2,1)} %copy-done.18, bf16[256,2048]{1,0:T(8,128)(2,1)} %collective-permute-done.6.refs_2_.refs_0_, bf16[256,2048]{1,0:T(8,128)(2,1)S(1)} %copy-done.7, bf16[256,2048]{1,0:T(8,128)(2,1)} %collective-permute-done.8.refs_4_.refs_2_, ...), custom_call_target="tpu_custom_call" | custom-call | flops 536870912 | bytes 1572864 | tf_op jit(solution)/shard_map/pallas_call | solution.py:414
  737.9 5.4 fusion.16
  746.5 3.4 collective-permute-start.81
  754.5 4.4 fusion.20
  759.2 8.8 collective-permute-done.81
  769.5 35.1 %collective-permute-done.80 = bf16[64,2048]{1,0:T(8,128)(2,1)S(1)} collective-permute-done((bf16[64,2048]{1,0:T(8,128)(2,1)S(1)}, bf16[64,2048]{1,0:T(8,128)(2,1)S(1)}, u32[]{:S(2)}, u32[]{:S(2)}) %collective-permute-start.80) | collective-permute-done | bytes 262176 | tf_op jit(solution)/shard_map/ppermute | solution.py:456
  806.8 6.1 convolution_convert_fusion.3
  825.0 8.7 collective-permute-done.72
  835.9 3.6 all-to-all-start.1
  839.5 2.8 convert_element_type.594
  851.1 2.7 collective-permute-start.77
  862.7 6.5 add_convert_fusion
  869.2 5.2 convert_add_fusion.2
  882.6 2.7 slice.466
  891.2 11.7 %collective-permute-done.66 = bf16[256,2048]{1,0:T(8,128)(2,1)} collective-permute-done((bf16[256,2048]{1,0:T(8,128)(2,1)}, bf16[256,2048]{1,0:T(8,128)(2,1)}, u32[]{:S(2)}, u32[]{:S(2)}) %collective-permute-start.66) | collective-permute-done | bytes 1048608 | tf_op jit(solution)/shard_map/ppermute | solution.py:520
  904.5 4.9 collective-permute-done.65
  (562 shorter events, 211.5 us)
Async XLA Ops:
  7.3 41.9 %all-gather.5.cloned.1.call-start = ((), (), s32[]{:S(2)}) async-start(), calls=%async_computation.4 | async-start | bytes 1310720 | tf_op jit(solution)/shard_map/all_gather | solution.py:594
  10.1 27.0 %collective-permute-start = (bf16[256,2048]{1,0:T(8,128)(2,1)S(1)}, bf16[256,2048]{1,0:T(8,128)(2,1)}, u32[]{:S(2)}, u32[]{:S(2)}) collective-permute-start(bf16[256,2048]{1,0:T(8,128)(2,1)S(1)} %get-tuple-element.295), channel_id=1, source_target_pairs={{0,8},{4,12},{8,0},{12,4},{16,24},{20,28},{24,16},{28,20},{1,9},{5... | collective-permute-start | bytes 3145736 | tf_op jit(solution)/shard_map/ppermute | solution.py:520
  13.1 27.4 %collective-permute-start.1 = (bf16[256,2048]{1,0:T(8,128)(2,1)}, bf16[256,2048]{1,0:T(8,128)(2,1)}, u32[]{:S(2)}, u32[]{:S(2)}) collective-permute-start(bf16[256,2048]{1,0:T(8,128)(2,1)} %get-tuple-element.294), channel_id=1, source_target_pairs={{0,16},{4,20},{8,24},{12,28},{16,0},{20,4},{24,8},{28,12},{1,17},{... | collective-permute-start | bytes 3145736 | tf_op jit(solution)/shard_map/ppermute | solution.py:520
  15.7 33.5 %all-to-all-start = ((bf16[64,8,1024]{2,0,1:T(8,128)(2,1)}), bf16[64,8,1024]{2,0,1:T(8,128)(2,1)S(1)}, u32[]{:S(2)}, u32[]{:S(2)}) async-start(bf16[64,8,1024]{2,0,1:T(8,128)(2,1)} %bitcast.169), calls=%async_computation | async-start | bytes 2097152 | tf_op jit(solution)/shard_map/all_to_all | solution.py:599
  19.3 79.4 %all-gather.7.cloned.1.call-start = ((), (), s32[]{:S(2)}) async-start(), calls=%async_computation.5 | async-start | bytes 2359296 | tf_op jit(solution)/shard_map/all_gather | solution.py:604
  51.8 338.5 %all-gather.9.cloned.1.call-start = ((), (), s32[]{:S(2)}) async-start(), calls=%async_computation.6 | async-start | bytes 5242880 | tf_op jit(solution)/shard_map/all_gather | solution.py:610
  68.2 29.2 %collective-permute-start.6 = (bf16[256,2048]{1,0:T(8,128)(2,1)S(1)}, bf16[256,2048]{1,0:T(8,128)(2,1)}, u32[]{:S(2)}, u32[]{:S(2)}) collective-permute-start(bf16[256,2048]{1,0:T(8,128)(2,1)S(1)} %pad_maximum_fusion.8.refs_3_.refs_1_), channel_id=1, source_target_pairs={{0,16},{4,20},{8,24},{12,28},{16,0},{20,4},{24,8},{28,12},{1,17},{... | collective-permute-start | bytes 3145736 | tf_op jit(solution)/shard_map/ppermute | solution.py:520
  71.9 26.8 %collective-permute-start.8 = (bf16[256,2048]{1,0:T(8,128)(2,1)}, bf16[256,2048]{1,0:T(8,128)(2,1)}, u32[]{:S(2)}, u32[]{:S(2)}) collective-permute-start(bf16[256,2048]{1,0:T(8,128)(2,1)} %pad_maximum_fusion.9.refs_5_.refs_3_), channel_id=1, source_target_pairs={{0,8},{4,12},{8,0},{12,4},{16,24},{20,28},{24,16},{28,20},{1,9},{5... | collective-permute-start | bytes 3145736 | tf_op jit(solution)/shard_map/ppermute | solution.py:520
  77.2 45.4 %collective-permute-start.16 = (bf16[64,2048]{1,0:T(8,128)(2,1)S(1)}, bf16[64,2048]{1,0:T(8,128)(2,1)}, u32[]{:S(2)}, u32[]{:S(2)}) collective-permute-start(bf16[64,2048]{1,0:T(8,128)(2,1)S(1)} %copy-done.81), channel_id=1, source_target_pairs={{0,1},{1,2},{2,3},{3,0},{4,5},{5,6},{6,7},{7,4},{8,9},{9,10},{10,1... | collective-permute-start | bytes 786440 | tf_op jit(solution)/shard_map/ppermute | solution.py:456
  79.3 38.2 %collective-permute-start.10 = (bf16[256,2048]{1,0:T(8,128)(2,1)S(1)}, bf16[256,2048]{1,0:T(8,128)(2,1)}, u32[]{:S(2)}, u32[]{:S(2)}) collective-permute-start(bf16[256,2048]{1,0:T(8,128)(2,1)S(1)} %pad_maximum_fusion.8.refs_3_.refs_1_), channel_id=1, source_target_pairs={{0,4},{4,0},{8,12},{12,8},{16,20},{20,16},{24,28},{28,24},{1,5},{5... | collective-permute-start | bytes 3145736 | tf_op jit(solution)/shard_map/ppermute | solution.py:520
  79.3 39.9 %collective-permute-start.12 = (bf16[256,2048]{1,0:T(8,128)(2,1)}, bf16[256,2048]{1,0:T(8,128)(2,1)}, u32[]{:S(2)}, u32[]{:S(2)}) collective-permute-start(bf16[256,2048]{1,0:T(8,128)(2,1)} %pad_maximum_fusion.9.refs_5_.refs_3_), channel_id=1, source_target_pairs={{0,4},{4,0},{8,12},{12,8},{16,20},{20,16},{24,28},{28,24},{1,5},{5... | collective-permute-start | bytes 3145736 | tf_op jit(solution)/shard_map/ppermute | solution.py:520
  98.7 320.7 %all-gather.11.cloned.1.call-start = ((), (), s32[]{:S(2)}) async-start(), calls=%async_computation.7 | async-start | bytes 5242880 | tf_op jit(solution)/shard_map/all_gather | solution.py:623
  117.5 26.9 %collective-permute-start.17 = (bf16[64,2048]{1,0:T(8,128)(2,1)S(1)}, bf16[64,2048]{1,0:T(8,128)(2,1)S(1)}, u32[]{:S(2)}, u32[]{:S(2)}) collective-permute-start(bf16[64,2048]{1,0:T(8,128)(2,1)S(1)} %copy-done.81), channel_id=1, source_target_pairs={{0,2},{1,3},{2,0},{3,1},{4,6},{5,7},{6,4},{7,5},{8,10},{9,11},{10,... | collective-permute-start | bytes 786440 | tf_op jit(solution)/shard_map/ppermute | solution.py:456
  119.2 26.5 %collective-permute-start.18 = (bf16[64,2048]{1,0:T(8,128)(2,1)S(1)}, bf16[64,2048]{1,0:T(8,128)(2,1)S(1)}, u32[]{:S(2)}, u32[]{:S(2)}) collective-permute-start(bf16[64,2048]{1,0:T(8,128)(2,1)S(1)} %copy-done.81), channel_id=1, source_target_pairs={{0,3},{1,0},{2,1},{3,2},{4,7},{5,4},{6,5},{7,6},{8,11},{9,8},{10,9... | collective-permute-start | bytes 786440 | tf_op jit(solution)/shard_map/ppermute | solution.py:456
  120.4 40.1 %collective-permute-start.13 = (bf16[2,256,256]{2,1,0:T(8,128)(2,1)}, bf16[2,256,256]{2,1,0:T(8,128)(2,1)}, u32[]{:S(2)}, u32[]{:S(2)}) collective-permute-start(bf16[2,256,256]{2,1,0:T(8,128)(2,1)} %bitcast.26), channel_id=1, source_target_pairs={{0,1},{1,2},{2,3},{3,0},{4,5},{5,6},{6,7},{7,4},{8,9},{9,10},{10,1... | collective-permute-start | bytes 786440 | tf_op jit(solution)/shard_map/ppermute | solution.py:456
  121.3 73.8 %collective-permute-start.14 = (bf16[2,256,256]{2,1,0:T(8,128)(2,1)}, bf16[2,256,256]{2,1,0:T(8,128)(2,1)}, u32[]{:S(2)}, u32[]{:S(2)}) collective-permute-start(bf16[2,256,256]{2,1,0:T(8,128)(2,1)} %bitcast.26), channel_id=1, source_target_pairs={{0,2},{1,3},{2,0},{3,1},{4,6},{5,7},{6,4},{7,5},{8,10},{9,11},{10,... | collective-permute-start | bytes 786440 | tf_op jit(solution)/shard_map/ppermute | solution.py:456
  122.6 73.4 %collective-permute-start.15 = (bf16[2,256,256]{2,1,0:T(8,128)(2,1)}, bf16[2,256,256]{2,1,0:T(8,128)(2,1)}, u32[]{:S(2)}, u32[]{:S(2)}) collective-permute-start(bf16[2,256,256]{2,1,0:T(8,128)(2,1)} %bitcast.26), channel_id=1, source_target_pairs={{0,3},{1,0},{2,1},{3,2},{4,7},{5,4},{6,5},{7,6},{8,11},{9,8},{10,9... | collective-permute-start | bytes 786440 | tf_op jit(solution)/shard_map/ppermute | solution.py:456
  146.9 50.1 %collective-permute-start.19 = (bf16[128,2048]{1,0:T(8,128)(2,1)}, bf16[128,2048]{1,0:T(8,128)(2,1)S(1)}, u32[]{:S(2)}, u32[]{:S(2)}) collective-permute-start(bf16[128,2048]{1,0:T(8,128)(2,1)} %get-tuple-element.308), channel_id=1, source_target_pairs={{0,8},{4,12},{8,0},{12,4},{16,24},{20,28},{24,16},{28,20},{1,9},{5... | collective-permute-start | bytes 1572872 | tf_op jit(solution)/shard_map/ppermute | solution.py:520
  148.7 48.4 %collective-permute-start.20 = (bf16[128,2048]{1,0:T(8,128)(2,1)}, bf16[128,2048]{1,0:T(8,128)(2,1)S(1)}, u32[]{:S(2)}, u32[]{:S(2)}) collective-permute-start(bf16[128,2048]{1,0:T(8,128)(2,1)} %get-tuple-element.307), channel_id=1, source_target_pairs={{0,16},{4,20},{8,24},{12,28},{16,0},{20,4},{24,8},{28,12},{1,17},{... | collective-permute-start | bytes 1572872 | tf_op jit(solution)/shard_map/ppermute | solution.py:520
  200.9 47.6 %collective-permute-start.24 = (bf16[256,2048]{1,0:T(8,128)(2,1)S(1)}, bf16[256,2048]{1,0:T(8,128)(2,1)}, u32[]{:S(2)}, u32[]{:S(2)}) collective-permute-start(bf16[256,2048]{1,0:T(8,128)(2,1)S(1)} %pad_maximum_fusion.10.refs_3_.refs_1_), channel_id=1, source_target_pairs={{0,4},{4,0},{8,12},{12,8},{16,20},{20,16},{24,28},{28,24},{1,5},{5... | collective-permute-start | bytes 3145736 | tf_op jit(solution)/shard_map/ppermute | solution.py:520
  200.9 47.6 %collective-permute-start.26 = (bf16[256,2048]{1,0:T(8,128)(2,1)}, bf16[256,2048]{1,0:T(8,128)(2,1)}, u32[]{:S(2)}, u32[]{:S(2)}) collective-permute-start(bf16[256,2048]{1,0:T(8,128)(2,1)} %pad_maximum_fusion.11.refs_5_.refs_3_), channel_id=1, source_target_pairs={{0,4},{4,0},{8,12},{12,8},{16,20},{20,16},{24,28},{28,24},{1,5},{5... | collective-permute-start | bytes 3145736 | tf_op jit(solution)/shard_map/ppermute | solution.py:520
  223.4 25.1 %collective-permute-start.23 = (bf16[256,2048]{1,0:T(8,128)(2,1)}, bf16[256,2048]{1,0:T(8,128)(2,1)}, u32[]{:S(2)}, u32[]{:S(2)}) collective-permute-start(bf16[256,2048]{1,0:T(8,128)(2,1)} %collective-permute-done.21.refs_2_.refs_0_), channel_id=1, source_target_pairs={{0,4},{4,0},{8,12},{12,8},{16,20},{20,16},{24,28},{28,24},{1,5},{5... | collective-permute-start | bytes 3145736 | tf_op jit(solution)/shard_map/ppermute | solution.py:520
  225.5 599.6 %reduce-scatter.3.cloned.1.call-start = ((), (), s32[]{:S(2)}) async-start(), calls=%async_computation.8 | async-start | bytes 5242880 | tf_op jit(solution)/shard_map/reduce_scatter | solution.py:686
  262.8 76.2 %collective-permute-start.29 = (bf16[512,2048]{1,0:T(8,128)(2,1)S(1)}, bf16[512,2048]{1,0:T(8,128)(2,1)S(1)}, u32[]{:S(2)}, u32[]{:S(2)}) collective-permute-start(bf16[512,2048]{1,0:T(8,128)(2,1)S(1)} %pad_maximum_fusion.1.refs_0_.refs_8_), channel_id=1, source_target_pairs={{0,16},{4,20},{8,24},{12,28},{16,0},{20,4},{24,8},{28,12},{1,17},{... | collective-permute-start | bytes 6291464 | tf_op jit(solution)/shard_map/ppermute | solution.py:520
  265.4 73.6 %collective-permute-start.30 = (bf16[512,2048]{1,0:T(8,128)(2,1)S(1)}, bf16[512,2048]{1,0:T(8,128)(2,1)}, u32[]{:S(2)}, u32[]{:S(2)}) collective-permute-start(bf16[512,2048]{1,0:T(8,128)(2,1)S(1)} %copy-done.1), channel_id=1, source_target_pairs={{0,8},{4,12},{8,0},{12,4},{16,24},{20,28},{24,16},{28,20},{1,9},{5... | collective-permute-start | bytes 6291464 | tf_op jit(solution)/shard_map/ppermute | solution.py:520
  267.3 68.5 %collective-permute-start.27 = (bf16[256,2048]{1,0:T(8,128)(2,1)S(1)}, bf16[256,2048]{1,0:T(8,128)(2,1)S(1)}, u32[]{:S(2)}, u32[]{:S(2)}) collective-permute-start(bf16[256,2048]{1,0:T(8,128)(2,1)S(1)} %get-tuple-element.291), channel_id=1, source_target_pairs={{0,8},{4,12},{8,0},{12,4},{16,24},{20,28},{24,16},{28,20},{1,9},{5... | collective-permute-start | bytes 3145736 | tf_op jit(solution)/shard_map/ppermute | solution.py:520
  268.5 68.9 %collective-permute-start.28 = (bf16[256,2048]{1,0:T(8,128)(2,1)S(1)}, bf16[256,2048]{1,0:T(8,128)(2,1)S(1)}, u32[]{:S(2)}, u32[]{:S(2)}) collective-permute-start(bf16[256,2048]{1,0:T(8,128)(2,1)S(1)} %get-tuple-element.290), channel_id=1, source_target_pairs={{0,16},{4,20},{8,24},{12,28},{16,0},{20,4},{24,8},{28,12},{1,17},{... | collective-permute-start | bytes 3145736 | tf_op jit(solution)/shard_map/ppermute | solution.py:520
  269.4 72.8 %collective-permute-start.35 = (bf16[512,2048]{1,0:T(8,128)(2,1)S(1)}, bf16[512,2048]{1,0:T(8,128)(2,1)S(1)}, u32[]{:S(2)}, u32[]{:S(2)}) collective-permute-start(bf16[512,2048]{1,0:T(8,128)(2,1)S(1)} %pad_maximum_fusion.1.refs_0_.refs_8_), channel_id=1, source_target_pairs={{0,4},{4,0},{8,12},{12,8},{16,20},{20,16},{24,28},{28,24},{1,5},{5... | collective-permute-start | bytes 6291464 | tf_op jit(solution)/shard_map/ppermute | solution.py:520
  339.0 48.4 %collective-permute-start.31 = (bf16[512,2048]{1,0:T(8,128)(2,1)}, bf16[512,2048]{1,0:T(8,128)(2,1)}, u32[]{:S(2)}, u32[]{:S(2)}) collective-permute-start(bf16[512,2048]{1,0:T(8,128)(2,1)} %pad_maximum_fusion.3.refs_0_), channel_id=1, source_target_pairs={{0,16},{4,20},{8,24},{12,28},{16,0},{20,4},{24,8},{28,12},{1,17},{... | collective-permute-start | bytes 6291464 | tf_op jit(solution)/shard_map/ppermute | solution.py:520
  339.6 48.1 %collective-permute-start.32 = (bf16[512,2048]{1,0:T(8,128)(2,1)}, bf16[512,2048]{1,0:T(8,128)(2,1)}, u32[]{:S(2)}, u32[]{:S(2)}) collective-permute-start(bf16[512,2048]{1,0:T(8,128)(2,1)} %pad_maximum_fusion.4.refs_1_), channel_id=1, source_target_pairs={{0,8},{4,12},{8,0},{12,4},{16,24},{20,28},{24,16},{28,20},{1,9},{5... | collective-permute-start | bytes 6291464 | tf_op jit(solution)/shard_map/ppermute | solution.py:520
  340.8 47.0 %collective-permute-start.37 = (bf16[512,2048]{1,0:T(8,128)(2,1)S(1)}, bf16[512,2048]{1,0:T(8,128)(2,1)S(1)}, u32[]{:S(2)}, u32[]{:S(2)}) collective-permute-start(bf16[512,2048]{1,0:T(8,128)(2,1)S(1)} %collective-permute-done.29.refs_0_.refs_12_), channel_id=1, source_target_pairs={{0,4},{4,0},{8,12},{12,8},{16,20},{20,16},{24,28},{28,24},{1,5},{5... | collective-permute-start | bytes 6291464 | tf_op jit(solution)/shard_map/ppermute | solution.py:520
  342.2 63.2 %collective-permute-start.38 = (bf16[512,2048]{1,0:T(8,128)(2,1)}, bf16[512,2048]{1,0:T(8,128)(2,1)}, u32[]{:S(2)}, u32[]{:S(2)}) collective-permute-start(bf16[512,2048]{1,0:T(8,128)(2,1)} %collective-permute-done.30.refs_1_.refs_13_), channel_id=1, source_target_pairs={{0,4},{4,0},{8,12},{12,8},{16,20},{20,16},{24,28},{28,24},{1,5},{5... | collective-permute-start | bytes 6291464 | tf_op jit(solution)/shard_map/ppermute | solution.py:520
  342.7 76.8 %collective-permute-start.39 = (bf16[512,2048]{1,0:T(8,128)(2,1)}, bf16[512,2048]{1,0:T(8,128)(2,1)}, u32[]{:S(2)}, u32[]{:S(2)}) collective-permute-start(bf16[512,2048]{1,0:T(8,128)(2,1)} %pad_maximum_fusion.3.refs_0_), channel_id=1, source_target_pairs={{0,4},{4,0},{8,12},{12,8},{16,20},{20,16},{24,28},{28,24},{1,5},{5... | collective-permute-start | bytes 6291464 | tf_op jit(solution)/shard_map/ppermute | solution.py:520
  387.4 32.1 %collective-permute-start.40 = (bf16[512,2048]{1,0:T(8,128)(2,1)}, bf16[512,2048]{1,0:T(8,128)(2,1)}, u32[]{:S(2)}, u32[]{:S(2)}) collective-permute-start(bf16[512,2048]{1,0:T(8,128)(2,1)} %pad_maximum_fusion.4.refs_1_), channel_id=1, source_target_pairs={{0,4},{4,0},{8,12},{12,8},{16,20},{20,16},{24,28},{28,24},{1,5},{5... | collective-permute-start | bytes 6291464 | tf_op jit(solution)/shard_map/ppermute | solution.py:520
  387.6 54.3 %collective-permute-start.33 = (bf16[512,2048]{1,0:T(8,128)(2,1)}, bf16[512,2048]{1,0:T(8,128)(2,1)}, u32[]{:S(2)}, u32[]{:S(2)}) collective-permute-start(bf16[512,2048]{1,0:T(8,128)(2,1)} %collective-permute-done.31.refs_0_.refs_4_), channel_id=1, source_target_pairs={{0,4},{4,0},{8,12},{12,8},{16,20},{20,16},{24,28},{28,24},{1,5},{5... | collective-permute-start | bytes 6291464 | tf_op jit(solution)/shard_map/ppermute | solution.py:520
  389.2 52.7 %collective-permute-start.34 = (bf16[512,2048]{1,0:T(8,128)(2,1)}, bf16[512,2048]{1,0:T(8,128)(2,1)}, u32[]{:S(2)}, u32[]{:S(2)}) collective-permute-start(bf16[512,2048]{1,0:T(8,128)(2,1)} %collective-permute-done.32.refs_1_.refs_5_), channel_id=1, source_target_pairs={{0,4},{4,0},{8,12},{12,8},{16,20},{20,16},{24,28},{28,24},{1,5},{5... | collective-permute-start | bytes 6291464 | tf_op jit(solution)/shard_map/ppermute | solution.py:520
  483.3 48.0 %collective-permute-start.45 = (bf16[512,2048]{1,0:T(8,128)(2,1)}, bf16[512,2048]{1,0:T(8,128)(2,1)S(1)}, u32[]{:S(2)}, u32[]{:S(2)}) collective-permute-start(bf16[512,2048]{1,0:T(8,128)(2,1)} %add_convert_fusion.6), channel_id=1, source_target_pairs={{0,8},{4,12},{8,0},{12,4},{16,24},{20,28},{24,16},{28,20},{1,9},{5... | collective-permute-start | bytes 6291464 | tf_op jit(solution)/shard_map/ppermute | solution.py:520
  484.5 47.9 %collective-permute-start.44 = (bf16[512,2048]{1,0:T(8,128)(2,1)}, bf16[512,2048]{1,0:T(8,128)(2,1)}, u32[]{:S(2)}, u32[]{:S(2)}) collective-permute-start(bf16[512,2048]{1,0:T(8,128)(2,1)} %add_convert_fusion.7), channel_id=1, source_target_pairs={{0,16},{4,20},{8,24},{12,28},{16,0},{20,4},{24,8},{28,12},{1,17},{... | collective-permute-start | bytes 6291464 | tf_op jit(solution)/shard_map/ppermute | solution.py:520
  538.4 38.1 %collective-permute-start.47 = (bf16[256,2048]{1,0:T(8,128)(2,1)}, bf16[256,2048]{1,0:T(8,128)(2,1)}, u32[]{:S(2)}, u32[]{:S(2)}) collective-permute-start(bf16[256,2048]{1,0:T(8,128)(2,1)} %slice.467), channel_id=1, source_target_pairs={{0,16},{4,20},{8,24},{12,28},{16,0},{20,4},{24,8},{28,12},{1,17},{... | collective-permute-start | bytes 3145736 | tf_op jit(solution)/shard_map/ppermute | solution.py:520
  540.5 38.3 %collective-permute-start.46 = (bf16[256,2048]{1,0:T(8,128)(2,1)}, bf16[256,2048]{1,0:T(8,128)(2,1)}, u32[]{:S(2)}, u32[]{:S(2)}) collective-permute-start(bf16[256,2048]{1,0:T(8,128)(2,1)} %slice.468), channel_id=1, source_target_pairs={{0,8},{4,12},{8,0},{12,4},{16,24},{20,28},{24,16},{28,20},{1,9},{5... | collective-permute-start | bytes 3145736 | tf_op jit(solution)/shard_map/ppermute | solution.py:520
  546.1 35.6 %collective-permute-start.48 = (bf16[512,2048]{1,0:T(8,128)(2,1)}, bf16[512,2048]{1,0:T(8,128)(2,1)}, u32[]{:S(2)}, u32[]{:S(2)}) collective-permute-start(bf16[512,2048]{1,0:T(8,128)(2,1)} %convolution_convert_fusion.6), channel_id=1, source_target_pairs={{0,4},{4,0},{8,12},{12,8},{16,20},{20,16},{24,28},{28,24},{1,5},{5... | collective-permute-start | bytes 6291464 | tf_op jit(solution)/shard_map/ppermute | solution.py:520
  549.8 39.5 %collective-permute-start.49 = (bf16[512,2048]{1,0:T(8,128)(2,1)}, bf16[512,2048]{1,0:T(8,128)(2,1)}, u32[]{:S(2)}, u32[]{:S(2)}) collective-permute-start(bf16[512,2048]{1,0:T(8,128)(2,1)} %convolution_convert_fusion.5), channel_id=1, source_target_pairs={{0,4},{4,0},{8,12},{12,8},{16,20},{20,16},{24,28},{28,24},{1,5},{5... | collective-permute-start | bytes 6291464 | tf_op jit(solution)/shard_map/ppermute | solution.py:520
  605.7 219.3 %reduce-scatter.5.cloned.1.call-start = ((), (), s32[]{:S(2)}) async-start(), calls=%async_computation.9 | async-start | bytes 5242880 | tf_op jit(solution)/shard_map/reduce_scatter | solution.py:693
  606.0 50.8 %collective-permute-start.51 = (bf16[512,2048]{1,0:T(8,128)(2,1)}, bf16[512,2048]{1,0:T(8,128)(2,1)S(1)}, u32[]{:S(2)}, u32[]{:S(2)}) collective-permute-start(bf16[512,2048]{1,0:T(8,128)(2,1)} %add_convert_fusion.5), channel_id=1, source_target_pairs={{0,16},{4,20},{8,24},{12,28},{16,0},{20,4},{24,8},{28,12},{1,17},{... | collective-permute-start | bytes 6291464 | tf_op jit(solution)/shard_map/ppermute | solution.py:520
  607.1 49.8 %collective-permute-start.52 = (bf16[512,2048]{1,0:T(8,128)(2,1)}, bf16[512,2048]{1,0:T(8,128)(2,1)}, u32[]{:S(2)}, u32[]{:S(2)}) collective-permute-start(bf16[512,2048]{1,0:T(8,128)(2,1)} %add_convert_fusion.4), channel_id=1, source_target_pairs={{0,8},{4,12},{8,0},{12,4},{16,24},{20,28},{24,16},{28,20},{1,9},{5... | collective-permute-start | bytes 6291464 | tf_op jit(solution)/shard_map/ppermute | solution.py:520
  661.2 41.3 %collective-permute-start.53 = (bf16[1024,2048]{1,0:T(8,128)(2,1)}, bf16[1024,2048]{1,0:T(8,128)(2,1)}, u32[]{:S(2)}, u32[]{:S(2)}) collective-permute-start(bf16[1024,2048]{1,0:T(8,128)(2,1)} %convolution_convert_fusion.1), channel_id=1, source_target_pairs={{0,4},{4,0},{8,12},{12,8},{16,20},{20,16},{24,28},{28,24},{1,5},{5... | collective-permute-start | bytes 12582920 | tf_op jit(solution)/shard_map/ppermute | solution.py:520
  663.5 25.9 %collective-permute-start.54 = (bf16[256,2048]{1,0:T(8,128)(2,1)}, bf16[256,2048]{1,0:T(8,128)(2,1)}, u32[]{:S(2)}, u32[]{:S(2)}) collective-permute-start(bf16[256,2048]{1,0:T(8,128)(2,1)} %get-tuple-element.227), channel_id=1, source_target_pairs={{0,16},{4,20},{8,24},{12,28},{16,0},{20,4},{24,8},{28,12},{1,17},{... | collective-permute-start | bytes 3145736 | tf_op jit(solution)/shard_map/ppermute | solution.py:520
  664.3 38.2 %collective-permute-start.55 = (bf16[256,2048]{1,0:T(8,128)(2,1)}, bf16[256,2048]{1,0:T(8,128)(2,1)}, u32[]{:S(2)}, u32[]{:S(2)}) collective-permute-start(bf16[256,2048]{1,0:T(8,128)(2,1)} %get-tuple-element.228), channel_id=1, source_target_pairs={{0,8},{4,12},{8,0},{12,4},{16,24},{20,28},{24,16},{28,20},{1,9},{5... | collective-permute-start | bytes 3145736 | tf_op jit(solution)/shard_map/ppermute | solution.py:520
  671.5 46.3 %collective-permute-start.56 = (bf16[2,256,256]{2,1,0:T(8,128)(2,1)}, bf16[2,256,256]{2,1,0:T(8,128)(2,1)}, u32[]{:S(2)}, u32[]{:S(2)}) collective-permute-start(bf16[2,256,256]{2,1,0:T(8,128)(2,1)} %get-tuple-element.305), channel_id=1, source_target_pairs={{0,1},{1,2},{2,3},{3,0},{4,5},{5,6},{6,7},{7,4},{8,9},{9,10},{10,1... | collective-permute-start | bytes 786440 | tf_op jit(solution)/shard_map/ppermute | solution.py:456
  687.7 30.1 %collective-permute-start.57 = (bf16[2,256,256]{2,1,0:T(8,128)(2,1)}, bf16[2,256,256]{2,1,0:T(8,128)(2,1)}, u32[]{:S(2)}, u32[]{:S(2)}) collective-permute-start(bf16[2,256,256]{2,1,0:T(8,128)(2,1)} %get-tuple-element.304), channel_id=1, source_target_pairs={{0,2},{1,3},{2,0},{3,1},{4,6},{5,7},{6,4},{7,5},{8,10},{9,11},{10,... | collective-permute-start | bytes 786440 | tf_op jit(solution)/shard_map/ppermute | solution.py:456
  689.4 28.4 %collective-permute-start.58 = (bf16[2,256,256]{2,1,0:T(8,128)(2,1)}, bf16[2,256,256]{2,1,0:T(8,128)(2,1)}, u32[]{:S(2)}, u32[]{:S(2)}) collective-permute-start(bf16[2,256,256]{2,1,0:T(8,128)(2,1)} %get-tuple-element.303), channel_id=1, source_target_pairs={{0,3},{1,0},{2,1},{3,2},{4,7},{5,4},{6,5},{7,6},{8,11},{9,8},{10,9... | collective-permute-start | bytes 786440 | tf_op jit(solution)/shard_map/ppermute | solution.py:456
  720.7 86.0 %collective-permute-start.62 = (bf16[256,2048]{1,0:T(8,128)(2,1)}, bf16[256,2048]{1,0:T(8,128)(2,1)}, u32[]{:S(2)}, u32[]{:S(2)}) collective-permute-start(bf16[256,2048]{1,0:T(8,128)(2,1)} %get-tuple-element.276), channel_id=1, source_target_pairs={{0,16},{4,20},{8,24},{12,28},{16,0},{20,4},{24,8},{28,12},{1,17},{... | collective-permute-start | bytes 3145736 | tf_op jit(solution)/shard_map/ppermute | solution.py:520
  744.5 62.1 %collective-permute-start.61 = (bf16[1152,256]{1,0:T(8,128)(2,1)S(1)}, bf16[1152,256]{1,0:T(8,128)(2,1)S(1)}, u32[]{:S(2)}, u32[]{:S(2)}) collective-permute-start(bf16[1152,256]{1,0:T(8,128)(2,1)S(1)} %bitcast.204), channel_id=1, source_target_pairs={{0,4},{4,0},{8,12},{12,8},{16,20},{20,16},{24,28},{28,24},{1,5},{5... | collective-permute-start | bytes 1769480 | tf_op jit(solution)/shard_map/ppermute | solution.py:520
  749.8 54.8 %collective-permute-start.80 = (bf16[64,2048]{1,0:T(8,128)(2,1)S(1)}, bf16[64,2048]{1,0:T(8,128)(2,1)S(1)}, u32[]{:S(2)}, u32[]{:S(2)}) collective-permute-start(bf16[64,2048]{1,0:T(8,128)(2,1)S(1)} %get-tuple-element.286), channel_id=1, source_target_pairs={{0,2},{1,3},{2,0},{3,1},{4,6},{5,7},{6,4},{7,5},{8,10},{9,11},{10,... | collective-permute-start | bytes 786440 | tf_op jit(solution)/shard_map/ppermute | solution.py:456
  751.8 52.8 %collective-permute-start.79 = (bf16[64,2048]{1,0:T(8,128)(2,1)S(1)}, bf16[64,2048]{1,0:T(8,128)(2,1)S(1)}, u32[]{:S(2)}, u32[]{:S(2)}) collective-permute-start(bf16[64,2048]{1,0:T(8,128)(2,1)S(1)} %get-tuple-element.284), channel_id=1, source_target_pairs={{0,1},{1,2},{2,3},{3,0},{4,5},{5,6},{6,7},{7,4},{8,9},{9,10},{10,1... | collective-permute-start | bytes 786440 | tf_op jit(solution)/shard_map/ppermute | solution.py:456
  768.1 38.7 %collective-permute-start.63 = (bf16[256,2048]{1,0:T(8,128)(2,1)S(1)}, bf16[256,2048]{1,0:T(8,128)(2,1)S(1)}, u32[]{:S(2)}, u32[]{:S(2)}) collective-permute-start(bf16[256,2048]{1,0:T(8,128)(2,1)S(1)} %copy-done.79), channel_id=1, source_target_pairs={{0,8},{4,12},{8,0},{12,4},{16,24},{20,28},{24,16},{28,20},{1,9},{5... | collective-permute-start | bytes 3145736 | tf_op jit(solution)/shard_map/ppermute | solution.py:520
  812.9 49.7 %collective-permute-start.64 = (bf16[1024,2048]{1,0:T(8,128)(2,1)}, bf16[1024,2048]{1,0:T(8,128)(2,1)}, u32[]{:S(2)}, u32[]{:S(2)}) collective-permute-start(bf16[1024,2048]{1,0:T(8,128)(2,1)} %convolution_convert_fusion.3), channel_id=1, source_target_pairs={{0,4},{4,0},{8,12},{12,8},{16,20},{20,16},{24,28},{28,24},{1,5},{5... | collective-permute-start | bytes 12582920 | tf_op jit(solution)/shard_map/ppermute | solution.py:520
  815.6 39.2 %collective-permute-start.68 = (bf16[128,2048]{1,0:T(8,128)(2,1)}, bf16[128,2048]{1,0:T(8,128)(2,1)}, u32[]{:S(2)}, u32[]{:S(2)}) collective-permute-start(bf16[128,2048]{1,0:T(8,128)(2,1)} %slice.469), channel_id=1, source_target_pairs={{0,16},{4,20},{8,24},{12,28},{16,0},{20,4},{24,8},{28,12},{1,17},{... | collective-permute-start | bytes 1572872 | tf_op jit(solution)/shard_map/ppermute | solution.py:520
  822.3 35.7 %collective-permute-start.67 = (bf16[128,2048]{1,0:T(8,128)(2,1)}, bf16[128,2048]{1,0:T(8,128)(2,1)}, u32[]{:S(2)}, u32[]{:S(2)}) collective-permute-start(bf16[128,2048]{1,0:T(8,128)(2,1)} %slice.470), channel_id=1, source_target_pairs={{0,8},{4,12},{8,0},{12,4},{16,24},{20,28},{24,16},{28,20},{1,9},{5... | collective-permute-start | bytes 1572872 | tf_op jit(solution)/shard_map/ppermute | solution.py:520
  835.9 53.6 %all-to-all-start.1 = ((bf16[8,64,1024]{2,1,0:T(8,128)(2,1)}), bf16[8,64,1024]{2,1,0:T(8,128)(2,1)S(1)}, u32[]{:S(2)}, u32[]{:S(2)}) async-start(bf16[8,64,1024]{2,1,0:T(8,128)(2,1)} %reduce-scatter.3.cloned.1.call-done), calls=%async_computation.3 | async-start | bytes 2097152 | tf_op jit(solution)/shard_map/all_to_all | solution.py:800
  851.0 26.6 %collective-permute-start.78 = (bf16[17664]{0:T(1024)(128)(2,1)S(1)}, bf16[17664]{0:T(1024)(128)(2,1)S(1)}, u32[]{:S(2)}, u32[]{:S(2)}) collective-permute-start(bf16[17664]{0:T(1024)(128)(2,1)S(1)} %get-tuple-element.267), channel_id=1, source_target_pairs={{0,3},{1,0},{2,1},{3,2},{4,7},{5,4},{6,5},{7,6},{8,11},{9,8},{10,9... | collective-permute-start | bytes 105992 | tf_op jit(solution)/shard_map/ppermute | solution.py:456
  851.1 27.3 %collective-permute-start.77 = (bf16[17664]{0:T(1024)(128)(2,1)S(1)}, bf16[17664]{0:T(1024)(128)(2,1)S(1)}, u32[]{:S(2)}, u32[]{:S(2)}) collective-permute-start(bf16[17664]{0:T(1024)(128)(2,1)S(1)} %get-tuple-element.268), channel_id=1, source_target_pairs={{0,2},{1,3},{2,0},{3,1},{4,6},{5,7},{6,4},{7,5},{8,10},{9,11},{10,... | collective-permute-start | bytes 105992 | tf_op jit(solution)/shard_map/ppermute | solution.py:456
  854.9 25.4 %collective-permute-start.76 = (bf16[17664]{0:T(1024)(128)(2,1)S(1)}, bf16[17664]{0:T(1024)(128)(2,1)S(1)}, u32[]{:S(2)}, u32[]{:S(2)}) collective-permute-start(bf16[17664]{0:T(1024)(128)(2,1)S(1)} %get-tuple-element.266), channel_id=1, source_target_pairs={{0,1},{1,2},{2,3},{3,0},{4,5},{5,6},{6,7},{7,4},{8,9},{9,10},{10,1... | collective-permute-start | bytes 105992 | tf_op jit(solution)/shard_map/ppermute | solution.py:456
  860.7 26.1 %collective-permute-start.71 = (bf16[64,2048]{1,0:T(8,128)(2,1)}, bf16[64,2048]{1,0:T(8,128)(2,1)}, u32[]{:S(2)}, u32[]{:S(2)}) collective-permute-start(bf16[64,2048]{1,0:T(8,128)(2,1)} %get-tuple-element.288), channel_id=1, source_target_pairs={{0,3},{1,0},{2,1},{3,2},{4,7},{5,4},{6,5},{7,6},{8,11},{9,8},{10,9... | collective-permute-start | bytes 786440 | tf_op jit(solution)/shard_map/ppermute | solution.py:456
  (132 other events, 2295.0 us)
Sparse Core Ops, SparseCore 0:
  13.2 34.4 all-gather.4
  51.9 36.4 all-gather.6
  98.9 119.8 all-gather.8
  225.6 93.5 all-gather.10
  605.9 98.9 reduce-scatter.2
  707.1 99.4 reduce-scatter.4

commit v7 on v6

--- a/solution.py
+++ b/solution.py
@@ -14,7 +14,7 @@
 F32 = jnp.float32
 BF16 = jnp.bfloat16
 BOTH = ("dp", "fsdp")
-HASTE = 8
+HASTE = 64
 
 
 def dot_nn(left, right):
@@ -507,13 +507,14 @@
             [jnp.stack([2 * (me ^ o ^ core) + h for o, h in order]) for core in (0, 1)]
         ).astype(jnp.int32)
 
-    def lots(self, block, apart):
+    def start(self, block):
         size = block.shape[0] // 2
-        near = self.grow([block[:size], block[size:]])
-        near = list(apart(near))
+        return self.grow([block[:size], block[size:]])
+
+    def lots(self, near, near_sib):
         far = self.across(near, self.last)
+        far_sib = self.cross(far)
         mine = [far[0], near[0], far[1], near[1]]
-        near_sib, far_sib = self.cross(near), self.cross(far)
         return mine + [far_sib[0], near_sib[0], far_sib[1], near_sib[1]]
 
     def swap(self, block, bit):
@@ -591,23 +592,23 @@
         small_row = jnp.pad(small_row, (0, (lines - kv_lines) * width - small_row.shape[0]))
         places = plane.places()
 
-        query_own = lax.all_gather(query_weight, "fsdp", axis=0, tiled=True)
         grad_low = cotangent.reshape(rows, width)
         grad_near = plane.grow([grad_low[:half], grad_low[half:]])
+        query_pieces = line.gather(query_weight)
         packed = jnp.concatenate([kv_weight.reshape(kv_lines, width), small_row.reshape(-1, width)])
-        packed_pieces = line.gather(packed)
+        packed = lax.all_gather(packed, BOTH, axis=0, tiled=True)
         up_cols = lax.all_to_all(up_weight, "dp", 1, 0, tiled=True).reshape(n_dp, own, ff_own)
-        query_own, up_cols, out_weight, grad_near[0], grad_near[1], *packed_pieces = tie(
-            query_own, up_cols, out_weight, *grad_near, *packed_pieces
-        )
-
-        packed = lax.all_gather(line.in_order(packed_pieces), "dp", axis=0, tiled=True)
+        out_weight, *query_pieces = tie(out_weight, *query_pieces)
+
         out_pieces = line.gather(out_weight)
+        query_near = plane.start(line.in_order(query_pieces))
         inputs = tokens.reshape(rows, width).astype(F32)
         mean_one, recip_one = norm_stats(inputs)
-        query_lots = plane.lots(query_own, lambda near: near)
-        packed, mean_one, down_late = tie(packed, mean_one, down_weight)
+        packed, mean_one, up_cols, down_late, grad_near[0], grad_near[1], *query_near = tie(
+            packed, mean_one, up_cols, down_weight, *grad_near, *query_near
+        )
         down_part = lax.all_gather(down_late, "fsdp", axis=0, tiled=True)
+        query_sib, grad_near_sib = plane.cross(query_near), plane.cross(grad_near)
         packed = packed.reshape(n_dev, lines, width)
         full_kv = packed[:, :kv_lines].reshape(width, 2 * HD)
         small_all = packed[:, kv_lines:].reshape(n_dev, -1)
@@ -619,10 +620,16 @@
         normed_one = (xhat_one * gain_one + shift_one).astype(BF16)
         kv_bias = jnp.concatenate([jnp.zeros((HD,), F32), bias_v])
         key_value = (dot_nn(normed_one, full_kv) + kv_bias).astype(BF16)
-        key_value, normed_late, up_cols = tie(key_value, normed_one, up_cols)
-        up_part = lax.all_gather(up_cols, "fsdp", axis=1, tiled=True).reshape(width, ff_own)
+        late = len(query_sib + grad_near_sib)
+        key_value, normed_late, *arrived = tie(
+            key_value, normed_one, *query_sib, *grad_near_sib, *out_pieces
+        )
+        query_sib, grad_near_sib, out_pieces = arrived[:2], arrived[2:late], arrived[late:]
+        query_lots = plane.lots(query_near, query_sib)
         kv_pieces = line.gather(key_value.reshape(windows, local_len, 2 * HD))
-        normed_late, out_pieces[0], *query_lots = tie(normed_late, out_pieces[0], *query_lots)
+        normed_late, out_pieces[0], *arrived = tie(normed_late, out_pieces[0], *query_lots, *kv_pieces)
+        query_lots, kv_pieces = arrived[: len(query_lots)], arrived[len(query_lots) :]
+        out_near = plane.start(line.in_order(out_pieces))
         queries, one_mine, one_sib = lots_product(normed_late, places, query_lots, bias_q, BF16)
         kv_window = line.in_order(kv_pieces, 1)
 
@@ -630,18 +637,15 @@
         file_count = lengths.shape[1]
         upto = jnp.arange(file_count)[:, None] <= jnp.arange(file_count)[None, :]
         file_ends = jnp.sum(jnp.where(upto[None], lengths[:, :, None], 0), axis=1)
-        held = {}
-
-        def before_attention(near):
-            held["queries"], held["keys"], *near = tie(queries, kv_window, *near)
-            return near
-
-        out_lots = plane.lots(line.in_order(out_pieces), before_attention)
-        queries, kv_window = held["queries"], held["keys"]
+        out_sib = plane.cross(out_near)
+        queries, kv_window, up_cols, *arrived = tie(queries, kv_window, up_cols, *out_near, *out_sib)
+        up_part = lax.all_gather(up_cols, "fsdp", axis=1, tiled=True).reshape(width, ff_own)
+        out_lots = plane.lots(arrived[:2], arrived[2:])
         attended, norms = attn_forward(queries, kv_window, first, file_ends)
         attended, grad_near[0], grad_near[1], *out_lots = tie(attended, *grad_near, *out_lots)
         grad_far = plane.across(grad_near, plane.last)
         branch, att_mine, att_sib = lots_product(attended, places, out_lots, bias_o, F32)
+        branch, *grad_far = tie(branch, *grad_far)
         middle = inputs + branch
         mean_two, recip_two = norm_stats(middle)
         xhat_two = (middle - mean_two) * recip_two
@@ -649,9 +653,10 @@
 
         normed_two, *grad_near = tie(normed_two, *grad_near)
         two_near = plane.grow([normed_two[:half], normed_two[half:]])
-        two_near[0], two_near[1], *grad_far = tie(*two_near, *grad_far)
+        grad_far_sib = plane.cross(grad_far)
+        two_near[0], two_near[1], *grad_far_sib = tie(*two_near, *grad_far_sib)
         two_far = plane.across(two_near, plane.last)
-        grad_lots = [[*halves, *plane.cross(halves)] for halves in (grad_near, grad_far)]
+        grad_lots = [[*grad_near, *grad_near_sib], [*grad_far, *grad_far_sib]]
         two_lots = [[*two_near, *plane.cross(two_near)]]
         back_near = back_product(grad_lots[0], down_part)
         back_far = back_product(grad_lots[1], down_part)
@@ -727,7 +732,7 @@
         query_grad, kv_terms, *out_got = tie(query_grad, kv_terms, *out_got)
         kv_got = line.scatter(kv_terms.reshape(windows, n_z, local_len, 2 * HD), 1)
         theirs = plane.swap(dot_tn(one_sib, query_grad).astype(BF16), 1)
-        theirs, *wo_got = tie(theirs, *wo_got)
+        theirs, grad_up, *wo_got = tie(theirs, grad_up, *wo_got)
         wq_parts = cut(plus(one_mine, query_grad, theirs))
         wq_got = send_rows(wq_parts)
         wq_parts[1], query_late, hid_late = tie(wq_parts[1], query_grad, hid_near[1])
@@ -735,7 +740,7 @@
         query_part = lots_turned(query_late, places, query_lots, F32)
         kv_grad = total(kv_got).astype(BF16).reshape(rows, 2 * HD)
         wo_rows = own_rows(wo_parts, wo_got)
-        query_part, kv_grad, wo_rows = tie(query_part, kv_grad, wo_rows)
+        query_part, kv_grad, wo_rows, grad_down = tie(query_part, kv_grad, wo_rows, grad_down)
 
         one_grad = query_part + dot_nt(kv_grad, full_kv)
         grad_bq = jnp.sum(query_late.astype(F32), axis=0)
@@ -780,9 +785,9 @@
         kv_parts[1], hid_late, hid_near[0], *wq_got = tie(kv_parts[1], hid_late, hid_near[0], *wq_got)
         theirs = plane.swap(dot_nn(hid_late, down_part).astype(BF16), 1)
 
-        wo_last = line.scatter(wo_rows.reshape(n_z, own, width), 0)
-        wq_last = line.scatter(own_rows(wq_parts, wq_got).reshape(n_z, own, width), 0)
-        kv_parts_got[0], grad_up, grad_down = tie(kv_parts_got[0], grad_up, grad_down)
+        grad_wo = lax.psum_scatter(wo_rows.astype(BF16), "fsdp", scatter_dimension=0, tiled=True)
+        wq_rows = own_rows(wq_parts, wq_got).astype(BF16)
+        grad_wq = lax.psum_scatter(wq_rows, "fsdp", scatter_dimension=0, tiled=True)
         kv_last = own_rows(kv_parts, kv_parts_got).reshape(2, -1, 2 * HD)
         kv_rows = kv_last.shape[1] - more
         kv_last = jnp.concatenate(
@@ -808,9 +813,9 @@
         return (
             output,
             tokens_grad,
-            total(wq_last),
+            grad_wq.astype(F32),
             kv_own[: own * 2 * HD].reshape(own, 2 * HD),
-            total(wo_last),
+            grad_wo.astype(F32),
             bq,
             bv,
             bo,

time: 930 us -> 918 us (0.987)
  waiting for transfers between devices: 324 us -> 296 us
    ppermute x21 -> x15, waiting for transfers between devices: 96.7 us -> 62.9 us  [send(): lax.ppermute(block, 'fsdp', [(i, (i + places) % self.count) for i in rang...]
    ppermute x61, waiting for transfers between devices: 222 us -> 233 us  [swap(): return lax.ppermute(block, 'dp', [(i, i ^ bit) for i in range(self.count)])]
    unnamed x235 -> x202, local copies, waits for them, and re-layouts: 29.2 us -> 33.1 us
    ppermute x21 -> x15, starting transfers between devices: 60.2 us -> 63.7 us  [send(): lax.ppermute(block, 'fsdp', [(i, (i + places) % self.count) for i in rang...]
  transfers between devices with their start and end apart: 90 -> 85, of which waited for: 26 -> 29; matrix products, arithmetic and copies ran while one was open for 20% -> 23% of each run, Pallas kernels for 21% -> 21%
where the time goes in v7:
time: 918 us; the launch traced here: 908 us
  waiting for transfers between devices  296 us (32%)
  Pallas kernels  210 us (23%)
  starting transfers between devices  116 us (13%)
  other arithmetic  94.2 us (10%)
  matrix products  88.3 us (10%)
  local copies, waits for them, and re-layouts  86.9 us (9%)
  between operations  16 us (2%)
    ppermute x61, waiting for transfers between devices, swap(): return lax.ppermute(block, 'dp', [(i, i ^ bit) for i in range(self.count)])  233 us
    ppermute x15, starting transfers between devices, send(): lax.ppermute(block, 'fsdp', [(i, (i + places) % self.count) for i in rang...  63.7 us
    ppermute x15, waiting for transfers between devices, send(): lax.ppermute(block, 'fsdp', [(i, (i + places) % self.count) for i in rang...  62.9 us
    pallas_call x2, Pallas kernels, weight_grad(): pl.pallas_call(functools.partial(weight_kernel, count), out_shape=jax.Sha...  50.6 us
    ppermute x61, starting transfers between devices, swap(): return lax.ppermute(block, 'dp', [(i, i ^ bit) for i in range(self.count)])  43.3 us
    pallas_call x2, Pallas kernels, middle_layer(): pl.pallas_call(functools.partial(middle_kernel, count), out_shape=[jax.Sh...  39.9 us
    dot_general x7, matrix products, dot_nn(): return jnp.dot(left, right, preferred_element_type=F32)  35 us
    unnamed x202, local copies, waits for them, and re-layouts  33.1 us
  transfers between devices with their start and end apart: 85, of which 29 were waited for; matrix products, arithmetic and copies ran while one was open for 23% of the time, Pallas kernels for 21%

profile of v7, /device:TPU:0, one launch (start us, length us, event | category | flops | bytes accessed | tf_op | source)
XLA Modules:
  0.0 908.0 jit_solution(9142616586700158317)
XLA Ops:
  16.5 3.1 collective-permute-start.2
  23.5 3.1 slice_bitcast_fusion
  29.1 11.2 %collective-permute-done.3 = bf16[64,2048]{1,0:T(8,128)(2,1)S(1)} collective-permute-done((bf16[64,2048]{1,0:T(8,128)(2,1)}, bf16[64,2048]{1,0:T(8,128)(2,1)S(1)}, u32[]{:S(2)}, u32[]{:S(2)}) %collective-permute-start.3) | collective-permute-done | bytes 262176 | tf_op jit(solution)/shard_map/ppermute | solution.py:456
  49.7 4.2 all-to-all-start
  56.6 6.0 collective-permute-start.11
  62.6 3.9 collective-permute-done.5
  69.1 36.7 %collective-permute-done.6 = bf16[128,2048]{1,0:T(8,128)(2,1)S(1)} collective-permute-done((bf16[128,2048]{1,0:T(8,128)(2,1)S(1)}, bf16[128,2048]{1,0:T(8,128)(2,1)S(1)}, u32[]{:S(2)}, u32[]{:S(2)}) %collective-permute-start.6) | collective-permute-done | bytes 524320 | tf_op jit(solution)/shard_map/ppermute | solution.py:521
  105.7 7.8 collective-permute-start.13
  129.4 3.7 fusion.5
  136.4 9.9 %collective-permute-done.14.refs_2_.refs_0_ = bf16[256,2048]{1,0:T(8,128)(2,1)} collective-permute-done((bf16[256,2048]{1,0:T(8,128)(2,1)S(1)}, bf16[256,2048]{1,0:T(8,128)(2,1)}, u32[]{:S(2)}, u32[]{:S(2)}) %collective-permute-start.14) | collective-permute-done | bytes 1048608 | tf_op jit(solution)/shard_map/ppermute | solution.py:521
  147.1 3.3 fusion.21
  153.5 2.9 collective-permute-start.20
  157.0 7.0 collective-permute-done.18
  163.9 20.9 %collective-permute-done.19 = bf16[2,256,256]{2,1,0:T(8,128)(2,1)} collective-permute-done((bf16[2,256,256]{2,1,0:T(8,128)(2,1)}, bf16[2,256,256]{2,1,0:T(8,128)(2,1)}, u32[]{:S(2)}, u32[]{:S(2)}) %collective-permute-start.19) | collective-permute-done | bytes 262176 | tf_op jit(solution)/shard_map/ppermute | solution.py:456
  191.3 9.2 %collective-permute-done.21 = bf16[128,2048]{1,0:T(8,128)(2,1)S(1)} collective-permute-done((bf16[128,2048]{1,0:T(8,128)(2,1)S(1)}, bf16[128,2048]{1,0:T(8,128)(2,1)S(1)}, u32[]{:S(2)}, u32[]{:S(2)}) %collective-permute-start.21) | collective-permute-done | bytes 524320 | tf_op jit(solution)/shard_map/ppermute | solution.py:521
  205.1 9.7 %shard_map.288 = (bf16[512,2048]{1,0:T(8,128)(2,1)}, bf16[512,1024]{1,0:T(8,128)(2,1)S(1)}, bf16[512,1024]{1,0:T(8,128)(2,1)S(1)}) custom-call(s32[2,8]{1,0:T(2,128)S(1)} %pad_add_fusion.place_ref, bf16[512,2048]{1,0:T(8,128)(2,1)} %fusion.14.refs_0_, f32[1,2048]{1,0:T(1,128)S(1)} %reshape.412.refs_1_, ...), custom_call_target="tpu_custom_call" | custom-call | flops 67108864 | bytes 229376 | tf_op jit(solution)/shard_map/pallas_call | solution.py:367
  222.4 23.2 %collective-permute-done.25.refs_2_.refs_0_ = bf16[256,2048]{1,0:T(8,128)(2,1)} collective-permute-done((bf16[256,2048]{1,0:T(8,128)(2,1)S(1)}, bf16[256,2048]{1,0:T(8,128)(2,1)}, u32[]{:S(2)}, u32[]{:S(2)}) %collective-permute-start.25) | collective-permute-done | bytes 1048608 | tf_op jit(solution)/shard_map/ppermute | solution.py:521
  250.0 18.9 %shard_map.289 = (bf16[512,2048]{1,0:T(8,128)(2,1)S(1)}, f32[512,128]{1,0:T(8,128)S(1)}) custom-call(s32[1]{0:T(128)} %bitcast.19.pos_ref, s32[2,8]{1,0:T(2,128)S(1)} %select_reduce_fusion.ends_ref, bf16[512,2048]{1,0:T(8,128)(2,1)S(1)} %copy-done.16, bf16[2,1024,256]{2,1,0:T(8,128)(2,1)S(1)} %copy-done.3), custom_call_target="tpu_custom_call" | custom-call | flops 67108864 | bytes 65536 | tf_op jit(solution)/shard_map/pallas_call | solution.py:132
  271.7 10.2 %shard_map.290 = (f32[512,2048]{1,0:T(8,128)}, bf16[512,1024]{1,0:T(8,128)(2,1)S(1)}, bf16[512,1024]{1,0:T(8,128)(2,1)S(1)}) custom-call(s32[2,8]{1,0:T(2,128)S(1)} %pad_add_fusion.place_ref, bf16[512,2048]{1,0:T(8,128)(2,1)} %copy-done.20, f32[1,2048]{1,0:T(1,128)S(1)} %reshape.413.refs_1_, bf16[256,2048]{1,0:T(8,128)(2,1)} %collective-permute-done.25.refs_2_.refs_0_, ...), custom_call_target="tpu_custom_call" | custom-call | flops 67108864 | bytes 229376 | tf_op jit(solution)/shard_map/pallas_call | solution.py:367
  281.9 36.5 %collective-permute-done.29.refs_0_.refs_12_ = bf16[512,2048]{1,0:T(8,128)(2,1)} collective-permute-done((bf16[512,2048]{1,0:T(8,128)(2,1)S(1)}, bf16[512,2048]{1,0:T(8,128)(2,1)}, u32[]{:S(2)}, u32[]{:S(2)}) %collective-permute-start.29) | collective-permute-done | bytes 2097184 | tf_op jit(solution)/shard_map/ppermute | solution.py:521
  318.8 2.7 fusion.49
  326.5 23.0 %collective-permute-done.31 = bf16[256,2048]{1,0:T(8,128)(2,1)S(1)} collective-permute-done((bf16[256,2048]{1,0:T(8,128)(2,1)S(1)}, bf16[256,2048]{1,0:T(8,128)(2,1)S(1)}, u32[]{:S(2)}, u32[]{:S(2)}) %collective-permute-start.31) | collective-permute-done | bytes 1048608 | tf_op jit(solution)/shard_map/ppermute | solution.py:521
  355.2 44.5 %collective-permute-done.35.refs_0_.refs_4_ = bf16[512,2048]{1,0:T(8,128)(2,1)} collective-permute-done((bf16[512,2048]{1,0:T(8,128)(2,1)}, bf16[512,2048]{1,0:T(8,128)(2,1)}, u32[]{:S(2)}, u32[]{:S(2)}) %collective-permute-start.35) | collective-permute-done | bytes 2097184 | tf_op jit(solution)/shard_map/ppermute | solution.py:521
  403.4 13.3 %shard_map.291.refs_4_ = bf16[2048,1024]{1,0:T(8,128)(2,1)} custom-call(bf16[512,2048]{1,0:T(8,128)(2,1)S(1)} %pad_maximum_fusion.1.refs_0_.refs_8_, bf16[512,2048]{1,0:T(8,128)(2,1)S(1)} %copy-done.1, bf16[512,2048]{1,0:T(8,128)(2,1)} %collective-permute-done.9.refs_2_.refs_10_, bf16[512,2048]{1,0:T(8,128)(2,1)} %collective-permute-done.10.refs_3_.refs_11_, ...), custom_call_target="tpu_custom_call" | custom-call | flops 134217728 | bytes 262144 | tf_op jit(solution)/shard_map/pallas_call | solution.py:236
  416.7 14.6 %shard_map.292.refs_4_ = bf16[2048,1024]{1,0:T(8,128)(2,1)} custom-call(bf16[512,2048]{1,0:T(8,128)(2,1)} %collective-permute-done.29.refs_0_.refs_12_, bf16[512,2048]{1,0:T(8,128)(2,1)} %collective-permute-done.30.refs_1_.refs_13_, bf16[512,2048]{1,0:T(8,128)(2,1)} %collective-permute-done.33.refs_2_.refs_14_, ...), custom_call_target="tpu_custom_call" | custom-call | flops 134217728 | bytes 262144 | tf_op jit(solution)/shard_map/pallas_call | solution.py:236
  431.3 19.8 %shard_map.293 = (bf16[1024,1024]{1,0:T(8,128)(2,1)S(1)}, bf16[1024,1024]{1,0:T(8,128)(2,1)S(1)}, bf16[1024,1024]{1,0:T(8,128)(2,1)}, bf16[1024,1024]{1,0:T(8,128)(2,1)}) custom-call(bf16[512,2048]{1,0:T(8,128)(2,1)} %pad_maximum_fusion.3.refs_0_, bf16[512,2048]{1,0:T(8,128)(2,1)} %pad_maximum_fusion.4.refs_1_, ...), custom_call_target="tpu_custom_call" | custom-call | flops 134217728 | bytes 393216 | tf_op jit(solution)/shard_map/pallas_call | solution.py:202
  453.8 20.0 %shard_map.294 = (bf16[1024,1024]{1,0:T(8,128)(2,1)S(1)}, bf16[1024,1024]{1,0:T(8,128)(2,1)S(1)}, bf16[1024,1024]{1,0:T(8,128)(2,1)}, bf16[1024,1024]{1,0:T(8,128)(2,1)}) custom-call(bf16[512,2048]{1,0:T(8,128)(2,1)} %collective-permute-done.35.refs_0_.refs_4_, bf16[512,2048]{1,0:T(8,128)(2,1)} %collective-permute-done.36.refs_1_.refs_5_, ...), custom_call_target="tpu_custom_call" | custom-call | flops 134217728 | bytes 393216 | tf_op jit(solution)/shard_map/pallas_call | solution.py:202
  473.8 4.6 convolution_convert_fusion.8
  482.8 3.7 add_convert_fusion.7
  486.5 3.7 add_convert_fusion.6
  490.2 4.8 convolution_convert_fusion.4
  496.5 5.9 collective-permute-done.43
  502.4 24.4 %shard_map.295 = bf16[2048,1024]{1,0:T(8,128)(2,1)} custom-call(bf16[512,2048]{1,0:T(8,128)(2,1)} %pad_maximum_fusion.3.refs_0_, bf16[512,2048]{1,0:T(8,128)(2,1)} %pad_maximum_fusion.4.refs_1_, bf16[512,2048]{1,0:T(8,128)(2,1)} %collective-permute-done.39.refs_2_, bf16[512,2048]{1,0:T(8,128)(2,1)} %collective-permute-done.40.refs_3_, ...), custom_call_target="tpu_custom_call" | custom-call | flops 268435456 | bytes 458752 | tf_op jit(solution)/shard_map/pallas_call | solution.py:276
  526.8 8.2 add_convert_fusion.3
  535.0 8.4 collective-permute-done.45
  543.8 4.7 convert_add_fusion.3
  553.7 3.7 convolution_convert_fusion.6
  557.4 3.7 convolution_convert_fusion.5
  561.7 26.2 %shard_map.296 = bf16[1024,2048]{1,0:T(8,128)(2,1)} custom-call(bf16[1024,1024]{1,0:T(8,128)(2,1)} %copy-done.9, bf16[1024,1024]{1,0:T(8,128)(2,1)} %copy-done.9, bf16[1024,1024]{1,0:T(8,128)(2,1)} %copy-done.11, bf16[1024,1024]{1,0:T(8,128)(2,1)} %copy-done.11, bf16[1024,1024]{1,0:T(8,128)(2,1)} %copy-done.13, bf16[1024,1024]{1,0:T(8,128)(2,1)} %copy-done.13, ...), custom_call_target="tpu_custom_call" | custom-call | flops 268435456 | bytes 458752 | tf_op jit(solution)/shard_map/pallas_call | solution.py:276
  595.5 5.3 add_convert_fusion.5
  600.8 5.5 add_convert_fusion.4
  612.9 4.5 convolution_convert_fusion.2
  620.2 11.0 %shard_map.297.grad_ref = bf16[512,2048]{1,0:T(8,128)(2,1)} custom-call(s32[2,8]{1,0:T(2,128)S(1)} %pad_add_fusion.place_ref, bf16[512,2048]{1,0:T(8,128)(2,1)} %copy-done.57, bf16[256,2048]{1,0:T(8,128)(2,1)} %collective-permute-done.25.refs_2_.refs_0_, bf16[256,2048]{1,0:T(8,128)(2,1)S(1)} %pad_maximum_fusion.9.refs_3_.refs_1_, ...), custom_call_target="tpu_custom_call" | custom-call | flops 67108864 | bytes 196608 | tf_op jit(solution)/shard_map/pallas_call | solution.py:414
  631.2 4.6 add_convert_fusion.2
  638.0 31.0 %shard_map.298 = (bf16[512,2048]{1,0:T(8,128)(2,1)S(1)}, bf16[2,1024,256]{2,1,0:T(8,128)(2,1)S(1)}) custom-call(s32[1]{0:T(128)} %bitcast.19.pos_ref, s32[2,8]{1,0:T(2,128)S(1)} %select_reduce_fusion.ends_ref, bf16[512,2048]{1,0:T(8,128)(2,1)} %get-tuple-element.189.q_ref, bf16[2,1024,256]{2,1,0:T(8,128)(2,1)S(1)} %copy-done.4, ...), custom_call_target="tpu_custom_call" | custom-call | flops 167772160 | bytes 163840 | tf_op jit(solution)/shard_map/pallas_call | solution.py:152
  669.0 4.5 convolution_convert_fusion.1
  684.9 23.7 %collective-permute-start.56 = (bf16[2,256,256]{2,1,0:T(8,128)(2,1)}, bf16[2,256,256]{2,1,0:T(8,128)(2,1)S(1)}, u32[]{:S(2)}, u32[]{:S(2)}) collective-permute-start(bf16[2,256,256]{2,1,0:T(8,128)(2,1)} %get-tuple-element.333), channel_id=1, source_target_pairs={{0,1},{1,2},{2,3},{3,0},{4,5},{5,6},{6,7},{7,4},{8,9},{9,10},{10,1... | collective-permute-start | bytes 786440 | tf_op jit(solution)/shard_map/ppermute | solution.py:456
  708.6 2.8 collective-permute-start.58
  716.1 4.6 add_convert_fusion.1
  722.6 3.7 convert_add_fusion.8
  726.8 9.1 %collective-permute-done.57 = bf16[2,256,256]{2,1,0:T(8,128)(2,1)} collective-permute-done((bf16[2,256,256]{2,1,0:T(8,128)(2,1)}, bf16[2,256,256]{2,1,0:T(8,128)(2,1)}, u32[]{:S(2)}, u32[]{:S(2)}) %collective-permute-start.57) | collective-permute-done | bytes 262176 | tf_op jit(solution)/shard_map/ppermute | solution.py:456
  735.9 13.7 %collective-permute-done.58 = bf16[2,256,256]{2,1,0:T(8,128)(2,1)} collective-permute-done((bf16[2,256,256]{2,1,0:T(8,128)(2,1)}, bf16[2,256,256]{2,1,0:T(8,128)(2,1)}, u32[]{:S(2)}, u32[]{:S(2)}) %collective-permute-start.58) | collective-permute-done | bytes 262176 | tf_op jit(solution)/shard_map/ppermute | solution.py:456
  754.9 4.3 all-to-all-start.1
  763.6 11.0 %shard_map.299 = f32[512,2048]{1,0:T(8,128)} custom-call(s32[2,8]{1,0:T(2,128)S(1)} %pad_add_fusion.place_ref, bf16[512,2048]{1,0:T(8,128)(2,1)} %copy-done.17, bf16[256,2048]{1,0:T(8,128)(2,1)} %collective-permute-done.14.refs_2_.refs_0_, bf16[256,2048]{1,0:T(8,128)(2,1)S(1)} %copy-done.7, bf16[256,2048]{1,0:T(8,128)(2,1)} %collective-permute-done.15.refs_4_.refs_2_, ...), custom_call_target="tpu_custom_call" | custom-call | flops 67108864 | bytes 196608 | tf_op jit(solution)/shard_map/pallas_call | solution.py:414
  779.9 5.5 fusion.16
  793.0 5.4 fusion.20
  803.1 6.0 convolution_convert_fusion.3
  820.7 9.7 %collective-permute-done.69 = bf16[288,256]{1,0:T(8,128)(2,1)S(1)} collective-permute-done((bf16[288,256]{1,0:T(8,128)(2,1)S(1)}, bf16[288,256]{1,0:T(8,128)(2,1)S(1)}, u32[]{:S(2)}, u32[]{:S(2)}) %collective-permute-start.69) | collective-permute-done | bytes 147488 | tf_op jit(solution)/shard_map/ppermute | solution.py:521
  835.8 10.2 %collective-permute-start.75 = (bf16[17664]{0:T(1024)(128)(2,1)S(1)}, bf16[17664]{0:T(1024)(128)(2,1)}, u32[]{:S(2)}, u32[]{:S(2)}) collective-permute-start(bf16[17664]{0:T(1024)(128)(2,1)S(1)} %get-tuple-element.301), channel_id=1, source_target_pairs={{0,3},{1,0},{2,1},{3,2},{4,7},{5,4},{6,5},{7,6},{8,11},{9,8},{10,9... | collective-permute-start | bytes 105992 | tf_op jit(solution)/shard_map/ppermute | solution.py:456
  851.0 7.5 add_convert_fusion
  858.5 5.4 convert_add_fusion.2
  872.1 2.7 slice.472
  883.1 6.4 collective-permute-done.66
  891.4 5.6 collective-permute-done.65
  (518 shorter events, 217.0 us)
Async XLA Ops:
  7.2 111.0 %all-gather.4.cloned.1.call-start = ((), (), s32[]{:S(2)}) async-start(), calls=%async_computation.6 | async-start | bytes 2162688 | tf_op jit(solution)/shard_map/all_gather | solution.py:599
  19.5 20.7 %collective-permute-start.3 = (bf16[64,2048]{1,0:T(8,128)(2,1)}, bf16[64,2048]{1,0:T(8,128)(2,1)S(1)}, u32[]{:S(2)}, u32[]{:S(2)}) collective-permute-start(bf16[64,2048]{1,0:T(8,128)(2,1)} %param.20), channel_id=1, source_target_pairs={{0,2},{1,3},{2,0},{3,1},{4,6},{5,7},{6,4},{7,5},{8,10},{9,11},{10,... | collective-permute-start | bytes 786440 | tf_op jit(solution)/shard_map/ppermute | solution.py:456
  26.6 88.0 %collective-permute-start = (bf16[256,2048]{1,0:T(8,128)(2,1)}, bf16[256,2048]{1,0:T(8,128)(2,1)}, u32[]{:S(2)}, u32[]{:S(2)}) collective-permute-start(bf16[256,2048]{1,0:T(8,128)(2,1)} %get-tuple-element.323), channel_id=1, source_target_pairs={{0,8},{4,12},{8,0},{12,4},{16,24},{20,28},{24,16},{28,20},{1,9},{5... | collective-permute-start | bytes 3145736 | tf_op jit(solution)/shard_map/ppermute | solution.py:521
  49.7 68.4 %all-to-all-start = ((bf16[64,8,1024]{2,0,1:T(8,128)(2,1)}), bf16[64,8,1024]{2,0,1:T(8,128)(2,1)}, u32[]{:S(2)}, u32[]{:S(2)}) async-start(bf16[64,8,1024]{2,0,1:T(8,128)(2,1)} %bitcast.143), calls=%async_computation | async-start | bytes 2097152 | tf_op jit(solution)/shard_map/all_to_all | solution.py:600
  54.0 347.7 %all-gather.6.cloned.1.call-start = ((), (), s32[]{:S(2)}) async-start(), calls=%async_computation.7 | async-start | bytes 5242880 | tf_op jit(solution)/shard_map/all_gather | solution.py:610
  54.1 62.3 %collective-permute-start.1 = (bf16[256,2048]{1,0:T(8,128)(2,1)}, bf16[256,2048]{1,0:T(8,128)(2,1)S(1)}, u32[]{:S(2)}, u32[]{:S(2)}) collective-permute-start(bf16[256,2048]{1,0:T(8,128)(2,1)} %get-tuple-element.322), channel_id=1, source_target_pairs={{0,16},{4,20},{8,24},{12,28},{16,0},{20,4},{24,8},{28,12},{1,17},{... | collective-permute-start | bytes 3145736 | tf_op jit(solution)/shard_map/ppermute | solution.py:521
  55.9 49.8 %collective-permute-start.6 = (bf16[128,2048]{1,0:T(8,128)(2,1)S(1)}, bf16[128,2048]{1,0:T(8,128)(2,1)S(1)}, u32[]{:S(2)}, u32[]{:S(2)}) collective-permute-start(bf16[128,2048]{1,0:T(8,128)(2,1)S(1)} %copy-done.68), channel_id=1, source_target_pairs={{0,16},{4,20},{8,24},{12,28},{16,0},{20,4},{24,8},{28,12},{1,17},{... | collective-permute-start | bytes 1572872 | tf_op jit(solution)/shard_map/ppermute | solution.py:521
  56.6 64.4 %collective-permute-start.11 = (bf16[64,2048]{1,0:T(8,128)(2,1)S(1)}, bf16[64,2048]{1,0:T(8,128)(2,1)}, u32[]{:S(2)}, u32[]{:S(2)}) collective-permute-start(bf16[64,2048]{1,0:T(8,128)(2,1)S(1)} %copy-done.74), channel_id=1, source_target_pairs={{0,1},{1,2},{2,3},{3,0},{4,5},{5,6},{6,7},{7,4},{8,9},{9,10},{10,1... | collective-permute-start | bytes 786440 | tf_op jit(solution)/shard_map/ppermute | solution.py:456
  66.5 54.7 %collective-permute-start.12 = (bf16[64,2048]{1,0:T(8,128)(2,1)S(1)}, bf16[64,2048]{1,0:T(8,128)(2,1)}, u32[]{:S(2)}, u32[]{:S(2)}) collective-permute-start(bf16[64,2048]{1,0:T(8,128)(2,1)S(1)} %copy-done.74), channel_id=1, source_target_pairs={{0,2},{1,3},{2,0},{3,1},{4,6},{5,7},{6,4},{7,5},{8,10},{9,11},{10,... | collective-permute-start | bytes 786440 | tf_op jit(solution)/shard_map/ppermute | solution.py:456
  120.5 25.7 %collective-permute-start.14 = (bf16[256,2048]{1,0:T(8,128)(2,1)S(1)}, bf16[256,2048]{1,0:T(8,128)(2,1)}, u32[]{:S(2)}, u32[]{:S(2)}) collective-permute-start(bf16[256,2048]{1,0:T(8,128)(2,1)S(1)} %pad_maximum_fusion.7.refs_3_.refs_1_), channel_id=1, source_target_pairs={{0,16},{4,20},{8,24},{12,28},{16,0},{20,4},{24,8},{28,12},{1,17},{... | collective-permute-start | bytes 3145736 | tf_op jit(solution)/shard_map/ppermute | solution.py:521
  120.9 31.6 %collective-permute-start.9 = (bf16[512,2048]{1,0:T(8,128)(2,1)S(1)}, bf16[512,2048]{1,0:T(8,128)(2,1)}, u32[]{:S(2)}, u32[]{:S(2)}) collective-permute-start(bf16[512,2048]{1,0:T(8,128)(2,1)S(1)} %pad_maximum_fusion.1.refs_0_.refs_8_), channel_id=1, source_target_pairs={{0,4},{4,0},{8,12},{12,8},{16,20},{20,16},{24,28},{28,24},{1,5},{5... | collective-permute-start | bytes 6291464 | tf_op jit(solution)/shard_map/ppermute | solution.py:521
  121.2 31.4 %collective-permute-start.10 = (bf16[512,2048]{1,0:T(8,128)(2,1)}, bf16[512,2048]{1,0:T(8,128)(2,1)}, u32[]{:S(2)}, u32[]{:S(2)}) collective-permute-start(bf16[512,2048]{1,0:T(8,128)(2,1)} %pad_maximum_fusion.2.refs_1_.refs_9_), channel_id=1, source_target_pairs={{0,4},{4,0},{8,12},{12,8},{16,20},{20,16},{24,28},{28,24},{1,5},{5... | collective-permute-start | bytes 6291464 | tf_op jit(solution)/shard_map/ppermute | solution.py:521
  121.4 25.6 %collective-permute-start.15 = (bf16[256,2048]{1,0:T(8,128)(2,1)}, bf16[256,2048]{1,0:T(8,128)(2,1)}, u32[]{:S(2)}, u32[]{:S(2)}) collective-permute-start(bf16[256,2048]{1,0:T(8,128)(2,1)} %pad_maximum_fusion.8.refs_5_.refs_3_), channel_id=1, source_target_pairs={{0,8},{4,12},{8,0},{12,4},{16,24},{20,28},{24,16},{28,20},{1,9},{5... | collective-permute-start | bytes 3145736 | tf_op jit(solution)/shard_map/ppermute | solution.py:521
  129.3 23.2 %collective-permute-start.8 = (bf16[256,2048]{1,0:T(8,128)(2,1)}, bf16[256,2048]{1,0:T(8,128)(2,1)}, u32[]{:S(2)}, u32[]{:S(2)}) collective-permute-start(bf16[256,2048]{1,0:T(8,128)(2,1)} %pad_maximum_fusion.8.refs_5_.refs_3_), channel_id=1, source_target_pairs={{0,4},{4,0},{8,12},{12,8},{16,20},{20,16},{24,28},{28,24},{1,5},{5... | collective-permute-start | bytes 3145736 | tf_op jit(solution)/shard_map/ppermute | solution.py:521
  152.6 32.3 %collective-permute-start.19 = (bf16[2,256,256]{2,1,0:T(8,128)(2,1)}, bf16[2,256,256]{2,1,0:T(8,128)(2,1)}, u32[]{:S(2)}, u32[]{:S(2)}) collective-permute-start(bf16[2,256,256]{2,1,0:T(8,128)(2,1)} %bitcast.26), channel_id=1, source_target_pairs={{0,2},{1,3},{2,0},{3,1},{4,6},{5,7},{6,4},{7,5},{8,10},{9,11},{10,... | collective-permute-start | bytes 786440 | tf_op jit(solution)/shard_map/ppermute | solution.py:456
  153.5 31.4 %collective-permute-start.20 = (bf16[2,256,256]{2,1,0:T(8,128)(2,1)}, bf16[2,256,256]{2,1,0:T(8,128)(2,1)}, u32[]{:S(2)}, u32[]{:S(2)}) collective-permute-start(bf16[2,256,256]{2,1,0:T(8,128)(2,1)} %bitcast.26), channel_id=1, source_target_pairs={{0,3},{1,0},{2,1},{3,2},{4,7},{5,4},{6,5},{7,6},{8,11},{9,8},{10,9... | collective-permute-start | bytes 786440 | tf_op jit(solution)/shard_map/ppermute | solution.py:456
  156.4 274.8 %all-gather.8.cloned.1.call-start = ((), (), s32[]{:S(2)}) async-start(), calls=%async_computation.8 | async-start | bytes 5242880 | tf_op jit(solution)/shard_map/all_gather | solution.py:642
  220.0 25.7 %collective-permute-start.25 = (bf16[256,2048]{1,0:T(8,128)(2,1)S(1)}, bf16[256,2048]{1,0:T(8,128)(2,1)}, u32[]{:S(2)}, u32[]{:S(2)}) collective-permute-start(bf16[256,2048]{1,0:T(8,128)(2,1)S(1)} %pad_maximum_fusion.9.refs_3_.refs_1_), channel_id=1, source_target_pairs={{0,16},{4,20},{8,24},{12,28},{16,0},{20,4},{24,8},{28,12},{1,17},{... | collective-permute-start | bytes 3145736 | tf_op jit(solution)/shard_map/ppermute | solution.py:521
  221.5 25.6 %collective-permute-start.26 = (bf16[256,2048]{1,0:T(8,128)(2,1)}, bf16[256,2048]{1,0:T(8,128)(2,1)}, u32[]{:S(2)}, u32[]{:S(2)}) collective-permute-start(bf16[256,2048]{1,0:T(8,128)(2,1)} %pad_maximum_fusion.10.refs_5_.refs_3_), channel_id=1, source_target_pairs={{0,8},{4,12},{8,0},{12,4},{16,24},{20,28},{24,16},{28,20},{1,9},{5... | collective-permute-start | bytes 3145736 | tf_op jit(solution)/shard_map/ppermute | solution.py:521
  245.7 24.5 %collective-permute-start.27 = (bf16[256,2048]{1,0:T(8,128)(2,1)}, bf16[256,2048]{1,0:T(8,128)(2,1)}, u32[]{:S(2)}, u32[]{:S(2)}) collective-permute-start(bf16[256,2048]{1,0:T(8,128)(2,1)} %collective-permute-done.25.refs_2_.refs_0_), channel_id=1, source_target_pairs={{0,4},{4,0},{8,12},{12,8},{16,20},{20,16},{24,28},{28,24},{1,5},{5... | collective-permute-start | bytes 3145736 | tf_op jit(solution)/shard_map/ppermute | solution.py:521
  247.1 23.1 %collective-permute-start.28 = (bf16[256,2048]{1,0:T(8,128)(2,1)}, bf16[256,2048]{1,0:T(8,128)(2,1)}, u32[]{:S(2)}, u32[]{:S(2)}) collective-permute-start(bf16[256,2048]{1,0:T(8,128)(2,1)} %collective-permute-done.26.refs_4_.refs_2_), channel_id=1, source_target_pairs={{0,4},{4,0},{8,12},{12,8},{16,20},{20,16},{24,28},{28,24},{1,5},{5... | collective-permute-start | bytes 3145736 | tf_op jit(solution)/shard_map/ppermute | solution.py:521
  270.2 48.1 %collective-permute-start.29 = (bf16[512,2048]{1,0:T(8,128)(2,1)S(1)}, bf16[512,2048]{1,0:T(8,128)(2,1)}, u32[]{:S(2)}, u32[]{:S(2)}) collective-permute-start(bf16[512,2048]{1,0:T(8,128)(2,1)S(1)} %pad_maximum_fusion.1.refs_0_.refs_8_), channel_id=1, source_target_pairs={{0,16},{4,20},{8,24},{12,28},{16,0},{20,4},{24,8},{28,12},{1,17},{... | collective-permute-start | bytes 6291464 | tf_op jit(solution)/shard_map/ppermute | solution.py:521
  270.8 48.0 %collective-permute-start.30 = (bf16[512,2048]{1,0:T(8,128)(2,1)}, bf16[512,2048]{1,0:T(8,128)(2,1)}, u32[]{:S(2)}, u32[]{:S(2)}) collective-permute-start(bf16[512,2048]{1,0:T(8,128)(2,1)} %pad_maximum_fusion.2.refs_1_.refs_9_), channel_id=1, source_target_pairs={{0,8},{4,12},{8,0},{12,4},{16,24},{20,28},{24,16},{28,20},{1,9},{5... | collective-permute-start | bytes 6291464 | tf_op jit(solution)/shard_map/ppermute | solution.py:521
  271.6 439.8 %reduce-scatter.5.cloned.1.call-start = ((), (), s32[]{:S(2)}) async-start(), calls=%async_computation.9 | async-start | bytes 5242880 | tf_op jit(solution)/shard_map/reduce_scatter | solution.py:691
  323.6 29.0 %collective-permute-start.33 = (bf16[512,2048]{1,0:T(8,128)(2,1)}, bf16[512,2048]{1,0:T(8,128)(2,1)}, u32[]{:S(2)}, u32[]{:S(2)}) collective-permute-start(bf16[512,2048]{1,0:T(8,128)(2,1)} %collective-permute-done.29.refs_0_.refs_12_), channel_id=1, source_target_pairs={{0,4},{4,0},{8,12},{12,8},{16,20},{20,16},{24,28},{28,24},{1,5},{5... | collective-permute-start | bytes 6291464 | tf_op jit(solution)/shard_map/ppermute | solution.py:521
  323.6 29.0 %collective-permute-start.34 = (bf16[512,2048]{1,0:T(8,128)(2,1)}, bf16[512,2048]{1,0:T(8,128)(2,1)}, u32[]{:S(2)}, u32[]{:S(2)}) collective-permute-start(bf16[512,2048]{1,0:T(8,128)(2,1)} %collective-permute-done.30.refs_1_.refs_13_), channel_id=1, source_target_pairs={{0,4},{4,0},{8,12},{12,8},{16,20},{20,16},{24,28},{28,24},{1,5},{5... | collective-permute-start | bytes 6291464 | tf_op jit(solution)/shard_map/ppermute | solution.py:521
  324.4 25.1 %collective-permute-start.31 = (bf16[256,2048]{1,0:T(8,128)(2,1)S(1)}, bf16[256,2048]{1,0:T(8,128)(2,1)S(1)}, u32[]{:S(2)}, u32[]{:S(2)}) collective-permute-start(bf16[256,2048]{1,0:T(8,128)(2,1)S(1)} %get-tuple-element.319), channel_id=1, source_target_pairs={{0,8},{4,12},{8,0},{12,4},{16,24},{20,28},{24,16},{28,20},{1,9},{5... | collective-permute-start | bytes 3145736 | tf_op jit(solution)/shard_map/ppermute | solution.py:521
  324.9 26.1 %collective-permute-start.32 = (bf16[256,2048]{1,0:T(8,128)(2,1)S(1)}, bf16[256,2048]{1,0:T(8,128)(2,1)S(1)}, u32[]{:S(2)}, u32[]{:S(2)}) collective-permute-start(bf16[256,2048]{1,0:T(8,128)(2,1)S(1)} %get-tuple-element.318), channel_id=1, source_target_pairs={{0,16},{4,20},{8,24},{12,28},{16,0},{20,4},{24,8},{28,12},{1,17},{... | collective-permute-start | bytes 3145736 | tf_op jit(solution)/shard_map/ppermute | solution.py:521
  352.6 47.1 %collective-permute-start.35 = (bf16[512,2048]{1,0:T(8,128)(2,1)}, bf16[512,2048]{1,0:T(8,128)(2,1)}, u32[]{:S(2)}, u32[]{:S(2)}) collective-permute-start(bf16[512,2048]{1,0:T(8,128)(2,1)} %pad_maximum_fusion.3.refs_0_), channel_id=1, source_target_pairs={{0,16},{4,20},{8,24},{12,28},{16,0},{20,4},{24,8},{28,12},{1,17},{... | collective-permute-start | bytes 6291464 | tf_op jit(solution)/shard_map/ppermute | solution.py:521
  354.1 46.8 %collective-permute-start.36 = (bf16[512,2048]{1,0:T(8,128)(2,1)}, bf16[512,2048]{1,0:T(8,128)(2,1)}, u32[]{:S(2)}, u32[]{:S(2)}) collective-permute-start(bf16[512,2048]{1,0:T(8,128)(2,1)} %pad_maximum_fusion.4.refs_1_), channel_id=1, source_target_pairs={{0,8},{4,12},{8,0},{12,4},{16,24},{20,28},{24,16},{28,20},{1,9},{5... | collective-permute-start | bytes 6291464 | tf_op jit(solution)/shard_map/ppermute | solution.py:521
  354.7 76.6 %collective-permute-start.39 = (bf16[512,2048]{1,0:T(8,128)(2,1)}, bf16[512,2048]{1,0:T(8,128)(2,1)}, u32[]{:S(2)}, u32[]{:S(2)}) collective-permute-start(bf16[512,2048]{1,0:T(8,128)(2,1)} %pad_maximum_fusion.3.refs_0_), channel_id=1, source_target_pairs={{0,4},{4,0},{8,12},{12,8},{16,20},{20,16},{24,28},{28,24},{1,5},{5... | collective-permute-start | bytes 6291464 | tf_op jit(solution)/shard_map/ppermute | solution.py:521
  354.7 76.6 %collective-permute-start.40 = (bf16[512,2048]{1,0:T(8,128)(2,1)}, bf16[512,2048]{1,0:T(8,128)(2,1)}, u32[]{:S(2)}, u32[]{:S(2)}) collective-permute-start(bf16[512,2048]{1,0:T(8,128)(2,1)} %pad_maximum_fusion.4.refs_1_), channel_id=1, source_target_pairs={{0,4},{4,0},{8,12},{12,8},{16,20},{20,16},{24,28},{28,24},{1,5},{5... | collective-permute-start | bytes 6291464 | tf_op jit(solution)/shard_map/ppermute | solution.py:521
  399.7 54.0 %collective-permute-start.37 = (bf16[512,2048]{1,0:T(8,128)(2,1)}, bf16[512,2048]{1,0:T(8,128)(2,1)}, u32[]{:S(2)}, u32[]{:S(2)}) collective-permute-start(bf16[512,2048]{1,0:T(8,128)(2,1)} %collective-permute-done.35.refs_0_.refs_4_), channel_id=1, source_target_pairs={{0,4},{4,0},{8,12},{12,8},{16,20},{20,16},{24,28},{28,24},{1,5},{5... | collective-permute-start | bytes 6291464 | tf_op jit(solution)/shard_map/ppermute | solution.py:521
  401.0 52.8 %collective-permute-start.38 = (bf16[512,2048]{1,0:T(8,128)(2,1)}, bf16[512,2048]{1,0:T(8,128)(2,1)}, u32[]{:S(2)}, u32[]{:S(2)}) collective-permute-start(bf16[512,2048]{1,0:T(8,128)(2,1)} %collective-permute-done.36.refs_1_.refs_5_), channel_id=1, source_target_pairs={{0,4},{4,0},{8,12},{12,8},{16,20},{20,16},{24,28},{28,24},{1,5},{5... | collective-permute-start | bytes 6291464 | tf_op jit(solution)/shard_map/ppermute | solution.py:521
  495.5 47.9 %collective-permute-start.45 = (bf16[512,2048]{1,0:T(8,128)(2,1)}, bf16[512,2048]{1,0:T(8,128)(2,1)S(1)}, u32[]{:S(2)}, u32[]{:S(2)}) collective-permute-start(bf16[512,2048]{1,0:T(8,128)(2,1)} %add_convert_fusion.6), channel_id=1, source_target_pairs={{0,8},{4,12},{8,0},{12,4},{16,24},{20,28},{24,16},{28,20},{1,9},{5... | collective-permute-start | bytes 6291464 | tf_op jit(solution)/shard_map/ppermute | solution.py:521
  496.1 47.7 %collective-permute-start.44 = (bf16[512,2048]{1,0:T(8,128)(2,1)}, bf16[512,2048]{1,0:T(8,128)(2,1)}, u32[]{:S(2)}, u32[]{:S(2)}) collective-permute-start(bf16[512,2048]{1,0:T(8,128)(2,1)} %add_convert_fusion.7), channel_id=1, source_target_pairs={{0,16},{4,20},{8,24},{12,28},{16,0},{20,4},{24,8},{28,12},{1,17},{... | collective-permute-start | bytes 6291464 | tf_op jit(solution)/shard_map/ppermute | solution.py:521
  549.6 38.3 %collective-permute-start.47 = (bf16[256,2048]{1,0:T(8,128)(2,1)}, bf16[256,2048]{1,0:T(8,128)(2,1)}, u32[]{:S(2)}, u32[]{:S(2)}) collective-permute-start(bf16[256,2048]{1,0:T(8,128)(2,1)} %slice.473), channel_id=1, source_target_pairs={{0,16},{4,20},{8,24},{12,28},{16,0},{20,4},{24,8},{28,12},{1,17},{... | collective-permute-start | bytes 3145736 | tf_op jit(solution)/shard_map/ppermute | solution.py:521
  551.4 39.0 %collective-permute-start.46 = (bf16[256,2048]{1,0:T(8,128)(2,1)}, bf16[256,2048]{1,0:T(8,128)(2,1)}, u32[]{:S(2)}, u32[]{:S(2)}) collective-permute-start(bf16[256,2048]{1,0:T(8,128)(2,1)} %slice.474), channel_id=1, source_target_pairs={{0,8},{4,12},{8,0},{12,4},{16,24},{20,28},{24,16},{28,20},{1,9},{5... | collective-permute-start | bytes 3145736 | tf_op jit(solution)/shard_map/ppermute | solution.py:521
  557.4 35.7 %collective-permute-start.48 = (bf16[512,2048]{1,0:T(8,128)(2,1)}, bf16[512,2048]{1,0:T(8,128)(2,1)}, u32[]{:S(2)}, u32[]{:S(2)}) collective-permute-start(bf16[512,2048]{1,0:T(8,128)(2,1)} %convolution_convert_fusion.6), channel_id=1, source_target_pairs={{0,4},{4,0},{8,12},{12,8},{16,20},{20,16},{24,28},{28,24},{1,5},{5... | collective-permute-start | bytes 6291464 | tf_op jit(solution)/shard_map/ppermute | solution.py:521
  561.1 39.7 %collective-permute-start.49 = (bf16[512,2048]{1,0:T(8,128)(2,1)}, bf16[512,2048]{1,0:T(8,128)(2,1)}, u32[]{:S(2)}, u32[]{:S(2)}) collective-permute-start(bf16[512,2048]{1,0:T(8,128)(2,1)} %convolution_convert_fusion.5), channel_id=1, source_target_pairs={{0,4},{4,0},{8,12},{12,8},{16,20},{20,16},{24,28},{28,24},{1,5},{5... | collective-permute-start | bytes 6291464 | tf_op jit(solution)/shard_map/ppermute | solution.py:521
  561.7 216.7 %reduce-scatter.7.cloned.1.call-start = ((), (), s32[]{:S(2)}) async-start(), calls=%async_computation.10 | async-start | bytes 5242880 | tf_op jit(solution)/shard_map/reduce_scatter | solution.py:698
  617.6 51.4 %collective-permute-start.51 = (bf16[512,2048]{1,0:T(8,128)(2,1)}, bf16[512,2048]{1,0:T(8,128)(2,1)}, u32[]{:S(2)}, u32[]{:S(2)}) collective-permute-start(bf16[512,2048]{1,0:T(8,128)(2,1)} %add_convert_fusion.5), channel_id=1, source_target_pairs={{0,16},{4,20},{8,24},{12,28},{16,0},{20,4},{24,8},{28,12},{1,17},{... | collective-permute-start | bytes 6291464 | tf_op jit(solution)/shard_map/ppermute | solution.py:521
  618.7 50.3 %collective-permute-start.52 = (bf16[512,2048]{1,0:T(8,128)(2,1)}, bf16[512,2048]{1,0:T(8,128)(2,1)}, u32[]{:S(2)}, u32[]{:S(2)}) collective-permute-start(bf16[512,2048]{1,0:T(8,128)(2,1)} %add_convert_fusion.4), channel_id=1, source_target_pairs={{0,8},{4,12},{8,0},{12,4},{16,24},{20,28},{24,16},{28,20},{1,9},{5... | collective-permute-start | bytes 6291464 | tf_op jit(solution)/shard_map/ppermute | solution.py:521
  673.5 37.9 %collective-permute-start.53 = (bf16[1024,2048]{1,0:T(8,128)(2,1)}, bf16[1024,2048]{1,0:T(8,128)(2,1)}, u32[]{:S(2)}, u32[]{:S(2)}) collective-permute-start(bf16[1024,2048]{1,0:T(8,128)(2,1)} %convolution_convert_fusion.1), channel_id=1, source_target_pairs={{0,4},{4,0},{8,12},{12,8},{16,20},{20,16},{24,28},{28,24},{1,5},{5... | collective-permute-start | bytes 12582920 | tf_op jit(solution)/shard_map/ppermute | solution.py:521
  675.8 32.8 %collective-permute-start.54 = (bf16[256,2048]{1,0:T(8,128)(2,1)}, bf16[256,2048]{1,0:T(8,128)(2,1)}, u32[]{:S(2)}, u32[]{:S(2)}) collective-permute-start(bf16[256,2048]{1,0:T(8,128)(2,1)} %get-tuple-element.263), channel_id=1, source_target_pairs={{0,16},{4,20},{8,24},{12,28},{16,0},{20,4},{24,8},{28,12},{1,17},{... | collective-permute-start | bytes 3145736 | tf_op jit(solution)/shard_map/ppermute | solution.py:521
  676.8 34.6 %collective-permute-start.55 = (bf16[256,2048]{1,0:T(8,128)(2,1)}, bf16[256,2048]{1,0:T(8,128)(2,1)}, u32[]{:S(2)}, u32[]{:S(2)}) collective-permute-start(bf16[256,2048]{1,0:T(8,128)(2,1)} %get-tuple-element.264), channel_id=1, source_target_pairs={{0,8},{4,12},{8,0},{12,4},{16,24},{20,28},{24,16},{28,20},{1,9},{5... | collective-permute-start | bytes 3145736 | tf_op jit(solution)/shard_map/ppermute | solution.py:521
  684.9 41.9 %collective-permute-start.56 = (bf16[2,256,256]{2,1,0:T(8,128)(2,1)}, bf16[2,256,256]{2,1,0:T(8,128)(2,1)S(1)}, u32[]{:S(2)}, u32[]{:S(2)}) collective-permute-start(bf16[2,256,256]{2,1,0:T(8,128)(2,1)} %get-tuple-element.333), channel_id=1, source_target_pairs={{0,1},{1,2},{2,3},{3,0},{4,5},{5,6},{6,7},{7,4},{8,9},{9,10},{10,1... | collective-permute-start | bytes 786440 | tf_op jit(solution)/shard_map/ppermute | solution.py:456
  708.6 27.3 %collective-permute-start.57 = (bf16[2,256,256]{2,1,0:T(8,128)(2,1)}, bf16[2,256,256]{2,1,0:T(8,128)(2,1)}, u32[]{:S(2)}, u32[]{:S(2)}) collective-permute-start(bf16[2,256,256]{2,1,0:T(8,128)(2,1)} %get-tuple-element.332), channel_id=1, source_target_pairs={{0,2},{1,3},{2,0},{3,1},{4,6},{5,7},{6,4},{7,5},{8,10},{9,11},{10,... | collective-permute-start | bytes 786440 | tf_op jit(solution)/shard_map/ppermute | solution.py:456
  708.6 41.0 %collective-permute-start.58 = (bf16[2,256,256]{2,1,0:T(8,128)(2,1)}, bf16[2,256,256]{2,1,0:T(8,128)(2,1)}, u32[]{:S(2)}, u32[]{:S(2)}) collective-permute-start(bf16[2,256,256]{2,1,0:T(8,128)(2,1)} %get-tuple-element.331), channel_id=1, source_target_pairs={{0,3},{1,0},{2,1},{3,2},{4,7},{5,4},{6,5},{7,6},{8,11},{9,8},{10,9... | collective-permute-start | bytes 786440 | tf_op jit(solution)/shard_map/ppermute | solution.py:456
  715.5 59.1 %collective-permute-start.60 = (bf16[128,2048]{1,0:T(8,128)(2,1)}, bf16[128,2048]{1,0:T(8,128)(2,1)}, u32[]{:S(2)}, u32[]{:S(2)}) collective-permute-start(bf16[128,2048]{1,0:T(8,128)(2,1)} %slice.477), channel_id=1, source_target_pairs={{0,16},{4,20},{8,24},{12,28},{16,0},{20,4},{24,8},{28,12},{1,17},{... | collective-permute-start | bytes 1572872 | tf_op jit(solution)/shard_map/ppermute | solution.py:521
  751.7 24.3 %collective-permute-start.59 = (bf16[128,2048]{1,0:T(8,128)(2,1)}, bf16[128,2048]{1,0:T(8,128)(2,1)}, u32[]{:S(2)}, u32[]{:S(2)}) collective-permute-start(bf16[128,2048]{1,0:T(8,128)(2,1)} %slice.478), channel_id=1, source_target_pairs={{0,8},{4,12},{8,0},{12,4},{16,24},{20,28},{24,16},{28,20},{1,9},{5... | collective-permute-start | bytes 1572872 | tf_op jit(solution)/shard_map/ppermute | solution.py:521
  752.9 50.1 %collective-permute-start.62 = (bf16[256,2048]{1,0:T(8,128)(2,1)}, bf16[256,2048]{1,0:T(8,128)(2,1)}, u32[]{:S(2)}, u32[]{:S(2)}) collective-permute-start(bf16[256,2048]{1,0:T(8,128)(2,1)} %get-tuple-element.310), channel_id=1, source_target_pairs={{0,16},{4,20},{8,24},{12,28},{16,0},{20,4},{24,8},{28,12},{1,17},{... | collective-permute-start | bytes 3145736 | tf_op jit(solution)/shard_map/ppermute | solution.py:521
  754.5 48.6 %collective-permute-start.63 = (bf16[256,2048]{1,0:T(8,128)(2,1)}, bf16[256,2048]{1,0:T(8,128)(2,1)}, u32[]{:S(2)}, u32[]{:S(2)}) collective-permute-start(bf16[256,2048]{1,0:T(8,128)(2,1)} %get-tuple-element.309), channel_id=1, source_target_pairs={{0,8},{4,12},{8,0},{12,4},{16,24},{20,28},{24,16},{28,20},{1,9},{5... | collective-permute-start | bytes 3145736 | tf_op jit(solution)/shard_map/ppermute | solution.py:521
  754.9 113.9 %all-to-all-start.1 = ((bf16[8,64,1024]{2,1,0:T(8,128)(2,1)}), bf16[8,64,1024]{2,1,0:T(8,128)(2,1)}, u32[]{:S(2)}, u32[]{:S(2)}) async-start(bf16[8,64,1024]{2,1,0:T(8,128)(2,1)} %reduce-scatter.5.cloned.1.call-done), calls=%async_computation.5 | async-start | bytes 2097152 | tf_op jit(solution)/shard_map/all_to_all | solution.py:805
  759.2 120.3 %reduce-scatter.11.cloned.1.call-start = ((), (), s32[]{:S(2)}) async-start(), calls=%async_computation.12 | async-start | bytes 1310720 | tf_op jit(solution)/shard_map/reduce_scatter | solution.py:788
  792.8 88.4 %reduce-scatter.9.cloned.1.call-start = ((), (), s32[]{:S(2)}) async-start(), calls=%async_computation.11 | async-start | bytes 1310720 | tf_op jit(solution)/shard_map/reduce_scatter | solution.py:790
  809.1 41.8 %collective-permute-start.64 = (bf16[1024,2048]{1,0:T(8,128)(2,1)}, bf16[1024,2048]{1,0:T(8,128)(2,1)}, u32[]{:S(2)}, u32[]{:S(2)}) collective-permute-start(bf16[1024,2048]{1,0:T(8,128)(2,1)} %convolution_convert_fusion.3), channel_id=1, source_target_pairs={{0,4},{4,0},{8,12},{12,8},{16,20},{20,16},{24,28},{28,24},{1,5},{5... | collective-permute-start | bytes 12582920 | tf_op jit(solution)/shard_map/ppermute | solution.py:521
  812.2 33.8 %collective-permute-start.68 = (bf16[128,2048]{1,0:T(8,128)(2,1)}, bf16[128,2048]{1,0:T(8,128)(2,1)}, u32[]{:S(2)}, u32[]{:S(2)}) collective-permute-start(bf16[128,2048]{1,0:T(8,128)(2,1)} %slice.475), channel_id=1, source_target_pairs={{0,16},{4,20},{8,24},{12,28},{16,0},{20,4},{24,8},{28,12},{1,17},{... | collective-permute-start | bytes 1572872 | tf_op jit(solution)/shard_map/ppermute | solution.py:521
  818.0 30.3 %collective-permute-start.67 = (bf16[128,2048]{1,0:T(8,128)(2,1)}, bf16[128,2048]{1,0:T(8,128)(2,1)}, u32[]{:S(2)}, u32[]{:S(2)}) collective-permute-start(bf16[128,2048]{1,0:T(8,128)(2,1)} %slice.476), channel_id=1, source_target_pairs={{0,8},{4,12},{8,0},{12,4},{16,24},{20,28},{24,16},{28,20},{1,9},{5... | collective-permute-start | bytes 1572872 | tf_op jit(solution)/shard_map/ppermute | solution.py:521
  835.8 40.5 %collective-permute-start.75 = (bf16[17664]{0:T(1024)(128)(2,1)S(1)}, bf16[17664]{0:T(1024)(128)(2,1)}, u32[]{:S(2)}, u32[]{:S(2)}) collective-permute-start(bf16[17664]{0:T(1024)(128)(2,1)S(1)} %get-tuple-element.301), channel_id=1, source_target_pairs={{0,3},{1,0},{2,1},{3,2},{4,7},{5,4},{6,5},{7,6},{8,11},{9,8},{10,9... | collective-permute-start | bytes 105992 | tf_op jit(solution)/shard_map/ppermute | solution.py:456
  846.0 30.3 %collective-permute-start.74 = (bf16[17664]{0:T(1024)(128)(2,1)S(1)}, bf16[17664]{0:T(1024)(128)(2,1)}, u32[]{:S(2)}, u32[]{:S(2)}) collective-permute-start(bf16[17664]{0:T(1024)(128)(2,1)S(1)} %get-tuple-element.302), channel_id=1, source_target_pairs={{0,2},{1,3},{2,0},{3,1},{4,6},{5,7},{6,4},{7,5},{8,10},{9,11},{10,... | collective-permute-start | bytes 105992 | tf_op jit(solution)/shard_map/ppermute | solution.py:456
  846.0 30.3 %collective-permute-start.73 = (bf16[17664]{0:T(1024)(128)(2,1)S(1)}, bf16[17664]{0:T(1024)(128)(2,1)}, u32[]{:S(2)}, u32[]{:S(2)}) collective-permute-start(bf16[17664]{0:T(1024)(128)(2,1)S(1)} %get-tuple-element.300), channel_id=1, source_target_pairs={{0,1},{1,2},{2,3},{3,0},{4,5},{5,6},{6,7},{7,4},{8,9},{9,10},{10,1... | collective-permute-start | bytes 105992 | tf_op jit(solution)/shard_map/ppermute | solution.py:456
  867.1 22.5 %collective-permute-start.66 = (bf16[256,2048]{1,0:T(8,128)(2,1)}, bf16[256,2048]{1,0:T(8,128)(2,1)S(1)}, u32[]{:S(2)}, u32[]{:S(2)}) collective-permute-start(bf16[256,2048]{1,0:T(8,128)(2,1)} %slice.471), channel_id=1, source_target_pairs={{0,16},{4,20},{8,24},{12,28},{16,0},{20,4},{24,8},{28,12},{1,17},{... | collective-permute-start | bytes 3145736 | tf_op jit(solution)/shard_map/ppermute | solution.py:521
  874.8 22.2 %collective-permute-start.65 = (bf16[256,2048]{1,0:T(8,128)(2,1)}, bf16[256,2048]{1,0:T(8,128)(2,1)}, u32[]{:S(2)}, u32[]{:S(2)}) collective-permute-start(bf16[256,2048]{1,0:T(8,128)(2,1)} %slice.472), channel_id=1, source_target_pairs={{0,8},{4,12},{8,0},{12,4},{16,24},{20,28},{24,16},{28,20},{1,9},{5... | collective-permute-start | bytes 3145736 | tf_op jit(solution)/shard_map/ppermute | solution.py:521
  (111 other events, 1844.3 us)
Sparse Core Ops, SparseCore 0:
  16.6 73.1 all-gather.3
  156.6 90.7 all-gather.5
  271.7 100.4 all-gather.7
  561.8 96.3 reduce-scatter.4
  660.5 94.0 reduce-scatter.6
  792.9 35.1 reduce-scatter.10
  851.1 28.1 reduce-scatter.8

commit v8 on v5

--- a/solution.py
+++ b/solution.py
@@ -14,7 +14,7 @@
 F32 = jnp.float32
 BF16 = jnp.bfloat16
 BOTH = ("dp", "fsdp")
-HASTE = 8
+HASTE = 64
 
 
 def dot_nn(left, right):
@@ -350,10 +350,6 @@
     def gather(self, block):
         return [block] + [self.send(block, step) for step in range(1, self.count)]
 
-    def more(self, pieces, steps, block):
-        for step in steps:
-            pieces[step] = self.send(block, step)
-
     def in_order(self, pieces, axis=0):
         me = lax.axis_index("fsdp")
         size = pieces[0].shape[axis]
@@ -373,19 +369,6 @@
             return lax.dynamic_index_in_dim(terms, place, axis, keepdims=False)
 
         return [term(0)] + [self.send(term(step).astype(BF16), step) for step in range(1, self.count)]
-
-
-def thirds(count):
-    steps = sorted(range(1, count), key=lambda step: min(step, count - step))
-    lot = -(-len(steps) // 3)
-    return steps[:lot], steps[lot : 2 * lot], steps[2 * lot :]
-
-
-def meet(pieces, steps, *arrays):
-    out = tie(*arrays, *[pieces[step] for step in steps])
-    for step, piece in zip(steps, out[len(arrays) :]):
-        pieces[step] = piece
-    return out[: len(arrays)]
 
 
 def total(terms):
@@ -442,7 +425,6 @@
     n_dev = n_dp * n_z
     plane = Plane(n_dp)
     line = Line(n_z)
-    soon, later, last = thirds(n_z)
 
     def local(
         tokens,
@@ -490,11 +472,11 @@
         kv_lines = kv_weight.size // width
         filled = own + kv_lines + -(-small_row.shape[0] // width)
         lines = -(-filled // 16) * 16
-        spare = (lines - own - kv_lines) * width
-        small_row = jnp.pad(small_row, (0, spare - small_row.shape[0]))
+        small_row = jnp.pad(small_row, (0, (lines - own - kv_lines) * width - small_row.shape[0]))
         packed = jnp.concatenate(
             [query_weight, kv_weight.reshape(kv_lines, width), small_row.reshape(-1, width)]
         )
+        places = plane.places()
 
         grad_low = cotangent.reshape(rows, width)
         packed = lax.all_gather(packed, "fsdp", axis=0, tiled=True)
@@ -506,16 +488,18 @@
         out_pieces = line.gather(out_weight)
         *out_pieces, down_late = tie(*out_pieces, down_weight)
         full_o = line.in_order(out_pieces)
-        down_pieces = [down_weight] + [None] * (n_z - 1)
-        line.more(down_pieces, last, down_late)
+        down_pieces = [down_late]
+        while len(down_pieces) < min(3, n_z):
+            down_pieces.append(line.send(down_pieces[-1], 1))
         inputs = tokens.reshape(rows, width).astype(F32)
         mean_one, recip_one = norm_stats(inputs)
-        packed, full_o, mean_one, grad_near[0], grad_near[1] = meet(
-            down_pieces, last, packed, full_o, mean_one, *grad_near
-        )
+        grad_near_sib = plane.cross(grad_near)
+        packed, full_o, mean_one, down_pieces[-1], *arrived = tie(
+            packed, full_o, mean_one, down_pieces[-1], *grad_near, *grad_near_sib
+        )
+        grad_near, grad_near_sib = arrived[:2], arrived[2:]
 
         full_o = lax.all_gather(full_o, "dp", axis=0, tiled=True)
-        grad_far = plane.across(grad_near, plane.last)
         packed = packed.reshape(n_dev, lines, width)
         full_q = packed[:, :own].reshape(width, width)
         full_kv = packed[:, own : own + kv_lines].reshape(width, 2 * HD)
@@ -528,46 +512,49 @@
         normed_one = (xhat_one * gain_one + shift_one).astype(BF16)
         kv_bias = jnp.concatenate([jnp.zeros((HD,), F32), bias_v])
         key_value = (dot_nn(normed_one, full_kv) + kv_bias).astype(BF16)
-        key_value, normed_late = tie(key_value, normed_one)
+        key_value, normed_late, up_cols = tie(key_value, normed_one, up_cols)
         kv_pieces = line.gather(key_value.reshape(windows, local_len, 2 * HD))
         queries = (dot_nn(normed_late, full_q) + bias_q).astype(BF16)
+        queries, *kv_pieces = tie(queries, *kv_pieces)
         kv_window = line.in_order(kv_pieces, 1)
 
         first = (lax.axis_index("fsdp") * local_len).astype(jnp.int32).reshape(1)
         file_count = lengths.shape[1]
         upto = jnp.arange(file_count)[:, None] <= jnp.arange(file_count)[None, :]
         file_ends = jnp.sum(jnp.where(upto[None], lengths[:, :, None], 0), axis=1)
-        queries, kv_window, down_late = tie(queries, kv_window, down_late)
-        line.more(down_pieces, soon + later, down_late)
+        grad_far = plane.across(grad_near, plane.last)
+        while len(down_pieces) < n_z:
+            down_pieces.append(line.send(down_pieces[-1], 1))
+        up_part = lax.all_gather(up_cols, "fsdp", axis=1, tiled=True).reshape(width, ff_own)
         attended, norms = attn_forward(queries, kv_window, first, file_ends)
-        attended, up_cols = meet(down_pieces, soon + later, attended, up_cols)
-        up_pieces = [up_cols] + [None] * (n_z - 1)
-        line.more(up_pieces, soon + later, up_cols)
-        down_part = line.in_order(down_pieces)
-        grad_lots = [[*grad_near, *plane.cross(grad_near)]]
-        back_near = back_product(grad_lots[0], down_part)
-        grad_far = list(grad_far)
-        grad_lots.append([*grad_far, *plane.cross(grad_far)])
-        attended, back_near, *grad_lots[1] = meet(up_pieces, soon, attended, back_near, *grad_lots[1])
-        line.more(up_pieces, last, up_cols)
+        attended, down_pieces[-1] = tie(attended, down_pieces[-1])
         middle = inputs + dot_nn(attended, full_o) + bias_o
         mean_two, recip_two = norm_stats(middle)
         xhat_two = (middle - mean_two) * recip_two
         normed_two = (xhat_two * gain_two + shift_two).astype(BF16)
 
-        normed_two, down_part = tie(normed_two, down_part)
-        back_far = back_product(grad_lots[1], down_part)
-        two_near = list(meet(up_pieces, later, *plane.grow([normed_two[:half], normed_two[half:]])))
-
+        normed_two, normed_late, *arrived = tie(normed_two, normed_late, *grad_far, *down_pieces)
+        grad_far, down_pieces = arrived[:2], arrived[2:]
+        two_near = plane.grow([normed_two[:half], normed_two[half:]])
+        down_part = line.in_order(down_pieces)
+        grad_lots = [[*grad_near, *grad_near_sib], [*grad_far, *plane.cross(grad_far)]]
+        back_near = back_product(grad_lots[0], down_part)
+        two_near[0], two_near[1], back_near = tie(*two_near, back_near)
         two_far = plane.across(two_near, plane.last)
-        two_lots = [[*two_near, *plane.cross(two_near)], [*two_far, *plane.cross(two_far)]]
-        up_part = line.in_order(up_pieces, 1).reshape(width, ff_own)
+        two_lots = [[*two_near, *plane.cross(two_near)]]
+        back_near, down_late, attended_late, normed_late = tie(
+            back_near, down_part, attended, normed_late
+        )
+        back_far = back_product(grad_lots[1], down_late)
         bias_up_part = lax.dynamic_slice_in_dim(bias_up, my_dp * ff_own, ff_own)
         hid_near, pre_near = middle_layer(two_lots[0], back_near, up_part, bias_up_part)
-        places = plane.places()
-        back_far, attended, pre_near[0], pre_near[1], places = tie(
-            back_far, attended, *pre_near, places
-        )
+        att_mine, att_sib = reorder(attended_late, places)
+        one_mine, one_sib = reorder(normed_late, places)
+        back_far, pre_near[0], pre_near[1], *arrived = tie(
+            back_far, *pre_near, att_mine, att_sib, one_mine, one_sib
+        )
+        att_mine, att_sib, one_mine, one_sib = arrived
+        two_lots.append([*two_far, *plane.cross(two_far)])
         hid_far, pre_far = middle_layer(two_lots[1], back_far, up_part, bias_up_part)
         block = two_near[0].shape[0]
         lots = (slice(None, block), slice(block, None))
@@ -591,12 +578,14 @@
         up_terms = weight_grad(two_lots[0] + two_lots[1], pre_near + pre_far, block)
         pre_near[0], up_terms = tie(pre_near[0], up_terms)
         two_sum = ours(pre_near, up_part, dot_nt, theirs, got)
-        up_got = line.scatter(up_terms.reshape(n_dp, n_z, own, ff_own), 1)
+        grad_up = lax.psum_scatter(
+            up_terms.reshape(n_dp, n_z * own, ff_own), "fsdp", scatter_dimension=1, tiled=True
+        )
         hid_far[0], hid_far[1], *two_sum = tie(*hid_far, *two_sum)
         two_grad = plane.fold(two_sum)
         down_terms = weight_grad(hid_near + hid_far, grad_lots[0] + grad_lots[1], block)
-        two_grad, down_terms, hid_far[0] = meet(up_got, soon, two_grad, down_terms, hid_far[0])
-        down_got = line.scatter(down_terms.reshape(n_z, ff_own // n_z, width), 0)
+        two_grad, down_terms, hid_far[0] = tie(two_grad, down_terms, hid_far[0])
+        grad_down = lax.psum_scatter(down_terms, "fsdp", scatter_dimension=0, tiled=True)
         out_far = halves(hid_far, down_part, dot_nn)
         two_grad, *out_far = tie(two_grad, *out_far)
 
@@ -608,8 +597,6 @@
         middle_grad = grad_out + norm_pull(two_grad, xhat_two, recip_two, gain_two)
         grad_bo = jnp.sum(middle_grad, axis=0)
         branch_grad = middle_grad.astype(BF16)
-        att_mine, att_sib = reorder(attended, places)
-        one_mine, one_sib = reorder(normed_one, places)
 
         def cut(rows_of_lots):
             size = rows_of_lots.shape[0] // 4
@@ -626,7 +613,7 @@
 
         theirs = plane.swap(dot_tn(att_sib, branch_grad).astype(BF16), 1)
         attended_grad = dot_nt(branch_grad, full_o).astype(BF16)
-        attended_grad, branch_late = meet(up_got, later, attended_grad, branch_grad)
+        attended_grad, branch_late = tie(attended_grad, branch_grad)
         wo_parts = cut(plus(att_mine, branch_late, theirs))
         attended_grad, *wo_parts = tie(attended_grad, *wo_parts)
         wo_got = send_rows(wo_parts)
@@ -634,21 +621,16 @@
         query_grad, kv_terms = attn_backward(queries, kv_window, norms, attended_grad, first, file_ends)
         query_grad, kv_terms, *out_got = tie(query_grad, kv_terms, *out_got)
         kv_got = line.scatter(kv_terms.reshape(windows, n_z, local_len, 2 * HD), 1)
-        (query_grad,) = meet(up_got, last, query_grad)
         theirs = plane.swap(dot_tn(one_sib, query_grad).astype(BF16), 1)
-        theirs, *wo_got = tie(theirs, *wo_got)
+        theirs, grad_up, *wo_got = tie(theirs, grad_up, *wo_got)
         wq_parts = cut(plus(one_mine, query_grad, theirs))
         wq_got = send_rows(wq_parts)
-        wq_parts[1], query_late, hid_late = meet(down_got, soon, wq_parts[1], query_grad, hid_near[1])
+        wq_parts[1], query_late, hid_late = tie(wq_parts[1], query_grad, hid_near[1])
         wq_parts[1], *kv_got = tie(wq_parts[1], *kv_got)
-        wq_parts[3], *up_got = tie(wq_parts[3], *up_got)
-        theirs = plane.swap(dot_nn(hid_late, down_part).astype(BF16), 1)
         query_part = dot_nt(query_late, full_q)
-        query_part, hid_near[0], theirs = tie(query_part, hid_near[0], theirs)
-        out_sum = ours(hid_near, down_part, dot_nn, theirs, out_got)
-        query_part, *out_sum = tie(query_part, *out_sum)
         kv_grad = total(kv_got).astype(BF16).reshape(rows, 2 * HD)
-        query_part, kv_grad = meet(down_got, later, query_part, kv_grad)
+        wo_rows = own_rows(wo_parts, wo_got)
+        query_part, kv_grad, wo_rows, grad_down = tie(query_part, kv_grad, wo_rows, grad_down)
 
         one_grad = query_part + dot_nt(kv_grad, full_kv)
         grad_bq = jnp.sum(query_late.astype(F32), axis=0)
@@ -690,10 +672,12 @@
         theirs = plane.swap(with_vectors(dot_tn(one_sib, kv_grad), 1).astype(BF16), 1)
         kv_parts = cut((with_vectors(dot_tn(one_mine, kv_grad), 0) + theirs.astype(F32)).astype(BF16))
         kv_parts_got = send_rows(kv_parts)
-        query_part, *kv_parts = tie(query_part, *kv_parts)
-
-        wo_last = line.scatter(own_rows(wo_parts, wo_got).reshape(n_z, own, width), 0)
-        wq_last = line.scatter(own_rows(wq_parts, wq_got).reshape(n_z, own, width), 0)
+        kv_parts[1], hid_late, hid_near[0], *wq_got = tie(kv_parts[1], hid_late, hid_near[0], *wq_got)
+        theirs = plane.swap(dot_nn(hid_late, down_part).astype(BF16), 1)
+
+        grad_wo = lax.psum_scatter(wo_rows.astype(BF16), "fsdp", scatter_dimension=0, tiled=True)
+        wq_rows = own_rows(wq_parts, wq_got).astype(BF16)
+        grad_wq = lax.psum_scatter(wq_rows, "fsdp", scatter_dimension=0, tiled=True)
         kv_last = own_rows(kv_parts, kv_parts_got).reshape(2, -1, 2 * HD)
         kv_rows = kv_last.shape[1] - more
         kv_last = jnp.concatenate(
@@ -704,11 +688,12 @@
             axis=1,
         )
         kv_last = line.scatter(kv_last, 0)
+        out_sum = ours(hid_near, down_part, dot_nn, theirs, out_got)
         output = (middle + plane.fold(out_sum) + bias_down).astype(BF16).reshape(windows, local_len, width)
         tokens_grad = middle_grad + norm_pull(one_grad, xhat_one, recip_one, gain_one)
         tokens_grad = tokens_grad.astype(BF16).reshape(windows, local_len, width)
         grad_up = lax.all_to_all(
-            total(up_got).astype(BF16).reshape(n_dp * own, ff_own), "dp", 0, 1, tiled=True
+            grad_up.reshape(n_dp * own, ff_own), "dp", 0, 1, tiled=True
         ).astype(F32)
         kv_own = total(kv_last)
         flat = kv_own[own * 2 * HD :]
@@ -718,16 +703,16 @@
         return (
             output,
             tokens_grad,
-            total(wq_last),
+            grad_wq.astype(F32),
             kv_own[: own * 2 * HD].reshape(own, 2 * HD),
-            total(wo_last),
+            grad_wo.astype(F32),
             bq,
             bv,
             bo,
             gain1,
             shift1,
             grad_up,
-            total(down_got),
+            grad_down.astype(F32),
             bup,
             bdown,
             gain2,

time: 993 us -> 833 us (0.84)
  waiting for transfers between devices: 354 us -> 234 us
  starting transfers between devices: 131 us -> 101 us
  matrix products: 133 us -> 115 us
    ppermute x30 -> x15, waiting for transfers between devices: 178 us -> 78.3 us  [send(): lax.ppermute(block, 'fsdp', [(i, (i + places) % self.count) for i in rang...]
    ppermute x45, waiting for transfers between devices: 169 us -> 130 us  [swap(): return lax.ppermute(block, 'dp', [(i, i ^ bit) for i in range(self.count)])]
    ppermute x30 -> x15, starting transfers between devices: 86 us -> 57.7 us  [send(): lax.ppermute(block, 'fsdp', [(i, (i + places) % self.count) for i in rang...]
    reduce_scatter x0 -> x4, waiting for transfers between devices: none -> 19 us  [the longest x1 17.3 us: local(): lax.psum_scatter(down_terms, 'fsdp', scatter_dimension=0, tiled=True)]
    dot_general x9, matrix products: 61.1 us -> 49.2 us  [dot_nn(): return jnp.dot(left, right, preferred_element_type=F32)]
    unnamed x196 -> x188, local copies, waits for them, and re-layouts: 16.8 us -> 28.3 us
  transfers between devices with their start and end apart: 80 -> 70, of which waited for: 32 -> 26; matrix products, arithmetic and copies ran while one was open for 23% -> 29% of each run, Pallas kernels for 16% -> 20%
where the time goes in v8:
time: 833 us; the launch traced here: 823 us
  waiting for transfers between devices  234 us (28%)
  Pallas kernels  182 us (22%)
  matrix products  115 us (14%)
  starting transfers between devices  101 us (12%)
  local copies, waits for them, and re-layouts  91 us (11%)
  other arithmetic  84.4 us (10%)
  between operations  16 us (2%)
    ppermute x45, waiting for transfers between devices, swap(): return lax.ppermute(block, 'dp', [(i, i ^ bit) for i in range(self.count)])  130 us
    ppermute x15, waiting for transfers between devices, send(): lax.ppermute(block, 'fsdp', [(i, (i + places) % self.count) for i in rang...  78.3 us
    ppermute x15, starting transfers between devices, send(): lax.ppermute(block, 'fsdp', [(i, (i + places) % self.count) for i in rang...  57.7 us
    pallas_call x2, Pallas kernels, weight_grad(): pl.pallas_call(functools.partial(weight_kernel, count), out_shape=jax.Sha...  50.7 us
    dot_general x9, matrix products, dot_nn(): return jnp.dot(left, right, preferred_element_type=F32)  49.2 us
    dot_general x9, matrix products, dot_nt(): lax.dot_general(left, right, (((1,), (1,)), ((), ())), preferred_element_...  46.4 us
    pallas_call x2, Pallas kernels, middle_layer(): pl.pallas_call(functools.partial(middle_kernel, count), out_shape=[jax.Sh...  39.6 us
    ppermute x45, starting transfers between devices, swap(): return lax.ppermute(block, 'dp', [(i, i ^ bit) for i in range(self.count)])  35.7 us
  transfers between devices with their start and end apart: 70, of which 26 were waited for; matrix products, arithmetic and copies ran while one was open for 29% of the time, Pallas kernels for 20%

profile of v8, /device:TPU:0, one launch (start us, length us, event | category | flops | bytes accessed | tf_op | source)
XLA Modules:
  0.0 823.4 jit_solution(10421099172503758650)
XLA Ops:
  17.6 2.7 slice_bitcast_fusion
  20.3 2.9 collective-permute-start
  25.8 3.6 all-to-all-start
  29.4 17.9 %collective-permute-done = bf16[256,2048]{1,0:T(8,128)(2,1)} collective-permute-done((bf16[256,2048]{1,0:T(8,128)(2,1)S(1)}, bf16[256,2048]{1,0:T(8,128)(2,1)}, u32[]{:S(2)}, u32[]{:S(2)}) %collective-permute-start) | collective-permute-done | bytes 1048608 | tf_op jit(solution)/shard_map/ppermute | solution.py:403
  49.9 3.1 pad_maximum_fusion.2.refs_1_.refs_9_
  53.0 6.3 all-to-all-done
  61.0 2.6 collective-permute-start.3
  64.9 5.6 collective-permute-done.2
  70.5 7.0 collective-permute-done.3
  77.5 28.5 %collective-permute-start.5 = (bf16[256,2048]{1,0:T(8,128)(2,1)}, bf16[256,2048]{1,0:T(8,128)(2,1)}, u32[]{:S(2)}, u32[]{:S(2)}) collective-permute-start(bf16[256,2048]{1,0:T(8,128)(2,1)} %param.29), channel_id=1, source_target_pairs={{0,1},{1,2},{2,3},{3,0},{4,5},{5,6},{6,7},{7,4},{8,9},{9,10},{10,1... | collective-permute-start | bytes 3145736 | tf_op jit(solution)/shard_map/ppermute | solution.py:348
  108.6 20.6 %collective-permute-done.5 = bf16[256,2048]{1,0:T(8,128)(2,1)} collective-permute-done((bf16[256,2048]{1,0:T(8,128)(2,1)}, bf16[256,2048]{1,0:T(8,128)(2,1)}, u32[]{:S(2)}, u32[]{:S(2)}) %collective-permute-start.5) | collective-permute-done | bytes 1048608 | tf_op jit(solution)/shard_map/ppermute | solution.py:348
  138.5 17.1 %collective-permute-done.6 = bf16[256,2048]{1,0:T(8,128)(2,1)} collective-permute-done((bf16[256,2048]{1,0:T(8,128)(2,1)}, bf16[256,2048]{1,0:T(8,128)(2,1)}, u32[]{:S(2)}, u32[]{:S(2)}) %collective-permute-start.6) | collective-permute-done | bytes 1048608 | tf_op jit(solution)/shard_map/ppermute | solution.py:348
  158.1 9.2 %slice.340 = bf16[32,64,2048]{2,1,0:T(8,128)(2,1)} slice(bf16[32,80,2048]{2,1,0:T(8,128)(2,1)} %bitcast.166), slice={[0:32], [0:64], [0:2048]} | slice | bytes 16777216 | tf_op jit(solution)/shard_map/slice | solution.py:504
  180.0 3.4 collective-permute-start.11
  184.7 8.5 %add_convert_fusion.9.q_ref = bf16[512,2048]{1,0:T(8,128)(2,1)S(1)} fusion(bf16[512,2048]{1,0:T(8,128)(2,1)} %fusion.14.first_ref.second_ref, bf16[2048,2048]{1,0:T(8,128)(2,1)} %bitcast.168, f32[2048]{0:T(1024)S(1)} %reshape.404), kind=kOutput, calls=%fused_computation.51 | convolution fusion | flops 4297064448 | bytes 12591104 | tf_op jit(solution)/shard_map/dot_general | solution.py:21
  193.3 28.0 %collective-permute-done.10 = bf16[2,256,256]{2,1,0:T(8,128)(2,1)} collective-permute-done((bf16[2,256,256]{2,1,0:T(8,128)(2,1)S(1)}, bf16[2,256,256]{2,1,0:T(8,128)(2,1)}, u32[]{:S(2)}, u32[]{:S(2)}) %collective-permute-start.10) | collective-permute-done | bytes 262176 | tf_op jit(solution)/shard_map/ppermute | solution.py:348
  224.4 18.8 %shard_map.288 = (bf16[512,2048]{1,0:T(8,128)(2,1)S(1)}, f32[512,128]{1,0:T(8,128)S(1)}) custom-call(s32[1]{0:T(128)} %bitcast.1.pos_ref, s32[2,8]{1,0:T(2,128)S(1)} %select_reduce_fusion.ends_ref, bf16[512,2048]{1,0:T(8,128)(2,1)S(1)} %add_convert_fusion.9.q_ref, bf16[2,1024,256]{2,1,0:T(8,128)(2,1)S(1)} %constant_dynamic-update-slice_fusion.15.kv_ref), custom_call_target="tpu_custom_call" | custom-call | flops 67108864 | bytes 65536 | tf_op jit(solution)/shard_map/pallas_call | solution.py:132
  245.5 9.9 %fusion.50 = (f32[512]{0:T(512)S(1)}, f32[512,2048]{1,0:T(8,128)S(1)}) fusion(f32[2048]{0:T(1024)S(1)} %reshape.405, bf16[512,2048]{1,0:T(8,128)(2,1)} %copy-done.11, bf16[2048,2048]{1,0:T(8,128)(2,1)} %all-gather.9.cloned.1.call-done, bf16[2,256,2048]{2,1,0:T(8,128)(2,1)} %param.17), kind=kOutput, calls=%fused_computation.196 | convolution fusion | flops 4299161088 | bytes 16787456 | tf_op jit(solution)/shard_map/dot_general | solution.py:21
  257.4 3.0 collective-permute-done.14.refs_1_.refs_13_
  268.1 14.1 %shard_map.289.refs_4_ = bf16[2048,1024]{1,0:T(8,128)(2,1)} custom-call(bf16[512,2048]{1,0:T(8,128)(2,1)S(1)} %pad_maximum_fusion.1.refs_0_.refs_8_, bf16[512,2048]{1,0:T(8,128)(2,1)} %pad_maximum_fusion.2.refs_1_.refs_9_, bf16[512,2048]{1,0:T(8,128)(2,1)} %collective-permute-done.7.refs_2_.refs_10_, ...), custom_call_target="tpu_custom_call" | custom-call | flops 134217728 | bytes 262144 | tf_op jit(solution)/shard_map/pallas_call | solution.py:236
  290.1 43.7 %collective-permute-done.21.refs_0_.refs_4_ = bf16[512,2048]{1,0:T(8,128)(2,1)} collective-permute-done((bf16[512,2048]{1,0:T(8,128)(2,1)}, bf16[512,2048]{1,0:T(8,128)(2,1)}, u32[]{:S(2)}, u32[]{:S(2)}) %collective-permute-start.21) | collective-permute-done | bytes 2097184 | tf_op jit(solution)/shard_map/ppermute | solution.py:403
  336.3 6.6 shard_map.292
  342.8 6.6 shard_map.293
  349.5 14.6 %shard_map.290.refs_4_ = bf16[2048,1024]{1,0:T(8,128)(2,1)} custom-call(bf16[512,2048]{1,0:T(8,128)(2,1)} %collective-permute-done.13.refs_0_.refs_12_, bf16[512,2048]{1,0:T(8,128)(2,1)} %collective-permute-done.14.refs_1_.refs_13_, bf16[512,2048]{1,0:T(8,128)(2,1)} %collective-permute-done.15.refs_2_.refs_14_, ...), custom_call_target="tpu_custom_call" | custom-call | flops 134217728 | bytes 262144 | tf_op jit(solution)/shard_map/pallas_call | solution.py:236
  364.1 19.7 %shard_map.291 = (bf16[1024,1024]{1,0:T(8,128)(2,1)S(1)}, bf16[1024,1024]{1,0:T(8,128)(2,1)S(1)}, bf16[1024,1024]{1,0:T(8,128)(2,1)}, bf16[1024,1024]{1,0:T(8,128)(2,1)}) custom-call(bf16[512,2048]{1,0:T(8,128)(2,1)} %pad_maximum_fusion.3.refs_0_, bf16[512,2048]{1,0:T(8,128)(2,1)} %pad_maximum_fusion.4.refs_1_, ...), custom_call_target="tpu_custom_call" | custom-call | flops 134217728 | bytes 393216 | tf_op jit(solution)/shard_map/pallas_call | solution.py:202
  386.5 19.9 %shard_map.294 = (bf16[1024,1024]{1,0:T(8,128)(2,1)S(1)}, bf16[1024,1024]{1,0:T(8,128)(2,1)S(1)}, bf16[1024,1024]{1,0:T(8,128)(2,1)}, bf16[1024,1024]{1,0:T(8,128)(2,1)}) custom-call(bf16[512,2048]{1,0:T(8,128)(2,1)} %collective-permute-done.21.refs_0_.refs_4_, bf16[512,2048]{1,0:T(8,128)(2,1)} %collective-permute-done.22.refs_1_.refs_5_, ...), custom_call_target="tpu_custom_call" | custom-call | flops 134217728 | bytes 393216 | tf_op jit(solution)/shard_map/pallas_call | solution.py:202
  406.4 4.5 convolution_convert_fusion.8
  415.4 3.7 add_convert_fusion.7
  419.1 3.7 add_convert_fusion.6
  422.8 4.8 convolution_convert_fusion.4
  430.7 4.2 collective-permute-done.27
  435.0 24.3 %shard_map.295 = bf16[2048,1024]{1,0:T(8,128)(2,1)} custom-call(bf16[512,2048]{1,0:T(8,128)(2,1)} %pad_maximum_fusion.3.refs_0_, bf16[512,2048]{1,0:T(8,128)(2,1)} %pad_maximum_fusion.4.refs_1_, bf16[512,2048]{1,0:T(8,128)(2,1)} %collective-permute-done.19.refs_2_, bf16[512,2048]{1,0:T(8,128)(2,1)} %collective-permute-done.20.refs_3_, ...), custom_call_target="tpu_custom_call" | custom-call | flops 268435456 | bytes 458752 | tf_op jit(solution)/shard_map/pallas_call | solution.py:276
  459.3 6.8 add_convert_fusion.3
  466.1 9.8 %collective-permute-done.29 = bf16[512,2048]{1,0:T(8,128)(2,1)S(1)} collective-permute-done((bf16[512,2048]{1,0:T(8,128)(2,1)}, bf16[512,2048]{1,0:T(8,128)(2,1)S(1)}, u32[]{:S(2)}, u32[]{:S(2)}) %collective-permute-start.29) | collective-permute-done | bytes 2097184 | tf_op jit(solution)/shard_map/ppermute | solution.py:403
  477.2 3.8 convert_add_fusion.3
  486.3 3.7 convolution_convert_fusion.6
  490.0 3.7 convolution_convert_fusion.5
  494.2 26.3 %shard_map.296 = bf16[1024,2048]{1,0:T(8,128)(2,1)} custom-call(bf16[1024,1024]{1,0:T(8,128)(2,1)} %copy-done.3, bf16[1024,1024]{1,0:T(8,128)(2,1)} %copy-done.3, bf16[1024,1024]{1,0:T(8,128)(2,1)} %copy-done.5, bf16[1024,1024]{1,0:T(8,128)(2,1)} %copy-done.5, bf16[1024,1024]{1,0:T(8,128)(2,1)} %copy-done.7, bf16[1024,1024]{1,0:T(8,128)(2,1)} %copy-done.7, ...), custom_call_target="tpu_custom_call" | custom-call | flops 268435456 | bytes 458752 | tf_op jit(solution)/shard_map/pallas_call | solution.py:276
  527.0 5.3 add_convert_fusion.5
  532.3 3.7 add_convert_fusion.4
  542.7 4.3 convolution_convert_fusion.2
  549.6 5.8 convolution_convert_fusion.9.grad_ref
  560.1 30.8 %shard_map.297 = (bf16[512,2048]{1,0:T(8,128)(2,1)S(1)}, bf16[2,1024,256]{2,1,0:T(8,128)(2,1)S(1)}) custom-call(s32[1]{0:T(128)} %bitcast.1.pos_ref, s32[2,8]{1,0:T(2,128)S(1)} %copy-done.13, bf16[512,2048]{1,0:T(8,128)(2,1)} %copy-done.10, bf16[2,1024,256]{2,1,0:T(8,128)(2,1)S(1)} %copy-done.2, f32[512,128]{1,0:T(8,128)S(1)} %get-tuple-element.183.norm_ref, ...), custom_call_target="tpu_custom_call" | custom-call | flops 167772160 | bytes 163840 | tf_op jit(solution)/shard_map/pallas_call | solution.py:152
  590.9 4.4 collective-permute-done.35
  596.1 4.4 convolution_convert_fusion.1
  611.1 3.0 collective-permute-start.40
  615.2 13.5 %collective-permute-done.38 = bf16[256,2048]{1,0:T(8,128)(2,1)} collective-permute-done((bf16[256,2048]{1,0:T(8,128)(2,1)}, bf16[256,2048]{1,0:T(8,128)(2,1)}, u32[]{:S(2)}, u32[]{:S(2)}) %collective-permute-start.38) | collective-permute-done | bytes 1048608 | tf_op jit(solution)/shard_map/ppermute | solution.py:403
  628.7 3.3 collective-permute-start.42
  632.0 4.9 add_convert_fusion.1
  644.2 9.4 %fusion.51 = f32[512,2048]{1,0:T(8,128)} fusion(bf16[512,2048]{1,0:T(8,128)(2,1)S(1)} %get-tuple-element.222, bf16[2048,2048]{1,0:T(8,128)(2,1)} %bitcast.169), kind=kOutput, calls=%fused_computation.197 | convolution fusion | flops 4294967296 | bytes 14680064 | tf_op jit(solution)/shard_map/dot_general | solution.py:25
  653.7 2.9 convert_add_fusion.8
  662.7 3.6 all-to-all-start.1
  670.1 4.5 collective-permute-done.43
  677.2 17.3 %reduce-scatter.7.cloned.1.call-done = bf16[256,2048]{1,0:T(8,128)(2,1)} async-done(((bf16[1024,2048]{1,0:T(8,128)(2,1)}), bf16[256,2048]{1,0:T(8,128)(2,1)}) %reduce-scatter.7.cloned.1.call-update) | async-done | bytes 1048592 | tf_op jit(solution)/shard_map/reduce_scatter | solution.py:588
  697.2 5.3 fusion.16
  710.8 5.4 fusion.20
  720.8 6.1 convolution_convert_fusion.3
  738.4 9.9 %collective-permute-done.53 = bf16[288,256]{1,0:T(8,128)(2,1)S(1)} collective-permute-done((bf16[288,256]{1,0:T(8,128)(2,1)S(1)}, bf16[288,256]{1,0:T(8,128)(2,1)S(1)}, u32[]{:S(2)}, u32[]{:S(2)}) %collective-permute-start.53) | collective-permute-done | bytes 147488 | tf_op jit(solution)/shard_map/ppermute | solution.py:403
  749.9 2.9 collective-permute-done.54
  760.6 6.1 collective-permute-start.58
  771.5 7.7 add_convert_fusion
  779.2 3.8 convert_add_fusion.2
  801.5 6.5 collective-permute-done.50
  810.0 3.7 collective-permute-done.49
  (472 shorter events, 206.2 us)
Async XLA Ops:
  7.2 52.1 %all-gather.5.cloned.1.call-start = ((), (), s32[]{:S(2)}) async-start(), calls=%async_computation.6 | async-start | bytes 1638400 | tf_op jit(solution)/shard_map/all_gather | solution.py:482
  20.3 27.0 %collective-permute-start = (bf16[256,2048]{1,0:T(8,128)(2,1)S(1)}, bf16[256,2048]{1,0:T(8,128)(2,1)}, u32[]{:S(2)}, u32[]{:S(2)}) collective-permute-start(bf16[256,2048]{1,0:T(8,128)(2,1)S(1)} %get-tuple-element.277), channel_id=1, source_target_pairs={{0,8},{4,12},{8,0},{12,4},{16,24},{20,28},{24,16},{28,20},{1,9},{5... | collective-permute-start | bytes 3145736 | tf_op jit(solution)/shard_map/ppermute | solution.py:403
  23.2 26.7 %collective-permute-start.1 = (bf16[256,2048]{1,0:T(8,128)(2,1)}, bf16[256,2048]{1,0:T(8,128)(2,1)}, u32[]{:S(2)}, u32[]{:S(2)}) collective-permute-start(bf16[256,2048]{1,0:T(8,128)(2,1)} %get-tuple-element.276), channel_id=1, source_target_pairs={{0,16},{4,20},{8,24},{12,28},{16,0},{20,4},{24,8},{28,12},{1,17},{... | collective-permute-start | bytes 3145736 | tf_op jit(solution)/shard_map/ppermute | solution.py:403
  25.8 33.5 %all-to-all-start = ((bf16[64,8,1024]{2,0,1:T(8,128)(2,1)}), bf16[64,8,1024]{2,0,1:T(8,128)(2,1)S(1)}, u32[]{:S(2)}, u32[]{:S(2)}) async-start(bf16[64,8,1024]{2,0,1:T(8,128)(2,1)} %bitcast.153), calls=%async_computation | async-start | bytes 2097152 | tf_op jit(solution)/shard_map/all_to_all | solution.py:484
  29.4 126.2 %all-gather.7.cloned.1.call-start = ((), (), s32[]{:S(2)}) async-start(), calls=%async_computation.7 | async-start | bytes 11796480 | tf_op jit(solution)/shard_map/all_gather | solution.py:487
  59.3 186.1 %all-gather.9.cloned.1.call-start = ((), (), s32[]{:S(2)}) async-start(), calls=%async_computation.8 | async-start | bytes 9437184 | tf_op jit(solution)/shard_map/all_gather | solution.py:502
  59.4 11.1 %collective-permute-start.2 = (bf16[64,2048]{1,0:T(8,128)(2,1)S(1)}, bf16[64,2048]{1,0:T(8,128)(2,1)S(1)}, u32[]{:S(2)}, u32[]{:S(2)}) collective-permute-start(bf16[64,2048]{1,0:T(8,128)(2,1)S(1)} %copy-done.62), channel_id=1, source_target_pairs={{0,1},{1,2},{2,3},{3,0},{4,5},{5,6},{6,7},{7,4},{8,9},{9,10},{10,1... | collective-permute-start | bytes 786440 | tf_op jit(solution)/shard_map/ppermute | solution.py:348
  61.0 16.5 %collective-permute-start.3 = (bf16[64,2048]{1,0:T(8,128)(2,1)S(1)}, bf16[64,2048]{1,0:T(8,128)(2,1)S(1)}, u32[]{:S(2)}, u32[]{:S(2)}) collective-permute-start(bf16[64,2048]{1,0:T(8,128)(2,1)S(1)} %copy-done.62), channel_id=1, source_target_pairs={{0,2},{1,3},{2,0},{3,1},{4,6},{5,7},{6,4},{7,5},{8,10},{9,11},{10,... | collective-permute-start | bytes 786440 | tf_op jit(solution)/shard_map/ppermute | solution.py:348
  63.6 13.9 %collective-permute-start.4 = (bf16[64,2048]{1,0:T(8,128)(2,1)S(1)}, bf16[64,2048]{1,0:T(8,128)(2,1)S(1)}, u32[]{:S(2)}, u32[]{:S(2)}) collective-permute-start(bf16[64,2048]{1,0:T(8,128)(2,1)S(1)} %copy-done.62), channel_id=1, source_target_pairs={{0,3},{1,0},{2,1},{3,2},{4,7},{5,4},{6,5},{7,6},{8,11},{9,8},{10,9... | collective-permute-start | bytes 786440 | tf_op jit(solution)/shard_map/ppermute | solution.py:348
  77.5 51.6 %collective-permute-start.5 = (bf16[256,2048]{1,0:T(8,128)(2,1)}, bf16[256,2048]{1,0:T(8,128)(2,1)}, u32[]{:S(2)}, u32[]{:S(2)}) collective-permute-start(bf16[256,2048]{1,0:T(8,128)(2,1)} %param.29), channel_id=1, source_target_pairs={{0,1},{1,2},{2,3},{3,0},{4,5},{5,6},{6,7},{7,4},{8,9},{9,10},{10,1... | collective-permute-start | bytes 3145736 | tf_op jit(solution)/shard_map/ppermute | solution.py:348
  106.1 32.4 %collective-permute-start.7 = (bf16[512,2048]{1,0:T(8,128)(2,1)S(1)}, bf16[512,2048]{1,0:T(8,128)(2,1)}, u32[]{:S(2)}, u32[]{:S(2)}) collective-permute-start(bf16[512,2048]{1,0:T(8,128)(2,1)S(1)} %pad_maximum_fusion.1.refs_0_.refs_8_), channel_id=1, source_target_pairs={{0,4},{4,0},{8,12},{12,8},{16,20},{20,16},{24,28},{28,24},{1,5},{5... | collective-permute-start | bytes 6291464 | tf_op jit(solution)/shard_map/ppermute | solution.py:403
  106.1 32.3 %collective-permute-start.8 = (bf16[512,2048]{1,0:T(8,128)(2,1)}, bf16[512,2048]{1,0:T(8,128)(2,1)}, u32[]{:S(2)}, u32[]{:S(2)}) collective-permute-start(bf16[512,2048]{1,0:T(8,128)(2,1)} %pad_maximum_fusion.2.refs_1_.refs_9_), channel_id=1, source_target_pairs={{0,4},{4,0},{8,12},{12,8},{16,20},{20,16},{24,28},{28,24},{1,5},{5... | collective-permute-start | bytes 6291464 | tf_op jit(solution)/shard_map/ppermute | solution.py:403
  129.1 26.5 %collective-permute-start.6 = (bf16[256,2048]{1,0:T(8,128)(2,1)}, bf16[256,2048]{1,0:T(8,128)(2,1)}, u32[]{:S(2)}, u32[]{:S(2)}) collective-permute-start(bf16[256,2048]{1,0:T(8,128)(2,1)} %collective-permute-done.5), channel_id=1, source_target_pairs={{0,1},{1,2},{2,3},{3,0},{4,5},{5,6},{6,7},{7,4},{8,9},{9,10},{10,1... | collective-permute-start | bytes 3145736 | tf_op jit(solution)/shard_map/ppermute | solution.py:348
  155.6 208.4 %all-gather.11.cloned.1.call-start = ((), (), s32[]{:S(2)}) async-start(), calls=%async_computation.9 | async-start | bytes 5242880 | tf_op jit(solution)/shard_map/all_gather | solution.py:528
  179.5 13.8 %collective-permute-start.9 = (bf16[2,256,256]{2,1,0:T(8,128)(2,1)S(1)}, bf16[2,256,256]{2,1,0:T(8,128)(2,1)}, u32[]{:S(2)}, u32[]{:S(2)}) collective-permute-start(bf16[2,256,256]{2,1,0:T(8,128)(2,1)S(1)} %bitcast.189), channel_id=1, source_target_pairs={{0,1},{1,2},{2,3},{3,0},{4,5},{5,6},{6,7},{7,4},{8,9},{9,10},{10,1... | collective-permute-start | bytes 786440 | tf_op jit(solution)/shard_map/ppermute | solution.py:348
  180.0 41.4 %collective-permute-start.10 = (bf16[2,256,256]{2,1,0:T(8,128)(2,1)S(1)}, bf16[2,256,256]{2,1,0:T(8,128)(2,1)}, u32[]{:S(2)}, u32[]{:S(2)}) collective-permute-start(bf16[2,256,256]{2,1,0:T(8,128)(2,1)S(1)} %bitcast.190), channel_id=1, source_target_pairs={{0,2},{1,3},{2,0},{3,1},{4,6},{5,7},{6,4},{7,5},{8,10},{9,11},{10,... | collective-permute-start | bytes 786440 | tf_op jit(solution)/shard_map/ppermute | solution.py:348
  180.0 41.4 %collective-permute-start.11 = (bf16[2,256,256]{2,1,0:T(8,128)(2,1)S(1)}, bf16[2,256,256]{2,1,0:T(8,128)(2,1)}, u32[]{:S(2)}, u32[]{:S(2)}) collective-permute-start(bf16[2,256,256]{2,1,0:T(8,128)(2,1)S(1)} %bitcast.191), channel_id=1, source_target_pairs={{0,3},{1,0},{2,1},{3,2},{4,7},{5,4},{6,5},{7,6},{8,11},{9,8},{10,9... | collective-permute-start | bytes 786440 | tf_op jit(solution)/shard_map/ppermute | solution.py:348
  183.5 62.0 %collective-permute-start.12 = (bf16[256,2048]{1,0:T(8,128)(2,1)}, bf16[256,2048]{1,0:T(8,128)(2,1)S(1)}, u32[]{:S(2)}, u32[]{:S(2)}) collective-permute-start(bf16[256,2048]{1,0:T(8,128)(2,1)} %collective-permute-done.6), channel_id=1, source_target_pairs={{0,1},{1,2},{2,3},{3,0},{4,5},{5,6},{6,7},{7,4},{8,9},{9,10},{10,1... | collective-permute-start | bytes 3145736 | tf_op jit(solution)/shard_map/ppermute | solution.py:348
  184.2 73.2 %collective-permute-start.13 = (bf16[512,2048]{1,0:T(8,128)(2,1)S(1)}, bf16[512,2048]{1,0:T(8,128)(2,1)}, u32[]{:S(2)}, u32[]{:S(2)}) collective-permute-start(bf16[512,2048]{1,0:T(8,128)(2,1)S(1)} %pad_maximum_fusion.1.refs_0_.refs_8_), channel_id=1, source_target_pairs={{0,16},{4,20},{8,24},{12,28},{16,0},{20,4},{24,8},{28,12},{1,17},{... | collective-permute-start | bytes 6291464 | tf_op jit(solution)/shard_map/ppermute | solution.py:403
  184.2 447.8 %reduce-scatter.5.cloned.1.call-start = ((), (), s32[]{:S(2)}) async-start(), calls=%async_computation.10 | async-start | bytes 5242880 | tf_op jit(solution)/shard_map/reduce_scatter | solution.py:581
  193.3 67.1 %collective-permute-start.14 = (bf16[512,2048]{1,0:T(8,128)(2,1)}, bf16[512,2048]{1,0:T(8,128)(2,1)}, u32[]{:S(2)}, u32[]{:S(2)}) collective-permute-start(bf16[512,2048]{1,0:T(8,128)(2,1)} %pad_maximum_fusion.2.refs_1_.refs_9_), channel_id=1, source_target_pairs={{0,8},{4,12},{8,0},{12,4},{16,24},{20,28},{24,16},{28,20},{1,9},{5... | collective-permute-start | bytes 6291464 | tf_op jit(solution)/shard_map/ppermute | solution.py:403
  260.5 23.8 %collective-permute-start.17 = (bf16[256,2048]{1,0:T(8,128)(2,1)S(1)}, bf16[256,2048]{1,0:T(8,128)(2,1)S(1)}, u32[]{:S(2)}, u32[]{:S(2)}) collective-permute-start(bf16[256,2048]{1,0:T(8,128)(2,1)S(1)} %get-tuple-element.275), channel_id=1, source_target_pairs={{0,8},{4,12},{8,0},{12,4},{16,24},{20,28},{24,16},{28,20},{1,9},{5... | collective-permute-start | bytes 3145736 | tf_op jit(solution)/shard_map/ppermute | solution.py:403
  260.9 25.0 %collective-permute-start.18 = (bf16[256,2048]{1,0:T(8,128)(2,1)S(1)}, bf16[256,2048]{1,0:T(8,128)(2,1)S(1)}, u32[]{:S(2)}, u32[]{:S(2)}) collective-permute-start(bf16[256,2048]{1,0:T(8,128)(2,1)S(1)} %get-tuple-element.274), channel_id=1, source_target_pairs={{0,16},{4,20},{8,24},{12,28},{16,0},{20,4},{24,8},{28,12},{1,17},{... | collective-permute-start | bytes 3145736 | tf_op jit(solution)/shard_map/ppermute | solution.py:403
  262.6 27.4 %collective-permute-start.15 = (bf16[512,2048]{1,0:T(8,128)(2,1)}, bf16[512,2048]{1,0:T(8,128)(2,1)}, u32[]{:S(2)}, u32[]{:S(2)}) collective-permute-start(bf16[512,2048]{1,0:T(8,128)(2,1)} %collective-permute-done.13.refs_0_.refs_12_), channel_id=1, source_target_pairs={{0,4},{4,0},{8,12},{12,8},{16,20},{20,16},{24,28},{28,24},{1,5},{5... | collective-permute-start | bytes 6291464 | tf_op jit(solution)/shard_map/ppermute | solution.py:403
  287.5 46.2 %collective-permute-start.21 = (bf16[512,2048]{1,0:T(8,128)(2,1)}, bf16[512,2048]{1,0:T(8,128)(2,1)}, u32[]{:S(2)}, u32[]{:S(2)}) collective-permute-start(bf16[512,2048]{1,0:T(8,128)(2,1)} %pad_maximum_fusion.3.refs_0_), channel_id=1, source_target_pairs={{0,16},{4,20},{8,24},{12,28},{16,0},{20,4},{24,8},{28,12},{1,17},{... | collective-permute-start | bytes 6291464 | tf_op jit(solution)/shard_map/ppermute | solution.py:403
  288.9 45.4 %collective-permute-start.22 = (bf16[512,2048]{1,0:T(8,128)(2,1)}, bf16[512,2048]{1,0:T(8,128)(2,1)}, u32[]{:S(2)}, u32[]{:S(2)}) collective-permute-start(bf16[512,2048]{1,0:T(8,128)(2,1)} %pad_maximum_fusion.4.refs_1_), channel_id=1, source_target_pairs={{0,8},{4,12},{8,0},{12,4},{16,24},{20,28},{24,16},{28,20},{1,9},{5... | collective-permute-start | bytes 6291464 | tf_op jit(solution)/shard_map/ppermute | solution.py:403
  289.6 59.9 %collective-permute-start.16 = (bf16[512,2048]{1,0:T(8,128)(2,1)}, bf16[512,2048]{1,0:T(8,128)(2,1)}, u32[]{:S(2)}, u32[]{:S(2)}) collective-permute-start(bf16[512,2048]{1,0:T(8,128)(2,1)} %collective-permute-done.14.refs_1_.refs_13_), channel_id=1, source_target_pairs={{0,4},{4,0},{8,12},{12,8},{16,20},{20,16},{24,28},{28,24},{1,5},{5... | collective-permute-start | bytes 6291464 | tf_op jit(solution)/shard_map/ppermute | solution.py:403
  289.6 74.5 %collective-permute-start.19 = (bf16[512,2048]{1,0:T(8,128)(2,1)}, bf16[512,2048]{1,0:T(8,128)(2,1)}, u32[]{:S(2)}, u32[]{:S(2)}) collective-permute-start(bf16[512,2048]{1,0:T(8,128)(2,1)} %pad_maximum_fusion.3.refs_0_), channel_id=1, source_target_pairs={{0,4},{4,0},{8,12},{12,8},{16,20},{20,16},{24,28},{28,24},{1,5},{5... | collective-permute-start | bytes 6291464 | tf_op jit(solution)/shard_map/ppermute | solution.py:403
  290.1 74.0 %collective-permute-start.20 = (bf16[512,2048]{1,0:T(8,128)(2,1)}, bf16[512,2048]{1,0:T(8,128)(2,1)}, u32[]{:S(2)}, u32[]{:S(2)}) collective-permute-start(bf16[512,2048]{1,0:T(8,128)(2,1)} %pad_maximum_fusion.4.refs_1_), channel_id=1, source_target_pairs={{0,4},{4,0},{8,12},{12,8},{16,20},{20,16},{24,28},{28,24},{1,5},{5... | collective-permute-start | bytes 6291464 | tf_op jit(solution)/shard_map/ppermute | solution.py:403
  333.7 52.7 %collective-permute-start.23 = (bf16[512,2048]{1,0:T(8,128)(2,1)}, bf16[512,2048]{1,0:T(8,128)(2,1)}, u32[]{:S(2)}, u32[]{:S(2)}) collective-permute-start(bf16[512,2048]{1,0:T(8,128)(2,1)} %collective-permute-done.21.refs_0_.refs_4_), channel_id=1, source_target_pairs={{0,4},{4,0},{8,12},{12,8},{16,20},{20,16},{24,28},{28,24},{1,5},{5... | collective-permute-start | bytes 6291464 | tf_op jit(solution)/shard_map/ppermute | solution.py:403
  334.3 52.2 %collective-permute-start.24 = (bf16[512,2048]{1,0:T(8,128)(2,1)}, bf16[512,2048]{1,0:T(8,128)(2,1)}, u32[]{:S(2)}, u32[]{:S(2)}) collective-permute-start(bf16[512,2048]{1,0:T(8,128)(2,1)} %collective-permute-done.22.refs_1_.refs_5_), channel_id=1, source_target_pairs={{0,4},{4,0},{8,12},{12,8},{16,20},{20,16},{24,28},{28,24},{1,5},{5... | collective-permute-start | bytes 6291464 | tf_op jit(solution)/shard_map/ppermute | solution.py:403
  428.0 47.9 %collective-permute-start.29 = (bf16[512,2048]{1,0:T(8,128)(2,1)}, bf16[512,2048]{1,0:T(8,128)(2,1)S(1)}, u32[]{:S(2)}, u32[]{:S(2)}) collective-permute-start(bf16[512,2048]{1,0:T(8,128)(2,1)} %add_convert_fusion.6), channel_id=1, source_target_pairs={{0,8},{4,12},{8,0},{12,4},{16,24},{20,28},{24,16},{28,20},{1,9},{5... | collective-permute-start | bytes 6291464 | tf_op jit(solution)/shard_map/ppermute | solution.py:403
  429.3 48.0 %collective-permute-start.28 = (bf16[512,2048]{1,0:T(8,128)(2,1)}, bf16[512,2048]{1,0:T(8,128)(2,1)}, u32[]{:S(2)}, u32[]{:S(2)}) collective-permute-start(bf16[512,2048]{1,0:T(8,128)(2,1)} %add_convert_fusion.7), channel_id=1, source_target_pairs={{0,16},{4,20},{8,24},{12,28},{16,0},{20,4},{24,8},{28,12},{1,17},{... | collective-permute-start | bytes 6291464 | tf_op jit(solution)/shard_map/ppermute | solution.py:403
  482.3 38.3 %collective-permute-start.31 = (bf16[256,2048]{1,0:T(8,128)(2,1)}, bf16[256,2048]{1,0:T(8,128)(2,1)}, u32[]{:S(2)}, u32[]{:S(2)}) collective-permute-start(bf16[256,2048]{1,0:T(8,128)(2,1)} %slice.454), channel_id=1, source_target_pairs={{0,16},{4,20},{8,24},{12,28},{16,0},{20,4},{24,8},{28,12},{1,17},{... | collective-permute-start | bytes 3145736 | tf_op jit(solution)/shard_map/ppermute | solution.py:403
  484.6 38.4 %collective-permute-start.30 = (bf16[256,2048]{1,0:T(8,128)(2,1)}, bf16[256,2048]{1,0:T(8,128)(2,1)S(1)}, u32[]{:S(2)}, u32[]{:S(2)}) collective-permute-start(bf16[256,2048]{1,0:T(8,128)(2,1)} %slice.455), channel_id=1, source_target_pairs={{0,8},{4,12},{8,0},{12,4},{16,24},{20,28},{24,16},{28,20},{1,9},{5... | collective-permute-start | bytes 3145736 | tf_op jit(solution)/shard_map/ppermute | solution.py:403
  490.0 34.7 %collective-permute-start.32 = (bf16[512,2048]{1,0:T(8,128)(2,1)}, bf16[512,2048]{1,0:T(8,128)(2,1)}, u32[]{:S(2)}, u32[]{:S(2)}) collective-permute-start(bf16[512,2048]{1,0:T(8,128)(2,1)} %convolution_convert_fusion.6), channel_id=1, source_target_pairs={{0,4},{4,0},{8,12},{12,8},{16,20},{20,16},{24,28},{28,24},{1,5},{5... | collective-permute-start | bytes 6291464 | tf_op jit(solution)/shard_map/ppermute | solution.py:403
  493.7 38.6 %collective-permute-start.33 = (bf16[512,2048]{1,0:T(8,128)(2,1)}, bf16[512,2048]{1,0:T(8,128)(2,1)S(1)}, u32[]{:S(2)}, u32[]{:S(2)}) collective-permute-start(bf16[512,2048]{1,0:T(8,128)(2,1)} %convolution_convert_fusion.5), channel_id=1, source_target_pairs={{0,4},{4,0},{8,12},{12,8},{16,20},{20,16},{24,28},{28,24},{1,5},{5... | collective-permute-start | bytes 6291464 | tf_op jit(solution)/shard_map/ppermute | solution.py:403
  494.2 200.3 %reduce-scatter.7.cloned.1.call-start = ((), (), s32[]{:S(2)}) async-start(), calls=%async_computation.11 | async-start | bytes 5242880 | tf_op jit(solution)/shard_map/reduce_scatter | solution.py:588
  547.0 8.4 %collective-permute-start.34 = (bf16[1024,2048]{1,0:T(8,128)(2,1)}, bf16[1024,2048]{1,0:T(8,128)(2,1)S(1)}, u32[]{:S(2)}, u32[]{:S(2)}) collective-permute-start(bf16[1024,2048]{1,0:T(8,128)(2,1)} %convolution_convert_fusion.2), channel_id=1, source_target_pairs={{0,4},{4,0},{8,12},{12,8},{16,20},{20,16},{24,28},{28,24},{1,5},{5... | collective-permute-start | bytes 12582920 | tf_op jit(solution)/shard_map/ppermute | solution.py:403
  547.0 48.3 %collective-permute-start.35 = (bf16[512,2048]{1,0:T(8,128)(2,1)}, bf16[512,2048]{1,0:T(8,128)(2,1)S(1)}, u32[]{:S(2)}, u32[]{:S(2)}) collective-permute-start(bf16[512,2048]{1,0:T(8,128)(2,1)} %add_convert_fusion.5), channel_id=1, source_target_pairs={{0,16},{4,20},{8,24},{12,28},{16,0},{20,4},{24,8},{28,12},{1,17},{... | collective-permute-start | bytes 6291464 | tf_op jit(solution)/shard_map/ppermute | solution.py:403
  548.1 47.9 %collective-permute-start.36 = (bf16[512,2048]{1,0:T(8,128)(2,1)}, bf16[512,2048]{1,0:T(8,128)(2,1)S(1)}, u32[]{:S(2)}, u32[]{:S(2)}) collective-permute-start(bf16[512,2048]{1,0:T(8,128)(2,1)} %add_convert_fusion.4), channel_id=1, source_target_pairs={{0,8},{4,12},{8,0},{12,4},{16,24},{20,28},{24,16},{28,20},{1,9},{5... | collective-permute-start | bytes 6291464 | tf_op jit(solution)/shard_map/ppermute | solution.py:403
  600.4 31.6 %collective-permute-start.37 = (bf16[1024,2048]{1,0:T(8,128)(2,1)}, bf16[1024,2048]{1,0:T(8,128)(2,1)}, u32[]{:S(2)}, u32[]{:S(2)}) collective-permute-start(bf16[1024,2048]{1,0:T(8,128)(2,1)} %convolution_convert_fusion.1), channel_id=1, source_target_pairs={{0,4},{4,0},{8,12},{12,8},{16,20},{20,16},{24,28},{28,24},{1,5},{5... | collective-permute-start | bytes 12582920 | tf_op jit(solution)/shard_map/ppermute | solution.py:403
  602.8 25.9 %collective-permute-start.38 = (bf16[256,2048]{1,0:T(8,128)(2,1)}, bf16[256,2048]{1,0:T(8,128)(2,1)}, u32[]{:S(2)}, u32[]{:S(2)}) collective-permute-start(bf16[256,2048]{1,0:T(8,128)(2,1)} %get-tuple-element.219), channel_id=1, source_target_pairs={{0,16},{4,20},{8,24},{12,28},{16,0},{20,4},{24,8},{28,12},{1,17},{... | collective-permute-start | bytes 3145736 | tf_op jit(solution)/shard_map/ppermute | solution.py:403
  603.7 28.3 %collective-permute-start.39 = (bf16[256,2048]{1,0:T(8,128)(2,1)}, bf16[256,2048]{1,0:T(8,128)(2,1)}, u32[]{:S(2)}, u32[]{:S(2)}) collective-permute-start(bf16[256,2048]{1,0:T(8,128)(2,1)} %get-tuple-element.220), channel_id=1, source_target_pairs={{0,8},{4,12},{8,0},{12,4},{16,24},{20,28},{24,16},{28,20},{1,9},{5... | collective-permute-start | bytes 3145736 | tf_op jit(solution)/shard_map/ppermute | solution.py:403
  611.1 45.9 %collective-permute-start.40 = (bf16[2,256,256]{2,1,0:T(8,128)(2,1)}, bf16[2,256,256]{2,1,0:T(8,128)(2,1)S(1)}, u32[]{:S(2)}, u32[]{:S(2)}) collective-permute-start(bf16[2,256,256]{2,1,0:T(8,128)(2,1)} %get-tuple-element.287), channel_id=1, source_target_pairs={{0,1},{1,2},{2,3},{3,0},{4,5},{5,6},{6,7},{7,4},{8,9},{9,10},{10,1... | collective-permute-start | bytes 786440 | tf_op jit(solution)/shard_map/ppermute | solution.py:348
  614.1 42.9 %collective-permute-start.41 = (bf16[2,256,256]{2,1,0:T(8,128)(2,1)}, bf16[2,256,256]{2,1,0:T(8,128)(2,1)S(1)}, u32[]{:S(2)}, u32[]{:S(2)}) collective-permute-start(bf16[2,256,256]{2,1,0:T(8,128)(2,1)} %get-tuple-element.286), channel_id=1, source_target_pairs={{0,2},{1,3},{2,0},{3,1},{4,6},{5,7},{6,4},{7,5},{8,10},{9,11},{10,... | collective-permute-start | bytes 786440 | tf_op jit(solution)/shard_map/ppermute | solution.py:348
  628.7 28.4 %collective-permute-start.42 = (bf16[2,256,256]{2,1,0:T(8,128)(2,1)}, bf16[2,256,256]{2,1,0:T(8,128)(2,1)S(1)}, u32[]{:S(2)}, u32[]{:S(2)}) collective-permute-start(bf16[2,256,256]{2,1,0:T(8,128)(2,1)} %get-tuple-element.285), channel_id=1, source_target_pairs={{0,3},{1,0},{2,1},{3,2},{4,7},{5,4},{6,5},{7,6},{8,11},{9,8},{10,9... | collective-permute-start | bytes 786440 | tf_op jit(solution)/shard_map/ppermute | solution.py:348
  643.5 25.0 %collective-permute-start.44 = (bf16[128,2048]{1,0:T(8,128)(2,1)}, bf16[128,2048]{1,0:T(8,128)(2,1)}, u32[]{:S(2)}, u32[]{:S(2)}) collective-permute-start(bf16[128,2048]{1,0:T(8,128)(2,1)} %slice.458), channel_id=1, source_target_pairs={{0,16},{4,20},{8,24},{12,28},{16,0},{20,4},{24,8},{28,12},{1,17},{... | collective-permute-start | bytes 1572872 | tf_op jit(solution)/shard_map/ppermute | solution.py:403
  659.4 15.2 %collective-permute-start.43 = (bf16[128,2048]{1,0:T(8,128)(2,1)}, bf16[128,2048]{1,0:T(8,128)(2,1)}, u32[]{:S(2)}, u32[]{:S(2)}) collective-permute-start(bf16[128,2048]{1,0:T(8,128)(2,1)} %slice.459), channel_id=1, source_target_pairs={{0,8},{4,12},{8,0},{12,4},{16,24},{20,28},{24,16},{28,20},{1,9},{5... | collective-permute-start | bytes 1572872 | tf_op jit(solution)/shard_map/ppermute | solution.py:403
  660.8 60.0 %collective-permute-start.46 = (bf16[256,2048]{1,0:T(8,128)(2,1)}, bf16[256,2048]{1,0:T(8,128)(2,1)}, u32[]{:S(2)}, u32[]{:S(2)}) collective-permute-start(bf16[256,2048]{1,0:T(8,128)(2,1)} %get-tuple-element.266), channel_id=1, source_target_pairs={{0,16},{4,20},{8,24},{12,28},{16,0},{20,4},{24,8},{28,12},{1,17},{... | collective-permute-start | bytes 3145736 | tf_op jit(solution)/shard_map/ppermute | solution.py:403
  662.1 58.6 %collective-permute-start.47 = (bf16[256,2048]{1,0:T(8,128)(2,1)}, bf16[256,2048]{1,0:T(8,128)(2,1)}, u32[]{:S(2)}, u32[]{:S(2)}) collective-permute-start(bf16[256,2048]{1,0:T(8,128)(2,1)} %get-tuple-element.265), channel_id=1, source_target_pairs={{0,8},{4,12},{8,0},{12,4},{16,24},{20,28},{24,16},{28,20},{1,9},{5... | collective-permute-start | bytes 3145736 | tf_op jit(solution)/shard_map/ppermute | solution.py:403
  662.7 124.9 %all-to-all-start.1 = ((bf16[8,64,1024]{2,1,0:T(8,128)(2,1)}), bf16[8,64,1024]{2,1,0:T(8,128)(2,1)S(1)}, u32[]{:S(2)}, u32[]{:S(2)}) async-start(bf16[8,64,1024]{2,1,0:T(8,128)(2,1)} %reduce-scatter.5.cloned.1.call-done), calls=%async_computation.5 | async-start | bytes 2097152 | tf_op jit(solution)/shard_map/all_to_all | solution.py:695
  666.3 129.8 %reduce-scatter.11.cloned.1.call-start = ((), (), s32[]{:S(2)}) async-start(), calls=%async_computation.13 | async-start | bytes 1310720 | tf_op jit(solution)/shard_map/reduce_scatter | solution.py:678
  710.7 88.9 %reduce-scatter.9.cloned.1.call-start = ((), (), s32[]{:S(2)}) async-start(), calls=%async_computation.12 | async-start | bytes 1310720 | tf_op jit(solution)/shard_map/reduce_scatter | solution.py:680
  726.9 44.6 %collective-permute-start.48 = (bf16[1024,2048]{1,0:T(8,128)(2,1)}, bf16[1024,2048]{1,0:T(8,128)(2,1)}, u32[]{:S(2)}, u32[]{:S(2)}) collective-permute-start(bf16[1024,2048]{1,0:T(8,128)(2,1)} %convolution_convert_fusion.3), channel_id=1, source_target_pairs={{0,4},{4,0},{8,12},{12,8},{16,20},{20,16},{24,28},{28,24},{1,5},{5... | collective-permute-start | bytes 12582920 | tf_op jit(solution)/shard_map/ppermute | solution.py:403
  730.2 36.4 %collective-permute-start.52 = (bf16[128,2048]{1,0:T(8,128)(2,1)}, bf16[128,2048]{1,0:T(8,128)(2,1)}, u32[]{:S(2)}, u32[]{:S(2)}) collective-permute-start(bf16[128,2048]{1,0:T(8,128)(2,1)} %slice.456), channel_id=1, source_target_pairs={{0,16},{4,20},{8,24},{12,28},{16,0},{20,4},{24,8},{28,12},{1,17},{... | collective-permute-start | bytes 1572872 | tf_op jit(solution)/shard_map/ppermute | solution.py:403
  735.7 33.1 %collective-permute-start.51 = (bf16[128,2048]{1,0:T(8,128)(2,1)}, bf16[128,2048]{1,0:T(8,128)(2,1)}, u32[]{:S(2)}, u32[]{:S(2)}) collective-permute-start(bf16[128,2048]{1,0:T(8,128)(2,1)} %slice.457), channel_id=1, source_target_pairs={{0,8},{4,12},{8,0},{12,4},{16,24},{20,28},{24,16},{28,20},{1,9},{5... | collective-permute-start | bytes 1572872 | tf_op jit(solution)/shard_map/ppermute | solution.py:403
  736.3 12.0 %collective-permute-start.53 = (bf16[288,256]{1,0:T(8,128)(2,1)S(1)}, bf16[288,256]{1,0:T(8,128)(2,1)S(1)}, u32[]{:S(2)}, u32[]{:S(2)}) collective-permute-start(bf16[288,256]{1,0:T(8,128)(2,1)S(1)} %get-tuple-element.289), channel_id=1, source_target_pairs={{0,16},{4,20},{8,24},{12,28},{16,0},{20,4},{24,8},{28,12},{1,17},{... | collective-permute-start | bytes 442376 | tf_op jit(solution)/shard_map/ppermute | solution.py:403
  737.3 12.6 %collective-permute-start.56 = (bf16[144,256]{1,0:T(8,128)(2,1)S(1)}, bf16[144,256]{1,0:T(8,128)(2,1)S(1)}, u32[]{:S(2)}, u32[]{:S(2)}) collective-permute-start(bf16[144,256]{1,0:T(8,128)(2,1)S(1)} %slice.460), channel_id=1, source_target_pairs={{0,16},{4,20},{8,24},{12,28},{16,0},{20,4},{24,8},{28,12},{1,17},{... | collective-permute-start | bytes 221192 | tf_op jit(solution)/shard_map/ppermute | solution.py:403
  758.0 35.8 %collective-permute-start.59 = (bf16[17664]{0:T(1024)(128)(2,1)S(1)}, bf16[17664]{0:T(1024)(128)(2,1)S(1)}, u32[]{:S(2)}, u32[]{:S(2)}) collective-permute-start(bf16[17664]{0:T(1024)(128)(2,1)S(1)} %get-tuple-element.257), channel_id=1, source_target_pairs={{0,3},{1,0},{2,1},{3,2},{4,7},{5,4},{6,5},{7,6},{8,11},{9,8},{10,9... | collective-permute-start | bytes 105992 | tf_op jit(solution)/shard_map/ppermute | solution.py:348
  760.6 33.2 %collective-permute-start.58 = (bf16[17664]{0:T(1024)(128)(2,1)S(1)}, bf16[17664]{0:T(1024)(128)(2,1)S(1)}, u32[]{:S(2)}, u32[]{:S(2)}) collective-permute-start(bf16[17664]{0:T(1024)(128)(2,1)S(1)} %get-tuple-element.258), channel_id=1, source_target_pairs={{0,2},{1,3},{2,0},{3,1},{4,6},{5,7},{6,4},{7,5},{8,10},{9,11},{10,... | collective-permute-start | bytes 105992 | tf_op jit(solution)/shard_map/ppermute | solution.py:348
  766.7 27.1 %collective-permute-start.57 = (bf16[17664]{0:T(1024)(128)(2,1)S(1)}, bf16[17664]{0:T(1024)(128)(2,1)S(1)}, u32[]{:S(2)}, u32[]{:S(2)}) collective-permute-start(bf16[17664]{0:T(1024)(128)(2,1)S(1)} %get-tuple-element.256), channel_id=1, source_target_pairs={{0,1},{1,2},{2,3},{3,0},{4,5},{5,6},{6,7},{7,4},{8,9},{9,10},{10,1... | collective-permute-start | bytes 105992 | tf_op jit(solution)/shard_map/ppermute | solution.py:348
  786.1 21.9 %collective-permute-start.50 = (bf16[256,2048]{1,0:T(8,128)(2,1)}, bf16[256,2048]{1,0:T(8,128)(2,1)S(1)}, u32[]{:S(2)}, u32[]{:S(2)}) collective-permute-start(bf16[256,2048]{1,0:T(8,128)(2,1)} %slice.452), channel_id=1, source_target_pairs={{0,16},{4,20},{8,24},{12,28},{16,0},{20,4},{24,8},{28,12},{1,17},{... | collective-permute-start | bytes 3145736 | tf_op jit(solution)/shard_map/ppermute | solution.py:403
  792.3 21.4 %collective-permute-start.49 = (bf16[256,2048]{1,0:T(8,128)(2,1)S(1)}, bf16[256,2048]{1,0:T(8,128)(2,1)S(1)}, u32[]{:S(2)}, u32[]{:S(2)}) collective-permute-start(bf16[256,2048]{1,0:T(8,128)(2,1)S(1)} %slice.453), channel_id=1, source_target_pairs={{0,8},{4,12},{8,0},{12,4},{16,24},{20,28},{24,16},{28,20},{1,9},{5... | collective-permute-start | bytes 3145736 | tf_op jit(solution)/shard_map/ppermute | solution.py:403
  (89 other events, 1353.4 us)
Sparse Core Ops, SparseCore 0:
  17.7 35.3 all-gather.4
  59.4 63.6 all-gather.6
  155.7 84.1 all-gather.8
  241.4 80.7 all-gather.10
  494.3 77.4 reduce-scatter.4
  600.6 93.8 reduce-scatter.6
  710.8 31.9 reduce-scatter.10
  771.6 27.9 reduce-scatter.8

commit v9 on v8

--- a/solution.py
+++ b/solution.py
@@ -488,9 +488,7 @@
         out_pieces = line.gather(out_weight)
         *out_pieces, down_late = tie(*out_pieces, down_weight)
         full_o = line.in_order(out_pieces)
-        down_pieces = [down_late]
-        while len(down_pieces) < min(3, n_z):
-            down_pieces.append(line.send(down_pieces[-1], 1))
+        down_pieces = [down_late, line.send(down_late, 1)]
         inputs = tokens.reshape(rows, width).astype(F32)
         mean_one, recip_one = norm_stats(inputs)
         grad_near_sib = plane.cross(grad_near)
@@ -515,7 +513,7 @@
         key_value, normed_late, up_cols = tie(key_value, normed_one, up_cols)
         kv_pieces = line.gather(key_value.reshape(windows, local_len, 2 * HD))
         queries = (dot_nn(normed_late, full_q) + bias_q).astype(BF16)
-        queries, *kv_pieces = tie(queries, *kv_pieces)
+        queries, down_late, *kv_pieces = tie(queries, down_pieces[-1], *kv_pieces)
         kv_window = line.in_order(kv_pieces, 1)
 
         first = (lax.axis_index("fsdp") * local_len).astype(jnp.int32).reshape(1)
@@ -523,11 +521,13 @@
         upto = jnp.arange(file_count)[:, None] <= jnp.arange(file_count)[None, :]
         file_ends = jnp.sum(jnp.where(upto[None], lengths[:, :, None], 0), axis=1)
         grad_far = plane.across(grad_near, plane.last)
-        while len(down_pieces) < n_z:
-            down_pieces.append(line.send(down_pieces[-1], 1))
+        while len(down_pieces) < n_z - 1:
+            down_late = line.send(down_late, 1)
+            down_pieces.append(down_late)
         up_part = lax.all_gather(up_cols, "fsdp", axis=1, tiled=True).reshape(width, ff_own)
         attended, norms = attn_forward(queries, kv_window, first, file_ends)
         attended, down_pieces[-1] = tie(attended, down_pieces[-1])
+        down_pieces.append(line.send(down_pieces[-1], 1))
         middle = inputs + dot_nn(attended, full_o) + bias_o
         mean_two, recip_two = norm_stats(middle)
         xhat_two = (middle - mean_two) * recip_two
@@ -548,13 +548,13 @@
         back_far = back_product(grad_lots[1], down_late)
         bias_up_part = lax.dynamic_slice_in_dim(bias_up, my_dp * ff_own, ff_own)
         hid_near, pre_near = middle_layer(two_lots[0], back_near, up_part, bias_up_part)
+        back_far, attended_late, normed_late, pre_near[0], pre_near[1], *two_far = tie(
+            back_far, attended_late, normed_late, *pre_near, *two_far
+        )
+        two_lots.append([*two_far, *plane.cross(two_far)])
         att_mine, att_sib = reorder(attended_late, places)
         one_mine, one_sib = reorder(normed_late, places)
-        back_far, pre_near[0], pre_near[1], *arrived = tie(
-            back_far, *pre_near, att_mine, att_sib, one_mine, one_sib
-        )
-        att_mine, att_sib, one_mine, one_sib = arrived
-        two_lots.append([*two_far, *plane.cross(two_far)])
+        back_far, att_mine, att_sib, one_mine, one_sib = tie(back_far, att_mine, att_sib, one_mine, one_sib)
         hid_far, pre_far = middle_layer(two_lots[1], back_far, up_part, bias_up_part)
         block = two_near[0].shape[0]
         lots = (slice(None, block), slice(block, None))
@@ -619,18 +619,22 @@
         wo_got = send_rows(wo_parts)
 
         query_grad, kv_terms = attn_backward(queries, kv_window, norms, attended_grad, first, file_ends)
-        query_grad, kv_terms, *out_got = tie(query_grad, kv_terms, *out_got)
+        query_grad, kv_terms, grad_up, *arrived = tie(query_grad, kv_terms, grad_up, *out_got, *wo_got)
+        out_got, wo_got = arrived[:2], arrived[2:]
         kv_got = line.scatter(kv_terms.reshape(windows, n_z, local_len, 2 * HD), 1)
         theirs = plane.swap(dot_tn(one_sib, query_grad).astype(BF16), 1)
-        theirs, grad_up, *wo_got = tie(theirs, grad_up, *wo_got)
         wq_parts = cut(plus(one_mine, query_grad, theirs))
         wq_got = send_rows(wq_parts)
         wq_parts[1], query_late, hid_late = tie(wq_parts[1], query_grad, hid_near[1])
-        wq_parts[1], *kv_got = tie(wq_parts[1], *kv_got)
+        theirs = plane.swap(dot_nn(hid_late, down_part).astype(BF16), 1)
         query_part = dot_nt(query_late, full_q)
+        query_part, hid_near[0], theirs, *kv_got = tie(query_part, hid_near[0], theirs, *kv_got)
+        out_sum = ours(hid_near, down_part, dot_nn, theirs, out_got)
         kv_grad = total(kv_got).astype(BF16).reshape(rows, 2 * HD)
         wo_rows = own_rows(wo_parts, wo_got)
-        query_part, kv_grad, wo_rows, grad_down = tie(query_part, kv_grad, wo_rows, grad_down)
+        query_part, kv_grad, wo_rows, *arrived = tie(query_part, kv_grad, wo_rows, *out_sum, *wq_got)
+        out_sum, wq_got = arrived[:2], arrived[2:]
+        branch_out = plane.fold(out_sum)
 
         one_grad = query_part + dot_nt(kv_grad, full_kv)
         grad_bq = jnp.sum(query_late.astype(F32), axis=0)
@@ -640,23 +644,25 @@
         up_bias_part = sum(jnp.sum(lot.astype(F32), axis=0) for lot in pre_near + pre_far)
         grad_bup = jnp.where(jnp.arange(n_dp)[:, None] == my_dp, up_bias_part[None], 0.0).reshape(-1)
         sums = (
-            grad_bq,
-            grad_bv,
-            grad_bo,
-            grad_gain_one,
-            grad_shift_one,
-            grad_bup,
-            grad_bdown,
-            grad_gain_two,
-            grad_shift_two,
+            (0, grad_bq),
+            (2, grad_bo),
+            (5, grad_bup),
+            (6, grad_bdown),
+            (7, grad_gain_two),
+            (8, grad_shift_two),
+            (1, grad_bv),
+            (3, grad_gain_one),
+            (4, grad_shift_one),
         )
         row_of = jnp.concatenate(
             [
-                jnp.pad(v.reshape(n_dev, size), ((0, 0), (0, room - size)))
-                for v, size, room in zip(sums, sizes, rooms)
+                jnp.pad(v.reshape(n_dev, sizes[i]), ((0, 0), (0, rooms[i] - sizes[i])))
+                for i, v in sums
             ],
             axis=1,
         )
+        order = [i for i, _ in sums]
+        sum_starts = {i: sum(rooms[j] for j in order[:at]) for at, i in enumerate(order)}
         per_half = n_z // 2 * row_of.shape[1]
         more = -(-per_half // (16 * 2 * HD)) * 16
         row_of = jnp.pad(row_of.reshape(2 * n_dp, per_half), ((0, 0), (0, more * 2 * HD - per_half)))
@@ -672,8 +678,7 @@
         theirs = plane.swap(with_vectors(dot_tn(one_sib, kv_grad), 1).astype(BF16), 1)
         kv_parts = cut((with_vectors(dot_tn(one_mine, kv_grad), 0) + theirs.astype(F32)).astype(BF16))
         kv_parts_got = send_rows(kv_parts)
-        kv_parts[1], hid_late, hid_near[0], *wq_got = tie(kv_parts[1], hid_late, hid_near[0], *wq_got)
-        theirs = plane.swap(dot_nn(hid_late, down_part).astype(BF16), 1)
+        kv_parts[1], grad_down = tie(kv_parts[1], grad_down)
 
         grad_wo = lax.psum_scatter(wo_rows.astype(BF16), "fsdp", scatter_dimension=0, tiled=True)
         wq_rows = own_rows(wq_parts, wq_got).astype(BF16)
@@ -688,8 +693,7 @@
             axis=1,
         )
         kv_last = line.scatter(kv_last, 0)
-        out_sum = ours(hid_near, down_part, dot_nn, theirs, out_got)
-        output = (middle + plane.fold(out_sum) + bias_down).astype(BF16).reshape(windows, local_len, width)
+        output = (middle + branch_out + bias_down).astype(BF16).reshape(windows, local_len, width)
         tokens_grad = middle_grad + norm_pull(one_grad, xhat_one, recip_one, gain_one)
         tokens_grad = tokens_grad.astype(BF16).reshape(windows, local_len, width)
         grad_up = lax.all_to_all(
@@ -698,7 +702,7 @@
         kv_own = total(kv_last)
         flat = kv_own[own * 2 * HD :]
         bq, bv, bo, gain1, shift1, bup, bdown, gain2, shift2 = (
-            flat[start : start + size] for start, size in zip(starts, sizes)
+            flat[sum_starts[i] : sum_starts[i] + size] for i, size in enumerate(sizes)
         )
         return (
             output,

time: 833 us -> 819 us (0.983)
  waiting for transfers between devices: 234 us -> 219 us
  starting transfers between devices: 101 us -> 110 us
    ppermute x45, waiting for transfers between devices: 130 us -> 102 us  [swap(): return lax.ppermute(block, 'dp', [(i, i ^ bit) for i in range(self.count)])]
    reduce_scatter x1, waiting for transfers between devices: 17.3 us -> 0.01 us  [local(): lax.psum_scatter(down_terms, 'fsdp', scatter_dimension=0, tiled=True)]
    all_gather x1, waiting for transfers between devices: 0.01 us -> 11.5 us  [local(): packed = lax.all_gather(packed, 'dp', axis=0, tiled=True)]
    reduce_scatter x1, waiting for transfers between devices: 1.7 us -> 12.3 us  [local(): grad_wq = lax.psum_scatter(wq_rows, 'fsdp', scatter_dimension=0, tiled=True)]
    unnamed x188 -> x192, local copies, waits for them, and re-layouts: 28.3 us -> 31.4 us
  transfers between devices with their start and end apart: 70 -> 70, of which waited for: 26 -> 33; matrix products, arithmetic and copies ran while one was open for 29% -> 28% of each run, Pallas kernels for 20% -> 20%
where the time goes in v9:
time: 819 us; the launch traced here: 810 us
  waiting for transfers between devices  219 us (27%)
  Pallas kernels  181 us (22%)
  starting transfers between devices  110 us (13%)
  matrix products  109 us (13%)
  local copies, waits for them, and re-layouts  89.6 us (11%)
  other arithmetic  85.5 us (10%)
  between operations  15.9 us (2%)
    ppermute x45, waiting for transfers between devices, swap(): return lax.ppermute(block, 'dp', [(i, i ^ bit) for i in range(self.count)])  102 us
    ppermute x15, waiting for transfers between devices, send(): lax.ppermute(block, 'fsdp', [(i, (i + places) % self.count) for i in rang...  80.5 us
    ppermute x15, starting transfers between devices, send(): lax.ppermute(block, 'fsdp', [(i, (i + places) % self.count) for i in rang...  64.6 us
    pallas_call x2, Pallas kernels, weight_grad(): pl.pallas_call(functools.partial(weight_kernel, count), out_shape=jax.Sha...  50.5 us
    dot_general x9, matrix products, dot_nn(): return jnp.dot(left, right, preferred_element_type=F32)  49.2 us
    dot_general x9, matrix products, dot_nt(): lax.dot_general(left, right, (((1,), (1,)), ((), ())), preferred_element_...  42.2 us
    pallas_call x2, Pallas kernels, middle_layer(): pl.pallas_call(functools.partial(middle_kernel, count), out_shape=[jax.Sh...  39.7 us
    ppermute x45, starting transfers between devices, swap(): return lax.ppermute(block, 'dp', [(i, i ^ bit) for i in range(self.count)])  37.5 us
  transfers between devices with their start and end apart: 70, of which 33 were waited for; matrix products, arithmetic and copies ran while one was open for 28% of the time, Pallas kernels for 20%

profile of v9, /device:TPU:0, one launch (start us, length us, event | category | flops | bytes accessed | tf_op | source)
XLA Modules:
  0.0 809.9 jit_solution(12072819700486962852)
XLA Ops:
  20.3 2.9 collective-permute-start
  25.8 3.6 all-to-all-start
  29.4 17.9 %collective-permute-done = bf16[256,2048]{1,0:T(8,128)(2,1)} collective-permute-done((bf16[256,2048]{1,0:T(8,128)(2,1)S(1)}, bf16[256,2048]{1,0:T(8,128)(2,1)}, u32[]{:S(2)}, u32[]{:S(2)}) %collective-permute-start) | collective-permute-done | bytes 1048608 | tf_op jit(solution)/shard_map/ppermute | solution.py:403
  49.9 3.1 pad_maximum_fusion.2.refs_1_.refs_9_
  53.0 6.3 all-to-all-done
  67.7 3.5 collective-permute-done.2
  71.1 10.4 %collective-permute-done.3 = bf16[64,2048]{1,0:T(8,128)(2,1)} collective-permute-done((bf16[64,2048]{1,0:T(8,128)(2,1)S(1)}, bf16[64,2048]{1,0:T(8,128)(2,1)}, u32[]{:S(2)}, u32[]{:S(2)}) %collective-permute-start.3) | collective-permute-done | bytes 262176 | tf_op jit(solution)/shard_map/ppermute | solution.py:348
  81.6 6.1 collective-permute-start.5
  94.6 17.0 %collective-permute-done.5 = bf16[256,2048]{1,0:T(8,128)(2,1)} collective-permute-done((bf16[256,2048]{1,0:T(8,128)(2,1)}, bf16[256,2048]{1,0:T(8,128)(2,1)}, u32[]{:S(2)}, u32[]{:S(2)}) %collective-permute-start.5) | collective-permute-done | bytes 1048608 | tf_op jit(solution)/shard_map/ppermute | solution.py:348
  111.6 11.5 %all-gather.7.cloned.1.call-done = bf16[2560,2048]{1,0:T(8,128)(2,1)} async-done(((bf16[320,2048]{1,0:T(8,128)(2,1)}), bf16[2560,2048]{1,0:T(8,128)(2,1)}) %all-gather.7.cloned.1.call-update) | async-done | bytes 10485776 | tf_op jit(solution)/shard_map/all_gather | solution.py:487
  125.4 8.6 %slice.340 = bf16[32,64,2048]{2,1,0:T(8,128)(2,1)} slice(bf16[32,80,2048]{2,1,0:T(8,128)(2,1)} %bitcast.166), slice={[0:32], [0:64], [0:2048]} | slice | bytes 16777216 | tf_op jit(solution)/shard_map/slice | solution.py:502
  134.1 3.0 fusion.44
  153.4 10.5 %add_convert_fusion.9.q_ref = bf16[512,2048]{1,0:T(8,128)(2,1)} fusion(bf16[512,2048]{1,0:T(8,128)(2,1)} %fusion.14.first_ref.second_ref, bf16[2048,2048]{1,0:T(8,128)(2,1)} %bitcast.168, f32[2048]{0:T(1024)S(1)} %reshape.404), kind=kOutput, calls=%fused_computation.51 | convolution fusion | flops 4297064448 | bytes 12591104 | tf_op jit(solution)/shard_map/dot_general | solution.py:21
  163.8 5.7 collective-permute-done.9
  170.3 5.5 collective-permute-start.11
  181.0 18.8 %shard_map.288 = (bf16[512,2048]{1,0:T(8,128)(2,1)S(1)}, f32[512,128]{1,0:T(8,128)S(1)}) custom-call(s32[1]{0:T(128)} %bitcast.1.pos_ref, s32[2,8]{1,0:T(2,128)S(1)} %select_reduce_fusion.ends_ref, bf16[512,2048]{1,0:T(8,128)(2,1)S(1)} %copy-done.11, bf16[2,1024,256]{2,1,0:T(8,128)(2,1)S(1)} %constant_dynamic-update-slice_fusion.15.kv_ref), custom_call_target="tpu_custom_call" | custom-call | flops 67108864 | bytes 65536 | tf_op jit(solution)/shard_map/pallas_call | solution.py:132
  202.0 4.1 collective-permute-done.11
  206.1 4.3 collective-permute-start.14
  210.5 9.3 %fusion.50 = (f32[512]{0:T(512)S(1)}, f32[512,2048]{1,0:T(8,128)S(1)}) fusion(f32[2048]{0:T(1024)S(1)} %reshape.405, bf16[512,2048]{1,0:T(8,128)(2,1)} %copy-done.12, bf16[2048,2048]{1,0:T(8,128)(2,1)} %all-gather.9.cloned.1.call-done, bf16[2,256,2048]{2,1,0:T(8,128)(2,1)} %param.17), kind=kOutput, calls=%fused_computation.195 | convolution fusion | flops 4299161088 | bytes 16787456 | tf_op jit(solution)/shard_map/dot_general | solution.py:21
  224.1 36.9 %collective-permute-done.14 = bf16[256,2048]{1,0:T(8,128)(2,1)} collective-permute-done((bf16[256,2048]{1,0:T(8,128)(2,1)S(1)}, bf16[256,2048]{1,0:T(8,128)(2,1)}, u32[]{:S(2)}, u32[]{:S(2)}) %collective-permute-start.14) | collective-permute-done | bytes 1048608 | tf_op jit(solution)/shard_map/ppermute | solution.py:348
  268.6 13.8 %shard_map.289.refs_4_ = bf16[2048,1024]{1,0:T(8,128)(2,1)} custom-call(bf16[512,2048]{1,0:T(8,128)(2,1)S(1)} %pad_maximum_fusion.1.refs_0_.refs_8_, bf16[512,2048]{1,0:T(8,128)(2,1)S(1)} %copy-done.1, bf16[512,2048]{1,0:T(8,128)(2,1)} %collective-permute-done.6.refs_2_.refs_10_, bf16[512,2048]{1,0:T(8,128)(2,1)} %collective-permute-done.7.refs_3_.refs_11_, ...), custom_call_target="tpu_custom_call" | custom-call | flops 134217728 | bytes 262144 | tf_op jit(solution)/shard_map/pallas_call | solution.py:236
  282.4 4.4 collective-permute-done.17
  292.7 14.6 %shard_map.290.refs_4_ = bf16[2048,1024]{1,0:T(8,128)(2,1)} custom-call(bf16[512,2048]{1,0:T(8,128)(2,1)} %collective-permute-done.12.refs_0_.refs_12_, bf16[512,2048]{1,0:T(8,128)(2,1)} %collective-permute-done.13.refs_1_.refs_13_, bf16[512,2048]{1,0:T(8,128)(2,1)} %collective-permute-done.15.refs_2_.refs_14_, ...), custom_call_target="tpu_custom_call" | custom-call | flops 134217728 | bytes 262144 | tf_op jit(solution)/shard_map/pallas_call | solution.py:236
  307.3 19.8 %shard_map.291 = (bf16[1024,1024]{1,0:T(8,128)(2,1)S(1)}, bf16[1024,1024]{1,0:T(8,128)(2,1)S(1)}, bf16[1024,1024]{1,0:T(8,128)(2,1)}, bf16[1024,1024]{1,0:T(8,128)(2,1)}) custom-call(bf16[512,2048]{1,0:T(8,128)(2,1)} %pad_maximum_fusion.3.refs_0_, bf16[512,2048]{1,0:T(8,128)(2,1)} %pad_maximum_fusion.4.refs_1_, ...), custom_call_target="tpu_custom_call" | custom-call | flops 134217728 | bytes 393216 | tf_op jit(solution)/shard_map/pallas_call | solution.py:202
  329.8 8.5 %collective-permute-done.21.refs_0_.refs_4_ = bf16[512,2048]{1,0:T(8,128)(2,1)} collective-permute-done((bf16[512,2048]{1,0:T(8,128)(2,1)}, bf16[512,2048]{1,0:T(8,128)(2,1)}, u32[]{:S(2)}, u32[]{:S(2)}) %collective-permute-start.21) | collective-permute-done | bytes 2097184 | tf_op jit(solution)/shard_map/ppermute | solution.py:403
  339.6 6.5 shard_map.292
  346.2 6.6 shard_map.293
  352.8 19.9 %shard_map.294 = (bf16[1024,1024]{1,0:T(8,128)(2,1)S(1)}, bf16[1024,1024]{1,0:T(8,128)(2,1)S(1)}, bf16[1024,1024]{1,0:T(8,128)(2,1)}, bf16[1024,1024]{1,0:T(8,128)(2,1)}) custom-call(bf16[512,2048]{1,0:T(8,128)(2,1)} %collective-permute-done.21.refs_0_.refs_4_, bf16[512,2048]{1,0:T(8,128)(2,1)} %collective-permute-done.22.refs_1_.refs_5_, ...), custom_call_target="tpu_custom_call" | custom-call | flops 134217728 | bytes 393216 | tf_op jit(solution)/shard_map/pallas_call | solution.py:202
  372.8 4.5 convolution_convert_fusion.8
  381.6 3.7 add_convert_fusion.7
  385.3 3.7 add_convert_fusion.6
  389.1 4.8 convolution_convert_fusion.4
  397.2 4.0 collective-permute-done.27
  401.2 24.3 %shard_map.295 = bf16[2048,1024]{1,0:T(8,128)(2,1)} custom-call(bf16[512,2048]{1,0:T(8,128)(2,1)} %pad_maximum_fusion.3.refs_0_, bf16[512,2048]{1,0:T(8,128)(2,1)} %pad_maximum_fusion.4.refs_1_, bf16[512,2048]{1,0:T(8,128)(2,1)} %collective-permute-done.19.refs_2_, bf16[512,2048]{1,0:T(8,128)(2,1)} %collective-permute-done.20.refs_3_, ...), custom_call_target="tpu_custom_call" | custom-call | flops 268435456 | bytes 458752 | tf_op jit(solution)/shard_map/pallas_call | solution.py:276
  425.6 6.8 add_convert_fusion.3
  432.4 9.8 %collective-permute-done.29 = bf16[512,2048]{1,0:T(8,128)(2,1)S(1)} collective-permute-done((bf16[512,2048]{1,0:T(8,128)(2,1)}, bf16[512,2048]{1,0:T(8,128)(2,1)S(1)}, u32[]{:S(2)}, u32[]{:S(2)}) %collective-permute-start.29) | collective-permute-done | bytes 2097184 | tf_op jit(solution)/shard_map/ppermute | solution.py:403
  443.5 3.8 convert_add_fusion.3
  452.8 3.7 convolution_convert_fusion.6
  456.5 3.7 convolution_convert_fusion.5
  460.7 26.2 %shard_map.296 = bf16[1024,2048]{1,0:T(8,128)(2,1)} custom-call(bf16[1024,1024]{1,0:T(8,128)(2,1)} %copy-done.4, bf16[1024,1024]{1,0:T(8,128)(2,1)} %copy-done.4, bf16[1024,1024]{1,0:T(8,128)(2,1)} %copy-done.6, bf16[1024,1024]{1,0:T(8,128)(2,1)} %copy-done.6, bf16[1024,1024]{1,0:T(8,128)(2,1)} %copy-done.8, bf16[1024,1024]{1,0:T(8,128)(2,1)} %copy-done.8, ...), custom_call_target="tpu_custom_call" | custom-call | flops 268435456 | bytes 458752 | tf_op jit(solution)/shard_map/pallas_call | solution.py:276
  494.0 5.3 add_convert_fusion.5
  499.3 3.7 add_convert_fusion.4
  513.1 5.8 convolution_convert_fusion.9.grad_ref
  527.4 30.7 %shard_map.297 = (bf16[512,2048]{1,0:T(8,128)(2,1)S(1)}, bf16[2,1024,256]{2,1,0:T(8,128)(2,1)S(1)}) custom-call(s32[1]{0:T(128)} %bitcast.1.pos_ref, s32[2,8]{1,0:T(2,128)S(1)} %copy-done.14, bf16[512,2048]{1,0:T(8,128)(2,1)} %add_convert_fusion.9.q_ref, bf16[2,1024,256]{2,1,0:T(8,128)(2,1)S(1)} %copy-done.3, f32[512,128]{1,0:T(8,128)S(1)} %get-tuple-element.194.norm_ref, ...), custom_call_target="tpu_custom_call" | custom-call | flops 167772160 | bytes 163840 | tf_op jit(solution)/shard_map/pallas_call | solution.py:152
  558.0 9.6 %collective-permute-done.35 = bf16[512,2048]{1,0:T(8,128)(2,1)} collective-permute-done((bf16[512,2048]{1,0:T(8,128)(2,1)}, bf16[512,2048]{1,0:T(8,128)(2,1)}, u32[]{:S(2)}, u32[]{:S(2)}) %collective-permute-start.35) | collective-permute-done | bytes 2097184 | tf_op jit(solution)/shard_map/ppermute | solution.py:403
  569.2 20.0 %collective-permute-done.37 = bf16[256,2048]{1,0:T(8,128)(2,1)} collective-permute-done((bf16[256,2048]{1,0:T(8,128)(2,1)S(1)}, bf16[256,2048]{1,0:T(8,128)(2,1)}, u32[]{:S(2)}, u32[]{:S(2)}) %collective-permute-start.37) | collective-permute-done | bytes 1048608 | tf_op jit(solution)/shard_map/ppermute | solution.py:403
  590.4 5.6 convolution_convert_fusion.1
  603.5 4.9 add_convert_fusion.1
  613.8 6.0 convolution_convert_fusion.3
  628.2 21.5 %collective-permute-start.41 = (bf16[2,256,256]{2,1,0:T(8,128)(2,1)}, bf16[2,256,256]{2,1,0:T(8,128)(2,1)S(1)}, u32[]{:S(2)}, u32[]{:S(2)}) collective-permute-start(bf16[2,256,256]{2,1,0:T(8,128)(2,1)} %get-tuple-element.302), channel_id=1, source_target_pairs={{0,1},{1,2},{2,3},{3,0},{4,5},{5,6},{6,7},{7,4},{8,9},{9,10},{10,1... | collective-permute-start | bytes 786440 | tf_op jit(solution)/shard_map/ppermute | solution.py:348
  649.7 5.3 collective-permute-start.42
  655.0 3.6 all-to-all-start.1
  658.6 5.5 collective-permute-start.43
  668.1 5.8 all-to-all-done.1
  678.5 9.8 %fusion.51 = f32[512,2048]{1,0:T(8,128)} fusion(bf16[512,2048]{1,0:T(8,128)(2,1)S(1)} %get-tuple-element.234, bf16[2048,2048]{1,0:T(8,128)(2,1)} %bitcast.169), kind=kOutput, calls=%fused_computation.196 | convolution fusion | flops 4294967296 | bytes 14680064 | tf_op jit(solution)/shard_map/dot_general | solution.py:25
  690.8 6.4 add_convert_fusion
  698.4 4.0 convert_add_fusion.1
  702.5 11.2 %collective-permute-done.47 = bf16[256,2048]{1,0:T(8,128)(2,1)S(1)} collective-permute-done((bf16[256,2048]{1,0:T(8,128)(2,1)S(1)}, bf16[256,2048]{1,0:T(8,128)(2,1)S(1)}, u32[]{:S(2)}, u32[]{:S(2)}) %collective-permute-start.47) | collective-permute-done | bytes 1048608 | tf_op jit(solution)/shard_map/ppermute | solution.py:403
  729.3 3.6 fusion.20
  738.7 5.6 fusion.19
  745.2 4.4 collective-permute-done.51
  762.4 3.2 collective-permute-done.54
  766.6 4.2 collective-permute-start.59
  788.7 12.3 %reduce-scatter.7.cloned.1.call-done = bf16[64,2048]{1,0:T(8,128)(2,1)} async-done(((bf16[256,2048]{1,0:T(8,128)(2,1)}), bf16[64,2048]{1,0:T(8,128)(2,1)}) %reduce-scatter.7.cloned.1.call-update) | async-done | bytes 262160 | tf_op jit(solution)/shard_map/reduce_scatter | solution.py:685
  (477 shorter events, 213.9 us)
Async XLA Ops:
  7.2 52.1 %all-gather.5.cloned.1.call-start = ((), (), s32[]{:S(2)}) async-start(), calls=%async_computation.6 | async-start | bytes 1638400 | tf_op jit(solution)/shard_map/all_gather | solution.py:482
  20.3 27.0 %collective-permute-start = (bf16[256,2048]{1,0:T(8,128)(2,1)S(1)}, bf16[256,2048]{1,0:T(8,128)(2,1)}, u32[]{:S(2)}, u32[]{:S(2)}) collective-permute-start(bf16[256,2048]{1,0:T(8,128)(2,1)S(1)} %get-tuple-element.292), channel_id=1, source_target_pairs={{0,8},{4,12},{8,0},{12,4},{16,24},{20,28},{24,16},{28,20},{1,9},{5... | collective-permute-start | bytes 3145736 | tf_op jit(solution)/shard_map/ppermute | solution.py:403
  23.2 26.7 %collective-permute-start.1 = (bf16[256,2048]{1,0:T(8,128)(2,1)}, bf16[256,2048]{1,0:T(8,128)(2,1)}, u32[]{:S(2)}, u32[]{:S(2)}) collective-permute-start(bf16[256,2048]{1,0:T(8,128)(2,1)} %get-tuple-element.291), channel_id=1, source_target_pairs={{0,16},{4,20},{8,24},{12,28},{16,0},{20,4},{24,8},{28,12},{1,17},{... | collective-permute-start | bytes 3145736 | tf_op jit(solution)/shard_map/ppermute | solution.py:403
  25.8 33.5 %all-to-all-start = ((bf16[64,8,1024]{2,0,1:T(8,128)(2,1)}), bf16[64,8,1024]{2,0,1:T(8,128)(2,1)S(1)}, u32[]{:S(2)}, u32[]{:S(2)}) async-start(bf16[64,8,1024]{2,0,1:T(8,128)(2,1)} %bitcast.153), calls=%async_computation | async-start | bytes 2097152 | tf_op jit(solution)/shard_map/all_to_all | solution.py:484
  29.4 93.7 %all-gather.7.cloned.1.call-start = ((), (), s32[]{:S(2)}) async-start(), calls=%async_computation.7 | async-start | bytes 11796480 | tf_op jit(solution)/shard_map/all_gather | solution.py:487
  59.3 151.1 %all-gather.9.cloned.1.call-start = ((), (), s32[]{:S(2)}) async-start(), calls=%async_computation.8 | async-start | bytes 9437184 | tf_op jit(solution)/shard_map/all_gather | solution.py:500
  59.4 52.2 %collective-permute-start.6 = (bf16[512,2048]{1,0:T(8,128)(2,1)S(1)}, bf16[512,2048]{1,0:T(8,128)(2,1)}, u32[]{:S(2)}, u32[]{:S(2)}) collective-permute-start(bf16[512,2048]{1,0:T(8,128)(2,1)S(1)} %pad_maximum_fusion.1.refs_0_.refs_8_), channel_id=1, source_target_pairs={{0,4},{4,0},{8,12},{12,8},{16,20},{20,16},{24,28},{28,24},{1,5},{5... | collective-permute-start | bytes 6291464 | tf_op jit(solution)/shard_map/ppermute | solution.py:403
  59.4 52.1 %collective-permute-start.7 = (bf16[512,2048]{1,0:T(8,128)(2,1)}, bf16[512,2048]{1,0:T(8,128)(2,1)}, u32[]{:S(2)}, u32[]{:S(2)}) collective-permute-start(bf16[512,2048]{1,0:T(8,128)(2,1)} %pad_maximum_fusion.2.refs_1_.refs_9_), channel_id=1, source_target_pairs={{0,4},{4,0},{8,12},{12,8},{16,20},{20,16},{24,28},{28,24},{1,5},{5... | collective-permute-start | bytes 6291464 | tf_op jit(solution)/shard_map/ppermute | solution.py:403
  59.9 11.2 %collective-permute-start.2 = (bf16[64,2048]{1,0:T(8,128)(2,1)S(1)}, bf16[64,2048]{1,0:T(8,128)(2,1)}, u32[]{:S(2)}, u32[]{:S(2)}) collective-permute-start(bf16[64,2048]{1,0:T(8,128)(2,1)S(1)} %copy-done.66), channel_id=1, source_target_pairs={{0,1},{1,2},{2,3},{3,0},{4,5},{5,6},{6,7},{7,4},{8,9},{9,10},{10,1... | collective-permute-start | bytes 786440 | tf_op jit(solution)/shard_map/ppermute | solution.py:348
  61.5 20.0 %collective-permute-start.3 = (bf16[64,2048]{1,0:T(8,128)(2,1)S(1)}, bf16[64,2048]{1,0:T(8,128)(2,1)}, u32[]{:S(2)}, u32[]{:S(2)}) collective-permute-start(bf16[64,2048]{1,0:T(8,128)(2,1)S(1)} %copy-done.66), channel_id=1, source_target_pairs={{0,2},{1,3},{2,0},{3,1},{4,6},{5,7},{6,4},{7,5},{8,10},{9,11},{10,... | collective-permute-start | bytes 786440 | tf_op jit(solution)/shard_map/ppermute | solution.py:348
  64.1 17.5 %collective-permute-start.4 = (bf16[64,2048]{1,0:T(8,128)(2,1)S(1)}, bf16[64,2048]{1,0:T(8,128)(2,1)}, u32[]{:S(2)}, u32[]{:S(2)}) collective-permute-start(bf16[64,2048]{1,0:T(8,128)(2,1)S(1)} %copy-done.66), channel_id=1, source_target_pairs={{0,3},{1,0},{2,1},{3,2},{4,7},{5,4},{6,5},{7,6},{8,11},{9,8},{10,9... | collective-permute-start | bytes 786440 | tf_op jit(solution)/shard_map/ppermute | solution.py:348
  81.6 30.0 %collective-permute-start.5 = (bf16[256,2048]{1,0:T(8,128)(2,1)}, bf16[256,2048]{1,0:T(8,128)(2,1)}, u32[]{:S(2)}, u32[]{:S(2)}) collective-permute-start(bf16[256,2048]{1,0:T(8,128)(2,1)} %param.29), channel_id=1, source_target_pairs={{0,1},{1,2},{2,3},{3,0},{4,5},{5,6},{6,7},{7,4},{8,9},{9,10},{10,1... | collective-permute-start | bytes 3145736 | tf_op jit(solution)/shard_map/ppermute | solution.py:348
  123.1 184.2 %all-gather.11.cloned.1.call-start = ((), (), s32[]{:S(2)}) async-start(), calls=%async_computation.9 | async-start | bytes 5242880 | tf_op jit(solution)/shard_map/all_gather | solution.py:527
  147.9 15.9 %collective-permute-start.8 = (bf16[2,256,256]{2,1,0:T(8,128)(2,1)S(1)}, bf16[2,256,256]{2,1,0:T(8,128)(2,1)S(1)}, u32[]{:S(2)}, u32[]{:S(2)}) collective-permute-start(bf16[2,256,256]{2,1,0:T(8,128)(2,1)S(1)} %bitcast.189), channel_id=1, source_target_pairs={{0,1},{1,2},{2,3},{3,0},{4,5},{5,6},{6,7},{7,4},{8,9},{9,10},{10,1... | collective-permute-start | bytes 786440 | tf_op jit(solution)/shard_map/ppermute | solution.py:348
  149.3 20.3 %collective-permute-start.9 = (bf16[2,256,256]{2,1,0:T(8,128)(2,1)S(1)}, bf16[2,256,256]{2,1,0:T(8,128)(2,1)S(1)}, u32[]{:S(2)}, u32[]{:S(2)}) collective-permute-start(bf16[2,256,256]{2,1,0:T(8,128)(2,1)S(1)} %bitcast.190), channel_id=1, source_target_pairs={{0,2},{1,3},{2,0},{3,1},{4,6},{5,7},{6,4},{7,5},{8,10},{9,11},{10,... | collective-permute-start | bytes 786440 | tf_op jit(solution)/shard_map/ppermute | solution.py:348
  151.7 18.6 %collective-permute-start.10 = (bf16[2,256,256]{2,1,0:T(8,128)(2,1)S(1)}, bf16[2,256,256]{2,1,0:T(8,128)(2,1)}, u32[]{:S(2)}, u32[]{:S(2)}) collective-permute-start(bf16[2,256,256]{2,1,0:T(8,128)(2,1)S(1)} %bitcast.191), channel_id=1, source_target_pairs={{0,3},{1,0},{2,1},{3,2},{4,7},{5,4},{6,5},{7,6},{8,11},{9,8},{10,9... | collective-permute-start | bytes 786440 | tf_op jit(solution)/shard_map/ppermute | solution.py:348
  170.3 35.9 %collective-permute-start.11 = (bf16[256,2048]{1,0:T(8,128)(2,1)}, bf16[256,2048]{1,0:T(8,128)(2,1)S(1)}, u32[]{:S(2)}, u32[]{:S(2)}) collective-permute-start(bf16[256,2048]{1,0:T(8,128)(2,1)} %collective-permute-done.5), channel_id=1, source_target_pairs={{0,1},{1,2},{2,3},{3,0},{4,5},{5,6},{6,7},{7,4},{8,9},{9,10},{10,1... | collective-permute-start | bytes 3145736 | tf_op jit(solution)/shard_map/ppermute | solution.py:348
  176.1 47.4 %collective-permute-start.12 = (bf16[512,2048]{1,0:T(8,128)(2,1)S(1)}, bf16[512,2048]{1,0:T(8,128)(2,1)}, u32[]{:S(2)}, u32[]{:S(2)}) collective-permute-start(bf16[512,2048]{1,0:T(8,128)(2,1)S(1)} %pad_maximum_fusion.1.refs_0_.refs_8_), channel_id=1, source_target_pairs={{0,16},{4,20},{8,24},{12,28},{16,0},{20,4},{24,8},{28,12},{1,17},{... | collective-permute-start | bytes 6291464 | tf_op jit(solution)/shard_map/ppermute | solution.py:403
  176.8 47.3 %collective-permute-start.13 = (bf16[512,2048]{1,0:T(8,128)(2,1)}, bf16[512,2048]{1,0:T(8,128)(2,1)}, u32[]{:S(2)}, u32[]{:S(2)}) collective-permute-start(bf16[512,2048]{1,0:T(8,128)(2,1)} %pad_maximum_fusion.2.refs_1_.refs_9_), channel_id=1, source_target_pairs={{0,8},{4,12},{8,0},{12,4},{16,24},{20,28},{24,16},{28,20},{1,9},{5... | collective-permute-start | bytes 6291464 | tf_op jit(solution)/shard_map/ppermute | solution.py:403
  177.7 412.7 %reduce-scatter.5.cloned.1.call-start = ((), (), s32[]{:S(2)}) async-start(), calls=%async_computation.10 | async-start | bytes 5242880 | tf_op jit(solution)/shard_map/reduce_scatter | solution.py:581
  206.1 54.9 %collective-permute-start.14 = (bf16[256,2048]{1,0:T(8,128)(2,1)S(1)}, bf16[256,2048]{1,0:T(8,128)(2,1)}, u32[]{:S(2)}, u32[]{:S(2)}) collective-permute-start(bf16[256,2048]{1,0:T(8,128)(2,1)S(1)} %collective-permute-done.11), channel_id=1, source_target_pairs={{0,1},{1,2},{2,3},{3,0},{4,5},{5,6},{6,7},{7,4},{8,9},{9,10},{10,1... | collective-permute-start | bytes 3145736 | tf_op jit(solution)/shard_map/ppermute | solution.py:348
  261.0 29.6 %collective-permute-start.15 = (bf16[512,2048]{1,0:T(8,128)(2,1)}, bf16[512,2048]{1,0:T(8,128)(2,1)}, u32[]{:S(2)}, u32[]{:S(2)}) collective-permute-start(bf16[512,2048]{1,0:T(8,128)(2,1)} %collective-permute-done.12.refs_0_.refs_12_), channel_id=1, source_target_pairs={{0,4},{4,0},{8,12},{12,8},{16,20},{20,16},{24,28},{28,24},{1,5},{5... | collective-permute-start | bytes 6291464 | tf_op jit(solution)/shard_map/ppermute | solution.py:403
  261.2 25.6 %collective-permute-start.17 = (bf16[256,2048]{1,0:T(8,128)(2,1)S(1)}, bf16[256,2048]{1,0:T(8,128)(2,1)S(1)}, u32[]{:S(2)}, u32[]{:S(2)}) collective-permute-start(bf16[256,2048]{1,0:T(8,128)(2,1)S(1)} %get-tuple-element.290), channel_id=1, source_target_pairs={{0,8},{4,12},{8,0},{12,4},{16,24},{20,28},{24,16},{28,20},{1,9},{5... | collective-permute-start | bytes 3145736 | tf_op jit(solution)/shard_map/ppermute | solution.py:403
  262.7 30.0 %collective-permute-start.16 = (bf16[512,2048]{1,0:T(8,128)(2,1)}, bf16[512,2048]{1,0:T(8,128)(2,1)}, u32[]{:S(2)}, u32[]{:S(2)}) collective-permute-start(bf16[512,2048]{1,0:T(8,128)(2,1)} %collective-permute-done.13.refs_1_.refs_13_), channel_id=1, source_target_pairs={{0,4},{4,0},{8,12},{12,8},{16,20},{20,16},{24,28},{28,24},{1,5},{5... | collective-permute-start | bytes 6291464 | tf_op jit(solution)/shard_map/ppermute | solution.py:403
  263.0 25.4 %collective-permute-start.18 = (bf16[256,2048]{1,0:T(8,128)(2,1)S(1)}, bf16[256,2048]{1,0:T(8,128)(2,1)S(1)}, u32[]{:S(2)}, u32[]{:S(2)}) collective-permute-start(bf16[256,2048]{1,0:T(8,128)(2,1)S(1)} %get-tuple-element.289), channel_id=1, source_target_pairs={{0,16},{4,20},{8,24},{12,28},{16,0},{20,4},{24,8},{28,12},{1,17},{... | collective-permute-start | bytes 3145736 | tf_op jit(solution)/shard_map/ppermute | solution.py:403
  289.9 17.4 %collective-permute-start.19 = (bf16[512,2048]{1,0:T(8,128)(2,1)}, bf16[512,2048]{1,0:T(8,128)(2,1)}, u32[]{:S(2)}, u32[]{:S(2)}) collective-permute-start(bf16[512,2048]{1,0:T(8,128)(2,1)} %pad_maximum_fusion.3.refs_0_), channel_id=1, source_target_pairs={{0,4},{4,0},{8,12},{12,8},{16,20},{20,16},{24,28},{28,24},{1,5},{5... | collective-permute-start | bytes 6291464 | tf_op jit(solution)/shard_map/ppermute | solution.py:403
  289.9 17.4 %collective-permute-start.20 = (bf16[512,2048]{1,0:T(8,128)(2,1)}, bf16[512,2048]{1,0:T(8,128)(2,1)}, u32[]{:S(2)}, u32[]{:S(2)}) collective-permute-start(bf16[512,2048]{1,0:T(8,128)(2,1)} %pad_maximum_fusion.4.refs_1_), channel_id=1, source_target_pairs={{0,4},{4,0},{8,12},{12,8},{16,20},{20,16},{24,28},{28,24},{1,5},{5... | collective-permute-start | bytes 6291464 | tf_op jit(solution)/shard_map/ppermute | solution.py:403
  290.4 47.9 %collective-permute-start.21 = (bf16[512,2048]{1,0:T(8,128)(2,1)}, bf16[512,2048]{1,0:T(8,128)(2,1)}, u32[]{:S(2)}, u32[]{:S(2)}) collective-permute-start(bf16[512,2048]{1,0:T(8,128)(2,1)} %pad_maximum_fusion.3.refs_0_), channel_id=1, source_target_pairs={{0,16},{4,20},{8,24},{12,28},{16,0},{20,4},{24,8},{28,12},{1,17},{... | collective-permute-start | bytes 6291464 | tf_op jit(solution)/shard_map/ppermute | solution.py:403
  290.6 47.7 %collective-permute-start.22 = (bf16[512,2048]{1,0:T(8,128)(2,1)}, bf16[512,2048]{1,0:T(8,128)(2,1)}, u32[]{:S(2)}, u32[]{:S(2)}) collective-permute-start(bf16[512,2048]{1,0:T(8,128)(2,1)} %pad_maximum_fusion.4.refs_1_), channel_id=1, source_target_pairs={{0,8},{4,12},{8,0},{12,4},{16,24},{20,28},{24,16},{28,20},{1,9},{5... | collective-permute-start | bytes 6291464 | tf_op jit(solution)/shard_map/ppermute | solution.py:403
  338.4 14.4 %collective-permute-start.23 = (bf16[512,2048]{1,0:T(8,128)(2,1)}, bf16[512,2048]{1,0:T(8,128)(2,1)}, u32[]{:S(2)}, u32[]{:S(2)}) collective-permute-start(bf16[512,2048]{1,0:T(8,128)(2,1)} %collective-permute-done.21.refs_0_.refs_4_), channel_id=1, source_target_pairs={{0,4},{4,0},{8,12},{12,8},{16,20},{20,16},{24,28},{28,24},{1,5},{5... | collective-permute-start | bytes 6291464 | tf_op jit(solution)/shard_map/ppermute | solution.py:403
  338.4 14.5 %collective-permute-start.24 = (bf16[512,2048]{1,0:T(8,128)(2,1)}, bf16[512,2048]{1,0:T(8,128)(2,1)}, u32[]{:S(2)}, u32[]{:S(2)}) collective-permute-start(bf16[512,2048]{1,0:T(8,128)(2,1)} %collective-permute-done.22.refs_1_.refs_5_), channel_id=1, source_target_pairs={{0,4},{4,0},{8,12},{12,8},{16,20},{20,16},{24,28},{28,24},{1,5},{5... | collective-permute-start | bytes 6291464 | tf_op jit(solution)/shard_map/ppermute | solution.py:403
  393.9 7.4 collective-permute-start.27
  394.1 48.1 %collective-permute-start.29 = (bf16[512,2048]{1,0:T(8,128)(2,1)}, bf16[512,2048]{1,0:T(8,128)(2,1)S(1)}, u32[]{:S(2)}, u32[]{:S(2)}) collective-permute-start(bf16[512,2048]{1,0:T(8,128)(2,1)} %add_convert_fusion.6), channel_id=1, source_target_pairs={{0,8},{4,12},{8,0},{12,4},{16,24},{20,28},{24,16},{28,20},{1,9},{5... | collective-permute-start | bytes 6291464 | tf_op jit(solution)/shard_map/ppermute | solution.py:403
  395.6 47.9 %collective-permute-start.28 = (bf16[512,2048]{1,0:T(8,128)(2,1)}, bf16[512,2048]{1,0:T(8,128)(2,1)}, u32[]{:S(2)}, u32[]{:S(2)}) collective-permute-start(bf16[512,2048]{1,0:T(8,128)(2,1)} %add_convert_fusion.7), channel_id=1, source_target_pairs={{0,16},{4,20},{8,24},{12,28},{16,0},{20,4},{24,8},{28,12},{1,17},{... | collective-permute-start | bytes 6291464 | tf_op jit(solution)/shard_map/ppermute | solution.py:403
  448.5 38.4 %collective-permute-start.31 = (bf16[256,2048]{1,0:T(8,128)(2,1)}, bf16[256,2048]{1,0:T(8,128)(2,1)}, u32[]{:S(2)}, u32[]{:S(2)}) collective-permute-start(bf16[256,2048]{1,0:T(8,128)(2,1)} %slice.452), channel_id=1, source_target_pairs={{0,16},{4,20},{8,24},{12,28},{16,0},{20,4},{24,8},{28,12},{1,17},{... | collective-permute-start | bytes 3145736 | tf_op jit(solution)/shard_map/ppermute | solution.py:403
  451.3 37.9 %collective-permute-start.30 = (bf16[256,2048]{1,0:T(8,128)(2,1)}, bf16[256,2048]{1,0:T(8,128)(2,1)S(1)}, u32[]{:S(2)}, u32[]{:S(2)}) collective-permute-start(bf16[256,2048]{1,0:T(8,128)(2,1)} %slice.453), channel_id=1, source_target_pairs={{0,8},{4,12},{8,0},{12,4},{16,24},{20,28},{24,16},{28,20},{1,9},{5... | collective-permute-start | bytes 3145736 | tf_op jit(solution)/shard_map/ppermute | solution.py:403
  456.5 34.4 %collective-permute-start.32 = (bf16[512,2048]{1,0:T(8,128)(2,1)}, bf16[512,2048]{1,0:T(8,128)(2,1)}, u32[]{:S(2)}, u32[]{:S(2)}) collective-permute-start(bf16[512,2048]{1,0:T(8,128)(2,1)} %convolution_convert_fusion.6), channel_id=1, source_target_pairs={{0,4},{4,0},{8,12},{12,8},{16,20},{20,16},{24,28},{28,24},{1,5},{5... | collective-permute-start | bytes 6291464 | tf_op jit(solution)/shard_map/ppermute | solution.py:403
  460.2 39.1 %collective-permute-start.33 = (bf16[512,2048]{1,0:T(8,128)(2,1)}, bf16[512,2048]{1,0:T(8,128)(2,1)S(1)}, u32[]{:S(2)}, u32[]{:S(2)}) collective-permute-start(bf16[512,2048]{1,0:T(8,128)(2,1)} %convolution_convert_fusion.5), channel_id=1, source_target_pairs={{0,4},{4,0},{8,12},{12,8},{16,20},{20,16},{24,28},{28,24},{1,5},{5... | collective-permute-start | bytes 6291464 | tf_op jit(solution)/shard_map/ppermute | solution.py:403
  460.7 297.1 %reduce-scatter.9.cloned.1.call-start = ((), (), s32[]{:S(2)}) async-start(), calls=%async_computation.12 | async-start | bytes 5242880 | tf_op jit(solution)/shard_map/reduce_scatter | solution.py:588
  512.1 9.7 %collective-permute-start.34 = (bf16[1024,2048]{1,0:T(8,128)(2,1)S(1)}, bf16[1024,2048]{1,0:T(8,128)(2,1)S(1)}, u32[]{:S(2)}, u32[]{:S(2)}) collective-permute-start(bf16[1024,2048]{1,0:T(8,128)(2,1)S(1)} %convolution_convert_fusion.2), channel_id=1, source_target_pairs={{0,4},{4,0},{8,12},{12,8},{16,20},{20,16},{24,28},{28,24},{1,5},{5... | collective-permute-start | bytes 12582920 | tf_op jit(solution)/shard_map/ppermute | solution.py:403
  518.9 48.8 %collective-permute-start.35 = (bf16[512,2048]{1,0:T(8,128)(2,1)}, bf16[512,2048]{1,0:T(8,128)(2,1)}, u32[]{:S(2)}, u32[]{:S(2)}) collective-permute-start(bf16[512,2048]{1,0:T(8,128)(2,1)} %add_convert_fusion.5), channel_id=1, source_target_pairs={{0,16},{4,20},{8,24},{12,28},{16,0},{20,4},{24,8},{28,12},{1,17},{... | collective-permute-start | bytes 6291464 | tf_op jit(solution)/shard_map/ppermute | solution.py:403
  520.4 48.9 %collective-permute-start.36 = (bf16[512,2048]{1,0:T(8,128)(2,1)}, bf16[512,2048]{1,0:T(8,128)(2,1)}, u32[]{:S(2)}, u32[]{:S(2)}) collective-permute-start(bf16[512,2048]{1,0:T(8,128)(2,1)} %add_convert_fusion.4), channel_id=1, source_target_pairs={{0,8},{4,12},{8,0},{12,4},{16,24},{20,28},{24,16},{28,20},{1,9},{5... | collective-permute-start | bytes 6291464 | tf_op jit(solution)/shard_map/ppermute | solution.py:403
  526.3 63.0 %collective-permute-start.37 = (bf16[256,2048]{1,0:T(8,128)(2,1)S(1)}, bf16[256,2048]{1,0:T(8,128)(2,1)}, u32[]{:S(2)}, u32[]{:S(2)}) collective-permute-start(bf16[256,2048]{1,0:T(8,128)(2,1)S(1)} %get-tuple-element.230), channel_id=1, source_target_pairs={{0,16},{4,20},{8,24},{12,28},{16,0},{20,4},{24,8},{28,12},{1,17},{... | collective-permute-start | bytes 3145736 | tf_op jit(solution)/shard_map/ppermute | solution.py:403
  526.7 63.7 %collective-permute-start.38 = (bf16[256,2048]{1,0:T(8,128)(2,1)S(1)}, bf16[256,2048]{1,0:T(8,128)(2,1)}, u32[]{:S(2)}, u32[]{:S(2)}) collective-permute-start(bf16[256,2048]{1,0:T(8,128)(2,1)S(1)} %get-tuple-element.231), channel_id=1, source_target_pairs={{0,8},{4,12},{8,0},{12,4},{16,24},{20,28},{24,16},{28,20},{1,9},{5... | collective-permute-start | bytes 3145736 | tf_op jit(solution)/shard_map/ppermute | solution.py:403
  596.0 7.5 collective-permute-start.39
  619.8 70.9 %collective-permute-start.40 = (bf16[1024,2048]{1,0:T(8,128)(2,1)}, bf16[1024,2048]{1,0:T(8,128)(2,1)}, u32[]{:S(2)}, u32[]{:S(2)}) collective-permute-start(bf16[1024,2048]{1,0:T(8,128)(2,1)} %convolution_convert_fusion.3), channel_id=1, source_target_pairs={{0,4},{4,0},{8,12},{12,8},{16,20},{20,16},{24,28},{28,24},{1,5},{5... | collective-permute-start | bytes 12582920 | tf_op jit(solution)/shard_map/ppermute | solution.py:403
  622.8 35.8 %collective-permute-start.45 = (bf16[128,2048]{1,0:T(8,128)(2,1)}, bf16[128,2048]{1,0:T(8,128)(2,1)}, u32[]{:S(2)}, u32[]{:S(2)}) collective-permute-start(bf16[128,2048]{1,0:T(8,128)(2,1)} %slice.456), channel_id=1, source_target_pairs={{0,16},{4,20},{8,24},{12,28},{16,0},{20,4},{24,8},{28,12},{1,17},{... | collective-permute-start | bytes 1572872 | tf_op jit(solution)/shard_map/ppermute | solution.py:403
  625.9 39.7 %collective-permute-start.44 = (bf16[128,2048]{1,0:T(8,128)(2,1)}, bf16[128,2048]{1,0:T(8,128)(2,1)}, u32[]{:S(2)}, u32[]{:S(2)}) collective-permute-start(bf16[128,2048]{1,0:T(8,128)(2,1)} %slice.457), channel_id=1, source_target_pairs={{0,8},{4,12},{8,0},{12,4},{16,24},{20,28},{24,16},{28,20},{1,9},{5... | collective-permute-start | bytes 1572872 | tf_op jit(solution)/shard_map/ppermute | solution.py:403
  628.2 61.9 %collective-permute-start.41 = (bf16[2,256,256]{2,1,0:T(8,128)(2,1)}, bf16[2,256,256]{2,1,0:T(8,128)(2,1)S(1)}, u32[]{:S(2)}, u32[]{:S(2)}) collective-permute-start(bf16[2,256,256]{2,1,0:T(8,128)(2,1)} %get-tuple-element.302), channel_id=1, source_target_pairs={{0,1},{1,2},{2,3},{3,0},{4,5},{5,6},{6,7},{7,4},{8,9},{9,10},{10,1... | collective-permute-start | bytes 786440 | tf_op jit(solution)/shard_map/ppermute | solution.py:348
  649.7 41.0 %collective-permute-start.42 = (bf16[2,256,256]{2,1,0:T(8,128)(2,1)}, bf16[2,256,256]{2,1,0:T(8,128)(2,1)}, u32[]{:S(2)}, u32[]{:S(2)}) collective-permute-start(bf16[2,256,256]{2,1,0:T(8,128)(2,1)} %get-tuple-element.301), channel_id=1, source_target_pairs={{0,2},{1,3},{2,0},{3,1},{4,6},{5,7},{6,4},{7,5},{8,10},{9,11},{10,... | collective-permute-start | bytes 786440 | tf_op jit(solution)/shard_map/ppermute | solution.py:348
  655.0 18.9 %all-to-all-start.1 = ((bf16[8,64,1024]{2,1,0:T(8,128)(2,1)}), bf16[8,64,1024]{2,1,0:T(8,128)(2,1)S(1)}, u32[]{:S(2)}, u32[]{:S(2)}) async-start(bf16[8,64,1024]{2,1,0:T(8,128)(2,1)} %reduce-scatter.5.cloned.1.call-done), calls=%async_computation.5 | async-start | bytes 2097152 | tf_op jit(solution)/shard_map/all_to_all | solution.py:699
  658.6 128.4 %reduce-scatter.11.cloned.1.call-start = ((), (), s32[]{:S(2)}) async-start(), calls=%async_computation.13 | async-start | bytes 1310720 | tf_op jit(solution)/shard_map/reduce_scatter | solution.py:683
  658.6 32.1 %collective-permute-start.43 = (bf16[2,256,256]{2,1,0:T(8,128)(2,1)}, bf16[2,256,256]{2,1,0:T(8,128)(2,1)}, u32[]{:S(2)}, u32[]{:S(2)}) collective-permute-start(bf16[2,256,256]{2,1,0:T(8,128)(2,1)} %get-tuple-element.300), channel_id=1, source_target_pairs={{0,3},{1,0},{2,1},{3,2},{4,7},{5,4},{6,5},{7,6},{8,11},{9,8},{10,9... | collective-permute-start | bytes 786440 | tf_op jit(solution)/shard_map/ppermute | solution.py:348
  675.6 26.8 %collective-permute-start.46 = (bf16[256,2048]{1,0:T(8,128)(2,1)}, bf16[256,2048]{1,0:T(8,128)(2,1)}, u32[]{:S(2)}, u32[]{:S(2)}) collective-permute-start(bf16[256,2048]{1,0:T(8,128)(2,1)} %get-tuple-element.279), channel_id=1, source_target_pairs={{0,16},{4,20},{8,24},{12,28},{16,0},{20,4},{24,8},{28,12},{1,17},{... | collective-permute-start | bytes 3145736 | tf_op jit(solution)/shard_map/ppermute | solution.py:403
  690.1 23.6 %collective-permute-start.47 = (bf16[256,2048]{1,0:T(8,128)(2,1)S(1)}, bf16[256,2048]{1,0:T(8,128)(2,1)S(1)}, u32[]{:S(2)}, u32[]{:S(2)}) collective-permute-start(bf16[256,2048]{1,0:T(8,128)(2,1)S(1)} %copy-done.64), channel_id=1, source_target_pairs={{0,8},{4,12},{8,0},{12,4},{16,24},{20,28},{24,16},{28,20},{1,9},{5... | collective-permute-start | bytes 3145736 | tf_op jit(solution)/shard_map/ppermute | solution.py:403
  714.8 65.4 %collective-permute-start.49 = (bf16[256,2048]{1,0:T(8,128)(2,1)}, bf16[256,2048]{1,0:T(8,128)(2,1)}, u32[]{:S(2)}, u32[]{:S(2)}) collective-permute-start(bf16[256,2048]{1,0:T(8,128)(2,1)} %slice.450), channel_id=1, source_target_pairs={{0,16},{4,20},{8,24},{12,28},{16,0},{20,4},{24,8},{28,12},{1,17},{... | collective-permute-start | bytes 3145736 | tf_op jit(solution)/shard_map/ppermute | solution.py:403
  717.6 65.2 %collective-permute-start.48 = (bf16[256,2048]{1,0:T(8,128)(2,1)}, bf16[256,2048]{1,0:T(8,128)(2,1)}, u32[]{:S(2)}, u32[]{:S(2)}) collective-permute-start(bf16[256,2048]{1,0:T(8,128)(2,1)} %slice.451), channel_id=1, source_target_pairs={{0,8},{4,12},{8,0},{12,4},{16,24},{20,28},{24,16},{28,20},{1,9},{5... | collective-permute-start | bytes 3145736 | tf_op jit(solution)/shard_map/ppermute | solution.py:403
  722.5 27.1 %collective-permute-start.51 = (bf16[128,2048]{1,0:T(8,128)(2,1)}, bf16[128,2048]{1,0:T(8,128)(2,1)}, u32[]{:S(2)}, u32[]{:S(2)}) collective-permute-start(bf16[128,2048]{1,0:T(8,128)(2,1)} %slice.454), channel_id=1, source_target_pairs={{0,16},{4,20},{8,24},{12,28},{16,0},{20,4},{24,8},{28,12},{1,17},{... | collective-permute-start | bytes 1572872 | tf_op jit(solution)/shard_map/ppermute | solution.py:403
  726.5 28.3 %collective-permute-start.50 = (bf16[128,2048]{1,0:T(8,128)(2,1)}, bf16[128,2048]{1,0:T(8,128)(2,1)}, u32[]{:S(2)}, u32[]{:S(2)}) collective-permute-start(bf16[128,2048]{1,0:T(8,128)(2,1)} %slice.455), channel_id=1, source_target_pairs={{0,8},{4,12},{8,0},{12,4},{16,24},{20,28},{24,16},{28,20},{1,9},{5... | collective-permute-start | bytes 1572872 | tf_op jit(solution)/shard_map/ppermute | solution.py:403
  738.6 12.2 %collective-permute-start.52 = (bf16[1152,256]{1,0:T(8,128)(2,1)}, bf16[1152,256]{1,0:T(8,128)(2,1)}, u32[]{:S(2)}, u32[]{:S(2)}) collective-permute-start(bf16[1152,256]{1,0:T(8,128)(2,1)} %bitcast.45), channel_id=1, source_target_pairs={{0,4},{4,0},{8,12},{12,8},{16,20},{20,16},{24,28},{28,24},{1,5},{5... | collective-permute-start | bytes 1769480 | tf_op jit(solution)/shard_map/ppermute | solution.py:403
  738.6 62.4 %reduce-scatter.7.cloned.1.call-start = ((), (), s32[]{:S(2)}) async-start(), calls=%async_computation.11 | async-start | bytes 1310720 | tf_op jit(solution)/shard_map/reduce_scatter | solution.py:685
  752.1 5.8 collective-permute-start.55
  766.6 8.4 %collective-permute-start.59 = (bf16[17664]{0:T(1024)(128)(2,1)S(1)}, bf16[17664]{0:T(1024)(128)(2,1)S(1)}, u32[]{:S(2)}, u32[]{:S(2)}) collective-permute-start(bf16[17664]{0:T(1024)(128)(2,1)S(1)} %get-tuple-element.271), channel_id=1, source_target_pairs={{0,3},{1,0},{2,1},{3,2},{4,7},{5,4},{6,5},{7,6},{8,11},{9,8},{10,9... | collective-permute-start | bytes 105992 | tf_op jit(solution)/shard_map/ppermute | solution.py:348
  772.1 5.8 collective-permute-start.57
  (91 other events, 1115.2 us)
Sparse Core Ops, SparseCore 0:
  17.7 35.3 all-gather.4
  59.4 63.5 all-gather.6
  125.5 54.3 all-gather.8
  181.4 109.2 all-gather.10
  460.8 101.2 reduce-scatter.4
  603.3 116.5 reduce-scatter.8
  738.8 29.2 reduce-scatter.10
  773.4 27.6 reduce-scatter.6

commit v10 on v9

--- a/solution.py
+++ b/solution.py
@@ -321,6 +321,48 @@
         cost_estimate=pl.CostEstimate(flops=0, transcendentals=0, bytes_accessed=4 * rows * width // HASTE),
     )(places, values, values)
 
+def product_kernel(form, given, values_ref, weight_ref, *refs):
+    extra, outs = refs[:given], refs[given:]
+    size = outs[0].shape[0]
+    for i, out in enumerate(outs):
+        rows = slice(i * size, (i + 1) * size)
+        if form == "tn":
+            total = dot_tn(values_ref[:, rows], weight_ref[...])
+        else:
+            total = (dot_nt if form == "nt" else dot_nn)(values_ref[rows, :], weight_ref[...])
+        if given:
+            each = extra[0].shape[0]
+            at = i * size % each
+            total += extra[i * size // each][at : at + size, :].astype(F32)
+        out[...] = total.astype(out.dtype)
+
+
+def product(values, weight, form="nn", parts=1, extra=(), kind=BF16, tile=512):
+    height = values.shape[1] if form == "tn" else values.shape[0]
+    depth = values.shape[0] if form == "tn" else values.shape[1]
+    breadth = weight.shape[0] if form == "nt" else weight.shape[1]
+    tile = min(tile, breadth)
+    size = height // parts
+    if form == "nt":
+        part = pl.BlockSpec((tile, depth), lambda j: (j, 0))
+    else:
+        part = pl.BlockSpec((depth, tile), lambda j: (0, j))
+    out = pl.pallas_call(
+        functools.partial(product_kernel, form, len(extra)),
+        out_shape=[jax.ShapeDtypeStruct((size, breadth), kind)] * parts,
+        grid=(breadth // tile,),
+        in_specs=[pl.BlockSpec(values.shape, lambda j: (0, 0), pipeline_mode=pl.Buffered(buffer_count=1)), part]
+        + [pl.BlockSpec((block.shape[0], tile), lambda j: (0, j)) for block in extra],
+        out_specs=[pl.BlockSpec((size, tile), lambda j: (0, j))] * parts,
+        compiler_params=pltpu.CompilerParams(vmem_limit_bytes=48 * 2**20),
+        cost_estimate=pl.CostEstimate(
+            flops=2 * height * depth * breadth // HASTE,
+            transcendentals=0,
+            bytes_accessed=2 * (height * (depth + breadth) + depth * breadth) // HASTE,
+        ),
+    )(values, weight, *extra)
+    return list(out) if parts > 1 else out[0]
+
 
 def norm_stats(values):
     average = jnp.mean(values, axis=-1, keepdims=True)
@@ -510,7 +552,11 @@
         normed_one = (xhat_one * gain_one + shift_one).astype(BF16)
         kv_bias = jnp.concatenate([jnp.zeros((HD,), F32), bias_v])
         key_value = (dot_nn(normed_one, full_kv) + kv_bias).astype(BF16)
-        key_value, normed_late, up_cols = tie(key_value, normed_one, up_cols)
+        if n_z > 2:
+            down_pieces.append(line.send(down_pieces[-1], 1))
+        key_value, normed_late, up_cols, down_pieces[-1] = tie(
+            key_value, normed_one, up_cols, down_pieces[-1]
+        )
         kv_pieces = line.gather(key_value.reshape(windows, local_len, 2 * HD))
         queries = (dot_nn(normed_late, full_q) + bias_q).astype(BF16)
         queries, down_late, *kv_pieces = tie(queries, down_pieces[-1], *kv_pieces)
@@ -521,13 +567,12 @@
         upto = jnp.arange(file_count)[:, None] <= jnp.arange(file_count)[None, :]
         file_ends = jnp.sum(jnp.where(upto[None], lengths[:, :, None], 0), axis=1)
         grad_far = plane.across(grad_near, plane.last)
-        while len(down_pieces) < n_z - 1:
+        while len(down_pieces) < n_z:
             down_late = line.send(down_late, 1)
             down_pieces.append(down_late)
         up_part = lax.all_gather(up_cols, "fsdp", axis=1, tiled=True).reshape(width, ff_own)
         attended, norms = attn_forward(queries, kv_window, first, file_ends)
         attended, down_pieces[-1] = tie(attended, down_pieces[-1])
-        down_pieces.append(line.send(down_pieces[-1], 1))
         middle = inputs + dot_nn(attended, full_o) + bias_o
         mean_two, recip_two = norm_stats(middle)
         xhat_two = (middle - mean_two) * recip_two
@@ -559,25 +604,26 @@
         block = two_near[0].shape[0]
         lots = (slice(None, block), slice(block, None))
 
-        def halves(lot, weight, product):
-            theirs = plane.cross([product(lot[1][at], weight).astype(BF16) for at in lots])
+        def halves(lot, weight, times):
+            theirs = plane.cross([times(lot[1][at], weight).astype(BF16) for at in lots])
             return [
-                (product(lot[0][at], weight) + there.astype(F32)).astype(BF16)
+                (times(lot[0][at], weight) + there.astype(F32)).astype(BF16)
                 for at, there in zip(lots, theirs)
             ]
 
-        def ours(lot, weight, product, theirs, got):
-            whole = (product(lot[0], weight) + theirs.astype(F32)).astype(BF16)
-            return [whole[at].astype(F32) + there.astype(F32) for at, there in zip(lots, got)]
+        def merge(near, got):
+            return [whole.astype(F32) + there.astype(F32) for whole, there in zip(near, got)]
 
         two_far_sum = halves(pre_far, up_part, dot_nt)
         pre_near[0], pre_near[1], *two_far_sum = tie(*pre_near, *two_far_sum)
         got = plane.across(two_far_sum, plane.last)
-        theirs = plane.swap(dot_nt(pre_near[1], up_part).astype(BF16), 1)
+        theirs = plane.swap(product(pre_near[1], up_part, "nt"), 1)
         pre_far[0], theirs = tie(pre_far[0], theirs)
         up_terms = weight_grad(two_lots[0] + two_lots[1], pre_near + pre_far, block)
         pre_near[0], up_terms = tie(pre_near[0], up_terms)
-        two_sum = ours(pre_near, up_part, dot_nt, theirs, got)
+        two_near_sum = product(pre_near[0], up_part, "nt", 2, [theirs])
+        two_near_sum[0], *got = tie(two_near_sum[0], *got)
+        two_sum = merge(two_near_sum, got)
         grad_up = lax.psum_scatter(
             up_terms.reshape(n_dp, n_z * own, ff_own), "fsdp", scatter_dimension=1, tiled=True
         )
@@ -602,38 +648,36 @@
             size = rows_of_lots.shape[0] // 4
             return [rows_of_lots[i * size : (i + 1) * size] for i in range(4)]
 
-        def plus(mine, right, theirs):
-            return (dot_tn(mine, right) + theirs.astype(F32)).astype(BF16)
-
         def send_rows(parts):
             return plane.across([parts[0], parts[2]], plane.last)
 
         def own_rows(parts, got):
             return plane.fold([n.astype(F32) + g.astype(F32) for n, g in zip((parts[1], parts[3]), got)])
 
-        theirs = plane.swap(dot_tn(att_sib, branch_grad).astype(BF16), 1)
         attended_grad = dot_nt(branch_grad, full_o).astype(BF16)
-        attended_grad, branch_late = tie(attended_grad, branch_grad)
-        wo_parts = cut(plus(att_mine, branch_late, theirs))
-        attended_grad, *wo_parts = tie(attended_grad, *wo_parts)
-        wo_got = send_rows(wo_parts)
 
         query_grad, kv_terms = attn_backward(queries, kv_window, norms, attended_grad, first, file_ends)
-        query_grad, kv_terms, grad_up, *arrived = tie(query_grad, kv_terms, grad_up, *out_got, *wo_got)
-        out_got, wo_got = arrived[:2], arrived[2:]
+        query_grad, kv_terms, grad_up, *out_got = tie(query_grad, kv_terms, grad_up, *out_got)
         kv_got = line.scatter(kv_terms.reshape(windows, n_z, local_len, 2 * HD), 1)
         theirs = plane.swap(dot_tn(one_sib, query_grad).astype(BF16), 1)
-        wq_parts = cut(plus(one_mine, query_grad, theirs))
+        wq_parts = product(one_mine, query_grad, "tn", 4, [theirs])
         wq_got = send_rows(wq_parts)
-        wq_parts[1], query_late, hid_late = tie(wq_parts[1], query_grad, hid_near[1])
-        theirs = plane.swap(dot_nn(hid_late, down_part).astype(BF16), 1)
-        query_part = dot_nt(query_late, full_q)
-        query_part, hid_near[0], theirs, *kv_got = tie(query_part, hid_near[0], theirs, *kv_got)
-        out_sum = ours(hid_near, down_part, dot_nn, theirs, out_got)
+        wq_parts[1], query_late = tie(wq_parts[1], query_grad)
+        query_part = product(query_late, full_q, "nt", kind=F32)
+        query_part, att_sib, branch_late, hid_late, *kv_got = tie(
+            query_part, att_sib, branch_grad, hid_near[1], *kv_got
+        )
+        wo_theirs = plane.swap(product(att_sib, branch_late, "tn"), 1)
+        theirs = plane.swap(product(hid_late, down_part), 1)
+        wo_theirs, *wq_got = tie(wo_theirs, *wq_got)
+        wo_parts = product(att_mine, branch_late, "tn", 4, [wo_theirs])
+        wo_got = send_rows(wo_parts)
+        query_part, hid_near[0], theirs, wo_parts[1], grad_down = tie(
+            query_part, hid_near[0], theirs, wo_parts[1], grad_down
+        )
+        out_sum = merge(product(hid_near[0], down_part, "nn", 2, [theirs]), out_got)
         kv_grad = total(kv_got).astype(BF16).reshape(rows, 2 * HD)
-        wo_rows = own_rows(wo_parts, wo_got)
-        query_part, kv_grad, wo_rows, *arrived = tie(query_part, kv_grad, wo_rows, *out_sum, *wq_got)
-        out_sum, wq_got = arrived[:2], arrived[2:]
+        query_part, kv_grad, *out_sum = tie(query_part, kv_grad, *out_sum)
         branch_out = plane.fold(out_sum)
 
         one_grad = query_part + dot_nt(kv_grad, full_kv)
@@ -678,11 +722,16 @@
         theirs = plane.swap(with_vectors(dot_tn(one_sib, kv_grad), 1).astype(BF16), 1)
         kv_parts = cut((with_vectors(dot_tn(one_mine, kv_grad), 0) + theirs.astype(F32)).astype(BF16))
         kv_parts_got = send_rows(kv_parts)
-        kv_parts[1], grad_down = tie(kv_parts[1], grad_down)
-
-        grad_wo = lax.psum_scatter(wo_rows.astype(BF16), "fsdp", scatter_dimension=0, tiled=True)
-        wq_rows = own_rows(wq_parts, wq_got).astype(BF16)
-        grad_wq = lax.psum_scatter(wq_rows, "fsdp", scatter_dimension=0, tiled=True)
+        kv_parts[1], *wo_got = tie(kv_parts[1], *wo_got)
+
+        both_rows = jnp.concatenate(
+            [
+                own_rows(parts, got).astype(BF16).reshape(n_z, own, width)
+                for parts, got in ((wq_parts, wq_got), (wo_parts, wo_got))
+            ],
+            axis=1,
+        ).reshape(2 * n_z * own, width)
+        both_rows = lax.psum_scatter(both_rows, "fsdp", scatter_dimension=0, tiled=True)
         kv_last = own_rows(kv_parts, kv_parts_got).reshape(2, -1, 2 * HD)
         kv_rows = kv_last.shape[1] - more
         kv_last = jnp.concatenate(
@@ -707,9 +756,9 @@
         return (
             output,
             tokens_grad,
-            grad_wq.astype(F32),
+            both_rows[:own].astype(F32),
             kv_own[: own * 2 * HD].reshape(own, 2 * HD),
-            grad_wo.astype(F32),
+            both_rows[own:].astype(F32),
             bq,
             bv,
             bo,

time: 819 us -> 881 us (1.076)
  Pallas kernels: 181 us -> 248 us
  waiting for transfers between devices: 219 us -> 269 us
  matrix products: 109 us -> 67.7 us
  other arithmetic: 85.5 us -> 73.7 us
    pallas_call x0 -> x8, Pallas kernels: none -> 57.5 us  [product(): pl.pallas_call(functools.partial(product_kernel, form, len(extra)), out_s...]
    ppermute x45, waiting for transfers between devices: 102 us -> 145 us  [swap(): return lax.ppermute(block, 'dp', [(i, i ^ bit) for i in range(self.count)])]
    dot_general x9 -> x6, matrix products: 42.2 us -> 23.8 us  [dot_nt(): lax.dot_general(left, right, (((1,), (1,)), ((), ())), preferred_element_...]
    reduce_scatter x2 -> x1, waiting for transfers between devices: 12.3 us -> 27 us  [local(): lax.psum_scatter(both_rows, 'fsdp', scatter_dimension=0, tiled=True)]
    dot_general x9 -> x7, matrix products: 49.2 us -> 34.9 us  [dot_nn(): return jnp.dot(left, right, preferred_element_type=F32)]
    ppermute x15, waiting for transfers between devices: 80.5 us -> 70.2 us  [send(): lax.ppermute(block, 'fsdp', [(i, (i + places) % self.count) for i in rang...]
    pallas_call x2, Pallas kernels: 28.4 us -> 37.7 us  [back_product(): pl.pallas_call(functools.partial(back_kernel, count), out_shape=jax.Shape...]
    dot_general x6 -> x3, matrix products: 17.6 us -> 8.67 us  [dot_tn(): lax.dot_general(left, right, (((0,), (0,)), ((), ())), preferred_element_...]
  transfers between devices with their start and end apart: 70 -> 69, of which waited for: 33 -> 29; matrix products, arithmetic and copies ran while one was open for 28% -> 18% of each run, Pallas kernels for 20% -> 24%
where the time goes in v10:
time: 881 us; the launch traced here: 870 us
  waiting for transfers between devices  269 us (31%)
  Pallas kernels  248 us (28%)
  starting transfers between devices  111 us (13%)
  local copies, waits for them, and re-layouts  84.3 us (10%)
  other arithmetic  73.7 us (8%)
  matrix products  67.7 us (8%)
  between operations  16.2 us (2%)
    ppermute x45, waiting for transfers between devices, swap(): return lax.ppermute(block, 'dp', [(i, i ^ bit) for i in range(self.count)])  145 us
    ppermute x15, waiting for transfers between devices, send(): lax.ppermute(block, 'fsdp', [(i, (i + places) % self.count) for i in rang...  70.2 us
    ppermute x15, starting transfers between devices, send(): lax.ppermute(block, 'fsdp', [(i, (i + places) % self.count) for i in rang...  62.9 us
    pallas_call x8, Pallas kernels, product(): pl.pallas_call(functools.partial(product_kernel, form, len(extra)), out_s...  57.5 us
    pallas_call x2, Pallas kernels, weight_grad(): pl.pallas_call(functools.partial(weight_kernel, count), out_shape=jax.Sha...  50.6 us
    pallas_call x2, Pallas kernels, middle_layer(): pl.pallas_call(functools.partial(middle_kernel, count), out_shape=[jax.Sh...  40.2 us
    ppermute x45, starting transfers between devices, swap(): return lax.ppermute(block, 'dp', [(i, i ^ bit) for i in range(self.count)])  39.4 us
    pallas_call x2, Pallas kernels, back_product(): pl.pallas_call(functools.partial(back_kernel, count), out_shape=jax.Shape...  37.7 us
  transfers between devices with their start and end apart: 69, of which 29 were waited for; matrix products, arithmetic and copies ran while one was open for 18% of the time, Pallas kernels for 24%

profile of v10, /device:TPU:0, one launch (start us, length us, event | category | flops | bytes accessed | tf_op | source)
XLA Modules:
  0.0 870.0 jit_solution(1945731410945033791)
XLA Ops:
  25.8 3.6 all-to-all-start
  29.4 17.9 %collective-permute-done = bf16[256,2048]{1,0:T(8,128)(2,1)} collective-permute-done((bf16[256,2048]{1,0:T(8,128)(2,1)S(1)}, bf16[256,2048]{1,0:T(8,128)(2,1)}, u32[]{:S(2)}, u32[]{:S(2)}) %collective-permute-start) | collective-permute-done | bytes 1048608 | tf_op jit(solution)/shard_map/ppermute | solution.py:445
  49.9 3.1 pad_maximum_fusion.2.refs_1_.refs_9_
  53.0 6.3 all-to-all-done
  67.7 3.5 collective-permute-done.2
  71.1 10.4 %collective-permute-done.3 = bf16[64,2048]{1,0:T(8,128)(2,1)} collective-permute-done((bf16[64,2048]{1,0:T(8,128)(2,1)S(1)}, bf16[64,2048]{1,0:T(8,128)(2,1)}, u32[]{:S(2)}, u32[]{:S(2)}) %collective-permute-start.3) | collective-permute-done | bytes 262176 | tf_op jit(solution)/shard_map/ppermute | solution.py:390
  81.6 6.1 collective-permute-start.5
  94.6 17.0 %collective-permute-done.5 = bf16[256,2048]{1,0:T(8,128)(2,1)} collective-permute-done((bf16[256,2048]{1,0:T(8,128)(2,1)}, bf16[256,2048]{1,0:T(8,128)(2,1)}, u32[]{:S(2)}, u32[]{:S(2)}) %collective-permute-start.5) | collective-permute-done | bytes 1048608 | tf_op jit(solution)/shard_map/ppermute | solution.py:390
  111.6 11.5 %all-gather.7.cloned.1.call-done = bf16[2560,2048]{1,0:T(8,128)(2,1)} async-done(((bf16[320,2048]{1,0:T(8,128)(2,1)}), bf16[2560,2048]{1,0:T(8,128)(2,1)}) %all-gather.7.cloned.1.call-update) | async-done | bytes 10485776 | tf_op jit(solution)/shard_map/all_gather | solution.py:529
  132.2 4.0 fusion.5
  136.9 8.3 slice.300
  150.3 7.8 collective-permute-done.8
  162.0 9.1 %add_convert_fusion.5.q_ref = bf16[512,2048]{1,0:T(8,128)(2,1)} fusion(bf16[512,2048]{1,0:T(8,128)(2,1)S(1)} %fusion.14.first_ref.second_ref, bf16[2048,2048]{1,0:T(8,128)(2,1)} %bitcast.152, f32[2048]{0:T(1024)S(1)} %reshape.414), kind=kOutput, calls=%fused_computation.47 | convolution fusion | flops 4297064448 | bytes 12591104 | tf_op jit(solution)/shard_map/dot_general | solution.py:21
  171.1 7.9 collective-permute-done.10
  179.1 5.1 collective-permute-start.12
  190.1 18.8 %shard_map.288 = (bf16[512,2048]{1,0:T(8,128)(2,1)S(1)}, f32[512,128]{1,0:T(8,128)S(1)}) custom-call(s32[1]{0:T(128)} %bitcast.1.pos_ref, s32[2,8]{1,0:T(2,128)S(1)} %select_reduce_fusion.ends_ref, bf16[512,2048]{1,0:T(8,128)(2,1)S(1)} %copy-done.14, bf16[2,1024,256]{2,1,0:T(8,128)(2,1)S(1)} %constant_dynamic-update-slice_fusion.15.kv_ref), custom_call_target="tpu_custom_call" | custom-call | flops 67108864 | bytes 65536 | tf_op jit(solution)/shard_map/pallas_call | solution.py:132
  210.2 11.1 %collective-permute-done.12 = bf16[256,2048]{1,0:T(8,128)(2,1)} collective-permute-done((bf16[256,2048]{1,0:T(8,128)(2,1)}, bf16[256,2048]{1,0:T(8,128)(2,1)}, u32[]{:S(2)}, u32[]{:S(2)}) %collective-permute-start.12) | collective-permute-done | bytes 1048608 | tf_op jit(solution)/shard_map/ppermute | solution.py:390
  221.2 9.3 %fusion.50 = (f32[512]{0:T(512)S(1)}, f32[512,2048]{1,0:T(8,128)S(1)}) fusion(f32[2048]{0:T(1024)S(1)} %reshape.415, bf16[512,2048]{1,0:T(8,128)(2,1)} %copy-done.15, bf16[2048,2048]{1,0:T(8,128)(2,1)} %all-gather.9.cloned.1.call-done, bf16[2,256,2048]{2,1,0:T(8,128)(2,1)} %param.17), kind=kOutput, calls=%fused_computation.192 | convolution fusion | flops 4299161088 | bytes 16787456 | tf_op jit(solution)/shard_map/dot_general | solution.py:21
  241.6 23.1 %shard_map.289.refs_4_ = bf16[2048,1024]{1,0:T(8,128)(2,1)} custom-call(bf16[512,2048]{1,0:T(8,128)(2,1)S(1)} %pad_maximum_fusion.1.refs_0_.refs_8_, bf16[512,2048]{1,0:T(8,128)(2,1)S(1)} %copy-done.10, bf16[512,2048]{1,0:T(8,128)(2,1)} %collective-permute-done.6.refs_2_.refs_10_, bf16[512,2048]{1,0:T(8,128)(2,1)} %collective-permute-done.7.refs_3_.refs_11_, ...), custom_call_target="tpu_custom_call" | custom-call | flops 134217728 | bytes 262144 | tf_op jit(solution)/shard_map/pallas_call | solution.py:236
  270.3 14.6 %shard_map.290.refs_4_ = bf16[2048,1024]{1,0:T(8,128)(2,1)} custom-call(bf16[512,2048]{1,0:T(8,128)(2,1)} %collective-permute-done.13.refs_0_.refs_12_, bf16[512,2048]{1,0:T(8,128)(2,1)} %collective-permute-done.14.refs_1_.refs_13_, bf16[512,2048]{1,0:T(8,128)(2,1)} %collective-permute-done.15.refs_2_.refs_14_, ...), custom_call_target="tpu_custom_call" | custom-call | flops 134217728 | bytes 262144 | tf_op jit(solution)/shard_map/pallas_call | solution.py:236
  284.9 19.6 %shard_map.291 = (bf16[1024,1024]{1,0:T(8,128)(2,1)S(1)}, bf16[1024,1024]{1,0:T(8,128)(2,1)S(1)}, bf16[1024,1024]{1,0:T(8,128)(2,1)}, bf16[1024,1024]{1,0:T(8,128)(2,1)}) custom-call(bf16[512,2048]{1,0:T(8,128)(2,1)} %copy-done.45, bf16[512,2048]{1,0:T(8,128)(2,1)} %pad_maximum_fusion.4.refs_1_, bf16[512,2048]{1,0:T(8,128)(2,1)} %collective-permute-done.19.refs_2_, ...), custom_call_target="tpu_custom_call" | custom-call | flops 134217728 | bytes 393216 | tf_op jit(solution)/shard_map/pallas_call | solution.py:202
  307.2 7.6 collective-permute-done.21.refs_0_.refs_4_
  317.6 6.6 shard_map.292
  324.1 6.5 shard_map.293
  332.0 20.6 %shard_map.294 = (bf16[1024,1024]{1,0:T(8,128)(2,1)S(1)}, bf16[1024,1024]{1,0:T(8,128)(2,1)S(1)}, bf16[1024,1024]{1,0:T(8,128)(2,1)}, bf16[1024,1024]{1,0:T(8,128)(2,1)}) custom-call(bf16[512,2048]{1,0:T(8,128)(2,1)} %collective-permute-done.21.refs_0_.refs_4_, bf16[512,2048]{1,0:T(8,128)(2,1)} %collective-permute-done.22.refs_1_.refs_5_, ...), custom_call_target="tpu_custom_call" | custom-call | flops 134217728 | bytes 393216 | tf_op jit(solution)/shard_map/pallas_call | solution.py:202
  352.6 4.5 convolution_convert_fusion.5
  361.4 3.7 add_convert_fusion.3
  365.1 3.7 add_convert_fusion.2
  368.8 7.8 shard_map.295
  377.9 6.2 collective-permute-done.27.refs_0_
  384.1 24.3 %shard_map.296 = bf16[2048,1024]{1,0:T(8,128)(2,1)} custom-call(bf16[512,2048]{1,0:T(8,128)(2,1)} %copy-done.45, bf16[512,2048]{1,0:T(8,128)(2,1)} %pad_maximum_fusion.4.refs_1_, bf16[512,2048]{1,0:T(8,128)(2,1)} %collective-permute-done.19.refs_2_, bf16[512,2048]{1,0:T(8,128)(2,1)} %collective-permute-done.20.refs_3_, ...), custom_call_target="tpu_custom_call" | custom-call | flops 268435456 | bytes 458752 | tf_op jit(solution)/shard_map/pallas_call | solution.py:276
  408.5 8.7 %shard_map.297 = (bf16[512,2048]{1,0:T(8,128)(2,1)S(1)}, bf16[512,2048]{1,0:T(8,128)(2,1)S(1)}) custom-call(bf16[1024,1024]{1,0:T(8,128)(2,1)} %get-tuple-element.221.refs_8_.refs_9_.values_ref, bf16[2048,1024]{1,0:T(8,128)(2,1)} %bitcast.147, bf16[1024,2048]{1,0:T(8,128)(2,1)} %collective-permute-done.27.refs_0_), custom_call_target="tpu_custom_call" | custom-call | flops 67108864 | bytes 163840 | tf_op jit(solution)/shard_map/pallas_call | solution.py:350
  417.2 7.7 collective-permute-done.28
  425.2 4.1 convert_add_fusion.3
  434.5 3.7 convolution_convert_fusion.3
  438.3 3.7 convolution_convert_fusion.2
  442.5 26.2 %shard_map.298 = bf16[1024,2048]{1,0:T(8,128)(2,1)} custom-call(bf16[1024,1024]{1,0:T(8,128)(2,1)} %copy-done.2, bf16[1024,1024]{1,0:T(8,128)(2,1)} %copy-done.2, bf16[1024,1024]{1,0:T(8,128)(2,1)} %copy-done.3, bf16[1024,1024]{1,0:T(8,128)(2,1)} %copy-done.3, bf16[1024,1024]{1,0:T(8,128)(2,1)} %copy-done.11, bf16[1024,1024]{1,0:T(8,128)(2,1)} %copy-done.11, ...), custom_call_target="tpu_custom_call" | custom-call | flops 268435456 | bytes 458752 | tf_op jit(solution)/shard_map/pallas_call | solution.py:276
  476.3 4.0 add_convert_fusion.1
  492.3 6.0 convolution_convert_fusion.6.grad_ref
  498.3 30.5 %shard_map.299 = (bf16[512,2048]{1,0:T(8,128)(2,1)S(1)}, bf16[2,1024,256]{2,1,0:T(8,128)(2,1)S(1)}) custom-call(s32[1]{0:T(128)} %bitcast.1.pos_ref, s32[2,8]{1,0:T(2,128)S(1)} %select_reduce_fusion.ends_ref, bf16[512,2048]{1,0:T(8,128)(2,1)} %add_convert_fusion.5.q_ref, bf16[2,1024,256]{2,1,0:T(8,128)(2,1)S(1)} %constant_dynamic-update-slice_fusion.15.kv_ref, ...), custom_call_target="tpu_custom_call" | custom-call | flops 167772160 | bytes 163840 | tf_op jit(solution)/shard_map/pallas_call | solution.py:152
  532.4 6.3 convolution_convert_fusion.1
  540.8 11.5 %collective-permute-start.37 = (bf16[2,256,256]{2,1,0:T(8,128)(2,1)S(1)}, bf16[2,256,256]{2,1,0:T(8,128)(2,1)S(1)}, u32[]{:S(2)}, u32[]{:S(2)}) collective-permute-start(bf16[2,256,256]{2,1,0:T(8,128)(2,1)S(1)} %get-tuple-element.316), channel_id=1, source_target_pairs={{0,1},{1,2},{2,3},{3,0},{4,5},{5,6},{6,7},{7,4},{8,9},{9,10},{10,1... | collective-permute-start | bytes 786440 | tf_op jit(solution)/shard_map/ppermute | solution.py:390
  557.4 5.4 shard_map.300
  563.9 9.8 %shard_map.301 = f32[512,2048]{1,0:T(8,128)} custom-call(bf16[512,2048]{1,0:T(8,128)(2,1)S(1)} %copy-done.7, bf16[2048,2048]{1,0:T(8,128)(2,1)} %bitcast.153), custom_call_target="tpu_custom_call" | custom-call | flops 67108864 | bytes 196608 | tf_op jit(solution)/shard_map/pallas_call | solution.py:350
  573.7 9.9 %collective-permute-done.38 = bf16[2,256,256]{2,1,0:T(8,128)(2,1)S(1)} collective-permute-done((bf16[2,256,256]{2,1,0:T(8,128)(2,1)S(1)}, bf16[2,256,256]{2,1,0:T(8,128)(2,1)S(1)}, u32[]{:S(2)}, u32[]{:S(2)}) %collective-permute-start.38) | collective-permute-done | bytes 262176 | tf_op jit(solution)/shard_map/ppermute | solution.py:390
  584.7 4.4 shard_map.303
  589.2 7.7 shard_map.302
  599.9 4.3 all-to-all-start.1
  611.1 9.0 %all-to-all-done.1 = bf16[8,64,1024]{2,1,0:T(8,128)(2,1)} async-done(((bf16[8,64,1024]{2,1,0:T(8,128)(2,1)}), bf16[8,64,1024]{2,1,0:T(8,128)(2,1)}, u32[]{:S(2)}, u32[]{:S(2)}) %all-to-all-start.1) | async-done | bytes 1048608 | tf_op jit(solution)/shard_map/all_to_all | solution.py:748
  628.4 12.6 %collective-permute-done.42 = bf16[256,2048]{1,0:T(8,128)(2,1)} collective-permute-done((bf16[256,2048]{1,0:T(8,128)(2,1)}, bf16[256,2048]{1,0:T(8,128)(2,1)}, u32[]{:S(2)}, u32[]{:S(2)}) %collective-permute-start.42) | collective-permute-done | bytes 1048608 | tf_op jit(solution)/shard_map/ppermute | solution.py:445
  642.4 5.6 shard_map.304
  650.0 8.0 shard_map.305
  660.9 4.6 convert_add_fusion.1
  665.6 3.5 fusion.20
  677.8 2.9 slice.402
  692.1 42.7 %collective-permute-done.47 = bf16[128,2048]{1,0:T(8,128)(2,1)S(1)} collective-permute-done((bf16[128,2048]{1,0:T(8,128)(2,1)S(1)}, bf16[128,2048]{1,0:T(8,128)(2,1)S(1)}, u32[]{:S(2)}, u32[]{:S(2)}) %collective-permute-start.47) | collective-permute-done | bytes 524320 | tf_op jit(solution)/shard_map/ppermute | solution.py:445
  737.2 33.2 %collective-permute-done.46 = bf16[128,2048]{1,0:T(8,128)(2,1)S(1)} collective-permute-done((bf16[128,2048]{1,0:T(8,128)(2,1)S(1)}, bf16[128,2048]{1,0:T(8,128)(2,1)S(1)}, u32[]{:S(2)}, u32[]{:S(2)}) %collective-permute-start.46) | collective-permute-done | bytes 524320 | tf_op jit(solution)/shard_map/ppermute | solution.py:445
  772.2 3.3 collective-permute-done.55
  776.6 4.0 collective-permute-done.56
  789.7 4.2 collective-permute-done.52
  795.7 3.6 convert_add_fusion.10
  800.3 23.6 %collective-permute-start.59 = (bf16[17664]{0:T(1024)(128)(2,1)S(1)}, bf16[17664]{0:T(1024)(128)(2,1)S(1)}, u32[]{:S(2)}, u32[]{:S(2)}) collective-permute-start(bf16[17664]{0:T(1024)(128)(2,1)S(1)} %get-tuple-element.297), channel_id=1, source_target_pairs={{0,3},{1,0},{2,1},{3,2},{4,7},{5,4},{6,5},{7,6},{8,11},{9,8},{10,9... | collective-permute-start | bytes 105992 | tf_op jit(solution)/shard_map/ppermute | solution.py:390
  824.5 5.2 fusion.1
  833.6 27.0 %reduce-scatter.8.cloned.1.call-done = bf16[128,2048]{1,0:T(8,128)(2,1)} async-done(((bf16[512,2048]{1,0:T(8,128)(2,1)}), bf16[128,2048]{1,0:T(8,128)(2,1)}) %reduce-scatter.8.cloned.1.call-update) | async-done | bytes 524304 | tf_op jit(solution)/shard_map/reduce_scatter | solution.py:734
  (465 shorter events, 197.4 us)
Async XLA Ops:
  7.2 52.1 %all-gather.5.cloned.1.call-start = ((), (), s32[]{:S(2)}) async-start(), calls=%async_computation.5 | async-start | bytes 1638400 | tf_op jit(solution)/shard_map/all_gather | solution.py:524
  20.3 27.0 %collective-permute-start = (bf16[256,2048]{1,0:T(8,128)(2,1)S(1)}, bf16[256,2048]{1,0:T(8,128)(2,1)}, u32[]{:S(2)}, u32[]{:S(2)}) collective-permute-start(bf16[256,2048]{1,0:T(8,128)(2,1)S(1)} %get-tuple-element.306), channel_id=1, source_target_pairs={{0,8},{4,12},{8,0},{12,4},{16,24},{20,28},{24,16},{28,20},{1,9},{5... | collective-permute-start | bytes 3145736 | tf_op jit(solution)/shard_map/ppermute | solution.py:445
  23.2 26.7 %collective-permute-start.1 = (bf16[256,2048]{1,0:T(8,128)(2,1)}, bf16[256,2048]{1,0:T(8,128)(2,1)}, u32[]{:S(2)}, u32[]{:S(2)}) collective-permute-start(bf16[256,2048]{1,0:T(8,128)(2,1)} %get-tuple-element.305), channel_id=1, source_target_pairs={{0,16},{4,20},{8,24},{12,28},{16,0},{20,4},{24,8},{28,12},{1,17},{... | collective-permute-start | bytes 3145736 | tf_op jit(solution)/shard_map/ppermute | solution.py:445
  25.8 33.5 %all-to-all-start = ((bf16[64,8,1024]{2,0,1:T(8,128)(2,1)}), bf16[64,8,1024]{2,0,1:T(8,128)(2,1)S(1)}, u32[]{:S(2)}, u32[]{:S(2)}) async-start(bf16[64,8,1024]{2,0,1:T(8,128)(2,1)} %bitcast.140), calls=%async_computation | async-start | bytes 2097152 | tf_op jit(solution)/shard_map/all_to_all | solution.py:526
  29.4 93.7 %all-gather.7.cloned.1.call-start = ((), (), s32[]{:S(2)}) async-start(), calls=%async_computation.6 | async-start | bytes 11796480 | tf_op jit(solution)/shard_map/all_gather | solution.py:529
  59.3 161.9 %all-gather.9.cloned.1.call-start = ((), (), s32[]{:S(2)}) async-start(), calls=%async_computation.7 | async-start | bytes 9437184 | tf_op jit(solution)/shard_map/all_gather | solution.py:542
  59.4 52.2 %collective-permute-start.6 = (bf16[512,2048]{1,0:T(8,128)(2,1)S(1)}, bf16[512,2048]{1,0:T(8,128)(2,1)}, u32[]{:S(2)}, u32[]{:S(2)}) collective-permute-start(bf16[512,2048]{1,0:T(8,128)(2,1)S(1)} %pad_maximum_fusion.1.refs_0_.refs_8_), channel_id=1, source_target_pairs={{0,4},{4,0},{8,12},{12,8},{16,20},{20,16},{24,28},{28,24},{1,5},{5... | collective-permute-start | bytes 6291464 | tf_op jit(solution)/shard_map/ppermute | solution.py:445
  59.4 52.1 %collective-permute-start.7 = (bf16[512,2048]{1,0:T(8,128)(2,1)}, bf16[512,2048]{1,0:T(8,128)(2,1)}, u32[]{:S(2)}, u32[]{:S(2)}) collective-permute-start(bf16[512,2048]{1,0:T(8,128)(2,1)} %pad_maximum_fusion.2.refs_1_.refs_9_), channel_id=1, source_target_pairs={{0,4},{4,0},{8,12},{12,8},{16,20},{20,16},{24,28},{28,24},{1,5},{5... | collective-permute-start | bytes 6291464 | tf_op jit(solution)/shard_map/ppermute | solution.py:445
  59.9 11.2 %collective-permute-start.2 = (bf16[64,2048]{1,0:T(8,128)(2,1)S(1)}, bf16[64,2048]{1,0:T(8,128)(2,1)}, u32[]{:S(2)}, u32[]{:S(2)}) collective-permute-start(bf16[64,2048]{1,0:T(8,128)(2,1)S(1)} %copy-done.67), channel_id=1, source_target_pairs={{0,1},{1,2},{2,3},{3,0},{4,5},{5,6},{6,7},{7,4},{8,9},{9,10},{10,1... | collective-permute-start | bytes 786440 | tf_op jit(solution)/shard_map/ppermute | solution.py:390
  61.5 20.0 %collective-permute-start.3 = (bf16[64,2048]{1,0:T(8,128)(2,1)S(1)}, bf16[64,2048]{1,0:T(8,128)(2,1)}, u32[]{:S(2)}, u32[]{:S(2)}) collective-permute-start(bf16[64,2048]{1,0:T(8,128)(2,1)S(1)} %copy-done.67), channel_id=1, source_target_pairs={{0,2},{1,3},{2,0},{3,1},{4,6},{5,7},{6,4},{7,5},{8,10},{9,11},{10,... | collective-permute-start | bytes 786440 | tf_op jit(solution)/shard_map/ppermute | solution.py:390
  64.1 17.5 %collective-permute-start.4 = (bf16[64,2048]{1,0:T(8,128)(2,1)S(1)}, bf16[64,2048]{1,0:T(8,128)(2,1)}, u32[]{:S(2)}, u32[]{:S(2)}) collective-permute-start(bf16[64,2048]{1,0:T(8,128)(2,1)S(1)} %copy-done.67), channel_id=1, source_target_pairs={{0,3},{1,0},{2,1},{3,2},{4,7},{5,4},{6,5},{7,6},{8,11},{9,8},{10,9... | collective-permute-start | bytes 786440 | tf_op jit(solution)/shard_map/ppermute | solution.py:390
  81.6 30.0 %collective-permute-start.5 = (bf16[256,2048]{1,0:T(8,128)(2,1)}, bf16[256,2048]{1,0:T(8,128)(2,1)}, u32[]{:S(2)}, u32[]{:S(2)}) collective-permute-start(bf16[256,2048]{1,0:T(8,128)(2,1)} %param.29), channel_id=1, source_target_pairs={{0,1},{1,2},{2,3},{3,0},{4,5},{5,6},{6,7},{7,4},{8,9},{9,10},{10,1... | collective-permute-start | bytes 3145736 | tf_op jit(solution)/shard_map/ppermute | solution.py:390
  123.1 161.8 %all-gather.11.cloned.1.call-start = ((), (), s32[]{:S(2)}) async-start(), calls=%async_computation.8 | async-start | bytes 5242880 | tf_op jit(solution)/shard_map/all_gather | solution.py:573
  130.7 27.5 %collective-permute-start.8 = (bf16[256,2048]{1,0:T(8,128)(2,1)}, bf16[256,2048]{1,0:T(8,128)(2,1)}, u32[]{:S(2)}, u32[]{:S(2)}) collective-permute-start(bf16[256,2048]{1,0:T(8,128)(2,1)} %collective-permute-done.5), channel_id=1, source_target_pairs={{0,1},{1,2},{2,3},{3,0},{4,5},{5,6},{6,7},{7,4},{8,9},{9,10},{10,1... | collective-permute-start | bytes 3145736 | tf_op jit(solution)/shard_map/ppermute | solution.py:390
  158.2 13.0 %collective-permute-start.9 = (bf16[2,256,256]{2,1,0:T(8,128)(2,1)S(1)}, bf16[2,256,256]{2,1,0:T(8,128)(2,1)S(1)}, u32[]{:S(2)}, u32[]{:S(2)}) collective-permute-start(bf16[2,256,256]{2,1,0:T(8,128)(2,1)S(1)} %bitcast.180), channel_id=1, source_target_pairs={{0,1},{1,2},{2,3},{3,0},{4,5},{5,6},{6,7},{7,4},{8,9},{9,10},{10,1... | collective-permute-start | bytes 786440 | tf_op jit(solution)/shard_map/ppermute | solution.py:390
  158.2 20.9 %collective-permute-start.10 = (bf16[2,256,256]{2,1,0:T(8,128)(2,1)S(1)}, bf16[2,256,256]{2,1,0:T(8,128)(2,1)S(1)}, u32[]{:S(2)}, u32[]{:S(2)}) collective-permute-start(bf16[2,256,256]{2,1,0:T(8,128)(2,1)S(1)} %bitcast.181), channel_id=1, source_target_pairs={{0,2},{1,3},{2,0},{3,1},{4,6},{5,7},{6,4},{7,5},{8,10},{9,11},{10,... | collective-permute-start | bytes 786440 | tf_op jit(solution)/shard_map/ppermute | solution.py:390
  160.3 18.8 %collective-permute-start.11 = (bf16[2,256,256]{2,1,0:T(8,128)(2,1)S(1)}, bf16[2,256,256]{2,1,0:T(8,128)(2,1)S(1)}, u32[]{:S(2)}, u32[]{:S(2)}) collective-permute-start(bf16[2,256,256]{2,1,0:T(8,128)(2,1)S(1)} %bitcast.182), channel_id=1, source_target_pairs={{0,3},{1,0},{2,1},{3,2},{4,7},{5,4},{6,5},{7,6},{8,11},{9,8},{10,9... | collective-permute-start | bytes 786440 | tf_op jit(solution)/shard_map/ppermute | solution.py:390
  179.1 42.2 %collective-permute-start.12 = (bf16[256,2048]{1,0:T(8,128)(2,1)}, bf16[256,2048]{1,0:T(8,128)(2,1)}, u32[]{:S(2)}, u32[]{:S(2)}) collective-permute-start(bf16[256,2048]{1,0:T(8,128)(2,1)} %collective-permute-done.8), channel_id=1, source_target_pairs={{0,1},{1,2},{2,3},{3,0},{4,5},{5,6},{6,7},{7,4},{8,9},{9,10},{10,1... | collective-permute-start | bytes 3145736 | tf_op jit(solution)/shard_map/ppermute | solution.py:390
  184.5 48.0 %collective-permute-start.13 = (bf16[512,2048]{1,0:T(8,128)(2,1)S(1)}, bf16[512,2048]{1,0:T(8,128)(2,1)}, u32[]{:S(2)}, u32[]{:S(2)}) collective-permute-start(bf16[512,2048]{1,0:T(8,128)(2,1)S(1)} %pad_maximum_fusion.1.refs_0_.refs_8_), channel_id=1, source_target_pairs={{0,16},{4,20},{8,24},{12,28},{16,0},{20,4},{24,8},{28,12},{1,17},{... | collective-permute-start | bytes 6291464 | tf_op jit(solution)/shard_map/ppermute | solution.py:445
  185.5 47.0 %collective-permute-start.14 = (bf16[512,2048]{1,0:T(8,128)(2,1)}, bf16[512,2048]{1,0:T(8,128)(2,1)}, u32[]{:S(2)}, u32[]{:S(2)}) collective-permute-start(bf16[512,2048]{1,0:T(8,128)(2,1)} %pad_maximum_fusion.2.refs_1_.refs_9_), channel_id=1, source_target_pairs={{0,8},{4,12},{8,0},{12,4},{16,24},{20,28},{24,16},{28,20},{1,9},{5... | collective-permute-start | bytes 6291464 | tf_op jit(solution)/shard_map/ppermute | solution.py:445
  186.6 345.8 %reduce-scatter.4.cloned.1.call-start = ((), (), s32[]{:S(2)}) async-start(), calls=%async_computation.9 | async-start | bytes 5242880 | tf_op jit(solution)/shard_map/reduce_scatter | solution.py:627
  232.6 36.1 %collective-permute-start.15 = (bf16[512,2048]{1,0:T(8,128)(2,1)}, bf16[512,2048]{1,0:T(8,128)(2,1)}, u32[]{:S(2)}, u32[]{:S(2)}) collective-permute-start(bf16[512,2048]{1,0:T(8,128)(2,1)} %collective-permute-done.13.refs_0_.refs_12_), channel_id=1, source_target_pairs={{0,4},{4,0},{8,12},{12,8},{16,20},{20,16},{24,28},{28,24},{1,5},{5... | collective-permute-start | bytes 6291464 | tf_op jit(solution)/shard_map/ppermute | solution.py:445
  232.8 31.9 %collective-permute-start.17 = (bf16[256,2048]{1,0:T(8,128)(2,1)S(1)}, bf16[256,2048]{1,0:T(8,128)(2,1)S(1)}, u32[]{:S(2)}, u32[]{:S(2)}) collective-permute-start(bf16[256,2048]{1,0:T(8,128)(2,1)S(1)} %get-tuple-element.304), channel_id=1, source_target_pairs={{0,8},{4,12},{8,0},{12,4},{16,24},{20,28},{24,16},{28,20},{1,9},{5... | collective-permute-start | bytes 3145736 | tf_op jit(solution)/shard_map/ppermute | solution.py:445
  234.1 36.2 %collective-permute-start.16 = (bf16[512,2048]{1,0:T(8,128)(2,1)}, bf16[512,2048]{1,0:T(8,128)(2,1)}, u32[]{:S(2)}, u32[]{:S(2)}) collective-permute-start(bf16[512,2048]{1,0:T(8,128)(2,1)} %collective-permute-done.14.refs_1_.refs_13_), channel_id=1, source_target_pairs={{0,4},{4,0},{8,12},{12,8},{16,20},{20,16},{24,28},{28,24},{1,5},{5... | collective-permute-start | bytes 6291464 | tf_op jit(solution)/shard_map/ppermute | solution.py:445
  234.3 30.6 %collective-permute-start.18 = (bf16[256,2048]{1,0:T(8,128)(2,1)S(1)}, bf16[256,2048]{1,0:T(8,128)(2,1)S(1)}, u32[]{:S(2)}, u32[]{:S(2)}) collective-permute-start(bf16[256,2048]{1,0:T(8,128)(2,1)S(1)} %get-tuple-element.303), channel_id=1, source_target_pairs={{0,16},{4,20},{8,24},{12,28},{16,0},{20,4},{24,8},{28,12},{1,17},{... | collective-permute-start | bytes 3145736 | tf_op jit(solution)/shard_map/ppermute | solution.py:445
  266.7 18.2 %collective-permute-start.19 = (bf16[512,2048]{1,0:T(8,128)(2,1)S(1)}, bf16[512,2048]{1,0:T(8,128)(2,1)}, u32[]{:S(2)}, u32[]{:S(2)}) collective-permute-start(bf16[512,2048]{1,0:T(8,128)(2,1)S(1)} %pad_maximum_fusion.3.refs_0_), channel_id=1, source_target_pairs={{0,4},{4,0},{8,12},{12,8},{16,20},{20,16},{24,28},{28,24},{1,5},{5... | collective-permute-start | bytes 6291464 | tf_op jit(solution)/shard_map/ppermute | solution.py:445
  266.7 18.2 %collective-permute-start.20 = (bf16[512,2048]{1,0:T(8,128)(2,1)}, bf16[512,2048]{1,0:T(8,128)(2,1)}, u32[]{:S(2)}, u32[]{:S(2)}) collective-permute-start(bf16[512,2048]{1,0:T(8,128)(2,1)} %pad_maximum_fusion.4.refs_1_), channel_id=1, source_target_pairs={{0,4},{4,0},{8,12},{12,8},{16,20},{20,16},{24,28},{28,24},{1,5},{5... | collective-permute-start | bytes 6291464 | tf_op jit(solution)/shard_map/ppermute | solution.py:445
  267.2 47.6 %collective-permute-start.21 = (bf16[512,2048]{1,0:T(8,128)(2,1)S(1)}, bf16[512,2048]{1,0:T(8,128)(2,1)}, u32[]{:S(2)}, u32[]{:S(2)}) collective-permute-start(bf16[512,2048]{1,0:T(8,128)(2,1)S(1)} %pad_maximum_fusion.3.refs_0_), channel_id=1, source_target_pairs={{0,16},{4,20},{8,24},{12,28},{16,0},{20,4},{24,8},{28,12},{1,17},{... | collective-permute-start | bytes 6291464 | tf_op jit(solution)/shard_map/ppermute | solution.py:445
  268.7 47.6 %collective-permute-start.22 = (bf16[512,2048]{1,0:T(8,128)(2,1)}, bf16[512,2048]{1,0:T(8,128)(2,1)}, u32[]{:S(2)}, u32[]{:S(2)}) collective-permute-start(bf16[512,2048]{1,0:T(8,128)(2,1)} %pad_maximum_fusion.4.refs_1_), channel_id=1, source_target_pairs={{0,8},{4,12},{8,0},{12,4},{16,24},{20,28},{24,16},{28,20},{1,9},{5... | collective-permute-start | bytes 6291464 | tf_op jit(solution)/shard_map/ppermute | solution.py:445
  316.3 14.3 %collective-permute-start.23 = (bf16[512,2048]{1,0:T(8,128)(2,1)}, bf16[512,2048]{1,0:T(8,128)(2,1)S(1)}, u32[]{:S(2)}, u32[]{:S(2)}) collective-permute-start(bf16[512,2048]{1,0:T(8,128)(2,1)} %collective-permute-done.21.refs_0_.refs_4_), channel_id=1, source_target_pairs={{0,4},{4,0},{8,12},{12,8},{16,20},{20,16},{24,28},{28,24},{1,5},{5... | collective-permute-start | bytes 6291464 | tf_op jit(solution)/shard_map/ppermute | solution.py:445
  316.3 15.7 %collective-permute-start.24 = (bf16[512,2048]{1,0:T(8,128)(2,1)}, bf16[512,2048]{1,0:T(8,128)(2,1)}, u32[]{:S(2)}, u32[]{:S(2)}) collective-permute-start(bf16[512,2048]{1,0:T(8,128)(2,1)} %collective-permute-done.22.refs_1_.refs_5_), channel_id=1, source_target_pairs={{0,4},{4,0},{8,12},{12,8},{16,20},{20,16},{24,28},{28,24},{1,5},{5... | collective-permute-start | bytes 6291464 | tf_op jit(solution)/shard_map/ppermute | solution.py:445
  376.6 7.5 collective-permute-start.27
  376.7 48.2 %collective-permute-start.28 = (bf16[512,2048]{1,0:T(8,128)(2,1)}, bf16[512,2048]{1,0:T(8,128)(2,1)}, u32[]{:S(2)}, u32[]{:S(2)}) collective-permute-start(bf16[512,2048]{1,0:T(8,128)(2,1)} %add_convert_fusion.3), channel_id=1, source_target_pairs={{0,16},{4,20},{8,24},{12,28},{16,0},{20,4},{24,8},{28,12},{1,17},{... | collective-permute-start | bytes 6291464 | tf_op jit(solution)/shard_map/ppermute | solution.py:445
  377.2 47.9 %collective-permute-start.29 = (bf16[512,2048]{1,0:T(8,128)(2,1)}, bf16[512,2048]{1,0:T(8,128)(2,1)}, u32[]{:S(2)}, u32[]{:S(2)}) collective-permute-start(bf16[512,2048]{1,0:T(8,128)(2,1)} %add_convert_fusion.2), channel_id=1, source_target_pairs={{0,8},{4,12},{8,0},{12,4},{16,24},{20,28},{24,16},{28,20},{1,9},{5... | collective-permute-start | bytes 6291464 | tf_op jit(solution)/shard_map/ppermute | solution.py:445
  408.5 241.5 %reduce-scatter.6.cloned.1.call-start = ((), (), s32[]{:S(2)}) async-start(), calls=%async_computation.10 | async-start | bytes 5242880 | tf_op jit(solution)/shard_map/reduce_scatter | solution.py:634
  430.5 38.2 %collective-permute-start.31 = (bf16[256,2048]{1,0:T(8,128)(2,1)}, bf16[256,2048]{1,0:T(8,128)(2,1)}, u32[]{:S(2)}, u32[]{:S(2)}) collective-permute-start(bf16[256,2048]{1,0:T(8,128)(2,1)} %slice.403), channel_id=1, source_target_pairs={{0,16},{4,20},{8,24},{12,28},{16,0},{20,4},{24,8},{28,12},{1,17},{... | collective-permute-start | bytes 3145736 | tf_op jit(solution)/shard_map/ppermute | solution.py:445
  433.3 37.8 %collective-permute-start.30 = (bf16[256,2048]{1,0:T(8,128)(2,1)}, bf16[256,2048]{1,0:T(8,128)(2,1)}, u32[]{:S(2)}, u32[]{:S(2)}) collective-permute-start(bf16[256,2048]{1,0:T(8,128)(2,1)} %slice.404), channel_id=1, source_target_pairs={{0,8},{4,12},{8,0},{12,4},{16,24},{20,28},{24,16},{28,20},{1,9},{5... | collective-permute-start | bytes 3145736 | tf_op jit(solution)/shard_map/ppermute | solution.py:445
  438.2 35.7 %collective-permute-start.32 = (bf16[512,2048]{1,0:T(8,128)(2,1)}, bf16[512,2048]{1,0:T(8,128)(2,1)}, u32[]{:S(2)}, u32[]{:S(2)}) collective-permute-start(bf16[512,2048]{1,0:T(8,128)(2,1)} %convolution_convert_fusion.3), channel_id=1, source_target_pairs={{0,4},{4,0},{8,12},{12,8},{16,20},{20,16},{24,28},{28,24},{1,5},{5... | collective-permute-start | bytes 6291464 | tf_op jit(solution)/shard_map/ppermute | solution.py:445
  442.0 38.3 %collective-permute-start.33 = (bf16[512,2048]{1,0:T(8,128)(2,1)}, bf16[512,2048]{1,0:T(8,128)(2,1)S(1)}, u32[]{:S(2)}, u32[]{:S(2)}) collective-permute-start(bf16[512,2048]{1,0:T(8,128)(2,1)} %convolution_convert_fusion.2), channel_id=1, source_target_pairs={{0,4},{4,0},{8,12},{12,8},{16,20},{20,16},{24,28},{28,24},{1,5},{5... | collective-permute-start | bytes 6291464 | tf_op jit(solution)/shard_map/ppermute | solution.py:445
  482.7 48.4 %collective-permute-start.34 = (bf16[512,2048]{1,0:T(8,128)(2,1)S(1)}, bf16[512,2048]{1,0:T(8,128)(2,1)S(1)}, u32[]{:S(2)}, u32[]{:S(2)}) collective-permute-start(bf16[512,2048]{1,0:T(8,128)(2,1)S(1)} %add_convert_fusion.1), channel_id=1, source_target_pairs={{0,16},{4,20},{8,24},{12,28},{16,0},{20,4},{24,8},{28,12},{1,17},{... | collective-permute-start | bytes 6291464 | tf_op jit(solution)/shard_map/ppermute | solution.py:445
  484.4 48.0 %collective-permute-start.35 = (bf16[512,2048]{1,0:T(8,128)(2,1)S(1)}, bf16[512,2048]{1,0:T(8,128)(2,1)}, u32[]{:S(2)}, u32[]{:S(2)}) collective-permute-start(bf16[512,2048]{1,0:T(8,128)(2,1)S(1)} %add_convert_fusion), channel_id=1, source_target_pairs={{0,8},{4,12},{8,0},{12,4},{16,24},{20,28},{24,16},{28,20},{1,9},{5... | collective-permute-start | bytes 6291464 | tf_op jit(solution)/shard_map/ppermute | solution.py:445
  538.7 18.7 %collective-permute-start.36 = (bf16[1024,2048]{1,0:T(8,128)(2,1)}, bf16[1024,2048]{1,0:T(8,128)(2,1)}, u32[]{:S(2)}, u32[]{:S(2)}) collective-permute-start(bf16[1024,2048]{1,0:T(8,128)(2,1)} %convolution_convert_fusion.1), channel_id=1, source_target_pairs={{0,4},{4,0},{8,12},{12,8},{16,20},{20,16},{24,28},{28,24},{1,5},{5... | collective-permute-start | bytes 12582920 | tf_op jit(solution)/shard_map/ppermute | solution.py:445
  540.8 32.8 %collective-permute-start.37 = (bf16[2,256,256]{2,1,0:T(8,128)(2,1)S(1)}, bf16[2,256,256]{2,1,0:T(8,128)(2,1)S(1)}, u32[]{:S(2)}, u32[]{:S(2)}) collective-permute-start(bf16[2,256,256]{2,1,0:T(8,128)(2,1)S(1)} %get-tuple-element.316), channel_id=1, source_target_pairs={{0,1},{1,2},{2,3},{3,0},{4,5},{5,6},{6,7},{7,4},{8,9},{9,10},{10,1... | collective-permute-start | bytes 786440 | tf_op jit(solution)/shard_map/ppermute | solution.py:390
  552.4 31.2 %collective-permute-start.38 = (bf16[2,256,256]{2,1,0:T(8,128)(2,1)S(1)}, bf16[2,256,256]{2,1,0:T(8,128)(2,1)S(1)}, u32[]{:S(2)}, u32[]{:S(2)}) collective-permute-start(bf16[2,256,256]{2,1,0:T(8,128)(2,1)S(1)} %get-tuple-element.315), channel_id=1, source_target_pairs={{0,2},{1,3},{2,0},{3,1},{4,6},{5,7},{6,4},{7,5},{8,10},{9,11},{10,... | collective-permute-start | bytes 786440 | tf_op jit(solution)/shard_map/ppermute | solution.py:390
  554.5 30.2 %collective-permute-start.39 = (bf16[2,256,256]{2,1,0:T(8,128)(2,1)S(1)}, bf16[2,256,256]{2,1,0:T(8,128)(2,1)S(1)}, u32[]{:S(2)}, u32[]{:S(2)}) collective-permute-start(bf16[2,256,256]{2,1,0:T(8,128)(2,1)S(1)} %get-tuple-element.314), channel_id=1, source_target_pairs={{0,3},{1,0},{2,1},{3,2},{4,7},{5,4},{6,5},{7,6},{8,11},{9,8},{10,9... | collective-permute-start | bytes 786440 | tf_op jit(solution)/shard_map/ppermute | solution.py:390
  589.2 52.0 %collective-permute-start.41 = (bf16[1024,2048]{1,0:T(8,128)(2,1)}, bf16[1024,2048]{1,0:T(8,128)(2,1)}, u32[]{:S(2)}, u32[]{:S(2)}) collective-permute-start(bf16[1024,2048]{1,0:T(8,128)(2,1)} %shard_map.303), channel_id=1, source_target_pairs={{0,4},{4,0},{8,12},{12,8},{16,20},{20,16},{24,28},{28,24},{1,5},{5... | collective-permute-start | bytes 12582920 | tf_op jit(solution)/shard_map/ppermute | solution.py:445
  596.9 53.1 %collective-permute-start.40 = (bf16[1024,2048]{1,0:T(8,128)(2,1)}, bf16[1024,2048]{1,0:T(8,128)(2,1)}, u32[]{:S(2)}, u32[]{:S(2)}) collective-permute-start(bf16[1024,2048]{1,0:T(8,128)(2,1)} %shard_map.302), channel_id=1, source_target_pairs={{0,4},{4,0},{8,12},{12,8},{16,20},{20,16},{24,28},{28,24},{1,5},{5... | collective-permute-start | bytes 12582920 | tf_op jit(solution)/shard_map/ppermute | solution.py:445
  599.9 20.2 %all-to-all-start.1 = ((bf16[8,64,1024]{2,1,0:T(8,128)(2,1)}), bf16[8,64,1024]{2,1,0:T(8,128)(2,1)}, u32[]{:S(2)}, u32[]{:S(2)}) async-start(bf16[8,64,1024]{2,1,0:T(8,128)(2,1)} %reduce-scatter.4.cloned.1.call-done), calls=%async_computation.4 | async-start | bytes 2097152 | tf_op jit(solution)/shard_map/all_to_all | solution.py:748
  604.1 256.5 %reduce-scatter.8.cloned.1.call-start = ((), (), s32[]{:S(2)}) async-start(), calls=%async_computation.11 | async-start | bytes 2621440 | tf_op jit(solution)/shard_map/reduce_scatter | solution.py:734
  607.8 33.3 %collective-permute-start.42 = (bf16[256,2048]{1,0:T(8,128)(2,1)}, bf16[256,2048]{1,0:T(8,128)(2,1)}, u32[]{:S(2)}, u32[]{:S(2)}) collective-permute-start(bf16[256,2048]{1,0:T(8,128)(2,1)} %copy-done.29), channel_id=1, source_target_pairs={{0,16},{4,20},{8,24},{12,28},{16,0},{20,4},{24,8},{28,12},{1,17},{... | collective-permute-start | bytes 3145736 | tf_op jit(solution)/shard_map/ppermute | solution.py:445
  609.6 31.5 %collective-permute-start.43 = (bf16[256,2048]{1,0:T(8,128)(2,1)}, bf16[256,2048]{1,0:T(8,128)(2,1)}, u32[]{:S(2)}, u32[]{:S(2)}) collective-permute-start(bf16[256,2048]{1,0:T(8,128)(2,1)} %copy-done.28), channel_id=1, source_target_pairs={{0,8},{4,12},{8,0},{12,4},{16,24},{20,28},{24,16},{28,20},{1,9},{5... | collective-permute-start | bytes 3145736 | tf_op jit(solution)/shard_map/ppermute | solution.py:445
  676.3 113.1 %collective-permute-start.45 = (bf16[256,2048]{1,0:T(8,128)(2,1)S(1)}, bf16[256,2048]{1,0:T(8,128)(2,1)S(1)}, u32[]{:S(2)}, u32[]{:S(2)}) collective-permute-start(bf16[256,2048]{1,0:T(8,128)(2,1)S(1)} %slice.401), channel_id=1, source_target_pairs={{0,16},{4,20},{8,24},{12,28},{16,0},{20,4},{24,8},{28,12},{1,17},{... | collective-permute-start | bytes 3145736 | tf_op jit(solution)/shard_map/ppermute | solution.py:445
  680.8 115.0 %collective-permute-start.44 = (bf16[256,2048]{1,0:T(8,128)(2,1)}, bf16[256,2048]{1,0:T(8,128)(2,1)}, u32[]{:S(2)}, u32[]{:S(2)}) collective-permute-start(bf16[256,2048]{1,0:T(8,128)(2,1)} %slice.402), channel_id=1, source_target_pairs={{0,8},{4,12},{8,0},{12,4},{16,24},{20,28},{24,16},{28,20},{1,9},{5... | collective-permute-start | bytes 3145736 | tf_op jit(solution)/shard_map/ppermute | solution.py:445
  681.5 55.2 %collective-permute-start.48 = (bf16[1152,256]{1,0:T(8,128)(2,1)S(1)}, bf16[1152,256]{1,0:T(8,128)(2,1)S(1)}, u32[]{:S(2)}, u32[]{:S(2)}) collective-permute-start(bf16[1152,256]{1,0:T(8,128)(2,1)S(1)} %bitcast.177), channel_id=1, source_target_pairs={{0,4},{4,0},{8,12},{12,8},{16,20},{20,16},{24,28},{28,24},{1,5},{5... | collective-permute-start | bytes 1769480 | tf_op jit(solution)/shard_map/ppermute | solution.py:445
  681.6 100.1 %collective-permute-start.49 = (bf16[256,2048]{1,0:T(8,128)(2,1)S(1)}, bf16[256,2048]{1,0:T(8,128)(2,1)S(1)}, u32[]{:S(2)}, u32[]{:S(2)}) collective-permute-start(bf16[256,2048]{1,0:T(8,128)(2,1)S(1)} %copy-done.27), channel_id=1, source_target_pairs={{0,16},{4,20},{8,24},{12,28},{16,0},{20,4},{24,8},{28,12},{1,17},{... | collective-permute-start | bytes 3145736 | tf_op jit(solution)/shard_map/ppermute | solution.py:445
  684.7 50.0 %collective-permute-start.47 = (bf16[128,2048]{1,0:T(8,128)(2,1)S(1)}, bf16[128,2048]{1,0:T(8,128)(2,1)S(1)}, u32[]{:S(2)}, u32[]{:S(2)}) collective-permute-start(bf16[128,2048]{1,0:T(8,128)(2,1)S(1)} %slice.407), channel_id=1, source_target_pairs={{0,16},{4,20},{8,24},{12,28},{16,0},{20,4},{24,8},{28,12},{1,17},{... | collective-permute-start | bytes 1572872 | tf_op jit(solution)/shard_map/ppermute | solution.py:445
  734.8 47.0 %collective-permute-start.50 = (bf16[256,2048]{1,0:T(8,128)(2,1)S(1)}, bf16[256,2048]{1,0:T(8,128)(2,1)S(1)}, u32[]{:S(2)}, u32[]{:S(2)}) collective-permute-start(bf16[256,2048]{1,0:T(8,128)(2,1)S(1)} %copy-done.25), channel_id=1, source_target_pairs={{0,8},{4,12},{8,0},{12,4},{16,24},{20,28},{24,16},{28,20},{1,9},{5... | collective-permute-start | bytes 3145736 | tf_op jit(solution)/shard_map/ppermute | solution.py:445
  736.7 33.7 %collective-permute-start.46 = (bf16[128,2048]{1,0:T(8,128)(2,1)S(1)}, bf16[128,2048]{1,0:T(8,128)(2,1)S(1)}, u32[]{:S(2)}, u32[]{:S(2)}) collective-permute-start(bf16[128,2048]{1,0:T(8,128)(2,1)S(1)} %slice.408), channel_id=1, source_target_pairs={{0,8},{4,12},{8,0},{12,4},{16,24},{20,28},{24,16},{28,20},{1,9},{5... | collective-permute-start | bytes 1572872 | tf_op jit(solution)/shard_map/ppermute | solution.py:445
  782.2 11.7 %collective-permute-start.52 = (bf16[128,2048]{1,0:T(8,128)(2,1)S(1)}, bf16[128,2048]{1,0:T(8,128)(2,1)S(1)}, u32[]{:S(2)}, u32[]{:S(2)}) collective-permute-start(bf16[128,2048]{1,0:T(8,128)(2,1)S(1)} %slice.405), channel_id=1, source_target_pairs={{0,16},{4,20},{8,24},{12,28},{16,0},{20,4},{24,8},{28,12},{1,17},{... | collective-permute-start | bytes 1572872 | tf_op jit(solution)/shard_map/ppermute | solution.py:445
  783.7 10.3 %collective-permute-start.51 = (bf16[128,2048]{1,0:T(8,128)(2,1)S(1)}, bf16[128,2048]{1,0:T(8,128)(2,1)S(1)}, u32[]{:S(2)}, u32[]{:S(2)}) collective-permute-start(bf16[128,2048]{1,0:T(8,128)(2,1)S(1)} %slice.406), channel_id=1, source_target_pairs={{0,8},{4,12},{8,0},{12,4},{16,24},{20,28},{24,16},{28,20},{1,9},{5... | collective-permute-start | bytes 1572872 | tf_op jit(solution)/shard_map/ppermute | solution.py:445
  787.5 11.8 %collective-permute-start.54 = (bf16[144,256]{1,0:T(8,128)(2,1)S(1)}, bf16[144,256]{1,0:T(8,128)(2,1)S(1)}, u32[]{:S(2)}, u32[]{:S(2)}) collective-permute-start(bf16[144,256]{1,0:T(8,128)(2,1)S(1)} %slice.410), channel_id=1, source_target_pairs={{0,8},{4,12},{8,0},{12,4},{16,24},{20,28},{24,16},{28,20},{1,9},{5... | collective-permute-start | bytes 221192 | tf_op jit(solution)/shard_map/ppermute | solution.py:445
  800.3 29.6 %collective-permute-start.59 = (bf16[17664]{0:T(1024)(128)(2,1)S(1)}, bf16[17664]{0:T(1024)(128)(2,1)S(1)}, u32[]{:S(2)}, u32[]{:S(2)}) collective-permute-start(bf16[17664]{0:T(1024)(128)(2,1)S(1)} %get-tuple-element.297), channel_id=1, source_target_pairs={{0,3},{1,0},{2,1},{3,2},{4,7},{5,4},{6,5},{7,6},{8,11},{9,8},{10,9... | collective-permute-start | bytes 105992 | tf_op jit(solution)/shard_map/ppermute | solution.py:390
  823.9 7.4 collective-permute-start.58
  823.9 7.4 collective-permute-start.57
  (86 other events, 1185.0 us)
Sparse Core Ops, SparseCore 0:
  17.7 35.3 all-gather.4
  59.4 63.5 all-gather.6
  125.5 54.3 all-gather.8
  186.7 87.8 all-gather.10
  408.6 87.0 reduce-scatter.3
  538.9 101.1 reduce-scatter.5
  795.8 64.7 reduce-scatter.7

commit v11 on v10

--- a/solution.py
+++ b/solution.py
@@ -116,11 +116,11 @@
     return smem, heads, keys, norm
 
 
-def attn_cost(windows, span, win, products):
+def attn_cost(windows, span, win, products, haste=HASTE):
     return pl.CostEstimate(
-        flops=2 * products * windows * HEADS * span * win * HD // HASTE,
-        transcendentals=windows * HEADS * span * win // HASTE,
-        bytes_accessed=products * windows * HEADS * span * HD * 2 // HASTE,
+        flops=2 * products * windows * HEADS * span * win * HD // haste,
+        transcendentals=windows * HEADS * span * win // haste,
+        bytes_accessed=products * windows * HEADS * span * HD * 2 // haste,
     )
 
 
@@ -173,10 +173,11 @@
 def middle_kernel(count, *refs):
     blocks, back_ref = refs[:count], refs[count]
     up_ref, bias_ref = refs[count + 1], refs[count + 2]
-    outs = refs[count + 3 :]
+    outs, sum_ref = refs[count + 3 : -1], refs[-1]
     groups = len(outs) // 2
     size = blocks[0].shape[0]
     root = math.sqrt(2.0 / math.pi)
+    summed = jnp.zeros(sum_ref.shape, F32)
     for i, block in enumerate(blocks):
         act = jnp.dot(block[...], up_ref[...], preferred_element_type=F32) + bias_ref[...]
         square = act * act
@@ -187,7 +188,10 @@
         group, place = divmod(i, count // groups)
         at = slice(place * size, (place + 1) * size)
         outs[group][at, :] = (act * upper).astype(BF16)
-        outs[groups + group][at, :] = (back * slope).astype(BF16)
+        pre = (back * slope).astype(BF16)
+        outs[groups + group][at, :] = pre
+        summed += jnp.sum(pre.astype(F32), axis=0, keepdims=True)
+    sum_ref[...] = summed
 
 
 def middle_layer(blocks, back, up_part, bias, tile=512):
@@ -201,7 +205,7 @@
     slab = pl.BlockSpec((group, tile), lambda j: (0, j))
     out = pl.pallas_call(
         functools.partial(middle_kernel, count),
-        out_shape=[jax.ShapeDtypeStruct((group, units), BF16)] * 4,
+        out_shape=[jax.ShapeDtypeStruct((group, units), BF16)] * 4 + [jax.ShapeDtypeStruct((1, units), F32)],
         grid=(units // tile,),
         in_specs=[whole] * count
         + [
@@ -209,7 +213,7 @@
             pl.BlockSpec((width, tile), lambda j: (0, j)),
             pl.BlockSpec((1, tile), lambda j: (0, j)),
         ],
-        out_specs=[slab] * 4,
+        out_specs=[slab] * 4 + [pl.BlockSpec((1, tile), lambda j: (0, j))],
         compiler_params=pltpu.CompilerParams(vmem_limit_bytes=48 * 2**20),
         cost_estimate=pl.CostEstimate(
             flops=2 * count * size * width * units // HASTE,
@@ -217,7 +221,7 @@
             bytes_accessed=2 * (count * size * (width + 3 * units) + width * units) // HASTE,
         ),
     )(*blocks, back, up_part, bias.reshape(1, units))
-    return list(out[:2]), list(out[2:])
+    return list(out[:2]), list(out[2:4]), out[4]
 
 
 def back_kernel(count, *refs):
@@ -281,9 +285,9 @@
         out_specs=pl.BlockSpec((tile, breadth), lambda i: (i, 0)),
         compiler_params=pltpu.CompilerParams(vmem_limit_bytes=52 * 2**20),
         cost_estimate=pl.CostEstimate(
-            flops=2 * count * size * height * breadth // HASTE,
+            flops=2 * count * size * height * breadth,
             transcendentals=0,
-            bytes_accessed=2 * (count * size * (height + breadth) + height * breadth) // HASTE,
+            bytes_accessed=2 * (count * size * (height + breadth) + height * breadth),
         ),
     )(*[array for array, _ in lefts], *[array for array, _ in rights])
 
@@ -592,7 +596,7 @@
         )
         back_far = back_product(grad_lots[1], down_late)
         bias_up_part = lax.dynamic_slice_in_dim(bias_up, my_dp * ff_own, ff_own)
-        hid_near, pre_near = middle_layer(two_lots[0], back_near, up_part, bias_up_part)
+        hid_near, pre_near, up_bias_near = middle_layer(two_lots[0], back_near, up_part, bias_up_part)
         back_far, attended_late, normed_late, pre_near[0], pre_near[1], *two_far = tie(
             back_far, attended_late, normed_late, *pre_near, *two_far
         )
@@ -600,7 +604,7 @@
         att_mine, att_sib = reorder(attended_late, places)
         one_mine, one_sib = reorder(normed_late, places)
         back_far, att_mine, att_sib, one_mine, one_sib = tie(back_far, att_mine, att_sib, one_mine, one_sib)
-        hid_far, pre_far = middle_layer(two_lots[1], back_far, up_part, bias_up_part)
+        hid_far, pre_far, up_bias_far = middle_layer(two_lots[1], back_far, up_part, bias_up_part)
         block = two_near[0].shape[0]
         lots = (slice(None, block), slice(block, None))
 
@@ -657,36 +661,35 @@
         attended_grad = dot_nt(branch_grad, full_o).astype(BF16)
 
         query_grad, kv_terms = attn_backward(queries, kv_window, norms, attended_grad, first, file_ends)
-        query_grad, kv_terms, grad_up, *out_got = tie(query_grad, kv_terms, grad_up, *out_got)
         kv_got = line.scatter(kv_terms.reshape(windows, n_z, local_len, 2 * HD), 1)
-        theirs = plane.swap(dot_tn(one_sib, query_grad).astype(BF16), 1)
-        wq_parts = product(one_mine, query_grad, "tn", 4, [theirs])
+        query_sib = dot_tn(one_sib, query_grad).astype(BF16)
+        query_sib, hid_late, grad_up, *out_got = tie(query_sib, hid_near[1], grad_up, *out_got)
+        theirs = plane.swap(query_sib, 1)
+        out_sib = product(hid_late, down_part)
+        out_sib, one_late = tie(out_sib, one_mine)
+        out_theirs = plane.swap(out_sib, 1)
+        wq_parts = product(one_late, query_grad, "tn", 4, [theirs])
         wq_got = send_rows(wq_parts)
-        wq_parts[1], query_late = tie(wq_parts[1], query_grad)
+        wq_parts[1], hid_late, out_theirs = tie(wq_parts[1], hid_near[0], out_theirs)
+        out_sum = merge(product(hid_late, down_part, "nn", 2, [out_theirs]), out_got)
+        out_sum[0], out_sum[1], att_sib, query_late, *kv_got = tie(*out_sum, att_sib, query_grad, *kv_got)
+        branch_out = plane.fold(out_sum)
+        wo_sib = product(att_sib, branch_grad, "tn")
+        wo_sib, query_late = tie(wo_sib, query_late)
+        wo_theirs = plane.swap(wo_sib, 1)
         query_part = product(query_late, full_q, "nt", kind=F32)
-        query_part, att_sib, branch_late, hid_late, *kv_got = tie(
-            query_part, att_sib, branch_grad, hid_near[1], *kv_got
-        )
-        wo_theirs = plane.swap(product(att_sib, branch_late, "tn"), 1)
-        theirs = plane.swap(product(hid_late, down_part), 1)
-        wo_theirs, *wq_got = tie(wo_theirs, *wq_got)
-        wo_parts = product(att_mine, branch_late, "tn", 4, [wo_theirs])
+        query_part, wo_theirs, *wq_got = tie(query_part, wo_theirs, *wq_got)
+        wo_parts = product(att_mine, branch_grad, "tn", 4, [wo_theirs])
         wo_got = send_rows(wo_parts)
-        query_part, hid_near[0], theirs, wo_parts[1], grad_down = tie(
-            query_part, hid_near[0], theirs, wo_parts[1], grad_down
-        )
-        out_sum = merge(product(hid_near[0], down_part, "nn", 2, [theirs]), out_got)
         kv_grad = total(kv_got).astype(BF16).reshape(rows, 2 * HD)
-        query_part, kv_grad, *out_sum = tie(query_part, kv_grad, *out_sum)
-        branch_out = plane.fold(out_sum)
+        query_part, kv_grad, wo_parts[1], branch_out = tie(query_part, kv_grad, wo_parts[1], branch_out)
 
         one_grad = query_part + dot_nt(kv_grad, full_kv)
-        grad_bq = jnp.sum(query_late.astype(F32), axis=0)
+        grad_bq = jnp.sum(query_grad.astype(F32), axis=0)
         grad_bv = jnp.sum(kv_grad[:, HD:].astype(F32), axis=0)
         grad_gain_one = jnp.sum(one_grad * xhat_one, axis=0)
         grad_shift_one = jnp.sum(one_grad, axis=0)
-        up_bias_part = sum(jnp.sum(lot.astype(F32), axis=0) for lot in pre_near + pre_far)
-        grad_bup = jnp.where(jnp.arange(n_dp)[:, None] == my_dp, up_bias_part[None], 0.0).reshape(-1)
+        grad_bup = jnp.where(jnp.arange(n_dp)[:, None] == my_dp, up_bias_near + up_bias_far, 0.0).reshape(-1)
         sums = (
             (0, grad_bq),
             (2, grad_bo),
@@ -722,7 +725,7 @@
         theirs = plane.swap(with_vectors(dot_tn(one_sib, kv_grad), 1).astype(BF16), 1)
         kv_parts = cut((with_vectors(dot_tn(one_mine, kv_grad), 0) + theirs.astype(F32)).astype(BF16))
         kv_parts_got = send_rows(kv_parts)
-        kv_parts[1], *wo_got = tie(kv_parts[1], *wo_got)
+        kv_parts[1], grad_down, *wo_got = tie(kv_parts[1], grad_down, *wo_got)
 
         both_rows = jnp.concatenate(
             [

time: 881 us -> 811 us (0.921)
  waiting for transfers between devices: 269 us -> 219 us
  starting transfers between devices: 111 us -> 86 us
    ppermute x45, waiting for transfers between devices: 145 us -> 109 us  [swap(): return lax.ppermute(block, 'dp', [(i, i ^ bit) for i in range(self.count)])]
    ppermute x15, starting transfers between devices: 62.9 us -> 41.4 us  [send(): lax.ppermute(block, 'fsdp', [(i, (i + places) % self.count) for i in rang...]
    all_to_all x1, waiting for transfers between devices: 8.99 us -> 0.01 us  [local(): lax.all_to_all(grad_up.reshape(n_dp * own, ff_own), 'dp', 0, 1, tiled=True)]
    unnamed x184 -> x200, local copies, waits for them, and re-layouts: 29.3 us -> 31.4 us
  transfers between devices with their start and end apart: 69 -> 69, of which waited for: 29 -> 26; matrix products, arithmetic and copies ran while one was open for 18% -> 22% of each run, Pallas kernels for 24% -> 27%
where the time goes in v11:
time: 811 us; the launch traced here: 800 us
  Pallas kernels  251 us (31%)
  waiting for transfers between devices  219 us (27%)
  starting transfers between devices  86 us (11%)
  local copies, waits for them, and re-layouts  84.8 us (10%)
  matrix products  73 us (9%)
  other arithmetic  69.9 us (9%)
  between operations  16.3 us (2%)
    ppermute x45, waiting for transfers between devices, swap(): return lax.ppermute(block, 'dp', [(i, i ^ bit) for i in range(self.count)])  109 us
    ppermute x15, waiting for transfers between devices, send(): lax.ppermute(block, 'fsdp', [(i, (i + places) % self.count) for i in rang...  62.8 us
    pallas_call x8, Pallas kernels, product(): pl.pallas_call(functools.partial(product_kernel, form, len(extra)), out_s...  56.6 us
    pallas_call x2, Pallas kernels, weight_grad(): pl.pallas_call(functools.partial(weight_kernel, count), out_shape=jax.Sha...  52 us
    pallas_call x2, Pallas kernels, middle_layer(): pl.pallas_call(functools.partial(middle_kernel, count), out_shape=[jax.Sh...  41.7 us
    ppermute x15, starting transfers between devices, send(): lax.ppermute(block, 'fsdp', [(i, (i + places) % self.count) for i in rang...  41.4 us
    pallas_call x2, Pallas kernels, back_product(): pl.pallas_call(functools.partial(back_kernel, count), out_shape=jax.Shape...  38.4 us
    dot_general x7, matrix products, dot_nn(): return jnp.dot(left, right, preferred_element_type=F32)  36.1 us
  transfers between devices with their start and end apart: 69, of which 26 were waited for; matrix products, arithmetic and copies ran while one was open for 22% of the time, Pallas kernels for 27%

profile of v11, /device:TPU:0, one launch (start us, length us, event | category | flops | bytes accessed | tf_op | source)
XLA Modules:
  0.0 800.3 jit_solution(9614178067749931914)
XLA Ops:
  20.3 2.9 collective-permute-start
  25.8 3.6 all-to-all-start
  29.4 17.9 %collective-permute-done = bf16[256,2048]{1,0:T(8,128)(2,1)} collective-permute-done((bf16[256,2048]{1,0:T(8,128)(2,1)S(1)}, bf16[256,2048]{1,0:T(8,128)(2,1)}, u32[]{:S(2)}, u32[]{:S(2)}) %collective-permute-start) | collective-permute-done | bytes 1048608 | tf_op jit(solution)/shard_map/ppermute | solution.py:449
  49.9 3.1 pad_maximum_fusion.3.refs_1_.refs_9_
  53.0 6.3 all-to-all-done
  67.7 3.5 collective-permute-done.2
  71.1 10.4 %collective-permute-done.3 = bf16[64,2048]{1,0:T(8,128)(2,1)} collective-permute-done((bf16[64,2048]{1,0:T(8,128)(2,1)S(1)}, bf16[64,2048]{1,0:T(8,128)(2,1)}, u32[]{:S(2)}, u32[]{:S(2)}) %collective-permute-start.3) | collective-permute-done | bytes 262176 | tf_op jit(solution)/shard_map/ppermute | solution.py:394
  81.6 6.1 collective-permute-start.5
  94.6 17.0 %collective-permute-done.5 = bf16[256,2048]{1,0:T(8,128)(2,1)} collective-permute-done((bf16[256,2048]{1,0:T(8,128)(2,1)}, bf16[256,2048]{1,0:T(8,128)(2,1)}, u32[]{:S(2)}, u32[]{:S(2)}) %collective-permute-start.5) | collective-permute-done | bytes 1048608 | tf_op jit(solution)/shard_map/ppermute | solution.py:394
  111.6 11.5 %all-gather.7.cloned.1.call-done = bf16[2560,2048]{1,0:T(8,128)(2,1)} async-done(((bf16[320,2048]{1,0:T(8,128)(2,1)}), bf16[2560,2048]{1,0:T(8,128)(2,1)}) %all-gather.7.cloned.1.call-update) | async-done | bytes 10485776 | tf_op jit(solution)/shard_map/all_gather | solution.py:533
  135.2 8.3 %slice.300 = bf16[32,64,2048]{2,1,0:T(8,128)(2,1)} slice(bf16[32,80,2048]{2,1,0:T(8,128)(2,1)} %bitcast.155), slice={[0:32], [0:64], [0:2048]} | slice | bytes 16777216 | tf_op jit(solution)/shard_map/slice | solution.py:548
  148.4 9.9 %collective-permute-done.8 = bf16[256,2048]{1,0:T(8,128)(2,1)} collective-permute-done((bf16[256,2048]{1,0:T(8,128)(2,1)}, bf16[256,2048]{1,0:T(8,128)(2,1)}, u32[]{:S(2)}, u32[]{:S(2)}) %collective-permute-start.8) | collective-permute-done | bytes 1048608 | tf_op jit(solution)/shard_map/ppermute | solution.py:394
  162.1 8.2 %add_convert_fusion.6.q_ref = bf16[512,2048]{1,0:T(8,128)(2,1)S(1)} fusion(bf16[512,2048]{1,0:T(8,128)(2,1)S(1)} %fusion.12.first_ref.second_ref, bf16[2048,2048]{1,0:T(8,128)(2,1)} %bitcast.152, f32[2048]{0:T(1024)S(1)} %reshape.396), kind=kOutput, calls=%fused_computation.42 | convolution fusion | flops 4297064448 | bytes 12591104 | tf_op jit(solution)/shard_map/dot_general | solution.py:21
  170.3 8.9 %collective-permute-done.10 = bf16[2,256,256]{2,1,0:T(8,128)(2,1)S(1)} collective-permute-done((bf16[2,256,256]{2,1,0:T(8,128)(2,1)S(1)}, bf16[2,256,256]{2,1,0:T(8,128)(2,1)S(1)}, u32[]{:S(2)}, u32[]{:S(2)}) %collective-permute-start.10) | collective-permute-done | bytes 262176 | tf_op jit(solution)/shard_map/ppermute | solution.py:394
  179.2 5.1 collective-permute-start.12
  187.2 18.8 %shard_map.288 = (bf16[512,2048]{1,0:T(8,128)(2,1)S(1)}, f32[512,128]{1,0:T(8,128)S(1)}) custom-call(s32[1]{0:T(128)} %bitcast.1.pos_ref, s32[2,8]{1,0:T(2,128)S(1)} %select_reduce_fusion.ends_ref, bf16[512,2048]{1,0:T(8,128)(2,1)S(1)} %add_convert_fusion.6.q_ref, bf16[2,1024,256]{2,1,0:T(8,128)(2,1)S(1)} %constant_dynamic-update-slice_fusion.15.kv_ref), custom_call_target="tpu_custom_call" | custom-call | flops 67108864 | bytes 65536 | tf_op jit(solution)/shard_map/pallas_call | solution.py:132
  208.3 13.1 %collective-permute-done.12 = bf16[256,2048]{1,0:T(8,128)(2,1)} collective-permute-done((bf16[256,2048]{1,0:T(8,128)(2,1)}, bf16[256,2048]{1,0:T(8,128)(2,1)}, u32[]{:S(2)}, u32[]{:S(2)}) %collective-permute-start.12) | collective-permute-done | bytes 1048608 | tf_op jit(solution)/shard_map/ppermute | solution.py:394
  221.4 9.3 %fusion.48 = (f32[512]{0:T(512)S(1)}, f32[512,2048]{1,0:T(8,128)S(1)}) fusion(f32[2048]{0:T(1024)S(1)} %reshape.397, bf16[512,2048]{1,0:T(8,128)(2,1)} %copy-done.6, bf16[2048,2048]{1,0:T(8,128)(2,1)} %all-gather.9.cloned.1.call-done, bf16[2,256,2048]{2,1,0:T(8,128)(2,1)} %param.17), kind=kOutput, calls=%fused_computation.187 | convolution fusion | flops 4299161088 | bytes 16787456 | tf_op jit(solution)/shard_map/dot_general | solution.py:21
  241.8 23.8 %shard_map.289.refs_4_ = bf16[2048,1024]{1,0:T(8,128)(2,1)} custom-call(bf16[512,2048]{1,0:T(8,128)(2,1)S(1)} %copy-done.8, bf16[512,2048]{1,0:T(8,128)(2,1)S(1)} %copy-done.9, bf16[512,2048]{1,0:T(8,128)(2,1)} %collective-permute-done.6.refs_2_.refs_10_, bf16[512,2048]{1,0:T(8,128)(2,1)} %collective-permute-done.7.refs_3_.refs_11_, ...), custom_call_target="tpu_custom_call" | custom-call | flops 134217728 | bytes 262144 | tf_op jit(solution)/shard_map/pallas_call | solution.py:240
  271.2 14.6 %shard_map.290.refs_4_ = bf16[2048,1024]{1,0:T(8,128)(2,1)} custom-call(bf16[512,2048]{1,0:T(8,128)(2,1)} %collective-permute-done.13.refs_0_.refs_12_, bf16[512,2048]{1,0:T(8,128)(2,1)} %collective-permute-done.14.refs_1_.refs_13_, bf16[512,2048]{1,0:T(8,128)(2,1)} %collective-permute-done.15.refs_2_.refs_14_, ...), custom_call_target="tpu_custom_call" | custom-call | flops 134217728 | bytes 262144 | tf_op jit(solution)/shard_map/pallas_call | solution.py:240
  285.8 20.5 %shard_map.291 = (bf16[1024,1024]{1,0:T(8,128)(2,1)S(1)}, bf16[1024,1024]{1,0:T(8,128)(2,1)S(1)}, bf16[1024,1024]{1,0:T(8,128)(2,1)}, bf16[1024,1024]{1,0:T(8,128)(2,1)}, f32[1,1024]{1,0:T(1,128)S(1)}) custom-call(bf16[512,2048]{1,0:T(8,128)(2,1)} %copy-done.52, bf16[512,2048]{1,0:T(8,128)(2,1)} %pad_maximum_fusion.5.refs_1_, ...), custom_call_target="tpu_custom_call" | custom-call | flops 134217728 | bytes 393216 | tf_op jit(solution)/shard_map/pallas_call | solution.py:206
  308.9 6.8 collective-permute-done.21.refs_0_.refs_4_
  318.5 6.6 shard_map.292
  325.1 6.6 shard_map.293
  333.0 21.2 %shard_map.294 = (bf16[1024,1024]{1,0:T(8,128)(2,1)S(1)}, bf16[1024,1024]{1,0:T(8,128)(2,1)S(1)}, bf16[1024,1024]{1,0:T(8,128)(2,1)}, bf16[1024,1024]{1,0:T(8,128)(2,1)}, f32[1,1024]{1,0:T(1,128)S(1)}) custom-call(bf16[512,2048]{1,0:T(8,128)(2,1)} %collective-permute-done.21.refs_0_.refs_4_, bf16[512,2048]{1,0:T(8,128)(2,1)} %collective-permute-done.22.refs_1_.refs_5_, ...), custom_call_target="tpu_custom_call" | custom-call | flops 134217728 | bytes 393216 | tf_op jit(solution)/shard_map/pallas_call | solution.py:206
  354.3 4.5 convolution_convert_fusion.5
  363.1 3.7 add_convert_fusion.4
  366.8 3.7 add_convert_fusion.3
  370.6 7.8 shard_map.295
  379.7 6.1 collective-permute-done.27.refs_0_
  385.8 25.8 %shard_map.296 = bf16[2048,1024]{1,0:T(8,128)(2,1)} custom-call(bf16[512,2048]{1,0:T(8,128)(2,1)} %copy-done.52, bf16[512,2048]{1,0:T(8,128)(2,1)} %pad_maximum_fusion.5.refs_1_, bf16[512,2048]{1,0:T(8,128)(2,1)} %collective-permute-done.19.refs_2_, bf16[512,2048]{1,0:T(8,128)(2,1)} %collective-permute-done.20.refs_3_, ...), custom_call_target="tpu_custom_call" | custom-call | flops 17179869184 | bytes 29360128 | tf_op jit(solution)/shard_map/pallas_call | solution.py:280
  411.7 8.7 %shard_map.297 = (bf16[512,2048]{1,0:T(8,128)(2,1)S(1)}, bf16[512,2048]{1,0:T(8,128)(2,1)S(1)}) custom-call(bf16[1024,1024]{1,0:T(8,128)(2,1)} %get-tuple-element.225.refs_8_.refs_9_.values_ref, bf16[2048,1024]{1,0:T(8,128)(2,1)} %bitcast.147, bf16[1024,2048]{1,0:T(8,128)(2,1)} %copy-done.54), custom_call_target="tpu_custom_call" | custom-call | flops 67108864 | bytes 163840 | tf_op jit(solution)/shard_map/pallas_call | solution.py:354
  420.4 6.3 collective-permute-done.28
  433.4 6.0 convolution_convert_fusion.3
  439.4 3.7 convolution_convert_fusion.2
  443.6 26.2 %shard_map.298 = bf16[1024,2048]{1,0:T(8,128)(2,1)} custom-call(bf16[1024,1024]{1,0:T(8,128)(2,1)} %copy-done.11, bf16[1024,1024]{1,0:T(8,128)(2,1)} %copy-done.11, bf16[1024,1024]{1,0:T(8,128)(2,1)} %copy-done.12, bf16[1024,1024]{1,0:T(8,128)(2,1)} %copy-done.12, bf16[1024,1024]{1,0:T(8,128)(2,1)} %copy-done.26, bf16[1024,1024]{1,0:T(8,128)(2,1)} %copy-done.26, ...), custom_call_target="tpu_custom_call" | custom-call | flops 17179869184 | bytes 29360128 | tf_op jit(solution)/shard_map/pallas_call | solution.py:280
  477.4 4.0 add_convert_fusion.2
  493.5 9.9 %convolution_convert_fusion.6.grad_ref = bf16[512,2048]{1,0:T(8,128)(2,1)} fusion(bf16[512,2048]{1,0:T(8,128)(2,1)S(1)} %convert_element_type.426.weight_ref, bf16[2048,2048]{1,0:T(8,128)(2,1)} %all-gather.9.cloned.1.call-done), kind=kOutput, calls=%fused_computation.52 | convolution fusion | flops 4296015872 | bytes 12582912 | tf_op jit(solution)/shard_map/dot_general | solution.py:25
  503.4 30.5 %shard_map.299 = (bf16[512,2048]{1,0:T(8,128)(2,1)S(1)}, bf16[2,1024,256]{2,1,0:T(8,128)(2,1)S(1)}) custom-call(s32[1]{0:T(128)} %bitcast.1.pos_ref, s32[2,8]{1,0:T(2,128)S(1)} %copy-done.25, bf16[512,2048]{1,0:T(8,128)(2,1)} %copy-done.5, bf16[2,1024,256]{2,1,0:T(8,128)(2,1)S(1)} %copy-done.4, f32[512,128]{1,0:T(8,128)S(1)} %get-tuple-element.212.norm_ref, ...), custom_call_target="tpu_custom_call" | custom-call | flops 167772160 | bytes 163840 | tf_op jit(solution)/shard_map/pallas_call | solution.py:152
  534.0 4.3 convolution_convert_fusion.1
  541.2 7.7 shard_map.300
  551.4 11.3 %collective-permute-start.38 = (bf16[2,256,256]{2,1,0:T(8,128)(2,1)S(1)}, bf16[2,256,256]{2,1,0:T(8,128)(2,1)S(1)}, u32[]{:S(2)}, u32[]{:S(2)}) collective-permute-start(bf16[2,256,256]{2,1,0:T(8,128)(2,1)S(1)} %get-tuple-element.324), channel_id=1, source_target_pairs={{0,1},{1,2},{2,3},{3,0},{4,5},{5,6},{6,7},{7,4},{8,9},{9,10},{10,1... | collective-permute-start | bytes 786440 | tf_op jit(solution)/shard_map/ppermute | solution.py:394
  562.7 3.1 collective-permute-start.39
  565.7 2.9 collective-permute-start.40
  568.7 5.4 shard_map.301
  577.0 8.3 %shard_map.302 = (bf16[512,2048]{1,0:T(8,128)(2,1)S(1)}, bf16[512,2048]{1,0:T(8,128)(2,1)S(1)}) custom-call(bf16[1024,1024]{1,0:T(8,128)(2,1)} %copy-done.11, bf16[1024,2048]{1,0:T(8,128)(2,1)} %copy-done.37, bf16[1024,2048]{1,0:T(8,128)(2,1)} %collective-permute-done.37.refs_0_), custom_call_target="tpu_custom_call" | custom-call | flops 67108864 | bytes 163840 | tf_op jit(solution)/shard_map/pallas_call | solution.py:354
  585.3 2.8 convert_add_fusion.2
  588.1 4.4 convert_add_fusion.1
  592.7 4.5 shard_map.303
  597.2 4.4 all-to-all-start.1
  606.3 2.7 slice.401
  613.3 2.7 slice.402
  621.5 8.8 %shard_map.304 = f32[512,2048]{1,0:T(8,128)} custom-call(bf16[512,2048]{1,0:T(8,128)(2,1)S(1)} %copy-done.2, bf16[2048,2048]{1,0:T(8,128)(2,1)} %bitcast.153), custom_call_target="tpu_custom_call" | custom-call | flops 67108864 | bytes 196608 | tf_op jit(solution)/shard_map/pallas_call | solution.py:354
  630.5 8.5 %collective-permute-done.45 = bf16[256,2048]{1,0:T(8,128)(2,1)} collective-permute-done((bf16[256,2048]{1,0:T(8,128)(2,1)}, bf16[256,2048]{1,0:T(8,128)(2,1)}, u32[]{:S(2)}, u32[]{:S(2)}) %collective-permute-start.45) | collective-permute-done | bytes 1048608 | tf_op jit(solution)/shard_map/ppermute | solution.py:449
  646.5 14.4 %collective-permute-done.42 = bf16[256,2048]{1,0:T(8,128)(2,1)S(1)} collective-permute-done((bf16[256,2048]{1,0:T(8,128)(2,1)S(1)}, bf16[256,2048]{1,0:T(8,128)(2,1)S(1)}, u32[]{:S(2)}, u32[]{:S(2)}) %collective-permute-start.42) | collective-permute-done | bytes 1048608 | tf_op jit(solution)/shard_map/ppermute | solution.py:449
  660.9 2.9 collective-permute-done.43
  663.8 5.4 shard_map.305
  672.4 5.6 fusion.18
  689.8 2.7 fusion.17
  693.4 26.7 %collective-permute-done.47 = bf16[128,2048]{1,0:T(8,128)(2,1)S(1)} collective-permute-done((bf16[128,2048]{1,0:T(8,128)(2,1)S(1)}, bf16[128,2048]{1,0:T(8,128)(2,1)S(1)}, u32[]{:S(2)}, u32[]{:S(2)}) %collective-permute-start.47) | collective-permute-done | bytes 524320 | tf_op jit(solution)/shard_map/ppermute | solution.py:449
  722.6 3.8 collective-permute-done.55
  738.6 5.6 collective-permute-done.52
  751.5 6.2 add_convert_fusion
  761.9 29.0 %reduce-scatter.8.cloned.1.call-done = bf16[128,2048]{1,0:T(8,128)(2,1)} async-done(((bf16[512,2048]{1,0:T(8,128)(2,1)}), bf16[128,2048]{1,0:T(8,128)(2,1)}) %reduce-scatter.8.cloned.1.call-update) | async-done | bytes 524304 | tf_op jit(solution)/shard_map/reduce_scatter | solution.py:737
  (477 shorter events, 189.0 us)
Async XLA Ops:
  7.2 52.1 %all-gather.5.cloned.1.call-start = ((), (), s32[]{:S(2)}) async-start(), calls=%async_computation.5 | async-start | bytes 1638400 | tf_op jit(solution)/shard_map/all_gather | solution.py:528
  20.3 27.0 %collective-permute-start = (bf16[256,2048]{1,0:T(8,128)(2,1)S(1)}, bf16[256,2048]{1,0:T(8,128)(2,1)}, u32[]{:S(2)}, u32[]{:S(2)}) collective-permute-start(bf16[256,2048]{1,0:T(8,128)(2,1)S(1)} %get-tuple-element.314), channel_id=1, source_target_pairs={{0,8},{4,12},{8,0},{12,4},{16,24},{20,28},{24,16},{28,20},{1,9},{5... | collective-permute-start | bytes 3145736 | tf_op jit(solution)/shard_map/ppermute | solution.py:449
  23.2 26.7 %collective-permute-start.1 = (bf16[256,2048]{1,0:T(8,128)(2,1)}, bf16[256,2048]{1,0:T(8,128)(2,1)}, u32[]{:S(2)}, u32[]{:S(2)}) collective-permute-start(bf16[256,2048]{1,0:T(8,128)(2,1)} %get-tuple-element.313), channel_id=1, source_target_pairs={{0,16},{4,20},{8,24},{12,28},{16,0},{20,4},{24,8},{28,12},{1,17},{... | collective-permute-start | bytes 3145736 | tf_op jit(solution)/shard_map/ppermute | solution.py:449
  25.8 33.5 %all-to-all-start = ((bf16[64,8,1024]{2,0,1:T(8,128)(2,1)}), bf16[64,8,1024]{2,0,1:T(8,128)(2,1)S(1)}, u32[]{:S(2)}, u32[]{:S(2)}) async-start(bf16[64,8,1024]{2,0,1:T(8,128)(2,1)} %bitcast.140), calls=%async_computation | async-start | bytes 2097152 | tf_op jit(solution)/shard_map/all_to_all | solution.py:530
  29.4 93.7 %all-gather.7.cloned.1.call-start = ((), (), s32[]{:S(2)}) async-start(), calls=%async_computation.6 | async-start | bytes 11796480 | tf_op jit(solution)/shard_map/all_gather | solution.py:533
  59.3 162.1 %all-gather.9.cloned.1.call-start = ((), (), s32[]{:S(2)}) async-start(), calls=%async_computation.7 | async-start | bytes 9437184 | tf_op jit(solution)/shard_map/all_gather | solution.py:546
  59.4 52.2 %collective-permute-start.6 = (bf16[512,2048]{1,0:T(8,128)(2,1)S(1)}, bf16[512,2048]{1,0:T(8,128)(2,1)}, u32[]{:S(2)}, u32[]{:S(2)}) collective-permute-start(bf16[512,2048]{1,0:T(8,128)(2,1)S(1)} %pad_maximum_fusion.2.refs_0_.refs_8_), channel_id=1, source_target_pairs={{0,4},{4,0},{8,12},{12,8},{16,20},{20,16},{24,28},{28,24},{1,5},{5... | collective-permute-start | bytes 6291464 | tf_op jit(solution)/shard_map/ppermute | solution.py:449
  59.4 52.1 %collective-permute-start.7 = (bf16[512,2048]{1,0:T(8,128)(2,1)}, bf16[512,2048]{1,0:T(8,128)(2,1)}, u32[]{:S(2)}, u32[]{:S(2)}) collective-permute-start(bf16[512,2048]{1,0:T(8,128)(2,1)} %pad_maximum_fusion.3.refs_1_.refs_9_), channel_id=1, source_target_pairs={{0,4},{4,0},{8,12},{12,8},{16,20},{20,16},{24,28},{28,24},{1,5},{5... | collective-permute-start | bytes 6291464 | tf_op jit(solution)/shard_map/ppermute | solution.py:449
  59.9 11.2 %collective-permute-start.2 = (bf16[64,2048]{1,0:T(8,128)(2,1)S(1)}, bf16[64,2048]{1,0:T(8,128)(2,1)}, u32[]{:S(2)}, u32[]{:S(2)}) collective-permute-start(bf16[64,2048]{1,0:T(8,128)(2,1)S(1)} %copy-done.73), channel_id=1, source_target_pairs={{0,1},{1,2},{2,3},{3,0},{4,5},{5,6},{6,7},{7,4},{8,9},{9,10},{10,1... | collective-permute-start | bytes 786440 | tf_op jit(solution)/shard_map/ppermute | solution.py:394
  61.5 20.0 %collective-permute-start.3 = (bf16[64,2048]{1,0:T(8,128)(2,1)S(1)}, bf16[64,2048]{1,0:T(8,128)(2,1)}, u32[]{:S(2)}, u32[]{:S(2)}) collective-permute-start(bf16[64,2048]{1,0:T(8,128)(2,1)S(1)} %copy-done.73), channel_id=1, source_target_pairs={{0,2},{1,3},{2,0},{3,1},{4,6},{5,7},{6,4},{7,5},{8,10},{9,11},{10,... | collective-permute-start | bytes 786440 | tf_op jit(solution)/shard_map/ppermute | solution.py:394
  64.1 17.5 %collective-permute-start.4 = (bf16[64,2048]{1,0:T(8,128)(2,1)S(1)}, bf16[64,2048]{1,0:T(8,128)(2,1)}, u32[]{:S(2)}, u32[]{:S(2)}) collective-permute-start(bf16[64,2048]{1,0:T(8,128)(2,1)S(1)} %copy-done.73), channel_id=1, source_target_pairs={{0,3},{1,0},{2,1},{3,2},{4,7},{5,4},{6,5},{7,6},{8,11},{9,8},{10,9... | collective-permute-start | bytes 786440 | tf_op jit(solution)/shard_map/ppermute | solution.py:394
  81.6 30.0 %collective-permute-start.5 = (bf16[256,2048]{1,0:T(8,128)(2,1)}, bf16[256,2048]{1,0:T(8,128)(2,1)}, u32[]{:S(2)}, u32[]{:S(2)}) collective-permute-start(bf16[256,2048]{1,0:T(8,128)(2,1)} %param.29), channel_id=1, source_target_pairs={{0,1},{1,2},{2,3},{3,0},{4,5},{5,6},{6,7},{7,4},{8,9},{9,10},{10,1... | collective-permute-start | bytes 3145736 | tf_op jit(solution)/shard_map/ppermute | solution.py:394
  123.1 162.7 %all-gather.11.cloned.1.call-start = ((), (), s32[]{:S(2)}) async-start(), calls=%async_computation.8 | async-start | bytes 5242880 | tf_op jit(solution)/shard_map/all_gather | solution.py:577
  130.8 27.5 %collective-permute-start.8 = (bf16[256,2048]{1,0:T(8,128)(2,1)}, bf16[256,2048]{1,0:T(8,128)(2,1)}, u32[]{:S(2)}, u32[]{:S(2)}) collective-permute-start(bf16[256,2048]{1,0:T(8,128)(2,1)} %collective-permute-done.5), channel_id=1, source_target_pairs={{0,1},{1,2},{2,3},{3,0},{4,5},{5,6},{6,7},{7,4},{8,9},{9,10},{10,1... | collective-permute-start | bytes 3145736 | tf_op jit(solution)/shard_map/ppermute | solution.py:394
  158.3 12.0 %collective-permute-start.9 = (bf16[2,256,256]{2,1,0:T(8,128)(2,1)S(1)}, bf16[2,256,256]{2,1,0:T(8,128)(2,1)S(1)}, u32[]{:S(2)}, u32[]{:S(2)}) collective-permute-start(bf16[2,256,256]{2,1,0:T(8,128)(2,1)S(1)} %bitcast.180), channel_id=1, source_target_pairs={{0,1},{1,2},{2,3},{3,0},{4,5},{5,6},{6,7},{7,4},{8,9},{9,10},{10,1... | collective-permute-start | bytes 786440 | tf_op jit(solution)/shard_map/ppermute | solution.py:394
  158.3 20.9 %collective-permute-start.10 = (bf16[2,256,256]{2,1,0:T(8,128)(2,1)S(1)}, bf16[2,256,256]{2,1,0:T(8,128)(2,1)S(1)}, u32[]{:S(2)}, u32[]{:S(2)}) collective-permute-start(bf16[2,256,256]{2,1,0:T(8,128)(2,1)S(1)} %bitcast.181), channel_id=1, source_target_pairs={{0,2},{1,3},{2,0},{3,1},{4,6},{5,7},{6,4},{7,5},{8,10},{9,11},{10,... | collective-permute-start | bytes 786440 | tf_op jit(solution)/shard_map/ppermute | solution.py:394
  160.4 18.8 %collective-permute-start.11 = (bf16[2,256,256]{2,1,0:T(8,128)(2,1)S(1)}, bf16[2,256,256]{2,1,0:T(8,128)(2,1)S(1)}, u32[]{:S(2)}, u32[]{:S(2)}) collective-permute-start(bf16[2,256,256]{2,1,0:T(8,128)(2,1)S(1)} %bitcast.182), channel_id=1, source_target_pairs={{0,3},{1,0},{2,1},{3,2},{4,7},{5,4},{6,5},{7,6},{8,11},{9,8},{10,9... | collective-permute-start | bytes 786440 | tf_op jit(solution)/shard_map/ppermute | solution.py:394
  179.2 42.2 %collective-permute-start.12 = (bf16[256,2048]{1,0:T(8,128)(2,1)}, bf16[256,2048]{1,0:T(8,128)(2,1)}, u32[]{:S(2)}, u32[]{:S(2)}) collective-permute-start(bf16[256,2048]{1,0:T(8,128)(2,1)} %collective-permute-done.8), channel_id=1, source_target_pairs={{0,1},{1,2},{2,3},{3,0},{4,5},{5,6},{6,7},{7,4},{8,9},{9,10},{10,1... | collective-permute-start | bytes 3145736 | tf_op jit(solution)/shard_map/ppermute | solution.py:394
  184.6 48.1 %collective-permute-start.13 = (bf16[512,2048]{1,0:T(8,128)(2,1)}, bf16[512,2048]{1,0:T(8,128)(2,1)}, u32[]{:S(2)}, u32[]{:S(2)}) collective-permute-start(bf16[512,2048]{1,0:T(8,128)(2,1)} %copy-done.7), channel_id=1, source_target_pairs={{0,16},{4,20},{8,24},{12,28},{16,0},{20,4},{24,8},{28,12},{1,17},{... | collective-permute-start | bytes 6291464 | tf_op jit(solution)/shard_map/ppermute | solution.py:449
  185.6 47.1 %collective-permute-start.14 = (bf16[512,2048]{1,0:T(8,128)(2,1)}, bf16[512,2048]{1,0:T(8,128)(2,1)}, u32[]{:S(2)}, u32[]{:S(2)}) collective-permute-start(bf16[512,2048]{1,0:T(8,128)(2,1)} %pad_maximum_fusion.3.refs_1_.refs_9_), channel_id=1, source_target_pairs={{0,8},{4,12},{8,0},{12,4},{16,24},{20,28},{24,16},{28,20},{1,9},{5... | collective-permute-start | bytes 6291464 | tf_op jit(solution)/shard_map/ppermute | solution.py:449
  186.7 353.0 %reduce-scatter.4.cloned.1.call-start = ((), (), s32[]{:S(2)}) async-start(), calls=%async_computation.9 | async-start | bytes 5242880 | tf_op jit(solution)/shard_map/reduce_scatter | solution.py:631
  232.7 36.9 %collective-permute-start.15 = (bf16[512,2048]{1,0:T(8,128)(2,1)}, bf16[512,2048]{1,0:T(8,128)(2,1)}, u32[]{:S(2)}, u32[]{:S(2)}) collective-permute-start(bf16[512,2048]{1,0:T(8,128)(2,1)} %collective-permute-done.13.refs_0_.refs_12_), channel_id=1, source_target_pairs={{0,4},{4,0},{8,12},{12,8},{16,20},{20,16},{24,28},{28,24},{1,5},{5... | collective-permute-start | bytes 6291464 | tf_op jit(solution)/shard_map/ppermute | solution.py:449
  233.0 32.6 %collective-permute-start.17 = (bf16[256,2048]{1,0:T(8,128)(2,1)S(1)}, bf16[256,2048]{1,0:T(8,128)(2,1)S(1)}, u32[]{:S(2)}, u32[]{:S(2)}) collective-permute-start(bf16[256,2048]{1,0:T(8,128)(2,1)S(1)} %get-tuple-element.312), channel_id=1, source_target_pairs={{0,8},{4,12},{8,0},{12,4},{16,24},{20,28},{24,16},{28,20},{1,9},{5... | collective-permute-start | bytes 3145736 | tf_op jit(solution)/shard_map/ppermute | solution.py:449
  234.3 36.9 %collective-permute-start.16 = (bf16[512,2048]{1,0:T(8,128)(2,1)}, bf16[512,2048]{1,0:T(8,128)(2,1)}, u32[]{:S(2)}, u32[]{:S(2)}) collective-permute-start(bf16[512,2048]{1,0:T(8,128)(2,1)} %collective-permute-done.14.refs_1_.refs_13_), channel_id=1, source_target_pairs={{0,4},{4,0},{8,12},{12,8},{16,20},{20,16},{24,28},{28,24},{1,5},{5... | collective-permute-start | bytes 6291464 | tf_op jit(solution)/shard_map/ppermute | solution.py:449
  234.5 31.3 %collective-permute-start.18 = (bf16[256,2048]{1,0:T(8,128)(2,1)S(1)}, bf16[256,2048]{1,0:T(8,128)(2,1)S(1)}, u32[]{:S(2)}, u32[]{:S(2)}) collective-permute-start(bf16[256,2048]{1,0:T(8,128)(2,1)S(1)} %get-tuple-element.311), channel_id=1, source_target_pairs={{0,16},{4,20},{8,24},{12,28},{16,0},{20,4},{24,8},{28,12},{1,17},{... | collective-permute-start | bytes 3145736 | tf_op jit(solution)/shard_map/ppermute | solution.py:449
  267.5 18.3 %collective-permute-start.19 = (bf16[512,2048]{1,0:T(8,128)(2,1)S(1)}, bf16[512,2048]{1,0:T(8,128)(2,1)}, u32[]{:S(2)}, u32[]{:S(2)}) collective-permute-start(bf16[512,2048]{1,0:T(8,128)(2,1)S(1)} %pad_maximum_fusion.4.refs_0_), channel_id=1, source_target_pairs={{0,4},{4,0},{8,12},{12,8},{16,20},{20,16},{24,28},{28,24},{1,5},{5... | collective-permute-start | bytes 6291464 | tf_op jit(solution)/shard_map/ppermute | solution.py:449
  267.5 18.3 %collective-permute-start.20 = (bf16[512,2048]{1,0:T(8,128)(2,1)}, bf16[512,2048]{1,0:T(8,128)(2,1)}, u32[]{:S(2)}, u32[]{:S(2)}) collective-permute-start(bf16[512,2048]{1,0:T(8,128)(2,1)} %pad_maximum_fusion.5.refs_1_), channel_id=1, source_target_pairs={{0,4},{4,0},{8,12},{12,8},{16,20},{20,16},{24,28},{28,24},{1,5},{5... | collective-permute-start | bytes 6291464 | tf_op jit(solution)/shard_map/ppermute | solution.py:449
  268.0 47.6 %collective-permute-start.21 = (bf16[512,2048]{1,0:T(8,128)(2,1)S(1)}, bf16[512,2048]{1,0:T(8,128)(2,1)}, u32[]{:S(2)}, u32[]{:S(2)}) collective-permute-start(bf16[512,2048]{1,0:T(8,128)(2,1)S(1)} %pad_maximum_fusion.4.refs_0_), channel_id=1, source_target_pairs={{0,16},{4,20},{8,24},{12,28},{16,0},{20,4},{24,8},{28,12},{1,17},{... | collective-permute-start | bytes 6291464 | tf_op jit(solution)/shard_map/ppermute | solution.py:449
  269.6 47.6 %collective-permute-start.22 = (bf16[512,2048]{1,0:T(8,128)(2,1)}, bf16[512,2048]{1,0:T(8,128)(2,1)}, u32[]{:S(2)}, u32[]{:S(2)}) collective-permute-start(bf16[512,2048]{1,0:T(8,128)(2,1)} %pad_maximum_fusion.5.refs_1_), channel_id=1, source_target_pairs={{0,8},{4,12},{8,0},{12,4},{16,24},{20,28},{24,16},{28,20},{1,9},{5... | collective-permute-start | bytes 6291464 | tf_op jit(solution)/shard_map/ppermute | solution.py:449
  317.2 14.5 %collective-permute-start.23 = (bf16[512,2048]{1,0:T(8,128)(2,1)}, bf16[512,2048]{1,0:T(8,128)(2,1)S(1)}, u32[]{:S(2)}, u32[]{:S(2)}) collective-permute-start(bf16[512,2048]{1,0:T(8,128)(2,1)} %collective-permute-done.21.refs_0_.refs_4_), channel_id=1, source_target_pairs={{0,4},{4,0},{8,12},{12,8},{16,20},{20,16},{24,28},{28,24},{1,5},{5... | collective-permute-start | bytes 6291464 | tf_op jit(solution)/shard_map/ppermute | solution.py:449
  317.2 15.8 %collective-permute-start.24 = (bf16[512,2048]{1,0:T(8,128)(2,1)}, bf16[512,2048]{1,0:T(8,128)(2,1)}, u32[]{:S(2)}, u32[]{:S(2)}) collective-permute-start(bf16[512,2048]{1,0:T(8,128)(2,1)} %collective-permute-done.22.refs_1_.refs_5_), channel_id=1, source_target_pairs={{0,4},{4,0},{8,12},{12,8},{16,20},{20,16},{24,28},{28,24},{1,5},{5... | collective-permute-start | bytes 6291464 | tf_op jit(solution)/shard_map/ppermute | solution.py:449
  378.6 48.1 %collective-permute-start.28 = (bf16[512,2048]{1,0:T(8,128)(2,1)}, bf16[512,2048]{1,0:T(8,128)(2,1)S(1)}, u32[]{:S(2)}, u32[]{:S(2)}) collective-permute-start(bf16[512,2048]{1,0:T(8,128)(2,1)} %add_convert_fusion.4), channel_id=1, source_target_pairs={{0,16},{4,20},{8,24},{12,28},{16,0},{20,4},{24,8},{28,12},{1,17},{... | collective-permute-start | bytes 6291464 | tf_op jit(solution)/shard_map/ppermute | solution.py:449
  379.0 47.8 %collective-permute-start.29 = (bf16[512,2048]{1,0:T(8,128)(2,1)}, bf16[512,2048]{1,0:T(8,128)(2,1)S(1)}, u32[]{:S(2)}, u32[]{:S(2)}) collective-permute-start(bf16[512,2048]{1,0:T(8,128)(2,1)} %add_convert_fusion.3), channel_id=1, source_target_pairs={{0,8},{4,12},{8,0},{12,4},{16,24},{20,28},{24,16},{28,20},{1,9},{5... | collective-permute-start | bytes 6291464 | tf_op jit(solution)/shard_map/ppermute | solution.py:449
  429.9 40.0 %collective-permute-start.31 = (bf16[256,2048]{1,0:T(8,128)(2,1)}, bf16[256,2048]{1,0:T(8,128)(2,1)}, u32[]{:S(2)}, u32[]{:S(2)}) collective-permute-start(bf16[256,2048]{1,0:T(8,128)(2,1)} %slice.403), channel_id=1, source_target_pairs={{0,16},{4,20},{8,24},{12,28},{16,0},{20,4},{24,8},{28,12},{1,17},{... | collective-permute-start | bytes 3145736 | tf_op jit(solution)/shard_map/ppermute | solution.py:449
  432.6 39.6 %collective-permute-start.30 = (bf16[256,2048]{1,0:T(8,128)(2,1)}, bf16[256,2048]{1,0:T(8,128)(2,1)}, u32[]{:S(2)}, u32[]{:S(2)}) collective-permute-start(bf16[256,2048]{1,0:T(8,128)(2,1)} %slice.404), channel_id=1, source_target_pairs={{0,8},{4,12},{8,0},{12,4},{16,24},{20,28},{24,16},{28,20},{1,9},{5... | collective-permute-start | bytes 3145736 | tf_op jit(solution)/shard_map/ppermute | solution.py:449
  439.4 35.7 %collective-permute-start.32 = (bf16[512,2048]{1,0:T(8,128)(2,1)}, bf16[512,2048]{1,0:T(8,128)(2,1)}, u32[]{:S(2)}, u32[]{:S(2)}) collective-permute-start(bf16[512,2048]{1,0:T(8,128)(2,1)} %convolution_convert_fusion.3), channel_id=1, source_target_pairs={{0,4},{4,0},{8,12},{12,8},{16,20},{20,16},{24,28},{28,24},{1,5},{5... | collective-permute-start | bytes 6291464 | tf_op jit(solution)/shard_map/ppermute | solution.py:449
  443.1 38.3 %collective-permute-start.33 = (bf16[512,2048]{1,0:T(8,128)(2,1)}, bf16[512,2048]{1,0:T(8,128)(2,1)S(1)}, u32[]{:S(2)}, u32[]{:S(2)}) collective-permute-start(bf16[512,2048]{1,0:T(8,128)(2,1)} %convolution_convert_fusion.2), channel_id=1, source_target_pairs={{0,4},{4,0},{8,12},{12,8},{16,20},{20,16},{24,28},{28,24},{1,5},{5... | collective-permute-start | bytes 6291464 | tf_op jit(solution)/shard_map/ppermute | solution.py:449
  483.8 54.5 %collective-permute-start.34 = (bf16[512,2048]{1,0:T(8,128)(2,1)S(1)}, bf16[512,2048]{1,0:T(8,128)(2,1)S(1)}, u32[]{:S(2)}, u32[]{:S(2)}) collective-permute-start(bf16[512,2048]{1,0:T(8,128)(2,1)S(1)} %add_convert_fusion.2), channel_id=1, source_target_pairs={{0,16},{4,20},{8,24},{12,28},{16,0},{20,4},{24,8},{28,12},{1,17},{... | collective-permute-start | bytes 6291464 | tf_op jit(solution)/shard_map/ppermute | solution.py:449
  485.3 54.3 %collective-permute-start.35 = (bf16[512,2048]{1,0:T(8,128)(2,1)S(1)}, bf16[512,2048]{1,0:T(8,128)(2,1)}, u32[]{:S(2)}, u32[]{:S(2)}) collective-permute-start(bf16[512,2048]{1,0:T(8,128)(2,1)S(1)} %add_convert_fusion.1), channel_id=1, source_target_pairs={{0,8},{4,12},{8,0},{12,4},{16,24},{20,28},{24,16},{28,20},{1,9},{5... | collective-permute-start | bytes 6291464 | tf_op jit(solution)/shard_map/ppermute | solution.py:449
  539.6 29.0 %collective-permute-start.36 = (bf16[1024,2048]{1,0:T(8,128)(2,1)}, bf16[1024,2048]{1,0:T(8,128)(2,1)}, u32[]{:S(2)}, u32[]{:S(2)}) collective-permute-start(bf16[1024,2048]{1,0:T(8,128)(2,1)} %convolution_convert_fusion.1), channel_id=1, source_target_pairs={{0,4},{4,0},{8,12},{12,8},{16,20},{20,16},{24,28},{28,24},{1,5},{5... | collective-permute-start | bytes 12582920 | tf_op jit(solution)/shard_map/ppermute | solution.py:449
  548.9 28.1 %collective-permute-start.37 = (bf16[1024,2048]{1,0:T(8,128)(2,1)}, bf16[1024,2048]{1,0:T(8,128)(2,1)}, u32[]{:S(2)}, u32[]{:S(2)}) collective-permute-start(bf16[1024,2048]{1,0:T(8,128)(2,1)} %shard_map.300), channel_id=1, source_target_pairs={{0,4},{4,0},{8,12},{12,8},{16,20},{20,16},{24,28},{28,24},{1,5},{5... | collective-permute-start | bytes 12582920 | tf_op jit(solution)/shard_map/ppermute | solution.py:449
  551.4 41.2 %collective-permute-start.38 = (bf16[2,256,256]{2,1,0:T(8,128)(2,1)S(1)}, bf16[2,256,256]{2,1,0:T(8,128)(2,1)S(1)}, u32[]{:S(2)}, u32[]{:S(2)}) collective-permute-start(bf16[2,256,256]{2,1,0:T(8,128)(2,1)S(1)} %get-tuple-element.324), channel_id=1, source_target_pairs={{0,1},{1,2},{2,3},{3,0},{4,5},{5,6},{6,7},{7,4},{8,9},{9,10},{10,1... | collective-permute-start | bytes 786440 | tf_op jit(solution)/shard_map/ppermute | solution.py:394
  562.7 29.9 %collective-permute-start.39 = (bf16[2,256,256]{2,1,0:T(8,128)(2,1)S(1)}, bf16[2,256,256]{2,1,0:T(8,128)(2,1)S(1)}, u32[]{:S(2)}, u32[]{:S(2)}) collective-permute-start(bf16[2,256,256]{2,1,0:T(8,128)(2,1)S(1)} %get-tuple-element.323), channel_id=1, source_target_pairs={{0,2},{1,3},{2,0},{3,1},{4,6},{5,7},{6,4},{7,5},{8,10},{9,11},{10,... | collective-permute-start | bytes 786440 | tf_op jit(solution)/shard_map/ppermute | solution.py:394
  565.7 26.9 %collective-permute-start.40 = (bf16[2,256,256]{2,1,0:T(8,128)(2,1)S(1)}, bf16[2,256,256]{2,1,0:T(8,128)(2,1)S(1)}, u32[]{:S(2)}, u32[]{:S(2)}) collective-permute-start(bf16[2,256,256]{2,1,0:T(8,128)(2,1)S(1)} %get-tuple-element.322), channel_id=1, source_target_pairs={{0,3},{1,0},{2,1},{3,2},{4,7},{5,4},{6,5},{7,6},{8,11},{9,8},{10,9... | collective-permute-start | bytes 786440 | tf_op jit(solution)/shard_map/ppermute | solution.py:394
  597.1 66.6 %collective-permute-start.41 = (bf16[1024,2048]{1,0:T(8,128)(2,1)}, bf16[1024,2048]{1,0:T(8,128)(2,1)}, u32[]{:S(2)}, u32[]{:S(2)}) collective-permute-start(bf16[1024,2048]{1,0:T(8,128)(2,1)} %shard_map.303), channel_id=1, source_target_pairs={{0,4},{4,0},{8,12},{12,8},{16,20},{20,16},{24,28},{28,24},{1,5},{5... | collective-permute-start | bytes 12582920 | tf_op jit(solution)/shard_map/ppermute | solution.py:449
  597.2 20.3 %all-to-all-start.1 = ((bf16[8,64,1024]{2,1,0:T(8,128)(2,1)}), bf16[8,64,1024]{2,1,0:T(8,128)(2,1)}, u32[]{:S(2)}, u32[]{:S(2)}) async-start(bf16[8,64,1024]{2,1,0:T(8,128)(2,1)} %reduce-scatter.4.cloned.1.call-done), calls=%async_computation.4 | async-start | bytes 2097152 | tf_op jit(solution)/shard_map/all_to_all | solution.py:751
  601.6 129.5 %reduce-scatter.6.cloned.1.call-start = ((), (), s32[]{:S(2)}) async-start(), calls=%async_computation.10 | async-start | bytes 5242880 | tf_op jit(solution)/shard_map/reduce_scatter | solution.py:638
  604.1 186.8 %reduce-scatter.8.cloned.1.call-start = ((), (), s32[]{:S(2)}) async-start(), calls=%async_computation.11 | async-start | bytes 2621440 | tf_op jit(solution)/shard_map/reduce_scatter | solution.py:737
  609.0 30.0 %collective-permute-start.45 = (bf16[256,2048]{1,0:T(8,128)(2,1)}, bf16[256,2048]{1,0:T(8,128)(2,1)}, u32[]{:S(2)}, u32[]{:S(2)}) collective-permute-start(bf16[256,2048]{1,0:T(8,128)(2,1)} %slice.401), channel_id=1, source_target_pairs={{0,16},{4,20},{8,24},{12,28},{16,0},{20,4},{24,8},{28,12},{1,17},{... | collective-permute-start | bytes 3145736 | tf_op jit(solution)/shard_map/ppermute | solution.py:449
  616.0 26.4 %collective-permute-start.44 = (bf16[256,2048]{1,0:T(8,128)(2,1)}, bf16[256,2048]{1,0:T(8,128)(2,1)}, u32[]{:S(2)}, u32[]{:S(2)}) collective-permute-start(bf16[256,2048]{1,0:T(8,128)(2,1)} %slice.402), channel_id=1, source_target_pairs={{0,8},{4,12},{8,0},{12,4},{16,24},{20,28},{24,16},{28,20},{1,9},{5... | collective-permute-start | bytes 3145736 | tf_op jit(solution)/shard_map/ppermute | solution.py:449
  620.8 40.2 %collective-permute-start.42 = (bf16[256,2048]{1,0:T(8,128)(2,1)S(1)}, bf16[256,2048]{1,0:T(8,128)(2,1)S(1)}, u32[]{:S(2)}, u32[]{:S(2)}) collective-permute-start(bf16[256,2048]{1,0:T(8,128)(2,1)S(1)} %copy-done.32), channel_id=1, source_target_pairs={{0,16},{4,20},{8,24},{12,28},{16,0},{20,4},{24,8},{28,12},{1,17},{... | collective-permute-start | bytes 3145736 | tf_op jit(solution)/shard_map/ppermute | solution.py:449
  621.3 42.5 %collective-permute-start.43 = (bf16[256,2048]{1,0:T(8,128)(2,1)S(1)}, bf16[256,2048]{1,0:T(8,128)(2,1)}, u32[]{:S(2)}, u32[]{:S(2)}) collective-permute-start(bf16[256,2048]{1,0:T(8,128)(2,1)S(1)} %copy-done.30), channel_id=1, source_target_pairs={{0,8},{4,12},{8,0},{12,4},{16,24},{20,28},{24,16},{28,20},{1,9},{5... | collective-permute-start | bytes 3145736 | tf_op jit(solution)/shard_map/ppermute | solution.py:449
  682.9 37.2 %collective-permute-start.48 = (bf16[1152,256]{1,0:T(8,128)(2,1)S(1)}, bf16[1152,256]{1,0:T(8,128)(2,1)S(1)}, u32[]{:S(2)}, u32[]{:S(2)}) collective-permute-start(bf16[1152,256]{1,0:T(8,128)(2,1)S(1)} %bitcast.177), channel_id=1, source_target_pairs={{0,4},{4,0},{8,12},{12,8},{16,20},{20,16},{24,28},{28,24},{1,5},{5... | collective-permute-start | bytes 1769480 | tf_op jit(solution)/shard_map/ppermute | solution.py:449
  683.0 48.1 %collective-permute-start.49 = (bf16[256,2048]{1,0:T(8,128)(2,1)}, bf16[256,2048]{1,0:T(8,128)(2,1)}, u32[]{:S(2)}, u32[]{:S(2)}) collective-permute-start(bf16[256,2048]{1,0:T(8,128)(2,1)} %copy-done.34), channel_id=1, source_target_pairs={{0,16},{4,20},{8,24},{12,28},{16,0},{20,4},{24,8},{28,12},{1,17},{... | collective-permute-start | bytes 3145736 | tf_op jit(solution)/shard_map/ppermute | solution.py:449
  683.5 47.7 %collective-permute-start.50 = (bf16[256,2048]{1,0:T(8,128)(2,1)}, bf16[256,2048]{1,0:T(8,128)(2,1)}, u32[]{:S(2)}, u32[]{:S(2)}) collective-permute-start(bf16[256,2048]{1,0:T(8,128)(2,1)} %copy-done.33), channel_id=1, source_target_pairs={{0,8},{4,12},{8,0},{12,4},{16,24},{20,28},{24,16},{28,20},{1,9},{5... | collective-permute-start | bytes 3145736 | tf_op jit(solution)/shard_map/ppermute | solution.py:449
  686.9 33.1 %collective-permute-start.47 = (bf16[128,2048]{1,0:T(8,128)(2,1)S(1)}, bf16[128,2048]{1,0:T(8,128)(2,1)S(1)}, u32[]{:S(2)}, u32[]{:S(2)}) collective-permute-start(bf16[128,2048]{1,0:T(8,128)(2,1)S(1)} %slice.407), channel_id=1, source_target_pairs={{0,16},{4,20},{8,24},{12,28},{16,0},{20,4},{24,8},{28,12},{1,17},{... | collective-permute-start | bytes 1572872 | tf_op jit(solution)/shard_map/ppermute | solution.py:449
  688.9 33.6 %collective-permute-start.46 = (bf16[128,2048]{1,0:T(8,128)(2,1)S(1)}, bf16[128,2048]{1,0:T(8,128)(2,1)S(1)}, u32[]{:S(2)}, u32[]{:S(2)}) collective-permute-start(bf16[128,2048]{1,0:T(8,128)(2,1)S(1)} %slice.408), channel_id=1, source_target_pairs={{0,8},{4,12},{8,0},{12,4},{16,24},{20,28},{24,16},{28,20},{1,9},{5... | collective-permute-start | bytes 1572872 | tf_op jit(solution)/shard_map/ppermute | solution.py:449
  727.0 10.2 %collective-permute-start.53 = (bf16[288,256]{1,0:T(8,128)(2,1)}, bf16[288,256]{1,0:T(8,128)(2,1)}, u32[]{:S(2)}, u32[]{:S(2)}) collective-permute-start(bf16[288,256]{1,0:T(8,128)(2,1)} %get-tuple-element.326), channel_id=1, source_target_pairs={{0,16},{4,20},{8,24},{12,28},{16,0},{20,4},{24,8},{28,12},{1,17},{... | collective-permute-start | bytes 442376 | tf_op jit(solution)/shard_map/ppermute | solution.py:449
  732.8 11.3 %collective-permute-start.52 = (bf16[128,2048]{1,0:T(8,128)(2,1)S(1)}, bf16[128,2048]{1,0:T(8,128)(2,1)S(1)}, u32[]{:S(2)}, u32[]{:S(2)}) collective-permute-start(bf16[128,2048]{1,0:T(8,128)(2,1)S(1)} %slice.405), channel_id=1, source_target_pairs={{0,16},{4,20},{8,24},{12,28},{16,0},{20,4},{24,8},{28,12},{1,17},{... | collective-permute-start | bytes 1572872 | tf_op jit(solution)/shard_map/ppermute | solution.py:449
  735.5 11.3 %collective-permute-start.51 = (bf16[128,2048]{1,0:T(8,128)(2,1)S(1)}, bf16[128,2048]{1,0:T(8,128)(2,1)S(1)}, u32[]{:S(2)}, u32[]{:S(2)}) collective-permute-start(bf16[128,2048]{1,0:T(8,128)(2,1)S(1)} %slice.406), channel_id=1, source_target_pairs={{0,8},{4,12},{8,0},{12,4},{16,24},{20,28},{24,16},{28,20},{1,9},{5... | collective-permute-start | bytes 1572872 | tf_op jit(solution)/shard_map/ppermute | solution.py:449
  738.2 10.3 %collective-permute-start.54 = (bf16[144,256]{1,0:T(8,128)(2,1)S(1)}, bf16[144,256]{1,0:T(8,128)(2,1)S(1)}, u32[]{:S(2)}, u32[]{:S(2)}) collective-permute-start(bf16[144,256]{1,0:T(8,128)(2,1)S(1)} %slice.410), channel_id=1, source_target_pairs={{0,8},{4,12},{8,0},{12,4},{16,24},{20,28},{24,16},{28,20},{1,9},{5... | collective-permute-start | bytes 221192 | tf_op jit(solution)/shard_map/ppermute | solution.py:449
  749.5 10.1 %collective-permute-start.59 = (bf16[17664]{0:T(1024)(128)(2,1)S(1)}, bf16[17664]{0:T(1024)(128)(2,1)S(1)}, u32[]{:S(2)}, u32[]{:S(2)}) collective-permute-start(bf16[17664]{0:T(1024)(128)(2,1)S(1)} %get-tuple-element.305), channel_id=1, source_target_pairs={{0,3},{1,0},{2,1},{3,2},{4,7},{5,4},{6,5},{7,6},{8,11},{9,8},{10,9... | collective-permute-start | bytes 105992 | tf_op jit(solution)/shard_map/ppermute | solution.py:394
  750.1 9.5 %collective-permute-start.58 = (bf16[17664]{0:T(1024)(128)(2,1)S(1)}, bf16[17664]{0:T(1024)(128)(2,1)S(1)}, u32[]{:S(2)}, u32[]{:S(2)}) collective-permute-start(bf16[17664]{0:T(1024)(128)(2,1)S(1)} %get-tuple-element.306), channel_id=1, source_target_pairs={{0,2},{1,3},{2,0},{3,1},{4,6},{5,7},{6,4},{7,5},{8,10},{9,11},{10,... | collective-permute-start | bytes 105992 | tf_op jit(solution)/shard_map/ppermute | solution.py:394
  750.3 9.2 %collective-permute-start.57 = (bf16[17664]{0:T(1024)(128)(2,1)S(1)}, bf16[17664]{0:T(1024)(128)(2,1)S(1)}, u32[]{:S(2)}, u32[]{:S(2)}) collective-permute-start(bf16[17664]{0:T(1024)(128)(2,1)S(1)} %get-tuple-element.304), channel_id=1, source_target_pairs={{0,1},{1,2},{2,3},{3,0},{4,5},{5,6},{6,7},{7,4},{8,9},{9,10},{10,1... | collective-permute-start | bytes 105992 | tf_op jit(solution)/shard_map/ppermute | solution.py:394
  (94 other events, 1199.3 us)
Sparse Core Ops, SparseCore 0:
  17.7 35.3 all-gather.4
  59.4 63.5 all-gather.6
  125.5 54.3 all-gather.8
  186.8 87.7 all-gather.10
  433.5 88.4 reduce-scatter.3
  604.5 75.3 reduce-scatter.5
  748.6 42.2 reduce-scatter.7

commit v12 on v11

--- a/solution.py
+++ b/solution.py
@@ -628,10 +628,10 @@
         two_near_sum = product(pre_near[0], up_part, "nt", 2, [theirs])
         two_near_sum[0], *got = tie(two_near_sum[0], *got)
         two_sum = merge(two_near_sum, got)
+        hid_far[0], hid_far[1], up_terms, *two_sum = tie(*hid_far, up_terms, *two_sum)
         grad_up = lax.psum_scatter(
             up_terms.reshape(n_dp, n_z * own, ff_own), "fsdp", scatter_dimension=1, tiled=True
         )
-        hid_far[0], hid_far[1], *two_sum = tie(*hid_far, *two_sum)
         two_grad = plane.fold(two_sum)
         down_terms = weight_grad(hid_near + hid_far, grad_lots[0] + grad_lots[1], block)
         two_grad, down_terms, hid_far[0] = tie(two_grad, down_terms, hid_far[0])
@@ -672,17 +672,23 @@
         wq_got = send_rows(wq_parts)
         wq_parts[1], hid_late, out_theirs = tie(wq_parts[1], hid_near[0], out_theirs)
         out_sum = merge(product(hid_late, down_part, "nn", 2, [out_theirs]), out_got)
-        out_sum[0], out_sum[1], att_sib, query_late, *kv_got = tie(*out_sum, att_sib, query_grad, *kv_got)
+        out_sum[0], out_sum[1], att_sib, query_late, grad_down, *kv_got = tie(
+            *out_sum, att_sib, query_grad, grad_down, *kv_got
+        )
         branch_out = plane.fold(out_sum)
         wo_sib = product(att_sib, branch_grad, "tn")
-        wo_sib, query_late = tie(wo_sib, query_late)
+        wo_sib, query_late, *wq_got = tie(wo_sib, query_late, *wq_got)
         wo_theirs = plane.swap(wo_sib, 1)
         query_part = product(query_late, full_q, "nt", kind=F32)
-        query_part, wo_theirs, *wq_got = tie(query_part, wo_theirs, *wq_got)
+        wq_rows = own_rows(wq_parts, wq_got).astype(BF16)
+        query_part, wo_theirs = tie(query_part, wo_theirs)
         wo_parts = product(att_mine, branch_grad, "tn", 4, [wo_theirs])
         wo_got = send_rows(wo_parts)
         kv_grad = total(kv_got).astype(BF16).reshape(rows, 2 * HD)
-        query_part, kv_grad, wo_parts[1], branch_out = tie(query_part, kv_grad, wo_parts[1], branch_out)
+        query_part, kv_grad, wo_parts[1], branch_out, wq_rows = tie(
+            query_part, kv_grad, wo_parts[1], branch_out, wq_rows
+        )
+        grad_wq = lax.psum_scatter(wq_rows, "fsdp", scatter_dimension=0, tiled=True)
 
         one_grad = query_part + dot_nt(kv_grad, full_kv)
         grad_bq = jnp.sum(query_grad.astype(F32), axis=0)
@@ -723,18 +729,13 @@
             ).reshape(-1, 2 * HD)
 
         theirs = plane.swap(with_vectors(dot_tn(one_sib, kv_grad), 1).astype(BF16), 1)
+        theirs, *wo_got = tie(theirs, *wo_got)
+        wo_rows = own_rows(wo_parts, wo_got).astype(BF16)
         kv_parts = cut((with_vectors(dot_tn(one_mine, kv_grad), 0) + theirs.astype(F32)).astype(BF16))
         kv_parts_got = send_rows(kv_parts)
-        kv_parts[1], grad_down, *wo_got = tie(kv_parts[1], grad_down, *wo_got)
-
-        both_rows = jnp.concatenate(
-            [
-                own_rows(parts, got).astype(BF16).reshape(n_z, own, width)
-                for parts, got in ((wq_parts, wq_got), (wo_parts, wo_got))
-            ],
-            axis=1,
-        ).reshape(2 * n_z * own, width)
-        both_rows = lax.psum_scatter(both_rows, "fsdp", scatter_dimension=0, tiled=True)
+        kv_parts_got[0], wo_rows = tie(kv_parts_got[0], wo_rows)
+        grad_wo = lax.psum_scatter(wo_rows, "fsdp", scatter_dimension=0, tiled=True)
+
         kv_last = own_rows(kv_parts, kv_parts_got).reshape(2, -1, 2 * HD)
         kv_rows = kv_last.shape[1] - more
         kv_last = jnp.concatenate(
@@ -759,9 +760,9 @@
         return (
             output,
             tokens_grad,
-            both_rows[:own].astype(F32),
+            grad_wq.astype(F32),
             kv_own[: own * 2 * HD].reshape(own, 2 * HD),
-            both_rows[own:].astype(F32),
+            grad_wo.astype(F32),
             bq,
             bv,
             bo,

time: 811 us -> 784 us (0.967)
  waiting for transfers between devices: 219 us -> 182 us
  other arithmetic: 69.9 us -> 84.9 us
  Pallas kernels: 251 us -> 241 us
    reduce_scatter x1 -> x2, waiting for transfers between devices: 29 us -> 8.22 us  [the longest x1 8.22 us: local(): grad_wo = lax.psum_scatter(wo_rows, 'fsdp', scatter_dimension=0, tiled=True)]
    ppermute x45, waiting for transfers between devices: 109 us -> 96.2 us  [swap(): return lax.ppermute(block, 'dp', [(i, i ^ bit) for i in range(self.count)])]
    pallas_call x2, Pallas kernels: 38.4 us -> 28.1 us  [back_product(): pl.pallas_call(functools.partial(back_kernel, count), out_shape=jax.Shape...]
    unnamed x200 -> x190, local copies, waits for them, and re-layouts: 31.4 us -> 28.7 us
  transfers between devices with their start and end apart: 69 -> 70, of which waited for: 26 -> 29; matrix products, arithmetic and copies ran while one was open for 22% -> 24% of each run, Pallas kernels for 27% -> 27%
where the time goes in v12:
time: 784 us; the launch traced here: 773 us
  Pallas kernels  241 us (31%)
  waiting for transfers between devices  182 us (23%)
  starting transfers between devices  86.8 us (11%)
  other arithmetic  84.9 us (11%)
  local copies, waits for them, and re-layouts  84.4 us (11%)
  matrix products  77.5 us (10%)
  between operations  15.9 us (2%)
    ppermute x45, waiting for transfers between devices, swap(): return lax.ppermute(block, 'dp', [(i, i ^ bit) for i in range(self.count)])  96.2 us
    ppermute x15, waiting for transfers between devices, send(): lax.ppermute(block, 'fsdp', [(i, (i + places) % self.count) for i in rang...  59.8 us
    pallas_call x8, Pallas kernels, product(): pl.pallas_call(functools.partial(product_kernel, form, len(extra)), out_s...  57.9 us
    pallas_call x2, Pallas kernels, weight_grad(): pl.pallas_call(functools.partial(weight_kernel, count), out_shape=jax.Sha...  52 us
    pallas_call x2, Pallas kernels, middle_layer(): pl.pallas_call(functools.partial(middle_kernel, count), out_shape=[jax.Sh...  41.2 us
    ppermute x15, starting transfers between devices, send(): lax.ppermute(block, 'fsdp', [(i, (i + places) % self.count) for i in rang...  39.7 us
    dot_general x7, matrix products, dot_nn(): return jnp.dot(left, right, preferred_element_type=F32)  39.1 us
    ppermute x45, starting transfers between devices, swap(): return lax.ppermute(block, 'dp', [(i, i ^ bit) for i in range(self.count)])  38.3 us
  transfers between devices with their start and end apart: 70, of which 29 were waited for; matrix products, arithmetic and copies ran while one was open for 24% of the time, Pallas kernels for 27%

profile of v12, /device:TPU:0, one launch (start us, length us, event | category | flops | bytes accessed | tf_op | source)
XLA Modules:
  0.0 773.1 jit_solution(17798119986646396166)
XLA Ops:
  20.3 2.9 collective-permute-start
  25.8 3.6 all-to-all-start
  29.4 17.9 %collective-permute-done = bf16[256,2048]{1,0:T(8,128)(2,1)} collective-permute-done((bf16[256,2048]{1,0:T(8,128)(2,1)S(1)}, bf16[256,2048]{1,0:T(8,128)(2,1)}, u32[]{:S(2)}, u32[]{:S(2)}) %collective-permute-start) | collective-permute-done | bytes 1048608 | tf_op jit(solution)/shard_map/ppermute | solution.py:449
  49.9 3.1 pad_maximum_fusion.3.refs_1_.refs_9_
  53.0 6.3 all-to-all-done
  67.7 3.5 collective-permute-done.2
  71.1 10.4 %collective-permute-done.3 = bf16[64,2048]{1,0:T(8,128)(2,1)} collective-permute-done((bf16[64,2048]{1,0:T(8,128)(2,1)S(1)}, bf16[64,2048]{1,0:T(8,128)(2,1)}, u32[]{:S(2)}, u32[]{:S(2)}) %collective-permute-start.3) | collective-permute-done | bytes 262176 | tf_op jit(solution)/shard_map/ppermute | solution.py:394
  81.6 6.1 collective-permute-start.5
  94.6 17.0 %collective-permute-done.5 = bf16[256,2048]{1,0:T(8,128)(2,1)} collective-permute-done((bf16[256,2048]{1,0:T(8,128)(2,1)}, bf16[256,2048]{1,0:T(8,128)(2,1)}, u32[]{:S(2)}, u32[]{:S(2)}) %collective-permute-start.5) | collective-permute-done | bytes 1048608 | tf_op jit(solution)/shard_map/ppermute | solution.py:394
  111.6 11.5 %all-gather.7.cloned.1.call-done = bf16[2560,2048]{1,0:T(8,128)(2,1)} async-done(((bf16[320,2048]{1,0:T(8,128)(2,1)}), bf16[2560,2048]{1,0:T(8,128)(2,1)}) %all-gather.7.cloned.1.call-update) | async-done | bytes 10485776 | tf_op jit(solution)/shard_map/all_gather | solution.py:533
  135.2 8.3 %slice.292 = bf16[32,64,2048]{2,1,0:T(8,128)(2,1)} slice(bf16[32,80,2048]{2,1,0:T(8,128)(2,1)} %bitcast.152), slice={[0:32], [0:64], [0:2048]} | slice | bytes 16777216 | tf_op jit(solution)/shard_map/slice | solution.py:548
  148.4 9.9 %collective-permute-done.8 = bf16[256,2048]{1,0:T(8,128)(2,1)} collective-permute-done((bf16[256,2048]{1,0:T(8,128)(2,1)}, bf16[256,2048]{1,0:T(8,128)(2,1)}, u32[]{:S(2)}, u32[]{:S(2)}) %collective-permute-start.8) | collective-permute-done | bytes 1048608 | tf_op jit(solution)/shard_map/ppermute | solution.py:394
  162.1 8.2 %add_convert_fusion.6.q_ref = bf16[512,2048]{1,0:T(8,128)(2,1)S(1)} fusion(bf16[512,2048]{1,0:T(8,128)(2,1)S(1)} %fusion.12.first_ref.second_ref, bf16[2048,2048]{1,0:T(8,128)(2,1)} %bitcast.149, f32[2048]{0:T(1024)S(1)} %reshape.386), kind=kOutput, calls=%fused_computation.42 | convolution fusion | flops 4297064448 | bytes 12591104 | tf_op jit(solution)/shard_map/dot_general | solution.py:21
  170.4 8.8 %collective-permute-done.10 = bf16[2,256,256]{2,1,0:T(8,128)(2,1)S(1)} collective-permute-done((bf16[2,256,256]{2,1,0:T(8,128)(2,1)S(1)}, bf16[2,256,256]{2,1,0:T(8,128)(2,1)S(1)}, u32[]{:S(2)}, u32[]{:S(2)}) %collective-permute-start.10) | collective-permute-done | bytes 262176 | tf_op jit(solution)/shard_map/ppermute | solution.py:394
  180.6 4.4 collective-permute-start.12
  191.0 18.8 %shard_map.288 = (bf16[512,2048]{1,0:T(8,128)(2,1)S(1)}, f32[512,128]{1,0:T(8,128)S(1)}) custom-call(s32[1]{0:T(128)} %bitcast.1.pos_ref, s32[2,8]{1,0:T(2,128)S(1)} %select_reduce_fusion.ends_ref, bf16[512,2048]{1,0:T(8,128)(2,1)S(1)} %add_convert_fusion.6.q_ref, bf16[2,1024,256]{2,1,0:T(8,128)(2,1)S(1)} %constant_dynamic-update-slice_fusion.15.kv_ref), custom_call_target="tpu_custom_call" | custom-call | flops 67108864 | bytes 65536 | tf_op jit(solution)/shard_map/pallas_call | solution.py:132
  212.1 9.2 %collective-permute-done.12 = bf16[256,2048]{1,0:T(8,128)(2,1)S(1)} collective-permute-done((bf16[256,2048]{1,0:T(8,128)(2,1)}, bf16[256,2048]{1,0:T(8,128)(2,1)S(1)}, u32[]{:S(2)}, u32[]{:S(2)}) %collective-permute-start.12) | collective-permute-done | bytes 1048608 | tf_op jit(solution)/shard_map/ppermute | solution.py:394
  221.3 9.3 %fusion.48 = (f32[512]{0:T(512)S(1)}, f32[512,2048]{1,0:T(8,128)S(1)}) fusion(f32[2048]{0:T(1024)S(1)} %reshape.387, bf16[512,2048]{1,0:T(8,128)(2,1)} %copy-done.6, bf16[2048,2048]{1,0:T(8,128)(2,1)} %all-gather.9.cloned.1.call-done, bf16[2,256,2048]{2,1,0:T(8,128)(2,1)} %param.17), kind=kOutput, calls=%fused_computation.184 | convolution fusion | flops 4299161088 | bytes 16787456 | tf_op jit(solution)/shard_map/dot_general | solution.py:21
  241.3 13.6 %shard_map.289.refs_4_ = bf16[2048,1024]{1,0:T(8,128)(2,1)} custom-call(bf16[512,2048]{1,0:T(8,128)(2,1)S(1)} %copy-done.8, bf16[512,2048]{1,0:T(8,128)(2,1)S(1)} %copy-done.9, bf16[512,2048]{1,0:T(8,128)(2,1)} %collective-permute-done.6.refs_2_.refs_10_, bf16[512,2048]{1,0:T(8,128)(2,1)} %collective-permute-done.7.refs_3_.refs_11_, ...), custom_call_target="tpu_custom_call" | custom-call | flops 134217728 | bytes 262144 | tf_op jit(solution)/shard_map/pallas_call | solution.py:240
  254.9 3.7 collective-permute-done.17
  265.4 14.6 %shard_map.290.refs_4_ = bf16[2048,1024]{1,0:T(8,128)(2,1)} custom-call(bf16[512,2048]{1,0:T(8,128)(2,1)} %collective-permute-done.13.refs_0_.refs_12_, bf16[512,2048]{1,0:T(8,128)(2,1)} %collective-permute-done.14.refs_1_.refs_13_, bf16[512,2048]{1,0:T(8,128)(2,1)} %collective-permute-done.15.refs_2_.refs_14_, ...), custom_call_target="tpu_custom_call" | custom-call | flops 134217728 | bytes 262144 | tf_op jit(solution)/shard_map/pallas_call | solution.py:240
  280.0 20.5 %shard_map.291 = (bf16[1024,1024]{1,0:T(8,128)(2,1)S(1)}, bf16[1024,1024]{1,0:T(8,128)(2,1)S(1)}, bf16[1024,1024]{1,0:T(8,128)(2,1)}, bf16[1024,1024]{1,0:T(8,128)(2,1)}, f32[1,1024]{1,0:T(1,128)S(1)}) custom-call(bf16[512,2048]{1,0:T(8,128)(2,1)} %pad_maximum_fusion.4.refs_0_, bf16[512,2048]{1,0:T(8,128)(2,1)} %pad_maximum_fusion.5.refs_1_, ...), custom_call_target="tpu_custom_call" | custom-call | flops 134217728 | bytes 393216 | tf_op jit(solution)/shard_map/pallas_call | solution.py:206
  303.1 7.0 collective-permute-done.21.refs_0_.refs_4_
  311.9 6.5 shard_map.292
  318.5 6.6 shard_map.293
  325.1 20.8 %shard_map.294 = (bf16[1024,1024]{1,0:T(8,128)(2,1)S(1)}, bf16[1024,1024]{1,0:T(8,128)(2,1)S(1)}, bf16[1024,1024]{1,0:T(8,128)(2,1)}, bf16[1024,1024]{1,0:T(8,128)(2,1)}, f32[1,1024]{1,0:T(1,128)S(1)}) custom-call(bf16[512,2048]{1,0:T(8,128)(2,1)} %collective-permute-done.21.refs_0_.refs_4_, bf16[512,2048]{1,0:T(8,128)(2,1)} %collective-permute-done.22.refs_1_.refs_5_, ...), custom_call_target="tpu_custom_call" | custom-call | flops 134217728 | bytes 393216 | tf_op jit(solution)/shard_map/pallas_call | solution.py:206
  345.9 4.5 convolution_convert_fusion.5
  354.7 3.7 add_convert_fusion.4
  358.4 3.7 add_convert_fusion.3
  362.2 7.8 %shard_map.295 = bf16[1024,2048]{1,0:T(8,128)(2,1)} custom-call(bf16[1024,1024]{1,0:T(8,128)(2,1)S(1)} %copy-done.14, bf16[2048,1024]{1,0:T(8,128)(2,1)} %bitcast.143), custom_call_target="tpu_custom_call" | custom-call | flops 67108864 | bytes 163840 | tf_op jit(solution)/shard_map/pallas_call | solution.py:354
  372.6 4.8 collective-permute-done.27.refs_0_
  377.4 25.8 %shard_map.296 = bf16[2048,1024]{1,0:T(8,128)(2,1)} custom-call(bf16[512,2048]{1,0:T(8,128)(2,1)} %pad_maximum_fusion.4.refs_0_, bf16[512,2048]{1,0:T(8,128)(2,1)} %pad_maximum_fusion.5.refs_1_, bf16[512,2048]{1,0:T(8,128)(2,1)} %collective-permute-done.19.refs_2_, bf16[512,2048]{1,0:T(8,128)(2,1)} %collective-permute-done.20.refs_3_, ...), custom_call_target="tpu_custom_call" | custom-call | flops 17179869184 | bytes 29360128 | tf_op jit(solution)/shard_map/pallas_call | solution.py:280
  403.2 8.7 %shard_map.297 = (bf16[512,2048]{1,0:T(8,128)(2,1)S(1)}, bf16[512,2048]{1,0:T(8,128)(2,1)S(1)}) custom-call(bf16[1024,1024]{1,0:T(8,128)(2,1)} %get-tuple-element.230.refs_8_.refs_9_.values_ref, bf16[2048,1024]{1,0:T(8,128)(2,1)} %bitcast.144, bf16[1024,2048]{1,0:T(8,128)(2,1)} %copy-done.47), custom_call_target="tpu_custom_call" | custom-call | flops 67108864 | bytes 163840 | tf_op jit(solution)/shard_map/pallas_call | solution.py:354
  411.9 6.3 collective-permute-done.28
  419.1 5.1 convert_add_fusion.3
  424.3 2.8 slice.392
  432.3 5.8 convolution_convert_fusion.3
  438.1 3.7 convolution_convert_fusion.2
  442.3 26.2 %shard_map.298 = bf16[1024,2048]{1,0:T(8,128)(2,1)} custom-call(bf16[1024,1024]{1,0:T(8,128)(2,1)} %copy-done.11, bf16[1024,1024]{1,0:T(8,128)(2,1)} %copy-done.11, bf16[1024,1024]{1,0:T(8,128)(2,1)} %copy-done.12, bf16[1024,1024]{1,0:T(8,128)(2,1)} %copy-done.12, bf16[1024,1024]{1,0:T(8,128)(2,1)} %copy-done.24, bf16[1024,1024]{1,0:T(8,128)(2,1)} %copy-done.24, ...), custom_call_target="tpu_custom_call" | custom-call | flops 17179869184 | bytes 29360128 | tf_op jit(solution)/shard_map/pallas_call | solution.py:280
  477.3 5.4 add_convert_fusion.2
  482.8 4.1 add_convert_fusion.1
  495.7 10.2 %convolution_convert_fusion.6.grad_ref = bf16[512,2048]{1,0:T(8,128)(2,1)} fusion(bf16[512,2048]{1,0:T(8,128)(2,1)S(1)} %convert_element_type.418.weight_ref, bf16[2048,2048]{1,0:T(8,128)(2,1)} %all-gather.9.cloned.1.call-done), kind=kOutput, calls=%fused_computation.52 | convolution fusion | flops 4296015872 | bytes 12582912 | tf_op jit(solution)/shard_map/dot_general | solution.py:25
  505.9 30.4 %shard_map.299 = (bf16[512,2048]{1,0:T(8,128)(2,1)S(1)}, bf16[2,1024,256]{2,1,0:T(8,128)(2,1)S(1)}) custom-call(s32[1]{0:T(128)} %bitcast.1.pos_ref, s32[2,8]{1,0:T(2,128)S(1)} %select_reduce_fusion.ends_ref, bf16[512,2048]{1,0:T(8,128)(2,1)} %copy-done.5, bf16[2,1024,256]{2,1,0:T(8,128)(2,1)S(1)} %copy-done.4, f32[512,128]{1,0:T(8,128)S(1)} %get-tuple-element.216.norm_ref, ...), custom_call_target="tpu_custom_call" | custom-call | flops 167772160 | bytes 163840 | tf_op jit(solution)/shard_map/pallas_call | solution.py:152
  536.3 4.3 convolution_convert_fusion.1
  543.6 7.7 shard_map.300
  559.0 9.9 %collective-permute-start.38 = (bf16[2,256,256]{2,1,0:T(8,128)(2,1)}, bf16[2,256,256]{2,1,0:T(8,128)(2,1)S(1)}, u32[]{:S(2)}, u32[]{:S(2)}) collective-permute-start(bf16[2,256,256]{2,1,0:T(8,128)(2,1)} %get-tuple-element.332), channel_id=1, source_target_pairs={{0,1},{1,2},{2,3},{3,0},{4,5},{5,6},{6,7},{7,4},{8,9},{9,10},{10,1... | collective-permute-start | bytes 786440 | tf_op jit(solution)/shard_map/ppermute | solution.py:394
  568.9 4.9 collective-permute-start.39
  578.6 4.2 all-to-all-start.1
  583.0 6.5 shard_map.301
  594.7 7.9 %shard_map.302 = (bf16[512,2048]{1,0:T(8,128)(2,1)S(1)}, bf16[512,2048]{1,0:T(8,128)(2,1)S(1)}) custom-call(bf16[1024,1024]{1,0:T(8,128)(2,1)} %copy-done.11, bf16[1024,2048]{1,0:T(8,128)(2,1)} %copy-done.32, bf16[1024,2048]{1,0:T(8,128)(2,1)} %collective-permute-done.37.refs_0_), custom_call_target="tpu_custom_call" | custom-call | flops 67108864 | bytes 163840 | tf_op jit(solution)/shard_map/pallas_call | solution.py:354
  605.4 4.4 convert_add_fusion.1
  611.1 4.5 shard_map.303
  615.6 4.3 collective-permute-done.41
  635.8 15.1 %collective-permute-done.45 = bf16[256,2048]{1,0:T(8,128)(2,1)S(1)} collective-permute-done((bf16[256,2048]{1,0:T(8,128)(2,1)S(1)}, bf16[256,2048]{1,0:T(8,128)(2,1)S(1)}, u32[]{:S(2)}, u32[]{:S(2)}) %collective-permute-start.45) | collective-permute-done | bytes 1048608 | tf_op jit(solution)/shard_map/ppermute | solution.py:449
  655.5 8.7 %shard_map.304 = f32[512,2048]{1,0:T(8,128)} custom-call(bf16[512,2048]{1,0:T(8,128)(2,1)S(1)} %copy-done.2, bf16[2048,2048]{1,0:T(8,128)(2,1)} %bitcast.150), custom_call_target="tpu_custom_call" | custom-call | flops 67108864 | bytes 196608 | tf_op jit(solution)/shard_map/pallas_call | solution.py:354
  667.7 6.1 shard_map.305
  674.9 3.2 convolution_convert_fusion.7
  678.1 4.1 fusion.18
  693.4 16.9 %collective-permute-done.49 = bf16[256,2048]{1,0:T(8,128)(2,1)} collective-permute-done((bf16[256,2048]{1,0:T(8,128)(2,1)}, bf16[256,2048]{1,0:T(8,128)(2,1)}, u32[]{:S(2)}, u32[]{:S(2)}) %collective-permute-start.49) | collective-permute-done | bytes 1048608 | tf_op jit(solution)/shard_map/ppermute | solution.py:449
  718.4 7.0 collective-permute-done.53
  731.5 5.3 fusion.17
  738.1 3.2 collective-permute-done.54
  744.9 5.8 add_convert_fusion
  756.1 8.2 %reduce-scatter.11.cloned.1.call-done = bf16[64,2048]{1,0:T(8,128)(2,1)} async-done(((bf16[256,2048]{1,0:T(8,128)(2,1)}), bf16[64,2048]{1,0:T(8,128)(2,1)}) %reduce-scatter.11.cloned.1.call-update) | async-done | bytes 262160 | tf_op jit(solution)/shard_map/reduce_scatter | solution.py:737
  (469 shorter events, 203.6 us)
Async XLA Ops:
  7.2 52.1 %all-gather.5.cloned.1.call-start = ((), (), s32[]{:S(2)}) async-start(), calls=%async_computation.6 | async-start | bytes 1638400 | tf_op jit(solution)/shard_map/all_gather | solution.py:528
  20.3 27.0 %collective-permute-start = (bf16[256,2048]{1,0:T(8,128)(2,1)S(1)}, bf16[256,2048]{1,0:T(8,128)(2,1)}, u32[]{:S(2)}, u32[]{:S(2)}) collective-permute-start(bf16[256,2048]{1,0:T(8,128)(2,1)S(1)} %get-tuple-element.322), channel_id=1, source_target_pairs={{0,8},{4,12},{8,0},{12,4},{16,24},{20,28},{24,16},{28,20},{1,9},{5... | collective-permute-start | bytes 3145736 | tf_op jit(solution)/shard_map/ppermute | solution.py:449
  23.2 26.7 %collective-permute-start.1 = (bf16[256,2048]{1,0:T(8,128)(2,1)}, bf16[256,2048]{1,0:T(8,128)(2,1)}, u32[]{:S(2)}, u32[]{:S(2)}) collective-permute-start(bf16[256,2048]{1,0:T(8,128)(2,1)} %get-tuple-element.321), channel_id=1, source_target_pairs={{0,16},{4,20},{8,24},{12,28},{16,0},{20,4},{24,8},{28,12},{1,17},{... | collective-permute-start | bytes 3145736 | tf_op jit(solution)/shard_map/ppermute | solution.py:449
  25.8 33.5 %all-to-all-start = ((bf16[64,8,1024]{2,0,1:T(8,128)(2,1)}), bf16[64,8,1024]{2,0,1:T(8,128)(2,1)S(1)}, u32[]{:S(2)}, u32[]{:S(2)}) async-start(bf16[64,8,1024]{2,0,1:T(8,128)(2,1)} %bitcast.137), calls=%async_computation | async-start | bytes 2097152 | tf_op jit(solution)/shard_map/all_to_all | solution.py:530
  29.4 93.7 %all-gather.7.cloned.1.call-start = ((), (), s32[]{:S(2)}) async-start(), calls=%async_computation.7 | async-start | bytes 11796480 | tf_op jit(solution)/shard_map/all_gather | solution.py:533
  59.3 162.0 %all-gather.9.cloned.1.call-start = ((), (), s32[]{:S(2)}) async-start(), calls=%async_computation.8 | async-start | bytes 9437184 | tf_op jit(solution)/shard_map/all_gather | solution.py:546
  59.4 52.2 %collective-permute-start.6 = (bf16[512,2048]{1,0:T(8,128)(2,1)S(1)}, bf16[512,2048]{1,0:T(8,128)(2,1)}, u32[]{:S(2)}, u32[]{:S(2)}) collective-permute-start(bf16[512,2048]{1,0:T(8,128)(2,1)S(1)} %pad_maximum_fusion.2.refs_0_.refs_8_), channel_id=1, source_target_pairs={{0,4},{4,0},{8,12},{12,8},{16,20},{20,16},{24,28},{28,24},{1,5},{5... | collective-permute-start | bytes 6291464 | tf_op jit(solution)/shard_map/ppermute | solution.py:449
  59.4 52.1 %collective-permute-start.7 = (bf16[512,2048]{1,0:T(8,128)(2,1)}, bf16[512,2048]{1,0:T(8,128)(2,1)}, u32[]{:S(2)}, u32[]{:S(2)}) collective-permute-start(bf16[512,2048]{1,0:T(8,128)(2,1)} %pad_maximum_fusion.3.refs_1_.refs_9_), channel_id=1, source_target_pairs={{0,4},{4,0},{8,12},{12,8},{16,20},{20,16},{24,28},{28,24},{1,5},{5... | collective-permute-start | bytes 6291464 | tf_op jit(solution)/shard_map/ppermute | solution.py:449
  59.9 11.2 %collective-permute-start.2 = (bf16[64,2048]{1,0:T(8,128)(2,1)S(1)}, bf16[64,2048]{1,0:T(8,128)(2,1)}, u32[]{:S(2)}, u32[]{:S(2)}) collective-permute-start(bf16[64,2048]{1,0:T(8,128)(2,1)S(1)} %copy-done.60), channel_id=1, source_target_pairs={{0,1},{1,2},{2,3},{3,0},{4,5},{5,6},{6,7},{7,4},{8,9},{9,10},{10,1... | collective-permute-start | bytes 786440 | tf_op jit(solution)/shard_map/ppermute | solution.py:394
  61.5 20.0 %collective-permute-start.3 = (bf16[64,2048]{1,0:T(8,128)(2,1)S(1)}, bf16[64,2048]{1,0:T(8,128)(2,1)}, u32[]{:S(2)}, u32[]{:S(2)}) collective-permute-start(bf16[64,2048]{1,0:T(8,128)(2,1)S(1)} %copy-done.60), channel_id=1, source_target_pairs={{0,2},{1,3},{2,0},{3,1},{4,6},{5,7},{6,4},{7,5},{8,10},{9,11},{10,... | collective-permute-start | bytes 786440 | tf_op jit(solution)/shard_map/ppermute | solution.py:394
  64.1 17.5 %collective-permute-start.4 = (bf16[64,2048]{1,0:T(8,128)(2,1)S(1)}, bf16[64,2048]{1,0:T(8,128)(2,1)}, u32[]{:S(2)}, u32[]{:S(2)}) collective-permute-start(bf16[64,2048]{1,0:T(8,128)(2,1)S(1)} %copy-done.60), channel_id=1, source_target_pairs={{0,3},{1,0},{2,1},{3,2},{4,7},{5,4},{6,5},{7,6},{8,11},{9,8},{10,9... | collective-permute-start | bytes 786440 | tf_op jit(solution)/shard_map/ppermute | solution.py:394
  81.6 30.0 %collective-permute-start.5 = (bf16[256,2048]{1,0:T(8,128)(2,1)}, bf16[256,2048]{1,0:T(8,128)(2,1)}, u32[]{:S(2)}, u32[]{:S(2)}) collective-permute-start(bf16[256,2048]{1,0:T(8,128)(2,1)} %param.29), channel_id=1, source_target_pairs={{0,1},{1,2},{2,3},{3,0},{4,5},{5,6},{6,7},{7,4},{8,9},{9,10},{10,1... | collective-permute-start | bytes 3145736 | tf_op jit(solution)/shard_map/ppermute | solution.py:394
  123.1 156.9 %all-gather.11.cloned.1.call-start = ((), (), s32[]{:S(2)}) async-start(), calls=%async_computation.9 | async-start | bytes 5242880 | tf_op jit(solution)/shard_map/all_gather | solution.py:577
  130.8 27.5 %collective-permute-start.8 = (bf16[256,2048]{1,0:T(8,128)(2,1)}, bf16[256,2048]{1,0:T(8,128)(2,1)}, u32[]{:S(2)}, u32[]{:S(2)}) collective-permute-start(bf16[256,2048]{1,0:T(8,128)(2,1)} %collective-permute-done.5), channel_id=1, source_target_pairs={{0,1},{1,2},{2,3},{3,0},{4,5},{5,6},{6,7},{7,4},{8,9},{9,10},{10,1... | collective-permute-start | bytes 3145736 | tf_op jit(solution)/shard_map/ppermute | solution.py:394
  158.3 12.0 %collective-permute-start.9 = (bf16[2,256,256]{2,1,0:T(8,128)(2,1)S(1)}, bf16[2,256,256]{2,1,0:T(8,128)(2,1)S(1)}, u32[]{:S(2)}, u32[]{:S(2)}) collective-permute-start(bf16[2,256,256]{2,1,0:T(8,128)(2,1)S(1)} %bitcast.174), channel_id=1, source_target_pairs={{0,1},{1,2},{2,3},{3,0},{4,5},{5,6},{6,7},{7,4},{8,9},{9,10},{10,1... | collective-permute-start | bytes 786440 | tf_op jit(solution)/shard_map/ppermute | solution.py:394
  158.3 20.8 %collective-permute-start.10 = (bf16[2,256,256]{2,1,0:T(8,128)(2,1)S(1)}, bf16[2,256,256]{2,1,0:T(8,128)(2,1)S(1)}, u32[]{:S(2)}, u32[]{:S(2)}) collective-permute-start(bf16[2,256,256]{2,1,0:T(8,128)(2,1)S(1)} %bitcast.175), channel_id=1, source_target_pairs={{0,2},{1,3},{2,0},{3,1},{4,6},{5,7},{6,4},{7,5},{8,10},{9,11},{10,... | collective-permute-start | bytes 786440 | tf_op jit(solution)/shard_map/ppermute | solution.py:394
  160.4 18.8 %collective-permute-start.11 = (bf16[2,256,256]{2,1,0:T(8,128)(2,1)S(1)}, bf16[2,256,256]{2,1,0:T(8,128)(2,1)S(1)}, u32[]{:S(2)}, u32[]{:S(2)}) collective-permute-start(bf16[2,256,256]{2,1,0:T(8,128)(2,1)S(1)} %bitcast.176), channel_id=1, source_target_pairs={{0,3},{1,0},{2,1},{3,2},{4,7},{5,4},{6,5},{7,6},{8,11},{9,8},{10,9... | collective-permute-start | bytes 786440 | tf_op jit(solution)/shard_map/ppermute | solution.py:394
  180.6 40.8 %collective-permute-start.12 = (bf16[256,2048]{1,0:T(8,128)(2,1)}, bf16[256,2048]{1,0:T(8,128)(2,1)S(1)}, u32[]{:S(2)}, u32[]{:S(2)}) collective-permute-start(bf16[256,2048]{1,0:T(8,128)(2,1)} %collective-permute-done.8), channel_id=1, source_target_pairs={{0,1},{1,2},{2,3},{3,0},{4,5},{5,6},{6,7},{7,4},{8,9},{9,10},{10,1... | collective-permute-start | bytes 3145736 | tf_op jit(solution)/shard_map/ppermute | solution.py:394
  185.3 47.4 %collective-permute-start.13 = (bf16[512,2048]{1,0:T(8,128)(2,1)}, bf16[512,2048]{1,0:T(8,128)(2,1)}, u32[]{:S(2)}, u32[]{:S(2)}) collective-permute-start(bf16[512,2048]{1,0:T(8,128)(2,1)} %copy-done.7), channel_id=1, source_target_pairs={{0,16},{4,20},{8,24},{12,28},{16,0},{20,4},{24,8},{28,12},{1,17},{... | collective-permute-start | bytes 6291464 | tf_op jit(solution)/shard_map/ppermute | solution.py:449
  186.4 46.3 %collective-permute-start.14 = (bf16[512,2048]{1,0:T(8,128)(2,1)}, bf16[512,2048]{1,0:T(8,128)(2,1)}, u32[]{:S(2)}, u32[]{:S(2)}) collective-permute-start(bf16[512,2048]{1,0:T(8,128)(2,1)} %pad_maximum_fusion.3.refs_1_.refs_9_), channel_id=1, source_target_pairs={{0,8},{4,12},{8,0},{12,4},{16,24},{20,28},{24,16},{28,20},{1,9},{5... | collective-permute-start | bytes 6291464 | tf_op jit(solution)/shard_map/ppermute | solution.py:449
  187.4 354.6 %reduce-scatter.5.cloned.1.call-start = ((), (), s32[]{:S(2)}) async-start(), calls=%async_computation.10 | async-start | bytes 5242880 | tf_op jit(solution)/shard_map/reduce_scatter | solution.py:632
  232.7 30.4 %collective-permute-start.15 = (bf16[512,2048]{1,0:T(8,128)(2,1)}, bf16[512,2048]{1,0:T(8,128)(2,1)}, u32[]{:S(2)}, u32[]{:S(2)}) collective-permute-start(bf16[512,2048]{1,0:T(8,128)(2,1)} %collective-permute-done.13.refs_0_.refs_12_), channel_id=1, source_target_pairs={{0,4},{4,0},{8,12},{12,8},{16,20},{20,16},{24,28},{28,24},{1,5},{5... | collective-permute-start | bytes 6291464 | tf_op jit(solution)/shard_map/ppermute | solution.py:449
  232.9 25.6 %collective-permute-start.17 = (bf16[256,2048]{1,0:T(8,128)(2,1)S(1)}, bf16[256,2048]{1,0:T(8,128)(2,1)S(1)}, u32[]{:S(2)}, u32[]{:S(2)}) collective-permute-start(bf16[256,2048]{1,0:T(8,128)(2,1)S(1)} %get-tuple-element.320), channel_id=1, source_target_pairs={{0,8},{4,12},{8,0},{12,4},{16,24},{20,28},{24,16},{28,20},{1,9},{5... | collective-permute-start | bytes 3145736 | tf_op jit(solution)/shard_map/ppermute | solution.py:449
  234.3 31.1 %collective-permute-start.16 = (bf16[512,2048]{1,0:T(8,128)(2,1)}, bf16[512,2048]{1,0:T(8,128)(2,1)}, u32[]{:S(2)}, u32[]{:S(2)}) collective-permute-start(bf16[512,2048]{1,0:T(8,128)(2,1)} %collective-permute-done.14.refs_1_.refs_13_), channel_id=1, source_target_pairs={{0,4},{4,0},{8,12},{12,8},{16,20},{20,16},{24,28},{28,24},{1,5},{5... | collective-permute-start | bytes 6291464 | tf_op jit(solution)/shard_map/ppermute | solution.py:449
  234.5 25.6 %collective-permute-start.18 = (bf16[256,2048]{1,0:T(8,128)(2,1)S(1)}, bf16[256,2048]{1,0:T(8,128)(2,1)S(1)}, u32[]{:S(2)}, u32[]{:S(2)}) collective-permute-start(bf16[256,2048]{1,0:T(8,128)(2,1)S(1)} %get-tuple-element.319), channel_id=1, source_target_pairs={{0,16},{4,20},{8,24},{12,28},{16,0},{20,4},{24,8},{28,12},{1,17},{... | collective-permute-start | bytes 3145736 | tf_op jit(solution)/shard_map/ppermute | solution.py:449
  261.7 18.3 %collective-permute-start.19 = (bf16[512,2048]{1,0:T(8,128)(2,1)}, bf16[512,2048]{1,0:T(8,128)(2,1)}, u32[]{:S(2)}, u32[]{:S(2)}) collective-permute-start(bf16[512,2048]{1,0:T(8,128)(2,1)} %pad_maximum_fusion.4.refs_0_), channel_id=1, source_target_pairs={{0,4},{4,0},{8,12},{12,8},{16,20},{20,16},{24,28},{28,24},{1,5},{5... | collective-permute-start | bytes 6291464 | tf_op jit(solution)/shard_map/ppermute | solution.py:449
  261.7 18.3 %collective-permute-start.20 = (bf16[512,2048]{1,0:T(8,128)(2,1)}, bf16[512,2048]{1,0:T(8,128)(2,1)}, u32[]{:S(2)}, u32[]{:S(2)}) collective-permute-start(bf16[512,2048]{1,0:T(8,128)(2,1)} %pad_maximum_fusion.5.refs_1_), channel_id=1, source_target_pairs={{0,4},{4,0},{8,12},{12,8},{16,20},{20,16},{24,28},{28,24},{1,5},{5... | collective-permute-start | bytes 6291464 | tf_op jit(solution)/shard_map/ppermute | solution.py:449
  262.2 47.9 %collective-permute-start.21 = (bf16[512,2048]{1,0:T(8,128)(2,1)}, bf16[512,2048]{1,0:T(8,128)(2,1)}, u32[]{:S(2)}, u32[]{:S(2)}) collective-permute-start(bf16[512,2048]{1,0:T(8,128)(2,1)} %pad_maximum_fusion.4.refs_0_), channel_id=1, source_target_pairs={{0,16},{4,20},{8,24},{12,28},{16,0},{20,4},{24,8},{28,12},{1,17},{... | collective-permute-start | bytes 6291464 | tf_op jit(solution)/shard_map/ppermute | solution.py:449
  263.1 47.6 %collective-permute-start.22 = (bf16[512,2048]{1,0:T(8,128)(2,1)}, bf16[512,2048]{1,0:T(8,128)(2,1)}, u32[]{:S(2)}, u32[]{:S(2)}) collective-permute-start(bf16[512,2048]{1,0:T(8,128)(2,1)} %pad_maximum_fusion.5.refs_1_), channel_id=1, source_target_pairs={{0,8},{4,12},{8,0},{12,4},{16,24},{20,28},{24,16},{28,20},{1,9},{5... | collective-permute-start | bytes 6291464 | tf_op jit(solution)/shard_map/ppermute | solution.py:449
  310.7 14.4 %collective-permute-start.23 = (bf16[512,2048]{1,0:T(8,128)(2,1)}, bf16[512,2048]{1,0:T(8,128)(2,1)}, u32[]{:S(2)}, u32[]{:S(2)}) collective-permute-start(bf16[512,2048]{1,0:T(8,128)(2,1)} %collective-permute-done.21.refs_0_.refs_4_), channel_id=1, source_target_pairs={{0,4},{4,0},{8,12},{12,8},{16,20},{20,16},{24,28},{28,24},{1,5},{5... | collective-permute-start | bytes 6291464 | tf_op jit(solution)/shard_map/ppermute | solution.py:449
  310.7 14.4 %collective-permute-start.24 = (bf16[512,2048]{1,0:T(8,128)(2,1)}, bf16[512,2048]{1,0:T(8,128)(2,1)}, u32[]{:S(2)}, u32[]{:S(2)}) collective-permute-start(bf16[512,2048]{1,0:T(8,128)(2,1)} %collective-permute-done.22.refs_1_.refs_5_), channel_id=1, source_target_pairs={{0,4},{4,0},{8,12},{12,8},{16,20},{20,16},{24,28},{28,24},{1,5},{5... | collective-permute-start | bytes 6291464 | tf_op jit(solution)/shard_map/ppermute | solution.py:449
  370.0 7.4 collective-permute-start.27
  370.1 48.1 %collective-permute-start.28 = (bf16[512,2048]{1,0:T(8,128)(2,1)}, bf16[512,2048]{1,0:T(8,128)(2,1)S(1)}, u32[]{:S(2)}, u32[]{:S(2)}) collective-permute-start(bf16[512,2048]{1,0:T(8,128)(2,1)} %add_convert_fusion.4), channel_id=1, source_target_pairs={{0,16},{4,20},{8,24},{12,28},{16,0},{20,4},{24,8},{28,12},{1,17},{... | collective-permute-start | bytes 6291464 | tf_op jit(solution)/shard_map/ppermute | solution.py:449
  371.3 47.8 %collective-permute-start.29 = (bf16[512,2048]{1,0:T(8,128)(2,1)}, bf16[512,2048]{1,0:T(8,128)(2,1)S(1)}, u32[]{:S(2)}, u32[]{:S(2)}) collective-permute-start(bf16[512,2048]{1,0:T(8,128)(2,1)} %add_convert_fusion.3), channel_id=1, source_target_pairs={{0,8},{4,12},{8,0},{12,4},{16,24},{20,28},{24,16},{28,20},{1,9},{5... | collective-permute-start | bytes 6291464 | tf_op jit(solution)/shard_map/ppermute | solution.py:449
  424.2 185.6 %reduce-scatter.7.cloned.1.call-start = ((), (), s32[]{:S(2)}) async-start(), calls=%async_computation.11 | async-start | bytes 5242880 | tf_op jit(solution)/shard_map/reduce_scatter | solution.py:638
  427.1 41.4 %collective-permute-start.31 = (bf16[256,2048]{1,0:T(8,128)(2,1)}, bf16[256,2048]{1,0:T(8,128)(2,1)}, u32[]{:S(2)}, u32[]{:S(2)}) collective-permute-start(bf16[256,2048]{1,0:T(8,128)(2,1)} %slice.392), channel_id=1, source_target_pairs={{0,16},{4,20},{8,24},{12,28},{16,0},{20,4},{24,8},{28,12},{1,17},{... | collective-permute-start | bytes 3145736 | tf_op jit(solution)/shard_map/ppermute | solution.py:449
  430.8 40.2 %collective-permute-start.30 = (bf16[256,2048]{1,0:T(8,128)(2,1)}, bf16[256,2048]{1,0:T(8,128)(2,1)}, u32[]{:S(2)}, u32[]{:S(2)}) collective-permute-start(bf16[256,2048]{1,0:T(8,128)(2,1)} %slice.393), channel_id=1, source_target_pairs={{0,8},{4,12},{8,0},{12,4},{16,24},{20,28},{24,16},{28,20},{1,9},{5... | collective-permute-start | bytes 3145736 | tf_op jit(solution)/shard_map/ppermute | solution.py:449
  438.1 37.6 %collective-permute-start.32 = (bf16[512,2048]{1,0:T(8,128)(2,1)}, bf16[512,2048]{1,0:T(8,128)(2,1)}, u32[]{:S(2)}, u32[]{:S(2)}) collective-permute-start(bf16[512,2048]{1,0:T(8,128)(2,1)} %convolution_convert_fusion.3), channel_id=1, source_target_pairs={{0,4},{4,0},{8,12},{12,8},{16,20},{20,16},{24,28},{28,24},{1,5},{5... | collective-permute-start | bytes 6291464 | tf_op jit(solution)/shard_map/ppermute | solution.py:449
  441.8 40.9 %collective-permute-start.33 = (bf16[512,2048]{1,0:T(8,128)(2,1)}, bf16[512,2048]{1,0:T(8,128)(2,1)}, u32[]{:S(2)}, u32[]{:S(2)}) collective-permute-start(bf16[512,2048]{1,0:T(8,128)(2,1)} %convolution_convert_fusion.2), channel_id=1, source_target_pairs={{0,4},{4,0},{8,12},{12,8},{16,20},{20,16},{24,28},{28,24},{1,5},{5... | collective-permute-start | bytes 6291464 | tf_op jit(solution)/shard_map/ppermute | solution.py:449
  489.1 51.6 %collective-permute-start.34 = (bf16[512,2048]{1,0:T(8,128)(2,1)S(1)}, bf16[512,2048]{1,0:T(8,128)(2,1)S(1)}, u32[]{:S(2)}, u32[]{:S(2)}) collective-permute-start(bf16[512,2048]{1,0:T(8,128)(2,1)S(1)} %add_convert_fusion.2), channel_id=1, source_target_pairs={{0,16},{4,20},{8,24},{12,28},{16,0},{20,4},{24,8},{28,12},{1,17},{... | collective-permute-start | bytes 6291464 | tf_op jit(solution)/shard_map/ppermute | solution.py:449
  490.1 51.8 %collective-permute-start.35 = (bf16[512,2048]{1,0:T(8,128)(2,1)S(1)}, bf16[512,2048]{1,0:T(8,128)(2,1)}, u32[]{:S(2)}, u32[]{:S(2)}) collective-permute-start(bf16[512,2048]{1,0:T(8,128)(2,1)S(1)} %add_convert_fusion.1), channel_id=1, source_target_pairs={{0,8},{4,12},{8,0},{12,4},{16,24},{20,28},{24,16},{28,20},{1,9},{5... | collective-permute-start | bytes 6291464 | tf_op jit(solution)/shard_map/ppermute | solution.py:449
  542.0 41.0 %collective-permute-start.36 = (bf16[1024,2048]{1,0:T(8,128)(2,1)}, bf16[1024,2048]{1,0:T(8,128)(2,1)}, u32[]{:S(2)}, u32[]{:S(2)}) collective-permute-start(bf16[1024,2048]{1,0:T(8,128)(2,1)} %convolution_convert_fusion.1), channel_id=1, source_target_pairs={{0,4},{4,0},{8,12},{12,8},{16,20},{20,16},{24,28},{28,24},{1,5},{5... | collective-permute-start | bytes 12582920 | tf_op jit(solution)/shard_map/ppermute | solution.py:449
  551.3 40.1 %collective-permute-start.37 = (bf16[1024,2048]{1,0:T(8,128)(2,1)}, bf16[1024,2048]{1,0:T(8,128)(2,1)}, u32[]{:S(2)}, u32[]{:S(2)}) collective-permute-start(bf16[1024,2048]{1,0:T(8,128)(2,1)} %shard_map.300), channel_id=1, source_target_pairs={{0,4},{4,0},{8,12},{12,8},{16,20},{20,16},{24,28},{28,24},{1,5},{5... | collective-permute-start | bytes 12582920 | tf_op jit(solution)/shard_map/ppermute | solution.py:449
  559.0 50.8 %collective-permute-start.38 = (bf16[2,256,256]{2,1,0:T(8,128)(2,1)}, bf16[2,256,256]{2,1,0:T(8,128)(2,1)S(1)}, u32[]{:S(2)}, u32[]{:S(2)}) collective-permute-start(bf16[2,256,256]{2,1,0:T(8,128)(2,1)} %get-tuple-element.332), channel_id=1, source_target_pairs={{0,1},{1,2},{2,3},{3,0},{4,5},{5,6},{6,7},{7,4},{8,9},{9,10},{10,1... | collective-permute-start | bytes 786440 | tf_op jit(solution)/shard_map/ppermute | solution.py:394
  568.9 40.9 %collective-permute-start.39 = (bf16[2,256,256]{2,1,0:T(8,128)(2,1)}, bf16[2,256,256]{2,1,0:T(8,128)(2,1)}, u32[]{:S(2)}, u32[]{:S(2)}) collective-permute-start(bf16[2,256,256]{2,1,0:T(8,128)(2,1)} %get-tuple-element.331), channel_id=1, source_target_pairs={{0,2},{1,3},{2,0},{3,1},{4,6},{5,7},{6,4},{7,5},{8,10},{9,11},{10,... | collective-permute-start | bytes 786440 | tf_op jit(solution)/shard_map/ppermute | solution.py:394
  573.8 36.0 %collective-permute-start.40 = (bf16[2,256,256]{2,1,0:T(8,128)(2,1)}, bf16[2,256,256]{2,1,0:T(8,128)(2,1)}, u32[]{:S(2)}, u32[]{:S(2)}) collective-permute-start(bf16[2,256,256]{2,1,0:T(8,128)(2,1)} %get-tuple-element.330), channel_id=1, source_target_pairs={{0,3},{1,0},{2,1},{3,2},{4,7},{5,4},{6,5},{7,6},{8,11},{9,8},{10,9... | collective-permute-start | bytes 786440 | tf_op jit(solution)/shard_map/ppermute | solution.py:394
  578.6 41.3 %all-to-all-start.1 = ((bf16[8,64,1024]{2,1,0:T(8,128)(2,1)}), bf16[8,64,1024]{2,1,0:T(8,128)(2,1)}, u32[]{:S(2)}, u32[]{:S(2)}) async-start(bf16[8,64,1024]{2,1,0:T(8,128)(2,1)} %reduce-scatter.5.cloned.1.call-done), calls=%async_computation.5 | async-start | bytes 2097152 | tf_op jit(solution)/shard_map/all_to_all | solution.py:752
  582.9 171.4 %reduce-scatter.9.cloned.1.call-start = ((), (), s32[]{:S(2)}) async-start(), calls=%async_computation.12 | async-start | bytes 1310720 | tf_op jit(solution)/shard_map/reduce_scatter | solution.py:691
  591.4 28.5 %collective-permute-start.41 = (bf16[256,2048]{1,0:T(8,128)(2,1)}, bf16[256,2048]{1,0:T(8,128)(2,1)}, u32[]{:S(2)}, u32[]{:S(2)}) collective-permute-start(bf16[256,2048]{1,0:T(8,128)(2,1)} %get-tuple-element.269), channel_id=1, source_target_pairs={{0,16},{4,20},{8,24},{12,28},{16,0},{20,4},{24,8},{28,12},{1,17},{... | collective-permute-start | bytes 3145736 | tf_op jit(solution)/shard_map/ppermute | solution.py:449
  593.3 26.7 %collective-permute-start.42 = (bf16[256,2048]{1,0:T(8,128)(2,1)}, bf16[256,2048]{1,0:T(8,128)(2,1)}, u32[]{:S(2)}, u32[]{:S(2)}) collective-permute-start(bf16[256,2048]{1,0:T(8,128)(2,1)} %get-tuple-element.270), channel_id=1, source_target_pairs={{0,8},{4,12},{8,0},{12,4},{16,24},{20,28},{24,16},{28,20},{1,9},{5... | collective-permute-start | bytes 3145736 | tf_op jit(solution)/shard_map/ppermute | solution.py:449
  619.9 47.7 %collective-permute-start.43 = (bf16[1024,2048]{1,0:T(8,128)(2,1)}, bf16[1024,2048]{1,0:T(8,128)(2,1)}, u32[]{:S(2)}, u32[]{:S(2)}) collective-permute-start(bf16[1024,2048]{1,0:T(8,128)(2,1)} %shard_map.303), channel_id=1, source_target_pairs={{0,4},{4,0},{8,12},{12,8},{16,20},{20,16},{24,28},{28,24},{1,5},{5... | collective-permute-start | bytes 12582920 | tf_op jit(solution)/shard_map/ppermute | solution.py:449
  624.9 26.0 %collective-permute-start.45 = (bf16[256,2048]{1,0:T(8,128)(2,1)S(1)}, bf16[256,2048]{1,0:T(8,128)(2,1)S(1)}, u32[]{:S(2)}, u32[]{:S(2)}) collective-permute-start(bf16[256,2048]{1,0:T(8,128)(2,1)S(1)} %slice.390), channel_id=1, source_target_pairs={{0,16},{4,20},{8,24},{12,28},{16,0},{20,4},{24,8},{28,12},{1,17},{... | collective-permute-start | bytes 3145736 | tf_op jit(solution)/shard_map/ppermute | solution.py:449
  626.6 26.1 %collective-permute-start.44 = (bf16[256,2048]{1,0:T(8,128)(2,1)S(1)}, bf16[256,2048]{1,0:T(8,128)(2,1)S(1)}, u32[]{:S(2)}, u32[]{:S(2)}) collective-permute-start(bf16[256,2048]{1,0:T(8,128)(2,1)S(1)} %slice.391), channel_id=1, source_target_pairs={{0,8},{4,12},{8,0},{12,4},{16,24},{20,28},{24,16},{28,20},{1,9},{5... | collective-permute-start | bytes 3145736 | tf_op jit(solution)/shard_map/ppermute | solution.py:449
  631.6 32.6 %collective-permute-start.47 = (bf16[128,2048]{1,0:T(8,128)(2,1)S(1)}, bf16[128,2048]{1,0:T(8,128)(2,1)}, u32[]{:S(2)}, u32[]{:S(2)}) collective-permute-start(bf16[128,2048]{1,0:T(8,128)(2,1)S(1)} %slice.396), channel_id=1, source_target_pairs={{0,16},{4,20},{8,24},{12,28},{16,0},{20,4},{24,8},{28,12},{1,17},{... | collective-permute-start | bytes 1572872 | tf_op jit(solution)/shard_map/ppermute | solution.py:449
  634.7 30.7 %collective-permute-start.46 = (bf16[128,2048]{1,0:T(8,128)(2,1)S(1)}, bf16[128,2048]{1,0:T(8,128)(2,1)}, u32[]{:S(2)}, u32[]{:S(2)}) collective-permute-start(bf16[128,2048]{1,0:T(8,128)(2,1)S(1)} %slice.397), channel_id=1, source_target_pairs={{0,8},{4,12},{8,0},{12,4},{16,24},{20,28},{24,16},{28,20},{1,9},{5... | collective-permute-start | bytes 1572872 | tf_op jit(solution)/shard_map/ppermute | solution.py:449
  686.1 24.2 %collective-permute-start.49 = (bf16[256,2048]{1,0:T(8,128)(2,1)}, bf16[256,2048]{1,0:T(8,128)(2,1)}, u32[]{:S(2)}, u32[]{:S(2)}) collective-permute-start(bf16[256,2048]{1,0:T(8,128)(2,1)} %copy-done.29), channel_id=1, source_target_pairs={{0,16},{4,20},{8,24},{12,28},{16,0},{20,4},{24,8},{28,12},{1,17},{... | collective-permute-start | bytes 3145736 | tf_op jit(solution)/shard_map/ppermute | solution.py:449
  686.7 23.9 %collective-permute-start.50 = (bf16[256,2048]{1,0:T(8,128)(2,1)}, bf16[256,2048]{1,0:T(8,128)(2,1)}, u32[]{:S(2)}, u32[]{:S(2)}) collective-permute-start(bf16[256,2048]{1,0:T(8,128)(2,1)} %copy-done.28), channel_id=1, source_target_pairs={{0,8},{4,12},{8,0},{12,4},{16,24},{20,28},{24,16},{28,20},{1,9},{5... | collective-permute-start | bytes 3145736 | tf_op jit(solution)/shard_map/ppermute | solution.py:449
  689.0 75.3 %reduce-scatter.11.cloned.1.call-start = ((), (), s32[]{:S(2)}) async-start(), calls=%async_computation.13 | async-start | bytes 1310720 | tf_op jit(solution)/shard_map/reduce_scatter | solution.py:737
  712.3 13.1 %collective-permute-start.53 = (bf16[128,2048]{1,0:T(8,128)(2,1)S(1)}, bf16[128,2048]{1,0:T(8,128)(2,1)S(1)}, u32[]{:S(2)}, u32[]{:S(2)}) collective-permute-start(bf16[128,2048]{1,0:T(8,128)(2,1)S(1)} %slice.394), channel_id=1, source_target_pairs={{0,16},{4,20},{8,24},{12,28},{16,0},{20,4},{24,8},{28,12},{1,17},{... | collective-permute-start | bytes 1572872 | tf_op jit(solution)/shard_map/ppermute | solution.py:449
  715.4 12.8 %collective-permute-start.52 = (bf16[128,2048]{1,0:T(8,128)(2,1)S(1)}, bf16[128,2048]{1,0:T(8,128)(2,1)S(1)}, u32[]{:S(2)}, u32[]{:S(2)}) collective-permute-start(bf16[128,2048]{1,0:T(8,128)(2,1)S(1)} %slice.395), channel_id=1, source_target_pairs={{0,8},{4,12},{8,0},{12,4},{16,24},{20,28},{24,16},{28,20},{1,9},{5... | collective-permute-start | bytes 1572872 | tf_op jit(solution)/shard_map/ppermute | solution.py:449
  716.1 13.3 %collective-permute-start.51 = (bf16[288,256]{1,0:T(8,128)(2,1)S(1)}, bf16[288,256]{1,0:T(8,128)(2,1)S(1)}, u32[]{:S(2)}, u32[]{:S(2)}) collective-permute-start(bf16[288,256]{1,0:T(8,128)(2,1)S(1)} %get-tuple-element.336), channel_id=1, source_target_pairs={{0,16},{4,20},{8,24},{12,28},{16,0},{20,4},{24,8},{28,12},{1,17},{... | collective-permute-start | bytes 442376 | tf_op jit(solution)/shard_map/ppermute | solution.py:449
  717.6 12.3 %collective-permute-start.55 = (bf16[288,256]{1,0:T(8,128)(2,1)S(1)}, bf16[288,256]{1,0:T(8,128)(2,1)}, u32[]{:S(2)}, u32[]{:S(2)}) collective-permute-start(bf16[288,256]{1,0:T(8,128)(2,1)S(1)} %get-tuple-element.337), channel_id=1, source_target_pairs={{0,8},{4,12},{8,0},{12,4},{16,24},{20,28},{24,16},{28,20},{1,9},{5... | collective-permute-start | bytes 442376 | tf_op jit(solution)/shard_map/ppermute | solution.py:449
  742.2 8.7 %collective-permute-start.59 = (bf16[17664]{0:T(1024)(128)(2,1)S(1)}, bf16[17664]{0:T(1024)(128)(2,1)S(1)}, u32[]{:S(2)}, u32[]{:S(2)}) collective-permute-start(bf16[17664]{0:T(1024)(128)(2,1)S(1)} %get-tuple-element.313), channel_id=1, source_target_pairs={{0,3},{1,0},{2,1},{3,2},{4,7},{5,4},{6,5},{7,6},{8,11},{9,8},{10,9... | collective-permute-start | bytes 105992 | tf_op jit(solution)/shard_map/ppermute | solution.py:394
  742.9 9.1 %collective-permute-start.58 = (bf16[17664]{0:T(1024)(128)(2,1)S(1)}, bf16[17664]{0:T(1024)(128)(2,1)S(1)}, u32[]{:S(2)}, u32[]{:S(2)}) collective-permute-start(bf16[17664]{0:T(1024)(128)(2,1)S(1)} %get-tuple-element.314), channel_id=1, source_target_pairs={{0,2},{1,3},{2,0},{3,1},{4,6},{5,7},{6,4},{7,5},{8,10},{9,11},{10,... | collective-permute-start | bytes 105992 | tf_op jit(solution)/shard_map/ppermute | solution.py:394
  (90 other events, 1063.4 us)
Sparse Core Ops, SparseCore 0:
  17.7 35.3 all-gather.4
  59.4 63.5 all-gather.6
  125.5 54.3 all-gather.8
  187.5 88.4 all-gather.10
  424.4 87.2 reduce-scatter.4
  513.9 94.1 reduce-scatter.6
  689.1 24.9 reduce-scatter.8
  738.2 26.0 reduce-scatter.10

commit v13 on v12

--- a/solution.py
+++ b/solution.py
@@ -535,6 +535,8 @@
         *out_pieces, down_late = tie(*out_pieces, down_weight)
         full_o = line.in_order(out_pieces)
         down_pieces = [down_late, line.send(down_late, 1)]
+        if n_z > 2:
+            down_pieces.append(line.send(down_pieces[-1], 1))
         inputs = tokens.reshape(rows, width).astype(F32)
         mean_one, recip_one = norm_stats(inputs)
         grad_near_sib = plane.cross(grad_near)
@@ -556,7 +558,7 @@
         normed_one = (xhat_one * gain_one + shift_one).astype(BF16)
         kv_bias = jnp.concatenate([jnp.zeros((HD,), F32), bias_v])
         key_value = (dot_nn(normed_one, full_kv) + kv_bias).astype(BF16)
-        if n_z > 2:
+        if n_z > 3:
             down_pieces.append(line.send(down_pieces[-1], 1))
         key_value, normed_late, up_cols, down_pieces[-1] = tie(
             key_value, normed_one, up_cols, down_pieces[-1]
@@ -672,18 +674,17 @@
         wq_got = send_rows(wq_parts)
         wq_parts[1], hid_late, out_theirs = tie(wq_parts[1], hid_near[0], out_theirs)
         out_sum = merge(product(hid_late, down_part, "nn", 2, [out_theirs]), out_got)
-        out_sum[0], out_sum[1], att_sib, query_late, grad_down, *kv_got = tie(
-            *out_sum, att_sib, query_grad, grad_down, *kv_got
+        out_sum[0], out_sum[1], att_sib, query_late, grad_down, grad_up, *kv_got = tie(
+            *out_sum, att_sib, query_grad, grad_down, grad_up, *kv_got
         )
         branch_out = plane.fold(out_sum)
-        wo_sib = product(att_sib, branch_grad, "tn")
-        wo_sib, query_late, *wq_got = tie(wo_sib, query_late, *wq_got)
+        wo_sib, *wq_got = tie(product(att_sib, branch_grad, "tn"), *wq_got)
         wo_theirs = plane.swap(wo_sib, 1)
-        query_part = product(query_late, full_q, "nt", kind=F32)
         wq_rows = own_rows(wq_parts, wq_got).astype(BF16)
-        query_part, wo_theirs = tie(query_part, wo_theirs)
         wo_parts = product(att_mine, branch_grad, "tn", 4, [wo_theirs])
         wo_got = send_rows(wo_parts)
+        wo_parts[1], query_late = tie(wo_parts[1], query_late)
+        query_part = product(query_late, full_q, "nt", kind=F32)
         kv_grad = total(kv_got).astype(BF16).reshape(rows, 2 * HD)
         query_part, kv_grad, wo_parts[1], branch_out, wq_rows = tie(
             query_part, kv_grad, wo_parts[1], branch_out, wq_rows
@@ -691,7 +692,7 @@
         grad_wq = lax.psum_scatter(wq_rows, "fsdp", scatter_dimension=0, tiled=True)
 
         one_grad = query_part + dot_nt(kv_grad, full_kv)
-        grad_bq = jnp.sum(query_grad.astype(F32), axis=0)
+        grad_bq = jnp.sum(query_late.astype(F32), axis=0)
         grad_bv = jnp.sum(kv_grad[:, HD:].astype(F32), axis=0)
         grad_gain_one = jnp.sum(one_grad * xhat_one, axis=0)
         grad_shift_one = jnp.sum(one_grad, axis=0)

time: 784 us -> 826 us (1.054)
  waiting for transfers between devices: 182 us -> 201 us
  starting transfers between devices: 86.8 us -> 99.3 us
  Pallas kernels: 241 us -> 253 us
    ppermute x15, waiting for transfers between devices: 59.8 us -> 77.8 us  [send(): lax.ppermute(block, 'fsdp', [(i, (i + places) % self.count) for i in rang...]
    ppermute x15, starting transfers between devices: 39.7 us -> 55.6 us  [send(): lax.ppermute(block, 'fsdp', [(i, (i + places) % self.count) for i in rang...]
    all_gather x1, waiting for transfers between devices: 0.01 us -> 15.7 us  [local(): lax.all_gather(up_cols, 'fsdp', axis=1, tiled=True).reshape(width, ff_own)]
    ppermute x45, waiting for transfers between devices: 96.2 us -> 84.1 us  [swap(): return lax.ppermute(block, 'dp', [(i, i ^ bit) for i in range(self.count)])]
    all_gather x1, waiting for transfers between devices: 11.5 us -> 0.01 us  [local(): packed = lax.all_gather(packed, 'dp', axis=0, tiled=True)]
    pallas_call x2, Pallas kernels: 28.1 us -> 39.6 us  [back_product(): pl.pallas_call(functools.partial(back_kernel, count), out_shape=jax.Shape...]
    reduce_scatter x1, waiting for transfers between devices: 0.02 us -> 11.1 us  [local(): lax.psum_scatter(down_terms, 'fsdp', scatter_dimension=0, tiled=True)]
    unnamed x190 -> x184, local copies, waits for them, and re-layouts: 28.7 us -> 30.4 us
  transfers between devices with their start and end apart: 70 -> 70, of which waited for: 29 -> 27; matrix products, arithmetic and copies ran while one was open for 24% -> 22% of each run, Pallas kernels for 27% -> 26%
where the time goes in v13:
time: 826 us; the launch traced here: 816 us
  Pallas kernels  253 us (31%)
  waiting for transfers between devices  201 us (24%)
  starting transfers between devices  99.3 us (12%)
  local copies, waits for them, and re-layouts  87.2 us (11%)
  other arithmetic  84.6 us (10%)
  matrix products  74.1 us (9%)
  between operations  15.9 us (2%)
    ppermute x45, waiting for transfers between devices, swap(): return lax.ppermute(block, 'dp', [(i, i ^ bit) for i in range(self.count)])  84.1 us
    ppermute x15, waiting for transfers between devices, send(): lax.ppermute(block, 'fsdp', [(i, (i + places) % self.count) for i in rang...  77.8 us
    pallas_call x8, Pallas kernels, product(): pl.pallas_call(functools.partial(product_kernel, form, len(extra)), out_s...  57.2 us
    ppermute x15, starting transfers between devices, send(): lax.ppermute(block, 'fsdp', [(i, (i + places) % self.count) for i in rang...  55.6 us
    pallas_call x2, Pallas kernels, weight_grad(): pl.pallas_call(functools.partial(weight_kernel, count), out_shape=jax.Sha...  52.1 us
    pallas_call x2, Pallas kernels, middle_layer(): pl.pallas_call(functools.partial(middle_kernel, count), out_shape=[jax.Sh...  41.9 us
    dot_general x7, matrix products, dot_nn(): return jnp.dot(left, right, preferred_element_type=F32)  39.8 us
    pallas_call x2, Pallas kernels, back_product(): pl.pallas_call(functools.partial(back_kernel, count), out_shape=jax.Shape...  39.6 us
  transfers between devices with their start and end apart: 70, of which 27 were waited for; matrix products, arithmetic and copies ran while one was open for 22% of the time, Pallas kernels for 26%

profile of v13, /device:TPU:0, one launch (start us, length us, event | category | flops | bytes accessed | tf_op | source)
XLA Modules:
  0.0 815.7 jit_solution(2272886369946900392)
XLA Ops:
  17.6 3.1 slice_bitcast_fusion
  20.7 3.0 collective-permute-start.1
  26.2 3.6 all-to-all-start
  29.9 18.1 %collective-permute-done.1 = bf16[256,2048]{1,0:T(8,128)(2,1)} collective-permute-done((bf16[256,2048]{1,0:T(8,128)(2,1)}, bf16[256,2048]{1,0:T(8,128)(2,1)}, u32[]{:S(2)}, u32[]{:S(2)}) %collective-permute-start.1) | collective-permute-done | bytes 1048608 | tf_op jit(solution)/shard_map/ppermute | solution.py:449
  47.9 3.1 pad_maximum_fusion.3.refs_1_.refs_9_
  51.1 3.1 pad_maximum_fusion.2.refs_0_.refs_8_
  54.2 5.3 all-to-all-done
  65.3 5.3 collective-permute-done.2
  70.6 8.4 %collective-permute-done.3 = bf16[64,2048]{1,0:T(8,128)(2,1)S(1)} collective-permute-done((bf16[64,2048]{1,0:T(8,128)(2,1)S(1)}, bf16[64,2048]{1,0:T(8,128)(2,1)S(1)}, u32[]{:S(2)}, u32[]{:S(2)}) %collective-permute-start.3) | collective-permute-done | bytes 262176 | tf_op jit(solution)/shard_map/ppermute | solution.py:394
  79.0 28.5 %collective-permute-start.5 = (bf16[256,2048]{1,0:T(8,128)(2,1)}, bf16[256,2048]{1,0:T(8,128)(2,1)}, u32[]{:S(2)}, u32[]{:S(2)}) collective-permute-start(bf16[256,2048]{1,0:T(8,128)(2,1)} %param.29), channel_id=1, source_target_pairs={{0,1},{1,2},{2,3},{3,0},{4,5},{5,6},{6,7},{7,4},{8,9},{9,10},{10,1... | collective-permute-start | bytes 3145736 | tf_op jit(solution)/shard_map/ppermute | solution.py:394
  108.5 22.1 %collective-permute-done.5 = bf16[256,2048]{1,0:T(8,128)(2,1)} collective-permute-done((bf16[256,2048]{1,0:T(8,128)(2,1)}, bf16[256,2048]{1,0:T(8,128)(2,1)}, u32[]{:S(2)}, u32[]{:S(2)}) %collective-permute-start.5) | collective-permute-done | bytes 1048608 | tf_op jit(solution)/shard_map/ppermute | solution.py:394
  139.9 17.1 %collective-permute-done.6 = bf16[256,2048]{1,0:T(8,128)(2,1)} collective-permute-done((bf16[256,2048]{1,0:T(8,128)(2,1)}, bf16[256,2048]{1,0:T(8,128)(2,1)}, u32[]{:S(2)}, u32[]{:S(2)}) %collective-permute-start.6) | collective-permute-done | bytes 1048608 | tf_op jit(solution)/shard_map/ppermute | solution.py:394
  158.0 8.4 %slice.292 = bf16[32,64,2048]{2,1,0:T(8,128)(2,1)} slice(bf16[32,80,2048]{2,1,0:T(8,128)(2,1)} %bitcast.151), slice={[0:32], [0:64], [0:2048]} | slice | bytes 16777216 | tf_op jit(solution)/shard_map/slice | solution.py:550
  183.9 13.5 %collective-permute-done.9 = bf16[256,2048]{1,0:T(8,128)(2,1)} collective-permute-done((bf16[256,2048]{1,0:T(8,128)(2,1)}, bf16[256,2048]{1,0:T(8,128)(2,1)}, u32[]{:S(2)}, u32[]{:S(2)}) %collective-permute-start.9) | collective-permute-done | bytes 1048608 | tf_op jit(solution)/shard_map/ppermute | solution.py:394
  197.6 3.7 collective-permute-start.12
  201.7 8.5 %add_convert_fusion.6.q_ref = bf16[512,2048]{1,0:T(8,128)(2,1)S(1)} fusion(bf16[512,2048]{1,0:T(8,128)(2,1)} %fusion.12.first_ref.second_ref, bf16[2048,2048]{1,0:T(8,128)(2,1)} %bitcast.149, f32[2048]{0:T(1024)S(1)} %reshape.386), kind=kOutput, calls=%fused_computation.42 | convolution fusion | flops 4297064448 | bytes 12591104 | tf_op jit(solution)/shard_map/dot_general | solution.py:21
  210.3 6.3 collective-permute-done.11
  216.7 18.9 %shard_map.288 = (bf16[512,2048]{1,0:T(8,128)(2,1)S(1)}, f32[512,128]{1,0:T(8,128)S(1)}) custom-call(s32[1]{0:T(128)} %bitcast.1.pos_ref, s32[2,8]{1,0:T(2,128)S(1)} %select_reduce_fusion.ends_ref, bf16[512,2048]{1,0:T(8,128)(2,1)S(1)} %add_convert_fusion.6.q_ref, bf16[2,1024,256]{2,1,0:T(8,128)(2,1)S(1)} %constant_dynamic-update-slice_fusion.15.kv_ref), custom_call_target="tpu_custom_call" | custom-call | flops 67108864 | bytes 65536 | tf_op jit(solution)/shard_map/pallas_call | solution.py:132
  236.6 9.4 %fusion.48 = (f32[512]{0:T(512)S(1)}, f32[512,2048]{1,0:T(8,128)S(1)}) fusion(f32[2048]{0:T(1024)S(1)} %reshape.387, bf16[512,2048]{1,0:T(8,128)(2,1)S(1)} %get-tuple-element.207.first_ref.second_ref, bf16[2048,2048]{1,0:T(8,128)(2,1)} %all-gather.9.cloned.1.call-done, bf16[2,256,2048]{2,1,0:T(8,128)(2,1)} %param.17), kind=kOutput, calls=%fused_computation.184 | convolution fusion | flops 4299161088 | bytes 16787456 | tf_op jit(solution)/shard_map/dot_general | solution.py:21
  257.7 25.0 %shard_map.289.refs_4_ = bf16[2048,1024]{1,0:T(8,128)(2,1)} custom-call(bf16[512,2048]{1,0:T(8,128)(2,1)} %pad_maximum_fusion.2.refs_0_.refs_8_, bf16[512,2048]{1,0:T(8,128)(2,1)} %pad_maximum_fusion.3.refs_1_.refs_9_, bf16[512,2048]{1,0:T(8,128)(2,1)} %collective-permute-done.7.refs_2_.refs_10_, bf16[512,2048]{1,0:T(8,128)(2,1)} %collective-permute-done.8.refs_3_.refs_11_, ...), custom_call_target="tpu_custom_call" | custom-call | flops 134217728 | bytes 262144 | tf_op jit(solution)/shard_map/pallas_call | solution.py:240
  287.5 14.6 %shard_map.290.refs_4_ = bf16[2048,1024]{1,0:T(8,128)(2,1)} custom-call(bf16[512,2048]{1,0:T(8,128)(2,1)} %collective-permute-done.13.refs_0_.refs_12_, bf16[512,2048]{1,0:T(8,128)(2,1)} %collective-permute-done.14.refs_1_.refs_13_, bf16[512,2048]{1,0:T(8,128)(2,1)} %collective-permute-done.15.refs_2_.refs_14_, ...), custom_call_target="tpu_custom_call" | custom-call | flops 134217728 | bytes 262144 | tf_op jit(solution)/shard_map/pallas_call | solution.py:240
  302.1 15.7 %all-gather.11.cloned.1.call-done = bf16[8,256,1024]{2,1,0:T(8,128)(2,1)} async-done(((bf16[8,64,1024]{2,1,0:T(8,128)(2,1)}), bf16[8,256,1024]{2,1,0:T(8,128)(2,1)}) %all-gather.11.cloned.1.call-update) | async-done | bytes 4194320 | tf_op jit(solution)/shard_map/all_gather | solution.py:579
  317.8 20.5 %shard_map.291 = (bf16[1024,1024]{1,0:T(8,128)(2,1)S(1)}, bf16[1024,1024]{1,0:T(8,128)(2,1)S(1)}, bf16[1024,1024]{1,0:T(8,128)(2,1)}, bf16[1024,1024]{1,0:T(8,128)(2,1)}, f32[1,1024]{1,0:T(1,128)S(1)}) custom-call(bf16[512,2048]{1,0:T(8,128)(2,1)} %pad_maximum_fusion.4.refs_0_, bf16[512,2048]{1,0:T(8,128)(2,1)} %copy-done.45, ...), custom_call_target="tpu_custom_call" | custom-call | flops 134217728 | bytes 393216 | tf_op jit(solution)/shard_map/pallas_call | solution.py:206
  342.3 6.6 shard_map.293
  348.8 6.6 shard_map.292
  356.8 21.3 %shard_map.294 = (bf16[1024,1024]{1,0:T(8,128)(2,1)S(1)}, bf16[1024,1024]{1,0:T(8,128)(2,1)S(1)}, bf16[1024,1024]{1,0:T(8,128)(2,1)}, bf16[1024,1024]{1,0:T(8,128)(2,1)}, f32[1,1024]{1,0:T(1,128)S(1)}) custom-call(bf16[512,2048]{1,0:T(8,128)(2,1)} %collective-permute-done.21.refs_0_.refs_4_, bf16[512,2048]{1,0:T(8,128)(2,1)} %collective-permute-done.22.refs_1_.refs_5_, ...), custom_call_target="tpu_custom_call" | custom-call | flops 134217728 | bytes 393216 | tf_op jit(solution)/shard_map/pallas_call | solution.py:206
  378.2 4.5 convolution_convert_fusion.4
  387.0 3.8 add_convert_fusion.3
  390.8 3.7 add_convert_fusion.4
  394.5 7.8 shard_map.295
  405.4 4.3 collective-permute-done.27.refs_0_
  409.7 25.9 %shard_map.296 = bf16[2048,1024]{1,0:T(8,128)(2,1)} custom-call(bf16[512,2048]{1,0:T(8,128)(2,1)} %pad_maximum_fusion.4.refs_0_, bf16[512,2048]{1,0:T(8,128)(2,1)} %copy-done.45, bf16[512,2048]{1,0:T(8,128)(2,1)} %collective-permute-done.19.refs_2_, bf16[512,2048]{1,0:T(8,128)(2,1)} %collective-permute-done.20.refs_3_, ...), custom_call_target="tpu_custom_call" | custom-call | flops 17179869184 | bytes 29360128 | tf_op jit(solution)/shard_map/pallas_call | solution.py:280
  435.5 8.7 %shard_map.297 = (bf16[512,2048]{1,0:T(8,128)(2,1)S(1)}, bf16[512,2048]{1,0:T(8,128)(2,1)S(1)}) custom-call(bf16[1024,1024]{1,0:T(8,128)(2,1)} %get-tuple-element.227.refs_8_.refs_9_.values_ref, bf16[2048,1024]{1,0:T(8,128)(2,1)} %bitcast.144, bf16[1024,2048]{1,0:T(8,128)(2,1)} %copy-done.46), custom_call_target="tpu_custom_call" | custom-call | flops 67108864 | bytes 163840 | tf_op jit(solution)/shard_map/pallas_call | solution.py:354
  444.2 6.3 collective-permute-done.28
  451.7 5.2 convert_add_fusion.3
  457.0 6.0 convolution_convert_fusion.2
  470.5 3.7 convolution_convert_fusion.3
  474.2 26.2 %shard_map.298 = bf16[1024,2048]{1,0:T(8,128)(2,1)} custom-call(bf16[1024,1024]{1,0:T(8,128)(2,1)} %copy-done.8, bf16[1024,1024]{1,0:T(8,128)(2,1)} %copy-done.8, bf16[1024,1024]{1,0:T(8,128)(2,1)} %copy-done.9, bf16[1024,1024]{1,0:T(8,128)(2,1)} %copy-done.9, bf16[1024,1024]{1,0:T(8,128)(2,1)} %copy-done.25, bf16[1024,1024]{1,0:T(8,128)(2,1)} %copy-done.25, ...), custom_call_target="tpu_custom_call" | custom-call | flops 17179869184 | bytes 29360128 | tf_op jit(solution)/shard_map/pallas_call | solution.py:280
  509.2 5.4 add_convert_fusion.1
  514.7 4.1 add_convert_fusion.2
  527.8 6.0 convolution_convert_fusion.6.grad_ref
  533.8 30.5 %shard_map.299 = (bf16[512,2048]{1,0:T(8,128)(2,1)S(1)}, bf16[2,1024,256]{2,1,0:T(8,128)(2,1)S(1)}) custom-call(s32[1]{0:T(128)} %bitcast.1.pos_ref, s32[2,8]{1,0:T(2,128)S(1)} %copy-done.24, bf16[512,2048]{1,0:T(8,128)(2,1)} %copy-done.5, bf16[2,1024,256]{2,1,0:T(8,128)(2,1)S(1)} %copy-done.4, f32[512,128]{1,0:T(8,128)S(1)} %get-tuple-element.246.norm_ref, ...), custom_call_target="tpu_custom_call" | custom-call | flops 167772160 | bytes 163840 | tf_op jit(solution)/shard_map/pallas_call | solution.py:152
  564.4 4.3 convolution_convert_fusion.1
  572.0 7.7 shard_map.300
  586.6 6.2 shard_map.301
  596.4 7.9 shard_map.302
  604.3 4.6 convert_add_fusion.1
  608.9 2.8 convert_add_fusion.2
  611.7 3.9 collective-permute-done.39
  616.8 11.1 %reduce-scatter.7.cloned.1.call-done = bf16[256,2048]{1,0:T(8,128)(2,1)} async-done(((bf16[1024,2048]{1,0:T(8,128)(2,1)}), bf16[256,2048]{1,0:T(8,128)(2,1)}) %reduce-scatter.7.cloned.1.call-update) | async-done | bytes 1048592 | tf_op jit(solution)/shard_map/reduce_scatter | solution.py:640
  627.9 4.2 all-to-all-start.1
  644.2 4.9 shard_map.303
  659.4 10.2 %collective-permute-done.44 = bf16[256,2048]{1,0:T(8,128)(2,1)} collective-permute-done((bf16[256,2048]{1,0:T(8,128)(2,1)}, bf16[256,2048]{1,0:T(8,128)(2,1)}, u32[]{:S(2)}, u32[]{:S(2)}) %collective-permute-start.44) | collective-permute-done | bytes 1048608 | tf_op jit(solution)/shard_map/ppermute | solution.py:449
  675.2 5.0 collective-permute-done.46
  683.7 5.4 shard_map.304
  693.1 8.7 %shard_map.305 = f32[512,2048]{1,0:T(8,128)} custom-call(bf16[512,2048]{1,0:T(8,128)(2,1)S(1)} %copy-done.2, bf16[2048,2048]{1,0:T(8,128)(2,1)} %bitcast.150), custom_call_target="tpu_custom_call" | custom-call | flops 67108864 | bytes 196608 | tf_op jit(solution)/shard_map/pallas_call | solution.py:354
  705.6 6.3 fusion.18
  722.4 23.5 %collective-permute-done.49 = bf16[256,2048]{1,0:T(8,128)(2,1)} collective-permute-done((bf16[256,2048]{1,0:T(8,128)(2,1)}, bf16[256,2048]{1,0:T(8,128)(2,1)}, u32[]{:S(2)}, u32[]{:S(2)}) %collective-permute-start.49) | collective-permute-done | bytes 1048608 | tf_op jit(solution)/shard_map/ppermute | solution.py:449
  755.1 7.6 collective-permute-done.52
  768.8 5.5 fusion.17
  775.6 3.1 collective-permute-done.56
  779.7 7.2 collective-permute-start.57
  789.6 5.9 add_convert_fusion
  799.8 7.1 reduce-scatter.11.cloned.1.call-done
  (464 shorter events, 194.9 us)
Async XLA Ops:
  7.2 52.2 %all-gather.5.cloned.1.call-start = ((), (), s32[]{:S(2)}) async-start(), calls=%async_computation.6 | async-start | bytes 1638400 | tf_op jit(solution)/shard_map/all_gather | solution.py:528
  20.7 27.3 %collective-permute-start.1 = (bf16[256,2048]{1,0:T(8,128)(2,1)}, bf16[256,2048]{1,0:T(8,128)(2,1)}, u32[]{:S(2)}, u32[]{:S(2)}) collective-permute-start(bf16[256,2048]{1,0:T(8,128)(2,1)} %get-tuple-element.319), channel_id=1, source_target_pairs={{0,16},{4,20},{8,24},{12,28},{16,0},{20,4},{24,8},{28,12},{1,17},{... | collective-permute-start | bytes 3145736 | tf_op jit(solution)/shard_map/ppermute | solution.py:449
  23.6 27.4 %collective-permute-start = (bf16[256,2048]{1,0:T(8,128)(2,1)}, bf16[256,2048]{1,0:T(8,128)(2,1)}, u32[]{:S(2)}, u32[]{:S(2)}) collective-permute-start(bf16[256,2048]{1,0:T(8,128)(2,1)} %get-tuple-element.320), channel_id=1, source_target_pairs={{0,8},{4,12},{8,0},{12,4},{16,24},{20,28},{24,16},{28,20},{1,9},{5... | collective-permute-start | bytes 3145736 | tf_op jit(solution)/shard_map/ppermute | solution.py:449
  26.2 33.2 %all-to-all-start = ((bf16[64,8,1024]{2,0,1:T(8,128)(2,1)}), bf16[64,8,1024]{2,0,1:T(8,128)(2,1)S(1)}, u32[]{:S(2)}, u32[]{:S(2)}) async-start(bf16[64,8,1024]{2,0,1:T(8,128)(2,1)} %bitcast.137), calls=%async_computation | async-start | bytes 2097152 | tf_op jit(solution)/shard_map/all_to_all | solution.py:530
  29.8 127.3 %all-gather.7.cloned.1.call-start = ((), (), s32[]{:S(2)}) async-start(), calls=%async_computation.7 | async-start | bytes 11796480 | tf_op jit(solution)/shard_map/all_gather | solution.py:533
  59.5 177.1 %all-gather.9.cloned.1.call-start = ((), (), s32[]{:S(2)}) async-start(), calls=%async_computation.8 | async-start | bytes 9437184 | tf_op jit(solution)/shard_map/all_gather | solution.py:548
  59.5 11.1 %collective-permute-start.2 = (bf16[64,2048]{1,0:T(8,128)(2,1)S(1)}, bf16[64,2048]{1,0:T(8,128)(2,1)S(1)}, u32[]{:S(2)}, u32[]{:S(2)}) collective-permute-start(bf16[64,2048]{1,0:T(8,128)(2,1)S(1)} %copy-done.56), channel_id=1, source_target_pairs={{0,1},{1,2},{2,3},{3,0},{4,5},{5,6},{6,7},{7,4},{8,9},{9,10},{10,1... | collective-permute-start | bytes 786440 | tf_op jit(solution)/shard_map/ppermute | solution.py:394
  61.4 17.6 %collective-permute-start.3 = (bf16[64,2048]{1,0:T(8,128)(2,1)S(1)}, bf16[64,2048]{1,0:T(8,128)(2,1)S(1)}, u32[]{:S(2)}, u32[]{:S(2)}) collective-permute-start(bf16[64,2048]{1,0:T(8,128)(2,1)S(1)} %copy-done.56), channel_id=1, source_target_pairs={{0,2},{1,3},{2,0},{3,1},{4,6},{5,7},{6,4},{7,5},{8,10},{9,11},{10,... | collective-permute-start | bytes 786440 | tf_op jit(solution)/shard_map/ppermute | solution.py:394
  64.0 15.1 %collective-permute-start.4 = (bf16[64,2048]{1,0:T(8,128)(2,1)S(1)}, bf16[64,2048]{1,0:T(8,128)(2,1)S(1)}, u32[]{:S(2)}, u32[]{:S(2)}) collective-permute-start(bf16[64,2048]{1,0:T(8,128)(2,1)S(1)} %copy-done.56), channel_id=1, source_target_pairs={{0,3},{1,0},{2,1},{3,2},{4,7},{5,4},{6,5},{7,6},{8,11},{9,8},{10,9... | collective-permute-start | bytes 786440 | tf_op jit(solution)/shard_map/ppermute | solution.py:394
  79.0 51.6 %collective-permute-start.5 = (bf16[256,2048]{1,0:T(8,128)(2,1)}, bf16[256,2048]{1,0:T(8,128)(2,1)}, u32[]{:S(2)}, u32[]{:S(2)}) collective-permute-start(bf16[256,2048]{1,0:T(8,128)(2,1)} %param.29), channel_id=1, source_target_pairs={{0,1},{1,2},{2,3},{3,0},{4,5},{5,6},{6,7},{7,4},{8,9},{9,10},{10,1... | collective-permute-start | bytes 3145736 | tf_op jit(solution)/shard_map/ppermute | solution.py:394
  107.6 32.4 %collective-permute-start.7 = (bf16[512,2048]{1,0:T(8,128)(2,1)}, bf16[512,2048]{1,0:T(8,128)(2,1)}, u32[]{:S(2)}, u32[]{:S(2)}) collective-permute-start(bf16[512,2048]{1,0:T(8,128)(2,1)} %pad_maximum_fusion.2.refs_0_.refs_8_), channel_id=1, source_target_pairs={{0,4},{4,0},{8,12},{12,8},{16,20},{20,16},{24,28},{28,24},{1,5},{5... | collective-permute-start | bytes 6291464 | tf_op jit(solution)/shard_map/ppermute | solution.py:449
  107.6 32.4 %collective-permute-start.8 = (bf16[512,2048]{1,0:T(8,128)(2,1)}, bf16[512,2048]{1,0:T(8,128)(2,1)}, u32[]{:S(2)}, u32[]{:S(2)}) collective-permute-start(bf16[512,2048]{1,0:T(8,128)(2,1)} %pad_maximum_fusion.3.refs_1_.refs_9_), channel_id=1, source_target_pairs={{0,4},{4,0},{8,12},{12,8},{16,20},{20,16},{24,28},{28,24},{1,5},{5... | collective-permute-start | bytes 6291464 | tf_op jit(solution)/shard_map/ppermute | solution.py:449
  130.6 26.5 %collective-permute-start.6 = (bf16[256,2048]{1,0:T(8,128)(2,1)}, bf16[256,2048]{1,0:T(8,128)(2,1)}, u32[]{:S(2)}, u32[]{:S(2)}) collective-permute-start(bf16[256,2048]{1,0:T(8,128)(2,1)} %collective-permute-done.5), channel_id=1, source_target_pairs={{0,1},{1,2},{2,3},{3,0},{4,5},{5,6},{6,7},{7,4},{8,9},{9,10},{10,1... | collective-permute-start | bytes 3145736 | tf_op jit(solution)/shard_map/ppermute | solution.py:394
  157.1 160.7 %all-gather.11.cloned.1.call-start = ((), (), s32[]{:S(2)}) async-start(), calls=%async_computation.9 | async-start | bytes 5242880 | tf_op jit(solution)/shard_map/all_gather | solution.py:579
  171.7 25.8 %collective-permute-start.9 = (bf16[256,2048]{1,0:T(8,128)(2,1)}, bf16[256,2048]{1,0:T(8,128)(2,1)}, u32[]{:S(2)}, u32[]{:S(2)}) collective-permute-start(bf16[256,2048]{1,0:T(8,128)(2,1)} %collective-permute-done.6), channel_id=1, source_target_pairs={{0,1},{1,2},{2,3},{3,0},{4,5},{5,6},{6,7},{7,4},{8,9},{9,10},{10,1... | collective-permute-start | bytes 3145736 | tf_op jit(solution)/shard_map/ppermute | solution.py:394
  172.6 75.5 %collective-permute-start.13 = (bf16[512,2048]{1,0:T(8,128)(2,1)}, bf16[512,2048]{1,0:T(8,128)(2,1)}, u32[]{:S(2)}, u32[]{:S(2)}) collective-permute-start(bf16[512,2048]{1,0:T(8,128)(2,1)} %pad_maximum_fusion.2.refs_0_.refs_8_), channel_id=1, source_target_pairs={{0,16},{4,20},{8,24},{12,28},{16,0},{20,4},{24,8},{28,12},{1,17},{... | collective-permute-start | bytes 6291464 | tf_op jit(solution)/shard_map/ppermute | solution.py:449
  173.5 74.6 %collective-permute-start.14 = (bf16[512,2048]{1,0:T(8,128)(2,1)}, bf16[512,2048]{1,0:T(8,128)(2,1)}, u32[]{:S(2)}, u32[]{:S(2)}) collective-permute-start(bf16[512,2048]{1,0:T(8,128)(2,1)} %pad_maximum_fusion.3.refs_1_.refs_9_), channel_id=1, source_target_pairs={{0,8},{4,12},{8,0},{12,4},{16,24},{20,28},{24,16},{28,20},{1,9},{5... | collective-permute-start | bytes 6291464 | tf_op jit(solution)/shard_map/ppermute | solution.py:449
  197.4 12.8 %collective-permute-start.10 = (bf16[2,256,256]{2,1,0:T(8,128)(2,1)S(1)}, bf16[2,256,256]{2,1,0:T(8,128)(2,1)S(1)}, u32[]{:S(2)}, u32[]{:S(2)}) collective-permute-start(bf16[2,256,256]{2,1,0:T(8,128)(2,1)S(1)} %bitcast.173), channel_id=1, source_target_pairs={{0,1},{1,2},{2,3},{3,0},{4,5},{5,6},{6,7},{7,4},{8,9},{9,10},{10,1... | collective-permute-start | bytes 786440 | tf_op jit(solution)/shard_map/ppermute | solution.py:394
  197.4 19.1 %collective-permute-start.11 = (bf16[2,256,256]{2,1,0:T(8,128)(2,1)S(1)}, bf16[2,256,256]{2,1,0:T(8,128)(2,1)S(1)}, u32[]{:S(2)}, u32[]{:S(2)}) collective-permute-start(bf16[2,256,256]{2,1,0:T(8,128)(2,1)S(1)} %bitcast.174), channel_id=1, source_target_pairs={{0,2},{1,3},{2,0},{3,1},{4,6},{5,7},{6,4},{7,5},{8,10},{9,11},{10,... | collective-permute-start | bytes 786440 | tf_op jit(solution)/shard_map/ppermute | solution.py:394
  197.6 19.0 %collective-permute-start.12 = (bf16[2,256,256]{2,1,0:T(8,128)(2,1)S(1)}, bf16[2,256,256]{2,1,0:T(8,128)(2,1)S(1)}, u32[]{:S(2)}, u32[]{:S(2)}) collective-permute-start(bf16[2,256,256]{2,1,0:T(8,128)(2,1)S(1)} %bitcast.175), channel_id=1, source_target_pairs={{0,3},{1,0},{2,1},{3,2},{4,7},{5,4},{6,5},{7,6},{8,11},{9,8},{10,9... | collective-permute-start | bytes 786440 | tf_op jit(solution)/shard_map/ppermute | solution.py:394
  201.3 369.1 %reduce-scatter.5.cloned.1.call-start = ((), (), s32[]{:S(2)}) async-start(), calls=%async_computation.10 | async-start | bytes 5242880 | tf_op jit(solution)/shard_map/reduce_scatter | solution.py:634
  248.1 37.8 %collective-permute-start.15 = (bf16[512,2048]{1,0:T(8,128)(2,1)}, bf16[512,2048]{1,0:T(8,128)(2,1)}, u32[]{:S(2)}, u32[]{:S(2)}) collective-permute-start(bf16[512,2048]{1,0:T(8,128)(2,1)} %collective-permute-done.13.refs_0_.refs_12_), channel_id=1, source_target_pairs={{0,4},{4,0},{8,12},{12,8},{16,20},{20,16},{24,28},{28,24},{1,5},{5... | collective-permute-start | bytes 6291464 | tf_op jit(solution)/shard_map/ppermute | solution.py:449
  248.3 34.4 %collective-permute-start.18 = (bf16[256,2048]{1,0:T(8,128)(2,1)S(1)}, bf16[256,2048]{1,0:T(8,128)(2,1)S(1)}, u32[]{:S(2)}, u32[]{:S(2)}) collective-permute-start(bf16[256,2048]{1,0:T(8,128)(2,1)S(1)} %get-tuple-element.317), channel_id=1, source_target_pairs={{0,16},{4,20},{8,24},{12,28},{16,0},{20,4},{24,8},{28,12},{1,17},{... | collective-permute-start | bytes 3145736 | tf_op jit(solution)/shard_map/ppermute | solution.py:449
  249.6 33.4 %collective-permute-start.17 = (bf16[256,2048]{1,0:T(8,128)(2,1)S(1)}, bf16[256,2048]{1,0:T(8,128)(2,1)S(1)}, u32[]{:S(2)}, u32[]{:S(2)}) collective-permute-start(bf16[256,2048]{1,0:T(8,128)(2,1)S(1)} %get-tuple-element.318), channel_id=1, source_target_pairs={{0,8},{4,12},{8,0},{12,4},{16,24},{20,28},{24,16},{28,20},{1,9},{5... | collective-permute-start | bytes 3145736 | tf_op jit(solution)/shard_map/ppermute | solution.py:449
  251.0 36.5 %collective-permute-start.16 = (bf16[512,2048]{1,0:T(8,128)(2,1)}, bf16[512,2048]{1,0:T(8,128)(2,1)}, u32[]{:S(2)}, u32[]{:S(2)}) collective-permute-start(bf16[512,2048]{1,0:T(8,128)(2,1)} %collective-permute-done.14.refs_1_.refs_13_), channel_id=1, source_target_pairs={{0,4},{4,0},{8,12},{12,8},{16,20},{20,16},{24,28},{28,24},{1,5},{5... | collective-permute-start | bytes 6291464 | tf_op jit(solution)/shard_map/ppermute | solution.py:449
  284.7 33.1 %collective-permute-start.19 = (bf16[512,2048]{1,0:T(8,128)(2,1)}, bf16[512,2048]{1,0:T(8,128)(2,1)}, u32[]{:S(2)}, u32[]{:S(2)}) collective-permute-start(bf16[512,2048]{1,0:T(8,128)(2,1)} %pad_maximum_fusion.4.refs_0_), channel_id=1, source_target_pairs={{0,4},{4,0},{8,12},{12,8},{16,20},{20,16},{24,28},{28,24},{1,5},{5... | collective-permute-start | bytes 6291464 | tf_op jit(solution)/shard_map/ppermute | solution.py:449
  285.2 32.6 %collective-permute-start.20 = (bf16[512,2048]{1,0:T(8,128)(2,1)S(1)}, bf16[512,2048]{1,0:T(8,128)(2,1)}, u32[]{:S(2)}, u32[]{:S(2)}) collective-permute-start(bf16[512,2048]{1,0:T(8,128)(2,1)S(1)} %pad_maximum_fusion.5.refs_1_), channel_id=1, source_target_pairs={{0,4},{4,0},{8,12},{12,8},{16,20},{20,16},{24,28},{28,24},{1,5},{5... | collective-permute-start | bytes 6291464 | tf_op jit(solution)/shard_map/ppermute | solution.py:449
  285.2 55.8 %collective-permute-start.21 = (bf16[512,2048]{1,0:T(8,128)(2,1)}, bf16[512,2048]{1,0:T(8,128)(2,1)}, u32[]{:S(2)}, u32[]{:S(2)}) collective-permute-start(bf16[512,2048]{1,0:T(8,128)(2,1)} %pad_maximum_fusion.4.refs_0_), channel_id=1, source_target_pairs={{0,16},{4,20},{8,24},{12,28},{16,0},{20,4},{24,8},{28,12},{1,17},{... | collective-permute-start | bytes 6291464 | tf_op jit(solution)/shard_map/ppermute | solution.py:449
  285.9 55.1 %collective-permute-start.22 = (bf16[512,2048]{1,0:T(8,128)(2,1)S(1)}, bf16[512,2048]{1,0:T(8,128)(2,1)}, u32[]{:S(2)}, u32[]{:S(2)}) collective-permute-start(bf16[512,2048]{1,0:T(8,128)(2,1)S(1)} %pad_maximum_fusion.5.refs_1_), channel_id=1, source_target_pairs={{0,8},{4,12},{8,0},{12,4},{16,24},{20,28},{24,16},{28,20},{1,9},{5... | collective-permute-start | bytes 6291464 | tf_op jit(solution)/shard_map/ppermute | solution.py:449
  341.0 14.5 %collective-permute-start.23 = (bf16[512,2048]{1,0:T(8,128)(2,1)}, bf16[512,2048]{1,0:T(8,128)(2,1)S(1)}, u32[]{:S(2)}, u32[]{:S(2)}) collective-permute-start(bf16[512,2048]{1,0:T(8,128)(2,1)} %collective-permute-done.21.refs_0_.refs_4_), channel_id=1, source_target_pairs={{0,4},{4,0},{8,12},{12,8},{16,20},{20,16},{24,28},{28,24},{1,5},{5... | collective-permute-start | bytes 6291464 | tf_op jit(solution)/shard_map/ppermute | solution.py:449
  341.0 15.8 %collective-permute-start.24 = (bf16[512,2048]{1,0:T(8,128)(2,1)}, bf16[512,2048]{1,0:T(8,128)(2,1)}, u32[]{:S(2)}, u32[]{:S(2)}) collective-permute-start(bf16[512,2048]{1,0:T(8,128)(2,1)} %collective-permute-done.22.refs_1_.refs_5_), channel_id=1, source_target_pairs={{0,4},{4,0},{8,12},{12,8},{16,20},{20,16},{24,28},{28,24},{1,5},{5... | collective-permute-start | bytes 6291464 | tf_op jit(solution)/shard_map/ppermute | solution.py:449
  402.4 48.1 %collective-permute-start.28 = (bf16[512,2048]{1,0:T(8,128)(2,1)}, bf16[512,2048]{1,0:T(8,128)(2,1)S(1)}, u32[]{:S(2)}, u32[]{:S(2)}) collective-permute-start(bf16[512,2048]{1,0:T(8,128)(2,1)} %add_convert_fusion.4), channel_id=1, source_target_pairs={{0,16},{4,20},{8,24},{12,28},{16,0},{20,4},{24,8},{28,12},{1,17},{... | collective-permute-start | bytes 6291464 | tf_op jit(solution)/shard_map/ppermute | solution.py:449
  403.9 47.8 %collective-permute-start.29 = (bf16[512,2048]{1,0:T(8,128)(2,1)}, bf16[512,2048]{1,0:T(8,128)(2,1)S(1)}, u32[]{:S(2)}, u32[]{:S(2)}) collective-permute-start(bf16[512,2048]{1,0:T(8,128)(2,1)} %add_convert_fusion.3), channel_id=1, source_target_pairs={{0,8},{4,12},{8,0},{12,4},{16,24},{20,28},{24,16},{28,20},{1,9},{5... | collective-permute-start | bytes 6291464 | tf_op jit(solution)/shard_map/ppermute | solution.py:449
  456.9 170.9 %reduce-scatter.7.cloned.1.call-start = ((), (), s32[]{:S(2)}) async-start(), calls=%async_computation.11 | async-start | bytes 5242880 | tf_op jit(solution)/shard_map/reduce_scatter | solution.py:640
  463.0 44.7 %collective-permute-start.33 = (bf16[512,2048]{1,0:T(8,128)(2,1)}, bf16[512,2048]{1,0:T(8,128)(2,1)}, u32[]{:S(2)}, u32[]{:S(2)}) collective-permute-start(bf16[512,2048]{1,0:T(8,128)(2,1)} %convolution_convert_fusion.2), channel_id=1, source_target_pairs={{0,4},{4,0},{8,12},{12,8},{16,20},{20,16},{24,28},{28,24},{1,5},{5... | collective-permute-start | bytes 6291464 | tf_op jit(solution)/shard_map/ppermute | solution.py:449
  465.7 34.7 %collective-permute-start.30 = (bf16[256,2048]{1,0:T(8,128)(2,1)}, bf16[256,2048]{1,0:T(8,128)(2,1)}, u32[]{:S(2)}, u32[]{:S(2)}) collective-permute-start(bf16[256,2048]{1,0:T(8,128)(2,1)} %slice.393), channel_id=1, source_target_pairs={{0,8},{4,12},{8,0},{12,4},{16,24},{20,28},{24,16},{28,20},{1,9},{5... | collective-permute-start | bytes 3145736 | tf_op jit(solution)/shard_map/ppermute | solution.py:449
  469.9 32.9 %collective-permute-start.31 = (bf16[256,2048]{1,0:T(8,128)(2,1)}, bf16[256,2048]{1,0:T(8,128)(2,1)}, u32[]{:S(2)}, u32[]{:S(2)}) collective-permute-start(bf16[256,2048]{1,0:T(8,128)(2,1)} %slice.392), channel_id=1, source_target_pairs={{0,16},{4,20},{8,24},{12,28},{16,0},{20,4},{24,8},{28,12},{1,17},{... | collective-permute-start | bytes 3145736 | tf_op jit(solution)/shard_map/ppermute | solution.py:449
  474.2 40.5 %collective-permute-start.32 = (bf16[512,2048]{1,0:T(8,128)(2,1)}, bf16[512,2048]{1,0:T(8,128)(2,1)}, u32[]{:S(2)}, u32[]{:S(2)}) collective-permute-start(bf16[512,2048]{1,0:T(8,128)(2,1)} %convolution_convert_fusion.3), channel_id=1, source_target_pairs={{0,4},{4,0},{8,12},{12,8},{16,20},{20,16},{24,28},{28,24},{1,5},{5... | collective-permute-start | bytes 6291464 | tf_op jit(solution)/shard_map/ppermute | solution.py:449
  521.0 48.1 %collective-permute-start.34 = (bf16[512,2048]{1,0:T(8,128)(2,1)S(1)}, bf16[512,2048]{1,0:T(8,128)(2,1)S(1)}, u32[]{:S(2)}, u32[]{:S(2)}) collective-permute-start(bf16[512,2048]{1,0:T(8,128)(2,1)S(1)} %add_convert_fusion.2), channel_id=1, source_target_pairs={{0,16},{4,20},{8,24},{12,28},{16,0},{20,4},{24,8},{28,12},{1,17},{... | collective-permute-start | bytes 6291464 | tf_op jit(solution)/shard_map/ppermute | solution.py:449
  522.5 47.8 %collective-permute-start.35 = (bf16[512,2048]{1,0:T(8,128)(2,1)S(1)}, bf16[512,2048]{1,0:T(8,128)(2,1)}, u32[]{:S(2)}, u32[]{:S(2)}) collective-permute-start(bf16[512,2048]{1,0:T(8,128)(2,1)S(1)} %add_convert_fusion.1), channel_id=1, source_target_pairs={{0,8},{4,12},{8,0},{12,4},{16,24},{20,28},{24,16},{28,20},{1,9},{5... | collective-permute-start | bytes 6291464 | tf_op jit(solution)/shard_map/ppermute | solution.py:449
  570.4 16.2 %collective-permute-start.36 = (bf16[1024,2048]{1,0:T(8,128)(2,1)}, bf16[1024,2048]{1,0:T(8,128)(2,1)}, u32[]{:S(2)}, u32[]{:S(2)}) collective-permute-start(bf16[1024,2048]{1,0:T(8,128)(2,1)} %convolution_convert_fusion.1), channel_id=1, source_target_pairs={{0,4},{4,0},{8,12},{12,8},{16,20},{20,16},{24,28},{28,24},{1,5},{5... | collective-permute-start | bytes 12582920 | tf_op jit(solution)/shard_map/ppermute | solution.py:449
  579.7 15.0 %collective-permute-start.37 = (bf16[1024,2048]{1,0:T(8,128)(2,1)}, bf16[1024,2048]{1,0:T(8,128)(2,1)}, u32[]{:S(2)}, u32[]{:S(2)}) collective-permute-start(bf16[1024,2048]{1,0:T(8,128)(2,1)} %shard_map.300), channel_id=1, source_target_pairs={{0,4},{4,0},{8,12},{12,8},{16,20},{20,16},{24,28},{28,24},{1,5},{5... | collective-permute-start | bytes 12582920 | tf_op jit(solution)/shard_map/ppermute | solution.py:449
  582.2 29.6 %collective-permute-start.38 = (bf16[2,256,256]{2,1,0:T(8,128)(2,1)S(1)}, bf16[2,256,256]{2,1,0:T(8,128)(2,1)}, u32[]{:S(2)}, u32[]{:S(2)}) collective-permute-start(bf16[2,256,256]{2,1,0:T(8,128)(2,1)S(1)} %get-tuple-element.330), channel_id=1, source_target_pairs={{0,1},{1,2},{2,3},{3,0},{4,5},{5,6},{6,7},{7,4},{8,9},{9,10},{10,1... | collective-permute-start | bytes 786440 | tf_op jit(solution)/shard_map/ppermute | solution.py:394
  582.2 33.4 %collective-permute-start.39 = (bf16[2,256,256]{2,1,0:T(8,128)(2,1)S(1)}, bf16[2,256,256]{2,1,0:T(8,128)(2,1)}, u32[]{:S(2)}, u32[]{:S(2)}) collective-permute-start(bf16[2,256,256]{2,1,0:T(8,128)(2,1)S(1)} %get-tuple-element.329), channel_id=1, source_target_pairs={{0,2},{1,3},{2,0},{3,1},{4,6},{5,7},{6,4},{7,5},{8,10},{9,11},{10,... | collective-permute-start | bytes 786440 | tf_op jit(solution)/shard_map/ppermute | solution.py:394
  584.3 32.5 %collective-permute-start.40 = (bf16[2,256,256]{2,1,0:T(8,128)(2,1)S(1)}, bf16[2,256,256]{2,1,0:T(8,128)(2,1)}, u32[]{:S(2)}, u32[]{:S(2)}) collective-permute-start(bf16[2,256,256]{2,1,0:T(8,128)(2,1)S(1)} %get-tuple-element.328), channel_id=1, source_target_pairs={{0,3},{1,0},{2,1},{3,2},{4,7},{5,4},{6,5},{7,6},{8,11},{9,8},{10,9... | collective-permute-start | bytes 786440 | tf_op jit(solution)/shard_map/ppermute | solution.py:394
  594.7 54.4 %collective-permute-start.41 = (bf16[256,2048]{1,0:T(8,128)(2,1)}, bf16[256,2048]{1,0:T(8,128)(2,1)}, u32[]{:S(2)}, u32[]{:S(2)}) collective-permute-start(bf16[256,2048]{1,0:T(8,128)(2,1)} %get-tuple-element.268), channel_id=1, source_target_pairs={{0,16},{4,20},{8,24},{12,28},{16,0},{20,4},{24,8},{28,12},{1,17},{... | collective-permute-start | bytes 3145736 | tf_op jit(solution)/shard_map/ppermute | solution.py:449
  595.8 53.3 %collective-permute-start.42 = (bf16[256,2048]{1,0:T(8,128)(2,1)}, bf16[256,2048]{1,0:T(8,128)(2,1)}, u32[]{:S(2)}, u32[]{:S(2)}) collective-permute-start(bf16[256,2048]{1,0:T(8,128)(2,1)} %get-tuple-element.269), channel_id=1, source_target_pairs={{0,8},{4,12},{8,0},{12,4},{16,24},{20,28},{24,16},{28,20},{1,9},{5... | collective-permute-start | bytes 3145736 | tf_op jit(solution)/shard_map/ppermute | solution.py:449
  627.9 24.1 %all-to-all-start.1 = ((bf16[8,64,1024]{2,1,0:T(8,128)(2,1)}), bf16[8,64,1024]{2,1,0:T(8,128)(2,1)}, u32[]{:S(2)}, u32[]{:S(2)}) async-start(bf16[8,64,1024]{2,1,0:T(8,128)(2,1)} %reduce-scatter.5.cloned.1.call-done), calls=%async_computation.5 | async-start | bytes 2097152 | tf_op jit(solution)/shard_map/all_to_all | solution.py:753
  632.1 165.9 %reduce-scatter.9.cloned.1.call-start = ((), (), s32[]{:S(2)}) async-start(), calls=%async_computation.12 | async-start | bytes 1310720 | tf_op jit(solution)/shard_map/reduce_scatter | solution.py:692
  638.2 31.4 %collective-permute-start.44 = (bf16[256,2048]{1,0:T(8,128)(2,1)}, bf16[256,2048]{1,0:T(8,128)(2,1)}, u32[]{:S(2)}, u32[]{:S(2)}) collective-permute-start(bf16[256,2048]{1,0:T(8,128)(2,1)} %slice.391), channel_id=1, source_target_pairs={{0,8},{4,12},{8,0},{12,4},{16,24},{20,28},{24,16},{28,20},{1,9},{5... | collective-permute-start | bytes 3145736 | tf_op jit(solution)/shard_map/ppermute | solution.py:449
  642.8 28.4 %collective-permute-start.45 = (bf16[256,2048]{1,0:T(8,128)(2,1)}, bf16[256,2048]{1,0:T(8,128)(2,1)}, u32[]{:S(2)}, u32[]{:S(2)}) collective-permute-start(bf16[256,2048]{1,0:T(8,128)(2,1)} %slice.390), channel_id=1, source_target_pairs={{0,16},{4,20},{8,24},{12,28},{16,0},{20,4},{24,8},{28,12},{1,17},{... | collective-permute-start | bytes 3145736 | tf_op jit(solution)/shard_map/ppermute | solution.py:449
  649.1 33.2 %collective-permute-start.43 = (bf16[1024,2048]{1,0:T(8,128)(2,1)}, bf16[1024,2048]{1,0:T(8,128)(2,1)}, u32[]{:S(2)}, u32[]{:S(2)}) collective-permute-start(bf16[1024,2048]{1,0:T(8,128)(2,1)} %shard_map.303), channel_id=1, source_target_pairs={{0,4},{4,0},{8,12},{12,8},{16,20},{20,16},{24,28},{28,24},{1,5},{5... | collective-permute-start | bytes 12582920 | tf_op jit(solution)/shard_map/ppermute | solution.py:449
  656.7 23.5 %collective-permute-start.46 = (bf16[128,2048]{1,0:T(8,128)(2,1)S(1)}, bf16[128,2048]{1,0:T(8,128)(2,1)S(1)}, u32[]{:S(2)}, u32[]{:S(2)}) collective-permute-start(bf16[128,2048]{1,0:T(8,128)(2,1)S(1)} %slice.397), channel_id=1, source_target_pairs={{0,8},{4,12},{8,0},{12,4},{16,24},{20,28},{24,16},{28,20},{1,9},{5... | collective-permute-start | bytes 1572872 | tf_op jit(solution)/shard_map/ppermute | solution.py:449
  659.3 21.9 %collective-permute-start.47 = (bf16[128,2048]{1,0:T(8,128)(2,1)S(1)}, bf16[128,2048]{1,0:T(8,128)(2,1)S(1)}, u32[]{:S(2)}, u32[]{:S(2)}) collective-permute-start(bf16[128,2048]{1,0:T(8,128)(2,1)S(1)} %slice.396), channel_id=1, source_target_pairs={{0,16},{4,20},{8,24},{12,28},{16,0},{20,4},{24,8},{28,12},{1,17},{... | collective-permute-start | bytes 1572872 | tf_op jit(solution)/shard_map/ppermute | solution.py:449
  720.1 25.9 %collective-permute-start.49 = (bf16[256,2048]{1,0:T(8,128)(2,1)}, bf16[256,2048]{1,0:T(8,128)(2,1)}, u32[]{:S(2)}, u32[]{:S(2)}) collective-permute-start(bf16[256,2048]{1,0:T(8,128)(2,1)} %copy-done.30), channel_id=1, source_target_pairs={{0,16},{4,20},{8,24},{12,28},{16,0},{20,4},{24,8},{28,12},{1,17},{... | collective-permute-start | bytes 3145736 | tf_op jit(solution)/shard_map/ppermute | solution.py:449
  720.8 25.4 %collective-permute-start.50 = (bf16[256,2048]{1,0:T(8,128)(2,1)S(1)}, bf16[256,2048]{1,0:T(8,128)(2,1)}, u32[]{:S(2)}, u32[]{:S(2)}) collective-permute-start(bf16[256,2048]{1,0:T(8,128)(2,1)S(1)} %copy-done.29), channel_id=1, source_target_pairs={{0,8},{4,12},{8,0},{12,4},{16,24},{20,28},{24,16},{28,20},{1,9},{5... | collective-permute-start | bytes 3145736 | tf_op jit(solution)/shard_map/ppermute | solution.py:449
  721.6 85.2 %reduce-scatter.11.cloned.1.call-start = ((), (), s32[]{:S(2)}) async-start(), calls=%async_computation.13 | async-start | bytes 1310720 | tf_op jit(solution)/shard_map/reduce_scatter | solution.py:738
  747.8 14.9 %collective-permute-start.52 = (bf16[128,2048]{1,0:T(8,128)(2,1)S(1)}, bf16[128,2048]{1,0:T(8,128)(2,1)S(1)}, u32[]{:S(2)}, u32[]{:S(2)}) collective-permute-start(bf16[128,2048]{1,0:T(8,128)(2,1)S(1)} %slice.395), channel_id=1, source_target_pairs={{0,8},{4,12},{8,0},{12,4},{16,24},{20,28},{24,16},{28,20},{1,9},{5... | collective-permute-start | bytes 1572872 | tf_op jit(solution)/shard_map/ppermute | solution.py:449
  750.1 14.6 %collective-permute-start.53 = (bf16[128,2048]{1,0:T(8,128)(2,1)S(1)}, bf16[128,2048]{1,0:T(8,128)(2,1)S(1)}, u32[]{:S(2)}, u32[]{:S(2)}) collective-permute-start(bf16[128,2048]{1,0:T(8,128)(2,1)S(1)} %slice.394), channel_id=1, source_target_pairs={{0,16},{4,20},{8,24},{12,28},{16,0},{20,4},{24,8},{28,12},{1,17},{... | collective-permute-start | bytes 1572872 | tf_op jit(solution)/shard_map/ppermute | solution.py:449
  752.8 13.5 %collective-permute-start.51 = (bf16[288,256]{1,0:T(8,128)(2,1)S(1)}, bf16[288,256]{1,0:T(8,128)(2,1)S(1)}, u32[]{:S(2)}, u32[]{:S(2)}) collective-permute-start(bf16[288,256]{1,0:T(8,128)(2,1)S(1)} %get-tuple-element.334), channel_id=1, source_target_pairs={{0,16},{4,20},{8,24},{12,28},{16,0},{20,4},{24,8},{28,12},{1,17},{... | collective-permute-start | bytes 442376 | tf_op jit(solution)/shard_map/ppermute | solution.py:449
  753.6 12.6 %collective-permute-start.55 = (bf16[288,256]{1,0:T(8,128)(2,1)S(1)}, bf16[288,256]{1,0:T(8,128)(2,1)}, u32[]{:S(2)}, u32[]{:S(2)}) collective-permute-start(bf16[288,256]{1,0:T(8,128)(2,1)S(1)} %get-tuple-element.335), channel_id=1, source_target_pairs={{0,8},{4,12},{8,0},{12,4},{16,24},{20,28},{24,16},{28,20},{1,9},{5... | collective-permute-start | bytes 442376 | tf_op jit(solution)/shard_map/ppermute | solution.py:449
  779.7 16.0 %collective-permute-start.57 = (bf16[17664]{0:T(1024)(128)(2,1)S(1)}, bf16[17664]{0:T(1024)(128)(2,1)S(1)}, u32[]{:S(2)}, u32[]{:S(2)}) collective-permute-start(bf16[17664]{0:T(1024)(128)(2,1)S(1)} %get-tuple-element.310), channel_id=1, source_target_pairs={{0,1},{1,2},{2,3},{3,0},{4,5},{5,6},{6,7},{7,4},{8,9},{9,10},{10,1... | collective-permute-start | bytes 105992 | tf_op jit(solution)/shard_map/ppermute | solution.py:394
  786.9 8.8 %collective-permute-start.58 = (bf16[17664]{0:T(1024)(128)(2,1)S(1)}, bf16[17664]{0:T(1024)(128)(2,1)S(1)}, u32[]{:S(2)}, u32[]{:S(2)}) collective-permute-start(bf16[17664]{0:T(1024)(128)(2,1)S(1)} %get-tuple-element.312), channel_id=1, source_target_pairs={{0,2},{1,3},{2,0},{3,1},{4,6},{5,7},{6,4},{7,5},{8,10},{9,11},{10,... | collective-permute-start | bytes 105992 | tf_op jit(solution)/shard_map/ppermute | solution.py:394
  787.0 8.7 %collective-permute-start.59 = (bf16[17664]{0:T(1024)(128)(2,1)S(1)}, bf16[17664]{0:T(1024)(128)(2,1)S(1)}, u32[]{:S(2)}, u32[]{:S(2)}) collective-permute-start(bf16[17664]{0:T(1024)(128)(2,1)S(1)} %get-tuple-element.311), channel_id=1, source_target_pairs={{0,3},{1,0},{2,1},{3,2},{4,7},{5,4},{6,5},{7,6},{8,11},{9,8},{10,9... | collective-permute-start | bytes 105992 | tf_op jit(solution)/shard_map/ppermute | solution.py:394
  (87 other events, 1283.3 us)
Sparse Core Ops, SparseCore 0:
  17.7 35.3 all-gather.4
  59.6 63.8 all-gather.6
  157.2 78.3 all-gather.8
  237.0 80.7 all-gather.10
  457.0 74.3 reduce-scatter.4
  533.7 94.1 reduce-scatter.6
  721.7 31.6 reduce-scatter.8
  775.7 31.1 reduce-scatter.10

commit v14 on v12

--- a/solution.py
+++ b/solution.py
@@ -635,7 +635,6 @@
         two_grad = plane.fold(two_sum)
         down_terms = weight_grad(hid_near + hid_far, grad_lots[0] + grad_lots[1], block)
         two_grad, down_terms, hid_far[0] = tie(two_grad, down_terms, hid_far[0])
-        grad_down = lax.psum_scatter(down_terms, "fsdp", scatter_dimension=0, tiled=True)
         out_far = halves(hid_far, down_part, dot_nn)
         two_grad, *out_far = tie(two_grad, *out_far)
 
@@ -672,9 +671,10 @@
         wq_got = send_rows(wq_parts)
         wq_parts[1], hid_late, out_theirs = tie(wq_parts[1], hid_near[0], out_theirs)
         out_sum = merge(product(hid_late, down_part, "nn", 2, [out_theirs]), out_got)
-        out_sum[0], out_sum[1], att_sib, query_late, grad_down, *kv_got = tie(
-            *out_sum, att_sib, query_grad, grad_down, *kv_got
-        )
+        out_sum[0], out_sum[1], att_sib, query_late, grad_up, down_terms, *kv_got = tie(
+            *out_sum, att_sib, query_grad, grad_up, down_terms, *kv_got
+        )
+        grad_down = lax.psum_scatter(down_terms, "fsdp", scatter_dimension=0, tiled=True)
         branch_out = plane.fold(out_sum)
         wo_sib = product(att_sib, branch_grad, "tn")
         wo_sib, query_late, *wq_got = tie(wo_sib, query_late, *wq_got)
@@ -691,7 +691,7 @@
         grad_wq = lax.psum_scatter(wq_rows, "fsdp", scatter_dimension=0, tiled=True)
 
         one_grad = query_part + dot_nt(kv_grad, full_kv)
-        grad_bq = jnp.sum(query_grad.astype(F32), axis=0)
+        grad_bq = jnp.sum(query_late.astype(F32), axis=0)
         grad_bv = jnp.sum(kv_grad[:, HD:].astype(F32), axis=0)
         grad_gain_one = jnp.sum(one_grad * xhat_one, axis=0)
         grad_shift_one = jnp.sum(one_grad, axis=0)
@@ -733,7 +733,7 @@
         wo_rows = own_rows(wo_parts, wo_got).astype(BF16)
         kv_parts = cut((with_vectors(dot_tn(one_mine, kv_grad), 0) + theirs.astype(F32)).astype(BF16))
         kv_parts_got = send_rows(kv_parts)
-        kv_parts_got[0], wo_rows = tie(kv_parts_got[0], wo_rows)
+        kv_parts_got[0], wo_rows, grad_down = tie(kv_parts_got[0], wo_rows, grad_down)
         grad_wo = lax.psum_scatter(wo_rows, "fsdp", scatter_dimension=0, tiled=True)
 
         kv_last = own_rows(kv_parts, kv_parts_got).reshape(2, -1, 2 * HD)

time: 784 us -> 786 us (level)
  waiting for transfers between devices: 182 us -> 194 us
    ppermute x45, waiting for transfers between devices: 96.2 us -> 105 us  [swap(): return lax.ppermute(block, 'dp', [(i, i ^ bit) for i in range(self.count)])]
    unnamed x190 -> x186, local copies, waits for them, and re-layouts: 28.7 us -> 31.2 us
  transfers between devices with their start and end apart: 70 -> 70, of which waited for: 29 -> 29; matrix products, arithmetic and copies ran while one was open for 24% -> 25% of each run, Pallas kernels for 27% -> 27%
where the time goes in v14:
time: 786 us; the launch traced here: 775 us
  Pallas kernels  242 us (31%)
  waiting for transfers between devices  194 us (25%)
  local copies, waits for them, and re-layouts  86.6 us (11%)
  starting transfers between devices  82.8 us (11%)
  other arithmetic  82.1 us (10%)
  matrix products  72.5 us (9%)
  between operations  15.9 us (2%)
    ppermute x45, waiting for transfers between devices, swap(): return lax.ppermute(block, 'dp', [(i, i ^ bit) for i in range(self.count)])  105 us
    ppermute x15, waiting for transfers between devices, send(): lax.ppermute(block, 'fsdp', [(i, (i + places) % self.count) for i in rang...  62.6 us
    pallas_call x8, Pallas kernels, product(): pl.pallas_call(functools.partial(product_kernel, form, len(extra)), out_s...  57.3 us
    pallas_call x2, Pallas kernels, weight_grad(): pl.pallas_call(functools.partial(weight_kernel, count), out_shape=jax.Sha...  52.2 us
    pallas_call x2, Pallas kernels, middle_layer(): pl.pallas_call(functools.partial(middle_kernel, count), out_shape=[jax.Sh...  41.7 us
    ppermute x15, starting transfers between devices, send(): lax.ppermute(block, 'fsdp', [(i, (i + places) % self.count) for i in rang...  41.4 us
    dot_general x7, matrix products, dot_nn(): return jnp.dot(left, right, preferred_element_type=F32)  36.1 us
    ppermute x45, starting transfers between devices, swap(): return lax.ppermute(block, 'dp', [(i, i ^ bit) for i in range(self.count)])  32.6 us
  transfers between devices with their start and end apart: 70, of which 29 were waited for; matrix products, arithmetic and copies ran while one was open for 25% of the time, Pallas kernels for 27%

profile of v14, /device:TPU:0, one launch (start us, length us, event | category | flops | bytes accessed | tf_op | source)
XLA Modules:
  0.0 775.0 jit_solution(6332537891751242810)
XLA Ops:
  20.3 2.9 collective-permute-start
  25.8 3.6 all-to-all-start
  29.5 17.9 %collective-permute-done = bf16[256,2048]{1,0:T(8,128)(2,1)} collective-permute-done((bf16[256,2048]{1,0:T(8,128)(2,1)S(1)}, bf16[256,2048]{1,0:T(8,128)(2,1)}, u32[]{:S(2)}, u32[]{:S(2)}) %collective-permute-start) | collective-permute-done | bytes 1048608 | tf_op jit(solution)/shard_map/ppermute | solution.py:449
  49.9 3.1 pad_maximum_fusion.3.refs_1_.refs_9_
  53.0 6.3 all-to-all-done
  67.7 3.5 collective-permute-done.2
  71.1 10.4 %collective-permute-done.3 = bf16[64,2048]{1,0:T(8,128)(2,1)} collective-permute-done((bf16[64,2048]{1,0:T(8,128)(2,1)S(1)}, bf16[64,2048]{1,0:T(8,128)(2,1)}, u32[]{:S(2)}, u32[]{:S(2)}) %collective-permute-start.3) | collective-permute-done | bytes 262176 | tf_op jit(solution)/shard_map/ppermute | solution.py:394
  81.6 6.1 collective-permute-start.5
  94.6 17.0 %collective-permute-done.5 = bf16[256,2048]{1,0:T(8,128)(2,1)} collective-permute-done((bf16[256,2048]{1,0:T(8,128)(2,1)}, bf16[256,2048]{1,0:T(8,128)(2,1)}, u32[]{:S(2)}, u32[]{:S(2)}) %collective-permute-start.5) | collective-permute-done | bytes 1048608 | tf_op jit(solution)/shard_map/ppermute | solution.py:394
  111.6 11.5 %all-gather.7.cloned.1.call-done = bf16[2560,2048]{1,0:T(8,128)(2,1)} async-done(((bf16[320,2048]{1,0:T(8,128)(2,1)}), bf16[2560,2048]{1,0:T(8,128)(2,1)}) %all-gather.7.cloned.1.call-update) | async-done | bytes 10485776 | tf_op jit(solution)/shard_map/all_gather | solution.py:533
  135.2 8.2 %slice.292 = bf16[32,64,2048]{2,1,0:T(8,128)(2,1)} slice(bf16[32,80,2048]{2,1,0:T(8,128)(2,1)} %bitcast.152), slice={[0:32], [0:64], [0:2048]} | slice | bytes 16777216 | tf_op jit(solution)/shard_map/slice | solution.py:548
  148.4 9.9 %collective-permute-done.8 = bf16[256,2048]{1,0:T(8,128)(2,1)} collective-permute-done((bf16[256,2048]{1,0:T(8,128)(2,1)}, bf16[256,2048]{1,0:T(8,128)(2,1)}, u32[]{:S(2)}, u32[]{:S(2)}) %collective-permute-start.8) | collective-permute-done | bytes 1048608 | tf_op jit(solution)/shard_map/ppermute | solution.py:394
  162.1 8.2 %add_convert_fusion.6.q_ref = bf16[512,2048]{1,0:T(8,128)(2,1)S(1)} fusion(bf16[512,2048]{1,0:T(8,128)(2,1)S(1)} %fusion.12.first_ref.second_ref, bf16[2048,2048]{1,0:T(8,128)(2,1)} %bitcast.149, f32[2048]{0:T(1024)S(1)} %reshape.386), kind=kOutput, calls=%fused_computation.42 | convolution fusion | flops 4297064448 | bytes 12591104 | tf_op jit(solution)/shard_map/dot_general | solution.py:21
  170.4 8.9 %collective-permute-done.10 = bf16[2,256,256]{2,1,0:T(8,128)(2,1)S(1)} collective-permute-done((bf16[2,256,256]{2,1,0:T(8,128)(2,1)S(1)}, bf16[2,256,256]{2,1,0:T(8,128)(2,1)S(1)}, u32[]{:S(2)}, u32[]{:S(2)}) %collective-permute-start.10) | collective-permute-done | bytes 262176 | tf_op jit(solution)/shard_map/ppermute | solution.py:394
  179.2 5.1 collective-permute-start.12
  187.4 18.8 %shard_map.288 = (bf16[512,2048]{1,0:T(8,128)(2,1)S(1)}, f32[512,128]{1,0:T(8,128)S(1)}) custom-call(s32[1]{0:T(128)} %bitcast.1.pos_ref, s32[2,8]{1,0:T(2,128)S(1)} %select_reduce_fusion.ends_ref, bf16[512,2048]{1,0:T(8,128)(2,1)S(1)} %add_convert_fusion.6.q_ref, bf16[2,1024,256]{2,1,0:T(8,128)(2,1)S(1)} %constant_dynamic-update-slice_fusion.15.kv_ref), custom_call_target="tpu_custom_call" | custom-call | flops 67108864 | bytes 65536 | tf_op jit(solution)/shard_map/pallas_call | solution.py:132
  208.5 13.0 %collective-permute-done.12 = bf16[256,2048]{1,0:T(8,128)(2,1)} collective-permute-done((bf16[256,2048]{1,0:T(8,128)(2,1)}, bf16[256,2048]{1,0:T(8,128)(2,1)}, u32[]{:S(2)}, u32[]{:S(2)}) %collective-permute-start.12) | collective-permute-done | bytes 1048608 | tf_op jit(solution)/shard_map/ppermute | solution.py:394
  221.4 9.3 %fusion.48 = (f32[512]{0:T(512)S(1)}, f32[512,2048]{1,0:T(8,128)S(1)}) fusion(f32[2048]{0:T(1024)S(1)} %reshape.387, bf16[512,2048]{1,0:T(8,128)(2,1)} %copy-done.6, bf16[2048,2048]{1,0:T(8,128)(2,1)} %all-gather.9.cloned.1.call-done, bf16[2,256,2048]{2,1,0:T(8,128)(2,1)} %param.17), kind=kOutput, calls=%fused_computation.184 | convolution fusion | flops 4299161088 | bytes 16787456 | tf_op jit(solution)/shard_map/dot_general | solution.py:21
  241.7 13.6 %shard_map.289.refs_4_ = bf16[2048,1024]{1,0:T(8,128)(2,1)} custom-call(bf16[512,2048]{1,0:T(8,128)(2,1)S(1)} %copy-done.8, bf16[512,2048]{1,0:T(8,128)(2,1)S(1)} %copy-done.9, bf16[512,2048]{1,0:T(8,128)(2,1)} %collective-permute-done.6.refs_2_.refs_10_, bf16[512,2048]{1,0:T(8,128)(2,1)} %collective-permute-done.7.refs_3_.refs_11_, ...), custom_call_target="tpu_custom_call" | custom-call | flops 134217728 | bytes 262144 | tf_op jit(solution)/shard_map/pallas_call | solution.py:240
  255.3 3.3 collective-permute-done.17
  263.8 14.6 %shard_map.290.refs_4_ = bf16[2048,1024]{1,0:T(8,128)(2,1)} custom-call(bf16[512,2048]{1,0:T(8,128)(2,1)} %collective-permute-done.13.refs_0_.refs_12_, bf16[512,2048]{1,0:T(8,128)(2,1)} %collective-permute-done.14.refs_1_.refs_13_, bf16[512,2048]{1,0:T(8,128)(2,1)} %collective-permute-done.15.refs_2_.refs_14_, ...), custom_call_target="tpu_custom_call" | custom-call | flops 134217728 | bytes 262144 | tf_op jit(solution)/shard_map/pallas_call | solution.py:240
  278.5 20.5 %shard_map.291 = (bf16[1024,1024]{1,0:T(8,128)(2,1)S(1)}, bf16[1024,1024]{1,0:T(8,128)(2,1)S(1)}, bf16[1024,1024]{1,0:T(8,128)(2,1)}, bf16[1024,1024]{1,0:T(8,128)(2,1)}, f32[1,1024]{1,0:T(1,128)S(1)}) custom-call(bf16[512,2048]{1,0:T(8,128)(2,1)} %copy-done.46, bf16[512,2048]{1,0:T(8,128)(2,1)} %pad_maximum_fusion.5.refs_1_, ...), custom_call_target="tpu_custom_call" | custom-call | flops 134217728 | bytes 393216 | tf_op jit(solution)/shard_map/pallas_call | solution.py:206
  301.5 8.1 %collective-permute-done.21.refs_0_.refs_4_ = bf16[512,2048]{1,0:T(8,128)(2,1)} collective-permute-done((bf16[512,2048]{1,0:T(8,128)(2,1)S(1)}, bf16[512,2048]{1,0:T(8,128)(2,1)}, u32[]{:S(2)}, u32[]{:S(2)}) %collective-permute-start.21) | collective-permute-done | bytes 2097184 | tf_op jit(solution)/shard_map/ppermute | solution.py:449
  311.2 6.6 shard_map.292
  317.8 6.6 shard_map.293
  325.7 21.2 %shard_map.294 = (bf16[1024,1024]{1,0:T(8,128)(2,1)S(1)}, bf16[1024,1024]{1,0:T(8,128)(2,1)S(1)}, bf16[1024,1024]{1,0:T(8,128)(2,1)}, bf16[1024,1024]{1,0:T(8,128)(2,1)}, f32[1,1024]{1,0:T(1,128)S(1)}) custom-call(bf16[512,2048]{1,0:T(8,128)(2,1)} %collective-permute-done.21.refs_0_.refs_4_, bf16[512,2048]{1,0:T(8,128)(2,1)} %collective-permute-done.22.refs_1_.refs_5_, ...), custom_call_target="tpu_custom_call" | custom-call | flops 134217728 | bytes 393216 | tf_op jit(solution)/shard_map/pallas_call | solution.py:206
  347.0 4.5 convolution_convert_fusion.5
  355.8 3.7 add_convert_fusion.4
  359.5 3.8 add_convert_fusion.3
  363.2 7.8 %shard_map.295 = bf16[1024,2048]{1,0:T(8,128)(2,1)} custom-call(bf16[1024,1024]{1,0:T(8,128)(2,1)S(1)} %copy-done.14, bf16[2048,1024]{1,0:T(8,128)(2,1)} %bitcast.143), custom_call_target="tpu_custom_call" | custom-call | flops 67108864 | bytes 163840 | tf_op jit(solution)/shard_map/pallas_call | solution.py:354
  373.6 4.8 collective-permute-done.27.refs_0_
  378.4 25.8 %shard_map.296 = bf16[2048,1024]{1,0:T(8,128)(2,1)} custom-call(bf16[512,2048]{1,0:T(8,128)(2,1)} %copy-done.46, bf16[512,2048]{1,0:T(8,128)(2,1)} %pad_maximum_fusion.5.refs_1_, bf16[512,2048]{1,0:T(8,128)(2,1)} %collective-permute-done.19.refs_2_, bf16[512,2048]{1,0:T(8,128)(2,1)} %collective-permute-done.20.refs_3_, ...), custom_call_target="tpu_custom_call" | custom-call | flops 17179869184 | bytes 29360128 | tf_op jit(solution)/shard_map/pallas_call | solution.py:280
  404.3 8.7 %shard_map.297 = (bf16[512,2048]{1,0:T(8,128)(2,1)S(1)}, bf16[512,2048]{1,0:T(8,128)(2,1)S(1)}) custom-call(bf16[1024,1024]{1,0:T(8,128)(2,1)} %get-tuple-element.232.refs_8_.refs_9_.values_ref, bf16[2048,1024]{1,0:T(8,128)(2,1)} %bitcast.144, bf16[1024,2048]{1,0:T(8,128)(2,1)} %copy-done.51), custom_call_target="tpu_custom_call" | custom-call | flops 67108864 | bytes 163840 | tf_op jit(solution)/shard_map/pallas_call | solution.py:354
  413.0 6.3 collective-permute-done.28
  427.2 6.0 convolution_convert_fusion.3
  433.2 3.7 convolution_convert_fusion.2
  437.4 26.3 %shard_map.298 = bf16[1024,2048]{1,0:T(8,128)(2,1)} custom-call(bf16[1024,1024]{1,0:T(8,128)(2,1)} %copy-done.11, bf16[1024,1024]{1,0:T(8,128)(2,1)} %copy-done.11, bf16[1024,1024]{1,0:T(8,128)(2,1)} %copy-done.12, bf16[1024,1024]{1,0:T(8,128)(2,1)} %copy-done.12, bf16[1024,1024]{1,0:T(8,128)(2,1)} %copy-done.26, bf16[1024,1024]{1,0:T(8,128)(2,1)} %copy-done.26, ...), custom_call_target="tpu_custom_call" | custom-call | flops 17179869184 | bytes 29360128 | tf_op jit(solution)/shard_map/pallas_call | solution.py:280
  471.3 4.0 add_convert_fusion.2
  486.3 10.1 %convolution_convert_fusion.6.grad_ref = bf16[512,2048]{1,0:T(8,128)(2,1)} fusion(bf16[512,2048]{1,0:T(8,128)(2,1)S(1)} %convert_element_type.418.weight_ref, bf16[2048,2048]{1,0:T(8,128)(2,1)} %all-gather.9.cloned.1.call-done), kind=kOutput, calls=%fused_computation.52 | convolution fusion | flops 4296015872 | bytes 12582912 | tf_op jit(solution)/shard_map/dot_general | solution.py:25
  496.4 30.4 %shard_map.299 = (bf16[512,2048]{1,0:T(8,128)(2,1)S(1)}, bf16[2,1024,256]{2,1,0:T(8,128)(2,1)S(1)}) custom-call(s32[1]{0:T(128)} %bitcast.1.pos_ref, s32[2,8]{1,0:T(2,128)S(1)} %copy-done.25, bf16[512,2048]{1,0:T(8,128)(2,1)} %copy-done.5, bf16[2,1024,256]{2,1,0:T(8,128)(2,1)S(1)} %copy-done.4, f32[512,128]{1,0:T(8,128)S(1)} %get-tuple-element.218.norm_ref, ...), custom_call_target="tpu_custom_call" | custom-call | flops 167772160 | bytes 163840 | tf_op jit(solution)/shard_map/pallas_call | solution.py:152
  526.8 4.3 convolution_convert_fusion.1
  534.1 7.7 shard_map.300
  544.2 11.3 %collective-permute-start.38 = (bf16[2,256,256]{2,1,0:T(8,128)(2,1)S(1)}, bf16[2,256,256]{2,1,0:T(8,128)(2,1)S(1)}, u32[]{:S(2)}, u32[]{:S(2)}) collective-permute-start(bf16[2,256,256]{2,1,0:T(8,128)(2,1)S(1)} %get-tuple-element.336), channel_id=1, source_target_pairs={{0,1},{1,2},{2,3},{3,0},{4,5},{5,6},{6,7},{7,4},{8,9},{9,10},{10,1... | collective-permute-start | bytes 786440 | tf_op jit(solution)/shard_map/ppermute | solution.py:394
  555.5 3.1 collective-permute-start.39
  558.6 2.9 collective-permute-start.40
  561.5 5.4 shard_map.301
  570.8 8.0 %shard_map.302 = (bf16[512,2048]{1,0:T(8,128)(2,1)S(1)}, bf16[512,2048]{1,0:T(8,128)(2,1)S(1)}) custom-call(bf16[1024,1024]{1,0:T(8,128)(2,1)} %copy-done.11, bf16[1024,2048]{1,0:T(8,128)(2,1)} %copy-done.33, bf16[1024,2048]{1,0:T(8,128)(2,1)} %collective-permute-done.37.refs_0_), custom_call_target="tpu_custom_call" | custom-call | flops 67108864 | bytes 163840 | tf_op jit(solution)/shard_map/pallas_call | solution.py:354
  578.9 2.7 convert_add_fusion.2
  581.6 4.3 convert_add_fusion.1
  586.0 4.4 all-to-all-start.1
  597.0 2.8 slice.390
  600.4 2.7 slice.391
  603.3 4.8 shard_map.303
  612.4 15.4 %collective-permute-done.41 = bf16[256,2048]{1,0:T(8,128)(2,1)} collective-permute-done((bf16[256,2048]{1,0:T(8,128)(2,1)}, bf16[256,2048]{1,0:T(8,128)(2,1)}, u32[]{:S(2)}, u32[]{:S(2)}) %collective-permute-start.41) | collective-permute-done | bytes 1048608 | tf_op jit(solution)/shard_map/ppermute | solution.py:449
  638.4 11.9 %collective-permute-done.45 = bf16[256,2048]{1,0:T(8,128)(2,1)} collective-permute-done((bf16[256,2048]{1,0:T(8,128)(2,1)}, bf16[256,2048]{1,0:T(8,128)(2,1)}, u32[]{:S(2)}, u32[]{:S(2)}) %collective-permute-start.45) | collective-permute-done | bytes 1048608 | tf_op jit(solution)/shard_map/ppermute | solution.py:449
  657.7 8.7 %shard_map.304 = f32[512,2048]{1,0:T(8,128)} custom-call(bf16[512,2048]{1,0:T(8,128)(2,1)S(1)} %copy-done.2, bf16[2048,2048]{1,0:T(8,128)(2,1)} %bitcast.150), custom_call_target="tpu_custom_call" | custom-call | flops 67108864 | bytes 196608 | tf_op jit(solution)/shard_map/pallas_call | solution.py:354
  670.0 6.0 shard_map.305
  677.3 6.2 fusion.18
  692.1 18.9 %collective-permute-done.49 = bf16[256,2048]{1,0:T(8,128)(2,1)} collective-permute-done((bf16[256,2048]{1,0:T(8,128)(2,1)}, bf16[256,2048]{1,0:T(8,128)(2,1)}, u32[]{:S(2)}, u32[]{:S(2)}) %collective-permute-start.49) | collective-permute-done | bytes 1048608 | tf_op jit(solution)/shard_map/ppermute | solution.py:449
  720.2 6.6 collective-permute-done.53
  726.9 3.4 collective-permute-done.52
  733.7 5.4 fusion.17
  746.6 5.8 add_convert_fusion
  758.3 7.9 %reduce-scatter.11.cloned.1.call-done = bf16[64,2048]{1,0:T(8,128)(2,1)} async-done(((bf16[256,2048]{1,0:T(8,128)(2,1)}), bf16[64,2048]{1,0:T(8,128)(2,1)}) %reduce-scatter.11.cloned.1.call-update) | async-done | bytes 262160 | tf_op jit(solution)/shard_map/reduce_scatter | solution.py:737
  (465 shorter events, 194.3 us)
Async XLA Ops:
  7.2 52.1 %all-gather.5.cloned.1.call-start = ((), (), s32[]{:S(2)}) async-start(), calls=%async_computation.6 | async-start | bytes 1638400 | tf_op jit(solution)/shard_map/all_gather | solution.py:528
  20.3 27.0 %collective-permute-start = (bf16[256,2048]{1,0:T(8,128)(2,1)S(1)}, bf16[256,2048]{1,0:T(8,128)(2,1)}, u32[]{:S(2)}, u32[]{:S(2)}) collective-permute-start(bf16[256,2048]{1,0:T(8,128)(2,1)S(1)} %get-tuple-element.326), channel_id=1, source_target_pairs={{0,8},{4,12},{8,0},{12,4},{16,24},{20,28},{24,16},{28,20},{1,9},{5... | collective-permute-start | bytes 3145736 | tf_op jit(solution)/shard_map/ppermute | solution.py:449
  23.2 26.7 %collective-permute-start.1 = (bf16[256,2048]{1,0:T(8,128)(2,1)}, bf16[256,2048]{1,0:T(8,128)(2,1)}, u32[]{:S(2)}, u32[]{:S(2)}) collective-permute-start(bf16[256,2048]{1,0:T(8,128)(2,1)} %get-tuple-element.325), channel_id=1, source_target_pairs={{0,16},{4,20},{8,24},{12,28},{16,0},{20,4},{24,8},{28,12},{1,17},{... | collective-permute-start | bytes 3145736 | tf_op jit(solution)/shard_map/ppermute | solution.py:449
  25.8 33.5 %all-to-all-start = ((bf16[64,8,1024]{2,0,1:T(8,128)(2,1)}), bf16[64,8,1024]{2,0,1:T(8,128)(2,1)S(1)}, u32[]{:S(2)}, u32[]{:S(2)}) async-start(bf16[64,8,1024]{2,0,1:T(8,128)(2,1)} %bitcast.137), calls=%async_computation | async-start | bytes 2097152 | tf_op jit(solution)/shard_map/all_to_all | solution.py:530
  29.4 93.7 %all-gather.7.cloned.1.call-start = ((), (), s32[]{:S(2)}) async-start(), calls=%async_computation.7 | async-start | bytes 11796480 | tf_op jit(solution)/shard_map/all_gather | solution.py:533
  59.3 162.1 %all-gather.9.cloned.1.call-start = ((), (), s32[]{:S(2)}) async-start(), calls=%async_computation.8 | async-start | bytes 9437184 | tf_op jit(solution)/shard_map/all_gather | solution.py:546
  59.4 52.2 %collective-permute-start.6 = (bf16[512,2048]{1,0:T(8,128)(2,1)S(1)}, bf16[512,2048]{1,0:T(8,128)(2,1)}, u32[]{:S(2)}, u32[]{:S(2)}) collective-permute-start(bf16[512,2048]{1,0:T(8,128)(2,1)S(1)} %pad_maximum_fusion.2.refs_0_.refs_8_), channel_id=1, source_target_pairs={{0,4},{4,0},{8,12},{12,8},{16,20},{20,16},{24,28},{28,24},{1,5},{5... | collective-permute-start | bytes 6291464 | tf_op jit(solution)/shard_map/ppermute | solution.py:449
  59.4 52.1 %collective-permute-start.7 = (bf16[512,2048]{1,0:T(8,128)(2,1)}, bf16[512,2048]{1,0:T(8,128)(2,1)}, u32[]{:S(2)}, u32[]{:S(2)}) collective-permute-start(bf16[512,2048]{1,0:T(8,128)(2,1)} %pad_maximum_fusion.3.refs_1_.refs_9_), channel_id=1, source_target_pairs={{0,4},{4,0},{8,12},{12,8},{16,20},{20,16},{24,28},{28,24},{1,5},{5... | collective-permute-start | bytes 6291464 | tf_op jit(solution)/shard_map/ppermute | solution.py:449
  59.9 11.2 %collective-permute-start.2 = (bf16[64,2048]{1,0:T(8,128)(2,1)S(1)}, bf16[64,2048]{1,0:T(8,128)(2,1)}, u32[]{:S(2)}, u32[]{:S(2)}) collective-permute-start(bf16[64,2048]{1,0:T(8,128)(2,1)S(1)} %copy-done.64), channel_id=1, source_target_pairs={{0,1},{1,2},{2,3},{3,0},{4,5},{5,6},{6,7},{7,4},{8,9},{9,10},{10,1... | collective-permute-start | bytes 786440 | tf_op jit(solution)/shard_map/ppermute | solution.py:394
  61.5 20.0 %collective-permute-start.3 = (bf16[64,2048]{1,0:T(8,128)(2,1)S(1)}, bf16[64,2048]{1,0:T(8,128)(2,1)}, u32[]{:S(2)}, u32[]{:S(2)}) collective-permute-start(bf16[64,2048]{1,0:T(8,128)(2,1)S(1)} %copy-done.64), channel_id=1, source_target_pairs={{0,2},{1,3},{2,0},{3,1},{4,6},{5,7},{6,4},{7,5},{8,10},{9,11},{10,... | collective-permute-start | bytes 786440 | tf_op jit(solution)/shard_map/ppermute | solution.py:394
  64.1 17.5 %collective-permute-start.4 = (bf16[64,2048]{1,0:T(8,128)(2,1)S(1)}, bf16[64,2048]{1,0:T(8,128)(2,1)}, u32[]{:S(2)}, u32[]{:S(2)}) collective-permute-start(bf16[64,2048]{1,0:T(8,128)(2,1)S(1)} %copy-done.64), channel_id=1, source_target_pairs={{0,3},{1,0},{2,1},{3,2},{4,7},{5,4},{6,5},{7,6},{8,11},{9,8},{10,9... | collective-permute-start | bytes 786440 | tf_op jit(solution)/shard_map/ppermute | solution.py:394
  81.6 30.0 %collective-permute-start.5 = (bf16[256,2048]{1,0:T(8,128)(2,1)}, bf16[256,2048]{1,0:T(8,128)(2,1)}, u32[]{:S(2)}, u32[]{:S(2)}) collective-permute-start(bf16[256,2048]{1,0:T(8,128)(2,1)} %param.29), channel_id=1, source_target_pairs={{0,1},{1,2},{2,3},{3,0},{4,5},{5,6},{6,7},{7,4},{8,9},{9,10},{10,1... | collective-permute-start | bytes 3145736 | tf_op jit(solution)/shard_map/ppermute | solution.py:394
  123.1 155.4 %all-gather.11.cloned.1.call-start = ((), (), s32[]{:S(2)}) async-start(), calls=%async_computation.9 | async-start | bytes 5242880 | tf_op jit(solution)/shard_map/all_gather | solution.py:577
  130.8 27.5 %collective-permute-start.8 = (bf16[256,2048]{1,0:T(8,128)(2,1)}, bf16[256,2048]{1,0:T(8,128)(2,1)}, u32[]{:S(2)}, u32[]{:S(2)}) collective-permute-start(bf16[256,2048]{1,0:T(8,128)(2,1)} %collective-permute-done.5), channel_id=1, source_target_pairs={{0,1},{1,2},{2,3},{3,0},{4,5},{5,6},{6,7},{7,4},{8,9},{9,10},{10,1... | collective-permute-start | bytes 3145736 | tf_op jit(solution)/shard_map/ppermute | solution.py:394
  158.3 12.0 %collective-permute-start.9 = (bf16[2,256,256]{2,1,0:T(8,128)(2,1)S(1)}, bf16[2,256,256]{2,1,0:T(8,128)(2,1)S(1)}, u32[]{:S(2)}, u32[]{:S(2)}) collective-permute-start(bf16[2,256,256]{2,1,0:T(8,128)(2,1)S(1)} %bitcast.173), channel_id=1, source_target_pairs={{0,1},{1,2},{2,3},{3,0},{4,5},{5,6},{6,7},{7,4},{8,9},{9,10},{10,1... | collective-permute-start | bytes 786440 | tf_op jit(solution)/shard_map/ppermute | solution.py:394
  158.3 20.9 %collective-permute-start.10 = (bf16[2,256,256]{2,1,0:T(8,128)(2,1)S(1)}, bf16[2,256,256]{2,1,0:T(8,128)(2,1)S(1)}, u32[]{:S(2)}, u32[]{:S(2)}) collective-permute-start(bf16[2,256,256]{2,1,0:T(8,128)(2,1)S(1)} %bitcast.174), channel_id=1, source_target_pairs={{0,2},{1,3},{2,0},{3,1},{4,6},{5,7},{6,4},{7,5},{8,10},{9,11},{10,... | collective-permute-start | bytes 786440 | tf_op jit(solution)/shard_map/ppermute | solution.py:394
  160.4 18.8 %collective-permute-start.11 = (bf16[2,256,256]{2,1,0:T(8,128)(2,1)S(1)}, bf16[2,256,256]{2,1,0:T(8,128)(2,1)S(1)}, u32[]{:S(2)}, u32[]{:S(2)}) collective-permute-start(bf16[2,256,256]{2,1,0:T(8,128)(2,1)S(1)} %bitcast.175), channel_id=1, source_target_pairs={{0,3},{1,0},{2,1},{3,2},{4,7},{5,4},{6,5},{7,6},{8,11},{9,8},{10,9... | collective-permute-start | bytes 786440 | tf_op jit(solution)/shard_map/ppermute | solution.py:394
  179.2 42.2 %collective-permute-start.12 = (bf16[256,2048]{1,0:T(8,128)(2,1)}, bf16[256,2048]{1,0:T(8,128)(2,1)}, u32[]{:S(2)}, u32[]{:S(2)}) collective-permute-start(bf16[256,2048]{1,0:T(8,128)(2,1)} %collective-permute-done.8), channel_id=1, source_target_pairs={{0,1},{1,2},{2,3},{3,0},{4,5},{5,6},{6,7},{7,4},{8,9},{9,10},{10,1... | collective-permute-start | bytes 3145736 | tf_op jit(solution)/shard_map/ppermute | solution.py:394
  184.6 48.1 %collective-permute-start.13 = (bf16[512,2048]{1,0:T(8,128)(2,1)}, bf16[512,2048]{1,0:T(8,128)(2,1)}, u32[]{:S(2)}, u32[]{:S(2)}) collective-permute-start(bf16[512,2048]{1,0:T(8,128)(2,1)} %copy-done.7), channel_id=1, source_target_pairs={{0,16},{4,20},{8,24},{12,28},{16,0},{20,4},{24,8},{28,12},{1,17},{... | collective-permute-start | bytes 6291464 | tf_op jit(solution)/shard_map/ppermute | solution.py:449
  185.7 47.1 %collective-permute-start.14 = (bf16[512,2048]{1,0:T(8,128)(2,1)}, bf16[512,2048]{1,0:T(8,128)(2,1)}, u32[]{:S(2)}, u32[]{:S(2)}) collective-permute-start(bf16[512,2048]{1,0:T(8,128)(2,1)} %pad_maximum_fusion.3.refs_1_.refs_9_), channel_id=1, source_target_pairs={{0,8},{4,12},{8,0},{12,4},{16,24},{20,28},{24,16},{28,20},{1,9},{5... | collective-permute-start | bytes 6291464 | tf_op jit(solution)/shard_map/ppermute | solution.py:449
  186.7 345.8 %reduce-scatter.5.cloned.1.call-start = ((), (), s32[]{:S(2)}) async-start(), calls=%async_computation.10 | async-start | bytes 5242880 | tf_op jit(solution)/shard_map/reduce_scatter | solution.py:632
  232.8 29.6 %collective-permute-start.15 = (bf16[512,2048]{1,0:T(8,128)(2,1)}, bf16[512,2048]{1,0:T(8,128)(2,1)}, u32[]{:S(2)}, u32[]{:S(2)}) collective-permute-start(bf16[512,2048]{1,0:T(8,128)(2,1)} %collective-permute-done.13.refs_0_.refs_12_), channel_id=1, source_target_pairs={{0,4},{4,0},{8,12},{12,8},{16,20},{20,16},{24,28},{28,24},{1,5},{5... | collective-permute-start | bytes 6291464 | tf_op jit(solution)/shard_map/ppermute | solution.py:449
  233.0 25.6 %collective-permute-start.17 = (bf16[256,2048]{1,0:T(8,128)(2,1)S(1)}, bf16[256,2048]{1,0:T(8,128)(2,1)S(1)}, u32[]{:S(2)}, u32[]{:S(2)}) collective-permute-start(bf16[256,2048]{1,0:T(8,128)(2,1)S(1)} %get-tuple-element.324), channel_id=1, source_target_pairs={{0,8},{4,12},{8,0},{12,4},{16,24},{20,28},{24,16},{28,20},{1,9},{5... | collective-permute-start | bytes 3145736 | tf_op jit(solution)/shard_map/ppermute | solution.py:449
  234.3 29.5 %collective-permute-start.16 = (bf16[512,2048]{1,0:T(8,128)(2,1)}, bf16[512,2048]{1,0:T(8,128)(2,1)}, u32[]{:S(2)}, u32[]{:S(2)}) collective-permute-start(bf16[512,2048]{1,0:T(8,128)(2,1)} %collective-permute-done.14.refs_1_.refs_13_), channel_id=1, source_target_pairs={{0,4},{4,0},{8,12},{12,8},{16,20},{20,16},{24,28},{28,24},{1,5},{5... | collective-permute-start | bytes 6291464 | tf_op jit(solution)/shard_map/ppermute | solution.py:449
  234.5 25.4 %collective-permute-start.18 = (bf16[256,2048]{1,0:T(8,128)(2,1)S(1)}, bf16[256,2048]{1,0:T(8,128)(2,1)S(1)}, u32[]{:S(2)}, u32[]{:S(2)}) collective-permute-start(bf16[256,2048]{1,0:T(8,128)(2,1)S(1)} %get-tuple-element.323), channel_id=1, source_target_pairs={{0,16},{4,20},{8,24},{12,28},{16,0},{20,4},{24,8},{28,12},{1,17},{... | collective-permute-start | bytes 3145736 | tf_op jit(solution)/shard_map/ppermute | solution.py:449
  261.4 17.0 %collective-permute-start.19 = (bf16[512,2048]{1,0:T(8,128)(2,1)S(1)}, bf16[512,2048]{1,0:T(8,128)(2,1)}, u32[]{:S(2)}, u32[]{:S(2)}) collective-permute-start(bf16[512,2048]{1,0:T(8,128)(2,1)S(1)} %pad_maximum_fusion.4.refs_0_), channel_id=1, source_target_pairs={{0,4},{4,0},{8,12},{12,8},{16,20},{20,16},{24,28},{28,24},{1,5},{5... | collective-permute-start | bytes 6291464 | tf_op jit(solution)/shard_map/ppermute | solution.py:449
  261.4 17.0 %collective-permute-start.20 = (bf16[512,2048]{1,0:T(8,128)(2,1)}, bf16[512,2048]{1,0:T(8,128)(2,1)}, u32[]{:S(2)}, u32[]{:S(2)}) collective-permute-start(bf16[512,2048]{1,0:T(8,128)(2,1)} %pad_maximum_fusion.5.refs_1_), channel_id=1, source_target_pairs={{0,4},{4,0},{8,12},{12,8},{16,20},{20,16},{24,28},{28,24},{1,5},{5... | collective-permute-start | bytes 6291464 | tf_op jit(solution)/shard_map/ppermute | solution.py:449
  262.0 47.6 %collective-permute-start.21 = (bf16[512,2048]{1,0:T(8,128)(2,1)S(1)}, bf16[512,2048]{1,0:T(8,128)(2,1)}, u32[]{:S(2)}, u32[]{:S(2)}) collective-permute-start(bf16[512,2048]{1,0:T(8,128)(2,1)S(1)} %pad_maximum_fusion.4.refs_0_), channel_id=1, source_target_pairs={{0,16},{4,20},{8,24},{12,28},{16,0},{20,4},{24,8},{28,12},{1,17},{... | collective-permute-start | bytes 6291464 | tf_op jit(solution)/shard_map/ppermute | solution.py:449
  262.3 47.6 %collective-permute-start.22 = (bf16[512,2048]{1,0:T(8,128)(2,1)}, bf16[512,2048]{1,0:T(8,128)(2,1)}, u32[]{:S(2)}, u32[]{:S(2)}) collective-permute-start(bf16[512,2048]{1,0:T(8,128)(2,1)} %pad_maximum_fusion.5.refs_1_), channel_id=1, source_target_pairs={{0,8},{4,12},{8,0},{12,4},{16,24},{20,28},{24,16},{28,20},{1,9},{5... | collective-permute-start | bytes 6291464 | tf_op jit(solution)/shard_map/ppermute | solution.py:449
  309.9 14.5 %collective-permute-start.23 = (bf16[512,2048]{1,0:T(8,128)(2,1)}, bf16[512,2048]{1,0:T(8,128)(2,1)S(1)}, u32[]{:S(2)}, u32[]{:S(2)}) collective-permute-start(bf16[512,2048]{1,0:T(8,128)(2,1)} %collective-permute-done.21.refs_0_.refs_4_), channel_id=1, source_target_pairs={{0,4},{4,0},{8,12},{12,8},{16,20},{20,16},{24,28},{28,24},{1,5},{5... | collective-permute-start | bytes 6291464 | tf_op jit(solution)/shard_map/ppermute | solution.py:449
  309.9 15.8 %collective-permute-start.24 = (bf16[512,2048]{1,0:T(8,128)(2,1)}, bf16[512,2048]{1,0:T(8,128)(2,1)}, u32[]{:S(2)}, u32[]{:S(2)}) collective-permute-start(bf16[512,2048]{1,0:T(8,128)(2,1)} %collective-permute-done.22.refs_1_.refs_5_), channel_id=1, source_target_pairs={{0,4},{4,0},{8,12},{12,8},{16,20},{20,16},{24,28},{28,24},{1,5},{5... | collective-permute-start | bytes 6291464 | tf_op jit(solution)/shard_map/ppermute | solution.py:449
  371.2 48.1 %collective-permute-start.28 = (bf16[512,2048]{1,0:T(8,128)(2,1)}, bf16[512,2048]{1,0:T(8,128)(2,1)S(1)}, u32[]{:S(2)}, u32[]{:S(2)}) collective-permute-start(bf16[512,2048]{1,0:T(8,128)(2,1)} %add_convert_fusion.4), channel_id=1, source_target_pairs={{0,16},{4,20},{8,24},{12,28},{16,0},{20,4},{24,8},{28,12},{1,17},{... | collective-permute-start | bytes 6291464 | tf_op jit(solution)/shard_map/ppermute | solution.py:449
  372.8 47.8 %collective-permute-start.29 = (bf16[512,2048]{1,0:T(8,128)(2,1)}, bf16[512,2048]{1,0:T(8,128)(2,1)S(1)}, u32[]{:S(2)}, u32[]{:S(2)}) collective-permute-start(bf16[512,2048]{1,0:T(8,128)(2,1)} %add_convert_fusion.3), channel_id=1, source_target_pairs={{0,8},{4,12},{8,0},{12,4},{16,24},{20,28},{24,16},{28,20},{1,9},{5... | collective-permute-start | bytes 6291464 | tf_op jit(solution)/shard_map/ppermute | solution.py:449
  423.7 40.0 %collective-permute-start.31 = (bf16[256,2048]{1,0:T(8,128)(2,1)}, bf16[256,2048]{1,0:T(8,128)(2,1)}, u32[]{:S(2)}, u32[]{:S(2)}) collective-permute-start(bf16[256,2048]{1,0:T(8,128)(2,1)} %slice.392), channel_id=1, source_target_pairs={{0,16},{4,20},{8,24},{12,28},{16,0},{20,4},{24,8},{28,12},{1,17},{... | collective-permute-start | bytes 3145736 | tf_op jit(solution)/shard_map/ppermute | solution.py:449
  426.3 39.9 %collective-permute-start.30 = (bf16[256,2048]{1,0:T(8,128)(2,1)}, bf16[256,2048]{1,0:T(8,128)(2,1)}, u32[]{:S(2)}, u32[]{:S(2)}) collective-permute-start(bf16[256,2048]{1,0:T(8,128)(2,1)} %slice.393), channel_id=1, source_target_pairs={{0,8},{4,12},{8,0},{12,4},{16,24},{20,28},{24,16},{28,20},{1,9},{5... | collective-permute-start | bytes 3145736 | tf_op jit(solution)/shard_map/ppermute | solution.py:449
  427.1 304.5 %reduce-scatter.9.cloned.1.call-start = ((), (), s32[]{:S(2)}) async-start(), calls=%async_computation.12 | async-start | bytes 5242880 | tf_op jit(solution)/shard_map/reduce_scatter | solution.py:677
  433.2 35.9 %collective-permute-start.32 = (bf16[512,2048]{1,0:T(8,128)(2,1)}, bf16[512,2048]{1,0:T(8,128)(2,1)}, u32[]{:S(2)}, u32[]{:S(2)}) collective-permute-start(bf16[512,2048]{1,0:T(8,128)(2,1)} %convolution_convert_fusion.3), channel_id=1, source_target_pairs={{0,4},{4,0},{8,12},{12,8},{16,20},{20,16},{24,28},{28,24},{1,5},{5... | collective-permute-start | bytes 6291464 | tf_op jit(solution)/shard_map/ppermute | solution.py:449
  436.9 38.5 %collective-permute-start.33 = (bf16[512,2048]{1,0:T(8,128)(2,1)}, bf16[512,2048]{1,0:T(8,128)(2,1)S(1)}, u32[]{:S(2)}, u32[]{:S(2)}) collective-permute-start(bf16[512,2048]{1,0:T(8,128)(2,1)} %convolution_convert_fusion.2), channel_id=1, source_target_pairs={{0,4},{4,0},{8,12},{12,8},{16,20},{20,16},{24,28},{28,24},{1,5},{5... | collective-permute-start | bytes 6291464 | tf_op jit(solution)/shard_map/ppermute | solution.py:449
  477.7 53.4 %collective-permute-start.34 = (bf16[512,2048]{1,0:T(8,128)(2,1)S(1)}, bf16[512,2048]{1,0:T(8,128)(2,1)S(1)}, u32[]{:S(2)}, u32[]{:S(2)}) collective-permute-start(bf16[512,2048]{1,0:T(8,128)(2,1)S(1)} %add_convert_fusion.2), channel_id=1, source_target_pairs={{0,16},{4,20},{8,24},{12,28},{16,0},{20,4},{24,8},{28,12},{1,17},{... | collective-permute-start | bytes 6291464 | tf_op jit(solution)/shard_map/ppermute | solution.py:449
  478.2 54.3 %collective-permute-start.35 = (bf16[512,2048]{1,0:T(8,128)(2,1)S(1)}, bf16[512,2048]{1,0:T(8,128)(2,1)}, u32[]{:S(2)}, u32[]{:S(2)}) collective-permute-start(bf16[512,2048]{1,0:T(8,128)(2,1)S(1)} %add_convert_fusion.1), channel_id=1, source_target_pairs={{0,8},{4,12},{8,0},{12,4},{16,24},{20,28},{24,16},{28,20},{1,9},{5... | collective-permute-start | bytes 6291464 | tf_op jit(solution)/shard_map/ppermute | solution.py:449
  532.5 29.1 %collective-permute-start.36 = (bf16[1024,2048]{1,0:T(8,128)(2,1)}, bf16[1024,2048]{1,0:T(8,128)(2,1)}, u32[]{:S(2)}, u32[]{:S(2)}) collective-permute-start(bf16[1024,2048]{1,0:T(8,128)(2,1)} %convolution_convert_fusion.1), channel_id=1, source_target_pairs={{0,4},{4,0},{8,12},{12,8},{16,20},{20,16},{24,28},{28,24},{1,5},{5... | collective-permute-start | bytes 12582920 | tf_op jit(solution)/shard_map/ppermute | solution.py:449
  541.8 29.1 %collective-permute-start.37 = (bf16[1024,2048]{1,0:T(8,128)(2,1)}, bf16[1024,2048]{1,0:T(8,128)(2,1)}, u32[]{:S(2)}, u32[]{:S(2)}) collective-permute-start(bf16[1024,2048]{1,0:T(8,128)(2,1)} %shard_map.300), channel_id=1, source_target_pairs={{0,4},{4,0},{8,12},{12,8},{16,20},{20,16},{24,28},{28,24},{1,5},{5... | collective-permute-start | bytes 12582920 | tf_op jit(solution)/shard_map/ppermute | solution.py:449
  544.2 41.7 %collective-permute-start.38 = (bf16[2,256,256]{2,1,0:T(8,128)(2,1)S(1)}, bf16[2,256,256]{2,1,0:T(8,128)(2,1)S(1)}, u32[]{:S(2)}, u32[]{:S(2)}) collective-permute-start(bf16[2,256,256]{2,1,0:T(8,128)(2,1)S(1)} %get-tuple-element.336), channel_id=1, source_target_pairs={{0,1},{1,2},{2,3},{3,0},{4,5},{5,6},{6,7},{7,4},{8,9},{9,10},{10,1... | collective-permute-start | bytes 786440 | tf_op jit(solution)/shard_map/ppermute | solution.py:394
  555.5 30.5 %collective-permute-start.39 = (bf16[2,256,256]{2,1,0:T(8,128)(2,1)S(1)}, bf16[2,256,256]{2,1,0:T(8,128)(2,1)}, u32[]{:S(2)}, u32[]{:S(2)}) collective-permute-start(bf16[2,256,256]{2,1,0:T(8,128)(2,1)S(1)} %get-tuple-element.335), channel_id=1, source_target_pairs={{0,2},{1,3},{2,0},{3,1},{4,6},{5,7},{6,4},{7,5},{8,10},{9,11},{10,... | collective-permute-start | bytes 786440 | tf_op jit(solution)/shard_map/ppermute | solution.py:394
  558.6 27.4 %collective-permute-start.40 = (bf16[2,256,256]{2,1,0:T(8,128)(2,1)S(1)}, bf16[2,256,256]{2,1,0:T(8,128)(2,1)}, u32[]{:S(2)}, u32[]{:S(2)}) collective-permute-start(bf16[2,256,256]{2,1,0:T(8,128)(2,1)S(1)} %get-tuple-element.334), channel_id=1, source_target_pairs={{0,3},{1,0},{2,1},{3,2},{4,7},{5,4},{6,5},{7,6},{8,11},{9,8},{10,9... | collective-permute-start | bytes 786440 | tf_op jit(solution)/shard_map/ppermute | solution.py:394
  586.0 23.4 %all-to-all-start.1 = ((bf16[8,64,1024]{2,1,0:T(8,128)(2,1)}), bf16[8,64,1024]{2,1,0:T(8,128)(2,1)}, u32[]{:S(2)}, u32[]{:S(2)}) async-start(bf16[8,64,1024]{2,1,0:T(8,128)(2,1)} %reduce-scatter.5.cloned.1.call-done), calls=%async_computation.5 | async-start | bytes 2097152 | tf_op jit(solution)/shard_map/all_to_all | solution.py:752
  590.4 161.9 %reduce-scatter.7.cloned.1.call-start = ((), (), s32[]{:S(2)}) async-start(), calls=%async_computation.11 | async-start | bytes 1310720 | tf_op jit(solution)/shard_map/reduce_scatter | solution.py:691
  590.5 37.4 %collective-permute-start.41 = (bf16[256,2048]{1,0:T(8,128)(2,1)}, bf16[256,2048]{1,0:T(8,128)(2,1)}, u32[]{:S(2)}, u32[]{:S(2)}) collective-permute-start(bf16[256,2048]{1,0:T(8,128)(2,1)} %copy-done.30), channel_id=1, source_target_pairs={{0,16},{4,20},{8,24},{12,28},{16,0},{20,4},{24,8},{28,12},{1,17},{... | collective-permute-start | bytes 3145736 | tf_op jit(solution)/shard_map/ppermute | solution.py:449
  592.3 35.6 %collective-permute-start.42 = (bf16[256,2048]{1,0:T(8,128)(2,1)}, bf16[256,2048]{1,0:T(8,128)(2,1)}, u32[]{:S(2)}, u32[]{:S(2)}) collective-permute-start(bf16[256,2048]{1,0:T(8,128)(2,1)} %copy-done.29), channel_id=1, source_target_pairs={{0,8},{4,12},{8,0},{12,4},{16,24},{20,28},{24,16},{28,20},{1,9},{5... | collective-permute-start | bytes 3145736 | tf_op jit(solution)/shard_map/ppermute | solution.py:449
  599.8 50.5 %collective-permute-start.45 = (bf16[256,2048]{1,0:T(8,128)(2,1)}, bf16[256,2048]{1,0:T(8,128)(2,1)}, u32[]{:S(2)}, u32[]{:S(2)}) collective-permute-start(bf16[256,2048]{1,0:T(8,128)(2,1)} %slice.390), channel_id=1, source_target_pairs={{0,16},{4,20},{8,24},{12,28},{16,0},{20,4},{24,8},{28,12},{1,17},{... | collective-permute-start | bytes 3145736 | tf_op jit(solution)/shard_map/ppermute | solution.py:449
  603.1 49.4 %collective-permute-start.44 = (bf16[256,2048]{1,0:T(8,128)(2,1)}, bf16[256,2048]{1,0:T(8,128)(2,1)}, u32[]{:S(2)}, u32[]{:S(2)}) collective-permute-start(bf16[256,2048]{1,0:T(8,128)(2,1)} %slice.391), channel_id=1, source_target_pairs={{0,8},{4,12},{8,0},{12,4},{16,24},{20,28},{24,16},{28,20},{1,9},{5... | collective-permute-start | bytes 3145736 | tf_op jit(solution)/shard_map/ppermute | solution.py:449
  627.9 42.1 %collective-permute-start.43 = (bf16[1024,2048]{1,0:T(8,128)(2,1)}, bf16[1024,2048]{1,0:T(8,128)(2,1)}, u32[]{:S(2)}, u32[]{:S(2)}) collective-permute-start(bf16[1024,2048]{1,0:T(8,128)(2,1)} %shard_map.303), channel_id=1, source_target_pairs={{0,4},{4,0},{8,12},{12,8},{16,20},{20,16},{24,28},{28,24},{1,5},{5... | collective-permute-start | bytes 12582920 | tf_op jit(solution)/shard_map/ppermute | solution.py:449
  630.4 36.1 %collective-permute-start.47 = (bf16[128,2048]{1,0:T(8,128)(2,1)}, bf16[128,2048]{1,0:T(8,128)(2,1)}, u32[]{:S(2)}, u32[]{:S(2)}) collective-permute-start(bf16[128,2048]{1,0:T(8,128)(2,1)} %slice.396), channel_id=1, source_target_pairs={{0,16},{4,20},{8,24},{12,28},{16,0},{20,4},{24,8},{28,12},{1,17},{... | collective-permute-start | bytes 1572872 | tf_op jit(solution)/shard_map/ppermute | solution.py:449
  634.9 32.8 %collective-permute-start.46 = (bf16[128,2048]{1,0:T(8,128)(2,1)}, bf16[128,2048]{1,0:T(8,128)(2,1)}, u32[]{:S(2)}, u32[]{:S(2)}) collective-permute-start(bf16[128,2048]{1,0:T(8,128)(2,1)} %slice.397), channel_id=1, source_target_pairs={{0,8},{4,12},{8,0},{12,4},{16,24},{20,28},{24,16},{28,20},{1,9},{5... | collective-permute-start | bytes 1572872 | tf_op jit(solution)/shard_map/ppermute | solution.py:449
  686.4 24.6 %collective-permute-start.49 = (bf16[256,2048]{1,0:T(8,128)(2,1)}, bf16[256,2048]{1,0:T(8,128)(2,1)}, u32[]{:S(2)}, u32[]{:S(2)}) collective-permute-start(bf16[256,2048]{1,0:T(8,128)(2,1)} %get-tuple-element.296), channel_id=1, source_target_pairs={{0,16},{4,20},{8,24},{12,28},{16,0},{20,4},{24,8},{28,12},{1,17},{... | collective-permute-start | bytes 3145736 | tf_op jit(solution)/shard_map/ppermute | solution.py:449
  686.6 24.7 %collective-permute-start.50 = (bf16[256,2048]{1,0:T(8,128)(2,1)}, bf16[256,2048]{1,0:T(8,128)(2,1)}, u32[]{:S(2)}, u32[]{:S(2)}) collective-permute-start(bf16[256,2048]{1,0:T(8,128)(2,1)} %get-tuple-element.297), channel_id=1, source_target_pairs={{0,8},{4,12},{8,0},{12,4},{16,24},{20,28},{24,16},{28,20},{1,9},{5... | collective-permute-start | bytes 3145736 | tf_op jit(solution)/shard_map/ppermute | solution.py:449
  689.8 76.4 %reduce-scatter.11.cloned.1.call-start = ((), (), s32[]{:S(2)}) async-start(), calls=%async_computation.13 | async-start | bytes 1310720 | tf_op jit(solution)/shard_map/reduce_scatter | solution.py:737
  712.9 13.8 %collective-permute-start.53 = (bf16[128,2048]{1,0:T(8,128)(2,1)S(1)}, bf16[128,2048]{1,0:T(8,128)(2,1)S(1)}, u32[]{:S(2)}, u32[]{:S(2)}) collective-permute-start(bf16[128,2048]{1,0:T(8,128)(2,1)S(1)} %slice.394), channel_id=1, source_target_pairs={{0,16},{4,20},{8,24},{12,28},{16,0},{20,4},{24,8},{28,12},{1,17},{... | collective-permute-start | bytes 1572872 | tf_op jit(solution)/shard_map/ppermute | solution.py:449
  716.3 14.0 %collective-permute-start.52 = (bf16[128,2048]{1,0:T(8,128)(2,1)S(1)}, bf16[128,2048]{1,0:T(8,128)(2,1)S(1)}, u32[]{:S(2)}, u32[]{:S(2)}) collective-permute-start(bf16[128,2048]{1,0:T(8,128)(2,1)S(1)} %slice.395), channel_id=1, source_target_pairs={{0,8},{4,12},{8,0},{12,4},{16,24},{20,28},{24,16},{28,20},{1,9},{5... | collective-permute-start | bytes 1572872 | tf_op jit(solution)/shard_map/ppermute | solution.py:449
  719.4 12.1 %collective-permute-start.51 = (bf16[288,256]{1,0:T(8,128)(2,1)S(1)}, bf16[288,256]{1,0:T(8,128)(2,1)S(1)}, u32[]{:S(2)}, u32[]{:S(2)}) collective-permute-start(bf16[288,256]{1,0:T(8,128)(2,1)S(1)} %get-tuple-element.340), channel_id=1, source_target_pairs={{0,16},{4,20},{8,24},{12,28},{16,0},{20,4},{24,8},{28,12},{1,17},{... | collective-permute-start | bytes 442376 | tf_op jit(solution)/shard_map/ppermute | solution.py:449
  719.9 12.1 %collective-permute-start.55 = (bf16[288,256]{1,0:T(8,128)(2,1)S(1)}, bf16[288,256]{1,0:T(8,128)(2,1)}, u32[]{:S(2)}, u32[]{:S(2)}) collective-permute-start(bf16[288,256]{1,0:T(8,128)(2,1)S(1)} %get-tuple-element.341), channel_id=1, source_target_pairs={{0,8},{4,12},{8,0},{12,4},{16,24},{20,28},{24,16},{28,20},{1,9},{5... | collective-permute-start | bytes 442376 | tf_op jit(solution)/shard_map/ppermute | solution.py:449
  744.5 11.5 %collective-permute-start.59 = (bf16[17664]{0:T(1024)(128)(2,1)S(1)}, bf16[17664]{0:T(1024)(128)(2,1)S(1)}, u32[]{:S(2)}, u32[]{:S(2)}) collective-permute-start(bf16[17664]{0:T(1024)(128)(2,1)S(1)} %get-tuple-element.317), channel_id=1, source_target_pairs={{0,3},{1,0},{2,1},{3,2},{4,7},{5,4},{6,5},{7,6},{8,11},{9,8},{10,9... | collective-permute-start | bytes 105992 | tf_op jit(solution)/shard_map/ppermute | solution.py:394
  744.6 11.3 %collective-permute-start.58 = (bf16[17664]{0:T(1024)(128)(2,1)S(1)}, bf16[17664]{0:T(1024)(128)(2,1)S(1)}, u32[]{:S(2)}, u32[]{:S(2)}) collective-permute-start(bf16[17664]{0:T(1024)(128)(2,1)S(1)} %get-tuple-element.318), channel_id=1, source_target_pairs={{0,2},{1,3},{2,0},{3,1},{4,6},{5,7},{6,4},{7,5},{8,10},{9,11},{10,... | collective-permute-start | bytes 105992 | tf_op jit(solution)/shard_map/ppermute | solution.py:394
  745.2 10.7 %collective-permute-start.57 = (bf16[17664]{0:T(1024)(128)(2,1)S(1)}, bf16[17664]{0:T(1024)(128)(2,1)S(1)}, u32[]{:S(2)}, u32[]{:S(2)}) collective-permute-start(bf16[17664]{0:T(1024)(128)(2,1)S(1)} %get-tuple-element.316), channel_id=1, source_target_pairs={{0,1},{1,2},{2,3},{3,0},{4,5},{5,6},{6,7},{7,4},{8,9},{9,10},{10,1... | collective-permute-start | bytes 105992 | tf_op jit(solution)/shard_map/ppermute | solution.py:394
  (88 other events, 1168.2 us)
Sparse Core Ops, SparseCore 0:
  17.7 35.3 all-gather.4
  59.4 63.5 all-gather.6
  125.5 54.3 all-gather.8
  186.8 87.7 all-gather.10
  427.2 87.5 reduce-scatter.4
  586.1 74.1 reduce-scatter.8
  689.9 25.1 reduce-scatter.6
  741.1 25.1 reduce-scatter.10

commit v15 on v14

--- a/solution.py
+++ b/solution.py
@@ -677,7 +677,7 @@
         grad_down = lax.psum_scatter(down_terms, "fsdp", scatter_dimension=0, tiled=True)
         branch_out = plane.fold(out_sum)
         wo_sib = product(att_sib, branch_grad, "tn")
-        wo_sib, query_late, *wq_got = tie(wo_sib, query_late, *wq_got)
+        wo_sib, *wq_got = tie(wo_sib, *wq_got)
         wo_theirs = plane.swap(wo_sib, 1)
         query_part = product(query_late, full_q, "nt", kind=F32)
         wq_rows = own_rows(wq_parts, wq_got).astype(BF16)

time: 786 us -> 777 us (0.989)
  waiting for transfers between devices: 194 us -> 178 us
  Pallas kernels: 242 us -> 251 us
    ppermute x45, waiting for transfers between devices: 105 us -> 70 us  [swap(): return lax.ppermute(block, 'dp', [(i, i ^ bit) for i in range(self.count)])]
    all_to_all x1, waiting for transfers between devices: 0.01 us -> 23.5 us  [local(): lax.all_to_all(grad_up.reshape(n_dp * own, ff_own), 'dp', 0, 1, tiled=True)]
    pallas_call x2, Pallas kernels: 28.1 us -> 38.4 us  [back_product(): pl.pallas_call(functools.partial(back_kernel, count), out_shape=jax.Shape...]
    unnamed x186 -> x176, local copies, waits for them, and re-layouts: 31.2 us -> 32 us
  transfers between devices with their start and end apart: 70 -> 70, of which waited for: 29 -> 28; matrix products, arithmetic and copies ran while one was open for 25% -> 25% of each run, Pallas kernels for 27% -> 29%
where the time goes in v15:
time: 777 us; the launch traced here: 769 us
  Pallas kernels  251 us (32%)
  waiting for transfers between devices  178 us (23%)
  local copies, waits for them, and re-layouts  87.1 us (11%)
  other arithmetic  82.9 us (11%)
  starting transfers between devices  81 us (10%)
  matrix products  72.7 us (9%)
  between operations  15.9 us (2%)
    ppermute x45, waiting for transfers between devices, swap(): return lax.ppermute(block, 'dp', [(i, i ^ bit) for i in range(self.count)])  70 us
    ppermute x15, waiting for transfers between devices, send(): lax.ppermute(block, 'fsdp', [(i, (i + places) % self.count) for i in rang...  59.2 us
    pallas_call x8, Pallas kernels, product(): pl.pallas_call(functools.partial(product_kernel, form, len(extra)), out_s...  56.8 us
    pallas_call x2, Pallas kernels, weight_grad(): pl.pallas_call(functools.partial(weight_kernel, count), out_shape=jax.Sha...  52.1 us
    pallas_call x2, Pallas kernels, middle_layer(): pl.pallas_call(functools.partial(middle_kernel, count), out_shape=[jax.Sh...  41.3 us
    ppermute x15, starting transfers between devices, send(): lax.ppermute(block, 'fsdp', [(i, (i + places) % self.count) for i in rang...  39.7 us
    pallas_call x2, Pallas kernels, back_product(): pl.pallas_call(functools.partial(back_kernel, count), out_shape=jax.Shape...  38.4 us
    dot_general x7, matrix products, dot_nn(): return jnp.dot(left, right, preferred_element_type=F32)  36.1 us
  transfers between devices with their start and end apart: 70, of which 28 were waited for; matrix products, arithmetic and copies ran while one was open for 25% of the time, Pallas kernels for 29%

profile of v15, /device:TPU:0, one launch (start us, length us, event | category | flops | bytes accessed | tf_op | source)
XLA Modules:
  0.0 768.6 jit_solution(13625942704107558210)
XLA Ops:
  17.6 2.7 slice_bitcast_fusion
  20.3 2.9 collective-permute-start
  25.8 3.6 all-to-all-start
  29.4 17.9 %collective-permute-done = bf16[256,2048]{1,0:T(8,128)(2,1)} collective-permute-done((bf16[256,2048]{1,0:T(8,128)(2,1)S(1)}, bf16[256,2048]{1,0:T(8,128)(2,1)}, u32[]{:S(2)}, u32[]{:S(2)}) %collective-permute-start) | collective-permute-done | bytes 1048608 | tf_op jit(solution)/shard_map/ppermute | solution.py:449
  49.9 3.1 pad_maximum_fusion.3.refs_1_.refs_9_
  53.0 6.3 all-to-all-done
  61.5 2.6 collective-permute-start.3
  67.7 3.5 collective-permute-done.2
  71.1 10.4 %collective-permute-done.3 = bf16[64,2048]{1,0:T(8,128)(2,1)} collective-permute-done((bf16[64,2048]{1,0:T(8,128)(2,1)S(1)}, bf16[64,2048]{1,0:T(8,128)(2,1)}, u32[]{:S(2)}, u32[]{:S(2)}) %collective-permute-start.3) | collective-permute-done | bytes 262176 | tf_op jit(solution)/shard_map/ppermute | solution.py:394
  81.6 6.1 collective-permute-start.5
  94.6 17.0 %collective-permute-done.5 = bf16[256,2048]{1,0:T(8,128)(2,1)} collective-permute-done((bf16[256,2048]{1,0:T(8,128)(2,1)}, bf16[256,2048]{1,0:T(8,128)(2,1)}, u32[]{:S(2)}, u32[]{:S(2)}) %collective-permute-start.5) | collective-permute-done | bytes 1048608 | tf_op jit(solution)/shard_map/ppermute | solution.py:394
  111.6 11.5 %all-gather.7.cloned.1.call-done = bf16[2560,2048]{1,0:T(8,128)(2,1)} async-done(((bf16[320,2048]{1,0:T(8,128)(2,1)}), bf16[2560,2048]{1,0:T(8,128)(2,1)}) %all-gather.7.cloned.1.call-update) | async-done | bytes 10485776 | tf_op jit(solution)/shard_map/all_gather | solution.py:533
  135.2 8.3 %slice.292 = bf16[32,64,2048]{2,1,0:T(8,128)(2,1)} slice(bf16[32,80,2048]{2,1,0:T(8,128)(2,1)} %bitcast.152), slice={[0:32], [0:64], [0:2048]} | slice | bytes 16777216 | tf_op jit(solution)/shard_map/slice | solution.py:548
  144.9 2.6 fusion.20
  148.4 9.9 %collective-permute-done.8 = bf16[256,2048]{1,0:T(8,128)(2,1)} collective-permute-done((bf16[256,2048]{1,0:T(8,128)(2,1)}, bf16[256,2048]{1,0:T(8,128)(2,1)}, u32[]{:S(2)}, u32[]{:S(2)}) %collective-permute-start.8) | collective-permute-done | bytes 1048608 | tf_op jit(solution)/shard_map/ppermute | solution.py:394
  162.1 8.2 %add_convert_fusion.6.q_ref = bf16[512,2048]{1,0:T(8,128)(2,1)S(1)} fusion(bf16[512,2048]{1,0:T(8,128)(2,1)S(1)} %fusion.12.first_ref.second_ref, bf16[2048,2048]{1,0:T(8,128)(2,1)} %bitcast.149, f32[2048]{0:T(1024)S(1)} %reshape.386), kind=kOutput, calls=%fused_computation.42 | convolution fusion | flops 4297064448 | bytes 12591104 | tf_op jit(solution)/shard_map/dot_general | solution.py:21
  170.3 8.8 %collective-permute-done.10 = bf16[2,256,256]{2,1,0:T(8,128)(2,1)S(1)} collective-permute-done((bf16[2,256,256]{2,1,0:T(8,128)(2,1)S(1)}, bf16[2,256,256]{2,1,0:T(8,128)(2,1)S(1)}, u32[]{:S(2)}, u32[]{:S(2)}) %collective-permute-start.10) | collective-permute-done | bytes 262176 | tf_op jit(solution)/shard_map/ppermute | solution.py:394
  180.6 4.4 collective-permute-start.12
  190.7 18.8 %shard_map.288 = (bf16[512,2048]{1,0:T(8,128)(2,1)S(1)}, f32[512,128]{1,0:T(8,128)S(1)}) custom-call(s32[1]{0:T(128)} %bitcast.1.pos_ref, s32[2,8]{1,0:T(2,128)S(1)} %select_reduce_fusion.ends_ref, bf16[512,2048]{1,0:T(8,128)(2,1)S(1)} %add_convert_fusion.6.q_ref, bf16[2,1024,256]{2,1,0:T(8,128)(2,1)S(1)} %constant_dynamic-update-slice_fusion.15.kv_ref), custom_call_target="tpu_custom_call" | custom-call | flops 67108864 | bytes 65536 | tf_op jit(solution)/shard_map/pallas_call | solution.py:132
  211.8 9.6 %collective-permute-done.12 = bf16[256,2048]{1,0:T(8,128)(2,1)S(1)} collective-permute-done((bf16[256,2048]{1,0:T(8,128)(2,1)}, bf16[256,2048]{1,0:T(8,128)(2,1)S(1)}, u32[]{:S(2)}, u32[]{:S(2)}) %collective-permute-start.12) | collective-permute-done | bytes 1048608 | tf_op jit(solution)/shard_map/ppermute | solution.py:394
  221.4 9.3 %fusion.48 = (f32[512]{0:T(512)S(1)}, f32[512,2048]{1,0:T(8,128)S(1)}) fusion(f32[2048]{0:T(1024)S(1)} %reshape.387, bf16[512,2048]{1,0:T(8,128)(2,1)} %copy-done.6, bf16[2048,2048]{1,0:T(8,128)(2,1)} %all-gather.9.cloned.1.call-done, bf16[2,256,2048]{2,1,0:T(8,128)(2,1)} %param.17), kind=kOutput, calls=%fused_computation.184 | convolution fusion | flops 4299161088 | bytes 16787456 | tf_op jit(solution)/shard_map/dot_general | solution.py:21
  241.3 23.8 %shard_map.289.refs_4_ = bf16[2048,1024]{1,0:T(8,128)(2,1)} custom-call(bf16[512,2048]{1,0:T(8,128)(2,1)S(1)} %copy-done.8, bf16[512,2048]{1,0:T(8,128)(2,1)S(1)} %copy-done.9, bf16[512,2048]{1,0:T(8,128)(2,1)} %collective-permute-done.6.refs_2_.refs_10_, bf16[512,2048]{1,0:T(8,128)(2,1)} %collective-permute-done.7.refs_3_.refs_11_, ...), custom_call_target="tpu_custom_call" | custom-call | flops 134217728 | bytes 262144 | tf_op jit(solution)/shard_map/pallas_call | solution.py:240
  271.2 14.6 %shard_map.290.refs_4_ = bf16[2048,1024]{1,0:T(8,128)(2,1)} custom-call(bf16[512,2048]{1,0:T(8,128)(2,1)} %collective-permute-done.13.refs_0_.refs_12_, bf16[512,2048]{1,0:T(8,128)(2,1)} %collective-permute-done.14.refs_1_.refs_13_, bf16[512,2048]{1,0:T(8,128)(2,1)} %collective-permute-done.15.refs_2_.refs_14_, ...), custom_call_target="tpu_custom_call" | custom-call | flops 134217728 | bytes 262144 | tf_op jit(solution)/shard_map/pallas_call | solution.py:240
  285.8 20.5 %shard_map.291 = (bf16[1024,1024]{1,0:T(8,128)(2,1)S(1)}, bf16[1024,1024]{1,0:T(8,128)(2,1)S(1)}, bf16[1024,1024]{1,0:T(8,128)(2,1)}, bf16[1024,1024]{1,0:T(8,128)(2,1)}, f32[1,1024]{1,0:T(1,128)S(1)}) custom-call(bf16[512,2048]{1,0:T(8,128)(2,1)} %pad_maximum_fusion.4.refs_0_, bf16[512,2048]{1,0:T(8,128)(2,1)} %pad_maximum_fusion.5.refs_1_, ...), custom_call_target="tpu_custom_call" | custom-call | flops 134217728 | bytes 393216 | tf_op jit(solution)/shard_map/pallas_call | solution.py:206
  308.9 7.6 collective-permute-done.21.refs_0_.refs_4_
  318.5 6.6 shard_map.292
  325.1 6.6 shard_map.293
  331.7 20.8 %shard_map.294 = (bf16[1024,1024]{1,0:T(8,128)(2,1)S(1)}, bf16[1024,1024]{1,0:T(8,128)(2,1)S(1)}, bf16[1024,1024]{1,0:T(8,128)(2,1)}, bf16[1024,1024]{1,0:T(8,128)(2,1)}, f32[1,1024]{1,0:T(1,128)S(1)}) custom-call(bf16[512,2048]{1,0:T(8,128)(2,1)} %collective-permute-done.21.refs_0_.refs_4_, bf16[512,2048]{1,0:T(8,128)(2,1)} %collective-permute-done.22.refs_1_.refs_5_, ...), custom_call_target="tpu_custom_call" | custom-call | flops 134217728 | bytes 393216 | tf_op jit(solution)/shard_map/pallas_call | solution.py:206
  352.5 4.5 convolution_convert_fusion.5
  361.3 3.7 add_convert_fusion.4
  365.0 3.7 add_convert_fusion.3
  368.8 7.8 %shard_map.295 = bf16[1024,2048]{1,0:T(8,128)(2,1)} custom-call(bf16[1024,1024]{1,0:T(8,128)(2,1)S(1)} %copy-done.14, bf16[2048,1024]{1,0:T(8,128)(2,1)} %bitcast.143), custom_call_target="tpu_custom_call" | custom-call | flops 67108864 | bytes 163840 | tf_op jit(solution)/shard_map/pallas_call | solution.py:354
  378.4 5.6 collective-permute-done.27.refs_0_
  384.0 25.8 %shard_map.296 = bf16[2048,1024]{1,0:T(8,128)(2,1)} custom-call(bf16[512,2048]{1,0:T(8,128)(2,1)} %pad_maximum_fusion.4.refs_0_, bf16[512,2048]{1,0:T(8,128)(2,1)} %pad_maximum_fusion.5.refs_1_, bf16[512,2048]{1,0:T(8,128)(2,1)} %collective-permute-done.19.refs_2_, bf16[512,2048]{1,0:T(8,128)(2,1)} %collective-permute-done.20.refs_3_, ...), custom_call_target="tpu_custom_call" | custom-call | flops 17179869184 | bytes 29360128 | tf_op jit(solution)/shard_map/pallas_call | solution.py:280
  409.8 8.7 %shard_map.297 = (bf16[512,2048]{1,0:T(8,128)(2,1)S(1)}, bf16[512,2048]{1,0:T(8,128)(2,1)S(1)}) custom-call(bf16[1024,1024]{1,0:T(8,128)(2,1)} %get-tuple-element.231.refs_8_.refs_9_.values_ref, bf16[2048,1024]{1,0:T(8,128)(2,1)} %bitcast.144, bf16[1024,2048]{1,0:T(8,128)(2,1)} %copy-done.46), custom_call_target="tpu_custom_call" | custom-call | flops 67108864 | bytes 163840 | tf_op jit(solution)/shard_map/pallas_call | solution.py:354
  418.5 6.3 collective-permute-done.28
  432.1 6.0 convolution_convert_fusion.3
  438.1 3.7 convolution_convert_fusion.2
  442.4 26.2 %shard_map.298 = bf16[1024,2048]{1,0:T(8,128)(2,1)} custom-call(bf16[1024,1024]{1,0:T(8,128)(2,1)} %copy-done.11, bf16[1024,1024]{1,0:T(8,128)(2,1)} %copy-done.11, bf16[1024,1024]{1,0:T(8,128)(2,1)} %copy-done.12, bf16[1024,1024]{1,0:T(8,128)(2,1)} %copy-done.12, bf16[1024,1024]{1,0:T(8,128)(2,1)} %copy-done.24, bf16[1024,1024]{1,0:T(8,128)(2,1)} %copy-done.24, ...), custom_call_target="tpu_custom_call" | custom-call | flops 17179869184 | bytes 29360128 | tf_op jit(solution)/shard_map/pallas_call | solution.py:280
  476.2 4.0 add_convert_fusion.2
  491.9 10.3 %convolution_convert_fusion.6.grad_ref = bf16[512,2048]{1,0:T(8,128)(2,1)} fusion(bf16[512,2048]{1,0:T(8,128)(2,1)S(1)} %convert_element_type.418.weight_ref, bf16[2048,2048]{1,0:T(8,128)(2,1)} %all-gather.9.cloned.1.call-done), kind=kOutput, calls=%fused_computation.52 | convolution fusion | flops 4296015872 | bytes 12582912 | tf_op jit(solution)/shard_map/dot_general | solution.py:25
  502.2 30.4 %shard_map.299 = (bf16[512,2048]{1,0:T(8,128)(2,1)S(1)}, bf16[2,1024,256]{2,1,0:T(8,128)(2,1)S(1)}) custom-call(s32[1]{0:T(128)} %bitcast.1.pos_ref, s32[2,8]{1,0:T(2,128)S(1)} %select_reduce_fusion.ends_ref, bf16[512,2048]{1,0:T(8,128)(2,1)} %copy-done.5, bf16[2,1024,256]{2,1,0:T(8,128)(2,1)S(1)} %copy-done.4, f32[512,128]{1,0:T(8,128)S(1)} %get-tuple-element.217.norm_ref, ...), custom_call_target="tpu_custom_call" | custom-call | flops 167772160 | bytes 163840 | tf_op jit(solution)/shard_map/pallas_call | solution.py:152
  532.6 4.3 convolution_convert_fusion.1
  539.9 7.7 %shard_map.300 = bf16[1024,2048]{1,0:T(8,128)(2,1)} custom-call(bf16[1024,1024]{1,0:T(8,128)(2,1)S(1)} %copy-done.13, bf16[1024,2048]{1,0:T(8,128)(2,1)} %copy-done.32), custom_call_target="tpu_custom_call" | custom-call | flops 67108864 | bytes 163840 | tf_op jit(solution)/shard_map/pallas_call | solution.py:354
  550.1 9.7 %collective-permute-start.38 = (bf16[2,256,256]{2,1,0:T(8,128)(2,1)S(1)}, bf16[2,256,256]{2,1,0:T(8,128)(2,1)}, u32[]{:S(2)}, u32[]{:S(2)}) collective-permute-start(bf16[2,256,256]{2,1,0:T(8,128)(2,1)S(1)} %get-tuple-element.334), channel_id=1, source_target_pairs={{0,1},{1,2},{2,3},{3,0},{4,5},{5,6},{6,7},{7,4},{8,9},{9,10},{10,1... | collective-permute-start | bytes 786440 | tf_op jit(solution)/shard_map/ppermute | solution.py:394
  559.8 4.8 collective-permute-start.39
  565.3 5.4 shard_map.301
  574.6 8.0 %shard_map.302 = (bf16[512,2048]{1,0:T(8,128)(2,1)S(1)}, bf16[512,2048]{1,0:T(8,128)(2,1)S(1)}) custom-call(bf16[1024,1024]{1,0:T(8,128)(2,1)} %copy-done.11, bf16[1024,2048]{1,0:T(8,128)(2,1)} %copy-done.32, bf16[1024,2048]{1,0:T(8,128)(2,1)} %collective-permute-done.37.refs_0_), custom_call_target="tpu_custom_call" | custom-call | flops 67108864 | bytes 163840 | tf_op jit(solution)/shard_map/pallas_call | solution.py:354
  582.7 2.8 convert_add_fusion.2
  585.5 4.3 convert_add_fusion.1
  593.9 2.7 slice.390
  598.4 2.7 slice.391
  604.6 4.2 all-to-all-start.1
  610.4 4.5 shard_map.304
  620.2 8.6 %shard_map.303 = f32[512,2048]{1,0:T(8,128)} custom-call(bf16[512,2048]{1,0:T(8,128)(2,1)S(1)} %copy-done.2, bf16[2048,2048]{1,0:T(8,128)(2,1)} %bitcast.150), custom_call_target="tpu_custom_call" | custom-call | flops 67108864 | bytes 196608 | tf_op jit(solution)/shard_map/pallas_call | solution.py:354
  628.8 23.5 %all-to-all-done.1 = bf16[8,64,1024]{2,1,0:T(8,128)(2,1)} async-done(((bf16[8,64,1024]{2,1,0:T(8,128)(2,1)}), bf16[8,64,1024]{2,1,0:T(8,128)(2,1)}, u32[]{:S(2)}, u32[]{:S(2)}) %all-to-all-start.1) | async-done | bytes 1048608 | tf_op jit(solution)/shard_map/all_to_all | solution.py:752
  663.3 2.5 pad_maximum_fusion.1
  670.5 6.1 shard_map.305
  677.8 6.2 fusion.18
  693.1 14.8 %collective-permute-done.49 = bf16[256,2048]{1,0:T(8,128)(2,1)} collective-permute-done((bf16[256,2048]{1,0:T(8,128)(2,1)}, bf16[256,2048]{1,0:T(8,128)(2,1)}, u32[]{:S(2)}, u32[]{:S(2)}) %collective-permute-start.49) | collective-permute-done | bytes 1048608 | tf_op jit(solution)/shard_map/ppermute | solution.py:449
  726.6 5.3 fusion.17
  732.8 3.5 collective-permute-done.54
  740.4 5.9 add_convert_fusion
  752.2 7.6 reduce-scatter.11.cloned.1.call-done
  (455 shorter events, 192.8 us)
Async XLA Ops:
  7.2 52.1 %all-gather.5.cloned.1.call-start = ((), (), s32[]{:S(2)}) async-start(), calls=%async_computation.6 | async-start | bytes 1638400 | tf_op jit(solution)/shard_map/all_gather | solution.py:528
  20.3 27.0 %collective-permute-start = (bf16[256,2048]{1,0:T(8,128)(2,1)S(1)}, bf16[256,2048]{1,0:T(8,128)(2,1)}, u32[]{:S(2)}, u32[]{:S(2)}) collective-permute-start(bf16[256,2048]{1,0:T(8,128)(2,1)S(1)} %get-tuple-element.324), channel_id=1, source_target_pairs={{0,8},{4,12},{8,0},{12,4},{16,24},{20,28},{24,16},{28,20},{1,9},{5... | collective-permute-start | bytes 3145736 | tf_op jit(solution)/shard_map/ppermute | solution.py:449
  23.2 26.7 %collective-permute-start.1 = (bf16[256,2048]{1,0:T(8,128)(2,1)}, bf16[256,2048]{1,0:T(8,128)(2,1)}, u32[]{:S(2)}, u32[]{:S(2)}) collective-permute-start(bf16[256,2048]{1,0:T(8,128)(2,1)} %get-tuple-element.323), channel_id=1, source_target_pairs={{0,16},{4,20},{8,24},{12,28},{16,0},{20,4},{24,8},{28,12},{1,17},{... | collective-permute-start | bytes 3145736 | tf_op jit(solution)/shard_map/ppermute | solution.py:449
  25.8 33.5 %all-to-all-start = ((bf16[64,8,1024]{2,0,1:T(8,128)(2,1)}), bf16[64,8,1024]{2,0,1:T(8,128)(2,1)S(1)}, u32[]{:S(2)}, u32[]{:S(2)}) async-start(bf16[64,8,1024]{2,0,1:T(8,128)(2,1)} %bitcast.137), calls=%async_computation | async-start | bytes 2097152 | tf_op jit(solution)/shard_map/all_to_all | solution.py:530
  29.4 93.7 %all-gather.7.cloned.1.call-start = ((), (), s32[]{:S(2)}) async-start(), calls=%async_computation.7 | async-start | bytes 11796480 | tf_op jit(solution)/shard_map/all_gather | solution.py:533
  59.3 162.1 %all-gather.9.cloned.1.call-start = ((), (), s32[]{:S(2)}) async-start(), calls=%async_computation.8 | async-start | bytes 9437184 | tf_op jit(solution)/shard_map/all_gather | solution.py:546
  59.4 52.2 %collective-permute-start.6 = (bf16[512,2048]{1,0:T(8,128)(2,1)S(1)}, bf16[512,2048]{1,0:T(8,128)(2,1)}, u32[]{:S(2)}, u32[]{:S(2)}) collective-permute-start(bf16[512,2048]{1,0:T(8,128)(2,1)S(1)} %pad_maximum_fusion.2.refs_0_.refs_8_), channel_id=1, source_target_pairs={{0,4},{4,0},{8,12},{12,8},{16,20},{20,16},{24,28},{28,24},{1,5},{5... | collective-permute-start | bytes 6291464 | tf_op jit(solution)/shard_map/ppermute | solution.py:449
  59.4 52.1 %collective-permute-start.7 = (bf16[512,2048]{1,0:T(8,128)(2,1)}, bf16[512,2048]{1,0:T(8,128)(2,1)}, u32[]{:S(2)}, u32[]{:S(2)}) collective-permute-start(bf16[512,2048]{1,0:T(8,128)(2,1)} %pad_maximum_fusion.3.refs_1_.refs_9_), channel_id=1, source_target_pairs={{0,4},{4,0},{8,12},{12,8},{16,20},{20,16},{24,28},{28,24},{1,5},{5... | collective-permute-start | bytes 6291464 | tf_op jit(solution)/shard_map/ppermute | solution.py:449
  59.9 11.2 %collective-permute-start.2 = (bf16[64,2048]{1,0:T(8,128)(2,1)S(1)}, bf16[64,2048]{1,0:T(8,128)(2,1)}, u32[]{:S(2)}, u32[]{:S(2)}) collective-permute-start(bf16[64,2048]{1,0:T(8,128)(2,1)S(1)} %copy-done.56), channel_id=1, source_target_pairs={{0,1},{1,2},{2,3},{3,0},{4,5},{5,6},{6,7},{7,4},{8,9},{9,10},{10,1... | collective-permute-start | bytes 786440 | tf_op jit(solution)/shard_map/ppermute | solution.py:394
  61.5 20.0 %collective-permute-start.3 = (bf16[64,2048]{1,0:T(8,128)(2,1)S(1)}, bf16[64,2048]{1,0:T(8,128)(2,1)}, u32[]{:S(2)}, u32[]{:S(2)}) collective-permute-start(bf16[64,2048]{1,0:T(8,128)(2,1)S(1)} %copy-done.56), channel_id=1, source_target_pairs={{0,2},{1,3},{2,0},{3,1},{4,6},{5,7},{6,4},{7,5},{8,10},{9,11},{10,... | collective-permute-start | bytes 786440 | tf_op jit(solution)/shard_map/ppermute | solution.py:394
  64.1 17.5 %collective-permute-start.4 = (bf16[64,2048]{1,0:T(8,128)(2,1)S(1)}, bf16[64,2048]{1,0:T(8,128)(2,1)}, u32[]{:S(2)}, u32[]{:S(2)}) collective-permute-start(bf16[64,2048]{1,0:T(8,128)(2,1)S(1)} %copy-done.56), channel_id=1, source_target_pairs={{0,3},{1,0},{2,1},{3,2},{4,7},{5,4},{6,5},{7,6},{8,11},{9,8},{10,9... | collective-permute-start | bytes 786440 | tf_op jit(solution)/shard_map/ppermute | solution.py:394
  81.6 30.0 %collective-permute-start.5 = (bf16[256,2048]{1,0:T(8,128)(2,1)}, bf16[256,2048]{1,0:T(8,128)(2,1)}, u32[]{:S(2)}, u32[]{:S(2)}) collective-permute-start(bf16[256,2048]{1,0:T(8,128)(2,1)} %param.29), channel_id=1, source_target_pairs={{0,1},{1,2},{2,3},{3,0},{4,5},{5,6},{6,7},{7,4},{8,9},{9,10},{10,1... | collective-permute-start | bytes 3145736 | tf_op jit(solution)/shard_map/ppermute | solution.py:394
  123.1 162.7 %all-gather.11.cloned.1.call-start = ((), (), s32[]{:S(2)}) async-start(), calls=%async_computation.9 | async-start | bytes 5242880 | tf_op jit(solution)/shard_map/all_gather | solution.py:577
  130.8 27.5 %collective-permute-start.8 = (bf16[256,2048]{1,0:T(8,128)(2,1)}, bf16[256,2048]{1,0:T(8,128)(2,1)}, u32[]{:S(2)}, u32[]{:S(2)}) collective-permute-start(bf16[256,2048]{1,0:T(8,128)(2,1)} %collective-permute-done.5), channel_id=1, source_target_pairs={{0,1},{1,2},{2,3},{3,0},{4,5},{5,6},{6,7},{7,4},{8,9},{9,10},{10,1... | collective-permute-start | bytes 3145736 | tf_op jit(solution)/shard_map/ppermute | solution.py:394
  158.3 12.0 %collective-permute-start.9 = (bf16[2,256,256]{2,1,0:T(8,128)(2,1)S(1)}, bf16[2,256,256]{2,1,0:T(8,128)(2,1)S(1)}, u32[]{:S(2)}, u32[]{:S(2)}) collective-permute-start(bf16[2,256,256]{2,1,0:T(8,128)(2,1)S(1)} %bitcast.173), channel_id=1, source_target_pairs={{0,1},{1,2},{2,3},{3,0},{4,5},{5,6},{6,7},{7,4},{8,9},{9,10},{10,1... | collective-permute-start | bytes 786440 | tf_op jit(solution)/shard_map/ppermute | solution.py:394
  158.3 20.9 %collective-permute-start.10 = (bf16[2,256,256]{2,1,0:T(8,128)(2,1)S(1)}, bf16[2,256,256]{2,1,0:T(8,128)(2,1)S(1)}, u32[]{:S(2)}, u32[]{:S(2)}) collective-permute-start(bf16[2,256,256]{2,1,0:T(8,128)(2,1)S(1)} %bitcast.174), channel_id=1, source_target_pairs={{0,2},{1,3},{2,0},{3,1},{4,6},{5,7},{6,4},{7,5},{8,10},{9,11},{10,... | collective-permute-start | bytes 786440 | tf_op jit(solution)/shard_map/ppermute | solution.py:394
  160.4 18.8 %collective-permute-start.11 = (bf16[2,256,256]{2,1,0:T(8,128)(2,1)S(1)}, bf16[2,256,256]{2,1,0:T(8,128)(2,1)S(1)}, u32[]{:S(2)}, u32[]{:S(2)}) collective-permute-start(bf16[2,256,256]{2,1,0:T(8,128)(2,1)S(1)} %bitcast.175), channel_id=1, source_target_pairs={{0,3},{1,0},{2,1},{3,2},{4,7},{5,4},{6,5},{7,6},{8,11},{9,8},{10,9... | collective-permute-start | bytes 786440 | tf_op jit(solution)/shard_map/ppermute | solution.py:394
  180.6 40.8 %collective-permute-start.12 = (bf16[256,2048]{1,0:T(8,128)(2,1)}, bf16[256,2048]{1,0:T(8,128)(2,1)S(1)}, u32[]{:S(2)}, u32[]{:S(2)}) collective-permute-start(bf16[256,2048]{1,0:T(8,128)(2,1)} %collective-permute-done.8), channel_id=1, source_target_pairs={{0,1},{1,2},{2,3},{3,0},{4,5},{5,6},{6,7},{7,4},{8,9},{9,10},{10,1... | collective-permute-start | bytes 3145736 | tf_op jit(solution)/shard_map/ppermute | solution.py:394
  185.3 47.4 %collective-permute-start.13 = (bf16[512,2048]{1,0:T(8,128)(2,1)}, bf16[512,2048]{1,0:T(8,128)(2,1)}, u32[]{:S(2)}, u32[]{:S(2)}) collective-permute-start(bf16[512,2048]{1,0:T(8,128)(2,1)} %copy-done.7), channel_id=1, source_target_pairs={{0,16},{4,20},{8,24},{12,28},{16,0},{20,4},{24,8},{28,12},{1,17},{... | collective-permute-start | bytes 6291464 | tf_op jit(solution)/shard_map/ppermute | solution.py:449
  186.3 46.4 %collective-permute-start.14 = (bf16[512,2048]{1,0:T(8,128)(2,1)}, bf16[512,2048]{1,0:T(8,128)(2,1)}, u32[]{:S(2)}, u32[]{:S(2)}) collective-permute-start(bf16[512,2048]{1,0:T(8,128)(2,1)} %pad_maximum_fusion.3.refs_1_.refs_9_), channel_id=1, source_target_pairs={{0,8},{4,12},{8,0},{12,4},{16,24},{20,28},{24,16},{28,20},{1,9},{5... | collective-permute-start | bytes 6291464 | tf_op jit(solution)/shard_map/ppermute | solution.py:449
  187.4 350.9 %reduce-scatter.5.cloned.1.call-start = ((), (), s32[]{:S(2)}) async-start(), calls=%async_computation.10 | async-start | bytes 5242880 | tf_op jit(solution)/shard_map/reduce_scatter | solution.py:632
  232.7 36.9 %collective-permute-start.15 = (bf16[512,2048]{1,0:T(8,128)(2,1)}, bf16[512,2048]{1,0:T(8,128)(2,1)}, u32[]{:S(2)}, u32[]{:S(2)}) collective-permute-start(bf16[512,2048]{1,0:T(8,128)(2,1)} %collective-permute-done.13.refs_0_.refs_12_), channel_id=1, source_target_pairs={{0,4},{4,0},{8,12},{12,8},{16,20},{20,16},{24,28},{28,24},{1,5},{5... | collective-permute-start | bytes 6291464 | tf_op jit(solution)/shard_map/ppermute | solution.py:449
  233.0 32.1 %collective-permute-start.17 = (bf16[256,2048]{1,0:T(8,128)(2,1)S(1)}, bf16[256,2048]{1,0:T(8,128)(2,1)S(1)}, u32[]{:S(2)}, u32[]{:S(2)}) collective-permute-start(bf16[256,2048]{1,0:T(8,128)(2,1)S(1)} %get-tuple-element.322), channel_id=1, source_target_pairs={{0,8},{4,12},{8,0},{12,4},{16,24},{20,28},{24,16},{28,20},{1,9},{5... | collective-permute-start | bytes 3145736 | tf_op jit(solution)/shard_map/ppermute | solution.py:449
  234.3 36.9 %collective-permute-start.16 = (bf16[512,2048]{1,0:T(8,128)(2,1)}, bf16[512,2048]{1,0:T(8,128)(2,1)}, u32[]{:S(2)}, u32[]{:S(2)}) collective-permute-start(bf16[512,2048]{1,0:T(8,128)(2,1)} %collective-permute-done.14.refs_1_.refs_13_), channel_id=1, source_target_pairs={{0,4},{4,0},{8,12},{12,8},{16,20},{20,16},{24,28},{28,24},{1,5},{5... | collective-permute-start | bytes 6291464 | tf_op jit(solution)/shard_map/ppermute | solution.py:449
  234.5 32.1 %collective-permute-start.18 = (bf16[256,2048]{1,0:T(8,128)(2,1)S(1)}, bf16[256,2048]{1,0:T(8,128)(2,1)S(1)}, u32[]{:S(2)}, u32[]{:S(2)}) collective-permute-start(bf16[256,2048]{1,0:T(8,128)(2,1)S(1)} %get-tuple-element.321), channel_id=1, source_target_pairs={{0,16},{4,20},{8,24},{12,28},{16,0},{20,4},{24,8},{28,12},{1,17},{... | collective-permute-start | bytes 3145736 | tf_op jit(solution)/shard_map/ppermute | solution.py:449
  268.2 17.6 %collective-permute-start.19 = (bf16[512,2048]{1,0:T(8,128)(2,1)}, bf16[512,2048]{1,0:T(8,128)(2,1)}, u32[]{:S(2)}, u32[]{:S(2)}) collective-permute-start(bf16[512,2048]{1,0:T(8,128)(2,1)} %pad_maximum_fusion.4.refs_0_), channel_id=1, source_target_pairs={{0,4},{4,0},{8,12},{12,8},{16,20},{20,16},{24,28},{28,24},{1,5},{5... | collective-permute-start | bytes 6291464 | tf_op jit(solution)/shard_map/ppermute | solution.py:449
  268.2 17.6 %collective-permute-start.20 = (bf16[512,2048]{1,0:T(8,128)(2,1)}, bf16[512,2048]{1,0:T(8,128)(2,1)}, u32[]{:S(2)}, u32[]{:S(2)}) collective-permute-start(bf16[512,2048]{1,0:T(8,128)(2,1)} %pad_maximum_fusion.5.refs_1_), channel_id=1, source_target_pairs={{0,4},{4,0},{8,12},{12,8},{16,20},{20,16},{24,28},{28,24},{1,5},{5... | collective-permute-start | bytes 6291464 | tf_op jit(solution)/shard_map/ppermute | solution.py:449
  268.7 47.9 %collective-permute-start.21 = (bf16[512,2048]{1,0:T(8,128)(2,1)}, bf16[512,2048]{1,0:T(8,128)(2,1)}, u32[]{:S(2)}, u32[]{:S(2)}) collective-permute-start(bf16[512,2048]{1,0:T(8,128)(2,1)} %pad_maximum_fusion.4.refs_0_), channel_id=1, source_target_pairs={{0,16},{4,20},{8,24},{12,28},{16,0},{20,4},{24,8},{28,12},{1,17},{... | collective-permute-start | bytes 6291464 | tf_op jit(solution)/shard_map/ppermute | solution.py:449
  269.6 47.6 %collective-permute-start.22 = (bf16[512,2048]{1,0:T(8,128)(2,1)}, bf16[512,2048]{1,0:T(8,128)(2,1)}, u32[]{:S(2)}, u32[]{:S(2)}) collective-permute-start(bf16[512,2048]{1,0:T(8,128)(2,1)} %pad_maximum_fusion.5.refs_1_), channel_id=1, source_target_pairs={{0,8},{4,12},{8,0},{12,4},{16,24},{20,28},{24,16},{28,20},{1,9},{5... | collective-permute-start | bytes 6291464 | tf_op jit(solution)/shard_map/ppermute | solution.py:449
  317.2 14.4 %collective-permute-start.23 = (bf16[512,2048]{1,0:T(8,128)(2,1)}, bf16[512,2048]{1,0:T(8,128)(2,1)}, u32[]{:S(2)}, u32[]{:S(2)}) collective-permute-start(bf16[512,2048]{1,0:T(8,128)(2,1)} %collective-permute-done.21.refs_0_.refs_4_), channel_id=1, source_target_pairs={{0,4},{4,0},{8,12},{12,8},{16,20},{20,16},{24,28},{28,24},{1,5},{5... | collective-permute-start | bytes 6291464 | tf_op jit(solution)/shard_map/ppermute | solution.py:449
  317.2 14.4 %collective-permute-start.24 = (bf16[512,2048]{1,0:T(8,128)(2,1)}, bf16[512,2048]{1,0:T(8,128)(2,1)}, u32[]{:S(2)}, u32[]{:S(2)}) collective-permute-start(bf16[512,2048]{1,0:T(8,128)(2,1)} %collective-permute-done.22.refs_1_.refs_5_), channel_id=1, source_target_pairs={{0,4},{4,0},{8,12},{12,8},{16,20},{20,16},{24,28},{28,24},{1,5},{5... | collective-permute-start | bytes 6291464 | tf_op jit(solution)/shard_map/ppermute | solution.py:449
  376.7 48.1 %collective-permute-start.28 = (bf16[512,2048]{1,0:T(8,128)(2,1)}, bf16[512,2048]{1,0:T(8,128)(2,1)S(1)}, u32[]{:S(2)}, u32[]{:S(2)}) collective-permute-start(bf16[512,2048]{1,0:T(8,128)(2,1)} %add_convert_fusion.4), channel_id=1, source_target_pairs={{0,16},{4,20},{8,24},{12,28},{16,0},{20,4},{24,8},{28,12},{1,17},{... | collective-permute-start | bytes 6291464 | tf_op jit(solution)/shard_map/ppermute | solution.py:449
  377.9 47.8 %collective-permute-start.29 = (bf16[512,2048]{1,0:T(8,128)(2,1)}, bf16[512,2048]{1,0:T(8,128)(2,1)S(1)}, u32[]{:S(2)}, u32[]{:S(2)}) collective-permute-start(bf16[512,2048]{1,0:T(8,128)(2,1)} %add_convert_fusion.3), channel_id=1, source_target_pairs={{0,8},{4,12},{8,0},{12,4},{16,24},{20,28},{24,16},{28,20},{1,9},{5... | collective-permute-start | bytes 6291464 | tf_op jit(solution)/shard_map/ppermute | solution.py:449
  428.6 40.0 %collective-permute-start.31 = (bf16[256,2048]{1,0:T(8,128)(2,1)}, bf16[256,2048]{1,0:T(8,128)(2,1)}, u32[]{:S(2)}, u32[]{:S(2)}) collective-permute-start(bf16[256,2048]{1,0:T(8,128)(2,1)} %slice.392), channel_id=1, source_target_pairs={{0,16},{4,20},{8,24},{12,28},{16,0},{20,4},{24,8},{28,12},{1,17},{... | collective-permute-start | bytes 3145736 | tf_op jit(solution)/shard_map/ppermute | solution.py:449
  431.5 39.5 %collective-permute-start.30 = (bf16[256,2048]{1,0:T(8,128)(2,1)}, bf16[256,2048]{1,0:T(8,128)(2,1)}, u32[]{:S(2)}, u32[]{:S(2)}) collective-permute-start(bf16[256,2048]{1,0:T(8,128)(2,1)} %slice.393), channel_id=1, source_target_pairs={{0,8},{4,12},{8,0},{12,4},{16,24},{20,28},{24,16},{28,20},{1,9},{5... | collective-permute-start | bytes 3145736 | tf_op jit(solution)/shard_map/ppermute | solution.py:449
  432.1 292.1 %reduce-scatter.9.cloned.1.call-start = ((), (), s32[]{:S(2)}) async-start(), calls=%async_computation.12 | async-start | bytes 5242880 | tf_op jit(solution)/shard_map/reduce_scatter | solution.py:677
  438.1 35.8 %collective-permute-start.32 = (bf16[512,2048]{1,0:T(8,128)(2,1)}, bf16[512,2048]{1,0:T(8,128)(2,1)}, u32[]{:S(2)}, u32[]{:S(2)}) collective-permute-start(bf16[512,2048]{1,0:T(8,128)(2,1)} %convolution_convert_fusion.3), channel_id=1, source_target_pairs={{0,4},{4,0},{8,12},{12,8},{16,20},{20,16},{24,28},{28,24},{1,5},{5... | collective-permute-start | bytes 6291464 | tf_op jit(solution)/shard_map/ppermute | solution.py:449
  441.8 38.4 %collective-permute-start.33 = (bf16[512,2048]{1,0:T(8,128)(2,1)}, bf16[512,2048]{1,0:T(8,128)(2,1)S(1)}, u32[]{:S(2)}, u32[]{:S(2)}) collective-permute-start(bf16[512,2048]{1,0:T(8,128)(2,1)} %convolution_convert_fusion.2), channel_id=1, source_target_pairs={{0,4},{4,0},{8,12},{12,8},{16,20},{20,16},{24,28},{28,24},{1,5},{5... | collective-permute-start | bytes 6291464 | tf_op jit(solution)/shard_map/ppermute | solution.py:449
  482.6 54.4 %collective-permute-start.34 = (bf16[512,2048]{1,0:T(8,128)(2,1)S(1)}, bf16[512,2048]{1,0:T(8,128)(2,1)S(1)}, u32[]{:S(2)}, u32[]{:S(2)}) collective-permute-start(bf16[512,2048]{1,0:T(8,128)(2,1)S(1)} %add_convert_fusion.2), channel_id=1, source_target_pairs={{0,16},{4,20},{8,24},{12,28},{16,0},{20,4},{24,8},{28,12},{1,17},{... | collective-permute-start | bytes 6291464 | tf_op jit(solution)/shard_map/ppermute | solution.py:449
  483.8 54.5 %collective-permute-start.35 = (bf16[512,2048]{1,0:T(8,128)(2,1)S(1)}, bf16[512,2048]{1,0:T(8,128)(2,1)}, u32[]{:S(2)}, u32[]{:S(2)}) collective-permute-start(bf16[512,2048]{1,0:T(8,128)(2,1)S(1)} %add_convert_fusion.1), channel_id=1, source_target_pairs={{0,8},{4,12},{8,0},{12,4},{16,24},{20,28},{24,16},{28,20},{1,9},{5... | collective-permute-start | bytes 6291464 | tf_op jit(solution)/shard_map/ppermute | solution.py:449
  538.3 26.9 %collective-permute-start.36 = (bf16[1024,2048]{1,0:T(8,128)(2,1)}, bf16[1024,2048]{1,0:T(8,128)(2,1)}, u32[]{:S(2)}, u32[]{:S(2)}) collective-permute-start(bf16[1024,2048]{1,0:T(8,128)(2,1)} %convolution_convert_fusion.1), channel_id=1, source_target_pairs={{0,4},{4,0},{8,12},{12,8},{16,20},{20,16},{24,28},{28,24},{1,5},{5... | collective-permute-start | bytes 12582920 | tf_op jit(solution)/shard_map/ppermute | solution.py:449
  547.6 27.0 %collective-permute-start.37 = (bf16[1024,2048]{1,0:T(8,128)(2,1)}, bf16[1024,2048]{1,0:T(8,128)(2,1)}, u32[]{:S(2)}, u32[]{:S(2)}) collective-permute-start(bf16[1024,2048]{1,0:T(8,128)(2,1)} %shard_map.300), channel_id=1, source_target_pairs={{0,4},{4,0},{8,12},{12,8},{16,20},{20,16},{24,28},{28,24},{1,5},{5... | collective-permute-start | bytes 12582920 | tf_op jit(solution)/shard_map/ppermute | solution.py:449
  550.1 39.8 %collective-permute-start.38 = (bf16[2,256,256]{2,1,0:T(8,128)(2,1)S(1)}, bf16[2,256,256]{2,1,0:T(8,128)(2,1)}, u32[]{:S(2)}, u32[]{:S(2)}) collective-permute-start(bf16[2,256,256]{2,1,0:T(8,128)(2,1)S(1)} %get-tuple-element.334), channel_id=1, source_target_pairs={{0,1},{1,2},{2,3},{3,0},{4,5},{5,6},{6,7},{7,4},{8,9},{9,10},{10,1... | collective-permute-start | bytes 786440 | tf_op jit(solution)/shard_map/ppermute | solution.py:394
  559.8 30.1 %collective-permute-start.39 = (bf16[2,256,256]{2,1,0:T(8,128)(2,1)S(1)}, bf16[2,256,256]{2,1,0:T(8,128)(2,1)}, u32[]{:S(2)}, u32[]{:S(2)}) collective-permute-start(bf16[2,256,256]{2,1,0:T(8,128)(2,1)S(1)} %get-tuple-element.333), channel_id=1, source_target_pairs={{0,2},{1,3},{2,0},{3,1},{4,6},{5,7},{6,4},{7,5},{8,10},{9,11},{10,... | collective-permute-start | bytes 786440 | tf_op jit(solution)/shard_map/ppermute | solution.py:394
  564.6 25.2 %collective-permute-start.40 = (bf16[2,256,256]{2,1,0:T(8,128)(2,1)S(1)}, bf16[2,256,256]{2,1,0:T(8,128)(2,1)}, u32[]{:S(2)}, u32[]{:S(2)}) collective-permute-start(bf16[2,256,256]{2,1,0:T(8,128)(2,1)S(1)} %get-tuple-element.332), channel_id=1, source_target_pairs={{0,3},{1,0},{2,1},{3,2},{4,7},{5,4},{6,5},{7,6},{8,11},{9,8},{10,9... | collective-permute-start | bytes 786440 | tf_op jit(solution)/shard_map/ppermute | solution.py:394
  592.8 26.4 %collective-permute-start.41 = (bf16[256,2048]{1,0:T(8,128)(2,1)}, bf16[256,2048]{1,0:T(8,128)(2,1)}, u32[]{:S(2)}, u32[]{:S(2)}) collective-permute-start(bf16[256,2048]{1,0:T(8,128)(2,1)} %copy-done.29), channel_id=1, source_target_pairs={{0,16},{4,20},{8,24},{12,28},{16,0},{20,4},{24,8},{28,12},{1,17},{... | collective-permute-start | bytes 3145736 | tf_op jit(solution)/shard_map/ppermute | solution.py:449
  593.1 26.4 %collective-permute-start.42 = (bf16[256,2048]{1,0:T(8,128)(2,1)}, bf16[256,2048]{1,0:T(8,128)(2,1)}, u32[]{:S(2)}, u32[]{:S(2)}) collective-permute-start(bf16[256,2048]{1,0:T(8,128)(2,1)} %copy-done.28), channel_id=1, source_target_pairs={{0,8},{4,12},{8,0},{12,4},{16,24},{20,28},{24,16},{28,20},{1,9},{5... | collective-permute-start | bytes 3145736 | tf_op jit(solution)/shard_map/ppermute | solution.py:449
  596.6 63.1 %collective-permute-start.45 = (bf16[256,2048]{1,0:T(8,128)(2,1)}, bf16[256,2048]{1,0:T(8,128)(2,1)}, u32[]{:S(2)}, u32[]{:S(2)}) collective-permute-start(bf16[256,2048]{1,0:T(8,128)(2,1)} %slice.390), channel_id=1, source_target_pairs={{0,16},{4,20},{8,24},{12,28},{16,0},{20,4},{24,8},{28,12},{1,17},{... | collective-permute-start | bytes 3145736 | tf_op jit(solution)/shard_map/ppermute | solution.py:449
  601.1 60.5 %collective-permute-start.44 = (bf16[256,2048]{1,0:T(8,128)(2,1)}, bf16[256,2048]{1,0:T(8,128)(2,1)}, u32[]{:S(2)}, u32[]{:S(2)}) collective-permute-start(bf16[256,2048]{1,0:T(8,128)(2,1)} %slice.391), channel_id=1, source_target_pairs={{0,8},{4,12},{8,0},{12,4},{16,24},{20,28},{24,16},{28,20},{1,9},{5... | collective-permute-start | bytes 3145736 | tf_op jit(solution)/shard_map/ppermute | solution.py:449
  604.6 47.6 %all-to-all-start.1 = ((bf16[8,64,1024]{2,1,0:T(8,128)(2,1)}), bf16[8,64,1024]{2,1,0:T(8,128)(2,1)}, u32[]{:S(2)}, u32[]{:S(2)}) async-start(bf16[8,64,1024]{2,1,0:T(8,128)(2,1)} %reduce-scatter.5.cloned.1.call-done), calls=%async_computation.5 | async-start | bytes 2097152 | tf_op jit(solution)/shard_map/all_to_all | solution.py:752
  608.9 137.4 %reduce-scatter.7.cloned.1.call-start = ((), (), s32[]{:S(2)}) async-start(), calls=%async_computation.11 | async-start | bytes 1310720 | tf_op jit(solution)/shard_map/reduce_scatter | solution.py:691
  619.5 51.0 %collective-permute-start.43 = (bf16[1024,2048]{1,0:T(8,128)(2,1)}, bf16[1024,2048]{1,0:T(8,128)(2,1)}, u32[]{:S(2)}, u32[]{:S(2)}) collective-permute-start(bf16[1024,2048]{1,0:T(8,128)(2,1)} %shard_map.304), channel_id=1, source_target_pairs={{0,4},{4,0},{8,12},{12,8},{16,20},{20,16},{24,28},{28,24},{1,5},{5... | collective-permute-start | bytes 12582920 | tf_op jit(solution)/shard_map/ppermute | solution.py:449
  656.9 10.5 %collective-permute-start.47 = (bf16[128,2048]{1,0:T(8,128)(2,1)S(1)}, bf16[128,2048]{1,0:T(8,128)(2,1)S(1)}, u32[]{:S(2)}, u32[]{:S(2)}) collective-permute-start(bf16[128,2048]{1,0:T(8,128)(2,1)S(1)} %slice.396), channel_id=1, source_target_pairs={{0,16},{4,20},{8,24},{12,28},{16,0},{20,4},{24,8},{28,12},{1,17},{... | collective-permute-start | bytes 1572872 | tf_op jit(solution)/shard_map/ppermute | solution.py:449
  659.2 10.1 %collective-permute-start.46 = (bf16[128,2048]{1,0:T(8,128)(2,1)S(1)}, bf16[128,2048]{1,0:T(8,128)(2,1)S(1)}, u32[]{:S(2)}, u32[]{:S(2)}) collective-permute-start(bf16[128,2048]{1,0:T(8,128)(2,1)S(1)} %slice.397), channel_id=1, source_target_pairs={{0,8},{4,12},{8,0},{12,4},{16,24},{20,28},{24,16},{28,20},{1,9},{5... | collective-permute-start | bytes 1572872 | tf_op jit(solution)/shard_map/ppermute | solution.py:449
  686.9 21.0 %collective-permute-start.49 = (bf16[256,2048]{1,0:T(8,128)(2,1)}, bf16[256,2048]{1,0:T(8,128)(2,1)}, u32[]{:S(2)}, u32[]{:S(2)}) collective-permute-start(bf16[256,2048]{1,0:T(8,128)(2,1)} %get-tuple-element.294), channel_id=1, source_target_pairs={{0,16},{4,20},{8,24},{12,28},{16,0},{20,4},{24,8},{28,12},{1,17},{... | collective-permute-start | bytes 3145736 | tf_op jit(solution)/shard_map/ppermute | solution.py:449
  688.6 20.5 %collective-permute-start.50 = (bf16[256,2048]{1,0:T(8,128)(2,1)}, bf16[256,2048]{1,0:T(8,128)(2,1)}, u32[]{:S(2)}, u32[]{:S(2)}) collective-permute-start(bf16[256,2048]{1,0:T(8,128)(2,1)} %get-tuple-element.295), channel_id=1, source_target_pairs={{0,8},{4,12},{8,0},{12,4},{16,24},{20,28},{24,16},{28,20},{1,9},{5... | collective-permute-start | bytes 3145736 | tf_op jit(solution)/shard_map/ppermute | solution.py:449
  690.8 69.0 %reduce-scatter.11.cloned.1.call-start = ((), (), s32[]{:S(2)}) async-start(), calls=%async_computation.13 | async-start | bytes 1310720 | tf_op jit(solution)/shard_map/reduce_scatter | solution.py:737
  710.7 9.7 %collective-permute-start.53 = (bf16[128,2048]{1,0:T(8,128)(2,1)S(1)}, bf16[128,2048]{1,0:T(8,128)(2,1)S(1)}, u32[]{:S(2)}, u32[]{:S(2)}) collective-permute-start(bf16[128,2048]{1,0:T(8,128)(2,1)S(1)} %slice.394), channel_id=1, source_target_pairs={{0,16},{4,20},{8,24},{12,28},{16,0},{20,4},{24,8},{28,12},{1,17},{... | collective-permute-start | bytes 1572872 | tf_op jit(solution)/shard_map/ppermute | solution.py:449
  713.8 9.2 %collective-permute-start.52 = (bf16[128,2048]{1,0:T(8,128)(2,1)S(1)}, bf16[128,2048]{1,0:T(8,128)(2,1)S(1)}, u32[]{:S(2)}, u32[]{:S(2)}) collective-permute-start(bf16[128,2048]{1,0:T(8,128)(2,1)S(1)} %slice.395), channel_id=1, source_target_pairs={{0,8},{4,12},{8,0},{12,4},{16,24},{20,28},{24,16},{28,20},{1,9},{5... | collective-permute-start | bytes 1572872 | tf_op jit(solution)/shard_map/ppermute | solution.py:449
  715.7 8.5 %collective-permute-start.51 = (bf16[288,256]{1,0:T(8,128)(2,1)S(1)}, bf16[288,256]{1,0:T(8,128)(2,1)S(1)}, u32[]{:S(2)}, u32[]{:S(2)}) collective-permute-start(bf16[288,256]{1,0:T(8,128)(2,1)S(1)} %get-tuple-element.338), channel_id=1, source_target_pairs={{0,16},{4,20},{8,24},{12,28},{16,0},{20,4},{24,8},{28,12},{1,17},{... | collective-permute-start | bytes 442376 | tf_op jit(solution)/shard_map/ppermute | solution.py:449
  716.6 8.1 %collective-permute-start.55 = (bf16[288,256]{1,0:T(8,128)(2,1)S(1)}, bf16[288,256]{1,0:T(8,128)(2,1)}, u32[]{:S(2)}, u32[]{:S(2)}) collective-permute-start(bf16[288,256]{1,0:T(8,128)(2,1)S(1)} %get-tuple-element.339), channel_id=1, source_target_pairs={{0,8},{4,12},{8,0},{12,4},{16,24},{20,28},{24,16},{28,20},{1,9},{5... | collective-permute-start | bytes 442376 | tf_op jit(solution)/shard_map/ppermute | solution.py:449
  737.2 12.6 %collective-permute-start.59 = (bf16[17664]{0:T(1024)(128)(2,1)S(1)}, bf16[17664]{0:T(1024)(128)(2,1)S(1)}, u32[]{:S(2)}, u32[]{:S(2)}) collective-permute-start(bf16[17664]{0:T(1024)(128)(2,1)S(1)} %get-tuple-element.315), channel_id=1, source_target_pairs={{0,3},{1,0},{2,1},{3,2},{4,7},{5,4},{6,5},{7,6},{8,11},{9,8},{10,9... | collective-permute-start | bytes 105992 | tf_op jit(solution)/shard_map/ppermute | solution.py:394
  738.4 11.5 %collective-permute-start.58 = (bf16[17664]{0:T(1024)(128)(2,1)S(1)}, bf16[17664]{0:T(1024)(128)(2,1)S(1)}, u32[]{:S(2)}, u32[]{:S(2)}) collective-permute-start(bf16[17664]{0:T(1024)(128)(2,1)S(1)} %get-tuple-element.316), channel_id=1, source_target_pairs={{0,2},{1,3},{2,0},{3,1},{4,6},{5,7},{6,4},{7,5},{8,10},{9,11},{10,... | collective-permute-start | bytes 105992 | tf_op jit(solution)/shard_map/ppermute | solution.py:394
  740.2 9.7 %collective-permute-start.57 = (bf16[17664]{0:T(1024)(128)(2,1)S(1)}, bf16[17664]{0:T(1024)(128)(2,1)S(1)}, u32[]{:S(2)}, u32[]{:S(2)}) collective-permute-start(bf16[17664]{0:T(1024)(128)(2,1)S(1)} %get-tuple-element.314), channel_id=1, source_target_pairs={{0,1},{1,2},{2,3},{3,0},{4,5},{5,6},{6,7},{7,4},{8,9},{9,10},{10,1... | collective-permute-start | bytes 105992 | tf_op jit(solution)/shard_map/ppermute | solution.py:394
  (83 other events, 949.6 us)
Sparse Core Ops, SparseCore 0:
  17.7 35.3 all-gather.4
  59.4 63.5 all-gather.6
  125.5 54.3 all-gather.8
  187.5 88.4 all-gather.10
  432.2 87.7 reduce-scatter.4
  590.0 74.0 reduce-scatter.8
  690.9 25.6 reduce-scatter.6
  732.9 26.8 reduce-scatter.10
